TPU v7x, 32 devices: a whole 2x2x4 slice. The times are simulated.
32 devices in a mesh: group: 2 (over x), seq: 8 (over z, y), fsdp: 2 (over core).
Axes of the slice: x: 2, y: 2, z: 4, core: 2. Of those that a mesh axis runs over, the one named last changes fastest.
Arguments:
- q_img: bfloat16 [2048, 2048], P(('group', 'seq'), 'fsdp'), parts along dimension 0, may hold values from -6 to 6
- k_img: bfloat16 [2048, 2048], P(('group', 'seq'), 'fsdp'), parts along dimension 0, may hold values from -6 to 6
- v_img: bfloat16 [2048, 2048], P(('group', 'seq'), 'fsdp'), parts along dimension 0, may hold values from -6 to 6
- k_txt: bfloat16 [1024, 2048], P('group', 'fsdp'), parts along dimension 0, may hold values from -6 to 6
- v_txt: bfloat16 [1024, 2048], P('group', 'fsdp'), parts along dimension 0, may hold values from -6 to 6
- out_weight: bfloat16 [3072, 2048], P('seq', 'fsdp'), may hold values from -0.125 to 0.125
- d_out: bfloat16 [2048, 3072], P(('group', 'seq')), parts along dimension 0, may hold values from -12 to 12
Outputs:
- q_grad: bfloat16 [2048, 2048], P(('group', 'seq'), 'fsdp'), parts along dimension 0
- k_grad: bfloat16 [2048, 2048], P(('group', 'seq'), 'fsdp'), parts along dimension 0
- v_grad: bfloat16 [2048, 2048], P(('group', 'seq'), 'fsdp'), parts along dimension 0
- d_weight: float32 [6144, 2048], P(('group', 'seq'), 'fsdp'), parts along dimension 0
There are 2 independent parts, one for each index of `group`. A program takes and returns all parts, laid end to end along the dimension named above; an argument that names none is the same for every part. Nothing has to cross between parts.
All inputs are finite; a program needn't handle non-finite values.
Results may differ from a plain program's by a relative error of at most 0.015.
Values may be sent and summed in bfloat16 or wider, within the bound.
No kernel may reach another device: no remote copies, remote signals or barrier semaphores. Data moves between devices by JAX's collectives and lax.ppermute only.
A program may use at most 128 MiB of HBM per device.

v0:
```python
import jax
import jax.numpy as jnp
from jax import lax
from jax.sharding import PartitionSpec as P

HD = 128


def attend(queries, cotangents, key_rows, value_rows, block_rows):
    score_scale = HD ** (-0.5)
    query_count = queries.shape[0]
    block_count = query_count // block_rows
    query_blocks = queries.reshape(block_count, block_rows, HD)
    grad_blocks = cotangents.reshape(block_count, block_rows, HD)

    def one_block(accumulated, pair_item):
        query_block, grad_block = pair_item
        scores = jnp.dot(query_block, key_rows.T, preferred_element_type=jnp.float32) * score_scale
        row_max = jnp.max(scores, axis=1, keepdims=True)
        probs = jnp.exp(scores - row_max)
        probs = probs / jnp.sum(probs, axis=1, keepdims=True)
        probs_low = probs.astype(jnp.bfloat16)
        out_rows = jnp.dot(probs_low, value_rows, preferred_element_type=jnp.float32).astype(
            jnp.bfloat16
        )
        prob_grad = jnp.dot(grad_block, value_rows.T, preferred_element_type=jnp.float32)
        row_dot = jnp.sum(
            grad_block.astype(jnp.float32) * out_rows.astype(jnp.float32), axis=1, keepdims=True
        )
        score_grad = (probs * (prob_grad - row_dot)).astype(jnp.bfloat16)
        query_grad = (
            jnp.dot(score_grad, key_rows, preferred_element_type=jnp.float32) * score_scale
        ).astype(jnp.bfloat16)
        key_grad = (
            accumulated[0]
            + jnp.dot(score_grad.T, query_block, preferred_element_type=jnp.float32) * score_scale
        )
        value_grad = accumulated[1] + jnp.dot(
            probs_low.T, grad_block, preferred_element_type=jnp.float32
        )
        return ((key_grad, value_grad), (query_grad, out_rows))

    empty = jnp.zeros((key_rows.shape[0], HD), jnp.float32)
    (key_grad, value_grad), (query_grad, out_rows) = lax.scan(
        one_block, (empty, empty), (query_blocks, grad_blocks)
    )
    return (
        query_grad.reshape(query_count, HD),
        out_rows.reshape(query_count, HD),
        key_grad,
        value_grad,
    )


def local(q_img, k_img, v_img, k_txt, v_txt, out_weight, d_out):
    rows_here = q_img.shape[0]
    heads_here = q_img.shape[1] // HD
    seq_count = lax.axis_size("seq")
    share_count = seq_count // heads_here
    part_rows = rows_here // share_count
    seq_index = lax.axis_index("seq")
    head_index = seq_index // share_count
    column_cut = d_out
    attn_grad = jnp.dot(
        column_cut,
        lax.all_gather(out_weight, "seq", axis=0, tiled=True),
        preferred_element_type=jnp.float32,
    ).astype(jnp.bfloat16)

    def to_heads(array_in):
        shaped = array_in.reshape(share_count, part_rows, heads_here, HD).transpose(2, 0, 1, 3)
        return shaped.reshape(seq_count, part_rows, HD)

    def whole_heads(array_in):
        shaped = array_in.reshape(rows_here, heads_here, HD).transpose(1, 0, 2)
        shaped = jnp.broadcast_to(shaped[:, None], (heads_here, share_count, rows_here, HD))
        return shaped.reshape(seq_count, rows_here, HD)

    def from_heads(array_in):
        shaped = array_in.reshape(heads_here, share_count, part_rows, HD).transpose(1, 2, 0, 3)
        return shaped.reshape(rows_here, heads_here * HD)

    text_keys = lax.dynamic_slice_in_dim(k_txt, head_index * HD, HD, 1)
    text_values = lax.dynamic_slice_in_dim(v_txt, head_index * HD, HD, 1)
    query_side = jnp.concatenate([to_heads(q_img), to_heads(attn_grad)], axis=2)
    key_side = jnp.concatenate([whole_heads(k_img), whole_heads(v_img)], axis=2)
    packed = jnp.concatenate([query_side, key_side], axis=1)
    received = lax.all_to_all(packed, "seq", split_axis=0, concat_axis=0, tiled=True)
    queries = received[:, :part_rows, :HD].reshape(seq_count * part_rows, HD)
    cotangents = received[:, :part_rows, HD:].reshape(seq_count * part_rows, HD)
    image_keys = received[:, part_rows:, :HD].reshape(seq_count * rows_here, HD)
    image_values = received[:, part_rows:, HD:].reshape(seq_count * rows_here, HD)
    key_rows = jnp.concatenate([image_keys, text_keys], axis=0)
    value_rows = jnp.concatenate([image_values, text_values], axis=0)
    query_grad, out_rows, key_grad, value_grad = attend(
        queries, cotangents, key_rows, value_rows, min(512, queries.shape[0])
    )
    image_count = image_keys.shape[0]
    query_part = (
        jnp.concatenate([query_grad, out_rows], axis=1)
        .astype(jnp.float32)
        .reshape(seq_count, part_rows, 2 * HD)
    )
    key_part = jnp.concatenate([key_grad[:image_count], value_grad[:image_count]], axis=1).reshape(
        seq_count, rows_here, 2 * HD
    )
    returned = lax.all_to_all(
        jnp.concatenate([query_part, key_part], axis=1).astype(jnp.bfloat16),
        "seq",
        split_axis=0,
        concat_axis=0,
        tiled=True,
    ).astype(jnp.float32)
    q_grad = from_heads(returned[:, :part_rows, :HD]).astype(jnp.bfloat16)
    out_tok = from_heads(returned[:, :part_rows, HD:]).astype(jnp.bfloat16)
    summed = jnp.sum(
        returned[:, part_rows:, :].reshape(heads_here, share_count, rows_here, 2 * HD), axis=1
    )
    summed = summed.transpose(1, 0, 2)
    k_grad = summed[:, :, :HD].reshape(rows_here, heads_here * HD).astype(jnp.bfloat16)
    v_grad = summed[:, :, HD:].reshape(rows_here, heads_here * HD).astype(jnp.bfloat16)
    column_cut = d_out
    d_weight = lax.psum_scatter(
        jnp.dot(column_cut.T, out_tok, preferred_element_type=jnp.float32).astype(jnp.bfloat16),
        "seq",
        scatter_dimension=0,
        tiled=True,
    ).astype(jnp.float32)
    return (q_grad, k_grad, v_grad, d_weight)


def solution(mesh):
    in_specs = (
        P(("group", "seq"), "fsdp"),
        P(("group", "seq"), "fsdp"),
        P(("group", "seq"), "fsdp"),
        P("group", "fsdp"),
        P("group", "fsdp"),
        P("seq", "fsdp"),
        P(("group", "seq"), None),
    )
    out_specs = (
        P(("group", "seq"), "fsdp"),
        P(("group", "seq"), "fsdp"),
        P(("group", "seq"), "fsdp"),
        P(("group", "seq"), "fsdp"),
    )
    return jax.shard_map(local, mesh=mesh, in_specs=in_specs, out_specs=out_specs, check_vma=False)
```

profile of v0, /device:TPU:0, one launch (start us, length us, event | category | flops | bytes accessed | tf_op | source)
XLA Modules:
  0.0 350.9 jit_solution(9652952957892336212)
XLA Ops:
  7.2 0.7 all-gather.2.cloned.1.call-update
  7.9 1.1 copy.58
  9.0 1.1 copy.60
  10.2 1.1 copy.61
  11.3 100.7 %all-gather.2.cloned.1.call-done = bf16[3072,1024]{1,0:T(8,128)(2,1)} async-done(((bf16[384,1024]{1,0:T(8,128)(2,1)}), bf16[3072,1024]{1,0:T(8,128)(2,1)}) %all-gather.2.cloned.1.call-update) | async-done | bytes 6291472 | tf_op jit(solution)/shard_map/all_gather | solution.py:66
  112.0 3.8 %convolution_convert_fusion.1 = bf16[128,1024]{1,0:T(8,128)(2,1)S(1)} fusion(bf16[128,3072]{1,0:T(8,128)(2,1)S(1)} %copy-done, bf16[3072,1024]{1,0:T(8,128)(2,1)} %all-gather.2.cloned.1.call-done), kind=kOutput, calls=%fused_computation.29 | convolution fusion | flops 805437440 | bytes 7340032 | tf_op jit(solution)/shard_map/dot_general | solution.py:64
  115.9 1.1 maximum_maximum_fusion
  117.0 3.6 %all-to-all-start = ((bf16[8,256,256]{1,2,0:T(8,128)(2,1)}), bf16[8,256,256]{1,2,0:T(8,128)(2,1)S(1)}, u32[]{:S(2)}, u32[]{:S(2)}) async-start(bf16[8,256,256]{1,2,0:T(8,128)(2,1)} %maximum_maximum_fusion), calls=%async_computation | async-start | bytes 2097152 | tf_op jit(solution)/shard_map/all_to_all | solution.py:88
  120.7 1.7 constant_dynamic-slice_fusion.1
  122.4 23.8 %all-to-all-done = bf16[8,256,256]{1,2,0:T(8,128)(2,1)S(1)} async-done(((bf16[8,256,256]{1,2,0:T(8,128)(2,1)}), bf16[8,256,256]{1,2,0:T(8,128)(2,1)S(1)}, u32[]{:S(2)}, u32[]{:S(2)}) %all-to-all-start) | async-done | bytes 1048608 | tf_op jit(solution)/shard_map/all_to_all | solution.py:88
  146.1 1.1 fusion.19
  147.3 1.1 copy.65
  148.4 1.1 copy.64
  149.5 1.8 copy.63
  151.3 1.8 copy.62
  153.1 0.9 pad_maximum_fusion.3
  154.0 1.0 pad_maximum_fusion.2
  155.1 25.0 %while.17 = (s32[]{:T(128)}, f32[1536,128]{1,0:T(8,128)S(1)}, f32[1536,128]{1,0:T(8,128)S(1)}, bf16[2,512,128]{2,1,0:T(8,128)(2,1)}, bf16[2,512,128]{2,1,0:T(8,1...) while((s32[]{:T(128)}, f32[1536,128]{1,0:T(8,128)S(1)}, ...), condition=%wide.region_4.5_spmd.clone, body=%wide.region_0.4_spmd.clone.sunk | while | flops 1218050560 | bytes 63846740 | solution.py:44
  155.1 0.7 copy-done.4
  155.9 1.6 fusion.57
  158.1 0.7 fusion.59
  158.8 1.6 copy-done.1
  160.4 0.7 multiply_reduce_fusion.2
  161.2 0.7 constant_dynamic-update-slice_fusion.2
  161.9 3.1 convolution_add_fusion.2
  165.1 0.6 fusion.60
  166.0 0.6 fusion.62
  166.6 0.9 fusion.61
  167.6 0.7 copy-done.4
  168.5 1.6 fusion.57
  170.6 0.7 fusion.59
  171.3 1.6 copy-done.1
  172.9 0.7 multiply_reduce_fusion.2
  173.7 0.7 constant_dynamic-update-slice_fusion.2
  174.4 3.2 convolution_add_fusion.2
  177.6 0.6 fusion.60
  178.5 0.6 fusion.62
  179.1 0.9 fusion.61
  180.3 1.1 pad_maximum_fusion
  181.4 29.2 %all_to_all.10 = bf16[8,256,256]{2,1,0:T(8,128)(2,1)S(1)} all-to-all(bf16[8,256,256]{2,1,0:T(8,128)(2,1)S(1)} %pad_maximum_fusion), channel_id=1, replica_groups=mesh['group'=2,'seq'=8,'fsdp'=2] {'seq'}, dimensions={0} | all-to-all | bytes 2097152 | tf_op jit(solution)/shard_map/all_to_all | solution.py:107
  210.9 4.4 %convert_bitcast_fusion = bf16[3072,1024]{0,1:T(8,128)(2,1)} fusion(bf16[128,1024]{0,1:T(8,128)(2,1)S(1)} %bitcast.100, bf16[128,3072]{1,0:T(8,128)(2,1)S(1)} %copy-done), kind=kOutput, calls=%fused_computation.28 | convolution fusion | flops 808452096 | bytes 7340032 | tf_op jit(solution)/shard_map/dot_general | solution.py:124
  215.3 8.6 %copy.78 = bf16[3072,1024]{1,0:T(8,128)(2,1)} copy(bf16[3072,1024]{0,1:T(8,128)(2,1)} %convert_bitcast_fusion) | data formatting | bytes 12582912
  224.3 0.9 copy.75
  225.4 0.9 copy.74
  226.4 0.9 copy.73
  227.3 113.8 %reduce-scatter.4.cloned.1.call-done = bf16[384,1024]{1,0:T(8,128)(2,1)} async-done(((bf16[3072,1024]{1,0:T(8,128)(2,1)}), bf16[384,1024]{1,0:T(8,128)(2,1)}) %reduce-scatter.4.cloned.1.call-update) | async-done | bytes 786448
  341.1 1.5 copy.79
  342.6 1.4 copy.76
  (52 shorter events, 3.8 us)
Async XLA Ops:
  7.2 104.8 %copy-start = (bf16[128,3072]{1,0:T(8,128)(2,1)S(1)}, bf16[128,3072]{1,0:T(8,128)(2,1)}, u32[]{:S(2)}) copy-start(bf16[128,3072]{1,0:T(8,128)(2,1)} %param.15) | copy-start | bytes 2359300
  7.2 104.8 %all-gather.2.cloned.1.call-start = ((), (), s32[]{:S(2)}) async-start(), calls=%async_computation.3 | async-start | bytes 7077888 | tf_op jit(solution)/shard_map/all_gather | solution.py:66
  117.0 29.1 %all-to-all-start = ((bf16[8,256,256]{1,2,0:T(8,128)(2,1)}), bf16[8,256,256]{1,2,0:T(8,128)(2,1)S(1)}, u32[]{:S(2)}, u32[]{:S(2)}) async-start(bf16[8,256,256]{1,2,0:T(8,128)(2,1)} %maximum_maximum_fusion), calls=%async_computation | async-start | bytes 2097152 | tf_op jit(solution)/shard_map/all_to_all | solution.py:88
  120.6 220.5 %reduce-scatter.4.cloned.1.call-start = ((), (), s32[]{:S(2)}) async-start(), calls=%async_computation.4 | async-start | bytes 7077888
  155.1 0.7 copy-start.4
  158.8 1.6 copy-start.1
  161.2 3.8 %copy-start.2 = (f32[512,1536]{1,0:T(8,128)S(1)}, f32[512,1536]{1,0:T(8,128)}, u32[]{:S(2)}) copy-start(f32[512,1536]{1,0:T(8,128)} %copy-done.1) | copy-start | bytes 9437188 | tf_op jit(solution)/shard_map/while
  165.0 1.0 copy-start.6
  165.0 1.6 copy-start.3
  166.0 1.6 copy-start.5
  166.6 1.0 copy-start.7
  167.6 0.7 copy-start.4
  171.3 1.6 copy-start.1
  173.7 3.8 %copy-start.2 = (f32[512,1536]{1,0:T(8,128)S(1)}, f32[512,1536]{1,0:T(8,128)}, u32[]{:S(2)}) copy-start(f32[512,1536]{1,0:T(8,128)} %copy-done.1) | copy-start | bytes 9437188 | tf_op jit(solution)/shard_map/while
  177.5 1.0 copy-start.6
  177.6 1.6 copy-start.3
  178.5 1.6 copy-start.5
  179.1 1.0 copy-start.7
Sparse Core Ops, SparseCore 0:
  10.2 101.7 all-gather.1
  224.1 116.9 reduce-scatter.3
where the time goes:
time: 352 us; the launch traced here: 351 us
  waiting for transfers between devices  239 us (68%)
  local copies, waits for them, and re-layouts  34.5 us (10%)
  blocking collectives  29.2 us (8%)
  matrix products  23.3 us (7%)
  between operations  14.2 us (4%)
  other arithmetic  6.75 us (2%)
  starting transfers between devices  3.64 us (1%)
    unnamed x3, waiting for transfers between devices  115 us
    all_gather x1, waiting for transfers between devices, local(): lax.all_gather(out_weight, 'seq', axis=0, tiled=True)  101 us
    all_to_all x1, blocking collectives, local(): lax.all_to_all(jnp.concatenate([query_part, key_part], axis=1).astype(jnp...  29.2 us
    all_to_all x1, waiting for transfers between devices, local(): lax.all_to_all(packed, 'seq', split_axis=0, concat_axis=0, tiled=True)  23.8 us
    unnamed x11, local copies, waits for them, and re-layouts  17.5 us
  transfers between devices with their start and end apart: 3, of which 3 were waited for; matrix products, arithmetic and copies ran while one was open for 2% of the time, Pallas kernels for 0%

commit v1 on v0

--- a/solution.py
+++ b/solution.py
@@ -1,9 +1,18 @@
+import functools
+import math
+
 import jax
 import jax.numpy as jnp
 from jax import lax
+from jax.experimental import pallas as pl
+from jax.experimental.pallas import tpu as pltpu
 from jax.sharding import PartitionSpec as P
 
 HD = 128
+F32 = jnp.float32
+BF16 = jnp.bfloat16
+LIMIT = 48 * 1024 * 1024
+NT = (((1,), (1,)), ((), ()))
 
 
 def attend(queries, cotangents, key_rows, value_rows, block_rows):
@@ -52,7 +61,7 @@
     )
 
 
-def local(q_img, k_img, v_img, k_txt, v_txt, out_weight, d_out):
+def local_general(q_img, k_img, v_img, k_txt, v_txt, out_weight, d_out):
     rows_here = q_img.shape[0]
     heads_here = q_img.shape[1] // HD
     seq_count = lax.axis_size("seq")
@@ -129,6 +138,246 @@
     return (q_grad, k_grad, v_grad, d_weight)
 
 
+def call(kernel, outs, args, specs=None, scratch=(), scalars=0, out_specs=None, flops=0, moved=0):
+    vmem = pl.BlockSpec(memory_space=pltpu.VMEM)
+    if specs is None:
+        specs = [vmem] * (len(args) - scalars)
+    if out_specs is None:
+        out_specs = [vmem] * len(outs)
+    return pl.pallas_call(
+        kernel,
+        out_shape=outs,
+        grid_spec=pltpu.PrefetchScalarGridSpec(
+            num_scalar_prefetch=scalars,
+            grid=(1,),
+            in_specs=specs,
+            out_specs=out_specs,
+            scratch_shapes=list(scratch),
+        ),
+        compiler_params=pltpu.CompilerParams(vmem_limit_bytes=LIMIT),
+        cost_estimate=pl.CostEstimate(flops=flops, bytes_accessed=moved, transcendentals=0),
+    )(*args)
+
+
+def pack_kernel(q_ref, k_ref, v_ref, w_ref, tok_ref, wt_ref):
+    heads = tok_ref.shape[0]
+    rows = q_ref.shape[0]
+    for h in range(heads):
+        cols = slice(h * HD, (h + 1) * HD)
+        tok_ref[h, 0:rows, :] = q_ref[:, cols]
+        tok_ref[h, rows : 2 * rows, :] = k_ref[:, cols]
+        tok_ref[h, 2 * rows : 3 * rows, :] = v_ref[:, cols]
+        wt_ref[h, :, :] = w_ref[:, cols]
+
+
+def forward_kernel(me_ref, tok_ref, kt_ref, vt_ref, probs_ref, out_ref, keys, vals_t, *, chunk):
+    n, three, _ = tok_ref.shape
+    rows = three // 3
+    image = n * rows
+    text = kt_ref.shape[0]
+    keys[0:image, :] = tok_ref[:, rows : 2 * rows, :].reshape(image, HD)
+    keys[image : image + text, :] = kt_ref[...]
+    vals_t[:, 0:image] = tok_ref[:, 2 * rows : 3 * rows, :].reshape(image, HD).T
+    vals_t[:, image : image + text] = vt_ref[...].T
+    factor = HD ** (-0.5) * math.log2(math.e)
+    per = chunk // rows
+    for c in range(image // chunk):
+        queries = tok_ref[c * per : (c + 1) * per, 0:rows, :].reshape(chunk, HD)
+        scores = lax.dot_general(keys[...], queries, NT, preferred_element_type=F32)
+        top = jnp.max(scores, axis=0, keepdims=True)
+        weights = jnp.exp2((scores - top) * factor)
+        total = jnp.sum(weights, axis=0, keepdims=True)
+        low = (weights * (1.0 / total)).astype(BF16)
+        probs_ref[:, c * chunk : (c + 1) * chunk] = low
+        out_ref[:, c * chunk : (c + 1) * chunk] = jnp.dot(
+            vals_t[...], low, preferred_element_type=F32
+        ).astype(BF16)
+
+
+def project_kernel(place_ref, *refs, pieces):
+    blocks = refs[: len(pieces)]
+    w_ref, out_ref, grad_ref, dw_ref, cot, sems = refs[len(pieces) :]
+    n, depth, _ = w_ref.shape
+    copies = []
+    for i, rows in enumerate(pieces):
+        at = pl.multiple_of(place_ref[i], 16)
+        copies.append(pltpu.make_async_copy(blocks[i], cot.at[pl.ds(at, rows), :], sems.at[i]))
+    for copy in copies:
+        copy.start()
+    for copy in copies:
+        copy.wait()
+    weight = w_ref[...].reshape(n * depth, HD)
+    step = 256
+
+    @pl.loop(0, cot.shape[0] // step)
+    def _(i):
+        at = pl.ds(pl.multiple_of(i * step, step), step)
+        grad_ref[at, :] = jnp.dot(cot[at, :], weight, preferred_element_type=F32).astype(BF16)
+
+    @pl.loop(0, n)
+    def _(i):
+        cols = pl.ds(pl.multiple_of(i * depth, depth), depth)
+        dw_ref[i] = jnp.dot(out_ref[...], cot[:, cols], preferred_element_type=F32).astype(BF16)
+
+
+def backward_kernel(
+    me_ref, tok_ref, kt_ref, vt_ref, probs_ref, out_ref, grad_ref, send_ref, keys_t, vals, dk, dv, *, chunk
+):
+    n, three, _ = tok_ref.shape
+    rows = three // 3
+    image = n * rows
+    text = kt_ref.shape[0]
+    scale = HD ** (-0.5)
+    vals[0:image, :] = tok_ref[:, 2 * rows : 3 * rows, :].reshape(image, HD)
+    vals[image : image + text, :] = vt_ref[...]
+    keys_t[:, 0:image] = tok_ref[:, rows : 2 * rows, :].reshape(image, HD).T
+    keys_t[:, image : image + text] = kt_ref[...].T
+    per = chunk // rows
+    for c in range(image // chunk):
+        span = slice(c * chunk, (c + 1) * chunk)
+        grads = grad_ref[span, :]
+        queries = tok_ref[c * per : (c + 1) * per, 0:rows, :].reshape(chunk, HD)
+        row_dot = jnp.sum(
+            grads.astype(F32).T * out_ref[:, span].astype(F32), axis=0, keepdims=True
+        )
+        prob_grad = lax.dot_general(vals[...], grads, NT, preferred_element_type=F32)
+        low = probs_ref[:, span]
+        score_grad = (low.astype(F32) * (prob_grad - row_dot)).astype(BF16)
+        dq_t = jnp.dot(keys_t[...], score_grad, preferred_element_type=F32) * scale
+        send_ref[c * per : (c + 1) * per, 0:rows, :] = dq_t.T.astype(BF16).reshape(per, rows, HD)
+        dk_part = jnp.dot(score_grad[0:image, :], queries, preferred_element_type=F32)
+        dv_part = jnp.dot(low[0:image, :], grads, preferred_element_type=F32)
+        if c == 0:
+            dk[...] = dk_part
+            dv[...] = dv_part
+        else:
+            dk[...] += dk_part
+            dv[...] += dv_part
+    send_ref[:, rows : 2 * rows, :] = (dk[...] * scale).astype(BF16).reshape(n, rows, HD)
+    send_ref[:, 2 * rows : 3 * rows, :] = dv[...].astype(BF16).reshape(n, rows, HD)
+
+
+def unpack_kernel(tok_ref, dw_ref, q_ref, k_ref, v_ref, w_ref):
+    heads, three, _ = tok_ref.shape
+    rows = three // 3
+    for h in range(heads):
+        cols = slice(h * HD, (h + 1) * HD)
+        q_ref[:, cols] = tok_ref[h, 0:rows, :]
+        k_ref[:, cols] = tok_ref[h, rows : 2 * rows, :]
+        v_ref[:, cols] = tok_ref[h, 2 * rows : 3 * rows, :]
+        w_ref[:, cols] = dw_ref[h].astype(F32).T
+
+
+def ring_order(n):
+    return list(range(0, n, 2)) + list(range(n - 1, 0, -2))
+
+
+def gather_cotangents(d_out, n):
+    rows = d_out.shape[0]
+    ring = ring_order(n)
+    onward, swap = [], []
+    for pos, s in enumerate(ring):
+        onward.append((2 * s, 2 * ring[(pos + 1) % n]))
+        onward.append((2 * s + 1, 2 * ring[(pos - 1) % n] + 1))
+    for s in range(n):
+        swap += [(2 * s, 2 * s + 1), (2 * s + 1, 2 * s)]
+    axes = ("seq", "fsdp")
+    core = lax.axis_index("fsdp")
+    position = [0] * n
+    for pos, s in enumerate(ring):
+        position[s] = pos
+    here = jnp.asarray(position, jnp.int32)[lax.axis_index("seq")]
+    ring_now = jnp.asarray(ring, jnp.int32)
+    sign = 2 * core - 1
+    pieces, places = [d_out], [lax.axis_index("seq") * rows]
+    held = d_out
+    for hop in range(1, n // 2 + 1):
+        if hop == n // 2:
+            half = rows // 2
+            held = jnp.where(core == 0, held[:half], held[half:])
+        held = lax.ppermute(held, axes, onward)
+        other = lax.ppermute(held, axes, swap)
+        mine = ring_now[(here + sign * hop) % n] * rows
+        theirs = ring_now[(here - sign * hop) % n] * rows
+        if hop == n // 2:
+            mine = mine + core * half
+            theirs = theirs + (1 - core) * half
+        pieces += [held, other]
+        places += [mine, theirs]
+    return pieces, jnp.stack(places).astype(jnp.int32)
+
+
+def local(q_img, k_img, v_img, k_txt, v_txt, out_weight, d_out):
+    n = lax.axis_size("seq")
+    rows, width = q_img.shape
+    args = (q_img, k_img, v_img, k_txt, v_txt, out_weight, d_out)
+    if width // HD != n or lax.axis_size("fsdp") != 2 or n % 2 or rows % 32:
+        return local_general(*args)
+    depth = out_weight.shape[0]
+    image = n * rows
+    text = k_txt.shape[0]
+    total = image + text
+    chunk = 2 * rows
+    shape = jax.ShapeDtypeStruct
+    vmem = pl.BlockSpec(memory_space=pltpu.VMEM)
+
+    pieces, places = gather_cotangents(d_out, n)
+    tok_out, w_out = call(
+        pack_kernel,
+        [shape((n, 3 * rows, HD), BF16), shape((n, depth, HD), BF16)],
+        [q_img, k_img, v_img, out_weight],
+        moved=4 * (3 * rows + depth) * width,
+    )
+    tok_in = lax.all_to_all(tok_out, "seq", split_axis=0, concat_axis=0, tiled=True)
+    w_in = lax.all_to_all(w_out, "seq", split_axis=0, concat_axis=0, tiled=True)
+
+    me = lax.axis_index("seq").astype(jnp.int32)[None]
+    text_spec = pl.BlockSpec((text, HD), lambda i, me_ref: (0, me_ref[0]))
+    probs, out_t = call(
+        functools.partial(forward_kernel, chunk=chunk),
+        [shape((total, image), BF16), shape((HD, image), BF16)],
+        [me, tok_in, k_txt, v_txt],
+        specs=[vmem, text_spec, text_spec],
+        scratch=[pltpu.VMEM((total, HD), BF16), pltpu.VMEM((HD, total), BF16)],
+        scalars=1,
+        flops=4 * total * image * HD,
+        moved=4 * total * image,
+    )
+    grads, dw_out = call(
+        functools.partial(project_kernel, pieces=[p.shape[0] for p in pieces]),
+        [shape((image, HD), BF16), shape((n, HD, depth), BF16)],
+        [places, *pieces, w_in, out_t],
+        specs=[pl.BlockSpec(memory_space=pl.ANY)] * len(pieces) + [vmem, vmem],
+        scratch=[pltpu.VMEM((image, n * depth), BF16), pltpu.SemaphoreType.DMA((len(pieces),))],
+        scalars=1,
+        flops=4 * image * n * depth * HD,
+        moved=2 * image * n * depth,
+    )
+    dw_in = lax.all_to_all(dw_out, "seq", split_axis=0, concat_axis=0, tiled=True)
+    (grad_out,) = call(
+        functools.partial(backward_kernel, chunk=chunk),
+        [shape((n, 3 * rows, HD), BF16)],
+        [me, tok_in, k_txt, v_txt, probs, out_t, grads],
+        specs=[vmem, text_spec, text_spec, vmem, vmem, vmem],
+        scratch=[
+            pltpu.VMEM((HD, total), BF16),
+            pltpu.VMEM((total, HD), BF16),
+            pltpu.VMEM((image, HD), F32),
+            pltpu.VMEM((image, HD), F32),
+        ],
+        scalars=1,
+        flops=8 * total * image * HD,
+        moved=4 * total * image,
+    )
+    grad_in = lax.all_to_all(grad_out, "seq", split_axis=0, concat_axis=0, tiled=True)
+    return call(
+        unpack_kernel,
+        [shape((rows, width), BF16)] * 3 + [shape((depth, width), F32)],
+        [grad_in, dw_in],
+        moved=4 * 3 * rows * width + 6 * depth * width,
+    )
+
+
 def solution(mesh):
     in_specs = (
         P(("group", "seq"), "fsdp"),

time: 352 us -> 159 us (0.45)
  waiting for transfers between devices: 239 us -> 35.5 us
  local copies, waits for them, and re-layouts: 34.5 us -> 8.33 us
  blocking collectives: 29.2 us -> 54.9 us
  matrix products: 23.3 us -> 0 us
  Pallas kernels: 0 us -> 22.8 us
  starting transfers between devices: 3.64 us -> 24.2 us
  other arithmetic: 6.75 us -> 1.16 us
    unnamed x3 -> x0, waiting for transfers between devices: 115 us -> none
    all_gather x1 -> x0, waiting for transfers between devices: 101 us -> none  [local(): lax.all_gather(out_weight, 'seq', axis=0, tiled=True)]
    all_to_all x1 -> x2, blocking collectives: 29.2 us -> 54.9 us  [the longest x1 31.2 us: local(): lax.all_to_all(grad_out, 'seq', split_axis=0, concat_axis=0, tiled=True)]
    dot_general x14 -> x0, matrix products: 23.3 us -> none  [the longest x2 6.3 us: one_block(): jnp.dot(probs_low.T, grad_block, preferred_element_type=jnp.float32)]
    pallas_call x0 -> x5, Pallas kernels: none -> 22.8 us  [call(): pl.pallas_call(kernel, out_shape=outs, grid_spec=pltpu.PrefetchScalarGrid...]
    ppermute x0 -> x8, waiting for transfers between devices: none -> 16.8 us  [the longest x4 16.8 us: gather_cotangents(): held = lax.ppermute(held, axes, onward)]
    ppermute x0 -> x8, starting transfers between devices: none -> 15.2 us  [the longest x4 13.7 us: gather_cotangents(): held = lax.ppermute(held, axes, onward)]
    unnamed x11 -> x22, local copies, waits for them, and re-layouts: 17.5 us -> 6.94 us
  transfers between devices with their start and end apart: 3 -> 10, of which waited for: 3 -> 3; matrix products, arithmetic and copies ran while one was open for 2% -> 2% of each run, Pallas kernels for 0% -> 4%
where the time goes in v1:
time: 159 us; the launch traced here: 158 us
  blocking collectives  54.9 us (35%)
  waiting for transfers between devices  35.5 us (22%)
  starting transfers between devices  24.2 us (15%)
  Pallas kernels  22.8 us (14%)
  between operations  11.3 us (7%)
  local copies, waits for them, and re-layouts  8.33 us (5%)
    all_to_all x1, blocking collectives, local(): lax.all_to_all(grad_out, 'seq', split_axis=0, concat_axis=0, tiled=True)  31.2 us
    all_to_all x1, blocking collectives, local(): lax.all_to_all(dw_out, 'seq', split_axis=0, concat_axis=0, tiled=True)  23.7 us
    pallas_call x5, Pallas kernels, call(): pl.pallas_call(kernel, out_shape=outs, grid_spec=pltpu.PrefetchScalarGrid...  22.8 us
    all_to_all x1, waiting for transfers between devices, local(): lax.all_to_all(tok_out, 'seq', split_axis=0, concat_axis=0, tiled=True)  18.7 us
    ppermute x4, waiting for transfers between devices, gather_cotangents(): held = lax.ppermute(held, axes, onward)  16.8 us
    ppermute x4, starting transfers between devices, gather_cotangents(): held = lax.ppermute(held, axes, onward)  13.7 us
    unnamed x22, local copies, waits for them, and re-layouts  6.94 us
    all_to_all x1, starting transfers between devices, local(): lax.all_to_all(tok_out, 'seq', split_axis=0, concat_axis=0, tiled=True)  4.82 us
  transfers between devices with their start and end apart: 10, of which 3 were waited for; matrix products, arithmetic and copies ran while one was open for 2% of the time, Pallas kernels for 4%

profile of v1, /device:TPU:0, one launch (start us, length us, event | category | flops | bytes accessed | tf_op | source)
XLA Modules:
  0.0 158.2 jit_solution(15271368047118045207)
XLA Ops:
  0.6 0.0 copy-start.10
  0.6 0.0 copy-start.9
  0.7 0.0 copy-start
  0.7 0.0 copy-start.1
  0.7 3.1 %collective-permute-start = (bf16[128,3072]{1,0:T(8,128)(2,1)}, bf16[128,3072]{1,0:T(8,128)(2,1)}, u32[]{:S(2)}, u32[]{:S(2)}) collective-permute-start(bf16[128,3072]{1,0:T(8,128)(2,1)} %refs_0_.1), channel_id=1, source_target_pairs={{0,4},{1,3},{4,8},{5,1},{8,12},{9,5},{12,14},{13,9},{14,10},{15,13... | collective-permute-start | bytes 2359304 | tf_op jit(solution)/shard_map/ppermute | solution.py:298
  3.8 10.2 %collective-permute-done.refs_1_ = bf16[128,3072]{1,0:T(8,128)(2,1)} collective-permute-done((bf16[128,3072]{1,0:T(8,128)(2,1)}, bf16[128,3072]{1,0:T(8,128)(2,1)}, u32[]{:S(2)}, u32[]{:S(2)}) %collective-permute-start) | collective-permute-done | bytes 786464 | tf_op jit(solution)/shard_map/ppermute | solution.py:298
  14.0 2.1 %collective-permute-start.2 = (bf16[128,3072]{1,0:T(8,128)(2,1)}, bf16[128,3072]{1,0:T(8,128)(2,1)}, u32[]{:S(2)}, u32[]{:S(2)}) collective-permute-start(bf16[128,3072]{1,0:T(8,128)(2,1)} %collective-permute-done.refs_1_), channel_id=1, source_target_pairs={{0,4},{1,3},{4,8},{5,1},{8,12},{9,5},{12,14},{13,9},{14,10},{15,13... | collective-permute-start | bytes 2359304 | tf_op jit(solution)/shard_map/ppermute | solution.py:298
  16.1 1.1 copy-done.2
  17.2 0.9 copy-done.6
  18.1 0.9 copy-done.7
  19.1 0.9 copy-done.8
  20.0 0.3 shard_map.120
  20.3 0.0 copy-start.3
  20.3 0.9 copy-done.3
  21.3 0.9 copy-done.4
  22.2 4.8 %all-to-all-start = ((bf16[8,384,128]{2,1,0:T(8,128)(2,1)}), bf16[8,384,128]{2,1,0:T(8,128)(2,1)S(1)}, u32[]{:S(2)}, u32[]{:S(2)}) async-start(bf16[8,384,128]{2,1,0:T(8,128)(2,1)} %copy-done.4), calls=%async_computation | async-start | bytes 1572864 | tf_op jit(solution)/shard_map/all_to_all | solution.py:331
  27.0 0.0 collective-permute-done.2.refs_3_
  27.0 2.0 %collective-permute-start.4 = (bf16[128,3072]{1,0:T(8,128)(2,1)}, bf16[128,3072]{1,0:T(8,128)(2,1)}, u32[]{:S(2)}, u32[]{:S(2)}) collective-permute-start(bf16[128,3072]{1,0:T(8,128)(2,1)} %collective-permute-done.2.refs_3_), channel_id=1, source_target_pairs={{0,4},{1,3},{4,8},{5,1},{8,12},{9,5},{12,14},{13,9},{14,10},{15,13... | collective-permute-start | bytes 2359304 | tf_op jit(solution)/shard_map/ppermute | solution.py:298
  29.0 0.0 collective-permute-start.1
  29.0 0.5 collective-permute-start.3
  29.5 18.7 %all-to-all-done.tok_ref = bf16[8,384,128]{2,1,0:T(8,128)(2,1)S(1)} async-done(((bf16[8,384,128]{2,1,0:T(8,128)(2,1)}), bf16[8,384,128]{2,1,0:T(8,128)(2,1)S(1)}, u32[]{:S(2)}, u32[]{:S(2)}) %all-to-all-start) | async-done | bytes 786464 | tf_op jit(solution)/shard_map/all_to_all | solution.py:331
  48.2 4.2 %all-to-all-start.1 = ((bf16[8,384,128]{2,1,0:T(8,128)(2,1)}), bf16[8,384,128]{2,1,0:T(8,128)(2,1)}, u32[]{:S(2)}, u32[]{:S(2)}) async-start(bf16[8,384,128]{2,1,0:T(8,128)(2,1)} %copy-done.3), calls=%async_computation.1 | async-start | bytes 1572864 | tf_op jit(solution)/shard_map/all_to_all | solution.py:332
  52.4 0.0 collective-permute-done.4.refs_5_
  52.4 1.2 slice_select_fusion
  53.6 6.5 %collective-permute-start.6 = (bf16[64,3072]{1,0:T(8,128)(2,1)S(1)}, bf16[64,3072]{1,0:T(8,128)(2,1)S(1)}, u32[]{:S(2)}, u32[]{:S(2)}) collective-permute-start(bf16[64,3072]{1,0:T(8,128)(2,1)S(1)} %slice_select_fusion), channel_id=1, source_target_pairs={{0,4},{1,3},{4,8},{5,1},{8,12},{9,5},{12,14},{13,9},{14,10},{15,13... | collective-permute-start | bytes 1179656 | tf_op jit(solution)/shard_map/ppermute | solution.py:298
  60.1 0.0 collective-permute-start.5
  60.1 6.6 %collective-permute-done.6.refs_7_ = bf16[64,3072]{1,0:T(8,128)(2,1)S(1)} collective-permute-done((bf16[64,3072]{1,0:T(8,128)(2,1)S(1)}, bf16[64,3072]{1,0:T(8,128)(2,1)S(1)}, u32[]{:S(2)}, u32[]{:S(2)}) %collective-permute-start.6) | collective-permute-done | bytes 393248 | tf_op jit(solution)/shard_map/ppermute | solution.py:298
  66.7 0.9 collective-permute-start.7
  67.7 0.0 copy-done.10
  67.7 0.6 dynamic_slice.27
  73.6 0.0 copy-done.9
  73.6 0.7 fusion
  79.5 0.1 stack.21.place_ref
  79.6 0.0 copy-done
  79.6 0.0 copy-done.1
  79.6 6.3 %shard_map.121 = (bf16[1536,1024]{1,0:T(8,128)(2,1)}, bf16[128,1024]{1,0:T(8,128)(2,1)S(1)}) custom-call(s32[1]{0:T(128)} %bitcast.me_ref, bf16[8,384,128]{2,1,0:T(8,128)(2,1)S(1)} %all-to-all-done.tok_ref, bf16[512,1024]{1,0:T(8,128)(2,1)S(1)} %copy-done, bf16[512,1024]{1,0:T(8,128)(2,1)S(1)} %copy-done.1), custom_call_target="tpu_custom_call" | custom-call | flops 805306368 | bytes 6291456 | tf_op jit(solution)/shard_map/pallas_call | solution.py:147
  85.8 0.0 all-to-all-done.1.refs_9_
  85.8 0.0 collective-permute-done.1.refs_2_
  85.8 0.0 collective-permute-done.3.refs_4_
  85.9 0.0 collective-permute-done.5.refs_6_
  85.9 0.0 collective-permute-done.7.refs_8_
  85.9 0.0 copy-start.5
  85.9 1.1 copy-done.5
  87.0 9.1 %shard_map.122 = (bf16[1024,128]{1,0:T(8,128)(2,1)S(1)}, bf16[8,128,384]{2,1,0:T(8,128)(2,1)S(1)}) custom-call(s32[9]{0:T(128)S(1)} %stack.21.place_ref, bf16[128,3072]{1,0:T(8,128)(2,1)S(1)} %copy-done.5, bf16[128,3072]{1,0:T(8,128)(2,1)} %collective-permute-done.refs_1_, bf16[128,3072]{1,0:T(8,128)(2,1)} %collective-permute-done.1.refs_2_, ...), custom_call_target="tpu_custom_call" | custom-call | flops 1610612736 | bytes 6291456 | tf_op jit(solution)/shard_map/pallas_call | solution.py:147
  96.1 5.5 %shard_map.123 = bf16[8,384,128]{2,1,0:T(8,128)(2,1)S(1)} custom-call(s32[1]{0:T(128)} %bitcast.me_ref, bf16[8,384,128]{2,1,0:T(8,128)(2,1)S(1)} %all-to-all-done.tok_ref, bf16[512,1024]{1,0:T(8,128)(2,1)S(1)} %copy-done, bf16[512,1024]{1,0:T(8,128)(2,1)S(1)} %copy-done.1, bf16[1536,1024]{1,0:T(8,128)(2,1)} %get-tuple-element.11.probs_ref, ...), custom_call_target="tpu_custom_call" | custom-call | flops 1610612736 | bytes 6291456 | tf_op jit(solution)/shard_map/pallas_call | solution.py:147
  101.6 31.2 %all_to_all.20.tok_ref = bf16[8,384,128]{2,1,0:T(8,128)(2,1)S(1)} all-to-all(bf16[8,384,128]{2,1,0:T(8,128)(2,1)S(1)} %shard_map.123), channel_id=1, replica_groups=mesh['group'=2,'seq'=8,'fsdp'=2] {'seq'}, dimensions={0} | all-to-all | bytes 1572864 | tf_op jit(solution)/shard_map/all_to_all | solution.py:372
  132.8 23.7 %all_to_all.21.dw_ref = bf16[8,128,384]{2,1,0:T(8,128)(2,1)S(1)} all-to-all(bf16[8,128,384]{2,1,0:T(8,128)(2,1)S(1)} %get-tuple-element.15), channel_id=1, replica_groups=mesh['group'=2,'seq'=8,'fsdp'=2] {'seq'}, dimensions={0} | all-to-all | bytes 1572864 | tf_op jit(solution)/shard_map/all_to_all | solution.py:356
  156.5 1.7 %shard_map.124 = (bf16[128,1024]{1,0:T(8,128)(2,1)}, bf16[128,1024]{1,0:T(8,128)(2,1)}, bf16[128,1024]{1,0:T(8,128)(2,1)}, f32[384,1024]{1,0:T(8,128)}) custom-call(bf16[8,384,128]{2,1,0:T(8,128)(2,1)S(1)} %all_to_all.20.tok_ref, bf16[8,128,384]{2,1,0:T(8,128)(2,1)S(1)} %all_to_all.21.dw_ref), custom_call_target="tpu_custom_call" | custom-call | bytes 3932160 | tf_op jit(solution)/shard_map/pallas_call | solution.py:147
  (5 shorter events, 0.0 us)
Async XLA Ops:
  0.6 67.0 %copy-start.10 = (s32[8]{0:T(128)S(1)}, s32[8]{0:T(128)}, u32[]{:S(2)}) copy-start(s32[8]{0:T(128)} %constant.77.clone) | copy-start | bytes 100
  0.6 72.9 %copy-start.9 = (s32[8]{0:T(128)S(1)}, s32[8]{0:T(128)}, u32[]{:S(2)}) copy-start(s32[8]{0:T(128)} %constant.78.clone) | copy-start | bytes 100
  0.7 78.9 %copy-start = (bf16[512,1024]{1,0:T(8,128)(2,1)S(1)}, bf16[512,1024]{1,0:T(8,128)(2,1)}, u32[]{:S(2)}) copy-start(bf16[512,1024]{1,0:T(8,128)(2,1)} %kt_ref.3) | copy-start | bytes 3145732
  0.7 78.9 %copy-start.1 = (bf16[512,1024]{1,0:T(8,128)(2,1)S(1)}, bf16[512,1024]{1,0:T(8,128)(2,1)}, u32[]{:S(2)}) copy-start(bf16[512,1024]{1,0:T(8,128)(2,1)} %vt_ref.3) | copy-start | bytes 3145732
  0.7 13.3 %collective-permute-start = (bf16[128,3072]{1,0:T(8,128)(2,1)}, bf16[128,3072]{1,0:T(8,128)(2,1)}, u32[]{:S(2)}, u32[]{:S(2)}) collective-permute-start(bf16[128,3072]{1,0:T(8,128)(2,1)} %refs_0_.1), channel_id=1, source_target_pairs={{0,4},{1,3},{4,8},{5,1},{8,12},{9,5},{12,14},{13,9},{14,10},{15,13... | collective-permute-start | bytes 2359304 | tf_op jit(solution)/shard_map/ppermute | solution.py:298
  14.0 13.0 %collective-permute-start.2 = (bf16[128,3072]{1,0:T(8,128)(2,1)}, bf16[128,3072]{1,0:T(8,128)(2,1)}, u32[]{:S(2)}, u32[]{:S(2)}) collective-permute-start(bf16[128,3072]{1,0:T(8,128)(2,1)} %collective-permute-done.refs_1_), channel_id=1, source_target_pairs={{0,4},{1,3},{4,8},{5,1},{8,12},{9,5},{12,14},{13,9},{14,10},{15,13... | collective-permute-start | bytes 2359304 | tf_op jit(solution)/shard_map/ppermute | solution.py:298
  16.1 1.1 copy-start.2
  17.2 0.9 copy-start.6
  18.1 0.9 copy-start.7
  19.1 0.9 copy-start.8
  20.3 0.9 copy-start.3
  21.3 0.9 copy-start.4
  22.2 26.1 %all-to-all-start = ((bf16[8,384,128]{2,1,0:T(8,128)(2,1)}), bf16[8,384,128]{2,1,0:T(8,128)(2,1)S(1)}, u32[]{:S(2)}, u32[]{:S(2)}) async-start(bf16[8,384,128]{2,1,0:T(8,128)(2,1)} %copy-done.4), calls=%async_computation | async-start | bytes 1572864 | tf_op jit(solution)/shard_map/all_to_all | solution.py:331
  27.0 25.4 %collective-permute-start.4 = (bf16[128,3072]{1,0:T(8,128)(2,1)}, bf16[128,3072]{1,0:T(8,128)(2,1)}, u32[]{:S(2)}, u32[]{:S(2)}) collective-permute-start(bf16[128,3072]{1,0:T(8,128)(2,1)} %collective-permute-done.2.refs_3_), channel_id=1, source_target_pairs={{0,4},{1,3},{4,8},{5,1},{8,12},{9,5},{12,14},{13,9},{14,10},{15,13... | collective-permute-start | bytes 2359304 | tf_op jit(solution)/shard_map/ppermute | solution.py:298
  29.0 56.8 %collective-permute-start.1 = (bf16[128,3072]{1,0:T(8,128)(2,1)}, bf16[128,3072]{1,0:T(8,128)(2,1)}, u32[]{:S(2)}, u32[]{:S(2)}) collective-permute-start(bf16[128,3072]{1,0:T(8,128)(2,1)} %collective-permute-done.refs_1_), channel_id=1, source_target_pairs={{0,1},{1,0},{2,3},{3,2},{4,5},{5,4},{6,7},{7,6},{8,9},{9,8},{10,11... | collective-permute-start | bytes 2359304 | tf_op jit(solution)/shard_map/ppermute | solution.py:299
  29.0 56.8 %collective-permute-start.3 = (bf16[128,3072]{1,0:T(8,128)(2,1)}, bf16[128,3072]{1,0:T(8,128)(2,1)}, u32[]{:S(2)}, u32[]{:S(2)}) collective-permute-start(bf16[128,3072]{1,0:T(8,128)(2,1)} %collective-permute-done.2.refs_3_), channel_id=1, source_target_pairs={{0,1},{1,0},{2,3},{3,2},{4,5},{5,4},{6,7},{7,6},{8,9},{9,8},{10,11... | collective-permute-start | bytes 2359304 | tf_op jit(solution)/shard_map/ppermute | solution.py:299
  48.2 37.6 %all-to-all-start.1 = ((bf16[8,384,128]{2,1,0:T(8,128)(2,1)}), bf16[8,384,128]{2,1,0:T(8,128)(2,1)}, u32[]{:S(2)}, u32[]{:S(2)}) async-start(bf16[8,384,128]{2,1,0:T(8,128)(2,1)} %copy-done.3), calls=%async_computation.1 | async-start | bytes 1572864 | tf_op jit(solution)/shard_map/all_to_all | solution.py:332
  53.6 13.1 %collective-permute-start.6 = (bf16[64,3072]{1,0:T(8,128)(2,1)S(1)}, bf16[64,3072]{1,0:T(8,128)(2,1)S(1)}, u32[]{:S(2)}, u32[]{:S(2)}) collective-permute-start(bf16[64,3072]{1,0:T(8,128)(2,1)S(1)} %slice_select_fusion), channel_id=1, source_target_pairs={{0,4},{1,3},{4,8},{5,1},{8,12},{9,5},{12,14},{13,9},{14,10},{15,13... | collective-permute-start | bytes 1179656 | tf_op jit(solution)/shard_map/ppermute | solution.py:298
  60.1 25.7 %collective-permute-start.5 = (bf16[128,3072]{1,0:T(8,128)(2,1)}, bf16[128,3072]{1,0:T(8,128)(2,1)}, u32[]{:S(2)}, u32[]{:S(2)}) collective-permute-start(bf16[128,3072]{1,0:T(8,128)(2,1)} %collective-permute-done.4.refs_5_), channel_id=1, source_target_pairs={{0,1},{1,0},{2,3},{3,2},{4,5},{5,4},{6,7},{7,6},{8,9},{9,8},{10,11... | collective-permute-start | bytes 2359304 | tf_op jit(solution)/shard_map/ppermute | solution.py:299
  66.7 19.1 %collective-permute-start.7 = (bf16[64,3072]{1,0:T(8,128)(2,1)S(1)}, bf16[64,3072]{1,0:T(8,128)(2,1)}, u32[]{:S(2)}, u32[]{:S(2)}) collective-permute-start(bf16[64,3072]{1,0:T(8,128)(2,1)S(1)} %collective-permute-done.6.refs_7_), channel_id=1, source_target_pairs={{0,1},{1,0},{2,3},{3,2},{4,5},{5,4},{6,7},{7,6},{8,9},{9,8},{10,11... | collective-permute-start | bytes 1179656 | tf_op jit(solution)/shard_map/ppermute | solution.py:299
  85.9 1.1 copy-start.5

commit v2 on v1

--- a/solution.py
+++ b/solution.py
@@ -11,7 +11,7 @@
 HD = 128
 F32 = jnp.float32
 BF16 = jnp.bfloat16
-LIMIT = 48 * 1024 * 1024
+LIMIT = 60 * 1024 * 1024
 NT = (((1,), (1,)), ((), ()))
 
 
@@ -194,18 +194,48 @@
         ).astype(BF16)
 
 
-def project_kernel(place_ref, *refs, pieces):
-    blocks = refs[: len(pieces)]
-    w_ref, out_ref, grad_ref, dw_ref, cot, sems = refs[len(pieces) :]
-    n, depth, _ = w_ref.shape
+def ring_order(n):
+    return list(range(0, n, 2)) + list(range(n - 1, 0, -2))
+
+
+def ring_index(position, n):
+    position = lax.rem(position + n, n)
+    return jnp.where(position < n // 2, 2 * position, 2 * (n - position) - 1)
+
+
+def piece_places(n, rows):
+    me = lax.axis_index("seq")
+    core = lax.axis_index("fsdp")
+    here = jnp.where(lax.rem(me, 2) == 0, me // 2, n - 1 - me // 2)
+    sign = 2 * core - 1
+    places = [me * rows]
+    for hop in range(1, n // 2 + 1):
+        mine = ring_index(here + sign * hop, n) * rows
+        theirs = ring_index(here - sign * hop, n) * rows
+        if hop == n // 2:
+            mine = mine + core * (rows // 2)
+            theirs = theirs + (1 - core) * (rows // 2)
+        places += [mine, theirs]
+    return places
+
+
+def load_pieces(blocks, cot, sems, n):
+    places = piece_places(n, blocks[0].shape[0])
     copies = []
-    for i, rows in enumerate(pieces):
-        at = pl.multiple_of(place_ref[i], 16)
-        copies.append(pltpu.make_async_copy(blocks[i], cot.at[pl.ds(at, rows), :], sems.at[i]))
+    for i, block in enumerate(blocks):
+        rows = block.shape[0]
+        at = pl.ds(pl.multiple_of(places[i], 16), rows)
+        copies.append(pltpu.make_async_copy(block, cot.at[at, :], sems.at[i]))
     for copy in copies:
         copy.start()
     for copy in copies:
         copy.wait()
+
+
+def attn_grad_kernel(*refs):
+    *blocks, w_ref, grad_ref, cot, sems = refs
+    n, depth, _ = w_ref.shape
+    load_pieces(blocks, cot, sems, n)
     weight = w_ref[...].reshape(n * depth, HD)
     step = 256
 
@@ -213,6 +243,12 @@
     def _(i):
         at = pl.ds(pl.multiple_of(i * step, step), step)
         grad_ref[at, :] = jnp.dot(cot[at, :], weight, preferred_element_type=F32).astype(BF16)
+
+
+def weight_grad_kernel(*refs):
+    *blocks, out_ref, dw_ref, cot, sems = refs
+    n, _, depth = dw_ref.shape
+    load_pieces(blocks, cot, sems, n)
 
     @pl.loop(0, n)
     def _(i):
@@ -268,10 +304,6 @@
         w_ref[:, cols] = dw_ref[h].astype(F32).T
 
 
-def ring_order(n):
-    return list(range(0, n, 2)) + list(range(n - 1, 0, -2))
-
-
 def gather_cotangents(d_out, n):
     rows = d_out.shape[0]
     ring = ring_order(n)
@@ -279,32 +311,17 @@
     for pos, s in enumerate(ring):
         onward.append((2 * s, 2 * ring[(pos + 1) % n]))
         onward.append((2 * s + 1, 2 * ring[(pos - 1) % n] + 1))
-    for s in range(n):
         swap += [(2 * s, 2 * s + 1), (2 * s + 1, 2 * s)]
     axes = ("seq", "fsdp")
-    core = lax.axis_index("fsdp")
-    position = [0] * n
-    for pos, s in enumerate(ring):
-        position[s] = pos
-    here = jnp.asarray(position, jnp.int32)[lax.axis_index("seq")]
-    ring_now = jnp.asarray(ring, jnp.int32)
-    sign = 2 * core - 1
-    pieces, places = [d_out], [lax.axis_index("seq") * rows]
+    pieces = [d_out]
     held = d_out
     for hop in range(1, n // 2 + 1):
         if hop == n // 2:
             half = rows // 2
-            held = jnp.where(core == 0, held[:half], held[half:])
+            held = lax.dynamic_slice_in_dim(held, lax.axis_index("fsdp") * half, half, 0)
         held = lax.ppermute(held, axes, onward)
-        other = lax.ppermute(held, axes, swap)
-        mine = ring_now[(here + sign * hop) % n] * rows
-        theirs = ring_now[(here - sign * hop) % n] * rows
-        if hop == n // 2:
-            mine = mine + core * half
-            theirs = theirs + (1 - core) * half
-        pieces += [held, other]
-        places += [mine, theirs]
-    return pieces, jnp.stack(places).astype(jnp.int32)
+        pieces += [held, lax.ppermute(held, axes, swap)]
+    return pieces
 
 
 def local(q_img, k_img, v_img, k_txt, v_txt, out_weight, d_out):
@@ -321,7 +338,7 @@
     shape = jax.ShapeDtypeStruct
     vmem = pl.BlockSpec(memory_space=pltpu.VMEM)
 
-    pieces, places = gather_cotangents(d_out, n)
+    pieces = gather_cotangents(d_out, n)
     tok_out, w_out = call(
         pack_kernel,
         [shape((n, 3 * rows, HD), BF16), shape((n, depth, HD), BF16)],
@@ -343,14 +360,24 @@
         flops=4 * total * image * HD,
         moved=4 * total * image,
     )
-    grads, dw_out = call(
-        functools.partial(project_kernel, pieces=[p.shape[0] for p in pieces]),
-        [shape((image, HD), BF16), shape((n, HD, depth), BF16)],
-        [places, *pieces, w_in, out_t],
-        specs=[pl.BlockSpec(memory_space=pl.ANY)] * len(pieces) + [vmem, vmem],
-        scratch=[pltpu.VMEM((image, n * depth), BF16), pltpu.SemaphoreType.DMA((len(pieces),))],
-        scalars=1,
-        flops=4 * image * n * depth * HD,
+    anywhere = [pl.BlockSpec(memory_space=pl.ANY)] * len(pieces)
+    landing = [pltpu.VMEM((image, n * depth), BF16), pltpu.SemaphoreType.DMA((len(pieces),))]
+    (dw_out,) = call(
+        weight_grad_kernel,
+        [shape((n, HD, depth), BF16)],
+        [*pieces, out_t],
+        specs=anywhere + [vmem],
+        scratch=landing,
+        flops=2 * image * n * depth * HD,
+        moved=2 * image * n * depth,
+    )
+    (grads,) = call(
+        attn_grad_kernel,
+        [shape((image, HD), BF16)],
+        [*pieces, w_in],
+        specs=anywhere + [vmem],
+        scratch=landing,
+        flops=2 * image * n * depth * HD,
         moved=2 * image * n * depth,
     )
     dw_in = lax.all_to_all(dw_out, "seq", split_axis=0, concat_axis=0, tiled=True)
@@ -369,13 +396,14 @@
         flops=8 * total * image * HD,
         moved=4 * total * image,
     )
+    grad_out, dw_in = lax.optimization_barrier((grad_out, dw_in))
     grad_in = lax.all_to_all(grad_out, "seq", split_axis=0, concat_axis=0, tiled=True)
-    return call(
+    return tuple(call(
         unpack_kernel,
         [shape((rows, width), BF16)] * 3 + [shape((depth, width), F32)],
         [grad_in, dw_in],
         moved=4 * 3 * rows * width + 6 * depth * width,
-    )
+    ))
 
 
 def solution(mesh):

time: 159 us -> 141 us (0.89)
  blocking collectives: 54.9 us -> 24.1 us
  starting transfers between devices: 24.2 us -> 41.2 us
  Pallas kernels: 22.8 us -> 34.5 us
  between operations: 11.3 us -> 0.75 us
  local copies, waits for them, and re-layouts: 8.33 us -> 0.86 us
  waiting for transfers between devices: 35.5 us -> 38.9 us
    all_to_all x1 -> x0, blocking collectives: 23.7 us -> none  [local(): lax.all_to_all(dw_out, 'seq', split_axis=0, concat_axis=0, tiled=True)]
    pallas_call x5 -> x6, Pallas kernels: 22.8 us -> 34.5 us  [call(): pl.pallas_call(kernel, out_shape=outs, grid_spec=pltpu.PrefetchScalarGrid...]
    ppermute x4, starting transfers between devices: 13.7 us -> 24.3 us  [gather_cotangents(): held = lax.ppermute(held, axes, onward)]
    all_to_all x0 -> x1, starting transfers between devices: none -> 7.26 us  [local(): lax.all_to_all(dw_out, 'seq', split_axis=0, concat_axis=0, tiled=True)]
    all_to_all x1, blocking collectives: 31.2 us -> 24.1 us  [local(): lax.all_to_all(grad_out, 'seq', split_axis=0, concat_axis=0, tiled=True)]
    all_to_all x0 -> x1, waiting for transfers between devices: none -> 6.84 us  [local(): lax.all_to_all(dw_out, 'seq', split_axis=0, concat_axis=0, tiled=True)]
    all_to_all x1, waiting for transfers between devices: 18.7 us -> 12 us  [local(): lax.all_to_all(tok_out, 'seq', split_axis=0, concat_axis=0, tiled=True)]
    unnamed x22 -> x14, local copies, waits for them, and re-layouts: 6.94 us -> 0.84 us
  transfers between devices with their start and end apart: 10 -> 11, of which waited for: 3 -> 5; matrix products, arithmetic and copies ran while one was open for 2% -> 0% of each run, Pallas kernels for 4% -> 22%
where the time goes in v2:
time: 141 us; the launch traced here: 140 us
  starting transfers between devices  41.2 us (29%)
  waiting for transfers between devices  38.9 us (28%)
  Pallas kernels  34.5 us (24%)
  blocking collectives  24.1 us (17%)
    pallas_call x6, Pallas kernels, call(): pl.pallas_call(kernel, out_shape=outs, grid_spec=pltpu.PrefetchScalarGrid...  34.5 us
    ppermute x4, starting transfers between devices, gather_cotangents(): held = lax.ppermute(held, axes, onward)  24.3 us
    all_to_all x1, blocking collectives, local(): lax.all_to_all(grad_out, 'seq', split_axis=0, concat_axis=0, tiled=True)  24.1 us
    ppermute x4, waiting for transfers between devices, gather_cotangents(): held = lax.ppermute(held, axes, onward)  20.1 us
    all_to_all x1, waiting for transfers between devices, local(): lax.all_to_all(tok_out, 'seq', split_axis=0, concat_axis=0, tiled=True)  12 us
    all_to_all x1, starting transfers between devices, local(): lax.all_to_all(dw_out, 'seq', split_axis=0, concat_axis=0, tiled=True)  7.26 us
    all_to_all x1, waiting for transfers between devices, local(): lax.all_to_all(dw_out, 'seq', split_axis=0, concat_axis=0, tiled=True)  6.84 us
    all_to_all x1, starting transfers between devices, local(): lax.all_to_all(tok_out, 'seq', split_axis=0, concat_axis=0, tiled=True)  4.82 us
  transfers between devices with their start and end apart: 11, of which 5 were waited for; matrix products, arithmetic and copies ran while one was open for 0% of the time, Pallas kernels for 22%

profile of v2, /device:TPU:0, one launch (start us, length us, event | category | flops | bytes accessed | tf_op | source)
XLA Modules:
  0.0 140.2 jit_solution(11985653560528153144)
XLA Ops:
  0.6 3.1 %collective-permute-start = (bf16[128,3072]{1,0:T(8,128)(2,1)}, bf16[128,3072]{1,0:T(8,128)(2,1)S(1)}, u32[]{:S(2)}, u32[]{:S(2)}) collective-permute-start(bf16[128,3072]{1,0:T(8,128)(2,1)} %refs_0_.3), channel_id=1, source_target_pairs={{0,4},{1,3},{4,8},{5,1},{8,12},{9,5},{12,14},{13,9},{14,10},{15,13... | collective-permute-start | bytes 2359304 | tf_op jit(solution)/shard_map/ppermute | solution.py:322
  3.7 10.1 %collective-permute-done.refs_1_ = bf16[128,3072]{1,0:T(8,128)(2,1)S(1)} collective-permute-done((bf16[128,3072]{1,0:T(8,128)(2,1)}, bf16[128,3072]{1,0:T(8,128)(2,1)S(1)}, u32[]{:S(2)}, u32[]{:S(2)}) %collective-permute-start) | collective-permute-done | bytes 786464 | tf_op jit(solution)/shard_map/ppermute | solution.py:322
  13.8 0.0 copy-start.1
  13.8 2.1 %collective-permute-start.2 = (bf16[128,3072]{1,0:T(8,128)(2,1)S(1)}, bf16[128,3072]{1,0:T(8,128)(2,1)S(1)}, u32[]{:S(2)}, u32[]{:S(2)}) collective-permute-start(bf16[128,3072]{1,0:T(8,128)(2,1)S(1)} %collective-permute-done.refs_1_), channel_id=1, source_target_pairs={{0,4},{1,3},{4,8},{5,1},{8,12},{9,5},{12,14},{13,9},{14,10},{15,13... | collective-permute-start | bytes 2359304 | tf_op jit(solution)/shard_map/ppermute | solution.py:322
  15.9 2.8 %shard_map.102 = (bf16[8,384,128]{2,1,0:T(8,128)(2,1)}, bf16[8,384,128]{2,1,0:T(8,128)(2,1)}) custom-call(bf16[128,1024]{1,0:T(8,128)(2,1)} %q_ref.1, bf16[128,1024]{1,0:T(8,128)(2,1)} %k_ref.1, bf16[128,1024]{1,0:T(8,128)(2,1)} %v_ref.1, bf16[384,1024]{1,0:T(8,128)(2,1)} %w_ref.1), custom_call_target="tpu_custom_call" | custom-call | bytes 3145728 | tf_op jit(solution)/shard_map/pallas_call | solution.py:147
  18.7 4.8 %all-to-all-start = ((bf16[8,384,128]{2,1,0:T(8,128)(2,1)}), bf16[8,384,128]{2,1,0:T(8,128)(2,1)S(1)}, u32[]{:S(2)}, u32[]{:S(2)}) async-start(bf16[8,384,128]{2,1,0:T(8,128)(2,1)} %get-tuple-element.10), calls=%async_computation | async-start | bytes 1572864 | tf_op jit(solution)/shard_map/all_to_all | solution.py:348
  23.6 4.6 %collective-permute-done.2.refs_3_ = bf16[128,3072]{1,0:T(8,128)(2,1)S(1)} collective-permute-done((bf16[128,3072]{1,0:T(8,128)(2,1)S(1)}, bf16[128,3072]{1,0:T(8,128)(2,1)S(1)}, u32[]{:S(2)}, u32[]{:S(2)}) %collective-permute-start.2) | collective-permute-done | bytes 786464 | tf_op jit(solution)/shard_map/ppermute | solution.py:322
  28.2 0.0 copy-start.2
  28.2 4.6 %collective-permute-start.4 = (bf16[128,3072]{1,0:T(8,128)(2,1)S(1)}, bf16[128,3072]{1,0:T(8,128)(2,1)S(1)}, u32[]{:S(2)}, u32[]{:S(2)}) collective-permute-start(bf16[128,3072]{1,0:T(8,128)(2,1)S(1)} %collective-permute-done.2.refs_3_), channel_id=1, source_target_pairs={{0,4},{1,3},{4,8},{5,1},{8,12},{9,5},{12,14},{13,9},{14,10},{15,13... | collective-permute-start | bytes 2359304 | tf_op jit(solution)/shard_map/ppermute | solution.py:322
  32.7 12.0 %all-to-all-done.tok_ref = bf16[8,384,128]{2,1,0:T(8,128)(2,1)S(1)} async-done(((bf16[8,384,128]{2,1,0:T(8,128)(2,1)}), bf16[8,384,128]{2,1,0:T(8,128)(2,1)S(1)}, u32[]{:S(2)}, u32[]{:S(2)}) %all-to-all-start) | async-done | bytes 786464 | tf_op jit(solution)/shard_map/all_to_all | solution.py:348
  44.7 0.0 copy-start.5
  44.7 4.2 %all-to-all-start.1 = ((bf16[8,384,128]{2,1,0:T(8,128)(2,1)}), bf16[8,384,128]{2,1,0:T(8,128)(2,1)}, u32[]{:S(2)}, u32[]{:S(2)}) async-start(bf16[8,384,128]{2,1,0:T(8,128)(2,1)} %get-tuple-element.13), calls=%async_computation.1 | async-start | bytes 1572864 | tf_op jit(solution)/shard_map/all_to_all | solution.py:349
  49.0 0.0 copy-done.5
  49.0 0.1 collective-permute-start.1
  49.0 0.5 collective-permute-start.3
  49.5 0.0 collective-permute-done.4.refs_5_
  49.5 0.0 copy-start
  49.6 14.6 %collective-permute-start.6 = (bf16[64,3072]{1,0:T(8,128)(2,1)S(1)}, bf16[64,3072]{1,0:T(8,128)(2,1)S(1)}, u32[]{:S(2)}, u32[]{:S(2)}) collective-permute-start(bf16[64,3072]{1,0:T(8,128)(2,1)S(1)} %constant_dynamic-slice_fusion), channel_id=1, source_target_pairs={{0,4},{1,3},{4,8},{5,1},{8,12},{9,5},{12,14},{13,9},{14,10},{15,13... | collective-permute-start | bytes 1179656 | tf_op jit(solution)/shard_map/ppermute | solution.py:322
  64.2 0.0 collective-permute-start.5
  64.2 5.3 %collective-permute-done.6.refs_7_ = bf16[64,3072]{1,0:T(8,128)(2,1)S(1)} collective-permute-done((bf16[64,3072]{1,0:T(8,128)(2,1)S(1)}, bf16[64,3072]{1,0:T(8,128)(2,1)S(1)}, u32[]{:S(2)}, u32[]{:S(2)}) %collective-permute-start.6) | collective-permute-done | bytes 393248 | tf_op jit(solution)/shard_map/ppermute | solution.py:322
  69.5 0.0 copy-start.6
  69.5 0.0 collective-permute-start.7
  69.5 7.6 %shard_map.103 = (bf16[1536,1024]{1,0:T(8,128)(2,1)}, bf16[128,1024]{1,0:T(8,128)(2,1)}) custom-call(s32[1]{0:T(128)} %bitcast.me_ref, bf16[8,384,128]{2,1,0:T(8,128)(2,1)} %copy-done.5, bf16[512,1024]{1,0:T(8,128)(2,1)} %kt_ref.3, bf16[512,1024]{1,0:T(8,128)(2,1)} %vt_ref.3), custom_call_target="tpu_custom_call" | custom-call | flops 805306368 | bytes 6291456 | tf_op jit(solution)/shard_map/pallas_call | solution.py:147
  77.1 0.0 copy-done.1
  77.1 0.0 collective-permute-done.1.refs_2_
  77.1 0.0 copy-start.3
  77.1 0.0 collective-permute-done.3.refs_4_
  77.2 0.0 collective-permute-done.7.refs_8_
  77.2 0.0 collective-permute-done.5.refs_6_
  77.2 0.0 copy-done.2
  77.2 0.0 copy-done
  77.2 0.0 copy-done.6
  77.2 0.8 copy-done.3
  78.0 7.2 %shard_map.106 = bf16[8,128,384]{2,1,0:T(8,128)(2,1)} custom-call(bf16[128,3072]{1,0:T(8,128)(2,1)} %refs_0_.3, bf16[128,3072]{1,0:T(8,128)(2,1)} %copy-done.1, bf16[128,3072]{1,0:T(8,128)(2,1)} %copy-done.3, bf16[128,3072]{1,0:T(8,128)(2,1)} %copy-done.2, bf16[128,3072]{1,0:T(8,128)(2,1)} %collective-permute-done.3.refs_4_, bf16[128,3072]{1,0:T(8,128)(2,1)} %copy-done, ...), custom_call_target="tpu_custom_call" | custom-call | flops 805306368 | bytes 6291456 | tf_op jit(solution)/shard_map/pallas_call | solution.py:147
  85.2 0.0 all-to-all-done.1.refs_9_
  85.2 7.3 %all-to-all-start.2 = ((bf16[8,128,384]{2,1,0:T(8,128)(2,1)}), bf16[8,128,384]{2,1,0:T(8,128)(2,1)S(1)}, u32[]{:S(2)}, u32[]{:S(2)}) async-start(bf16[8,128,384]{2,1,0:T(8,128)(2,1)} %shard_map.106), calls=%async_computation.2 | async-start | bytes 1572864 | tf_op jit(solution)/shard_map/all_to_all | solution.py:383
  92.5 7.0 %shard_map.104.grad_ref = bf16[1024,128]{1,0:T(8,128)(2,1)} custom-call(bf16[128,3072]{1,0:T(8,128)(2,1)} %refs_0_.3, bf16[128,3072]{1,0:T(8,128)(2,1)} %copy-done.1, bf16[128,3072]{1,0:T(8,128)(2,1)} %copy-done.3, bf16[128,3072]{1,0:T(8,128)(2,1)} %copy-done.2, bf16[128,3072]{1,0:T(8,128)(2,1)} %collective-permute-done.3.refs_4_, ...), custom_call_target="tpu_custom_call" | custom-call | flops 805306368 | bytes 6291456 | tf_op jit(solution)/shard_map/pallas_call | solution.py:147
  99.5 6.8 %shard_map.105 = bf16[8,384,128]{2,1,0:T(8,128)(2,1)} custom-call(s32[1]{0:T(128)} %bitcast.me_ref, bf16[8,384,128]{2,1,0:T(8,128)(2,1)} %copy-done.5, bf16[512,1024]{1,0:T(8,128)(2,1)} %kt_ref.3, bf16[512,1024]{1,0:T(8,128)(2,1)} %vt_ref.3, bf16[1536,1024]{1,0:T(8,128)(2,1)} %get-tuple-element.11.probs_ref, ...), custom_call_target="tpu_custom_call" | custom-call | flops 1610612736 | bytes 6291456 | tf_op jit(solution)/shard_map/pallas_call | solution.py:147
  106.3 6.8 %all-to-all-done.2.dw_ref = bf16[8,128,384]{2,1,0:T(8,128)(2,1)S(1)} async-done(((bf16[8,128,384]{2,1,0:T(8,128)(2,1)}), bf16[8,128,384]{2,1,0:T(8,128)(2,1)S(1)}, u32[]{:S(2)}, u32[]{:S(2)}) %all-to-all-start.2) | async-done | bytes 786464 | tf_op jit(solution)/shard_map/all_to_all | solution.py:383
  113.1 0.0 copy-start.4
  113.1 24.1 %all_to_all.20.tok_ref = bf16[8,384,128]{2,1,0:T(8,128)(2,1)} all-to-all(bf16[8,384,128]{2,1,0:T(8,128)(2,1)} %shard_map.105), channel_id=1, replica_groups=mesh['group'=2,'seq'=8,'fsdp'=2] {'seq'}, dimensions={0} | all-to-all | bytes 1572864 | tf_op jit(solution)/shard_map/all_to_all | solution.py:400
  137.2 0.0 copy-done.4
  137.2 3.0 %shard_map.107 = (bf16[128,1024]{1,0:T(8,128)(2,1)}, bf16[128,1024]{1,0:T(8,128)(2,1)}, bf16[128,1024]{1,0:T(8,128)(2,1)}, f32[384,1024]{1,0:T(8,128)}) custom-call(bf16[8,384,128]{2,1,0:T(8,128)(2,1)} %all_to_all.20.tok_ref, bf16[8,128,384]{2,1,0:T(8,128)(2,1)} %copy-done.4), custom_call_target="tpu_custom_call" | custom-call | bytes 3932160 | tf_op jit(solution)/shard_map/pallas_call | solution.py:147
  (1 shorter events, 0.0 us)
Async XLA Ops:
  0.6 13.2 %collective-permute-start = (bf16[128,3072]{1,0:T(8,128)(2,1)}, bf16[128,3072]{1,0:T(8,128)(2,1)S(1)}, u32[]{:S(2)}, u32[]{:S(2)}) collective-permute-start(bf16[128,3072]{1,0:T(8,128)(2,1)} %refs_0_.3), channel_id=1, source_target_pairs={{0,4},{1,3},{4,8},{5,1},{8,12},{9,5},{12,14},{13,9},{14,10},{15,13... | collective-permute-start | bytes 2359304 | tf_op jit(solution)/shard_map/ppermute | solution.py:322
  13.8 63.3 %copy-start.1 = (bf16[128,3072]{1,0:T(8,128)(2,1)}, bf16[128,3072]{1,0:T(8,128)(2,1)S(1)}, u32[]{:S(2)}) copy-start(bf16[128,3072]{1,0:T(8,128)(2,1)S(1)} %collective-permute-done.refs_1_) | copy-start | bytes 2359300
  13.8 14.4 %collective-permute-start.2 = (bf16[128,3072]{1,0:T(8,128)(2,1)S(1)}, bf16[128,3072]{1,0:T(8,128)(2,1)S(1)}, u32[]{:S(2)}, u32[]{:S(2)}) collective-permute-start(bf16[128,3072]{1,0:T(8,128)(2,1)S(1)} %collective-permute-done.refs_1_), channel_id=1, source_target_pairs={{0,4},{1,3},{4,8},{5,1},{8,12},{9,5},{12,14},{13,9},{14,10},{15,13... | collective-permute-start | bytes 2359304 | tf_op jit(solution)/shard_map/ppermute | solution.py:322
  18.7 26.0 %all-to-all-start = ((bf16[8,384,128]{2,1,0:T(8,128)(2,1)}), bf16[8,384,128]{2,1,0:T(8,128)(2,1)S(1)}, u32[]{:S(2)}, u32[]{:S(2)}) async-start(bf16[8,384,128]{2,1,0:T(8,128)(2,1)} %get-tuple-element.10), calls=%async_computation | async-start | bytes 1572864 | tf_op jit(solution)/shard_map/all_to_all | solution.py:348
  28.2 49.0 %copy-start.2 = (bf16[128,3072]{1,0:T(8,128)(2,1)}, bf16[128,3072]{1,0:T(8,128)(2,1)S(1)}, u32[]{:S(2)}) copy-start(bf16[128,3072]{1,0:T(8,128)(2,1)S(1)} %collective-permute-done.2.refs_3_) | copy-start | bytes 2359300
  28.2 21.4 %collective-permute-start.4 = (bf16[128,3072]{1,0:T(8,128)(2,1)S(1)}, bf16[128,3072]{1,0:T(8,128)(2,1)S(1)}, u32[]{:S(2)}, u32[]{:S(2)}) collective-permute-start(bf16[128,3072]{1,0:T(8,128)(2,1)S(1)} %collective-permute-done.2.refs_3_), channel_id=1, source_target_pairs={{0,4},{1,3},{4,8},{5,1},{8,12},{9,5},{12,14},{13,9},{14,10},{15,13... | collective-permute-start | bytes 2359304 | tf_op jit(solution)/shard_map/ppermute | solution.py:322
  44.7 4.2 %copy-start.5 = (bf16[8,384,128]{2,1,0:T(8,128)(2,1)}, bf16[8,384,128]{2,1,0:T(8,128)(2,1)S(1)}, u32[]{:S(2)}) copy-start(bf16[8,384,128]{2,1,0:T(8,128)(2,1)S(1)} %all-to-all-done.tok_ref) | copy-start | bytes 2359300
  44.7 40.5 %all-to-all-start.1 = ((bf16[8,384,128]{2,1,0:T(8,128)(2,1)}), bf16[8,384,128]{2,1,0:T(8,128)(2,1)}, u32[]{:S(2)}, u32[]{:S(2)}) async-start(bf16[8,384,128]{2,1,0:T(8,128)(2,1)} %get-tuple-element.13), calls=%async_computation.1 | async-start | bytes 1572864 | tf_op jit(solution)/shard_map/all_to_all | solution.py:349
  49.0 28.2 %collective-permute-start.1 = (bf16[128,3072]{1,0:T(8,128)(2,1)S(1)}, bf16[128,3072]{1,0:T(8,128)(2,1)S(1)}, u32[]{:S(2)}, u32[]{:S(2)}) collective-permute-start(bf16[128,3072]{1,0:T(8,128)(2,1)S(1)} %collective-permute-done.refs_1_), channel_id=1, source_target_pairs={{0,1},{1,0},{4,5},{5,4},{8,9},{9,8},{12,13},{13,12},{14,15},{15,14... | collective-permute-start | bytes 2359304 | tf_op jit(solution)/shard_map/ppermute | solution.py:323
  49.0 28.1 %collective-permute-start.3 = (bf16[128,3072]{1,0:T(8,128)(2,1)S(1)}, bf16[128,3072]{1,0:T(8,128)(2,1)}, u32[]{:S(2)}, u32[]{:S(2)}) collective-permute-start(bf16[128,3072]{1,0:T(8,128)(2,1)S(1)} %collective-permute-done.2.refs_3_), channel_id=1, source_target_pairs={{0,1},{1,0},{4,5},{5,4},{8,9},{9,8},{12,13},{13,12},{14,15},{15,14... | collective-permute-start | bytes 2359304 | tf_op jit(solution)/shard_map/ppermute | solution.py:323
  49.5 27.6 %copy-start = (bf16[128,3072]{1,0:T(8,128)(2,1)}, bf16[128,3072]{1,0:T(8,128)(2,1)S(1)}, u32[]{:S(2)}) copy-start(bf16[128,3072]{1,0:T(8,128)(2,1)S(1)} %collective-permute-done.4.refs_5_) | copy-start | bytes 2359300
  49.6 19.9 %collective-permute-start.6 = (bf16[64,3072]{1,0:T(8,128)(2,1)S(1)}, bf16[64,3072]{1,0:T(8,128)(2,1)S(1)}, u32[]{:S(2)}, u32[]{:S(2)}) collective-permute-start(bf16[64,3072]{1,0:T(8,128)(2,1)S(1)} %constant_dynamic-slice_fusion), channel_id=1, source_target_pairs={{0,4},{1,3},{4,8},{5,1},{8,12},{9,5},{12,14},{13,9},{14,10},{15,13... | collective-permute-start | bytes 1179656 | tf_op jit(solution)/shard_map/ppermute | solution.py:322
  64.2 13.0 %collective-permute-start.5 = (bf16[128,3072]{1,0:T(8,128)(2,1)S(1)}, bf16[128,3072]{1,0:T(8,128)(2,1)}, u32[]{:S(2)}, u32[]{:S(2)}) collective-permute-start(bf16[128,3072]{1,0:T(8,128)(2,1)S(1)} %collective-permute-done.4.refs_5_), channel_id=1, source_target_pairs={{0,1},{1,0},{4,5},{5,4},{8,9},{9,8},{12,13},{13,12},{14,15},{15,14... | collective-permute-start | bytes 2359304 | tf_op jit(solution)/shard_map/ppermute | solution.py:323
  69.5 7.7 %copy-start.6 = (bf16[64,3072]{1,0:T(8,128)(2,1)}, bf16[64,3072]{1,0:T(8,128)(2,1)S(1)}, u32[]{:S(2)}) copy-start(bf16[64,3072]{1,0:T(8,128)(2,1)S(1)} %collective-permute-done.6.refs_7_) | copy-start | bytes 1179652
  69.5 7.7 %collective-permute-start.7 = (bf16[64,3072]{1,0:T(8,128)(2,1)S(1)}, bf16[64,3072]{1,0:T(8,128)(2,1)}, u32[]{:S(2)}, u32[]{:S(2)}) collective-permute-start(bf16[64,3072]{1,0:T(8,128)(2,1)S(1)} %collective-permute-done.6.refs_7_), channel_id=1, source_target_pairs={{0,1},{1,0},{4,5},{5,4},{8,9},{9,8},{12,13},{13,12},{14,15},{15,14... | collective-permute-start | bytes 1179656 | tf_op jit(solution)/shard_map/ppermute | solution.py:323
  77.1 0.9 copy-start.3
  85.2 27.9 %all-to-all-start.2 = ((bf16[8,128,384]{2,1,0:T(8,128)(2,1)}), bf16[8,128,384]{2,1,0:T(8,128)(2,1)S(1)}, u32[]{:S(2)}, u32[]{:S(2)}) async-start(bf16[8,128,384]{2,1,0:T(8,128)(2,1)} %shard_map.106), calls=%async_computation.2 | async-start | bytes 1572864 | tf_op jit(solution)/shard_map/all_to_all | solution.py:383
  113.1 24.1 %copy-start.4 = (bf16[8,128,384]{2,1,0:T(8,128)(2,1)}, bf16[8,128,384]{2,1,0:T(8,128)(2,1)S(1)}, u32[]{:S(2)}) copy-start(bf16[8,128,384]{2,1,0:T(8,128)(2,1)S(1)} %all-to-all-done.2.dw_ref) | copy-start | bytes 2359300

commit v3 on v1

--- a/solution.py
+++ b/solution.py
@@ -11,7 +11,7 @@
 HD = 128
 F32 = jnp.float32
 BF16 = jnp.bfloat16
-LIMIT = 48 * 1024 * 1024
+LIMIT = 60 * 1024 * 1024
 NT = (((1,), (1,)), ((), ()))
 
 
@@ -159,7 +159,13 @@
     )(*args)
 
 
-def pack_kernel(q_ref, k_ref, v_ref, w_ref, tok_ref, wt_ref):
+def halves():
+    each = lax.axis_size("seq") // 2
+    me = lax.axis_index("seq")
+    return me // each, lax.rem(me, each)
+
+
+def pack_kernel(q_ref, k_ref, v_ref, w_ref, tok_ref, *wt_refs):
     heads = tok_ref.shape[0]
     rows = q_ref.shape[0]
     for h in range(heads):
@@ -167,7 +173,13 @@
         tok_ref[h, 0:rows, :] = q_ref[:, cols]
         tok_ref[h, rows : 2 * rows, :] = k_ref[:, cols]
         tok_ref[h, 2 * rows : 3 * rows, :] = v_ref[:, cols]
-        wt_ref[h, :, :] = w_ref[:, cols]
+    half, place = halves()
+    each = heads // 2
+    for d, wt_ref in enumerate(wt_refs):
+        to = jnp.bitwise_xor(place, d)
+        for i, side in enumerate((half, 1 - half)):
+            at = pl.multiple_of((side * each + to) * HD, HD)
+            wt_ref[:, i * HD : (i + 1) * HD] = w_ref[:, pl.ds(at, HD)]
 
 
 def forward_kernel(me_ref, tok_ref, kt_ref, vt_ref, probs_ref, out_ref, keys, vals_t, *, chunk):
@@ -194,34 +206,71 @@
         ).astype(BF16)
 
 
-def project_kernel(place_ref, *refs, pieces):
-    blocks = refs[: len(pieces)]
-    w_ref, out_ref, grad_ref, dw_ref, cot, sems = refs[len(pieces) :]
-    n, depth, _ = w_ref.shape
+def load_cotangents(pieces, cot, sems):
+    half, place = halves()
+    core = lax.axis_index("fsdp")
+    each = len(pieces) // 2
+    rows = pieces[0].shape[0]
     copies = []
-    for i, rows in enumerate(pieces):
-        at = pl.multiple_of(place_ref[i], 16)
-        copies.append(pltpu.make_async_copy(blocks[i], cot.at[pl.ds(at, rows), :], sems.at[i]))
+    for i, piece in enumerate(pieces):
+        source = jnp.bitwise_xor(place, i % each)
+        shift = (core if i < each else 1 - core) * (rows // 2)
+        for j, side in enumerate((half, 1 - half)):
+            at = pl.multiple_of((side * each + source) * rows + shift, 16)
+            copies.append(
+                pltpu.make_async_copy(
+                    piece.at[pl.ds(j * (rows // 2), rows // 2), :],
+                    cot.at[pl.ds(at, rows // 2), :],
+                    sems.at[2 * i + j],
+                )
+            )
+    return copies
+
+
+def partial_kernel(*refs, count):
+    pieces, weights = refs[:count], refs[count : count + count // 2]
+    mine_ref, theirs_ref, cot, weight, sems, wsems = refs[count + count // 2 :]
+    _, place = halves()
+    depth = weights[0].shape[0]
+    copies = load_cotangents(pieces, cot, sems)
+    for d, block in enumerate(weights):
+        at = pl.multiple_of(jnp.bitwise_xor(place, d) * depth, 16)
+        copies.append(pltpu.make_async_copy(block, weight.at[pl.ds(at, depth), :], wsems.at[d]))
     for copy in copies:
         copy.start()
     for copy in copies:
         copy.wait()
-    weight = w_ref[...].reshape(n * depth, HD)
     step = 256
 
     @pl.loop(0, cot.shape[0] // step)
     def _(i):
         at = pl.ds(pl.multiple_of(i * step, step), step)
-        grad_ref[at, :] = jnp.dot(cot[at, :], weight, preferred_element_type=F32).astype(BF16)
-
-    @pl.loop(0, n)
-    def _(i):
-        cols = pl.ds(pl.multiple_of(i * depth, depth), depth)
-        dw_ref[i] = jnp.dot(out_ref[...], cot[:, cols], preferred_element_type=F32).astype(BF16)
+        part = jnp.dot(cot[at, :], weight[...], preferred_element_type=F32)
+        mine_ref[at, :] = part[:, :HD]
+        theirs_ref[at, :] = part[:, HD:].astype(BF16)
+
+
+def weight_grad_kernel(*refs, count):
+    pieces = refs[:count]
+    mine_ref, theirs_ref = refs[count : count + 2]
+    dw_refs = refs[count + 2 : count + 2 + count // 2]
+    cot, outs, sems = refs[count + 2 + count // 2 :]
+    copies = load_cotangents(pieces, cot, sems)
+    for copy in copies:
+        copy.start()
+    outs[0:HD, :] = mine_ref[...]
+    outs[HD : 2 * HD, :] = theirs_ref[...]
+    for copy in copies:
+        copy.wait()
+    _, place = halves()
+    for d, dw_ref in enumerate(dw_refs):
+        depth = dw_ref.shape[1]
+        at = pl.multiple_of(jnp.bitwise_xor(place, d) * depth, HD)
+        dw_ref[...] = jnp.dot(outs[...], cot[:, pl.ds(at, depth)], preferred_element_type=F32).astype(BF16)
 
 
 def backward_kernel(
-    me_ref, tok_ref, kt_ref, vt_ref, probs_ref, out_ref, grad_ref, send_ref, keys_t, vals, dk, dv, *, chunk
+    me_ref, tok_ref, kt_ref, vt_ref, probs_ref, out_ref, mine_ref, theirs_ref, send_ref, keys_t, vals, dk, dv, *, chunk
 ):
     n, three, _ = tok_ref.shape
     rows = three // 3
@@ -235,7 +284,7 @@
     per = chunk // rows
     for c in range(image // chunk):
         span = slice(c * chunk, (c + 1) * chunk)
-        grads = grad_ref[span, :]
+        grads = (mine_ref[span, :] + theirs_ref[span, :].astype(F32)).astype(BF16)
         queries = tok_ref[c * per : (c + 1) * per, 0:rows, :].reshape(chunk, HD)
         row_dot = jnp.sum(
             grads.astype(F32).T * out_ref[:, span].astype(F32), axis=0, keepdims=True
@@ -257,7 +306,8 @@
     send_ref[:, 2 * rows : 3 * rows, :] = dv[...].astype(BF16).reshape(n, rows, HD)
 
 
-def unpack_kernel(tok_ref, dw_ref, q_ref, k_ref, v_ref, w_ref):
+def unpack_kernel(tok_ref, *refs):
+    *dw_refs, q_ref, k_ref, v_ref, w_ref = refs
     heads, three, _ = tok_ref.shape
     rows = three // 3
     for h in range(heads):
@@ -265,53 +315,38 @@
         q_ref[:, cols] = tok_ref[h, 0:rows, :]
         k_ref[:, cols] = tok_ref[h, rows : 2 * rows, :]
         v_ref[:, cols] = tok_ref[h, 2 * rows : 3 * rows, :]
-        w_ref[:, cols] = dw_ref[h].astype(F32).T
-
-
-def ring_order(n):
-    return list(range(0, n, 2)) + list(range(n - 1, 0, -2))
+    half, place = halves()
+    each = heads // 2
+    for d, dw_ref in enumerate(dw_refs):
+        source = jnp.bitwise_xor(place, d)
+        for i, side in enumerate((half, 1 - half)):
+            at = pl.multiple_of((side * each + source) * HD, HD)
+            w_ref[:, pl.ds(at, HD)] = dw_ref[i * HD : (i + 1) * HD, :].astype(F32).T
+
+
+def exchange(array, distance=0, cores=False):
+    size = 2 * lax.axis_size("seq")
+    pairs = [(i, i ^ (2 * distance + int(cores))) for i in range(size)]
+    return lax.ppermute(array, ("seq", "fsdp"), pairs)
 
 
 def gather_cotangents(d_out, n):
-    rows = d_out.shape[0]
-    ring = ring_order(n)
-    onward, swap = [], []
-    for pos, s in enumerate(ring):
-        onward.append((2 * s, 2 * ring[(pos + 1) % n]))
-        onward.append((2 * s + 1, 2 * ring[(pos - 1) % n] + 1))
-    for s in range(n):
-        swap += [(2 * s, 2 * s + 1), (2 * s + 1, 2 * s)]
-    axes = ("seq", "fsdp")
-    core = lax.axis_index("fsdp")
-    position = [0] * n
-    for pos, s in enumerate(ring):
-        position[s] = pos
-    here = jnp.asarray(position, jnp.int32)[lax.axis_index("seq")]
-    ring_now = jnp.asarray(ring, jnp.int32)
-    sign = 2 * core - 1
-    pieces, places = [d_out], [lax.axis_index("seq") * rows]
-    held = d_out
-    for hop in range(1, n // 2 + 1):
-        if hop == n // 2:
-            half = rows // 2
-            held = jnp.where(core == 0, held[:half], held[half:])
-        held = lax.ppermute(held, axes, onward)
-        other = lax.ppermute(held, axes, swap)
-        mine = ring_now[(here + sign * hop) % n] * rows
-        theirs = ring_now[(here - sign * hop) % n] * rows
-        if hop == n // 2:
-            mine = mine + core * half
-            theirs = theirs + (1 - core) * half
-        pieces += [held, other]
-        places += [mine, theirs]
-    return pieces, jnp.stack(places).astype(jnp.int32)
+    rows, width = d_out.shape
+    part, columns = rows // 2, width // 2
+    half, _ = halves()
+    first = lax.axis_index("fsdp") * part
+    away = lax.dynamic_slice(d_out, (first, (1 - half) * columns), (part, columns))
+    kept = lax.dynamic_slice(d_out, (first, half * columns), (part, columns))
+    both = jnp.concatenate([kept, exchange(away, n // 2)], axis=0)
+    pieces = [both] + [exchange(both, d) for d in range(1, n // 2)]
+    return pieces + [exchange(piece, cores=True) for piece in pieces]
 
 
 def local(q_img, k_img, v_img, k_txt, v_txt, out_weight, d_out):
     n = lax.axis_size("seq")
     rows, width = q_img.shape
     args = (q_img, k_img, v_img, k_txt, v_txt, out_weight, d_out)
-    if width // HD != n or lax.axis_size("fsdp") != 2 or n % 2 or rows % 32:
+    if width // HD != n or lax.axis_size("fsdp") != 2 or n < 4 or n & (n - 1) or rows % 32:
         return local_general(*args)
     depth = out_weight.shape[0]
     image = n * rows
@@ -321,15 +356,16 @@
     shape = jax.ShapeDtypeStruct
     vmem = pl.BlockSpec(memory_space=pltpu.VMEM)
 
-    pieces, places = gather_cotangents(d_out, n)
-    tok_out, w_out = call(
+    pieces = gather_cotangents(d_out, n)
+    each = n // 2
+    tok_out, *w_out = call(
         pack_kernel,
-        [shape((n, 3 * rows, HD), BF16), shape((n, depth, HD), BF16)],
+        [shape((n, 3 * rows, HD), BF16)] + [shape((depth, 2 * HD), BF16)] * each,
         [q_img, k_img, v_img, out_weight],
         moved=4 * (3 * rows + depth) * width,
     )
     tok_in = lax.all_to_all(tok_out, "seq", split_axis=0, concat_axis=0, tiled=True)
-    w_in = lax.all_to_all(w_out, "seq", split_axis=0, concat_axis=0, tiled=True)
+    w_in = [w_out[0]] + [exchange(w_out[d], d) for d in range(1, each)]
 
     me = lax.axis_index("seq").astype(jnp.int32)[None]
     text_spec = pl.BlockSpec((text, HD), lambda i, me_ref: (0, me_ref[0]))
@@ -343,22 +379,30 @@
         flops=4 * total * image * HD,
         moved=4 * total * image,
     )
-    grads, dw_out = call(
-        functools.partial(project_kernel, pieces=[p.shape[0] for p in pieces]),
-        [shape((image, HD), BF16), shape((n, HD, depth), BF16)],
-        [places, *pieces, w_in, out_t],
-        specs=[pl.BlockSpec(memory_space=pl.ANY)] * len(pieces) + [vmem, vmem],
-        scratch=[pltpu.VMEM((image, n * depth), BF16), pltpu.SemaphoreType.DMA((len(pieces),))],
-        scalars=1,
-        flops=4 * image * n * depth * HD,
-        moved=2 * image * n * depth,
-    )
-    dw_in = lax.all_to_all(dw_out, "seq", split_axis=0, concat_axis=0, tiled=True)
+    count = len(pieces)
+    anywhere = [pl.BlockSpec(memory_space=pl.ANY)]
+    half_width = d_out.shape[1] // 2
+    mine, theirs = call(
+        functools.partial(partial_kernel, count=count),
+        [shape((image, HD), F32), shape((image, HD), BF16)],
+        [*pieces, *w_in],
+        specs=anywhere * (count + each),
+        scratch=[
+            pltpu.VMEM((image, half_width), BF16),
+            pltpu.VMEM((half_width, 2 * HD), BF16),
+            pltpu.SemaphoreType.DMA((2 * count,)),
+            pltpu.SemaphoreType.DMA((each,)),
+        ],
+        flops=4 * image * half_width * HD,
+        moved=2 * image * half_width,
+    )
+    theirs = exchange(theirs, each)
+    out_other = exchange(out_t, each)
     (grad_out,) = call(
         functools.partial(backward_kernel, chunk=chunk),
         [shape((n, 3 * rows, HD), BF16)],
-        [me, tok_in, k_txt, v_txt, probs, out_t, grads],
-        specs=[vmem, text_spec, text_spec, vmem, vmem, vmem],
+        [me, tok_in, k_txt, v_txt, probs, out_t, mine, theirs],
+        specs=[vmem, text_spec, text_spec] + [vmem] * 4,
         scratch=[
             pltpu.VMEM((HD, total), BF16),
             pltpu.VMEM((total, HD), BF16),
@@ -370,11 +414,28 @@
         moved=4 * total * image,
     )
     grad_in = lax.all_to_all(grad_out, "seq", split_axis=0, concat_axis=0, tiled=True)
-    return call(
-        unpack_kernel,
-        [shape((rows, width), BF16)] * 3 + [shape((depth, width), F32)],
-        [grad_in, dw_in],
-        moved=4 * 3 * rows * width + 6 * depth * width,
+    out_other, _ = lax.optimization_barrier((out_other, grad_out))
+    dw_out = call(
+        functools.partial(weight_grad_kernel, count=count),
+        [shape((2 * HD, depth), BF16)] * each,
+        [*pieces, out_t, out_other],
+        specs=anywhere * count + [vmem, vmem],
+        scratch=[
+            pltpu.VMEM((image, half_width), BF16),
+            pltpu.VMEM((2 * HD, image), BF16),
+            pltpu.SemaphoreType.DMA((2 * count,)),
+        ],
+        flops=4 * image * half_width * HD,
+        moved=2 * image * half_width,
+    )
+    dw_in = [dw_out[0]] + [exchange(dw_out[d], d) for d in range(1, each)]
+    return tuple(
+        call(
+            unpack_kernel,
+            [shape((rows, width), BF16)] * 3 + [shape((depth, width), F32)],
+            [grad_in, *dw_in],
+            moved=4 * 3 * rows * width + 6 * depth * width,
+        )
     )
 
 

time: 159 us -> 142 us (0.89)
  blocking collectives: 54.9 us -> 0 us
  waiting for transfers between devices: 35.5 us -> 69.2 us
  starting transfers between devices: 24.2 us -> 35.9 us
  between operations: 11.3 us -> 0.82 us
  Pallas kernels: 22.8 us -> 30.2 us
  local copies, waits for them, and re-layouts: 8.33 us -> 5.67 us
    all_to_all x2 -> x0, blocking collectives: 54.9 us -> none  [the longest x1 31.2 us: local(): lax.all_to_all(grad_out, 'seq', split_axis=0, concat_axis=0, tiled=True)]
    ppermute x8 -> x16, waiting for transfers between devices: 16.8 us -> 69.2 us  [exchange(): return lax.ppermute(array, ('seq', 'fsdp'), pairs)]
    all_to_all x1, waiting for transfers between devices: 18.7 us -> 0.01 us  [local(): lax.all_to_all(tok_out, 'seq', split_axis=0, concat_axis=0, tiled=True)]
    ppermute x8 -> x16, starting transfers between devices: 15.2 us -> 28.5 us  [exchange(): return lax.ppermute(array, ('seq', 'fsdp'), pairs)]
    pallas_call x5 -> x6, Pallas kernels: 22.8 us -> 30.2 us  [call(): pl.pallas_call(kernel, out_shape=outs, grid_spec=pltpu.PrefetchScalarGrid...]
    unnamed x22 -> x38, local copies, waits for them, and re-layouts: 6.94 us -> 4.62 us
  transfers between devices with their start and end apart: 10 -> 18, of which waited for: 3 -> 9; matrix products, arithmetic and copies ran while one was open for 2% -> 0% of each run, Pallas kernels for 4% -> 14%
where the time goes in v3:
time: 142 us
  waiting for transfers between devices  69.2 us (49%)
  starting transfers between devices  35.9 us (25%)
  Pallas kernels  30.2 us (21%)
  local copies, waits for them, and re-layouts  5.67 us (4%)
    ppermute x16, waiting for transfers between devices, exchange(): return lax.ppermute(array, ('seq', 'fsdp'), pairs)  69.2 us
    pallas_call x6, Pallas kernels, call(): pl.pallas_call(kernel, out_shape=outs, grid_spec=pltpu.PrefetchScalarGrid...  30.2 us
    ppermute x16, starting transfers between devices, exchange(): return lax.ppermute(array, ('seq', 'fsdp'), pairs)  28.5 us
    unnamed x38, local copies, waits for them, and re-layouts  4.62 us
    all_to_all x1, starting transfers between devices, local(): lax.all_to_all(tok_out, 'seq', split_axis=0, concat_axis=0, tiled=True)  3.81 us
    all_to_all x1, starting transfers between devices, local(): lax.all_to_all(grad_out, 'seq', split_axis=0, concat_axis=0, tiled=True)  3.55 us
  transfers between devices with their start and end apart: 18, of which 9 were waited for; matrix products, arithmetic and copies ran while one was open for 0% of the time, Pallas kernels for 14%

profile of v3, /device:TPU:0, one launch (start us, length us, event | category | flops | bytes accessed | tf_op | source)
XLA Modules:
  0.0 141.8 jit_solution(2234743453329742430)
XLA Ops:
  0.7 1.1 fusion
  1.7 4.1 %collective-permute-start = (bf16[64,1536]{1,0:T(8,128)(2,1)S(1)}, bf16[64,1536]{1,0:T(8,128)(2,1)S(1)}, u32[]{:S(2)}, u32[]{:S(2)}) collective-permute-start(bf16[64,1536]{1,0:T(8,128)(2,1)S(1)} %get-tuple-element.33), channel_id=1, source_target_pairs={{0,8},{1,9},{2,10},{3,11},{4,12},{5,13},{6,14},{7,15},{8,0},{9,1},... | collective-permute-start | bytes 589832 | tf_op jit(solution)/shard_map/ppermute | solution.py:330
  5.8 2.8 %shard_map.102 = (bf16[8,384,128]{2,1,0:T(8,128)(2,1)}, bf16[384,256]{1,0:T(8,128)(2,1)}, bf16[384,256]{1,0:T(8,128)(2,1)}, bf16[384,256]{1,0:T(8,128)(2,1)}, bf16[384,256]{1,0:T(8,128)(2,1)}) custom-call(bf16[128,1024]{1,0:T(8,128)(2,1)} %q_ref.1, bf16[128,1024]{1,0:T(8,128)(2,1)} %k_ref.1, bf16[128,1024]{1,0:T(8,128)(2,1)} %v_ref.1, bf16[384,1024]{1,0:T(8,128)(2,1)} %w_ref.1), custom_call_target="tpu_custom_call" | custom-call | bytes 3145728 | tf_op jit(solution)/shard_map/pallas_call | solution.py:147
  8.6 3.8 %all-to-all-start = ((bf16[8,384,128]{2,1,0:T(8,128)(2,1)}), bf16[8,384,128]{2,1,0:T(8,128)(2,1)S(1)}, u32[]{:S(2)}, u32[]{:S(2)}) async-start(bf16[8,384,128]{2,1,0:T(8,128)(2,1)} %get-tuple-element.18), calls=%async_computation | async-start | bytes 1572864 | tf_op jit(solution)/shard_map/all_to_all | solution.py:367
  12.5 2.5 %collective-permute-done = bf16[64,1536]{1,0:T(8,128)(2,1)S(1)} collective-permute-done((bf16[64,1536]{1,0:T(8,128)(2,1)S(1)}, bf16[64,1536]{1,0:T(8,128)(2,1)S(1)}, u32[]{:S(2)}, u32[]{:S(2)}) %collective-permute-start) | collective-permute-done | bytes 196640 | tf_op jit(solution)/shard_map/ppermute | solution.py:330
  15.0 6.9 %collective-permute-start.3 = (bf16[128,1536]{1,0:T(8,128)(2,1)S(1)}, bf16[128,1536]{1,0:T(8,128)(2,1)S(1)}, u32[]{:S(2)}, u32[]{:S(2)}) collective-permute-start(bf16[128,1536]{1,0:T(8,128)(2,1)S(1)} %pad_maximum_fusion.refs_0_), channel_id=1, source_target_pairs={{0,6},{1,7},{2,4},{3,5},{4,2},{5,3},{6,0},{7,1},{8,14},{9,15},{10,... | collective-permute-start | bytes 1179656 | tf_op jit(solution)/shard_map/ppermute | solution.py:330
  21.9 0.0 collective-permute-start.2
  21.9 0.7 collective-permute-start.1
  22.6 1.4 collective-permute-start.8
  24.0 2.0 %collective-permute-start.9 = (bf16[384,256]{1,0:T(8,128)(2,1)}, bf16[384,256]{1,0:T(8,128)(2,1)S(1)}, u32[]{:S(2)}, u32[]{:S(2)}) collective-permute-start(bf16[384,256]{1,0:T(8,128)(2,1)} %get-tuple-element.23), channel_id=1, source_target_pairs={{0,4},{1,5},{2,6},{3,7},{4,0},{5,1},{6,2},{7,3},{8,12},{9,13},{10,... | collective-permute-start | bytes 589832 | tf_op jit(solution)/shard_map/ppermute | solution.py:330
  26.0 20.8 %collective-permute-done.8.refs_9_ = bf16[384,256]{1,0:T(8,128)(2,1)S(1)} collective-permute-done((bf16[384,256]{1,0:T(8,128)(2,1)}, bf16[384,256]{1,0:T(8,128)(2,1)S(1)}, u32[]{:S(2)}, u32[]{:S(2)}) %collective-permute-start.8) | collective-permute-done | bytes 196640 | tf_op jit(solution)/shard_map/ppermute | solution.py:330
  46.8 0.0 collective-permute-start.4
  46.8 0.0 collective-permute-done.3.refs_3_
  46.8 0.5 collective-permute-start.7
  47.3 0.0 collective-permute-done.2.refs_2_
  47.3 0.1 collective-permute-start.6
  47.4 0.0 collective-permute-done.1.refs_1_
  47.4 0.4 collective-permute-start.5
  47.8 0.9 collective-permute-done.9.refs_10_
  48.7 1.8 %collective-permute-start.10 = (bf16[384,256]{1,0:T(8,128)(2,1)}, bf16[384,256]{1,0:T(8,128)(2,1)S(1)}, u32[]{:S(2)}, u32[]{:S(2)}) collective-permute-start(bf16[384,256]{1,0:T(8,128)(2,1)} %get-tuple-element.24), channel_id=1, source_target_pairs={{0,6},{1,7},{2,4},{3,5},{4,2},{5,3},{6,0},{7,1},{8,14},{9,15},{10,... | collective-permute-start | bytes 589832 | tf_op jit(solution)/shard_map/ppermute | solution.py:330
  50.5 5.4 %collective-permute-done.10.refs_11_ = bf16[384,256]{1,0:T(8,128)(2,1)S(1)} collective-permute-done((bf16[384,256]{1,0:T(8,128)(2,1)}, bf16[384,256]{1,0:T(8,128)(2,1)S(1)}, u32[]{:S(2)}, u32[]{:S(2)}) %collective-permute-start.10) | collective-permute-done | bytes 196640 | tf_op jit(solution)/shard_map/ppermute | solution.py:330
  55.9 0.0 collective-permute-done.5.refs_5_
  56.0 0.6 copy-done.18
  56.6 0.1 copy-done.6
  56.7 0.1 copy-done.7
  56.8 0.1 copy-done.8
  56.9 0.4 copy-done.9
  57.3 4.7 %shard_map.104 = (f32[1024,128]{1,0:T(8,128)}, bf16[1024,128]{1,0:T(8,128)(2,1)}) custom-call(bf16[128,1536]{1,0:T(8,128)(2,1)} %copy-done, bf16[128,1536]{1,0:T(8,128)(2,1)} %copy-done.5, bf16[128,1536]{1,0:T(8,128)(2,1)} %copy-done.4, bf16[128,1536]{1,0:T(8,128)(2,1)} %copy-done.3, bf16[128,1536]{1,0:T(8,128)(2,1)} %copy-done.6, ...), custom_call_target="tpu_custom_call" | custom-call | flops 805306368 | bytes 3145728 | tf_op jit(solution)/shard_map/pallas_call | solution.py:147
  62.0 4.3 %collective-permute-start.11 = (bf16[1024,128]{1,0:T(8,128)(2,1)}, bf16[1024,128]{1,0:T(8,128)(2,1)S(1)}, u32[]{:S(2)}, u32[]{:S(2)}) collective-permute-start(bf16[1024,128]{1,0:T(8,128)(2,1)} %get-tuple-element.26), channel_id=1, source_target_pairs={{0,8},{1,9},{2,10},{3,11},{4,12},{5,13},{6,14},{7,15},{8,0},{9,1},... | collective-permute-start | bytes 786440 | tf_op jit(solution)/shard_map/ppermute | solution.py:330
  66.3 0.0 all-to-all-done.tok_ref
  66.3 0.9 copy-done.2
  67.2 7.5 %shard_map.103 = (bf16[1536,1024]{1,0:T(8,128)(2,1)}, bf16[128,1024]{1,0:T(8,128)(2,1)}) custom-call(s32[1]{0:T(128)} %bitcast.me_ref, bf16[8,384,128]{2,1,0:T(8,128)(2,1)} %copy-done.2, bf16[512,1024]{1,0:T(8,128)(2,1)} %kt_ref.3, bf16[512,1024]{1,0:T(8,128)(2,1)} %vt_ref.3), custom_call_target="tpu_custom_call" | custom-call | flops 805306368 | bytes 6291456 | tf_op jit(solution)/shard_map/pallas_call | solution.py:147
  74.7 3.1 %collective-permute-done.11.theirs_ref = bf16[1024,128]{1,0:T(8,128)(2,1)S(1)} collective-permute-done((bf16[1024,128]{1,0:T(8,128)(2,1)}, bf16[1024,128]{1,0:T(8,128)(2,1)S(1)}, u32[]{:S(2)}, u32[]{:S(2)}) %collective-permute-start.11) | collective-permute-done | bytes 262176 | tf_op jit(solution)/shard_map/ppermute | solution.py:330
  77.9 0.7 copy-done.12
  78.6 6.9 %shard_map.105 = bf16[8,384,128]{2,1,0:T(8,128)(2,1)} custom-call(s32[1]{0:T(128)} %bitcast.me_ref, bf16[8,384,128]{2,1,0:T(8,128)(2,1)} %copy-done.2, bf16[512,1024]{1,0:T(8,128)(2,1)} %kt_ref.3, bf16[512,1024]{1,0:T(8,128)(2,1)} %vt_ref.3, bf16[1536,1024]{1,0:T(8,128)(2,1)} %get-tuple-element.19.probs_ref, ...), custom_call_target="tpu_custom_call" | custom-call | flops 1610612736 | bytes 6291456 | tf_op jit(solution)/shard_map/pallas_call | solution.py:147
  85.5 3.5 %all-to-all-start.1 = ((bf16[8,384,128]{2,1,0:T(8,128)(2,1)}), bf16[8,384,128]{2,1,0:T(8,128)(2,1)S(1)}, u32[]{:S(2)}, u32[]{:S(2)}) async-start(bf16[8,384,128]{2,1,0:T(8,128)(2,1)} %shard_map.105), calls=%async_computation.1 | async-start | bytes 1572864 | tf_op jit(solution)/shard_map/all_to_all | solution.py:416
  89.1 2.8 %collective-permute-start.12 = (bf16[128,1024]{1,0:T(8,128)(2,1)S(1)}, bf16[128,1024]{1,0:T(8,128)(2,1)S(1)}, u32[]{:S(2)}, u32[]{:S(2)}) collective-permute-start(bf16[128,1024]{1,0:T(8,128)(2,1)S(1)} %copy-done.10), channel_id=1, source_target_pairs={{0,8},{1,9},{2,10},{3,11},{4,12},{5,13},{6,14},{7,15},{8,0},{9,1},... | collective-permute-start | bytes 786440 | tf_op jit(solution)/shard_map/ppermute | solution.py:330
  91.9 28.6 %collective-permute-done.12.refs_9_ = bf16[128,1024]{1,0:T(8,128)(2,1)S(1)} collective-permute-done((bf16[128,1024]{1,0:T(8,128)(2,1)S(1)}, bf16[128,1024]{1,0:T(8,128)(2,1)S(1)}, u32[]{:S(2)}, u32[]{:S(2)}) %collective-permute-start.12) | collective-permute-done | bytes 262176 | tf_op jit(solution)/shard_map/ppermute | solution.py:330
  120.5 0.7 copy-done.11
  121.2 5.1 %shard_map.106 = (bf16[256,384]{1,0:T(8,128)(2,1)}, bf16[256,384]{1,0:T(8,128)(2,1)}, bf16[256,384]{1,0:T(8,128)(2,1)}, bf16[256,384]{1,0:T(8,128)(2,1)}) custom-call(bf16[128,1536]{1,0:T(8,128)(2,1)} %copy-done, bf16[128,1536]{1,0:T(8,128)(2,1)} %copy-done.5, bf16[128,1536]{1,0:T(8,128)(2,1)} %copy-done.4, bf16[128,1536]{1,0:T(8,128)(2,1)} %copy-done.3, ...), custom_call_target="tpu_custom_call" | custom-call | flops 805306368 | bytes 3145728 | tf_op jit(solution)/shard_map/pallas_call | solution.py:147
  126.3 1.4 %collective-permute-start.13 = (bf16[256,384]{1,0:T(8,128)(2,1)}, bf16[256,384]{1,0:T(8,128)(2,1)S(1)}, u32[]{:S(2)}, u32[]{:S(2)}) collective-permute-start(bf16[256,384]{1,0:T(8,128)(2,1)} %get-tuple-element.29), channel_id=1, source_target_pairs={{0,2},{1,3},{2,0},{3,1},{4,6},{5,7},{6,4},{7,5},{8,10},{9,11},{10,... | collective-permute-start | bytes 589832 | tf_op jit(solution)/shard_map/ppermute | solution.py:330
  127.8 2.1 %collective-permute-start.15 = (bf16[256,384]{1,0:T(8,128)(2,1)}, bf16[256,384]{1,0:T(8,128)(2,1)S(1)}, u32[]{:S(2)}, u32[]{:S(2)}) collective-permute-start(bf16[256,384]{1,0:T(8,128)(2,1)} %get-tuple-element.31), channel_id=1, source_target_pairs={{0,6},{1,7},{2,4},{3,5},{4,2},{5,3},{6,0},{7,1},{8,14},{9,15},{10,... | collective-permute-start | bytes 589832 | tf_op jit(solution)/shard_map/ppermute | solution.py:330
  129.9 3.7 %collective-permute-done.13.refs_1_ = bf16[256,384]{1,0:T(8,128)(2,1)S(1)} collective-permute-done((bf16[256,384]{1,0:T(8,128)(2,1)}, bf16[256,384]{1,0:T(8,128)(2,1)S(1)}, u32[]{:S(2)}, u32[]{:S(2)}) %collective-permute-start.13) | collective-permute-done | bytes 196640 | tf_op jit(solution)/shard_map/ppermute | solution.py:330
  133.5 2.1 %collective-permute-done.14.refs_2_ = bf16[256,384]{1,0:T(8,128)(2,1)S(1)} collective-permute-done((bf16[256,384]{1,0:T(8,128)(2,1)}, bf16[256,384]{1,0:T(8,128)(2,1)S(1)}, u32[]{:S(2)}, u32[]{:S(2)}) %collective-permute-start.14) | collective-permute-done | bytes 196640 | tf_op jit(solution)/shard_map/ppermute | solution.py:330
  135.7 2.0 %collective-permute-done.15.refs_3_ = bf16[256,384]{1,0:T(8,128)(2,1)S(1)} collective-permute-done((bf16[256,384]{1,0:T(8,128)(2,1)}, bf16[256,384]{1,0:T(8,128)(2,1)S(1)}, u32[]{:S(2)}, u32[]{:S(2)}) %collective-permute-start.15) | collective-permute-done | bytes 196640 | tf_op jit(solution)/shard_map/ppermute | solution.py:330
  137.7 0.7 copy-done.15
  138.4 0.3 copy-done.1
  138.7 3.1 %shard_map.107 = (bf16[128,1024]{1,0:T(8,128)(2,1)}, bf16[128,1024]{1,0:T(8,128)(2,1)}, bf16[128,1024]{1,0:T(8,128)(2,1)}, f32[384,1024]{1,0:T(8,128)}) custom-call(bf16[8,384,128]{2,1,0:T(8,128)(2,1)} %copy-done.1, bf16[256,384]{1,0:T(8,128)(2,1)} %get-tuple-element.28.refs_0_, bf16[256,384]{1,0:T(8,128)(2,1)} %copy-done.13, bf16[256,384]{1,0:T(8,128)(2,1)} %copy-done.14, ...), custom_call_target="tpu_custom_call" | custom-call | bytes 3932160 | tf_op jit(solution)/shard_map/pallas_call | solution.py:147
  (34 shorter events, 0.1 us)
Async XLA Ops:
  1.7 13.3 %collective-permute-start = (bf16[64,1536]{1,0:T(8,128)(2,1)S(1)}, bf16[64,1536]{1,0:T(8,128)(2,1)S(1)}, u32[]{:S(2)}, u32[]{:S(2)}) collective-permute-start(bf16[64,1536]{1,0:T(8,128)(2,1)S(1)} %get-tuple-element.33), channel_id=1, source_target_pairs={{0,8},{1,9},{2,10},{3,11},{4,12},{5,13},{6,14},{7,15},{8,0},{9,1},... | collective-permute-start | bytes 589832 | tf_op jit(solution)/shard_map/ppermute | solution.py:330
  8.6 57.7 %all-to-all-start = ((bf16[8,384,128]{2,1,0:T(8,128)(2,1)}), bf16[8,384,128]{2,1,0:T(8,128)(2,1)S(1)}, u32[]{:S(2)}, u32[]{:S(2)}) async-start(bf16[8,384,128]{2,1,0:T(8,128)(2,1)} %get-tuple-element.18), calls=%async_computation | async-start | bytes 1572864 | tf_op jit(solution)/shard_map/all_to_all | solution.py:367
  15.0 41.5 %copy-start = (bf16[128,1536]{1,0:T(8,128)(2,1)}, bf16[128,1536]{1,0:T(8,128)(2,1)S(1)}, u32[]{:S(2)}) copy-start(bf16[128,1536]{1,0:T(8,128)(2,1)S(1)} %pad_maximum_fusion.refs_0_) | copy-start | bytes 1179652
  15.0 31.8 %collective-permute-start.3 = (bf16[128,1536]{1,0:T(8,128)(2,1)S(1)}, bf16[128,1536]{1,0:T(8,128)(2,1)S(1)}, u32[]{:S(2)}, u32[]{:S(2)}) collective-permute-start(bf16[128,1536]{1,0:T(8,128)(2,1)S(1)} %pad_maximum_fusion.refs_0_), channel_id=1, source_target_pairs={{0,6},{1,7},{2,4},{3,5},{4,2},{5,3},{6,0},{7,1},{8,14},{9,15},{10,... | collective-permute-start | bytes 1179656 | tf_op jit(solution)/shard_map/ppermute | solution.py:330
  21.9 25.4 %collective-permute-start.2 = (bf16[128,1536]{1,0:T(8,128)(2,1)S(1)}, bf16[128,1536]{1,0:T(8,128)(2,1)S(1)}, u32[]{:S(2)}, u32[]{:S(2)}) collective-permute-start(bf16[128,1536]{1,0:T(8,128)(2,1)S(1)} %pad_maximum_fusion.refs_0_), channel_id=1, source_target_pairs={{0,4},{1,5},{2,6},{3,7},{4,0},{5,1},{6,2},{7,3},{8,12},{9,13},{10,... | collective-permute-start | bytes 1179656 | tf_op jit(solution)/shard_map/ppermute | solution.py:330
  21.9 25.4 %collective-permute-start.1 = (bf16[128,1536]{1,0:T(8,128)(2,1)S(1)}, bf16[128,1536]{1,0:T(8,128)(2,1)S(1)}, u32[]{:S(2)}, u32[]{:S(2)}) collective-permute-start(bf16[128,1536]{1,0:T(8,128)(2,1)S(1)} %pad_maximum_fusion.refs_0_), channel_id=1, source_target_pairs={{0,2},{1,3},{2,0},{3,1},{4,6},{5,7},{6,4},{7,5},{8,10},{9,11},{10,... | collective-permute-start | bytes 1179656 | tf_op jit(solution)/shard_map/ppermute | solution.py:330
  22.6 24.2 %collective-permute-start.8 = (bf16[384,256]{1,0:T(8,128)(2,1)}, bf16[384,256]{1,0:T(8,128)(2,1)S(1)}, u32[]{:S(2)}, u32[]{:S(2)}) collective-permute-start(bf16[384,256]{1,0:T(8,128)(2,1)} %get-tuple-element.22), channel_id=1, source_target_pairs={{0,2},{1,3},{2,0},{3,1},{4,6},{5,7},{6,4},{7,5},{8,10},{9,11},{10,... | collective-permute-start | bytes 589832 | tf_op jit(solution)/shard_map/ppermute | solution.py:330
  24.0 24.8 %collective-permute-start.9 = (bf16[384,256]{1,0:T(8,128)(2,1)}, bf16[384,256]{1,0:T(8,128)(2,1)S(1)}, u32[]{:S(2)}, u32[]{:S(2)}) collective-permute-start(bf16[384,256]{1,0:T(8,128)(2,1)} %get-tuple-element.23), channel_id=1, source_target_pairs={{0,4},{1,5},{2,6},{3,7},{4,0},{5,1},{6,2},{7,3},{8,12},{9,13},{10,... | collective-permute-start | bytes 589832 | tf_op jit(solution)/shard_map/ppermute | solution.py:330
  46.8 9.2 %copy-start.16 = (bf16[384,256]{1,0:T(8,128)(2,1)}, bf16[384,256]{1,0:T(8,128)(2,1)S(1)}, u32[]{:S(2)}) copy-start(bf16[384,256]{1,0:T(8,128)(2,1)S(1)} %collective-permute-done.8.refs_9_) | copy-start | bytes 589828
  46.8 9.1 %collective-permute-start.4 = (bf16[128,1536]{1,0:T(8,128)(2,1)S(1)}, bf16[128,1536]{1,0:T(8,128)(2,1)S(1)}, u32[]{:S(2)}, u32[]{:S(2)}) collective-permute-start(bf16[128,1536]{1,0:T(8,128)(2,1)S(1)} %pad_maximum_fusion.refs_0_), channel_id=1, source_target_pairs={{0,1},{1,0},{2,3},{3,2},{4,5},{5,4},{6,7},{7,6},{8,9},{9,8},{10,11... | collective-permute-start | bytes 1179656 | tf_op jit(solution)/shard_map/ppermute | solution.py:330
  46.8 9.8 %copy-start.3 = (bf16[128,1536]{1,0:T(8,128)(2,1)}, bf16[128,1536]{1,0:T(8,128)(2,1)S(1)}, u32[]{:S(2)}) copy-start(bf16[128,1536]{1,0:T(8,128)(2,1)S(1)} %collective-permute-done.3.refs_3_) | copy-start | bytes 1179652
  46.8 9.1 %collective-permute-start.7 = (bf16[128,1536]{1,0:T(8,128)(2,1)S(1)}, bf16[128,1536]{1,0:T(8,128)(2,1)S(1)}, u32[]{:S(2)}, u32[]{:S(2)}) collective-permute-start(bf16[128,1536]{1,0:T(8,128)(2,1)S(1)} %collective-permute-done.3.refs_3_), channel_id=1, source_target_pairs={{0,1},{1,0},{2,3},{3,2},{4,5},{5,4},{6,7},{7,6},{8,9},{9,8},{10,11... | collective-permute-start | bytes 1179656 | tf_op jit(solution)/shard_map/ppermute | solution.py:330
  47.3 9.3 %copy-start.4 = (bf16[128,1536]{1,0:T(8,128)(2,1)}, bf16[128,1536]{1,0:T(8,128)(2,1)S(1)}, u32[]{:S(2)}) copy-start(bf16[128,1536]{1,0:T(8,128)(2,1)S(1)} %collective-permute-done.2.refs_2_) | copy-start | bytes 1179652
  47.3 8.6 %collective-permute-start.6 = (bf16[128,1536]{1,0:T(8,128)(2,1)S(1)}, bf16[128,1536]{1,0:T(8,128)(2,1)S(1)}, u32[]{:S(2)}, u32[]{:S(2)}) collective-permute-start(bf16[128,1536]{1,0:T(8,128)(2,1)S(1)} %collective-permute-done.2.refs_2_), channel_id=1, source_target_pairs={{0,1},{1,0},{2,3},{3,2},{4,5},{5,4},{6,7},{7,6},{8,9},{9,8},{10,11... | collective-permute-start | bytes 1179656 | tf_op jit(solution)/shard_map/ppermute | solution.py:330
  47.4 9.2 %copy-start.5 = (bf16[128,1536]{1,0:T(8,128)(2,1)}, bf16[128,1536]{1,0:T(8,128)(2,1)S(1)}, u32[]{:S(2)}) copy-start(bf16[128,1536]{1,0:T(8,128)(2,1)S(1)} %collective-permute-done.1.refs_1_) | copy-start | bytes 1179652
  47.4 8.5 %collective-permute-start.5 = (bf16[128,1536]{1,0:T(8,128)(2,1)S(1)}, bf16[128,1536]{1,0:T(8,128)(2,1)S(1)}, u32[]{:S(2)}, u32[]{:S(2)}) collective-permute-start(bf16[128,1536]{1,0:T(8,128)(2,1)S(1)} %collective-permute-done.1.refs_1_), channel_id=1, source_target_pairs={{0,1},{1,0},{2,3},{3,2},{4,5},{5,4},{6,7},{7,6},{8,9},{9,8},{10,11... | collective-permute-start | bytes 1179656 | tf_op jit(solution)/shard_map/ppermute | solution.py:330
  48.7 7.2 %copy-start.17 = (bf16[384,256]{1,0:T(8,128)(2,1)}, bf16[384,256]{1,0:T(8,128)(2,1)S(1)}, u32[]{:S(2)}) copy-start(bf16[384,256]{1,0:T(8,128)(2,1)S(1)} %collective-permute-done.9.refs_10_) | copy-start | bytes 589828
  48.7 7.1 %collective-permute-start.10 = (bf16[384,256]{1,0:T(8,128)(2,1)}, bf16[384,256]{1,0:T(8,128)(2,1)S(1)}, u32[]{:S(2)}, u32[]{:S(2)}) collective-permute-start(bf16[384,256]{1,0:T(8,128)(2,1)} %get-tuple-element.24), channel_id=1, source_target_pairs={{0,6},{1,7},{2,4},{3,5},{4,2},{5,3},{6,0},{7,1},{8,14},{9,15},{10,... | collective-permute-start | bytes 589832 | tf_op jit(solution)/shard_map/ppermute | solution.py:330
  55.9 0.7 copy-start.18
  55.9 0.8 copy-start.6
  55.9 0.9 copy-start.7
  55.9 1.0 copy-start.8
  56.6 0.8 copy-start.9
  62.0 15.8 %collective-permute-start.11 = (bf16[1024,128]{1,0:T(8,128)(2,1)}, bf16[1024,128]{1,0:T(8,128)(2,1)S(1)}, u32[]{:S(2)}, u32[]{:S(2)}) collective-permute-start(bf16[1024,128]{1,0:T(8,128)(2,1)} %get-tuple-element.26), channel_id=1, source_target_pairs={{0,8},{1,9},{2,10},{3,11},{4,12},{5,13},{6,14},{7,15},{8,0},{9,1},... | collective-permute-start | bytes 786440 | tf_op jit(solution)/shard_map/ppermute | solution.py:330
  66.3 0.9 copy-start.2
  77.9 0.7 copy-start.12
  78.6 10.5 %copy-start.10 = (bf16[128,1024]{1,0:T(8,128)(2,1)S(1)}, bf16[128,1024]{1,0:T(8,128)(2,1)}, u32[]{:S(2)}) copy-start(bf16[128,1024]{1,0:T(8,128)(2,1)} %get-tuple-element.20.out_ref.refs_8_) | copy-start | bytes 786436
  85.5 52.2 %all-to-all-start.1 = ((bf16[8,384,128]{2,1,0:T(8,128)(2,1)}), bf16[8,384,128]{2,1,0:T(8,128)(2,1)S(1)}, u32[]{:S(2)}, u32[]{:S(2)}) async-start(bf16[8,384,128]{2,1,0:T(8,128)(2,1)} %shard_map.105), calls=%async_computation.1 | async-start | bytes 1572864 | tf_op jit(solution)/shard_map/all_to_all | solution.py:416
  89.1 31.5 %collective-permute-start.12 = (bf16[128,1024]{1,0:T(8,128)(2,1)S(1)}, bf16[128,1024]{1,0:T(8,128)(2,1)S(1)}, u32[]{:S(2)}, u32[]{:S(2)}) collective-permute-start(bf16[128,1024]{1,0:T(8,128)(2,1)S(1)} %copy-done.10), channel_id=1, source_target_pairs={{0,8},{1,9},{2,10},{3,11},{4,12},{5,13},{6,14},{7,15},{8,0},{9,1},... | collective-permute-start | bytes 786440 | tf_op jit(solution)/shard_map/ppermute | solution.py:330
  120.5 0.7 copy-start.11
  126.3 7.2 %collective-permute-start.13 = (bf16[256,384]{1,0:T(8,128)(2,1)}, bf16[256,384]{1,0:T(8,128)(2,1)S(1)}, u32[]{:S(2)}, u32[]{:S(2)}) collective-permute-start(bf16[256,384]{1,0:T(8,128)(2,1)} %get-tuple-element.29), channel_id=1, source_target_pairs={{0,2},{1,3},{2,0},{3,1},{4,6},{5,7},{6,4},{7,5},{8,10},{9,11},{10,... | collective-permute-start | bytes 589832 | tf_op jit(solution)/shard_map/ppermute | solution.py:330
  127.8 7.9 %collective-permute-start.14 = (bf16[256,384]{1,0:T(8,128)(2,1)}, bf16[256,384]{1,0:T(8,128)(2,1)S(1)}, u32[]{:S(2)}, u32[]{:S(2)}) collective-permute-start(bf16[256,384]{1,0:T(8,128)(2,1)} %get-tuple-element.30), channel_id=1, source_target_pairs={{0,4},{1,5},{2,6},{3,7},{4,0},{5,1},{6,2},{7,3},{8,12},{9,13},{10,... | collective-permute-start | bytes 589832 | tf_op jit(solution)/shard_map/ppermute | solution.py:330
  127.8 9.9 %collective-permute-start.15 = (bf16[256,384]{1,0:T(8,128)(2,1)}, bf16[256,384]{1,0:T(8,128)(2,1)S(1)}, u32[]{:S(2)}, u32[]{:S(2)}) collective-permute-start(bf16[256,384]{1,0:T(8,128)(2,1)} %get-tuple-element.31), channel_id=1, source_target_pairs={{0,6},{1,7},{2,4},{3,5},{4,2},{5,3},{6,0},{7,1},{8,14},{9,15},{10,... | collective-permute-start | bytes 589832 | tf_op jit(solution)/shard_map/ppermute | solution.py:330
  133.5 4.2 %copy-start.13 = (bf16[256,384]{1,0:T(8,128)(2,1)}, bf16[256,384]{1,0:T(8,128)(2,1)S(1)}, u32[]{:S(2)}) copy-start(bf16[256,384]{1,0:T(8,128)(2,1)S(1)} %collective-permute-done.13.refs_1_) | copy-start | bytes 589828
  135.7 2.0 %copy-start.14 = (bf16[256,384]{1,0:T(8,128)(2,1)}, bf16[256,384]{1,0:T(8,128)(2,1)S(1)}, u32[]{:S(2)}) copy-start(bf16[256,384]{1,0:T(8,128)(2,1)S(1)} %collective-permute-done.14.refs_2_) | copy-start | bytes 589828
  137.7 0.7 copy-start.15
  137.7 1.0 copy-start.1

commit v4 on v3

--- a/solution.py
+++ b/solution.py
@@ -11,7 +11,7 @@
 HD = 128
 F32 = jnp.float32
 BF16 = jnp.bfloat16
-LIMIT = 60 * 1024 * 1024
+LIMIT = 28 * 1024 * 1024
 NT = (((1,), (1,)), ((), ()))
 
 
@@ -138,7 +138,7 @@
     return (q_grad, k_grad, v_grad, d_weight)
 
 
-def call(kernel, outs, args, specs=None, scratch=(), scalars=0, out_specs=None, flops=0, moved=0):
+def call(kernel, outs, args, specs=None, scratch=(), scalars=0, out_specs=None, flops=0, moved=0, limit=LIMIT):
     vmem = pl.BlockSpec(memory_space=pltpu.VMEM)
     if specs is None:
         specs = [vmem] * (len(args) - scalars)
@@ -154,7 +154,7 @@
             out_specs=out_specs,
             scratch_shapes=list(scratch),
         ),
-        compiler_params=pltpu.CompilerParams(vmem_limit_bytes=LIMIT),
+        compiler_params=pltpu.CompilerParams(vmem_limit_bytes=limit),
         cost_estimate=pl.CostEstimate(flops=flops, bytes_accessed=moved, transcendentals=0),
     )(*args)
 
@@ -363,6 +363,7 @@
         [shape((n, 3 * rows, HD), BF16)] + [shape((depth, 2 * HD), BF16)] * each,
         [q_img, k_img, v_img, out_weight],
         moved=4 * (3 * rows + depth) * width,
+        limit=60 * 1024 * 1024,
     )
     tok_in = lax.all_to_all(tok_out, "seq", split_axis=0, concat_axis=0, tiled=True)
     w_in = [w_out[0]] + [exchange(w_out[d], d) for d in range(1, each)]
@@ -382,10 +383,12 @@
     count = len(pieces)
     anywhere = [pl.BlockSpec(memory_space=pl.ANY)]
     half_width = d_out.shape[1] // 2
+    out_other = exchange(out_t, each)
+    w_own, _ = lax.optimization_barrier((w_in[0], out_t))
     mine, theirs = call(
         functools.partial(partial_kernel, count=count),
         [shape((image, HD), F32), shape((image, HD), BF16)],
-        [*pieces, *w_in],
+        [*pieces, w_own, *w_in[1:]],
         specs=anywhere * (count + each),
         scratch=[
             pltpu.VMEM((image, half_width), BF16),
@@ -397,7 +400,21 @@
         moved=2 * image * half_width,
     )
     theirs = exchange(theirs, each)
-    out_other = exchange(out_t, each)
+    out_other, mine = lax.optimization_barrier((out_other, mine))
+    dw_out = call(
+        functools.partial(weight_grad_kernel, count=count),
+        [shape((2 * HD, depth), BF16)] * each,
+        [*pieces, out_t, out_other],
+        specs=anywhere * count + [vmem, vmem],
+        scratch=[
+            pltpu.VMEM((image, half_width), BF16),
+            pltpu.VMEM((2 * HD, image), BF16),
+            pltpu.SemaphoreType.DMA((2 * count,)),
+        ],
+        flops=4 * image * half_width * HD,
+        moved=2 * image * half_width,
+    )
+    mine, *dw_out = lax.optimization_barrier((mine, *dw_out))
     (grad_out,) = call(
         functools.partial(backward_kernel, chunk=chunk),
         [shape((n, 3 * rows, HD), BF16)],
@@ -413,22 +430,8 @@
         flops=8 * total * image * HD,
         moved=4 * total * image,
     )
+    dw_in = [dw_out[0]] + [exchange(dw_out[d], d) for d in range(1, each)]
     grad_in = lax.all_to_all(grad_out, "seq", split_axis=0, concat_axis=0, tiled=True)
-    out_other, _ = lax.optimization_barrier((out_other, grad_out))
-    dw_out = call(
-        functools.partial(weight_grad_kernel, count=count),
-        [shape((2 * HD, depth), BF16)] * each,
-        [*pieces, out_t, out_other],
-        specs=anywhere * count + [vmem, vmem],
-        scratch=[
-            pltpu.VMEM((image, half_width), BF16),
-            pltpu.VMEM((2 * HD, image), BF16),
-            pltpu.SemaphoreType.DMA((2 * count,)),
-        ],
-        flops=4 * image * half_width * HD,
-        moved=2 * image * half_width,
-    )
-    dw_in = [dw_out[0]] + [exchange(dw_out[d], d) for d in range(1, each)]
     return tuple(
         call(
             unpack_kernel,

time: 142 us -> 135 us (0.951)
  starting transfers between devices: 35.9 us -> 27.9 us
  local copies, waits for them, and re-layouts: 5.67 us -> 9.42 us
  Pallas kernels: 30.2 us -> 27 us
    ppermute x16, starting transfers between devices: 28.5 us -> 16.8 us  [exchange(): return lax.ppermute(array, ('seq', 'fsdp'), pairs)]
    unnamed x38 -> x36, local copies, waits for them, and re-layouts: 4.62 us -> 9.39 us
    all_to_all x1, starting transfers between devices: 3.81 us -> 7.41 us  [local(): lax.all_to_all(tok_out, 'seq', split_axis=0, concat_axis=0, tiled=True)]
    pallas_call x6, Pallas kernels: 30.2 us -> 27 us  [call(): pl.pallas_call(kernel, out_shape=outs, grid_spec=pltpu.PrefetchScalarGrid...]
  transfers between devices with their start and end apart: 18 -> 18, of which waited for: 9 -> 7; matrix products, arithmetic and copies ran while one was open for 0% -> 0% of each run, Pallas kernels for 14% -> 13%
where the time goes in v4:
time: 135 us
  waiting for transfers between devices  69.8 us (52%)
  starting transfers between devices  27.9 us (21%)
  Pallas kernels  27 us (20%)
  local copies, waits for them, and re-layouts  9.42 us (7%)
    ppermute x16, waiting for transfers between devices, exchange(): return lax.ppermute(array, ('seq', 'fsdp'), pairs)  69.8 us
    pallas_call x6, Pallas kernels, call(): pl.pallas_call(kernel, out_shape=outs, grid_spec=pltpu.PrefetchScalarGrid...  27 us
    ppermute x16, starting transfers between devices, exchange(): return lax.ppermute(array, ('seq', 'fsdp'), pairs)  16.8 us
    unnamed x36, local copies, waits for them, and re-layouts  9.39 us
    all_to_all x1, starting transfers between devices, local(): lax.all_to_all(tok_out, 'seq', split_axis=0, concat_axis=0, tiled=True)  7.41 us
    all_to_all x1, starting transfers between devices, local(): lax.all_to_all(grad_out, 'seq', split_axis=0, concat_axis=0, tiled=True)  3.7 us
  transfers between devices with their start and end apart: 18, of which 7 were waited for; matrix products, arithmetic and copies ran while one was open for 0% of the time, Pallas kernels for 13%

profile of v4, /device:TPU:0, one launch (start us, length us, event | category | flops | bytes accessed | tf_op | source)
XLA Modules:
  0.0 134.9 jit_solution(13509603035002176265)
XLA Ops:
  0.6 2.9 %shard_map.102 = (bf16[8,384,128]{2,1,0:T(8,128)(2,1)}, bf16[384,256]{1,0:T(8,128)(2,1)}, bf16[384,256]{1,0:T(8,128)(2,1)}, bf16[384,256]{1,0:T(8,128)(2,1)}, bf16[384,256]{1,0:T(8,128)(2,1)}) custom-call(bf16[128,1024]{1,0:T(8,128)(2,1)} %q_ref.1, bf16[128,1024]{1,0:T(8,128)(2,1)} %k_ref.1, bf16[128,1024]{1,0:T(8,128)(2,1)} %v_ref.1, bf16[384,1024]{1,0:T(8,128)(2,1)} %w_ref.1), custom_call_target="tpu_custom_call" | custom-call | bytes 3145728 | tf_op jit(solution)/shard_map/pallas_call | solution.py:147
  3.5 7.4 %all-to-all-start = ((bf16[8,384,128]{2,1,0:T(8,128)(2,1)}), bf16[8,384,128]{2,1,0:T(8,128)(2,1)S(1)}, u32[]{:S(2)}, u32[]{:S(2)}) async-start(bf16[8,384,128]{2,1,0:T(8,128)(2,1)} %get-tuple-element.25), calls=%async_computation | async-start | bytes 1572864 | tf_op jit(solution)/shard_map/all_to_all | solution.py:368
  11.0 3.0 %collective-permute-start.1 = (bf16[64,1536]{1,0:T(8,128)(2,1)S(1)}, bf16[64,1536]{1,0:T(8,128)(2,1)S(1)}, u32[]{:S(2)}, u32[]{:S(2)}) collective-permute-start(bf16[64,1536]{1,0:T(8,128)(2,1)S(1)} %get-tuple-element.47), channel_id=1, source_target_pairs={{0,8},{1,9},{2,10},{3,11},{4,12},{5,13},{6,14},{7,15},{8,0},{9,1},... | collective-permute-start | bytes 589832 | tf_op jit(solution)/shard_map/ppermute | solution.py:330
  14.0 25.6 %collective-permute-done.1 = bf16[64,1536]{1,0:T(8,128)(2,1)S(1)} collective-permute-done((bf16[64,1536]{1,0:T(8,128)(2,1)S(1)}, bf16[64,1536]{1,0:T(8,128)(2,1)S(1)}, u32[]{:S(2)}, u32[]{:S(2)}) %collective-permute-start.1) | collective-permute-done | bytes 196640 | tf_op jit(solution)/shard_map/ppermute | solution.py:330
  39.6 0.1 collective-permute-start.4
  39.7 2.8 %collective-permute-start.3 = (bf16[128,1536]{1,0:T(8,128)(2,1)S(1)}, bf16[128,1536]{1,0:T(8,128)(2,1)S(1)}, u32[]{:S(2)}, u32[]{:S(2)}) collective-permute-start(bf16[128,1536]{1,0:T(8,128)(2,1)S(1)} %pad_maximum_fusion.refs_0_), channel_id=1, source_target_pairs={{0,4},{1,5},{2,6},{3,7},{4,0},{5,1},{6,2},{7,3},{8,12},{9,13},{10,... | collective-permute-start | bytes 1179656 | tf_op jit(solution)/shard_map/ppermute | solution.py:330
  42.5 0.6 collective-permute-start.2
  43.2 1.4 %collective-permute-start.9 = (bf16[384,256]{1,0:T(8,128)(2,1)S(1)}, bf16[384,256]{1,0:T(8,128)(2,1)S(1)}, u32[]{:S(2)}, u32[]{:S(2)}) collective-permute-start(bf16[384,256]{1,0:T(8,128)(2,1)S(1)} %copy-done.17), channel_id=1, source_target_pairs={{0,2},{1,3},{2,0},{3,1},{4,6},{5,7},{6,4},{7,5},{8,10},{9,11},{10,... | collective-permute-start | bytes 589832 | tf_op jit(solution)/shard_map/ppermute | solution.py:330
  44.5 0.0 collective-permute-start.10
  44.5 18.4 %collective-permute-done.9.refs_9_ = bf16[384,256]{1,0:T(8,128)(2,1)S(1)} collective-permute-done((bf16[384,256]{1,0:T(8,128)(2,1)S(1)}, bf16[384,256]{1,0:T(8,128)(2,1)S(1)}, u32[]{:S(2)}, u32[]{:S(2)}) %collective-permute-start.9) | collective-permute-done | bytes 196640 | tf_op jit(solution)/shard_map/ppermute | solution.py:330
  62.9 0.7 copy-done.6
  63.6 0.0 collective-permute-start.5
  63.6 0.0 collective-permute-done.4.refs_3_
  63.6 0.5 collective-permute-start.8
  64.1 0.0 collective-permute-done.3.refs_2_
  64.1 0.1 collective-permute-start.7
  64.2 0.0 collective-permute-done.2.refs_1_
  64.2 0.4 collective-permute-start.6
  64.7 0.0 collective-permute-done.10.refs_10_
  64.7 0.7 copy-done.8
  65.3 0.8 collective-permute-start.11
  66.1 1.2 copy-done
  67.3 1.2 copy-done.2
  68.5 4.9 %shard_map.103 = (bf16[1536,1024]{1,0:T(8,128)(2,1)S(1)}, bf16[128,1024]{1,0:T(8,128)(2,1)S(1)}) custom-call(s32[1]{0:T(128)} %bitcast.me_ref, bf16[8,384,128]{2,1,0:T(8,128)(2,1)S(1)} %all-to-all-done.tok_ref, bf16[512,1024]{1,0:T(8,128)(2,1)S(1)} %copy-done, bf16[512,1024]{1,0:T(8,128)(2,1)S(1)} %copy-done.2), custom_call_target="tpu_custom_call" | custom-call | flops 805306368 | bytes 6291456 | tf_op jit(solution)/shard_map/pallas_call | solution.py:147
  73.5 3.4 %collective-permute-start = (bf16[128,1024]{1,0:T(8,128)(2,1)S(1)}, bf16[128,1024]{1,0:T(8,128)(2,1)S(1)}, u32[]{:S(2)}, u32[]{:S(2)}) collective-permute-start(bf16[128,1024]{1,0:T(8,128)(2,1)S(1)} %get-tuple-element.27.refs_8_.out_ref), channel_id=1, source_target_pairs={{0,8},{1,9},{2,10},{3,11},{4,12},{5,13},{6,14},{7,15},{8,0},{9,1},... | collective-permute-start | bytes 786440 | tf_op jit(solution)/shard_map/ppermute | solution.py:330
  76.9 0.0 copy-start.5
  77.0 1.0 copy-done.5
  78.0 0.9 copy-done.7
  78.9 0.9 copy-done.9
  79.8 7.6 %shard_map.104 = (f32[1024,128]{1,0:T(8,128)S(1)}, bf16[1024,128]{1,0:T(8,128)(2,1)S(1)}) custom-call(bf16[128,1536]{1,0:T(8,128)(2,1)S(1)} %pad_maximum_fusion.refs_0_, bf16[128,1536]{1,0:T(8,128)(2,1)S(1)} %collective-permute-done.2.refs_1_, bf16[128,1536]{1,0:T(8,128)(2,1)S(1)} %collective-permute-done.3.refs_2_, ...), custom_call_target="tpu_custom_call" | custom-call | flops 805306368 | bytes 3145728 | tf_op jit(solution)/shard_map/pallas_call | solution.py:147
  87.4 0.1 collective-permute-start.12
  87.5 1.3 collective-permute-done.refs_9_
  88.8 5.5 %shard_map.105 = (bf16[256,384]{1,0:T(8,128)(2,1)S(1)}, bf16[256,384]{1,0:T(8,128)(2,1)S(1)}, bf16[256,384]{1,0:T(8,128)(2,1)S(1)}, bf16[256,384]{1,0:T(8,128)(2,1)S(1)}) custom-call(bf16[128,1536]{1,0:T(8,128)(2,1)S(1)} %pad_maximum_fusion.refs_0_, bf16[128,1536]{1,0:T(8,128)(2,1)S(1)} %collective-permute-done.2.refs_1_, ...), custom_call_target="tpu_custom_call" | custom-call | flops 805306368 | bytes 3145728 | tf_op jit(solution)/shard_map/pallas_call | solution.py:147
  94.3 0.0 copy-start.3
  94.3 0.7 copy-done.3
  95.0 0.7 copy-done.10
  95.7 0.7 copy-done.12
  96.3 0.7 copy-done.14
  97.0 3.5 %collective-permute-done.12.theirs_ref = bf16[1024,128]{1,0:T(8,128)(2,1)S(1)} collective-permute-done((bf16[1024,128]{1,0:T(8,128)(2,1)S(1)}, bf16[1024,128]{1,0:T(8,128)(2,1)S(1)}, u32[]{:S(2)}, u32[]{:S(2)}) %collective-permute-start.12) | collective-permute-done | bytes 262176 | tf_op jit(solution)/shard_map/ppermute | solution.py:330
  100.5 4.5 %shard_map.106 = bf16[8,384,128]{2,1,0:T(8,128)(2,1)} custom-call(s32[1]{0:T(128)} %bitcast.me_ref, bf16[8,384,128]{2,1,0:T(8,128)(2,1)S(1)} %all-to-all-done.tok_ref, bf16[512,1024]{1,0:T(8,128)(2,1)S(1)} %copy-done.1, bf16[512,1024]{1,0:T(8,128)(2,1)S(1)} %copy-done.2, bf16[1536,1024]{1,0:T(8,128)(2,1)S(1)} %get-tuple-element.26.probs_ref, ...), custom_call_target="tpu_custom_call" | custom-call | flops 1610612736 | bytes 6291456 | tf_op jit(solution)/shard_map/pallas_call | solution.py:147
  105.0 3.7 %all-to-all-start.1 = ((bf16[8,384,128]{2,1,0:T(8,128)(2,1)}), bf16[8,384,128]{2,1,0:T(8,128)(2,1)S(1)}, u32[]{:S(2)}, u32[]{:S(2)}) async-start(bf16[8,384,128]{2,1,0:T(8,128)(2,1)} %shard_map.106), calls=%async_computation.1 | async-start | bytes 1572864 | tf_op jit(solution)/shard_map/all_to_all | solution.py:434
  108.7 2.0 %collective-permute-start.13 = (bf16[256,384]{1,0:T(8,128)(2,1)S(1)}, bf16[256,384]{1,0:T(8,128)(2,1)S(1)}, u32[]{:S(2)}, u32[]{:S(2)}) collective-permute-start(bf16[256,384]{1,0:T(8,128)(2,1)S(1)} %copy-done.15), channel_id=1, source_target_pairs={{0,2},{1,3},{2,0},{3,1},{4,6},{5,7},{6,4},{7,5},{8,10},{9,11},{10,... | collective-permute-start | bytes 589832 | tf_op jit(solution)/shard_map/ppermute | solution.py:330
  110.7 1.5 %collective-permute-start.14 = (bf16[256,384]{1,0:T(8,128)(2,1)S(1)}, bf16[256,384]{1,0:T(8,128)(2,1)S(1)}, u32[]{:S(2)}, u32[]{:S(2)}) collective-permute-start(bf16[256,384]{1,0:T(8,128)(2,1)S(1)} %copy-done.13), channel_id=1, source_target_pairs={{0,4},{1,5},{2,6},{3,7},{4,0},{5,1},{6,2},{7,3},{8,12},{9,13},{10,... | collective-permute-start | bytes 589832 | tf_op jit(solution)/shard_map/ppermute | solution.py:330
  112.2 0.1 collective-permute-start.15
  112.2 10.0 %collective-permute-done.13.refs_1_ = bf16[256,384]{1,0:T(8,128)(2,1)S(1)} collective-permute-done((bf16[256,384]{1,0:T(8,128)(2,1)S(1)}, bf16[256,384]{1,0:T(8,128)(2,1)S(1)}, u32[]{:S(2)}, u32[]{:S(2)}) %collective-permute-start.13) | collective-permute-done | bytes 196640 | tf_op jit(solution)/shard_map/ppermute | solution.py:330
  122.2 7.1 %collective-permute-done.14.refs_2_ = bf16[256,384]{1,0:T(8,128)(2,1)S(1)} collective-permute-done((bf16[256,384]{1,0:T(8,128)(2,1)S(1)}, bf16[256,384]{1,0:T(8,128)(2,1)S(1)}, u32[]{:S(2)}, u32[]{:S(2)}) %collective-permute-start.14) | collective-permute-done | bytes 196640 | tf_op jit(solution)/shard_map/ppermute | solution.py:330
  129.3 3.9 %collective-permute-done.15.refs_3_ = bf16[256,384]{1,0:T(8,128)(2,1)S(1)} collective-permute-done((bf16[256,384]{1,0:T(8,128)(2,1)S(1)}, bf16[256,384]{1,0:T(8,128)(2,1)S(1)}, u32[]{:S(2)}, u32[]{:S(2)}) %collective-permute-start.15) | collective-permute-done | bytes 196640 | tf_op jit(solution)/shard_map/ppermute | solution.py:330
  133.2 1.7 %shard_map.107 = (bf16[128,1024]{1,0:T(8,128)(2,1)}, bf16[128,1024]{1,0:T(8,128)(2,1)}, bf16[128,1024]{1,0:T(8,128)(2,1)}, f32[384,1024]{1,0:T(8,128)}) custom-call(bf16[8,384,128]{2,1,0:T(8,128)(2,1)S(1)} %all-to-all-done.1.tok_ref, bf16[256,384]{1,0:T(8,128)(2,1)S(1)} %copy-done.4, bf16[256,384]{1,0:T(8,128)(2,1)S(1)} %collective-permute-done.13.refs_1_, ...), custom_call_target="tpu_custom_call" | custom-call | bytes 3932160 | tf_op jit(solution)/shard_map/pallas_call | solution.py:147
  (32 shorter events, 0.1 us)
Async XLA Ops:
  0.6 10.3 %copy-start.16 = (bf16[128,3072]{1,0:T(8,128)(2,1)S(1)}, bf16[128,3072]{1,0:T(8,128)(2,1)}, u32[]{:S(2)}) copy-start(bf16[128,3072]{1,0:T(8,128)(2,1)} %param.13) | copy-start | bytes 2359300
  3.5 39.6 %copy-start.17 = (bf16[384,256]{1,0:T(8,128)(2,1)S(1)}, bf16[384,256]{1,0:T(8,128)(2,1)}, u32[]{:S(2)}) copy-start(bf16[384,256]{1,0:T(8,128)(2,1)} %get-tuple-element.30) | copy-start | bytes 589828
  3.5 62.6 %all-to-all-start = ((bf16[8,384,128]{2,1,0:T(8,128)(2,1)}), bf16[8,384,128]{2,1,0:T(8,128)(2,1)S(1)}, u32[]{:S(2)}, u32[]{:S(2)}) async-start(bf16[8,384,128]{2,1,0:T(8,128)(2,1)} %get-tuple-element.25), calls=%async_computation | async-start | bytes 1572864 | tf_op jit(solution)/shard_map/all_to_all | solution.py:368
  11.0 28.6 %collective-permute-start.1 = (bf16[64,1536]{1,0:T(8,128)(2,1)S(1)}, bf16[64,1536]{1,0:T(8,128)(2,1)S(1)}, u32[]{:S(2)}, u32[]{:S(2)}) collective-permute-start(bf16[64,1536]{1,0:T(8,128)(2,1)S(1)} %get-tuple-element.47), channel_id=1, source_target_pairs={{0,8},{1,9},{2,10},{3,11},{4,12},{5,13},{6,14},{7,15},{8,0},{9,1},... | collective-permute-start | bytes 589832 | tf_op jit(solution)/shard_map/ppermute | solution.py:330
  39.6 24.0 %collective-permute-start.4 = (bf16[128,1536]{1,0:T(8,128)(2,1)S(1)}, bf16[128,1536]{1,0:T(8,128)(2,1)S(1)}, u32[]{:S(2)}, u32[]{:S(2)}) collective-permute-start(bf16[128,1536]{1,0:T(8,128)(2,1)S(1)} %pad_maximum_fusion.refs_0_), channel_id=1, source_target_pairs={{0,6},{1,7},{2,4},{3,5},{4,2},{5,3},{6,0},{7,1},{8,14},{9,15},{10,... | collective-permute-start | bytes 1179656 | tf_op jit(solution)/shard_map/ppermute | solution.py:330
  39.7 24.5 %collective-permute-start.3 = (bf16[128,1536]{1,0:T(8,128)(2,1)S(1)}, bf16[128,1536]{1,0:T(8,128)(2,1)S(1)}, u32[]{:S(2)}, u32[]{:S(2)}) collective-permute-start(bf16[128,1536]{1,0:T(8,128)(2,1)S(1)} %pad_maximum_fusion.refs_0_), channel_id=1, source_target_pairs={{0,4},{1,5},{2,6},{3,7},{4,0},{5,1},{6,2},{7,3},{8,12},{9,13},{10,... | collective-permute-start | bytes 1179656 | tf_op jit(solution)/shard_map/ppermute | solution.py:330
  42.5 21.7 %collective-permute-start.2 = (bf16[128,1536]{1,0:T(8,128)(2,1)S(1)}, bf16[128,1536]{1,0:T(8,128)(2,1)S(1)}, u32[]{:S(2)}, u32[]{:S(2)}) collective-permute-start(bf16[128,1536]{1,0:T(8,128)(2,1)S(1)} %pad_maximum_fusion.refs_0_), channel_id=1, source_target_pairs={{0,2},{1,3},{2,0},{3,1},{4,6},{5,7},{6,4},{7,5},{8,10},{9,11},{10,... | collective-permute-start | bytes 1179656 | tf_op jit(solution)/shard_map/ppermute | solution.py:330
  43.2 19.8 %collective-permute-start.9 = (bf16[384,256]{1,0:T(8,128)(2,1)S(1)}, bf16[384,256]{1,0:T(8,128)(2,1)S(1)}, u32[]{:S(2)}, u32[]{:S(2)}) collective-permute-start(bf16[384,256]{1,0:T(8,128)(2,1)S(1)} %copy-done.17), channel_id=1, source_target_pairs={{0,2},{1,3},{2,0},{3,1},{4,6},{5,7},{6,4},{7,5},{8,10},{9,11},{10,... | collective-permute-start | bytes 589832 | tf_op jit(solution)/shard_map/ppermute | solution.py:330
  44.5 20.1 %collective-permute-start.10 = (bf16[384,256]{1,0:T(8,128)(2,1)}, bf16[384,256]{1,0:T(8,128)(2,1)S(1)}, u32[]{:S(2)}, u32[]{:S(2)}) collective-permute-start(bf16[384,256]{1,0:T(8,128)(2,1)} %get-tuple-element.31), channel_id=1, source_target_pairs={{0,4},{1,5},{2,6},{3,7},{4,0},{5,1},{6,2},{7,3},{8,12},{9,13},{10,... | collective-permute-start | bytes 589832 | tf_op jit(solution)/shard_map/ppermute | solution.py:330
  62.9 0.7 copy-start.6
  63.6 13.3 %collective-permute-start.5 = (bf16[128,1536]{1,0:T(8,128)(2,1)S(1)}, bf16[128,1536]{1,0:T(8,128)(2,1)S(1)}, u32[]{:S(2)}, u32[]{:S(2)}) collective-permute-start(bf16[128,1536]{1,0:T(8,128)(2,1)S(1)} %pad_maximum_fusion.refs_0_), channel_id=1, source_target_pairs={{0,1},{1,0},{2,3},{3,2},{4,5},{5,4},{6,7},{7,6},{8,9},{9,8},{10,11... | collective-permute-start | bytes 1179656 | tf_op jit(solution)/shard_map/ppermute | solution.py:330
  63.6 13.3 %collective-permute-start.8 = (bf16[128,1536]{1,0:T(8,128)(2,1)S(1)}, bf16[128,1536]{1,0:T(8,128)(2,1)S(1)}, u32[]{:S(2)}, u32[]{:S(2)}) collective-permute-start(bf16[128,1536]{1,0:T(8,128)(2,1)S(1)} %collective-permute-done.4.refs_3_), channel_id=1, source_target_pairs={{0,1},{1,0},{2,3},{3,2},{4,5},{5,4},{6,7},{7,6},{8,9},{9,8},{10,11... | collective-permute-start | bytes 1179656 | tf_op jit(solution)/shard_map/ppermute | solution.py:330
  64.1 12.8 %collective-permute-start.7 = (bf16[128,1536]{1,0:T(8,128)(2,1)S(1)}, bf16[128,1536]{1,0:T(8,128)(2,1)S(1)}, u32[]{:S(2)}, u32[]{:S(2)}) collective-permute-start(bf16[128,1536]{1,0:T(8,128)(2,1)S(1)} %collective-permute-done.3.refs_2_), channel_id=1, source_target_pairs={{0,1},{1,0},{2,3},{3,2},{4,5},{5,4},{6,7},{7,6},{8,9},{9,8},{10,11... | collective-permute-start | bytes 1179656 | tf_op jit(solution)/shard_map/ppermute | solution.py:330
  64.2 12.7 %collective-permute-start.6 = (bf16[128,1536]{1,0:T(8,128)(2,1)S(1)}, bf16[128,1536]{1,0:T(8,128)(2,1)}, u32[]{:S(2)}, u32[]{:S(2)}) collective-permute-start(bf16[128,1536]{1,0:T(8,128)(2,1)S(1)} %collective-permute-done.2.refs_1_), channel_id=1, source_target_pairs={{0,1},{1,0},{2,3},{3,2},{4,5},{5,4},{6,7},{7,6},{8,9},{9,8},{10,11... | collective-permute-start | bytes 1179656 | tf_op jit(solution)/shard_map/ppermute | solution.py:330
  64.7 0.7 copy-start.8
  65.3 8.1 %collective-permute-start.11 = (bf16[384,256]{1,0:T(8,128)(2,1)}, bf16[384,256]{1,0:T(8,128)(2,1)}, u32[]{:S(2)}, u32[]{:S(2)}) collective-permute-start(bf16[384,256]{1,0:T(8,128)(2,1)} %get-tuple-element.32), channel_id=1, source_target_pairs={{0,6},{1,7},{2,4},{3,5},{4,2},{5,3},{6,0},{7,1},{8,14},{9,15},{10,... | collective-permute-start | bytes 589832 | tf_op jit(solution)/shard_map/ppermute | solution.py:330
  66.1 1.2 copy-start
  67.3 1.2 copy-start.2
  73.5 15.3 %collective-permute-start = (bf16[128,1024]{1,0:T(8,128)(2,1)S(1)}, bf16[128,1024]{1,0:T(8,128)(2,1)S(1)}, u32[]{:S(2)}, u32[]{:S(2)}) collective-permute-start(bf16[128,1024]{1,0:T(8,128)(2,1)S(1)} %get-tuple-element.27.refs_8_.out_ref), channel_id=1, source_target_pairs={{0,8},{1,9},{2,10},{3,11},{4,12},{5,13},{6,14},{7,15},{8,0},{9,1},... | collective-permute-start | bytes 786440 | tf_op jit(solution)/shard_map/ppermute | solution.py:330
  76.9 23.6 %copy-start.1 = (bf16[512,1024]{1,0:T(8,128)(2,1)S(1)}, bf16[512,1024]{1,0:T(8,128)(2,1)}, u32[]{:S(2)}) copy-start(bf16[512,1024]{1,0:T(8,128)(2,1)} %kt_ref.3) | copy-start | bytes 3145732
  76.9 1.0 copy-start.5
  78.0 0.9 copy-start.7
  78.9 0.9 copy-start.9
  87.4 13.1 %collective-permute-start.12 = (bf16[1024,128]{1,0:T(8,128)(2,1)S(1)}, bf16[1024,128]{1,0:T(8,128)(2,1)S(1)}, u32[]{:S(2)}, u32[]{:S(2)}) collective-permute-start(bf16[1024,128]{1,0:T(8,128)(2,1)S(1)} %get-tuple-element.41), channel_id=1, source_target_pairs={{0,8},{1,9},{2,10},{3,11},{4,12},{5,13},{6,14},{7,15},{8,0},{9,1},... | collective-permute-start | bytes 786440 | tf_op jit(solution)/shard_map/ppermute | solution.py:330
  94.3 0.7 copy-start.3
  95.0 0.7 copy-start.10
  95.7 0.7 copy-start.12
  96.3 0.7 copy-start.14
  100.5 8.2 %copy-start.15 = (bf16[256,384]{1,0:T(8,128)(2,1)S(1)}, bf16[256,384]{1,0:T(8,128)(2,1)}, u32[]{:S(2)}) copy-start(bf16[256,384]{1,0:T(8,128)(2,1)} %copy-done.14) | copy-start | bytes 589828
  100.5 10.2 %copy-start.13 = (bf16[256,384]{1,0:T(8,128)(2,1)S(1)}, bf16[256,384]{1,0:T(8,128)(2,1)}, u32[]{:S(2)}) copy-start(bf16[256,384]{1,0:T(8,128)(2,1)} %copy-done.12) | copy-start | bytes 589828
  100.5 11.7 %copy-start.11 = (bf16[256,384]{1,0:T(8,128)(2,1)S(1)}, bf16[256,384]{1,0:T(8,128)(2,1)}, u32[]{:S(2)}) copy-start(bf16[256,384]{1,0:T(8,128)(2,1)} %copy-done.10) | copy-start | bytes 589828
  100.5 32.7 %copy-start.4 = (bf16[256,384]{1,0:T(8,128)(2,1)S(1)}, bf16[256,384]{1,0:T(8,128)(2,1)}, u32[]{:S(2)}) copy-start(bf16[256,384]{1,0:T(8,128)(2,1)} %copy-done.3) | copy-start | bytes 589828
  105.0 28.2 %all-to-all-start.1 = ((bf16[8,384,128]{2,1,0:T(8,128)(2,1)}), bf16[8,384,128]{2,1,0:T(8,128)(2,1)S(1)}, u32[]{:S(2)}, u32[]{:S(2)}) async-start(bf16[8,384,128]{2,1,0:T(8,128)(2,1)} %shard_map.106), calls=%async_computation.1 | async-start | bytes 1572864 | tf_op jit(solution)/shard_map/all_to_all | solution.py:434
  108.7 13.5 %collective-permute-start.13 = (bf16[256,384]{1,0:T(8,128)(2,1)S(1)}, bf16[256,384]{1,0:T(8,128)(2,1)S(1)}, u32[]{:S(2)}, u32[]{:S(2)}) collective-permute-start(bf16[256,384]{1,0:T(8,128)(2,1)S(1)} %copy-done.15), channel_id=1, source_target_pairs={{0,2},{1,3},{2,0},{3,1},{4,6},{5,7},{6,4},{7,5},{8,10},{9,11},{10,... | collective-permute-start | bytes 589832 | tf_op jit(solution)/shard_map/ppermute | solution.py:330
  110.7 18.6 %collective-permute-start.14 = (bf16[256,384]{1,0:T(8,128)(2,1)S(1)}, bf16[256,384]{1,0:T(8,128)(2,1)S(1)}, u32[]{:S(2)}, u32[]{:S(2)}) collective-permute-start(bf16[256,384]{1,0:T(8,128)(2,1)S(1)} %copy-done.13), channel_id=1, source_target_pairs={{0,4},{1,5},{2,6},{3,7},{4,0},{5,1},{6,2},{7,3},{8,12},{9,13},{10,... | collective-permute-start | bytes 589832 | tf_op jit(solution)/shard_map/ppermute | solution.py:330
  112.2 21.0 %collective-permute-start.15 = (bf16[256,384]{1,0:T(8,128)(2,1)S(1)}, bf16[256,384]{1,0:T(8,128)(2,1)S(1)}, u32[]{:S(2)}, u32[]{:S(2)}) collective-permute-start(bf16[256,384]{1,0:T(8,128)(2,1)S(1)} %copy-done.11), channel_id=1, source_target_pairs={{0,6},{1,7},{2,4},{3,5},{4,2},{5,3},{6,0},{7,1},{8,14},{9,15},{10,... | collective-permute-start | bytes 589832 | tf_op jit(solution)/shard_map/ppermute | solution.py:330

commit v5 on v3

--- a/solution.py
+++ b/solution.py
@@ -11,7 +11,7 @@
 HD = 128
 F32 = jnp.float32
 BF16 = jnp.bfloat16
-LIMIT = 60 * 1024 * 1024
+LIMIT = 28 * 1024 * 1024
 NT = (((1,), (1,)), ((), ()))
 
 
@@ -138,7 +138,7 @@
     return (q_grad, k_grad, v_grad, d_weight)
 
 
-def call(kernel, outs, args, specs=None, scratch=(), scalars=0, out_specs=None, flops=0, moved=0):
+def call(kernel, outs, args, specs=None, scratch=(), scalars=0, out_specs=None, flops=0, moved=0, limit=LIMIT):
     vmem = pl.BlockSpec(memory_space=pltpu.VMEM)
     if specs is None:
         specs = [vmem] * (len(args) - scalars)
@@ -154,7 +154,7 @@
             out_specs=out_specs,
             scratch_shapes=list(scratch),
         ),
-        compiler_params=pltpu.CompilerParams(vmem_limit_bytes=LIMIT),
+        compiler_params=pltpu.CompilerParams(vmem_limit_bytes=limit),
         cost_estimate=pl.CostEstimate(flops=flops, bytes_accessed=moved, transcendentals=0),
     )(*args)
 
@@ -165,24 +165,49 @@
     return me // each, lax.rem(me, each)
 
 
-def pack_kernel(q_ref, k_ref, v_ref, w_ref, tok_ref, *wt_refs):
+def pack_kernel(q_ref, k_ref, v_ref, tok_ref, sems):
     heads = tok_ref.shape[0]
     rows = q_ref.shape[0]
+    copies = []
     for h in range(heads):
-        cols = slice(h * HD, (h + 1) * HD)
-        tok_ref[h, 0:rows, :] = q_ref[:, cols]
-        tok_ref[h, rows : 2 * rows, :] = k_ref[:, cols]
-        tok_ref[h, 2 * rows : 3 * rows, :] = v_ref[:, cols]
+        for i, ref in enumerate((q_ref, k_ref, v_ref)):
+            copies.append(
+                pltpu.make_async_copy(
+                    ref.at[:, h * HD : (h + 1) * HD],
+                    tok_ref.at[h, i * rows : (i + 1) * rows, :],
+                    sems.at[i, h],
+                )
+            )
+    for copy in copies:
+        copy.start()
+    for copy in copies:
+        copy.wait()
+
+
+def pack_weight_kernel(w_ref, kt_ref, vt_ref, *refs):
+    *wt_refs, kh_ref, vh_ref, sems, text_sems = refs
     half, place = halves()
-    each = heads // 2
+    each = len(wt_refs)
+    copies = []
+    here = pl.ds(pl.multiple_of(lax.axis_index("seq") * HD, HD), HD)
+    for i, (whole, head) in enumerate(((kt_ref, kh_ref), (vt_ref, vh_ref))):
+        copies.append(pltpu.make_async_copy(whole.at[:, here], head, text_sems.at[i]))
     for d, wt_ref in enumerate(wt_refs):
         to = jnp.bitwise_xor(place, d)
         for i, side in enumerate((half, 1 - half)):
             at = pl.multiple_of((side * each + to) * HD, HD)
-            wt_ref[:, i * HD : (i + 1) * HD] = w_ref[:, pl.ds(at, HD)]
-
-
-def forward_kernel(me_ref, tok_ref, kt_ref, vt_ref, probs_ref, out_ref, keys, vals_t, *, chunk):
+            copies.append(
+                pltpu.make_async_copy(
+                    w_ref.at[:, pl.ds(at, HD)], wt_ref.at[:, i * HD : (i + 1) * HD], sems.at[d, i]
+                )
+            )
+    for copy in copies:
+        copy.start()
+    for copy in copies:
+        copy.wait()
+
+
+def forward_kernel(tok_ref, kt_ref, vt_ref, probs_ref, out_ref, keys, vals_t, *, chunk):
     n, three, _ = tok_ref.shape
     rows = three // 3
     image = n * rows
@@ -250,27 +275,19 @@
         theirs_ref[at, :] = part[:, HD:].astype(BF16)
 
 
-def weight_grad_kernel(*refs, count):
-    pieces = refs[:count]
-    mine_ref, theirs_ref = refs[count : count + 2]
-    dw_refs = refs[count + 2 : count + 2 + count // 2]
-    cot, outs, sems = refs[count + 2 + count // 2 :]
-    copies = load_cotangents(pieces, cot, sems)
-    for copy in copies:
-        copy.start()
+def weight_grad_kernel(cot_ref, mine_ref, theirs_ref, *refs):
+    *dw_refs, outs = refs
     outs[0:HD, :] = mine_ref[...]
     outs[HD : 2 * HD, :] = theirs_ref[...]
-    for copy in copies:
-        copy.wait()
     _, place = halves()
     for d, dw_ref in enumerate(dw_refs):
         depth = dw_ref.shape[1]
         at = pl.multiple_of(jnp.bitwise_xor(place, d) * depth, HD)
-        dw_ref[...] = jnp.dot(outs[...], cot[:, pl.ds(at, depth)], preferred_element_type=F32).astype(BF16)
+        dw_ref[...] = jnp.dot(outs[...], cot_ref[:, pl.ds(at, depth)], preferred_element_type=F32).astype(BF16)
 
 
 def backward_kernel(
-    me_ref, tok_ref, kt_ref, vt_ref, probs_ref, out_ref, mine_ref, theirs_ref, send_ref, keys_t, vals, dk, dv, *, chunk
+    tok_ref, kt_ref, vt_ref, probs_ref, out_ref, mine_ref, theirs_ref, send_ref, keys_t, vals, dk, dv, *, chunk
 ):
     n, three, _ = tok_ref.shape
     rows = three // 3
@@ -330,14 +347,18 @@
     return lax.ppermute(array, ("seq", "fsdp"), pairs)
 
 
-def gather_cotangents(d_out, n):
+def cross_cotangents(d_out, n):
     rows, width = d_out.shape
     part, columns = rows // 2, width // 2
     half, _ = halves()
     first = lax.axis_index("fsdp") * part
     away = lax.dynamic_slice(d_out, (first, (1 - half) * columns), (part, columns))
     kept = lax.dynamic_slice(d_out, (first, half * columns), (part, columns))
-    both = jnp.concatenate([kept, exchange(away, n // 2)], axis=0)
+    return kept, exchange(away, n // 2)
+
+
+def gather_cotangents(kept, received, n):
+    both = jnp.concatenate([kept, received], axis=0)
     pieces = [both] + [exchange(both, d) for d in range(1, n // 2)]
     return pieces + [exchange(piece, cores=True) for piece in pieces]
 
@@ -356,39 +377,52 @@
     shape = jax.ShapeDtypeStruct
     vmem = pl.BlockSpec(memory_space=pltpu.VMEM)
 
-    pieces = gather_cotangents(d_out, n)
+    kept, received = cross_cotangents(d_out, n)
     each = n // 2
-    tok_out, *w_out = call(
+    hbm = pl.BlockSpec(memory_space=pltpu.HBM)
+    *w_out, k_head, v_head = call(
+        pack_weight_kernel,
+        [shape((depth, 2 * HD), BF16)] * each + [shape((text, HD), BF16)] * 2,
+        [out_weight, k_txt, v_txt],
+        specs=[hbm] * 3,
+        out_specs=[hbm] * (each + 2),
+        scratch=[pltpu.SemaphoreType.DMA((each, 2)), pltpu.SemaphoreType.DMA((2,))],
+        moved=4 * depth * width,
+        limit=60 * 1024 * 1024,
+    )
+    w_in = [w_out[0]] + [exchange(w_out[d], d) for d in range(1, each)]
+    (tok_out,) = call(
         pack_kernel,
-        [shape((n, 3 * rows, HD), BF16)] + [shape((depth, 2 * HD), BF16)] * each,
-        [q_img, k_img, v_img, out_weight],
-        moved=4 * (3 * rows + depth) * width,
-    )
+        [shape((n, 3 * rows, HD), BF16)],
+        [q_img, k_img, v_img],
+        specs=[hbm] * 3,
+        out_specs=[hbm],
+        scratch=[pltpu.SemaphoreType.DMA((3, n))],
+        moved=4 * 3 * rows * width,
+        limit=60 * 1024 * 1024,
+    )
+    tok_out, received = lax.optimization_barrier((tok_out, received))
+    received, w_in = lax.optimization_barrier((received, w_in))
+    pieces = gather_cotangents(kept, received, n)
     tok_in = lax.all_to_all(tok_out, "seq", split_axis=0, concat_axis=0, tiled=True)
-    w_in = [w_out[0]] + [exchange(w_out[d], d) for d in range(1, each)]
-
-    me = lax.axis_index("seq").astype(jnp.int32)[None]
-    text_spec = pl.BlockSpec((text, HD), lambda i, me_ref: (0, me_ref[0]))
+
     probs, out_t = call(
         functools.partial(forward_kernel, chunk=chunk),
         [shape((total, image), BF16), shape((HD, image), BF16)],
-        [me, tok_in, k_txt, v_txt],
-        specs=[vmem, text_spec, text_spec],
+        [tok_in, k_head, v_head],
         scratch=[pltpu.VMEM((total, HD), BF16), pltpu.VMEM((HD, total), BF16)],
-        scalars=1,
         flops=4 * total * image * HD,
         moved=4 * total * image,
     )
     count = len(pieces)
-    anywhere = [pl.BlockSpec(memory_space=pl.ANY)]
     half_width = d_out.shape[1] // 2
-    mine, theirs = call(
+    out_other = exchange(out_t, each)
+    mine, theirs, cot = call(
         functools.partial(partial_kernel, count=count),
-        [shape((image, HD), F32), shape((image, HD), BF16)],
+        [shape((image, HD), F32), shape((image, HD), BF16), shape((image, half_width), BF16)],
         [*pieces, *w_in],
-        specs=anywhere * (count + each),
+        specs=[hbm] * (count + each),
         scratch=[
-            pltpu.VMEM((image, half_width), BF16),
             pltpu.VMEM((half_width, 2 * HD), BF16),
             pltpu.SemaphoreType.DMA((2 * count,)),
             pltpu.SemaphoreType.DMA((each,)),
@@ -397,34 +431,27 @@
         moved=2 * image * half_width,
     )
     theirs = exchange(theirs, each)
-    out_other = exchange(out_t, each)
     (grad_out,) = call(
         functools.partial(backward_kernel, chunk=chunk),
         [shape((n, 3 * rows, HD), BF16)],
-        [me, tok_in, k_txt, v_txt, probs, out_t, mine, theirs],
-        specs=[vmem, text_spec, text_spec] + [vmem] * 4,
+        [tok_in, k_head, v_head, probs, out_t, mine, theirs],
+
         scratch=[
             pltpu.VMEM((HD, total), BF16),
             pltpu.VMEM((total, HD), BF16),
             pltpu.VMEM((image, HD), F32),
             pltpu.VMEM((image, HD), F32),
         ],
-        scalars=1,
         flops=8 * total * image * HD,
         moved=4 * total * image,
     )
+    grad_out, out_other = lax.optimization_barrier((grad_out, out_other))
     grad_in = lax.all_to_all(grad_out, "seq", split_axis=0, concat_axis=0, tiled=True)
-    out_other, _ = lax.optimization_barrier((out_other, grad_out))
     dw_out = call(
-        functools.partial(weight_grad_kernel, count=count),
+        weight_grad_kernel,
         [shape((2 * HD, depth), BF16)] * each,
-        [*pieces, out_t, out_other],
-        specs=anywhere * count + [vmem, vmem],
-        scratch=[
-            pltpu.VMEM((image, half_width), BF16),
-            pltpu.VMEM((2 * HD, image), BF16),
-            pltpu.SemaphoreType.DMA((2 * count,)),
-        ],
+        [cot, out_t, out_other],
+        scratch=[pltpu.VMEM((2 * HD, image), BF16)],
         flops=4 * image * half_width * HD,
         moved=2 * image * half_width,
     )

time: 142 us -> 174 us (1.23)
  Pallas kernels: 30.2 us -> 81.2 us
  waiting for transfers between devices: 69.2 us -> 55.1 us
  starting transfers between devices: 35.9 us -> 26.6 us
  local copies, waits for them, and re-layouts: 5.67 us -> 9.77 us
    pallas_call x6 -> x7, Pallas kernels: 30.2 us -> 81.2 us  [call(): pl.pallas_call(kernel, out_shape=outs, grid_spec=pltpu.PrefetchScalarGrid...]
    ppermute x16, waiting for transfers between devices: 69.2 us -> 55.1 us  [exchange(): return lax.ppermute(array, ('seq', 'fsdp'), pairs)]
    ppermute x16, starting transfers between devices: 28.5 us -> 18.1 us  [exchange(): return lax.ppermute(array, ('seq', 'fsdp'), pairs)]
    unnamed x38 -> x22, local copies, waits for them, and re-layouts: 4.62 us -> 8.71 us
  transfers between devices with their start and end apart: 18 -> 18, of which waited for: 9 -> 12; matrix products, arithmetic and copies ran while one was open for 0% -> 0% of each run, Pallas kernels for 14% -> 45%
where the time goes in v5:
time: 174 us; the launch traced here: 173 us
  Pallas kernels  81.2 us (47%)
  waiting for transfers between devices  55.1 us (32%)
  starting transfers between devices  26.6 us (15%)
  local copies, waits for them, and re-layouts  9.77 us (6%)
    pallas_call x7, Pallas kernels, call(): pl.pallas_call(kernel, out_shape=outs, grid_spec=pltpu.PrefetchScalarGrid...  81.2 us
    ppermute x16, waiting for transfers between devices, exchange(): return lax.ppermute(array, ('seq', 'fsdp'), pairs)  55.1 us
    ppermute x16, starting transfers between devices, exchange(): return lax.ppermute(array, ('seq', 'fsdp'), pairs)  18.1 us
    unnamed x22, local copies, waits for them, and re-layouts  8.71 us
    all_to_all x1, starting transfers between devices, local(): lax.all_to_all(tok_out, 'seq', split_axis=0, concat_axis=0, tiled=True)  4.23 us
    all_to_all x1, starting transfers between devices, local(): lax.all_to_all(grad_out, 'seq', split_axis=0, concat_axis=0, tiled=True)  4.21 us
  transfers between devices with their start and end apart: 18, of which 12 were waited for; matrix products, arithmetic and copies ran while one was open for 0% of the time, Pallas kernels for 45%

profile of v5, /device:TPU:0, one launch (start us, length us, event | category | flops | bytes accessed | tf_op | source)
XLA Modules:
  0.0 173.4 jit_solution(244896378491330240)
XLA Ops:
  0.7 1.1 fusion
  1.7 4.1 %collective-permute-start = (bf16[64,1536]{1,0:T(8,128)(2,1)S(1)}, bf16[64,1536]{1,0:T(8,128)(2,1)S(1)}, u32[]{:S(2)}, u32[]{:S(2)}) collective-permute-start(bf16[64,1536]{1,0:T(8,128)(2,1)S(1)} %get-tuple-element.53), channel_id=1, source_target_pairs={{0,8},{1,9},{2,10},{3,11},{4,12},{5,13},{6,14},{7,15},{8,0},{9,1},... | collective-permute-start | bytes 589832 | tf_op jit(solution)/shard_map/ppermute | solution.py:347
  5.8 25.1 %shard_map.102 = bf16[8,384,128]{2,1,0:T(8,128)(2,1)} custom-call(bf16[128,1024]{1,0:T(8,128)(2,1)} %q_ref.1, bf16[128,1024]{1,0:T(8,128)(2,1)} %k_ref.1, bf16[128,1024]{1,0:T(8,128)(2,1)} %v_ref.1), custom_call_target="tpu_custom_call" | custom-call | bytes 1572864 | tf_op jit(solution)/shard_map/pallas_call | solution.py:147
  31.0 4.2 %all-to-all-start = ((bf16[8,384,128]{2,1,0:T(8,128)(2,1)}), bf16[8,384,128]{2,1,0:T(8,128)(2,1)}, u32[]{:S(2)}, u32[]{:S(2)}) async-start(bf16[8,384,128]{2,1,0:T(8,128)(2,1)} %shard_map.102), calls=%async_computation | async-start | bytes 1572864 | tf_op jit(solution)/shard_map/all_to_all | solution.py:407
  35.2 33.0 %shard_map.103 = (bf16[384,256]{1,0:T(8,128)(2,1)}, bf16[384,256]{1,0:T(8,128)(2,1)}, bf16[384,256]{1,0:T(8,128)(2,1)}, bf16[384,256]{1,0:T(8,128)(2,1)}, bf16[5...) custom-call(bf16[384,1024]{1,0:T(8,128)(2,1)} %w_ref.1, bf16[512,1024]{1,0:T(8,128)(2,1)} %kt_ref.1, bf16[512,1024]{1,0:T(8,128)(2,1)} %vt_ref.1), custom_call_target="tpu_custom_call" | custom-call | bytes 1572864 | tf_op jit(solution)/shard_map/pallas_call | solution.py:147
  68.2 1.9 %collective-permute-start.1 = (bf16[384,256]{1,0:T(8,128)(2,1)}, bf16[384,256]{1,0:T(8,128)(2,1)S(1)}, u32[]{:S(2)}, u32[]{:S(2)}) collective-permute-start(bf16[384,256]{1,0:T(8,128)(2,1)} %get-tuple-element.35), channel_id=1, source_target_pairs={{0,2},{1,3},{2,0},{3,1},{4,6},{5,7},{6,4},{7,5},{8,10},{9,11},{10,... | collective-permute-start | bytes 589832 | tf_op jit(solution)/shard_map/ppermute | solution.py:347
  70.1 1.5 collective-permute-start.2
  71.6 0.1 collective-permute-start.3
  71.7 3.7 %collective-permute-done.1.refs_9_ = bf16[384,256]{1,0:T(8,128)(2,1)S(1)} collective-permute-done((bf16[384,256]{1,0:T(8,128)(2,1)}, bf16[384,256]{1,0:T(8,128)(2,1)S(1)}, u32[]{:S(2)}, u32[]{:S(2)}) %collective-permute-start.1) | collective-permute-done | bytes 196640 | tf_op jit(solution)/shard_map/ppermute | solution.py:347
  75.4 2.8 %collective-permute-done.2.refs_10_ = bf16[384,256]{1,0:T(8,128)(2,1)S(1)} collective-permute-done((bf16[384,256]{1,0:T(8,128)(2,1)}, bf16[384,256]{1,0:T(8,128)(2,1)S(1)}, u32[]{:S(2)}, u32[]{:S(2)}) %collective-permute-start.2) | collective-permute-done | bytes 196640 | tf_op jit(solution)/shard_map/ppermute | solution.py:347
  78.2 2.0 %collective-permute-done.3.refs_11_ = bf16[384,256]{1,0:T(8,128)(2,1)S(1)} collective-permute-done((bf16[384,256]{1,0:T(8,128)(2,1)}, bf16[384,256]{1,0:T(8,128)(2,1)S(1)}, u32[]{:S(2)}, u32[]{:S(2)}) %collective-permute-start.3) | collective-permute-done | bytes 196640 | tf_op jit(solution)/shard_map/ppermute | solution.py:347
  80.3 2.6 %collective-permute-start.6 = (bf16[128,1536]{1,0:T(8,128)(2,1)S(1)}, bf16[128,1536]{1,0:T(8,128)(2,1)S(1)}, u32[]{:S(2)}, u32[]{:S(2)}) collective-permute-start(bf16[128,1536]{1,0:T(8,128)(2,1)S(1)} %pad_maximum_fusion.refs_0_), channel_id=1, source_target_pairs={{0,6},{1,7},{2,4},{3,5},{4,2},{5,3},{6,0},{7,1},{8,14},{9,15},{10,... | collective-permute-start | bytes 1179656 | tf_op jit(solution)/shard_map/ppermute | solution.py:347
  82.8 0.5 collective-permute-start.5
  83.4 0.4 collective-permute-start.4
  83.8 9.5 %collective-permute-done.6.refs_3_ = bf16[128,1536]{1,0:T(8,128)(2,1)S(1)} collective-permute-done((bf16[128,1536]{1,0:T(8,128)(2,1)S(1)}, bf16[128,1536]{1,0:T(8,128)(2,1)S(1)}, u32[]{:S(2)}, u32[]{:S(2)}) %collective-permute-start.6) | collective-permute-done | bytes 393248 | tf_op jit(solution)/shard_map/ppermute | solution.py:347
  93.3 5.6 %collective-permute-done.5.refs_2_ = bf16[128,1536]{1,0:T(8,128)(2,1)S(1)} collective-permute-done((bf16[128,1536]{1,0:T(8,128)(2,1)S(1)}, bf16[128,1536]{1,0:T(8,128)(2,1)S(1)}, u32[]{:S(2)}, u32[]{:S(2)}) %collective-permute-start.5) | collective-permute-done | bytes 393248 | tf_op jit(solution)/shard_map/ppermute | solution.py:347
  98.9 0.1 collective-permute-done.4.refs_1_
  99.0 0.4 collective-permute-start.8
  99.4 1.2 collective-permute-done.9.refs_6_
  100.6 0.6 collective-permute-done.8.refs_5_
  101.2 0.9 copy-done.7
  102.1 8.3 %shard_map.105 = (f32[1024,128]{1,0:T(8,128)S(1)}, bf16[1024,128]{1,0:T(8,128)(2,1)}, bf16[1024,1536]{1,0:T(8,128)(2,1)S(1)}) custom-call(bf16[128,1536]{1,0:T(8,128)(2,1)S(1)} %pad_maximum_fusion.refs_0_, bf16[128,1536]{1,0:T(8,128)(2,1)S(1)} %collective-permute-done.4.refs_1_, bf16[128,1536]{1,0:T(8,128)(2,1)S(1)} %collective-permute-done.5.refs_2_, ...), custom_call_target="tpu_custom_call" | custom-call | flops 805306368 | bytes 3145728 | tf_op jit(solution)/shard_map/pallas_call | solution.py:147
  110.4 0.8 copy-done.1
  111.2 2.4 %collective-permute-start.11 = (bf16[1024,128]{1,0:T(8,128)(2,1)}, bf16[1024,128]{1,0:T(8,128)(2,1)}, u32[]{:S(2)}, u32[]{:S(2)}) collective-permute-start(bf16[1024,128]{1,0:T(8,128)(2,1)} %get-tuple-element.44), channel_id=1, source_target_pairs={{0,8},{1,9},{2,10},{3,11},{4,12},{5,13},{6,14},{7,15},{8,0},{9,1},... | collective-permute-start | bytes 786440 | tf_op jit(solution)/shard_map/ppermute | solution.py:347
  113.6 0.9 copy-done.9
  114.5 6.0 %shard_map.104 = (bf16[1536,1024]{1,0:T(8,128)(2,1)S(1)}, bf16[128,1024]{1,0:T(8,128)(2,1)S(1)}) custom-call(bf16[8,384,128]{2,1,0:T(8,128)(2,1)} %all-to-all-done.tok_ref, bf16[512,128]{1,0:T(8,128)(2,1)S(1)} %copy-done.8, bf16[512,128]{1,0:T(8,128)(2,1)S(1)} %copy-done.9), custom_call_target="tpu_custom_call" | custom-call | flops 805306368 | bytes 6291456 | tf_op jit(solution)/shard_map/pallas_call | solution.py:147
  120.5 0.6 collective-permute-start.12
  121.1 11.7 %collective-permute-done.11.theirs_ref = bf16[1024,128]{1,0:T(8,128)(2,1)} collective-permute-done((bf16[1024,128]{1,0:T(8,128)(2,1)}, bf16[1024,128]{1,0:T(8,128)(2,1)}, u32[]{:S(2)}, u32[]{:S(2)}) %collective-permute-start.11) | collective-permute-done | bytes 262176 | tf_op jit(solution)/shard_map/ppermute | solution.py:347
  132.8 1.0 copy-done.2
  133.9 0.9 copy-done.10
  134.8 4.7 %shard_map.106 = bf16[8,384,128]{2,1,0:T(8,128)(2,1)S(1)} custom-call(bf16[8,384,128]{2,1,0:T(8,128)(2,1)} %all-to-all-done.tok_ref, bf16[512,128]{1,0:T(8,128)(2,1)S(1)} %copy-done.8, bf16[512,128]{1,0:T(8,128)(2,1)S(1)} %copy-done.10, bf16[1536,1024]{1,0:T(8,128)(2,1)S(1)} %get-tuple-element.31.probs_ref, ...), custom_call_target="tpu_custom_call" | custom-call | flops 1610612736 | bytes 6291456 | tf_op jit(solution)/shard_map/pallas_call | solution.py:147
  139.5 0.0 copy-start
  139.5 0.9 copy-done
  140.4 0.7 copy-done.3
  141.1 4.2 %all-to-all-start.1 = ((bf16[8,384,128]{2,1,0:T(8,128)(2,1)}), bf16[8,384,128]{2,1,0:T(8,128)(2,1)}, u32[]{:S(2)}, u32[]{:S(2)}) async-start(bf16[8,384,128]{2,1,0:T(8,128)(2,1)} %copy-done), calls=%async_computation.1 | async-start | bytes 1572864 | tf_op jit(solution)/shard_map/all_to_all | solution.py:449
  145.3 0.0 copy-start.4
  145.4 0.9 copy-done.4
  146.3 1.3 shard_map.107
  147.6 0.0 copy-start.5
  147.6 0.7 copy-done.5
  148.2 1.9 %collective-permute-start.13 = (bf16[256,384]{1,0:T(8,128)(2,1)S(1)}, bf16[256,384]{1,0:T(8,128)(2,1)S(1)}, u32[]{:S(2)}, u32[]{:S(2)}) collective-permute-start(bf16[256,384]{1,0:T(8,128)(2,1)S(1)} %get-tuple-element.49), channel_id=1, source_target_pairs={{0,2},{1,3},{2,0},{3,1},{4,6},{5,7},{6,4},{7,5},{8,10},{9,11},{10,... | collective-permute-start | bytes 589832 | tf_op jit(solution)/shard_map/ppermute | solution.py:347
  150.2 1.5 collective-permute-start.14
  151.6 0.1 collective-permute-start.15
  151.7 7.6 %collective-permute-done.13.refs_1_ = bf16[256,384]{1,0:T(8,128)(2,1)S(1)} collective-permute-done((bf16[256,384]{1,0:T(8,128)(2,1)S(1)}, bf16[256,384]{1,0:T(8,128)(2,1)S(1)}, u32[]{:S(2)}, u32[]{:S(2)}) %collective-permute-start.13) | collective-permute-done | bytes 196640 | tf_op jit(solution)/shard_map/ppermute | solution.py:347
  159.4 4.0 %collective-permute-done.14.refs_2_ = bf16[256,384]{1,0:T(8,128)(2,1)S(1)} collective-permute-done((bf16[256,384]{1,0:T(8,128)(2,1)S(1)}, bf16[256,384]{1,0:T(8,128)(2,1)S(1)}, u32[]{:S(2)}, u32[]{:S(2)}) %collective-permute-start.14) | collective-permute-done | bytes 196640 | tf_op jit(solution)/shard_map/ppermute | solution.py:347
  163.4 6.3 %collective-permute-done.15.refs_3_ = bf16[256,384]{1,0:T(8,128)(2,1)S(1)} collective-permute-done((bf16[256,384]{1,0:T(8,128)(2,1)S(1)}, bf16[256,384]{1,0:T(8,128)(2,1)S(1)}, u32[]{:S(2)}, u32[]{:S(2)}) %collective-permute-start.15) | collective-permute-done | bytes 196640 | tf_op jit(solution)/shard_map/ppermute | solution.py:347
  169.7 0.9 copy-done.6
  170.6 2.8 %shard_map.108 = (bf16[128,1024]{1,0:T(8,128)(2,1)}, bf16[128,1024]{1,0:T(8,128)(2,1)}, bf16[128,1024]{1,0:T(8,128)(2,1)}, f32[384,1024]{1,0:T(8,128)}) custom-call(bf16[8,384,128]{2,1,0:T(8,128)(2,1)} %all-to-all-done.1.tok_ref, bf16[256,384]{1,0:T(8,128)(2,1)S(1)} %copy-done.6, bf16[256,384]{1,0:T(8,128)(2,1)S(1)} %collective-permute-done.13.refs_1_, ...), custom_call_target="tpu_custom_call" | custom-call | bytes 3932160 | tf_op jit(solution)/shard_map/pallas_call | solution.py:147
  (19 shorter events, 0.1 us)
Async XLA Ops:
  1.7 29.2 %collective-permute-start = (bf16[64,1536]{1,0:T(8,128)(2,1)S(1)}, bf16[64,1536]{1,0:T(8,128)(2,1)S(1)}, u32[]{:S(2)}, u32[]{:S(2)}) collective-permute-start(bf16[64,1536]{1,0:T(8,128)(2,1)S(1)} %get-tuple-element.53), channel_id=1, source_target_pairs={{0,8},{1,9},{2,10},{3,11},{4,12},{5,13},{6,14},{7,15},{8,0},{9,1},... | collective-permute-start | bytes 589832 | tf_op jit(solution)/shard_map/ppermute | solution.py:347
  31.0 82.7 %all-to-all-start = ((bf16[8,384,128]{2,1,0:T(8,128)(2,1)}), bf16[8,384,128]{2,1,0:T(8,128)(2,1)}, u32[]{:S(2)}, u32[]{:S(2)}) async-start(bf16[8,384,128]{2,1,0:T(8,128)(2,1)} %shard_map.102), calls=%async_computation | async-start | bytes 1572864 | tf_op jit(solution)/shard_map/all_to_all | solution.py:407
  68.2 45.4 %copy-start.8 = (bf16[512,128]{1,0:T(8,128)(2,1)S(1)}, bf16[512,128]{1,0:T(8,128)(2,1)}, u32[]{:S(2)}) copy-start(bf16[512,128]{1,0:T(8,128)(2,1)} %get-tuple-element.29.kt_ref) | copy-start | bytes 393220
  68.2 7.2 %collective-permute-start.1 = (bf16[384,256]{1,0:T(8,128)(2,1)}, bf16[384,256]{1,0:T(8,128)(2,1)S(1)}, u32[]{:S(2)}, u32[]{:S(2)}) collective-permute-start(bf16[384,256]{1,0:T(8,128)(2,1)} %get-tuple-element.35), channel_id=1, source_target_pairs={{0,2},{1,3},{2,0},{3,1},{4,6},{5,7},{6,4},{7,5},{8,10},{9,11},{10,... | collective-permute-start | bytes 589832 | tf_op jit(solution)/shard_map/ppermute | solution.py:347
  70.1 8.1 %collective-permute-start.2 = (bf16[384,256]{1,0:T(8,128)(2,1)}, bf16[384,256]{1,0:T(8,128)(2,1)S(1)}, u32[]{:S(2)}, u32[]{:S(2)}) collective-permute-start(bf16[384,256]{1,0:T(8,128)(2,1)} %get-tuple-element.36), channel_id=1, source_target_pairs={{0,4},{1,5},{2,6},{3,7},{4,0},{5,1},{6,2},{7,3},{8,12},{9,13},{10,... | collective-permute-start | bytes 589832 | tf_op jit(solution)/shard_map/ppermute | solution.py:347
  71.6 8.6 %collective-permute-start.3 = (bf16[384,256]{1,0:T(8,128)(2,1)}, bf16[384,256]{1,0:T(8,128)(2,1)S(1)}, u32[]{:S(2)}, u32[]{:S(2)}) collective-permute-start(bf16[384,256]{1,0:T(8,128)(2,1)} %get-tuple-element.37), channel_id=1, source_target_pairs={{0,6},{1,7},{2,4},{3,5},{4,2},{5,3},{6,0},{7,1},{8,14},{9,15},{10,... | collective-permute-start | bytes 589832 | tf_op jit(solution)/shard_map/ppermute | solution.py:347
  80.3 13.1 %collective-permute-start.6 = (bf16[128,1536]{1,0:T(8,128)(2,1)S(1)}, bf16[128,1536]{1,0:T(8,128)(2,1)S(1)}, u32[]{:S(2)}, u32[]{:S(2)}) collective-permute-start(bf16[128,1536]{1,0:T(8,128)(2,1)S(1)} %pad_maximum_fusion.refs_0_), channel_id=1, source_target_pairs={{0,6},{1,7},{2,4},{3,5},{4,2},{5,3},{6,0},{7,1},{8,14},{9,15},{10,... | collective-permute-start | bytes 1179656 | tf_op jit(solution)/shard_map/ppermute | solution.py:347
  82.8 16.1 %collective-permute-start.5 = (bf16[128,1536]{1,0:T(8,128)(2,1)S(1)}, bf16[128,1536]{1,0:T(8,128)(2,1)S(1)}, u32[]{:S(2)}, u32[]{:S(2)}) collective-permute-start(bf16[128,1536]{1,0:T(8,128)(2,1)S(1)} %pad_maximum_fusion.refs_0_), channel_id=1, source_target_pairs={{0,4},{1,5},{2,6},{3,7},{4,0},{5,1},{6,2},{7,3},{8,12},{9,13},{10,... | collective-permute-start | bytes 1179656 | tf_op jit(solution)/shard_map/ppermute | solution.py:347
  83.4 15.6 %collective-permute-start.4 = (bf16[128,1536]{1,0:T(8,128)(2,1)S(1)}, bf16[128,1536]{1,0:T(8,128)(2,1)S(1)}, u32[]{:S(2)}, u32[]{:S(2)}) collective-permute-start(bf16[128,1536]{1,0:T(8,128)(2,1)S(1)} %pad_maximum_fusion.refs_0_), channel_id=1, source_target_pairs={{0,2},{1,3},{2,0},{3,1},{4,6},{5,7},{6,4},{7,5},{8,10},{9,11},{10,... | collective-permute-start | bytes 1179656 | tf_op jit(solution)/shard_map/ppermute | solution.py:347
  83.8 15.6 %collective-permute-start.7 = (bf16[128,1536]{1,0:T(8,128)(2,1)S(1)}, bf16[128,1536]{1,0:T(8,128)(2,1)S(1)}, u32[]{:S(2)}, u32[]{:S(2)}) collective-permute-start(bf16[128,1536]{1,0:T(8,128)(2,1)S(1)} %pad_maximum_fusion.refs_0_), channel_id=1, source_target_pairs={{0,1},{1,0},{2,3},{3,2},{4,5},{5,4},{6,7},{7,6},{8,9},{9,8},{10,11... | collective-permute-start | bytes 1179656 | tf_op jit(solution)/shard_map/ppermute | solution.py:347
  93.3 6.1 %collective-permute-start.10 = (bf16[128,1536]{1,0:T(8,128)(2,1)S(1)}, bf16[128,1536]{1,0:T(8,128)(2,1)S(1)}, u32[]{:S(2)}, u32[]{:S(2)}) collective-permute-start(bf16[128,1536]{1,0:T(8,128)(2,1)S(1)} %collective-permute-done.6.refs_3_), channel_id=1, source_target_pairs={{0,1},{1,0},{2,3},{3,2},{4,5},{5,4},{6,7},{7,6},{8,9},{9,8},{10,11... | collective-permute-start | bytes 1179656 | tf_op jit(solution)/shard_map/ppermute | solution.py:347
  98.9 1.7 collective-permute-start.9
  99.0 2.2 %collective-permute-start.8 = (bf16[128,1536]{1,0:T(8,128)(2,1)S(1)}, bf16[128,1536]{1,0:T(8,128)(2,1)S(1)}, u32[]{:S(2)}, u32[]{:S(2)}) collective-permute-start(bf16[128,1536]{1,0:T(8,128)(2,1)S(1)} %collective-permute-done.4.refs_1_), channel_id=1, source_target_pairs={{0,1},{1,0},{2,3},{3,2},{4,5},{5,4},{6,7},{7,6},{8,9},{9,8},{10,11... | collective-permute-start | bytes 1179656 | tf_op jit(solution)/shard_map/ppermute | solution.py:347
  101.2 0.9 copy-start.7
  110.4 0.8 copy-start.1
  111.2 21.6 %collective-permute-start.11 = (bf16[1024,128]{1,0:T(8,128)(2,1)}, bf16[1024,128]{1,0:T(8,128)(2,1)}, u32[]{:S(2)}, u32[]{:S(2)}) collective-permute-start(bf16[1024,128]{1,0:T(8,128)(2,1)} %get-tuple-element.44), channel_id=1, source_target_pairs={{0,8},{1,9},{2,10},{3,11},{4,12},{5,13},{6,14},{7,15},{8,0},{9,1},... | collective-permute-start | bytes 786440 | tf_op jit(solution)/shard_map/ppermute | solution.py:347
  113.6 0.9 copy-start.9
  120.5 19.9 %collective-permute-start.12 = (bf16[128,1024]{1,0:T(8,128)(2,1)S(1)}, bf16[128,1024]{1,0:T(8,128)(2,1)S(1)}, u32[]{:S(2)}, u32[]{:S(2)}) collective-permute-start(bf16[128,1024]{1,0:T(8,128)(2,1)S(1)} %get-tuple-element.32.out_ref.mine_ref), channel_id=1, source_target_pairs={{0,8},{1,9},{2,10},{3,11},{4,12},{5,13},{6,14},{7,15},{8,0},{9,1},... | collective-permute-start | bytes 786440 | tf_op jit(solution)/shard_map/ppermute | solution.py:347
  132.8 1.0 copy-start.2
  133.9 0.9 copy-start.10
  139.5 0.9 copy-start
  140.4 0.7 copy-start.3
  141.1 28.6 %all-to-all-start.1 = ((bf16[8,384,128]{2,1,0:T(8,128)(2,1)}), bf16[8,384,128]{2,1,0:T(8,128)(2,1)}, u32[]{:S(2)}, u32[]{:S(2)}) async-start(bf16[8,384,128]{2,1,0:T(8,128)(2,1)} %copy-done), calls=%async_computation.1 | async-start | bytes 1572864 | tf_op jit(solution)/shard_map/all_to_all | solution.py:449
  145.3 1.0 copy-start.4
  147.6 0.7 copy-start.5
  148.2 11.1 %collective-permute-start.13 = (bf16[256,384]{1,0:T(8,128)(2,1)S(1)}, bf16[256,384]{1,0:T(8,128)(2,1)S(1)}, u32[]{:S(2)}, u32[]{:S(2)}) collective-permute-start(bf16[256,384]{1,0:T(8,128)(2,1)S(1)} %get-tuple-element.49), channel_id=1, source_target_pairs={{0,2},{1,3},{2,0},{3,1},{4,6},{5,7},{6,4},{7,5},{8,10},{9,11},{10,... | collective-permute-start | bytes 589832 | tf_op jit(solution)/shard_map/ppermute | solution.py:347
  150.2 13.2 %collective-permute-start.14 = (bf16[256,384]{1,0:T(8,128)(2,1)S(1)}, bf16[256,384]{1,0:T(8,128)(2,1)S(1)}, u32[]{:S(2)}, u32[]{:S(2)}) collective-permute-start(bf16[256,384]{1,0:T(8,128)(2,1)S(1)} %get-tuple-element.50), channel_id=1, source_target_pairs={{0,4},{1,5},{2,6},{3,7},{4,0},{5,1},{6,2},{7,3},{8,12},{9,13},{10,... | collective-permute-start | bytes 589832 | tf_op jit(solution)/shard_map/ppermute | solution.py:347
  151.6 18.0 %collective-permute-start.15 = (bf16[256,384]{1,0:T(8,128)(2,1)S(1)}, bf16[256,384]{1,0:T(8,128)(2,1)S(1)}, u32[]{:S(2)}, u32[]{:S(2)}) collective-permute-start(bf16[256,384]{1,0:T(8,128)(2,1)S(1)} %get-tuple-element.51), channel_id=1, source_target_pairs={{0,6},{1,7},{2,4},{3,5},{4,2},{5,3},{6,0},{7,1},{8,14},{9,15},{10,... | collective-permute-start | bytes 589832 | tf_op jit(solution)/shard_map/ppermute | solution.py:347
  169.7 0.9 copy-start.6

commit v6 on v5

--- a/solution.py
+++ b/solution.py
@@ -165,112 +165,74 @@
     return me // each, lax.rem(me, each)
 
 
-def pack_kernel(q_ref, k_ref, v_ref, tok_ref, sems):
-    heads = tok_ref.shape[0]
+def pack_kernel(q_ref, k_ref, v_ref, tok_ref):
     rows = q_ref.shape[0]
-    copies = []
-    for h in range(heads):
+    for h in range(tok_ref.shape[0]):
         for i, ref in enumerate((q_ref, k_ref, v_ref)):
-            copies.append(
-                pltpu.make_async_copy(
-                    ref.at[:, h * HD : (h + 1) * HD],
-                    tok_ref.at[h, i * rows : (i + 1) * rows, :],
-                    sems.at[i, h],
-                )
-            )
-    for copy in copies:
-        copy.start()
-    for copy in copies:
-        copy.wait()
+            tok_ref[h, i * rows : (i + 1) * rows, :] = ref[:, h * HD : (h + 1) * HD]
 
 
 def pack_weight_kernel(w_ref, kt_ref, vt_ref, *refs):
-    *wt_refs, kh_ref, vh_ref, sems, text_sems = refs
+    *wt_refs, text_ref = refs
     half, place = halves()
     each = len(wt_refs)
-    copies = []
-    here = pl.ds(pl.multiple_of(lax.axis_index("seq") * HD, HD), HD)
-    for i, (whole, head) in enumerate(((kt_ref, kh_ref), (vt_ref, vh_ref))):
-        copies.append(pltpu.make_async_copy(whole.at[:, here], head, text_sems.at[i]))
+    text_ref[0] = kt_ref[...]
+    text_ref[1] = vt_ref[...]
     for d, wt_ref in enumerate(wt_refs):
         to = jnp.bitwise_xor(place, d)
         for i, side in enumerate((half, 1 - half)):
             at = pl.multiple_of((side * each + to) * HD, HD)
-            copies.append(
-                pltpu.make_async_copy(
-                    w_ref.at[:, pl.ds(at, HD)], wt_ref.at[:, i * HD : (i + 1) * HD], sems.at[d, i]
-                )
-            )
-    for copy in copies:
-        copy.start()
-    for copy in copies:
-        copy.wait()
-
-
-def forward_kernel(tok_ref, kt_ref, vt_ref, probs_ref, out_ref, keys, vals_t, *, chunk):
+            wt_ref[:, i * HD : (i + 1) * HD] = w_ref[:, pl.ds(at, HD)]
+
+
+def forward_kernel(tok_ref, text_ref, probs_ref, out_ref, queries_ref, keys_t_ref, vals_ref, keys, vals_t, *, chunk):
     n, three, _ = tok_ref.shape
     rows = three // 3
     image = n * rows
-    text = kt_ref.shape[0]
+    text = text_ref.shape[1]
+    queries_ref[...] = tok_ref[:, 0:rows, :].reshape(image, HD)
     keys[0:image, :] = tok_ref[:, rows : 2 * rows, :].reshape(image, HD)
-    keys[image : image + text, :] = kt_ref[...]
-    vals_t[:, 0:image] = tok_ref[:, 2 * rows : 3 * rows, :].reshape(image, HD).T
-    vals_t[:, image : image + text] = vt_ref[...].T
+    keys[image : image + text, :] = text_ref[0]
+    vals_ref[0:image, :] = tok_ref[:, 2 * rows : 3 * rows, :].reshape(image, HD)
+    vals_ref[image : image + text, :] = text_ref[1]
+    keys_t_ref[...] = keys[...].T
+    vals_t[...] = vals_ref[...].T
     factor = HD ** (-0.5) * math.log2(math.e)
-    per = chunk // rows
     for c in range(image // chunk):
-        queries = tok_ref[c * per : (c + 1) * per, 0:rows, :].reshape(chunk, HD)
-        scores = lax.dot_general(keys[...], queries, NT, preferred_element_type=F32)
+        span = slice(c * chunk, (c + 1) * chunk)
+        scores = lax.dot_general(keys[...], queries_ref[span, :], NT, preferred_element_type=F32)
         top = jnp.max(scores, axis=0, keepdims=True)
         weights = jnp.exp2((scores - top) * factor)
         total = jnp.sum(weights, axis=0, keepdims=True)
         low = (weights * (1.0 / total)).astype(BF16)
-        probs_ref[:, c * chunk : (c + 1) * chunk] = low
-        out_ref[:, c * chunk : (c + 1) * chunk] = jnp.dot(
-            vals_t[...], low, preferred_element_type=F32
-        ).astype(BF16)
-
-
-def load_cotangents(pieces, cot, sems):
+        probs_ref[:, span] = low
+        out_ref[:, span] = jnp.dot(vals_t[...], low, preferred_element_type=F32).astype(BF16)
+
+
+def partial_kernel(*refs, count):
+    each = count // 2
+    pieces, weights = refs[:count], refs[count : count + each]
+    mine_ref, theirs_ref, cot_ref, weight = refs[count + each :]
     half, place = halves()
     core = lax.axis_index("fsdp")
-    each = len(pieces) // 2
     rows = pieces[0].shape[0]
-    copies = []
+    part = rows // 2
     for i, piece in enumerate(pieces):
         source = jnp.bitwise_xor(place, i % each)
-        shift = (core if i < each else 1 - core) * (rows // 2)
+        shift = (core if i < each else 1 - core) * part
         for j, side in enumerate((half, 1 - half)):
             at = pl.multiple_of((side * each + source) * rows + shift, 16)
-            copies.append(
-                pltpu.make_async_copy(
-                    piece.at[pl.ds(j * (rows // 2), rows // 2), :],
-                    cot.at[pl.ds(at, rows // 2), :],
-                    sems.at[2 * i + j],
-                )
-            )
-    return copies
-
-
-def partial_kernel(*refs, count):
-    pieces, weights = refs[:count], refs[count : count + count // 2]
-    mine_ref, theirs_ref, cot, weight, sems, wsems = refs[count + count // 2 :]
-    _, place = halves()
-    depth = weights[0].shape[0]
-    copies = load_cotangents(pieces, cot, sems)
+            cot_ref[pl.ds(at, part), :] = piece[j * part : (j + 1) * part, :]
     for d, block in enumerate(weights):
+        depth = block.shape[0]
         at = pl.multiple_of(jnp.bitwise_xor(place, d) * depth, 16)
-        copies.append(pltpu.make_async_copy(block, weight.at[pl.ds(at, depth), :], wsems.at[d]))
-    for copy in copies:
-        copy.start()
-    for copy in copies:
-        copy.wait()
+        weight[pl.ds(at, depth), :] = block[...]
     step = 256
 
-    @pl.loop(0, cot.shape[0] // step)
+    @pl.loop(0, cot_ref.shape[0] // step)
     def _(i):
         at = pl.ds(pl.multiple_of(i * step, step), step)
-        part = jnp.dot(cot[at, :], weight[...], preferred_element_type=F32)
+        part = jnp.dot(cot_ref[at, :], weight[...], preferred_element_type=F32)
         mine_ref[at, :] = part[:, :HD]
         theirs_ref[at, :] = part[:, HD:].astype(BF16)
 
@@ -287,31 +249,25 @@
 
 
 def backward_kernel(
-    tok_ref, kt_ref, vt_ref, probs_ref, out_ref, mine_ref, theirs_ref, send_ref, keys_t, vals, dk, dv, *, chunk
+    queries_ref, keys_t_ref, vals_ref, probs_ref, out_ref, mine_ref, theirs_ref, send_ref, dk, dv, *, chunk
 ):
-    n, three, _ = tok_ref.shape
+    n, three, _ = send_ref.shape
     rows = three // 3
     image = n * rows
-    text = kt_ref.shape[0]
     scale = HD ** (-0.5)
-    vals[0:image, :] = tok_ref[:, 2 * rows : 3 * rows, :].reshape(image, HD)
-    vals[image : image + text, :] = vt_ref[...]
-    keys_t[:, 0:image] = tok_ref[:, rows : 2 * rows, :].reshape(image, HD).T
-    keys_t[:, image : image + text] = kt_ref[...].T
     per = chunk // rows
     for c in range(image // chunk):
         span = slice(c * chunk, (c + 1) * chunk)
         grads = (mine_ref[span, :] + theirs_ref[span, :].astype(F32)).astype(BF16)
-        queries = tok_ref[c * per : (c + 1) * per, 0:rows, :].reshape(chunk, HD)
         row_dot = jnp.sum(
             grads.astype(F32).T * out_ref[:, span].astype(F32), axis=0, keepdims=True
         )
-        prob_grad = lax.dot_general(vals[...], grads, NT, preferred_element_type=F32)
+        prob_grad = lax.dot_general(vals_ref[...], grads, NT, preferred_element_type=F32)
         low = probs_ref[:, span]
         score_grad = (low.astype(F32) * (prob_grad - row_dot)).astype(BF16)
-        dq_t = jnp.dot(keys_t[...], score_grad, preferred_element_type=F32) * scale
+        dq_t = jnp.dot(keys_t_ref[...], score_grad, preferred_element_type=F32) * scale
         send_ref[c * per : (c + 1) * per, 0:rows, :] = dq_t.T.astype(BF16).reshape(per, rows, HD)
-        dk_part = jnp.dot(score_grad[0:image, :], queries, preferred_element_type=F32)
+        dk_part = jnp.dot(score_grad[0:image, :], queries_ref[span, :], preferred_element_type=F32)
         dv_part = jnp.dot(low[0:image, :], grads, preferred_element_type=F32)
         if c == 0:
             dk[...] = dk_part
@@ -323,17 +279,17 @@
     send_ref[:, 2 * rows : 3 * rows, :] = dv[...].astype(BF16).reshape(n, rows, HD)
 
 
-def unpack_kernel(tok_ref, *refs):
-    *dw_refs, q_ref, k_ref, v_ref, w_ref = refs
-    heads, three, _ = tok_ref.shape
-    rows = three // 3
-    for h in range(heads):
-        cols = slice(h * HD, (h + 1) * HD)
-        q_ref[:, cols] = tok_ref[h, 0:rows, :]
-        k_ref[:, cols] = tok_ref[h, rows : 2 * rows, :]
-        v_ref[:, cols] = tok_ref[h, 2 * rows : 3 * rows, :]
+def unpack_kernel(tok_ref, q_ref, k_ref, v_ref):
+    rows = q_ref.shape[0]
+    for h in range(tok_ref.shape[0]):
+        for i, ref in enumerate((q_ref, k_ref, v_ref)):
+            ref[:, h * HD : (h + 1) * HD] = tok_ref[h, i * rows : (i + 1) * rows, :]
+
+
+def unpack_weight_kernel(*refs):
+    *dw_refs, w_ref = refs
     half, place = halves()
-    each = heads // 2
+    each = len(dw_refs)
     for d, dw_ref in enumerate(dw_refs):
         source = jnp.bitwise_xor(place, d)
         for i, side in enumerate((half, 1 - half)):
@@ -379,54 +335,45 @@
 
     kept, received = cross_cotangents(d_out, n)
     each = n // 2
-    hbm = pl.BlockSpec(memory_space=pltpu.HBM)
-    *w_out, k_head, v_head = call(
-        pack_weight_kernel,
-        [shape((depth, 2 * HD), BF16)] * each + [shape((text, HD), BF16)] * 2,
-        [out_weight, k_txt, v_txt],
-        specs=[hbm] * 3,
-        out_specs=[hbm] * (each + 2),
-        scratch=[pltpu.SemaphoreType.DMA((each, 2)), pltpu.SemaphoreType.DMA((2,))],
+    big = 60 * 1024 * 1024
+    head = pl.BlockSpec((text, HD), lambda i, me_ref: (0, me_ref[0]))
+    *w_out, text_head = call(
+        lambda me_ref, *refs: pack_weight_kernel(*refs),
+        [shape((depth, 2 * HD), BF16)] * each + [shape((2, text, HD), BF16)],
+        [lax.axis_index("seq").astype(jnp.int32)[None], out_weight, k_txt, v_txt],
+        specs=[vmem, head, head],
+        scalars=1,
         moved=4 * depth * width,
-        limit=60 * 1024 * 1024,
+        limit=big,
     )
     w_in = [w_out[0]] + [exchange(w_out[d], d) for d in range(1, each)]
     (tok_out,) = call(
         pack_kernel,
         [shape((n, 3 * rows, HD), BF16)],
         [q_img, k_img, v_img],
-        specs=[hbm] * 3,
-        out_specs=[hbm],
-        scratch=[pltpu.SemaphoreType.DMA((3, n))],
         moved=4 * 3 * rows * width,
-        limit=60 * 1024 * 1024,
+        limit=big,
     )
     tok_out, received = lax.optimization_barrier((tok_out, received))
     received, w_in = lax.optimization_barrier((received, w_in))
     pieces = gather_cotangents(kept, received, n)
     tok_in = lax.all_to_all(tok_out, "seq", split_axis=0, concat_axis=0, tiled=True)
 
-    probs, out_t = call(
+    probs, out_t, queries, keys_t, vals = call(
         functools.partial(forward_kernel, chunk=chunk),
-        [shape((total, image), BF16), shape((HD, image), BF16)],
-        [tok_in, k_head, v_head],
+        [shape(dims, BF16) for dims in ((total, image), (HD, image), (image, HD), (HD, total), (total, HD))],
+        [tok_in, text_head],
         scratch=[pltpu.VMEM((total, HD), BF16), pltpu.VMEM((HD, total), BF16)],
         flops=4 * total * image * HD,
         moved=4 * total * image,
     )
-    count = len(pieces)
+    out_other = exchange(out_t, each)
     half_width = d_out.shape[1] // 2
-    out_other = exchange(out_t, each)
     mine, theirs, cot = call(
-        functools.partial(partial_kernel, count=count),
+        functools.partial(partial_kernel, count=len(pieces)),
         [shape((image, HD), F32), shape((image, HD), BF16), shape((image, half_width), BF16)],
         [*pieces, *w_in],
-        specs=[hbm] * (count + each),
-        scratch=[
-            pltpu.VMEM((half_width, 2 * HD), BF16),
-            pltpu.SemaphoreType.DMA((2 * count,)),
-            pltpu.SemaphoreType.DMA((each,)),
-        ],
+        scratch=[pltpu.VMEM((half_width, 2 * HD), BF16)],
         flops=4 * image * half_width * HD,
         moved=2 * image * half_width,
     )
@@ -434,14 +381,8 @@
     (grad_out,) = call(
         functools.partial(backward_kernel, chunk=chunk),
         [shape((n, 3 * rows, HD), BF16)],
-        [tok_in, k_head, v_head, probs, out_t, mine, theirs],
-
-        scratch=[
-            pltpu.VMEM((HD, total), BF16),
-            pltpu.VMEM((total, HD), BF16),
-            pltpu.VMEM((image, HD), F32),
-            pltpu.VMEM((image, HD), F32),
-        ],
+        [queries, keys_t, vals, probs, out_t, mine, theirs],
+        scratch=[pltpu.VMEM((image, HD), F32), pltpu.VMEM((image, HD), F32)],
         flops=8 * total * image * HD,
         moved=4 * total * image,
     )
@@ -456,14 +397,19 @@
         moved=2 * image * half_width,
     )
     dw_in = [dw_out[0]] + [exchange(dw_out[d], d) for d in range(1, each)]
-    return tuple(
-        call(
-            unpack_kernel,
-            [shape((rows, width), BF16)] * 3 + [shape((depth, width), F32)],
-            [grad_in, *dw_in],
-            moved=4 * 3 * rows * width + 6 * depth * width,
-        )
-    )
+    grads = call(
+        unpack_kernel,
+        [shape((rows, width), BF16)] * 3,
+        [grad_in],
+        moved=4 * 3 * rows * width,
+    )
+    (d_weight,) = call(
+        unpack_weight_kernel,
+        [shape((depth, width), F32)],
+        dw_in,
+        moved=6 * depth * width,
+    )
+    return (*grads, d_weight)
 
 
 def solution(mesh):

time: 174 us -> 132 us (0.76)
  Pallas kernels: 81.2 us -> 22.5 us
  waiting for transfers between devices: 55.1 us -> 72.1 us
  local copies, waits for them, and re-layouts: 9.77 us -> 7.37 us
  starting transfers between devices: 26.6 us -> 28.5 us
    pallas_call x7 -> x8, Pallas kernels: 81.2 us -> 22.5 us  [call(): pl.pallas_call(kernel, out_shape=outs, grid_spec=pltpu.PrefetchScalarGrid...]
    ppermute x16, waiting for transfers between devices: 55.1 us -> 72.1 us  [exchange(): return lax.ppermute(array, ('seq', 'fsdp'), pairs)]
    unnamed x22 -> x14, local copies, waits for them, and re-layouts: 8.71 us -> 6.32 us
  transfers between devices with their start and end apart: 18 -> 18, of which waited for: 12 -> 13; matrix products, arithmetic and copies ran while one was open for 0% -> 0% of each run, Pallas kernels for 45% -> 15%
where the time goes in v6:
time: 132 us; the launch traced here: 131 us
  waiting for transfers between devices  72.1 us (55%)
  starting transfers between devices  28.5 us (22%)
  Pallas kernels  22.5 us (17%)
  local copies, waits for them, and re-layouts  7.37 us (6%)
    ppermute x16, waiting for transfers between devices, exchange(): return lax.ppermute(array, ('seq', 'fsdp'), pairs)  72.1 us
    pallas_call x8, Pallas kernels, call(): pl.pallas_call(kernel, out_shape=outs, grid_spec=pltpu.PrefetchScalarGrid...  22.5 us
    ppermute x16, starting transfers between devices, exchange(): return lax.ppermute(array, ('seq', 'fsdp'), pairs)  17.8 us
    unnamed x14, local copies, waits for them, and re-layouts  6.32 us
    all_to_all x1, starting transfers between devices, local(): lax.all_to_all(tok_out, 'seq', split_axis=0, concat_axis=0, tiled=True)  5.77 us
    all_to_all x1, starting transfers between devices, local(): lax.all_to_all(grad_out, 'seq', split_axis=0, concat_axis=0, tiled=True)  4.9 us
  transfers between devices with their start and end apart: 18, of which 13 were waited for; matrix products, arithmetic and copies ran while one was open for 0% of the time, Pallas kernels for 15%

profile of v6, /device:TPU:0, one launch (start us, length us, event | category | flops | bytes accessed | tf_op | source)
XLA Modules:
  0.0 131.2 jit_solution(7882672744340784800)
XLA Ops:
  0.7 1.1 fusion
  1.7 4.1 %collective-permute-start = (bf16[64,1536]{1,0:T(8,128)(2,1)S(1)}, bf16[64,1536]{1,0:T(8,128)(2,1)S(1)}, u32[]{:S(2)}, u32[]{:S(2)}) collective-permute-start(bf16[64,1536]{1,0:T(8,128)(2,1)S(1)} %get-tuple-element.63), channel_id=1, source_target_pairs={{0,8},{1,9},{2,10},{3,11},{4,12},{5,13},{6,14},{7,15},{8,0},{9,1},... | collective-permute-start | bytes 589832 | tf_op jit(solution)/shard_map/ppermute | solution.py:303
  5.8 2.1 %shard_map.102 = bf16[8,384,128]{2,1,0:T(8,128)(2,1)} custom-call(bf16[128,1024]{1,0:T(8,128)(2,1)} %q_ref.1, bf16[128,1024]{1,0:T(8,128)(2,1)} %k_ref.1, bf16[128,1024]{1,0:T(8,128)(2,1)} %v_ref.1), custom_call_target="tpu_custom_call" | custom-call | bytes 1572864 | tf_op jit(solution)/shard_map/pallas_call | solution.py:147
  7.9 7.0 %collective-permute-done = bf16[64,1536]{1,0:T(8,128)(2,1)S(1)} collective-permute-done((bf16[64,1536]{1,0:T(8,128)(2,1)S(1)}, bf16[64,1536]{1,0:T(8,128)(2,1)S(1)}, u32[]{:S(2)}, u32[]{:S(2)}) %collective-permute-start) | collective-permute-done | bytes 196640 | tf_op jit(solution)/shard_map/ppermute | solution.py:303
  14.9 5.8 %all-to-all-start = ((bf16[8,384,128]{2,1,0:T(8,128)(2,1)}), bf16[8,384,128]{2,1,0:T(8,128)(2,1)}, u32[]{:S(2)}, u32[]{:S(2)}) async-start(bf16[8,384,128]{2,1,0:T(8,128)(2,1)} %shard_map.102), calls=%async_computation | async-start | bytes 1572864 | tf_op jit(solution)/shard_map/all_to_all | solution.py:360
  20.7 2.4 %shard_map.103 = (bf16[384,256]{1,0:T(8,128)(2,1)}, bf16[384,256]{1,0:T(8,128)(2,1)}, bf16[384,256]{1,0:T(8,128)(2,1)}, bf16[384,256]{1,0:T(8,128)(2,1)}, bf16[2,512,128]{2,1,0:T(8,128)(2,1)}) custom-call(s32[1]{0:T(128)} %bitcast.me_ref, bf16[384,1024]{1,0:T(8,128)(2,1)} %refs_0_.1, bf16[512,1024]{1,0:T(8,128)(2,1)} %refs_1_.1, bf16[512,1024]{1,0:T(8,128)(2,1)} %refs_2_.1), custom_call_target="tpu_custom_call" | custom-call | bytes 1572864 | tf_op jit(solution)/shard_map/pallas_call | solution.py:147
  23.1 2.0 %collective-permute-start.1 = (bf16[384,256]{1,0:T(8,128)(2,1)}, bf16[384,256]{1,0:T(8,128)(2,1)S(1)}, u32[]{:S(2)}, u32[]{:S(2)}) collective-permute-start(bf16[384,256]{1,0:T(8,128)(2,1)} %get-tuple-element.42), channel_id=1, source_target_pairs={{0,2},{1,3},{2,0},{3,1},{4,6},{5,7},{6,4},{7,5},{8,10},{9,11},{10,... | collective-permute-start | bytes 589832 | tf_op jit(solution)/shard_map/ppermute | solution.py:303
  25.1 1.5 %collective-permute-start.2 = (bf16[384,256]{1,0:T(8,128)(2,1)}, bf16[384,256]{1,0:T(8,128)(2,1)S(1)}, u32[]{:S(2)}, u32[]{:S(2)}) collective-permute-start(bf16[384,256]{1,0:T(8,128)(2,1)} %get-tuple-element.43), channel_id=1, source_target_pairs={{0,4},{1,5},{2,6},{3,7},{4,0},{5,1},{6,2},{7,3},{8,12},{9,13},{10,... | collective-permute-start | bytes 589832 | tf_op jit(solution)/shard_map/ppermute | solution.py:303
  26.6 0.0 collective-permute-start.3
  26.6 8.1 %collective-permute-done.1.refs_9_ = bf16[384,256]{1,0:T(8,128)(2,1)S(1)} collective-permute-done((bf16[384,256]{1,0:T(8,128)(2,1)}, bf16[384,256]{1,0:T(8,128)(2,1)S(1)}, u32[]{:S(2)}, u32[]{:S(2)}) %collective-permute-start.1) | collective-permute-done | bytes 196640 | tf_op jit(solution)/shard_map/ppermute | solution.py:303
  34.7 4.2 %collective-permute-done.2.refs_10_ = bf16[384,256]{1,0:T(8,128)(2,1)S(1)} collective-permute-done((bf16[384,256]{1,0:T(8,128)(2,1)}, bf16[384,256]{1,0:T(8,128)(2,1)S(1)}, u32[]{:S(2)}, u32[]{:S(2)}) %collective-permute-start.2) | collective-permute-done | bytes 196640 | tf_op jit(solution)/shard_map/ppermute | solution.py:303
  38.9 6.3 %collective-permute-done.3.refs_11_ = bf16[384,256]{1,0:T(8,128)(2,1)S(1)} collective-permute-done((bf16[384,256]{1,0:T(8,128)(2,1)}, bf16[384,256]{1,0:T(8,128)(2,1)S(1)}, u32[]{:S(2)}, u32[]{:S(2)}) %collective-permute-start.3) | collective-permute-done | bytes 196640 | tf_op jit(solution)/shard_map/ppermute | solution.py:303
  45.2 0.3 collective-permute-start.6
  45.6 1.8 %collective-permute-start.5 = (bf16[128,1536]{1,0:T(8,128)(2,1)S(1)}, bf16[128,1536]{1,0:T(8,128)(2,1)S(1)}, u32[]{:S(2)}, u32[]{:S(2)}) collective-permute-start(bf16[128,1536]{1,0:T(8,128)(2,1)S(1)} %pad_maximum_fusion.refs_0_), channel_id=1, source_target_pairs={{0,4},{1,5},{2,6},{3,7},{4,0},{5,1},{6,2},{7,3},{8,12},{9,13},{10,... | collective-permute-start | bytes 1179656 | tf_op jit(solution)/shard_map/ppermute | solution.py:303
  47.4 1.4 %collective-permute-start.4 = (bf16[128,1536]{1,0:T(8,128)(2,1)S(1)}, bf16[128,1536]{1,0:T(8,128)(2,1)S(1)}, u32[]{:S(2)}, u32[]{:S(2)}) collective-permute-start(bf16[128,1536]{1,0:T(8,128)(2,1)S(1)} %pad_maximum_fusion.refs_0_), channel_id=1, source_target_pairs={{0,2},{1,3},{2,0},{3,1},{4,6},{5,7},{6,4},{7,5},{8,10},{9,11},{10,... | collective-permute-start | bytes 1179656 | tf_op jit(solution)/shard_map/ppermute | solution.py:303
  48.8 0.0 collective-permute-start.7
  48.8 9.5 %collective-permute-done.6.refs_3_ = bf16[128,1536]{1,0:T(8,128)(2,1)S(1)} collective-permute-done((bf16[128,1536]{1,0:T(8,128)(2,1)S(1)}, bf16[128,1536]{1,0:T(8,128)(2,1)S(1)}, u32[]{:S(2)}, u32[]{:S(2)}) %collective-permute-start.6) | collective-permute-done | bytes 393248 | tf_op jit(solution)/shard_map/ppermute | solution.py:303
  58.3 0.0 collective-permute-start.10
  58.3 5.8 %collective-permute-done.5.refs_2_ = bf16[128,1536]{1,0:T(8,128)(2,1)S(1)} collective-permute-done((bf16[128,1536]{1,0:T(8,128)(2,1)S(1)}, bf16[128,1536]{1,0:T(8,128)(2,1)S(1)}, u32[]{:S(2)}, u32[]{:S(2)}) %collective-permute-start.5) | collective-permute-done | bytes 393248 | tf_op jit(solution)/shard_map/ppermute | solution.py:303
  64.1 0.0 collective-permute-start.9
  64.1 0.7 collective-permute-done.4.refs_1_
  64.7 0.0 collective-permute-start.8
  64.8 1.0 collective-permute-done.9.refs_6_
  65.8 0.7 collective-permute-done.8.refs_5_
  66.5 0.9 copy-done.5
  67.4 2.5 %shard_map.105 = (f32[1024,128]{1,0:T(8,128)S(1)}, bf16[1024,128]{1,0:T(8,128)(2,1)}, bf16[1024,1536]{1,0:T(8,128)(2,1)S(1)}) custom-call(bf16[128,1536]{1,0:T(8,128)(2,1)S(1)} %pad_maximum_fusion.refs_0_, bf16[128,1536]{1,0:T(8,128)(2,1)S(1)} %collective-permute-done.4.refs_1_, bf16[128,1536]{1,0:T(8,128)(2,1)S(1)} %collective-permute-done.5.refs_2_, ...), custom_call_target="tpu_custom_call" | custom-call | flops 805306368 | bytes 3145728 | tf_op jit(solution)/shard_map/pallas_call | solution.py:147
  69.9 0.8 copy-done.1
  70.7 2.2 %collective-permute-start.11 = (bf16[1024,128]{1,0:T(8,128)(2,1)}, bf16[1024,128]{1,0:T(8,128)(2,1)}, u32[]{:S(2)}, u32[]{:S(2)}) collective-permute-start(bf16[1024,128]{1,0:T(8,128)(2,1)} %get-tuple-element.51), channel_id=1, source_target_pairs={{0,8},{1,9},{2,10},{3,11},{4,12},{5,13},{6,14},{7,15},{8,0},{9,1},... | collective-permute-start | bytes 786440 | tf_op jit(solution)/shard_map/ppermute | solution.py:303
  72.9 0.9 copy-done.6
  73.8 6.0 %shard_map.104 = (bf16[1536,1024]{1,0:T(8,128)(2,1)S(1)}, bf16[128,1024]{1,0:T(8,128)(2,1)S(1)}, bf16[1024,128]{1,0:T(8,128)(2,1)S(1)}, bf16[128,1536]{1,0:T(8,128)(2,1)S(1)}, bf16[1536,128]{1,0:T(8,128)(2,1)S(1)}) custom-call(bf16[8,384,128]{2,1,0:T(8,128)(2,1)} %all-to-all-done.tok_ref, bf16[2,512,128]{2,1,0:T(8,128)(2,1)S(1)} %copy-done.6), custom_call_target="tpu_custom_call" | custom-call | flops 805306368 | bytes 6291456 | tf_op jit(solution)/shard_map/pallas_call | solution.py:147
  79.9 0.8 collective-permute-start.12
  80.7 11.0 %collective-permute-done.11.theirs_ref = bf16[1024,128]{1,0:T(8,128)(2,1)} collective-permute-done((bf16[1024,128]{1,0:T(8,128)(2,1)}, bf16[1024,128]{1,0:T(8,128)(2,1)}, u32[]{:S(2)}, u32[]{:S(2)}) %collective-permute-start.11) | collective-permute-done | bytes 262176 | tf_op jit(solution)/shard_map/ppermute | solution.py:303
  91.6 1.0 copy-done.2
  92.7 4.5 %shard_map.106 = bf16[8,384,128]{2,1,0:T(8,128)(2,1)S(1)} custom-call(bf16[1024,128]{1,0:T(8,128)(2,1)S(1)} %get-tuple-element.35.queries_ref, bf16[128,1536]{1,0:T(8,128)(2,1)S(1)} %get-tuple-element.36.keys_t_ref, bf16[1536,128]{1,0:T(8,128)(2,1)S(1)} %get-tuple-element.37.vals_ref, bf16[1536,1024]{1,0:T(8,128)(2,1)S(1)} %get-tuple-element.38.probs_ref, ...), custom_call_target="tpu_custom_call" | custom-call | flops 1610612736 | bytes 6291456 | tf_op jit(solution)/shard_map/pallas_call | solution.py:147
  97.2 0.9 copy-done
  98.1 0.7 copy-done.3
  98.8 4.9 %all-to-all-start.1 = ((bf16[8,384,128]{2,1,0:T(8,128)(2,1)}), bf16[8,384,128]{2,1,0:T(8,128)(2,1)}, u32[]{:S(2)}, u32[]{:S(2)}) async-start(bf16[8,384,128]{2,1,0:T(8,128)(2,1)} %copy-done), calls=%async_computation.1 | async-start | bytes 1572864 | tf_op jit(solution)/shard_map/all_to_all | solution.py:390
  103.7 0.9 copy-done.4
  104.7 1.3 shard_map.108
  105.9 2.1 %collective-permute-start.13 = (bf16[256,384]{1,0:T(8,128)(2,1)S(1)}, bf16[256,384]{1,0:T(8,128)(2,1)S(1)}, u32[]{:S(2)}, u32[]{:S(2)}) collective-permute-start(bf16[256,384]{1,0:T(8,128)(2,1)S(1)} %get-tuple-element.59), channel_id=1, source_target_pairs={{0,2},{1,3},{2,0},{3,1},{4,6},{5,7},{6,4},{7,5},{8,10},{9,11},{10,... | collective-permute-start | bytes 589832 | tf_op jit(solution)/shard_map/ppermute | solution.py:303
  108.0 1.5 %collective-permute-start.14 = (bf16[256,384]{1,0:T(8,128)(2,1)S(1)}, bf16[256,384]{1,0:T(8,128)(2,1)S(1)}, u32[]{:S(2)}, u32[]{:S(2)}) collective-permute-start(bf16[256,384]{1,0:T(8,128)(2,1)S(1)} %get-tuple-element.60), channel_id=1, source_target_pairs={{0,4},{1,5},{2,6},{3,7},{4,0},{5,1},{6,2},{7,3},{8,12},{9,13},{10,... | collective-permute-start | bytes 589832 | tf_op jit(solution)/shard_map/ppermute | solution.py:303
  109.5 0.1 collective-permute-start.15
  109.6 8.4 %collective-permute-done.13.refs_1_ = bf16[256,384]{1,0:T(8,128)(2,1)S(1)} collective-permute-done((bf16[256,384]{1,0:T(8,128)(2,1)S(1)}, bf16[256,384]{1,0:T(8,128)(2,1)S(1)}, u32[]{:S(2)}, u32[]{:S(2)}) %collective-permute-start.13) | collective-permute-done | bytes 196640 | tf_op jit(solution)/shard_map/ppermute | solution.py:303
  118.0 4.0 %collective-permute-done.14.refs_2_ = bf16[256,384]{1,0:T(8,128)(2,1)S(1)} collective-permute-done((bf16[256,384]{1,0:T(8,128)(2,1)S(1)}, bf16[256,384]{1,0:T(8,128)(2,1)S(1)}, u32[]{:S(2)}, u32[]{:S(2)}) %collective-permute-start.14) | collective-permute-done | bytes 196640 | tf_op jit(solution)/shard_map/ppermute | solution.py:303
  122.0 5.5 %collective-permute-done.15.refs_3_ = bf16[256,384]{1,0:T(8,128)(2,1)S(1)} collective-permute-done((bf16[256,384]{1,0:T(8,128)(2,1)S(1)}, bf16[256,384]{1,0:T(8,128)(2,1)S(1)}, u32[]{:S(2)}, u32[]{:S(2)}) %collective-permute-start.15) | collective-permute-done | bytes 196640 | tf_op jit(solution)/shard_map/ppermute | solution.py:303
  127.5 1.5 %shard_map.109 = f32[384,1024]{1,0:T(8,128)} custom-call(bf16[256,384]{1,0:T(8,128)(2,1)S(1)} %get-tuple-element.58.refs_0_, bf16[256,384]{1,0:T(8,128)(2,1)S(1)} %collective-permute-done.13.refs_1_, bf16[256,384]{1,0:T(8,128)(2,1)S(1)} %collective-permute-done.14.refs_2_, bf16[256,384]{1,0:T(8,128)(2,1)S(1)} %collective-permute-done.15.refs_3_), custom_call_target="tpu_custom_call" | custom-call | bytes 2359296 | tf_op jit(solution)/shard_map/pallas_call | solution.py:147
  129.0 0.0 all-to-all-done.1.tok_ref
  129.0 2.2 %shard_map.107 = (bf16[128,1024]{1,0:T(8,128)(2,1)}, bf16[128,1024]{1,0:T(8,128)(2,1)}, bf16[128,1024]{1,0:T(8,128)(2,1)}) custom-call(bf16[8,384,128]{2,1,0:T(8,128)(2,1)} %all-to-all-done.1.tok_ref), custom_call_target="tpu_custom_call" | custom-call | bytes 1572864 | tf_op jit(solution)/shard_map/pallas_call | solution.py:147
  (12 shorter events, 0.0 us)
Async XLA Ops:
  1.7 13.2 %collective-permute-start = (bf16[64,1536]{1,0:T(8,128)(2,1)S(1)}, bf16[64,1536]{1,0:T(8,128)(2,1)S(1)}, u32[]{:S(2)}, u32[]{:S(2)}) collective-permute-start(bf16[64,1536]{1,0:T(8,128)(2,1)S(1)} %get-tuple-element.63), channel_id=1, source_target_pairs={{0,8},{1,9},{2,10},{3,11},{4,12},{5,13},{6,14},{7,15},{8,0},{9,1},... | collective-permute-start | bytes 589832 | tf_op jit(solution)/shard_map/ppermute | solution.py:303
  14.9 58.0 %all-to-all-start = ((bf16[8,384,128]{2,1,0:T(8,128)(2,1)}), bf16[8,384,128]{2,1,0:T(8,128)(2,1)}, u32[]{:S(2)}, u32[]{:S(2)}) async-start(bf16[8,384,128]{2,1,0:T(8,128)(2,1)} %shard_map.102), calls=%async_computation | async-start | bytes 1572864 | tf_op jit(solution)/shard_map/all_to_all | solution.py:360
  23.1 11.6 %collective-permute-start.1 = (bf16[384,256]{1,0:T(8,128)(2,1)}, bf16[384,256]{1,0:T(8,128)(2,1)S(1)}, u32[]{:S(2)}, u32[]{:S(2)}) collective-permute-start(bf16[384,256]{1,0:T(8,128)(2,1)} %get-tuple-element.42), channel_id=1, source_target_pairs={{0,2},{1,3},{2,0},{3,1},{4,6},{5,7},{6,4},{7,5},{8,10},{9,11},{10,... | collective-permute-start | bytes 589832 | tf_op jit(solution)/shard_map/ppermute | solution.py:303
  25.1 13.8 %collective-permute-start.2 = (bf16[384,256]{1,0:T(8,128)(2,1)}, bf16[384,256]{1,0:T(8,128)(2,1)S(1)}, u32[]{:S(2)}, u32[]{:S(2)}) collective-permute-start(bf16[384,256]{1,0:T(8,128)(2,1)} %get-tuple-element.43), channel_id=1, source_target_pairs={{0,4},{1,5},{2,6},{3,7},{4,0},{5,1},{6,2},{7,3},{8,12},{9,13},{10,... | collective-permute-start | bytes 589832 | tf_op jit(solution)/shard_map/ppermute | solution.py:303
  26.6 18.6 %collective-permute-start.3 = (bf16[384,256]{1,0:T(8,128)(2,1)}, bf16[384,256]{1,0:T(8,128)(2,1)S(1)}, u32[]{:S(2)}, u32[]{:S(2)}) collective-permute-start(bf16[384,256]{1,0:T(8,128)(2,1)} %get-tuple-element.44), channel_id=1, source_target_pairs={{0,6},{1,7},{2,4},{3,5},{4,2},{5,3},{6,0},{7,1},{8,14},{9,15},{10,... | collective-permute-start | bytes 589832 | tf_op jit(solution)/shard_map/ppermute | solution.py:303
  45.2 13.1 %collective-permute-start.6 = (bf16[128,1536]{1,0:T(8,128)(2,1)S(1)}, bf16[128,1536]{1,0:T(8,128)(2,1)S(1)}, u32[]{:S(2)}, u32[]{:S(2)}) collective-permute-start(bf16[128,1536]{1,0:T(8,128)(2,1)S(1)} %pad_maximum_fusion.refs_0_), channel_id=1, source_target_pairs={{0,6},{1,7},{2,4},{3,5},{4,2},{5,3},{6,0},{7,1},{8,14},{9,15},{10,... | collective-permute-start | bytes 1179656 | tf_op jit(solution)/shard_map/ppermute | solution.py:303
  45.6 18.5 %collective-permute-start.5 = (bf16[128,1536]{1,0:T(8,128)(2,1)S(1)}, bf16[128,1536]{1,0:T(8,128)(2,1)S(1)}, u32[]{:S(2)}, u32[]{:S(2)}) collective-permute-start(bf16[128,1536]{1,0:T(8,128)(2,1)S(1)} %pad_maximum_fusion.refs_0_), channel_id=1, source_target_pairs={{0,4},{1,5},{2,6},{3,7},{4,0},{5,1},{6,2},{7,3},{8,12},{9,13},{10,... | collective-permute-start | bytes 1179656 | tf_op jit(solution)/shard_map/ppermute | solution.py:303
  47.4 17.4 %collective-permute-start.4 = (bf16[128,1536]{1,0:T(8,128)(2,1)S(1)}, bf16[128,1536]{1,0:T(8,128)(2,1)S(1)}, u32[]{:S(2)}, u32[]{:S(2)}) collective-permute-start(bf16[128,1536]{1,0:T(8,128)(2,1)S(1)} %pad_maximum_fusion.refs_0_), channel_id=1, source_target_pairs={{0,2},{1,3},{2,0},{3,1},{4,6},{5,7},{6,4},{7,5},{8,10},{9,11},{10,... | collective-permute-start | bytes 1179656 | tf_op jit(solution)/shard_map/ppermute | solution.py:303
  48.8 16.0 %collective-permute-start.7 = (bf16[128,1536]{1,0:T(8,128)(2,1)S(1)}, bf16[128,1536]{1,0:T(8,128)(2,1)S(1)}, u32[]{:S(2)}, u32[]{:S(2)}) collective-permute-start(bf16[128,1536]{1,0:T(8,128)(2,1)S(1)} %pad_maximum_fusion.refs_0_), channel_id=1, source_target_pairs={{0,1},{1,0},{2,3},{3,2},{4,5},{5,4},{6,7},{7,6},{8,9},{9,8},{10,11... | collective-permute-start | bytes 1179656 | tf_op jit(solution)/shard_map/ppermute | solution.py:303
  58.3 6.5 %collective-permute-start.10 = (bf16[128,1536]{1,0:T(8,128)(2,1)S(1)}, bf16[128,1536]{1,0:T(8,128)(2,1)S(1)}, u32[]{:S(2)}, u32[]{:S(2)}) collective-permute-start(bf16[128,1536]{1,0:T(8,128)(2,1)S(1)} %collective-permute-done.6.refs_3_), channel_id=1, source_target_pairs={{0,1},{1,0},{2,3},{3,2},{4,5},{5,4},{6,7},{7,6},{8,9},{9,8},{10,11... | collective-permute-start | bytes 1179656 | tf_op jit(solution)/shard_map/ppermute | solution.py:303
  64.1 1.7 %collective-permute-start.9 = (bf16[128,1536]{1,0:T(8,128)(2,1)S(1)}, bf16[128,1536]{1,0:T(8,128)(2,1)S(1)}, u32[]{:S(2)}, u32[]{:S(2)}) collective-permute-start(bf16[128,1536]{1,0:T(8,128)(2,1)S(1)} %collective-permute-done.5.refs_2_), channel_id=1, source_target_pairs={{0,1},{1,0},{2,3},{3,2},{4,5},{5,4},{6,7},{7,6},{8,9},{9,8},{10,11... | collective-permute-start | bytes 1179656 | tf_op jit(solution)/shard_map/ppermute | solution.py:303
  64.7 1.7 %collective-permute-start.8 = (bf16[128,1536]{1,0:T(8,128)(2,1)S(1)}, bf16[128,1536]{1,0:T(8,128)(2,1)S(1)}, u32[]{:S(2)}, u32[]{:S(2)}) collective-permute-start(bf16[128,1536]{1,0:T(8,128)(2,1)S(1)} %collective-permute-done.4.refs_1_), channel_id=1, source_target_pairs={{0,1},{1,0},{2,3},{3,2},{4,5},{5,4},{6,7},{7,6},{8,9},{9,8},{10,11... | collective-permute-start | bytes 1179656 | tf_op jit(solution)/shard_map/ppermute | solution.py:303
  66.5 0.9 copy-start.5
  69.8 0.8 copy-start.1
  70.7 20.9 %collective-permute-start.11 = (bf16[1024,128]{1,0:T(8,128)(2,1)}, bf16[1024,128]{1,0:T(8,128)(2,1)}, u32[]{:S(2)}, u32[]{:S(2)}) collective-permute-start(bf16[1024,128]{1,0:T(8,128)(2,1)} %get-tuple-element.51), channel_id=1, source_target_pairs={{0,8},{1,9},{2,10},{3,11},{4,12},{5,13},{6,14},{7,15},{8,0},{9,1},... | collective-permute-start | bytes 786440 | tf_op jit(solution)/shard_map/ppermute | solution.py:303
  72.9 1.0 copy-start.6
  79.9 18.2 %collective-permute-start.12 = (bf16[128,1024]{1,0:T(8,128)(2,1)S(1)}, bf16[128,1024]{1,0:T(8,128)(2,1)S(1)}, u32[]{:S(2)}, u32[]{:S(2)}) collective-permute-start(bf16[128,1024]{1,0:T(8,128)(2,1)S(1)} %get-tuple-element.39.out_ref.mine_ref), channel_id=1, source_target_pairs={{0,8},{1,9},{2,10},{3,11},{4,12},{5,13},{6,14},{7,15},{8,0},{9,1},... | collective-permute-start | bytes 786440 | tf_op jit(solution)/shard_map/ppermute | solution.py:303
  91.6 1.0 copy-start.2
  97.2 0.9 copy-start
  98.1 0.7 copy-start.3
  98.8 30.2 %all-to-all-start.1 = ((bf16[8,384,128]{2,1,0:T(8,128)(2,1)}), bf16[8,384,128]{2,1,0:T(8,128)(2,1)}, u32[]{:S(2)}, u32[]{:S(2)}) async-start(bf16[8,384,128]{2,1,0:T(8,128)(2,1)} %copy-done), calls=%async_computation.1 | async-start | bytes 1572864 | tf_op jit(solution)/shard_map/all_to_all | solution.py:390
  103.7 0.9 copy-start.4
  105.9 12.1 %collective-permute-start.13 = (bf16[256,384]{1,0:T(8,128)(2,1)S(1)}, bf16[256,384]{1,0:T(8,128)(2,1)S(1)}, u32[]{:S(2)}, u32[]{:S(2)}) collective-permute-start(bf16[256,384]{1,0:T(8,128)(2,1)S(1)} %get-tuple-element.59), channel_id=1, source_target_pairs={{0,2},{1,3},{2,0},{3,1},{4,6},{5,7},{6,4},{7,5},{8,10},{9,11},{10,... | collective-permute-start | bytes 589832 | tf_op jit(solution)/shard_map/ppermute | solution.py:303
  108.0 14.0 %collective-permute-start.14 = (bf16[256,384]{1,0:T(8,128)(2,1)S(1)}, bf16[256,384]{1,0:T(8,128)(2,1)S(1)}, u32[]{:S(2)}, u32[]{:S(2)}) collective-permute-start(bf16[256,384]{1,0:T(8,128)(2,1)S(1)} %get-tuple-element.60), channel_id=1, source_target_pairs={{0,4},{1,5},{2,6},{3,7},{4,0},{5,1},{6,2},{7,3},{8,12},{9,13},{10,... | collective-permute-start | bytes 589832 | tf_op jit(solution)/shard_map/ppermute | solution.py:303
  109.5 18.0 %collective-permute-start.15 = (bf16[256,384]{1,0:T(8,128)(2,1)S(1)}, bf16[256,384]{1,0:T(8,128)(2,1)S(1)}, u32[]{:S(2)}, u32[]{:S(2)}) collective-permute-start(bf16[256,384]{1,0:T(8,128)(2,1)S(1)} %get-tuple-element.61), channel_id=1, source_target_pairs={{0,6},{1,7},{2,4},{3,5},{4,2},{5,3},{6,0},{7,1},{8,14},{9,15},{10,... | collective-permute-start | bytes 589832 | tf_op jit(solution)/shard_map/ppermute | solution.py:303

commit v7 on v6

--- a/solution.py
+++ b/solution.py
@@ -159,30 +159,24 @@
     )(*args)
 
 
-def halves():
-    each = lax.axis_size("seq") // 2
-    me = lax.axis_index("seq")
-    return me // each, lax.rem(me, each)
-
-
-def pack_kernel(q_ref, k_ref, v_ref, tok_ref):
+STEPS = (0, 2, 4, 6)
+
+
+def head_columns(step, other_row):
+    return pl.ds(pl.multiple_of(jnp.bitwise_xor(lax.axis_index("seq"), step + other_row) * HD, HD), HD)
+
+
+def pack_kernel(me_ref, q_ref, k_ref, v_ref, w_ref, kt_ref, vt_ref, tok_ref, keep_ref, give_ref, text_ref):
     rows = q_ref.shape[0]
     for h in range(tok_ref.shape[0]):
         for i, ref in enumerate((q_ref, k_ref, v_ref)):
             tok_ref[h, i * rows : (i + 1) * rows, :] = ref[:, h * HD : (h + 1) * HD]
-
-
-def pack_weight_kernel(w_ref, kt_ref, vt_ref, *refs):
-    *wt_refs, text_ref = refs
-    half, place = halves()
-    each = len(wt_refs)
+    for i, step in enumerate(STEPS):
+        cols = slice(i * HD, (i + 1) * HD)
+        keep_ref[:, cols] = w_ref[:, head_columns(step, 0)]
+        give_ref[:, cols] = w_ref[:, head_columns(step, 1)]
     text_ref[0] = kt_ref[...]
     text_ref[1] = vt_ref[...]
-    for d, wt_ref in enumerate(wt_refs):
-        to = jnp.bitwise_xor(place, d)
-        for i, side in enumerate((half, 1 - half)):
-            at = pl.multiple_of((side * each + to) * HD, HD)
-            wt_ref[:, i * HD : (i + 1) * HD] = w_ref[:, pl.ds(at, HD)]
 
 
 def forward_kernel(tok_ref, text_ref, probs_ref, out_ref, queries_ref, keys_t_ref, vals_ref, keys, vals_t, *, chunk):
@@ -209,24 +203,22 @@
         out_ref[:, span] = jnp.dot(vals_t[...], low, preferred_element_type=F32).astype(BF16)
 
 
-def partial_kernel(*refs, count):
-    each = count // 2
-    pieces, weights = refs[:count], refs[count : count + each]
-    mine_ref, theirs_ref, cot_ref, weight = refs[count + each :]
-    half, place = halves()
+def partial_kernel(*refs):
+    *pieces, own_ref, other_ref, mine_ref, far_ref, near_ref, near_far_ref, cot_ref, weight = refs
+    me = lax.axis_index("seq")
     core = lax.axis_index("fsdp")
-    rows = pieces[0].shape[0]
-    part = rows // 2
-    for i, piece in enumerate(pieces):
-        source = jnp.bitwise_xor(place, i % each)
-        shift = (core if i < each else 1 - core) * part
-        for j, side in enumerate((half, 1 - half)):
-            at = pl.multiple_of((side * each + source) * rows + shift, 16)
-            cot_ref[pl.ds(at, part), :] = piece[j * part : (j + 1) * part, :]
-    for d, block in enumerate(weights):
-        depth = block.shape[0]
-        at = pl.multiple_of(jnp.bitwise_xor(place, d) * depth, 16)
-        weight[pl.ds(at, depth), :] = block[...]
+    count = len(STEPS)
+    part = pieces[0].shape[0] // count
+    for p, piece in enumerate(pieces):
+        row, swapped = p % 2, p // 2
+        shift = jnp.bitwise_xor(core, swapped) * part
+        for i, step in enumerate(STEPS):
+            at = pl.multiple_of(jnp.bitwise_xor(me, step + row) * (2 * part) + shift, 16)
+            cot_ref[pl.ds(at, part), :] = piece[i * part : (i + 1) * part, :]
+    depth = own_ref.shape[0]
+    y = lax.rem(me, 2)
+    weight[pl.ds(pl.multiple_of(y * depth, 16), depth), :] = own_ref[...]
+    weight[pl.ds(pl.multiple_of((1 - y) * depth, 16), depth), :] = other_ref[...]
     step = 256
 
     @pl.loop(0, cot_ref.shape[0] // step)
@@ -234,22 +226,24 @@
         at = pl.ds(pl.multiple_of(i * step, step), step)
         part = jnp.dot(cot_ref[at, :], weight[...], preferred_element_type=F32)
         mine_ref[at, :] = part[:, :HD]
-        theirs_ref[at, :] = part[:, HD:].astype(BF16)
-
-
-def weight_grad_kernel(cot_ref, mine_ref, theirs_ref, *refs):
-    *dw_refs, outs = refs
-    outs[0:HD, :] = mine_ref[...]
-    outs[HD : 2 * HD, :] = theirs_ref[...]
-    _, place = halves()
-    for d, dw_ref in enumerate(dw_refs):
-        depth = dw_ref.shape[1]
-        at = pl.multiple_of(jnp.bitwise_xor(place, d) * depth, HD)
-        dw_ref[...] = jnp.dot(outs[...], cot_ref[:, pl.ds(at, depth)], preferred_element_type=F32).astype(BF16)
+        near_ref[at, :] = part[:, HD : 2 * HD].astype(BF16)
+        far_ref[at, :] = part[:, 2 * HD : 3 * HD]
+        near_far_ref[at, :] = part[:, 3 * HD :].astype(BF16)
+
+
+def weight_grad_kernel(cot_ref, *refs):
+    *out_refs, own_ref, other_ref, outs = refs
+    for i, ref in enumerate(out_refs):
+        outs[i * HD : (i + 1) * HD, :] = ref[...]
+    depth = own_ref.shape[1]
+    y = lax.rem(lax.axis_index("seq"), 2)
+    for ref, row in ((own_ref, y), (other_ref, 1 - y)):
+        at = pl.multiple_of(row * depth, HD)
+        ref[...] = jnp.dot(outs[...], cot_ref[:, pl.ds(at, depth)], preferred_element_type=F32).astype(BF16)
 
 
 def backward_kernel(
-    queries_ref, keys_t_ref, vals_ref, probs_ref, out_ref, mine_ref, theirs_ref, send_ref, dk, dv, *, chunk
+    queries_ref, keys_t_ref, vals_ref, probs_ref, out_ref, mine_ref, near_ref, far_ref, send_ref, dk, dv, *, chunk
 ):
     n, three, _ = send_ref.shape
     rows = three // 3
@@ -258,7 +252,8 @@
     per = chunk // rows
     for c in range(image // chunk):
         span = slice(c * chunk, (c + 1) * chunk)
-        grads = (mine_ref[span, :] + theirs_ref[span, :].astype(F32)).astype(BF16)
+        grads = mine_ref[span, :] + near_ref[span, :].astype(F32) + far_ref[span, :].astype(F32)
+        grads = grads.astype(BF16)
         row_dot = jnp.sum(
             grads.astype(F32).T * out_ref[:, span].astype(F32), axis=0, keepdims=True
         )
@@ -286,36 +281,31 @@
             ref[:, h * HD : (h + 1) * HD] = tok_ref[h, i * rows : (i + 1) * rows, :]
 
 
-def unpack_weight_kernel(*refs):
-    *dw_refs, w_ref = refs
-    half, place = halves()
-    each = len(dw_refs)
-    for d, dw_ref in enumerate(dw_refs):
-        source = jnp.bitwise_xor(place, d)
-        for i, side in enumerate((half, 1 - half)):
-            at = pl.multiple_of((side * each + source) * HD, HD)
-            w_ref[:, pl.ds(at, HD)] = dw_ref[i * HD : (i + 1) * HD, :].astype(F32).T
+def unpack_weight_kernel(own_ref, other_ref, w_ref):
+    for other_row, ref in enumerate((own_ref, other_ref)):
+        for i, step in enumerate(STEPS):
+            w_ref[:, head_columns(step, other_row)] = ref[i * HD : (i + 1) * HD, :].astype(F32).T
 
 
 def exchange(array, distance=0, cores=False):
+    if not distance and not cores:
+        return array
     size = 2 * lax.axis_size("seq")
     pairs = [(i, i ^ (2 * distance + int(cores))) for i in range(size)]
     return lax.ppermute(array, ("seq", "fsdp"), pairs)
 
 
-def cross_cotangents(d_out, n):
+def gather_cotangents(d_out):
     rows, width = d_out.shape
-    part, columns = rows // 2, width // 2
-    half, _ = halves()
+    part, columns = rows // 2, width // len(STEPS)
+    z = lax.axis_index("seq") // 2
     first = lax.axis_index("fsdp") * part
-    away = lax.dynamic_slice(d_out, (first, (1 - half) * columns), (part, columns))
-    kept = lax.dynamic_slice(d_out, (first, half * columns), (part, columns))
-    return kept, exchange(away, n // 2)
-
-
-def gather_cotangents(kept, received, n):
-    both = jnp.concatenate([kept, received], axis=0)
-    pieces = [both] + [exchange(both, d) for d in range(1, n // 2)]
+    along = [
+        exchange(lax.dynamic_slice(d_out, (first, (z ^ (step // 2)) * columns), (part, columns)), step)
+        for step in STEPS
+    ]
+    row = jnp.concatenate(along, axis=0)
+    pieces = [row, exchange(row, 1)]
     return pieces + [exchange(piece, cores=True) for piece in pieces]
 
 
@@ -323,7 +313,7 @@
     n = lax.axis_size("seq")
     rows, width = q_img.shape
     args = (q_img, k_img, v_img, k_txt, v_txt, out_weight, d_out)
-    if width // HD != n or lax.axis_size("fsdp") != 2 or n < 4 or n & (n - 1) or rows % 32:
+    if n != 2 * len(STEPS) or width // HD != n or lax.axis_size("fsdp") != 2 or rows % 32:
         return local_general(*args)
     depth = out_weight.shape[0]
     image = n * rows
@@ -333,30 +323,18 @@
     shape = jax.ShapeDtypeStruct
     vmem = pl.BlockSpec(memory_space=pltpu.VMEM)
 
-    kept, received = cross_cotangents(d_out, n)
-    each = n // 2
-    big = 60 * 1024 * 1024
     head = pl.BlockSpec((text, HD), lambda i, me_ref: (0, me_ref[0]))
-    *w_out, text_head = call(
-        lambda me_ref, *refs: pack_weight_kernel(*refs),
-        [shape((depth, 2 * HD), BF16)] * each + [shape((2, text, HD), BF16)],
-        [lax.axis_index("seq").astype(jnp.int32)[None], out_weight, k_txt, v_txt],
-        specs=[vmem, head, head],
+    tok_out, keep, give, text_head = call(
+        pack_kernel,
+        [shape((n, 3 * rows, HD), BF16)] + [shape((depth, 4 * HD), BF16)] * 2 + [shape((2, text, HD), BF16)],
+        [lax.axis_index("seq").astype(jnp.int32)[None], q_img, k_img, v_img, out_weight, k_txt, v_txt],
+        specs=[vmem] * 4 + [head] * 2,
         scalars=1,
-        moved=4 * depth * width,
-        limit=big,
-    )
-    w_in = [w_out[0]] + [exchange(w_out[d], d) for d in range(1, each)]
-    (tok_out,) = call(
-        pack_kernel,
-        [shape((n, 3 * rows, HD), BF16)],
-        [q_img, k_img, v_img],
-        moved=4 * 3 * rows * width,
-        limit=big,
-    )
-    tok_out, received = lax.optimization_barrier((tok_out, received))
-    received, w_in = lax.optimization_barrier((received, w_in))
-    pieces = gather_cotangents(kept, received, n)
+        moved=4 * (3 * rows + depth) * width,
+        limit=60 * 1024 * 1024,
+    )
+    given = exchange(give, 1)
+    pieces = gather_cotangents(d_out)
     tok_in = lax.all_to_all(tok_out, "seq", split_axis=0, concat_axis=0, tiled=True)
 
     probs, out_t, queries, keys_t, vals = call(
@@ -367,36 +345,38 @@
         flops=4 * total * image * HD,
         moved=4 * total * image,
     )
-    out_other = exchange(out_t, each)
-    half_width = d_out.shape[1] // 2
-    mine, theirs, cot = call(
-        functools.partial(partial_kernel, count=len(pieces)),
-        [shape((image, HD), F32), shape((image, HD), BF16), shape((image, half_width), BF16)],
-        [*pieces, *w_in],
-        scratch=[pltpu.VMEM((half_width, 2 * HD), BF16)],
-        flops=4 * image * half_width * HD,
-        moved=2 * image * half_width,
-    )
-    theirs = exchange(theirs, each)
+    columns = pieces[0].shape[1]
+    mine, far, near, near_far, cot = call(
+        partial_kernel,
+        [shape((image, HD), F32)] * 2 + [shape((image, HD), BF16)] * 2 + [shape((image, columns), BF16)],
+        [*pieces, keep, given],
+        scratch=[pltpu.VMEM((columns, 4 * HD), BF16)],
+        flops=8 * image * columns * HD,
+        moved=2 * image * columns,
+    )
+    near_far = exchange(near_far, 2)
+    far = exchange((far + near_far.astype(F32)).astype(BF16), 4)
+    near, _ = lax.optimization_barrier((near, near_far))
+    near = exchange(near, 2)
+    out_far = exchange(out_t, 4)
+    outs = [out_t, exchange(out_t, 2), out_far, exchange(out_far, 2)]
     (grad_out,) = call(
         functools.partial(backward_kernel, chunk=chunk),
         [shape((n, 3 * rows, HD), BF16)],
-        [queries, keys_t, vals, probs, out_t, mine, theirs],
+        [queries, keys_t, vals, probs, out_t, mine, near, far],
         scratch=[pltpu.VMEM((image, HD), F32), pltpu.VMEM((image, HD), F32)],
         flops=8 * total * image * HD,
         moved=4 * total * image,
     )
-    grad_out, out_other = lax.optimization_barrier((grad_out, out_other))
     grad_in = lax.all_to_all(grad_out, "seq", split_axis=0, concat_axis=0, tiled=True)
-    dw_out = call(
+    dw_own, dw_other = call(
         weight_grad_kernel,
-        [shape((2 * HD, depth), BF16)] * each,
-        [cot, out_t, out_other],
-        scratch=[pltpu.VMEM((2 * HD, image), BF16)],
-        flops=4 * image * half_width * HD,
-        moved=2 * image * half_width,
-    )
-    dw_in = [dw_out[0]] + [exchange(dw_out[d], d) for d in range(1, each)]
+        [shape((4 * HD, depth), BF16)] * 2,
+        [cot, *outs],
+        scratch=[pltpu.VMEM((4 * HD, image), BF16)],
+        flops=8 * image * columns * HD,
+        moved=2 * image * columns,
+    )
     grads = call(
         unpack_kernel,
         [shape((rows, width), BF16)] * 3,
@@ -406,7 +386,7 @@
     (d_weight,) = call(
         unpack_weight_kernel,
         [shape((depth, width), F32)],
-        dw_in,
+        [dw_own, exchange(dw_other, 1)],
         moved=6 * depth * width,
     )
     return (*grads, d_weight)

time: 132 us -> 126 us (0.955)
  local copies, waits for them, and re-layouts: 7.37 us -> 2.23 us
  Pallas kernels: 22.5 us -> 17.8 us
  starting transfers between devices: 28.5 us -> 31.2 us
  waiting for transfers between devices: 72.1 us -> 73.5 us
    unnamed x14 -> x10, local copies, waits for them, and re-layouts: 6.32 us -> 1.15 us
    pallas_call x8 -> x7, Pallas kernels: 22.5 us -> 17.8 us  [call(): pl.pallas_call(kernel, out_shape=outs, grid_spec=pltpu.PrefetchScalarGrid...]
    all_to_all x1, starting transfers between devices: 4.9 us -> 7.94 us  [local(): lax.all_to_all(grad_out, 'seq', split_axis=0, concat_axis=0, tiled=True)]
    all_to_all x1, starting transfers between devices: 5.77 us -> 4.06 us  [local(): lax.all_to_all(tok_out, 'seq', split_axis=0, concat_axis=0, tiled=True)]
    ppermute x16 -> x14, starting transfers between devices: 17.8 us -> 19.2 us  [exchange(): return lax.ppermute(array, ('seq', 'fsdp'), pairs)]
    ppermute x16 -> x14, waiting for transfers between devices: 72.1 us -> 73.5 us  [exchange(): return lax.ppermute(array, ('seq', 'fsdp'), pairs)]
  transfers between devices with their start and end apart: 18 -> 16, of which waited for: 13 -> 10; matrix products, arithmetic and copies ran while one was open for 0% -> 0% of each run, Pallas kernels for 15% -> 10%
where the time goes in v7:
time: 126 us; the launch traced here: 125 us
  waiting for transfers between devices  73.5 us (58%)
  starting transfers between devices  31.2 us (25%)
  Pallas kernels  17.8 us (14%)
  local copies, waits for them, and re-layouts  2.23 us (2%)
    ppermute x14, waiting for transfers between devices, exchange(): return lax.ppermute(array, ('seq', 'fsdp'), pairs)  73.5 us
    ppermute x14, starting transfers between devices, exchange(): return lax.ppermute(array, ('seq', 'fsdp'), pairs)  19.2 us
    pallas_call x7, Pallas kernels, call(): pl.pallas_call(kernel, out_shape=outs, grid_spec=pltpu.PrefetchScalarGrid...  17.8 us
    all_to_all x1, starting transfers between devices, local(): lax.all_to_all(grad_out, 'seq', split_axis=0, concat_axis=0, tiled=True)  7.94 us
    all_to_all x1, starting transfers between devices, local(): lax.all_to_all(tok_out, 'seq', split_axis=0, concat_axis=0, tiled=True)  4.06 us
  transfers between devices with their start and end apart: 16, of which 10 were waited for; matrix products, arithmetic and copies ran while one was open for 0% of the time, Pallas kernels for 10%

profile of v7, /device:TPU:0, one launch (start us, length us, event | category | flops | bytes accessed | tf_op | source)
XLA Modules:
  0.0 125.5 jit_solution(4371933062053379231)
XLA Ops:
  0.7 1.1 fusion
  1.7 3.1 %collective-permute-start = (bf16[64,768]{1,0:T(8,128)(2,1)S(1)}, bf16[64,768]{1,0:T(8,128)(2,1)S(1)}, u32[]{:S(2)}, u32[]{:S(2)}) collective-permute-start(bf16[64,768]{1,0:T(8,128)(2,1)S(1)} %get-tuple-element.45), channel_id=1, source_target_pairs={{0,4},{1,5},{2,6},{3,7},{4,0},{5,1},{6,2},{7,3},{8,12},{9,13},{10,... | collective-permute-start | bytes 294920 | tf_op jit(solution)/shard_map/ppermute | solution.py:295
  4.8 2.5 %collective-permute-start.2 = (bf16[64,768]{1,0:T(8,128)(2,1)S(1)}, bf16[64,768]{1,0:T(8,128)(2,1)S(1)}, u32[]{:S(2)}, u32[]{:S(2)}) collective-permute-start(bf16[64,768]{1,0:T(8,128)(2,1)S(1)} %get-tuple-element.46), channel_id=1, source_target_pairs={{0,12},{1,13},{2,14},{3,15},{4,8},{5,9},{6,10},{7,11},{8,4},{9,5},... | collective-permute-start | bytes 294920 | tf_op jit(solution)/shard_map/ppermute | solution.py:295
  7.3 0.1 collective-permute-start.1
  7.4 0.2 collective-permute-done
  7.6 5.4 %collective-permute-done.2 = bf16[64,768]{1,0:T(8,128)(2,1)S(1)} collective-permute-done((bf16[64,768]{1,0:T(8,128)(2,1)S(1)}, bf16[64,768]{1,0:T(8,128)(2,1)S(1)}, u32[]{:S(2)}, u32[]{:S(2)}) %collective-permute-start.2) | collective-permute-done | bytes 98336 | tf_op jit(solution)/shard_map/ppermute | solution.py:295
  13.0 3.3 %collective-permute-done.1 = bf16[64,768]{1,0:T(8,128)(2,1)S(1)} collective-permute-done((bf16[64,768]{1,0:T(8,128)(2,1)S(1)}, bf16[64,768]{1,0:T(8,128)(2,1)S(1)}, u32[]{:S(2)}, u32[]{:S(2)}) %collective-permute-start.1) | collective-permute-done | bytes 98336 | tf_op jit(solution)/shard_map/ppermute | solution.py:295
  16.3 1.6 %collective-permute-start.3 = (bf16[256,768]{1,0:T(8,128)(2,1)S(1)}, bf16[256,768]{1,0:T(8,128)(2,1)S(1)}, u32[]{:S(2)}, u32[]{:S(2)}) collective-permute-start(bf16[256,768]{1,0:T(8,128)(2,1)S(1)} %pad_maximum_fusion.refs_0_), channel_id=1, source_target_pairs={{0,2},{1,3},{2,0},{3,1},{4,6},{5,7},{6,4},{7,5},{8,10},{9,11},{10,... | collective-permute-start | bytes 1179656 | tf_op jit(solution)/shard_map/ppermute | solution.py:295
  17.9 2.9 %shard_map.102 = (bf16[8,384,128]{2,1,0:T(8,128)(2,1)}, bf16[384,512]{1,0:T(8,128)(2,1)}, bf16[384,512]{1,0:T(8,128)(2,1)}, bf16[2,512,128]{2,1,0:T(8,128)(2,1)}) custom-call(s32[1]{0:T(128)} %bitcast.me_ref, bf16[128,1024]{1,0:T(8,128)(2,1)} %q_ref.1, bf16[128,1024]{1,0:T(8,128)(2,1)} %k_ref.1, bf16[128,1024]{1,0:T(8,128)(2,1)} %v_ref.1, ...), custom_call_target="tpu_custom_call" | custom-call | bytes 3145728 | tf_op jit(solution)/shard_map/pallas_call | solution.py:147
  20.8 4.1 %all-to-all-start = ((bf16[8,384,128]{2,1,0:T(8,128)(2,1)}), bf16[8,384,128]{2,1,0:T(8,128)(2,1)S(1)}, u32[]{:S(2)}, u32[]{:S(2)}) async-start(bf16[8,384,128]{2,1,0:T(8,128)(2,1)} %get-tuple-element.24), calls=%async_computation | async-start | bytes 1572864 | tf_op jit(solution)/shard_map/all_to_all | solution.py:338
  24.9 0.0 copy-done.4
  24.9 2.0 %collective-permute-start.6 = (bf16[384,512]{1,0:T(8,128)(2,1)S(1)}, bf16[384,512]{1,0:T(8,128)(2,1)S(1)}, u32[]{:S(2)}, u32[]{:S(2)}) collective-permute-start(bf16[384,512]{1,0:T(8,128)(2,1)S(1)} %copy-done.4), channel_id=1, source_target_pairs={{0,2},{1,3},{2,0},{3,1},{4,6},{5,7},{6,4},{7,5},{8,10},{9,11},{10,... | collective-permute-start | bytes 1179656 | tf_op jit(solution)/shard_map/ppermute | solution.py:295
  26.9 0.0 collective-permute-start.4
  26.9 4.0 %collective-permute-done.3.refs_1_ = bf16[256,768]{1,0:T(8,128)(2,1)S(1)} collective-permute-done((bf16[256,768]{1,0:T(8,128)(2,1)S(1)}, bf16[256,768]{1,0:T(8,128)(2,1)S(1)}, u32[]{:S(2)}, u32[]{:S(2)}) %collective-permute-start.3) | collective-permute-done | bytes 393248 | tf_op jit(solution)/shard_map/ppermute | solution.py:295
  30.9 0.0 collective-permute-start.5
  30.9 12.9 %collective-permute-done.6.refs_5_ = bf16[384,512]{1,0:T(8,128)(2,1)S(1)} collective-permute-done((bf16[384,512]{1,0:T(8,128)(2,1)S(1)}, bf16[384,512]{1,0:T(8,128)(2,1)S(1)}, u32[]{:S(2)}, u32[]{:S(2)}) %collective-permute-start.6) | collective-permute-done | bytes 393248 | tf_op jit(solution)/shard_map/ppermute | solution.py:295
  43.8 0.0 collective-permute-done.4.refs_2_
  43.8 0.0 collective-permute-done.5.refs_3_
  43.8 0.0 copy-done
  43.8 0.0 copy-start.1
  43.8 1.7 %shard_map.104 = (f32[1024,128]{1,0:T(8,128)S(1)}, f32[1024,128]{1,0:T(8,128)S(1)}, bf16[1024,128]{1,0:T(8,128)(2,1)S(1)}, bf16[1024,128]{1,0:T(8,128)(2,1)S(1)}, bf16[1024,768]{1,0:T(8,128)(2,1)S(1)}) custom-call(bf16[256,768]{1,0:T(8,128)(2,1)S(1)} %pad_maximum_fusion.refs_0_, bf16[256,768]{1,0:T(8,128)(2,1)S(1)} %collective-permute-done.3.refs_1_, ...), custom_call_target="tpu_custom_call" | custom-call | flops 805306368 | bytes 1572864 | tf_op jit(solution)/shard_map/pallas_call | solution.py:147
  45.5 0.0 copy-start.2
  45.5 1.1 copy-done.2
  46.6 1.0 collective-permute-start.7
  47.7 5.8 %collective-permute-done.7 = bf16[1024,128]{1,0:T(8,128)(2,1)S(1)} collective-permute-done((bf16[1024,128]{1,0:T(8,128)(2,1)S(1)}, bf16[1024,128]{1,0:T(8,128)(2,1)S(1)}, u32[]{:S(2)}, u32[]{:S(2)}) %collective-permute-start.7) | collective-permute-done | bytes 262176 | tf_op jit(solution)/shard_map/ppermute | solution.py:295
  53.4 0.6 collective-permute-start.8
  54.0 0.1 add_convert_fusion
  54.1 2.5 %collective-permute-start.9 = (bf16[1024,128]{1,0:T(8,128)(2,1)S(1)}, bf16[1024,128]{1,0:T(8,128)(2,1)S(1)}, u32[]{:S(2)}, u32[]{:S(2)}) collective-permute-start(bf16[1024,128]{1,0:T(8,128)(2,1)S(1)} %add_convert_fusion), channel_id=1, source_target_pairs={{0,8},{1,9},{2,10},{3,11},{4,12},{5,13},{6,14},{7,15},{8,0},{9,1},... | collective-permute-start | bytes 786440 | tf_op jit(solution)/shard_map/ppermute | solution.py:295
  56.5 0.0 all-to-all-done.tok_ref
  56.5 0.0 copy-done.1
  56.5 4.9 %shard_map.103 = (bf16[1536,1024]{1,0:T(8,128)(2,1)S(1)}, bf16[128,1024]{1,0:T(8,128)(2,1)S(1)}, bf16[1024,128]{1,0:T(8,128)(2,1)S(1)}, bf16[128,1536]{1,0:T(8,128)(2,1)S(1)}, bf16[1536,128]{1,0:T(8,128)(2,1)S(1)}) custom-call(bf16[8,384,128]{2,1,0:T(8,128)(2,1)S(1)} %all-to-all-done.tok_ref, bf16[2,512,128]{2,1,0:T(8,128)(2,1)S(1)} %copy-done.1), custom_call_target="tpu_custom_call" | custom-call | flops 805306368 | bytes 6291456 | tf_op jit(solution)/shard_map/pallas_call | solution.py:147
  61.5 3.5 %collective-permute-done.8.near_ref = bf16[1024,128]{1,0:T(8,128)(2,1)S(1)} collective-permute-done((bf16[1024,128]{1,0:T(8,128)(2,1)S(1)}, bf16[1024,128]{1,0:T(8,128)(2,1)S(1)}, u32[]{:S(2)}, u32[]{:S(2)}) %collective-permute-start.8) | collective-permute-done | bytes 262176 | tf_op jit(solution)/shard_map/ppermute | solution.py:295
  64.9 0.0 collective-permute-done.9.far_ref
  64.9 4.5 %shard_map.105 = bf16[8,384,128]{2,1,0:T(8,128)(2,1)} custom-call(bf16[1024,128]{1,0:T(8,128)(2,1)S(1)} %get-tuple-element.26.queries_ref, bf16[128,1536]{1,0:T(8,128)(2,1)S(1)} %get-tuple-element.27.keys_t_ref, bf16[1536,128]{1,0:T(8,128)(2,1)S(1)} %get-tuple-element.28.vals_ref, bf16[1536,1024]{1,0:T(8,128)(2,1)S(1)} %get-tuple-element.29.probs_ref, ...), custom_call_target="tpu_custom_call" | custom-call | flops 1610612736 | bytes 6291456 | tf_op jit(solution)/shard_map/pallas_call | solution.py:147
  69.4 7.9 %all-to-all-start.1 = ((bf16[8,384,128]{2,1,0:T(8,128)(2,1)}), bf16[8,384,128]{2,1,0:T(8,128)(2,1)S(1)}, u32[]{:S(2)}, u32[]{:S(2)}) async-start(bf16[8,384,128]{2,1,0:T(8,128)(2,1)} %shard_map.105), calls=%async_computation.1 | async-start | bytes 1572864 | tf_op jit(solution)/shard_map/all_to_all | solution.py:371
  77.3 2.9 %collective-permute-start.11 = (bf16[128,1024]{1,0:T(8,128)(2,1)S(1)}, bf16[128,1024]{1,0:T(8,128)(2,1)S(1)}, u32[]{:S(2)}, u32[]{:S(2)}) collective-permute-start(bf16[128,1024]{1,0:T(8,128)(2,1)S(1)} %get-tuple-element.30.out_ref.refs_0_), channel_id=1, source_target_pairs={{0,8},{1,9},{2,10},{3,11},{4,12},{5,13},{6,14},{7,15},{8,0},{9,1},... | collective-permute-start | bytes 786440 | tf_op jit(solution)/shard_map/ppermute | solution.py:295
  80.2 1.5 %collective-permute-start.10 = (bf16[128,1024]{1,0:T(8,128)(2,1)S(1)}, bf16[128,1024]{1,0:T(8,128)(2,1)S(1)}, u32[]{:S(2)}, u32[]{:S(2)}) collective-permute-start(bf16[128,1024]{1,0:T(8,128)(2,1)S(1)} %get-tuple-element.30.out_ref.refs_0_), channel_id=1, source_target_pairs={{0,4},{1,5},{2,6},{3,7},{4,0},{5,1},{6,2},{7,3},{8,12},{9,13},{10,... | collective-permute-start | bytes 786440 | tf_op jit(solution)/shard_map/ppermute | solution.py:295
  81.7 25.6 %collective-permute-done.11.refs_2_ = bf16[128,1024]{1,0:T(8,128)(2,1)S(1)} collective-permute-done((bf16[128,1024]{1,0:T(8,128)(2,1)S(1)}, bf16[128,1024]{1,0:T(8,128)(2,1)S(1)}, u32[]{:S(2)}, u32[]{:S(2)}) %collective-permute-start.11) | collective-permute-done | bytes 262176 | tf_op jit(solution)/shard_map/ppermute | solution.py:295
  107.3 0.0 collective-permute-start.12
  107.3 0.0 collective-permute-done.10.refs_1_
  107.3 6.4 %collective-permute-done.12.refs_3_ = bf16[128,1024]{1,0:T(8,128)(2,1)S(1)} collective-permute-done((bf16[128,1024]{1,0:T(8,128)(2,1)S(1)}, bf16[128,1024]{1,0:T(8,128)(2,1)S(1)}, u32[]{:S(2)}, u32[]{:S(2)}) %collective-permute-start.12) | collective-permute-done | bytes 262176 | tf_op jit(solution)/shard_map/ppermute | solution.py:295
  113.7 0.0 copy-done.3
  113.7 1.3 %shard_map.107 = (bf16[512,384]{1,0:T(8,128)(2,1)S(1)}, bf16[512,384]{1,0:T(8,128)(2,1)S(1)}) custom-call(bf16[1024,768]{1,0:T(8,128)(2,1)S(1)} %copy-done.3, bf16[128,1024]{1,0:T(8,128)(2,1)S(1)} %get-tuple-element.30.out_ref.refs_0_, bf16[128,1024]{1,0:T(8,128)(2,1)S(1)} %collective-permute-done.10.refs_1_, ...), custom_call_target="tpu_custom_call" | custom-call | flops 805306368 | bytes 1572864 | tf_op jit(solution)/shard_map/pallas_call | solution.py:147
  115.0 1.5 %collective-permute-start.13 = (bf16[512,384]{1,0:T(8,128)(2,1)S(1)}, bf16[512,384]{1,0:T(8,128)(2,1)S(1)}, u32[]{:S(2)}, u32[]{:S(2)}) collective-permute-start(bf16[512,384]{1,0:T(8,128)(2,1)S(1)} %get-tuple-element.43), channel_id=1, source_target_pairs={{0,2},{1,3},{2,0},{3,1},{4,6},{5,7},{6,4},{7,5},{8,10},{9,11},{10,... | collective-permute-start | bytes 1179656 | tf_op jit(solution)/shard_map/ppermute | solution.py:295
  116.4 6.5 %collective-permute-done.13.other_ref = bf16[512,384]{1,0:T(8,128)(2,1)S(1)} collective-permute-done((bf16[512,384]{1,0:T(8,128)(2,1)S(1)}, bf16[512,384]{1,0:T(8,128)(2,1)S(1)}, u32[]{:S(2)}, u32[]{:S(2)}) %collective-permute-start.13) | collective-permute-done | bytes 393248 | tf_op jit(solution)/shard_map/ppermute | solution.py:295
  122.9 1.5 %shard_map.108 = f32[384,1024]{1,0:T(8,128)} custom-call(bf16[512,384]{1,0:T(8,128)(2,1)S(1)} %get-tuple-element.42.own_ref, bf16[512,384]{1,0:T(8,128)(2,1)S(1)} %collective-permute-done.13.other_ref), custom_call_target="tpu_custom_call" | custom-call | bytes 2359296 | tf_op jit(solution)/shard_map/pallas_call | solution.py:147
  124.4 0.0 all-to-all-done.1.tok_ref
  124.4 1.1 shard_map.106
  (4 shorter events, 0.0 us)
Async XLA Ops:
  1.7 5.9 %collective-permute-start = (bf16[64,768]{1,0:T(8,128)(2,1)S(1)}, bf16[64,768]{1,0:T(8,128)(2,1)S(1)}, u32[]{:S(2)}, u32[]{:S(2)}) collective-permute-start(bf16[64,768]{1,0:T(8,128)(2,1)S(1)} %get-tuple-element.45), channel_id=1, source_target_pairs={{0,4},{1,5},{2,6},{3,7},{4,0},{5,1},{6,2},{7,3},{8,12},{9,13},{10,... | collective-permute-start | bytes 294920 | tf_op jit(solution)/shard_map/ppermute | solution.py:295
  4.8 8.2 %collective-permute-start.2 = (bf16[64,768]{1,0:T(8,128)(2,1)S(1)}, bf16[64,768]{1,0:T(8,128)(2,1)S(1)}, u32[]{:S(2)}, u32[]{:S(2)}) collective-permute-start(bf16[64,768]{1,0:T(8,128)(2,1)S(1)} %get-tuple-element.46), channel_id=1, source_target_pairs={{0,12},{1,13},{2,14},{3,15},{4,8},{5,9},{6,10},{7,11},{8,4},{9,5},... | collective-permute-start | bytes 294920 | tf_op jit(solution)/shard_map/ppermute | solution.py:295
  7.3 8.9 %collective-permute-start.1 = (bf16[64,768]{1,0:T(8,128)(2,1)S(1)}, bf16[64,768]{1,0:T(8,128)(2,1)S(1)}, u32[]{:S(2)}, u32[]{:S(2)}) collective-permute-start(bf16[64,768]{1,0:T(8,128)(2,1)S(1)} %get-tuple-element.47), channel_id=1, source_target_pairs={{0,8},{1,9},{2,10},{3,11},{4,12},{5,13},{6,14},{7,15},{8,0},{9,1},... | collective-permute-start | bytes 294920 | tf_op jit(solution)/shard_map/ppermute | solution.py:295
  16.3 14.6 %collective-permute-start.3 = (bf16[256,768]{1,0:T(8,128)(2,1)S(1)}, bf16[256,768]{1,0:T(8,128)(2,1)S(1)}, u32[]{:S(2)}, u32[]{:S(2)}) collective-permute-start(bf16[256,768]{1,0:T(8,128)(2,1)S(1)} %pad_maximum_fusion.refs_0_), channel_id=1, source_target_pairs={{0,2},{1,3},{2,0},{3,1},{4,6},{5,7},{6,4},{7,5},{8,10},{9,11},{10,... | collective-permute-start | bytes 1179656 | tf_op jit(solution)/shard_map/ppermute | solution.py:295
  20.8 4.1 %copy-start.4 = (bf16[384,512]{1,0:T(8,128)(2,1)S(1)}, bf16[384,512]{1,0:T(8,128)(2,1)}, u32[]{:S(2)}) copy-start(bf16[384,512]{1,0:T(8,128)(2,1)} %get-tuple-element.32) | copy-start | bytes 1179652
  20.8 23.0 %copy-start = (bf16[384,512]{1,0:T(8,128)(2,1)S(1)}, bf16[384,512]{1,0:T(8,128)(2,1)}, u32[]{:S(2)}) copy-start(bf16[384,512]{1,0:T(8,128)(2,1)} %get-tuple-element.31.refs_4_) | copy-start | bytes 1179652
  20.8 35.7 %all-to-all-start = ((bf16[8,384,128]{2,1,0:T(8,128)(2,1)}), bf16[8,384,128]{2,1,0:T(8,128)(2,1)S(1)}, u32[]{:S(2)}, u32[]{:S(2)}) async-start(bf16[8,384,128]{2,1,0:T(8,128)(2,1)} %get-tuple-element.24), calls=%async_computation | async-start | bytes 1572864 | tf_op jit(solution)/shard_map/all_to_all | solution.py:338
  24.9 18.9 %collective-permute-start.6 = (bf16[384,512]{1,0:T(8,128)(2,1)S(1)}, bf16[384,512]{1,0:T(8,128)(2,1)S(1)}, u32[]{:S(2)}, u32[]{:S(2)}) collective-permute-start(bf16[384,512]{1,0:T(8,128)(2,1)S(1)} %copy-done.4), channel_id=1, source_target_pairs={{0,2},{1,3},{2,0},{3,1},{4,6},{5,7},{6,4},{7,5},{8,10},{9,11},{10,... | collective-permute-start | bytes 1179656 | tf_op jit(solution)/shard_map/ppermute | solution.py:295
  26.9 16.9 %collective-permute-start.4 = (bf16[256,768]{1,0:T(8,128)(2,1)S(1)}, bf16[256,768]{1,0:T(8,128)(2,1)S(1)}, u32[]{:S(2)}, u32[]{:S(2)}) collective-permute-start(bf16[256,768]{1,0:T(8,128)(2,1)S(1)} %pad_maximum_fusion.refs_0_), channel_id=1, source_target_pairs={{0,1},{1,0},{2,3},{3,2},{4,5},{5,4},{6,7},{7,6},{8,9},{9,8},{10,11... | collective-permute-start | bytes 1179656 | tf_op jit(solution)/shard_map/ppermute | solution.py:295
  30.9 12.9 %collective-permute-start.5 = (bf16[256,768]{1,0:T(8,128)(2,1)S(1)}, bf16[256,768]{1,0:T(8,128)(2,1)S(1)}, u32[]{:S(2)}, u32[]{:S(2)}) collective-permute-start(bf16[256,768]{1,0:T(8,128)(2,1)S(1)} %collective-permute-done.3.refs_1_), channel_id=1, source_target_pairs={{0,1},{1,0},{2,3},{3,2},{4,5},{5,4},{6,7},{7,6},{8,9},{9,8},{10,11... | collective-permute-start | bytes 1179656 | tf_op jit(solution)/shard_map/ppermute | solution.py:295
  43.8 12.7 %copy-start.1 = (bf16[2,512,128]{2,1,0:T(8,128)(2,1)S(1)}, bf16[2,512,128]{2,1,0:T(8,128)(2,1)}, u32[]{:S(2)}) copy-start(bf16[2,512,128]{2,1,0:T(8,128)(2,1)} %get-tuple-element.25.text_ref) | copy-start | bytes 786436
  45.5 1.1 copy-start.2
  46.6 6.8 %collective-permute-start.7 = (bf16[1024,128]{1,0:T(8,128)(2,1)S(1)}, bf16[1024,128]{1,0:T(8,128)(2,1)S(1)}, u32[]{:S(2)}, u32[]{:S(2)}) collective-permute-start(bf16[1024,128]{1,0:T(8,128)(2,1)S(1)} %get-tuple-element.35), channel_id=1, source_target_pairs={{0,4},{1,5},{2,6},{3,7},{4,0},{5,1},{6,2},{7,3},{8,12},{9,13},{10,... | collective-permute-start | bytes 786440 | tf_op jit(solution)/shard_map/ppermute | solution.py:295
  53.4 11.5 %collective-permute-start.8 = (bf16[1024,128]{1,0:T(8,128)(2,1)S(1)}, bf16[1024,128]{1,0:T(8,128)(2,1)S(1)}, u32[]{:S(2)}, u32[]{:S(2)}) collective-permute-start(bf16[1024,128]{1,0:T(8,128)(2,1)S(1)} %get-tuple-element.36), channel_id=1, source_target_pairs={{0,4},{1,5},{2,6},{3,7},{4,0},{5,1},{6,2},{7,3},{8,12},{9,13},{10,... | collective-permute-start | bytes 786440 | tf_op jit(solution)/shard_map/ppermute | solution.py:295
  54.1 10.8 %collective-permute-start.9 = (bf16[1024,128]{1,0:T(8,128)(2,1)S(1)}, bf16[1024,128]{1,0:T(8,128)(2,1)S(1)}, u32[]{:S(2)}, u32[]{:S(2)}) collective-permute-start(bf16[1024,128]{1,0:T(8,128)(2,1)S(1)} %add_convert_fusion), channel_id=1, source_target_pairs={{0,8},{1,9},{2,10},{3,11},{4,12},{5,13},{6,14},{7,15},{8,0},{9,1},... | collective-permute-start | bytes 786440 | tf_op jit(solution)/shard_map/ppermute | solution.py:295
  69.4 44.3 %copy-start.3 = (bf16[1024,768]{1,0:T(8,128)(2,1)S(1)}, bf16[1024,768]{1,0:T(8,128)(2,1)}, u32[]{:S(2)}) copy-start(bf16[1024,768]{1,0:T(8,128)(2,1)} %copy-done.2) | copy-start | bytes 4718596
  69.4 55.0 %all-to-all-start.1 = ((bf16[8,384,128]{2,1,0:T(8,128)(2,1)}), bf16[8,384,128]{2,1,0:T(8,128)(2,1)S(1)}, u32[]{:S(2)}, u32[]{:S(2)}) async-start(bf16[8,384,128]{2,1,0:T(8,128)(2,1)} %shard_map.105), calls=%async_computation.1 | async-start | bytes 1572864 | tf_op jit(solution)/shard_map/all_to_all | solution.py:371
  77.3 30.0 %collective-permute-start.11 = (bf16[128,1024]{1,0:T(8,128)(2,1)S(1)}, bf16[128,1024]{1,0:T(8,128)(2,1)S(1)}, u32[]{:S(2)}, u32[]{:S(2)}) collective-permute-start(bf16[128,1024]{1,0:T(8,128)(2,1)S(1)} %get-tuple-element.30.out_ref.refs_0_), channel_id=1, source_target_pairs={{0,8},{1,9},{2,10},{3,11},{4,12},{5,13},{6,14},{7,15},{8,0},{9,1},... | collective-permute-start | bytes 786440 | tf_op jit(solution)/shard_map/ppermute | solution.py:295
  80.2 27.1 %collective-permute-start.10 = (bf16[128,1024]{1,0:T(8,128)(2,1)S(1)}, bf16[128,1024]{1,0:T(8,128)(2,1)S(1)}, u32[]{:S(2)}, u32[]{:S(2)}) collective-permute-start(bf16[128,1024]{1,0:T(8,128)(2,1)S(1)} %get-tuple-element.30.out_ref.refs_0_), channel_id=1, source_target_pairs={{0,4},{1,5},{2,6},{3,7},{4,0},{5,1},{6,2},{7,3},{8,12},{9,13},{10,... | collective-permute-start | bytes 786440 | tf_op jit(solution)/shard_map/ppermute | solution.py:295
  107.3 6.4 %collective-permute-start.12 = (bf16[128,1024]{1,0:T(8,128)(2,1)S(1)}, bf16[128,1024]{1,0:T(8,128)(2,1)S(1)}, u32[]{:S(2)}, u32[]{:S(2)}) collective-permute-start(bf16[128,1024]{1,0:T(8,128)(2,1)S(1)} %collective-permute-done.11.refs_2_), channel_id=1, source_target_pairs={{0,4},{1,5},{2,6},{3,7},{4,0},{5,1},{6,2},{7,3},{8,12},{9,13},{10,... | collective-permute-start | bytes 786440 | tf_op jit(solution)/shard_map/ppermute | solution.py:295
  115.0 7.9 %collective-permute-start.13 = (bf16[512,384]{1,0:T(8,128)(2,1)S(1)}, bf16[512,384]{1,0:T(8,128)(2,1)S(1)}, u32[]{:S(2)}, u32[]{:S(2)}) collective-permute-start(bf16[512,384]{1,0:T(8,128)(2,1)S(1)} %get-tuple-element.43), channel_id=1, source_target_pairs={{0,2},{1,3},{2,0},{3,1},{4,6},{5,7},{6,4},{7,5},{8,10},{9,11},{10,... | collective-permute-start | bytes 1179656 | tf_op jit(solution)/shard_map/ppermute | solution.py:295

commit v8 on v7

--- a/solution.py
+++ b/solution.py
@@ -166,11 +166,14 @@
     return pl.ds(pl.multiple_of(jnp.bitwise_xor(lax.axis_index("seq"), step + other_row) * HD, HD), HD)
 
 
-def pack_kernel(me_ref, q_ref, k_ref, v_ref, w_ref, kt_ref, vt_ref, tok_ref, keep_ref, give_ref, text_ref):
+def pack_kernel(q_ref, k_ref, v_ref, tok_ref):
     rows = q_ref.shape[0]
     for h in range(tok_ref.shape[0]):
         for i, ref in enumerate((q_ref, k_ref, v_ref)):
             tok_ref[h, i * rows : (i + 1) * rows, :] = ref[:, h * HD : (h + 1) * HD]
+
+
+def pack_weight_kernel(me_ref, w_ref, kt_ref, vt_ref, keep_ref, give_ref, text_ref):
     for i, step in enumerate(STEPS):
         cols = slice(i * HD, (i + 1) * HD)
         keep_ref[:, cols] = w_ref[:, head_columns(step, 0)]
@@ -324,17 +327,27 @@
     vmem = pl.BlockSpec(memory_space=pltpu.VMEM)
 
     head = pl.BlockSpec((text, HD), lambda i, me_ref: (0, me_ref[0]))
-    tok_out, keep, give, text_head = call(
-        pack_kernel,
-        [shape((n, 3 * rows, HD), BF16)] + [shape((depth, 4 * HD), BF16)] * 2 + [shape((2, text, HD), BF16)],
-        [lax.axis_index("seq").astype(jnp.int32)[None], q_img, k_img, v_img, out_weight, k_txt, v_txt],
-        specs=[vmem] * 4 + [head] * 2,
+    big = 60 * 1024 * 1024
+    keep, give, text_head = call(
+        pack_weight_kernel,
+        [shape((depth, 4 * HD), BF16)] * 2 + [shape((2, text, HD), BF16)],
+        [lax.axis_index("seq").astype(jnp.int32)[None], out_weight, k_txt, v_txt],
+        specs=[vmem] + [head] * 2,
         scalars=1,
-        moved=4 * (3 * rows + depth) * width,
-        limit=60 * 1024 * 1024,
-    )
+        moved=4 * depth * width,
+        limit=big,
+    )
+    d_out, give = lax.optimization_barrier((d_out, give))
     given = exchange(give, 1)
     pieces = gather_cotangents(d_out)
+    (tok_out,) = call(
+        pack_kernel,
+        [shape((n, 3 * rows, HD), BF16)],
+        [q_img, k_img, v_img],
+        moved=4 * 3 * rows * width,
+        limit=big,
+    )
+    tok_out, given = lax.optimization_barrier((tok_out, given))
     tok_in = lax.all_to_all(tok_out, "seq", split_axis=0, concat_axis=0, tiled=True)
 
     probs, out_t, queries, keys_t, vals = call(
@@ -358,8 +371,8 @@
     far = exchange((far + near_far.astype(F32)).astype(BF16), 4)
     near, _ = lax.optimization_barrier((near, near_far))
     near = exchange(near, 2)
-    out_far = exchange(out_t, 4)
-    outs = [out_t, exchange(out_t, 2), out_far, exchange(out_far, 2)]
+    out_late, far = lax.optimization_barrier((out_t, far))
+    out_far = exchange(out_late, 4)
     (grad_out,) = call(
         functools.partial(backward_kernel, chunk=chunk),
         [shape((n, 3 * rows, HD), BF16)],
@@ -368,7 +381,9 @@
         flops=8 * total * image * HD,
         moved=4 * total * image,
     )
+    grad_out, out_far = lax.optimization_barrier((grad_out, out_far))
     grad_in = lax.all_to_all(grad_out, "seq", split_axis=0, concat_axis=0, tiled=True)
+    outs = [out_t, exchange(out_t, 2), out_far, exchange(out_far, 2)]
     dw_own, dw_other = call(
         weight_grad_kernel,
         [shape((4 * HD, depth), BF16)] * 2,

time: 126 us -> 120 us (0.952)
  waiting for transfers between devices: 73.5 us -> 68.4 us
  starting transfers between devices: 31.2 us -> 28.4 us
  Pallas kernels: 17.8 us -> 19.3 us
    ppermute x14, waiting for transfers between devices: 73.5 us -> 68.4 us  [exchange(): return lax.ppermute(array, ('seq', 'fsdp'), pairs)]
    all_to_all x1, starting transfers between devices: 7.94 us -> 3.69 us  [local(): lax.all_to_all(grad_out, 'seq', split_axis=0, concat_axis=0, tiled=True)]
    all_to_all x1, starting transfers between devices: 4.06 us -> 6.78 us  [local(): lax.all_to_all(tok_out, 'seq', split_axis=0, concat_axis=0, tiled=True)]
    pallas_call x7 -> x8, Pallas kernels: 17.8 us -> 19.3 us  [call(): pl.pallas_call(kernel, out_shape=outs, grid_spec=pltpu.PrefetchScalarGrid...]
    unnamed x10, local copies, waits for them, and re-layouts: 1.15 us -> 2.56 us
    ppermute x14, starting transfers between devices: 19.2 us -> 17.9 us  [exchange(): return lax.ppermute(array, ('seq', 'fsdp'), pairs)]
  transfers between devices with their start and end apart: 16 -> 16, of which waited for: 10 -> 12; matrix products, arithmetic and copies ran while one was open for 0% -> 0% of each run, Pallas kernels for 10% -> 13%
where the time goes in v8:
time: 120 us; the launch traced here: 119 us
  waiting for transfers between devices  68.4 us (57%)
  starting transfers between devices  28.4 us (24%)
  Pallas kernels  19.3 us (16%)
  local copies, waits for them, and re-layouts  2.59 us (2%)
    ppermute x14, waiting for transfers between devices, exchange(): return lax.ppermute(array, ('seq', 'fsdp'), pairs)  68.4 us
    pallas_call x8, Pallas kernels, call(): pl.pallas_call(kernel, out_shape=outs, grid_spec=pltpu.PrefetchScalarGrid...  19.3 us
    ppermute x14, starting transfers between devices, exchange(): return lax.ppermute(array, ('seq', 'fsdp'), pairs)  17.9 us
    all_to_all x1, starting transfers between devices, local(): lax.all_to_all(tok_out, 'seq', split_axis=0, concat_axis=0, tiled=True)  6.78 us
    all_to_all x1, starting transfers between devices, local(): lax.all_to_all(grad_out, 'seq', split_axis=0, concat_axis=0, tiled=True)  3.69 us
    unnamed x10, local copies, waits for them, and re-layouts  2.56 us
  transfers between devices with their start and end apart: 16, of which 12 were waited for; matrix products, arithmetic and copies ran while one was open for 0% of the time, Pallas kernels for 13%

profile of v8, /device:TPU:0, one launch (start us, length us, event | category | flops | bytes accessed | tf_op | source)
XLA Modules:
  0.0 119.5 jit_solution(6018254334202443785)
XLA Ops:
  0.6 0.0 copy-start.4
  0.7 2.3 %shard_map.103 = (bf16[384,512]{1,0:T(8,128)(2,1)}, bf16[384,512]{1,0:T(8,128)(2,1)}, bf16[2,512,128]{2,1,0:T(8,128)(2,1)}) custom-call(s32[1]{0:T(128)} %bitcast.me_ref, bf16[384,1024]{1,0:T(8,128)(2,1)} %w_ref.1, bf16[512,1024]{1,0:T(8,128)(2,1)} %kt_ref.1, bf16[512,1024]{1,0:T(8,128)(2,1)} %vt_ref.1), custom_call_target="tpu_custom_call" | custom-call | bytes 1572864 | tf_op jit(solution)/shard_map/pallas_call | solution.py:147
  3.0 0.0 copy-done.4
  3.1 5.1 %collective-permute-start.3 = (bf16[64,768]{1,0:T(8,128)(2,1)S(1)}, bf16[64,768]{1,0:T(8,128)(2,1)S(1)}, u32[]{:S(2)}, u32[]{:S(2)}) collective-permute-start(bf16[64,768]{1,0:T(8,128)(2,1)S(1)} %get-tuple-element.59), channel_id=1, source_target_pairs={{0,12},{1,13},{2,14},{3,15},{4,8},{5,9},{6,10},{7,11},{8,4},{9,5},... | collective-permute-start | bytes 294920 | tf_op jit(solution)/shard_map/ppermute | solution.py:298
  8.2 0.0 collective-permute-start.2
  8.2 0.6 collective-permute-start.1
  8.8 1.7 %collective-permute-start = (bf16[384,512]{1,0:T(8,128)(2,1)}, bf16[384,512]{1,0:T(8,128)(2,1)S(1)}, u32[]{:S(2)}, u32[]{:S(2)}) collective-permute-start(bf16[384,512]{1,0:T(8,128)(2,1)} %get-tuple-element.32), channel_id=1, source_target_pairs={{0,2},{1,3},{2,0},{3,1},{4,6},{5,7},{6,4},{7,5},{8,10},{9,11},{10,... | collective-permute-start | bytes 1179656 | tf_op jit(solution)/shard_map/ppermute | solution.py:298
  10.5 1.4 %collective-permute-done.3 = bf16[64,768]{1,0:T(8,128)(2,1)S(1)} collective-permute-done((bf16[64,768]{1,0:T(8,128)(2,1)S(1)}, bf16[64,768]{1,0:T(8,128)(2,1)S(1)}, u32[]{:S(2)}, u32[]{:S(2)}) %collective-permute-start.3) | collective-permute-done | bytes 98336 | tf_op jit(solution)/shard_map/ppermute | solution.py:298
  11.9 4.6 %collective-permute-done.2 = bf16[64,768]{1,0:T(8,128)(2,1)S(1)} collective-permute-done((bf16[64,768]{1,0:T(8,128)(2,1)S(1)}, bf16[64,768]{1,0:T(8,128)(2,1)S(1)}, u32[]{:S(2)}, u32[]{:S(2)}) %collective-permute-start.2) | collective-permute-done | bytes 98336 | tf_op jit(solution)/shard_map/ppermute | solution.py:298
  16.4 0.0 collective-permute-done.1
  16.5 0.0 copy-start
  16.5 1.6 %collective-permute-start.4 = (bf16[256,768]{1,0:T(8,128)(2,1)S(1)}, bf16[256,768]{1,0:T(8,128)(2,1)S(1)}, u32[]{:S(2)}, u32[]{:S(2)}) collective-permute-start(bf16[256,768]{1,0:T(8,128)(2,1)S(1)} %pad_maximum_fusion.refs_0_), channel_id=1, source_target_pairs={{0,2},{1,3},{2,0},{3,1},{4,6},{5,7},{6,4},{7,5},{8,10},{9,11},{10,... | collective-permute-start | bytes 1179656 | tf_op jit(solution)/shard_map/ppermute | solution.py:298
  18.1 2.1 %shard_map.102 = bf16[8,384,128]{2,1,0:T(8,128)(2,1)} custom-call(bf16[128,1024]{1,0:T(8,128)(2,1)} %q_ref.1, bf16[128,1024]{1,0:T(8,128)(2,1)} %k_ref.1, bf16[128,1024]{1,0:T(8,128)(2,1)} %v_ref.1), custom_call_target="tpu_custom_call" | custom-call | bytes 1572864 | tf_op jit(solution)/shard_map/pallas_call | solution.py:147
  20.2 0.1 collective-permute-done.refs_5_
  20.3 6.8 %all-to-all-start = ((bf16[8,384,128]{2,1,0:T(8,128)(2,1)}), bf16[8,384,128]{2,1,0:T(8,128)(2,1)S(1)}, u32[]{:S(2)}, u32[]{:S(2)}) async-start(bf16[8,384,128]{2,1,0:T(8,128)(2,1)} %shard_map.102), calls=%async_computation | async-start | bytes 1572864 | tf_op jit(solution)/shard_map/all_to_all | solution.py:351
  27.1 0.0 collective-permute-start.5
  27.1 3.8 %collective-permute-done.4.refs_1_ = bf16[256,768]{1,0:T(8,128)(2,1)S(1)} collective-permute-done((bf16[256,768]{1,0:T(8,128)(2,1)S(1)}, bf16[256,768]{1,0:T(8,128)(2,1)S(1)}, u32[]{:S(2)}, u32[]{:S(2)}) %collective-permute-start.4) | collective-permute-done | bytes 393248 | tf_op jit(solution)/shard_map/ppermute | solution.py:298
  30.8 0.0 collective-permute-start.6
  30.8 0.0 collective-permute-done.5.refs_2_
  30.8 1.7 %collective-permute-done.6.refs_3_ = bf16[256,768]{1,0:T(8,128)(2,1)S(1)} collective-permute-done((bf16[256,768]{1,0:T(8,128)(2,1)S(1)}, bf16[256,768]{1,0:T(8,128)(2,1)S(1)}, u32[]{:S(2)}, u32[]{:S(2)}) %collective-permute-start.6) | collective-permute-done | bytes 393248 | tf_op jit(solution)/shard_map/ppermute | solution.py:298
  32.6 1.7 %shard_map.105 = (f32[1024,128]{1,0:T(8,128)S(1)}, f32[1024,128]{1,0:T(8,128)S(1)}, bf16[1024,128]{1,0:T(8,128)(2,1)S(1)}, bf16[1024,128]{1,0:T(8,128)(2,1)S(1)}, bf16[1024,768]{1,0:T(8,128)(2,1)S(1)}) custom-call(bf16[256,768]{1,0:T(8,128)(2,1)S(1)} %pad_maximum_fusion.refs_0_, bf16[256,768]{1,0:T(8,128)(2,1)S(1)} %collective-permute-done.4.refs_1_, ...), custom_call_target="tpu_custom_call" | custom-call | flops 805306368 | bytes 1572864 | tf_op jit(solution)/shard_map/pallas_call | solution.py:147
  34.2 0.0 copy-start.2
  34.2 1.1 copy-done.2
  35.4 0.5 collective-permute-start.7
  35.9 10.1 %collective-permute-done.7 = bf16[1024,128]{1,0:T(8,128)(2,1)S(1)} collective-permute-done((bf16[1024,128]{1,0:T(8,128)(2,1)S(1)}, bf16[1024,128]{1,0:T(8,128)(2,1)S(1)}, u32[]{:S(2)}, u32[]{:S(2)}) %collective-permute-start.7) | collective-permute-done | bytes 262176 | tf_op jit(solution)/shard_map/ppermute | solution.py:298
  46.0 0.1 add_convert_fusion
  46.1 2.4 %collective-permute-start.9 = (bf16[1024,128]{1,0:T(8,128)(2,1)S(1)}, bf16[1024,128]{1,0:T(8,128)(2,1)S(1)}, u32[]{:S(2)}, u32[]{:S(2)}) collective-permute-start(bf16[1024,128]{1,0:T(8,128)(2,1)S(1)} %add_convert_fusion), channel_id=1, source_target_pairs={{0,8},{1,9},{2,10},{3,11},{4,12},{5,13},{6,14},{7,15},{8,0},{9,1},... | collective-permute-start | bytes 786440 | tf_op jit(solution)/shard_map/ppermute | solution.py:298
  48.4 2.5 %collective-permute-start.8 = (bf16[1024,128]{1,0:T(8,128)(2,1)S(1)}, bf16[1024,128]{1,0:T(8,128)(2,1)S(1)}, u32[]{:S(2)}, u32[]{:S(2)}) collective-permute-start(bf16[1024,128]{1,0:T(8,128)(2,1)S(1)} %get-tuple-element.46), channel_id=1, source_target_pairs={{0,4},{1,5},{2,6},{3,7},{4,0},{5,1},{6,2},{7,3},{8,12},{9,13},{10,... | collective-permute-start | bytes 786440 | tf_op jit(solution)/shard_map/ppermute | solution.py:298
  50.9 0.0 all-to-all-done.tok_ref
  50.9 0.0 copy-done.1
  50.9 4.9 %shard_map.104 = (bf16[1536,1024]{1,0:T(8,128)(2,1)S(1)}, bf16[128,1024]{1,0:T(8,128)(2,1)S(1)}, bf16[1024,128]{1,0:T(8,128)(2,1)S(1)}, bf16[128,1536]{1,0:T(8,128)(2,1)S(1)}, bf16[1536,128]{1,0:T(8,128)(2,1)S(1)}) custom-call(bf16[8,384,128]{2,1,0:T(8,128)(2,1)S(1)} %all-to-all-done.tok_ref, bf16[2,512,128]{2,1,0:T(8,128)(2,1)S(1)} %copy-done.1), custom_call_target="tpu_custom_call" | custom-call | flops 805306368 | bytes 6291456 | tf_op jit(solution)/shard_map/pallas_call | solution.py:147
  55.8 4.8 %collective-permute-done.9.far_ref = bf16[1024,128]{1,0:T(8,128)(2,1)S(1)} collective-permute-done((bf16[1024,128]{1,0:T(8,128)(2,1)S(1)}, bf16[1024,128]{1,0:T(8,128)(2,1)S(1)}, u32[]{:S(2)}, u32[]{:S(2)}) %collective-permute-start.9) | collective-permute-done | bytes 262176 | tf_op jit(solution)/shard_map/ppermute | solution.py:298
  60.6 0.0 collective-permute-start.10
  60.6 0.1 collective-permute-done.8.near_ref
  60.7 4.5 %shard_map.106 = bf16[8,384,128]{2,1,0:T(8,128)(2,1)} custom-call(bf16[1024,128]{1,0:T(8,128)(2,1)S(1)} %get-tuple-element.35.queries_ref, bf16[128,1536]{1,0:T(8,128)(2,1)S(1)} %get-tuple-element.36.keys_t_ref, bf16[1536,128]{1,0:T(8,128)(2,1)S(1)} %get-tuple-element.37.vals_ref, bf16[1536,1024]{1,0:T(8,128)(2,1)S(1)} %get-tuple-element.38.probs_ref, ...), custom_call_target="tpu_custom_call" | custom-call | flops 1610612736 | bytes 6291456 | tf_op jit(solution)/shard_map/pallas_call | solution.py:147
  65.2 8.9 %collective-permute-done.10.refs_2_ = bf16[128,1024]{1,0:T(8,128)(2,1)S(1)} collective-permute-done((bf16[128,1024]{1,0:T(8,128)(2,1)S(1)}, bf16[128,1024]{1,0:T(8,128)(2,1)S(1)}, u32[]{:S(2)}, u32[]{:S(2)}) %collective-permute-start.10) | collective-permute-done | bytes 262176 | tf_op jit(solution)/shard_map/ppermute | solution.py:298
  74.1 3.7 %all-to-all-start.1 = ((bf16[8,384,128]{2,1,0:T(8,128)(2,1)}), bf16[8,384,128]{2,1,0:T(8,128)(2,1)S(1)}, u32[]{:S(2)}, u32[]{:S(2)}) async-start(bf16[8,384,128]{2,1,0:T(8,128)(2,1)} %shard_map.106), calls=%async_computation.1 | async-start | bytes 1572864 | tf_op jit(solution)/shard_map/all_to_all | solution.py:385
  77.8 2.0 %collective-permute-start.11 = (bf16[128,1024]{1,0:T(8,128)(2,1)S(1)}, bf16[128,1024]{1,0:T(8,128)(2,1)S(1)}, u32[]{:S(2)}, u32[]{:S(2)}) collective-permute-start(bf16[128,1024]{1,0:T(8,128)(2,1)S(1)} %get-tuple-element.49.out_ref.refs_0_), channel_id=1, source_target_pairs={{0,4},{1,5},{2,6},{3,7},{4,0},{5,1},{6,2},{7,3},{8,12},{9,13},{10,... | collective-permute-start | bytes 786440 | tf_op jit(solution)/shard_map/ppermute | solution.py:298
  79.8 0.0 collective-permute-start.12
  79.9 20.0 %collective-permute-done.11.refs_1_ = bf16[128,1024]{1,0:T(8,128)(2,1)S(1)} collective-permute-done((bf16[128,1024]{1,0:T(8,128)(2,1)S(1)}, bf16[128,1024]{1,0:T(8,128)(2,1)S(1)}, u32[]{:S(2)}, u32[]{:S(2)}) %collective-permute-start.11) | collective-permute-done | bytes 262176 | tf_op jit(solution)/shard_map/ppermute | solution.py:298
  99.8 4.4 %collective-permute-done.12.refs_3_ = bf16[128,1024]{1,0:T(8,128)(2,1)S(1)} collective-permute-done((bf16[128,1024]{1,0:T(8,128)(2,1)S(1)}, bf16[128,1024]{1,0:T(8,128)(2,1)S(1)}, u32[]{:S(2)}, u32[]{:S(2)}) %collective-permute-start.12) | collective-permute-done | bytes 262176 | tf_op jit(solution)/shard_map/ppermute | solution.py:298
  104.3 1.4 %copy-done.3 = bf16[1024,768]{1,0:T(8,128)(2,1)S(1)} copy-done((bf16[1024,768]{1,0:T(8,128)(2,1)S(1)}, bf16[1024,768]{1,0:T(8,128)(2,1)}, u32[]{:S(2)}) %copy-start.3) | copy-done | bytes 1572888
  105.7 1.3 %shard_map.108 = (bf16[512,384]{1,0:T(8,128)(2,1)S(1)}, bf16[512,384]{1,0:T(8,128)(2,1)S(1)}) custom-call(bf16[1024,768]{1,0:T(8,128)(2,1)S(1)} %copy-done.3, bf16[128,1024]{1,0:T(8,128)(2,1)S(1)} %get-tuple-element.49.out_ref.refs_0_, bf16[128,1024]{1,0:T(8,128)(2,1)S(1)} %collective-permute-done.11.refs_1_, ...), custom_call_target="tpu_custom_call" | custom-call | flops 805306368 | bytes 1572864 | tf_op jit(solution)/shard_map/pallas_call | solution.py:147
  106.9 1.5 %collective-permute-start.13 = (bf16[512,384]{1,0:T(8,128)(2,1)S(1)}, bf16[512,384]{1,0:T(8,128)(2,1)S(1)}, u32[]{:S(2)}, u32[]{:S(2)}) collective-permute-start(bf16[512,384]{1,0:T(8,128)(2,1)S(1)} %get-tuple-element.57), channel_id=1, source_target_pairs={{0,2},{1,3},{2,0},{3,1},{4,6},{5,7},{6,4},{7,5},{8,10},{9,11},{10,... | collective-permute-start | bytes 1179656 | tf_op jit(solution)/shard_map/ppermute | solution.py:298
  108.4 8.5 %collective-permute-done.13.other_ref = bf16[512,384]{1,0:T(8,128)(2,1)S(1)} collective-permute-done((bf16[512,384]{1,0:T(8,128)(2,1)S(1)}, bf16[512,384]{1,0:T(8,128)(2,1)S(1)}, u32[]{:S(2)}, u32[]{:S(2)}) %collective-permute-start.13) | collective-permute-done | bytes 393248 | tf_op jit(solution)/shard_map/ppermute | solution.py:298
  116.9 1.5 %shard_map.109 = f32[384,1024]{1,0:T(8,128)} custom-call(bf16[512,384]{1,0:T(8,128)(2,1)S(1)} %get-tuple-element.56.own_ref, bf16[512,384]{1,0:T(8,128)(2,1)S(1)} %collective-permute-done.13.other_ref), custom_call_target="tpu_custom_call" | custom-call | bytes 2359296 | tf_op jit(solution)/shard_map/pallas_call | solution.py:147
  118.4 0.0 all-to-all-done.1.tok_ref
  118.4 1.1 shard_map.107
  (5 shorter events, 0.1 us)
Async XLA Ops:
  0.6 2.4 %copy-start.4 = (bf16[128,3072]{1,0:T(8,128)(2,1)S(1)}, bf16[128,3072]{1,0:T(8,128)(2,1)}, u32[]{:S(2)}) copy-start(bf16[128,3072]{1,0:T(8,128)(2,1)} %param.13) | copy-start | bytes 2359300
  3.1 8.8 %collective-permute-start.3 = (bf16[64,768]{1,0:T(8,128)(2,1)S(1)}, bf16[64,768]{1,0:T(8,128)(2,1)S(1)}, u32[]{:S(2)}, u32[]{:S(2)}) collective-permute-start(bf16[64,768]{1,0:T(8,128)(2,1)S(1)} %get-tuple-element.59), channel_id=1, source_target_pairs={{0,12},{1,13},{2,14},{3,15},{4,8},{5,9},{6,10},{7,11},{8,4},{9,5},... | collective-permute-start | bytes 294920 | tf_op jit(solution)/shard_map/ppermute | solution.py:298
  8.2 8.3 %collective-permute-start.2 = (bf16[64,768]{1,0:T(8,128)(2,1)S(1)}, bf16[64,768]{1,0:T(8,128)(2,1)S(1)}, u32[]{:S(2)}, u32[]{:S(2)}) collective-permute-start(bf16[64,768]{1,0:T(8,128)(2,1)S(1)} %get-tuple-element.60), channel_id=1, source_target_pairs={{0,8},{1,9},{2,10},{3,11},{4,12},{5,13},{6,14},{7,15},{8,0},{9,1},... | collective-permute-start | bytes 294920 | tf_op jit(solution)/shard_map/ppermute | solution.py:298
  8.2 8.3 %collective-permute-start.1 = (bf16[64,768]{1,0:T(8,128)(2,1)S(1)}, bf16[64,768]{1,0:T(8,128)(2,1)S(1)}, u32[]{:S(2)}, u32[]{:S(2)}) collective-permute-start(bf16[64,768]{1,0:T(8,128)(2,1)S(1)} %get-tuple-element.61), channel_id=1, source_target_pairs={{0,4},{1,5},{2,6},{3,7},{4,0},{5,1},{6,2},{7,3},{8,12},{9,13},{10,... | collective-permute-start | bytes 294920 | tf_op jit(solution)/shard_map/ppermute | solution.py:298
  8.8 11.5 %collective-permute-start = (bf16[384,512]{1,0:T(8,128)(2,1)}, bf16[384,512]{1,0:T(8,128)(2,1)S(1)}, u32[]{:S(2)}, u32[]{:S(2)}) collective-permute-start(bf16[384,512]{1,0:T(8,128)(2,1)} %get-tuple-element.32), channel_id=1, source_target_pairs={{0,2},{1,3},{2,0},{3,1},{4,6},{5,7},{6,4},{7,5},{8,10},{9,11},{10,... | collective-permute-start | bytes 1179656 | tf_op jit(solution)/shard_map/ppermute | solution.py:298
  16.5 16.1 %copy-start = (bf16[384,512]{1,0:T(8,128)(2,1)S(1)}, bf16[384,512]{1,0:T(8,128)(2,1)}, u32[]{:S(2)}) copy-start(bf16[384,512]{1,0:T(8,128)(2,1)} %get-tuple-element.41.refs_4_) | copy-start | bytes 1179652
  16.5 14.3 %collective-permute-start.4 = (bf16[256,768]{1,0:T(8,128)(2,1)S(1)}, bf16[256,768]{1,0:T(8,128)(2,1)S(1)}, u32[]{:S(2)}, u32[]{:S(2)}) collective-permute-start(bf16[256,768]{1,0:T(8,128)(2,1)S(1)} %pad_maximum_fusion.refs_0_), channel_id=1, source_target_pairs={{0,2},{1,3},{2,0},{3,1},{4,6},{5,7},{6,4},{7,5},{8,10},{9,11},{10,... | collective-permute-start | bytes 1179656 | tf_op jit(solution)/shard_map/ppermute | solution.py:298
  20.3 30.6 %all-to-all-start = ((bf16[8,384,128]{2,1,0:T(8,128)(2,1)}), bf16[8,384,128]{2,1,0:T(8,128)(2,1)S(1)}, u32[]{:S(2)}, u32[]{:S(2)}) async-start(bf16[8,384,128]{2,1,0:T(8,128)(2,1)} %shard_map.102), calls=%async_computation | async-start | bytes 1572864 | tf_op jit(solution)/shard_map/all_to_all | solution.py:351
  27.1 3.8 %collective-permute-start.5 = (bf16[256,768]{1,0:T(8,128)(2,1)S(1)}, bf16[256,768]{1,0:T(8,128)(2,1)S(1)}, u32[]{:S(2)}, u32[]{:S(2)}) collective-permute-start(bf16[256,768]{1,0:T(8,128)(2,1)S(1)} %pad_maximum_fusion.refs_0_), channel_id=1, source_target_pairs={{0,1},{1,0},{2,3},{3,2},{4,5},{5,4},{6,7},{7,6},{8,9},{9,8},{10,11... | collective-permute-start | bytes 1179656 | tf_op jit(solution)/shard_map/ppermute | solution.py:298
  30.8 1.7 %collective-permute-start.6 = (bf16[256,768]{1,0:T(8,128)(2,1)S(1)}, bf16[256,768]{1,0:T(8,128)(2,1)S(1)}, u32[]{:S(2)}, u32[]{:S(2)}) collective-permute-start(bf16[256,768]{1,0:T(8,128)(2,1)S(1)} %collective-permute-done.4.refs_1_), channel_id=1, source_target_pairs={{0,1},{1,0},{2,3},{3,2},{4,5},{5,4},{6,7},{7,6},{8,9},{9,8},{10,11... | collective-permute-start | bytes 1179656 | tf_op jit(solution)/shard_map/ppermute | solution.py:298
  32.6 18.3 %copy-start.1 = (bf16[2,512,128]{2,1,0:T(8,128)(2,1)S(1)}, bf16[2,512,128]{2,1,0:T(8,128)(2,1)}, u32[]{:S(2)}) copy-start(bf16[2,512,128]{2,1,0:T(8,128)(2,1)} %get-tuple-element.34.text_ref) | copy-start | bytes 786436
  34.2 1.1 copy-start.2
  35.4 10.6 %collective-permute-start.7 = (bf16[1024,128]{1,0:T(8,128)(2,1)S(1)}, bf16[1024,128]{1,0:T(8,128)(2,1)S(1)}, u32[]{:S(2)}, u32[]{:S(2)}) collective-permute-start(bf16[1024,128]{1,0:T(8,128)(2,1)S(1)} %get-tuple-element.45), channel_id=1, source_target_pairs={{0,4},{1,5},{2,6},{3,7},{4,0},{5,1},{6,2},{7,3},{8,12},{9,13},{10,... | collective-permute-start | bytes 786440 | tf_op jit(solution)/shard_map/ppermute | solution.py:298
  46.1 14.6 %collective-permute-start.9 = (bf16[1024,128]{1,0:T(8,128)(2,1)S(1)}, bf16[1024,128]{1,0:T(8,128)(2,1)S(1)}, u32[]{:S(2)}, u32[]{:S(2)}) collective-permute-start(bf16[1024,128]{1,0:T(8,128)(2,1)S(1)} %add_convert_fusion), channel_id=1, source_target_pairs={{0,8},{1,9},{2,10},{3,11},{4,12},{5,13},{6,14},{7,15},{8,0},{9,1},... | collective-permute-start | bytes 786440 | tf_op jit(solution)/shard_map/ppermute | solution.py:298
  48.4 12.3 %collective-permute-start.8 = (bf16[1024,128]{1,0:T(8,128)(2,1)S(1)}, bf16[1024,128]{1,0:T(8,128)(2,1)S(1)}, u32[]{:S(2)}, u32[]{:S(2)}) collective-permute-start(bf16[1024,128]{1,0:T(8,128)(2,1)S(1)} %get-tuple-element.46), channel_id=1, source_target_pairs={{0,4},{1,5},{2,6},{3,7},{4,0},{5,1},{6,2},{7,3},{8,12},{9,13},{10,... | collective-permute-start | bytes 786440 | tf_op jit(solution)/shard_map/ppermute | solution.py:298
  60.6 13.5 %collective-permute-start.10 = (bf16[128,1024]{1,0:T(8,128)(2,1)S(1)}, bf16[128,1024]{1,0:T(8,128)(2,1)S(1)}, u32[]{:S(2)}, u32[]{:S(2)}) collective-permute-start(bf16[128,1024]{1,0:T(8,128)(2,1)S(1)} %get-tuple-element.49.out_ref.refs_0_), channel_id=1, source_target_pairs={{0,8},{1,9},{2,10},{3,11},{4,12},{5,13},{6,14},{7,15},{8,0},{9,1},... | collective-permute-start | bytes 786440 | tf_op jit(solution)/shard_map/ppermute | solution.py:298
  74.1 44.3 %all-to-all-start.1 = ((bf16[8,384,128]{2,1,0:T(8,128)(2,1)}), bf16[8,384,128]{2,1,0:T(8,128)(2,1)S(1)}, u32[]{:S(2)}, u32[]{:S(2)}) async-start(bf16[8,384,128]{2,1,0:T(8,128)(2,1)} %shard_map.106), calls=%async_computation.1 | async-start | bytes 1572864 | tf_op jit(solution)/shard_map/all_to_all | solution.py:385
  77.8 22.1 %collective-permute-start.11 = (bf16[128,1024]{1,0:T(8,128)(2,1)S(1)}, bf16[128,1024]{1,0:T(8,128)(2,1)S(1)}, u32[]{:S(2)}, u32[]{:S(2)}) collective-permute-start(bf16[128,1024]{1,0:T(8,128)(2,1)S(1)} %get-tuple-element.49.out_ref.refs_0_), channel_id=1, source_target_pairs={{0,4},{1,5},{2,6},{3,7},{4,0},{5,1},{6,2},{7,3},{8,12},{9,13},{10,... | collective-permute-start | bytes 786440 | tf_op jit(solution)/shard_map/ppermute | solution.py:298
  79.8 24.4 %collective-permute-start.12 = (bf16[128,1024]{1,0:T(8,128)(2,1)S(1)}, bf16[128,1024]{1,0:T(8,128)(2,1)S(1)}, u32[]{:S(2)}, u32[]{:S(2)}) collective-permute-start(bf16[128,1024]{1,0:T(8,128)(2,1)S(1)} %collective-permute-done.10.refs_2_), channel_id=1, source_target_pairs={{0,4},{1,5},{2,6},{3,7},{4,0},{5,1},{6,2},{7,3},{8,12},{9,13},{10,... | collective-permute-start | bytes 786440 | tf_op jit(solution)/shard_map/ppermute | solution.py:298
  104.3 1.4 %copy-start.3 = (bf16[1024,768]{1,0:T(8,128)(2,1)S(1)}, bf16[1024,768]{1,0:T(8,128)(2,1)}, u32[]{:S(2)}) copy-start(bf16[1024,768]{1,0:T(8,128)(2,1)} %copy-done.2) | copy-start | bytes 4718596
  106.9 10.0 %collective-permute-start.13 = (bf16[512,384]{1,0:T(8,128)(2,1)S(1)}, bf16[512,384]{1,0:T(8,128)(2,1)S(1)}, u32[]{:S(2)}, u32[]{:S(2)}) collective-permute-start(bf16[512,384]{1,0:T(8,128)(2,1)S(1)} %get-tuple-element.57), channel_id=1, source_target_pairs={{0,2},{1,3},{2,0},{3,1},{4,6},{5,7},{6,4},{7,5},{8,10},{9,11},{10,... | collective-permute-start | bytes 1179656 | tf_op jit(solution)/shard_map/ppermute | solution.py:298

commit v9 on v7

--- a/solution.py
+++ b/solution.py
@@ -334,6 +334,7 @@
         limit=60 * 1024 * 1024,
     )
     given = exchange(give, 1)
+    d_out, _ = lax.optimization_barrier((d_out, give))
     pieces = gather_cotangents(d_out)
     tok_in = lax.all_to_all(tok_out, "seq", split_axis=0, concat_axis=0, tiled=True)
 
@@ -345,7 +346,10 @@
         flops=4 * total * image * HD,
         moved=4 * total * image,
     )
+    out_far = exchange(out_t, 4)
+    outs = [out_t, exchange(out_t, 2), out_far, exchange(out_far, 2)]
     columns = pieces[0].shape[1]
+    keep, _ = lax.optimization_barrier((keep, out_t))
     mine, far, near, near_far, cot = call(
         partial_kernel,
         [shape((image, HD), F32)] * 2 + [shape((image, HD), BF16)] * 2 + [shape((image, columns), BF16)],
@@ -358,8 +362,15 @@
     far = exchange((far + near_far.astype(F32)).astype(BF16), 4)
     near, _ = lax.optimization_barrier((near, near_far))
     near = exchange(near, 2)
-    out_far = exchange(out_t, 4)
-    outs = [out_t, exchange(out_t, 2), out_far, exchange(out_far, 2)]
+    dw_own, dw_other = call(
+        weight_grad_kernel,
+        [shape((4 * HD, depth), BF16)] * 2,
+        [cot, *outs],
+        scratch=[pltpu.VMEM((4 * HD, image), BF16)],
+        flops=8 * image * columns * HD,
+        moved=2 * image * columns,
+    )
+    mine, _ = lax.optimization_barrier((mine, dw_own))
     (grad_out,) = call(
         functools.partial(backward_kernel, chunk=chunk),
         [shape((n, 3 * rows, HD), BF16)],
@@ -369,14 +380,6 @@
         moved=4 * total * image,
     )
     grad_in = lax.all_to_all(grad_out, "seq", split_axis=0, concat_axis=0, tiled=True)
-    dw_own, dw_other = call(
-        weight_grad_kernel,
-        [shape((4 * HD, depth), BF16)] * 2,
-        [cot, *outs],
-        scratch=[pltpu.VMEM((4 * HD, image), BF16)],
-        flops=8 * image * columns * HD,
-        moved=2 * image * columns,
-    )
     grads = call(
         unpack_kernel,
         [shape((rows, width), BF16)] * 3,

time: 126 us -> 127 us (level)
  waiting for transfers between devices: 73.5 us -> 80.9 us
  starting transfers between devices: 31.2 us -> 27 us
  local copies, waits for them, and re-layouts: 2.23 us -> 0.06 us
    ppermute x14, waiting for transfers between devices: 73.5 us -> 80.9 us  [exchange(): return lax.ppermute(array, ('seq', 'fsdp'), pairs)]
    ppermute x14, starting transfers between devices: 19.2 us -> 14.9 us  [exchange(): return lax.ppermute(array, ('seq', 'fsdp'), pairs)]
    all_to_all x1, starting transfers between devices: 4.06 us -> 7.43 us  [local(): lax.all_to_all(tok_out, 'seq', split_axis=0, concat_axis=0, tiled=True)]
    all_to_all x1, starting transfers between devices: 7.94 us -> 4.68 us  [local(): lax.all_to_all(grad_out, 'seq', split_axis=0, concat_axis=0, tiled=True)]
  transfers between devices with their start and end apart: 16 -> 16, of which waited for: 10 -> 8; matrix products, arithmetic and copies ran while one was open for 0% -> 0% of each run, Pallas kernels for 10% -> 6%
where the time goes in v9:
time: 127 us
  waiting for transfers between devices  80.9 us (64%)
  starting transfers between devices  27 us (21%)
  Pallas kernels  17.8 us (14%)
    ppermute x14, waiting for transfers between devices, exchange(): return lax.ppermute(array, ('seq', 'fsdp'), pairs)  80.9 us
    pallas_call x7, Pallas kernels, call(): pl.pallas_call(kernel, out_shape=outs, grid_spec=pltpu.PrefetchScalarGrid...  17.8 us
    ppermute x14, starting transfers between devices, exchange(): return lax.ppermute(array, ('seq', 'fsdp'), pairs)  14.9 us
    all_to_all x1, starting transfers between devices, local(): lax.all_to_all(tok_out, 'seq', split_axis=0, concat_axis=0, tiled=True)  7.43 us
    all_to_all x1, starting transfers between devices, local(): lax.all_to_all(grad_out, 'seq', split_axis=0, concat_axis=0, tiled=True)  4.68 us
  transfers between devices with their start and end apart: 16, of which 8 were waited for; matrix products, arithmetic and copies ran while one was open for 0% of the time, Pallas kernels for 6%

profile of v9, /device:TPU:0, one launch (start us, length us, event | category | flops | bytes accessed | tf_op | source)
XLA Modules:
  0.0 126.6 jit_solution(5286699780957357948)
XLA Ops:
  0.6 2.9 %shard_map.102 = (bf16[8,384,128]{2,1,0:T(8,128)(2,1)}, bf16[384,512]{1,0:T(8,128)(2,1)}, bf16[384,512]{1,0:T(8,128)(2,1)}, bf16[2,512,128]{2,1,0:T(8,128)(2,1)}) custom-call(s32[1]{0:T(128)} %bitcast.me_ref, bf16[128,1024]{1,0:T(8,128)(2,1)} %q_ref.1, bf16[128,1024]{1,0:T(8,128)(2,1)} %k_ref.1, bf16[128,1024]{1,0:T(8,128)(2,1)} %v_ref.1, ...), custom_call_target="tpu_custom_call" | custom-call | bytes 3145728 | tf_op jit(solution)/shard_map/pallas_call | solution.py:147
  3.6 0.0 copy-start.2
  3.6 0.0 copy-start.1
  3.6 7.4 %all-to-all-start = ((bf16[8,384,128]{2,1,0:T(8,128)(2,1)}), bf16[8,384,128]{2,1,0:T(8,128)(2,1)S(1)}, u32[]{:S(2)}, u32[]{:S(2)}) async-start(bf16[8,384,128]{2,1,0:T(8,128)(2,1)} %get-tuple-element.27), calls=%async_computation | async-start | bytes 1572864 | tf_op jit(solution)/shard_map/all_to_all | solution.py:339
  11.0 0.0 copy-done.2
  11.1 3.9 %collective-permute-start.2 = (bf16[64,768]{1,0:T(8,128)(2,1)S(1)}, bf16[64,768]{1,0:T(8,128)(2,1)S(1)}, u32[]{:S(2)}, u32[]{:S(2)}) collective-permute-start(bf16[64,768]{1,0:T(8,128)(2,1)S(1)} %get-tuple-element.51), channel_id=1, source_target_pairs={{0,12},{1,13},{2,14},{3,15},{4,8},{5,9},{6,10},{7,11},{8,4},{9,5},... | collective-permute-start | bytes 294920 | tf_op jit(solution)/shard_map/ppermute | solution.py:295
  14.9 0.0 collective-permute-start.1
  14.9 0.6 collective-permute-start
  15.6 15.8 %collective-permute-done.2 = bf16[64,768]{1,0:T(8,128)(2,1)S(1)} collective-permute-done((bf16[64,768]{1,0:T(8,128)(2,1)S(1)}, bf16[64,768]{1,0:T(8,128)(2,1)S(1)}, u32[]{:S(2)}, u32[]{:S(2)}) %collective-permute-start.2) | collective-permute-done | bytes 98336 | tf_op jit(solution)/shard_map/ppermute | solution.py:295
  31.4 8.2 %collective-permute-done.1 = bf16[64,768]{1,0:T(8,128)(2,1)S(1)} collective-permute-done((bf16[64,768]{1,0:T(8,128)(2,1)S(1)}, bf16[64,768]{1,0:T(8,128)(2,1)S(1)}, u32[]{:S(2)}, u32[]{:S(2)}) %collective-permute-start.1) | collective-permute-done | bytes 98336 | tf_op jit(solution)/shard_map/ppermute | solution.py:295
  39.6 0.0 collective-permute-done
  39.6 0.0 copy-start
  39.6 1.5 %collective-permute-start.3 = (bf16[256,768]{1,0:T(8,128)(2,1)S(1)}, bf16[256,768]{1,0:T(8,128)(2,1)S(1)}, u32[]{:S(2)}, u32[]{:S(2)}) collective-permute-start(bf16[256,768]{1,0:T(8,128)(2,1)S(1)} %pad_maximum_fusion.refs_0_), channel_id=1, source_target_pairs={{0,2},{1,3},{2,0},{3,1},{4,6},{5,7},{6,4},{7,5},{8,10},{9,11},{10,... | collective-permute-start | bytes 1179656 | tf_op jit(solution)/shard_map/ppermute | solution.py:295
  41.1 0.6 collective-permute-start.6
  41.7 0.0 collective-permute-start.4
  41.7 10.0 %collective-permute-done.3.refs_1_ = bf16[256,768]{1,0:T(8,128)(2,1)S(1)} collective-permute-done((bf16[256,768]{1,0:T(8,128)(2,1)S(1)}, bf16[256,768]{1,0:T(8,128)(2,1)S(1)}, u32[]{:S(2)}, u32[]{:S(2)}) %collective-permute-start.3) | collective-permute-done | bytes 393248 | tf_op jit(solution)/shard_map/ppermute | solution.py:295
  51.8 0.0 collective-permute-start.5
  51.8 0.0 all-to-all-done.tok_ref
  51.8 0.0 copy-done.1
  51.8 4.9 %shard_map.103 = (bf16[1536,1024]{1,0:T(8,128)(2,1)S(1)}, bf16[128,1024]{1,0:T(8,128)(2,1)S(1)}, bf16[1024,128]{1,0:T(8,128)(2,1)S(1)}, bf16[128,1536]{1,0:T(8,128)(2,1)S(1)}, bf16[1536,128]{1,0:T(8,128)(2,1)S(1)}) custom-call(bf16[8,384,128]{2,1,0:T(8,128)(2,1)S(1)} %all-to-all-done.tok_ref, bf16[2,512,128]{2,1,0:T(8,128)(2,1)S(1)} %copy-done.1), custom_call_target="tpu_custom_call" | custom-call | flops 805306368 | bytes 6291456 | tf_op jit(solution)/shard_map/pallas_call | solution.py:147
  56.7 0.9 collective-permute-done.6.refs_5_
  57.6 0.0 collective-permute-done.4.refs_2_
  57.6 0.0 collective-permute-done.5.refs_3_
  57.6 0.0 copy-done
  57.6 1.7 %shard_map.104 = (f32[1024,128]{1,0:T(8,128)S(1)}, f32[1024,128]{1,0:T(8,128)S(1)}, bf16[1024,128]{1,0:T(8,128)(2,1)S(1)}, bf16[1024,128]{1,0:T(8,128)(2,1)S(1)}, bf16[1024,768]{1,0:T(8,128)(2,1)S(1)}) custom-call(bf16[256,768]{1,0:T(8,128)(2,1)S(1)} %pad_maximum_fusion.refs_0_, bf16[256,768]{1,0:T(8,128)(2,1)S(1)} %collective-permute-done.3.refs_1_, ...), custom_call_target="tpu_custom_call" | custom-call | flops 805306368 | bytes 1572864 | tf_op jit(solution)/shard_map/pallas_call | solution.py:147
  59.3 0.1 collective-permute-start.10
  59.4 3.2 %collective-permute-start.8 = (bf16[128,1024]{1,0:T(8,128)(2,1)S(1)}, bf16[128,1024]{1,0:T(8,128)(2,1)S(1)}, u32[]{:S(2)}, u32[]{:S(2)}) collective-permute-start(bf16[128,1024]{1,0:T(8,128)(2,1)S(1)} %get-tuple-element.33.refs_0_.out_ref), channel_id=1, source_target_pairs={{0,8},{1,9},{2,10},{3,11},{4,12},{5,13},{6,14},{7,15},{8,0},{9,1},... | collective-permute-start | bytes 786440 | tf_op jit(solution)/shard_map/ppermute | solution.py:295
  62.6 0.1 collective-permute-start.7
  62.7 11.2 %collective-permute-done.10 = bf16[1024,128]{1,0:T(8,128)(2,1)S(1)} collective-permute-done((bf16[1024,128]{1,0:T(8,128)(2,1)S(1)}, bf16[1024,128]{1,0:T(8,128)(2,1)S(1)}, u32[]{:S(2)}, u32[]{:S(2)}) %collective-permute-start.10) | collective-permute-done | bytes 262176 | tf_op jit(solution)/shard_map/ppermute | solution.py:295
  73.9 0.0 collective-permute-start.11
  73.9 0.0 collective-permute-done.8.refs_2_
  73.9 2.0 %collective-permute-start.9 = (bf16[128,1024]{1,0:T(8,128)(2,1)S(1)}, bf16[128,1024]{1,0:T(8,128)(2,1)S(1)}, u32[]{:S(2)}, u32[]{:S(2)}) collective-permute-start(bf16[128,1024]{1,0:T(8,128)(2,1)S(1)} %collective-permute-done.8.refs_2_), channel_id=1, source_target_pairs={{0,4},{1,5},{2,6},{3,7},{4,0},{5,1},{6,2},{7,3},{8,12},{9,13},{10,... | collective-permute-start | bytes 786440 | tf_op jit(solution)/shard_map/ppermute | solution.py:295
  75.9 0.1 add_convert_fusion
  76.0 0.9 collective-permute-start.12
  76.9 8.3 %collective-permute-done.7.refs_1_ = bf16[128,1024]{1,0:T(8,128)(2,1)S(1)} collective-permute-done((bf16[128,1024]{1,0:T(8,128)(2,1)S(1)}, bf16[128,1024]{1,0:T(8,128)(2,1)S(1)}, u32[]{:S(2)}, u32[]{:S(2)}) %collective-permute-start.7) | collective-permute-done | bytes 262176 | tf_op jit(solution)/shard_map/ppermute | solution.py:295
  85.2 10.1 %collective-permute-done.9.refs_3_ = bf16[128,1024]{1,0:T(8,128)(2,1)S(1)} collective-permute-done((bf16[128,1024]{1,0:T(8,128)(2,1)S(1)}, bf16[128,1024]{1,0:T(8,128)(2,1)S(1)}, u32[]{:S(2)}, u32[]{:S(2)}) %collective-permute-start.9) | collective-permute-done | bytes 262176 | tf_op jit(solution)/shard_map/ppermute | solution.py:295
  95.3 1.3 shard_map.105
  96.5 0.0 collective-permute-done.11.near_ref
  96.5 0.0 collective-permute-done.12.far_ref
  96.6 4.5 %shard_map.106 = bf16[8,384,128]{2,1,0:T(8,128)(2,1)} custom-call(bf16[1024,128]{1,0:T(8,128)(2,1)S(1)} %get-tuple-element.29.queries_ref, bf16[128,1536]{1,0:T(8,128)(2,1)S(1)} %get-tuple-element.30.keys_t_ref, bf16[1536,128]{1,0:T(8,128)(2,1)S(1)} %get-tuple-element.31.vals_ref, bf16[1536,1024]{1,0:T(8,128)(2,1)S(1)} %get-tuple-element.32.probs_ref, ...), custom_call_target="tpu_custom_call" | custom-call | flops 1610612736 | bytes 6291456 | tf_op jit(solution)/shard_map/pallas_call | solution.py:147
  101.0 4.7 %all-to-all-start.1 = ((bf16[8,384,128]{2,1,0:T(8,128)(2,1)}), bf16[8,384,128]{2,1,0:T(8,128)(2,1)S(1)}, u32[]{:S(2)}, u32[]{:S(2)}) async-start(bf16[8,384,128]{2,1,0:T(8,128)(2,1)} %shard_map.106), calls=%async_computation.1 | async-start | bytes 1572864 | tf_op jit(solution)/shard_map/all_to_all | solution.py:382
  105.7 2.0 %collective-permute-start.13 = (bf16[512,384]{1,0:T(8,128)(2,1)S(1)}, bf16[512,384]{1,0:T(8,128)(2,1)S(1)}, u32[]{:S(2)}, u32[]{:S(2)}) collective-permute-start(bf16[512,384]{1,0:T(8,128)(2,1)S(1)} %get-tuple-element.49), channel_id=1, source_target_pairs={{0,2},{1,3},{2,0},{3,1},{4,6},{5,7},{6,4},{7,5},{8,10},{9,11},{10,... | collective-permute-start | bytes 1179656 | tf_op jit(solution)/shard_map/ppermute | solution.py:295
  107.7 16.3 %collective-permute-done.13.other_ref = bf16[512,384]{1,0:T(8,128)(2,1)S(1)} collective-permute-done((bf16[512,384]{1,0:T(8,128)(2,1)S(1)}, bf16[512,384]{1,0:T(8,128)(2,1)S(1)}, u32[]{:S(2)}, u32[]{:S(2)}) %collective-permute-start.13) | collective-permute-done | bytes 393248 | tf_op jit(solution)/shard_map/ppermute | solution.py:295
  124.0 1.5 %shard_map.108 = f32[384,1024]{1,0:T(8,128)} custom-call(bf16[512,384]{1,0:T(8,128)(2,1)S(1)} %get-tuple-element.40.own_ref, bf16[512,384]{1,0:T(8,128)(2,1)S(1)} %collective-permute-done.13.other_ref), custom_call_target="tpu_custom_call" | custom-call | bytes 2359296 | tf_op jit(solution)/shard_map/pallas_call | solution.py:147
  125.5 0.0 all-to-all-done.1.tok_ref
  125.5 1.1 shard_map.107
  (2 shorter events, 0.1 us)
Async XLA Ops:
  3.6 7.4 %copy-start.2 = (bf16[128,3072]{1,0:T(8,128)(2,1)S(1)}, bf16[128,3072]{1,0:T(8,128)(2,1)}, u32[]{:S(2)}) copy-start(bf16[128,3072]{1,0:T(8,128)(2,1)} %param.13) | copy-start | bytes 2359300
  3.6 48.2 %copy-start.1 = (bf16[2,512,128]{2,1,0:T(8,128)(2,1)S(1)}, bf16[2,512,128]{2,1,0:T(8,128)(2,1)}, u32[]{:S(2)}) copy-start(bf16[2,512,128]{2,1,0:T(8,128)(2,1)} %get-tuple-element.28.text_ref) | copy-start | bytes 786436
  3.6 48.2 %all-to-all-start = ((bf16[8,384,128]{2,1,0:T(8,128)(2,1)}), bf16[8,384,128]{2,1,0:T(8,128)(2,1)S(1)}, u32[]{:S(2)}, u32[]{:S(2)}) async-start(bf16[8,384,128]{2,1,0:T(8,128)(2,1)} %get-tuple-element.27), calls=%async_computation | async-start | bytes 1572864 | tf_op jit(solution)/shard_map/all_to_all | solution.py:339
  11.1 20.3 %collective-permute-start.2 = (bf16[64,768]{1,0:T(8,128)(2,1)S(1)}, bf16[64,768]{1,0:T(8,128)(2,1)S(1)}, u32[]{:S(2)}, u32[]{:S(2)}) collective-permute-start(bf16[64,768]{1,0:T(8,128)(2,1)S(1)} %get-tuple-element.51), channel_id=1, source_target_pairs={{0,12},{1,13},{2,14},{3,15},{4,8},{5,9},{6,10},{7,11},{8,4},{9,5},... | collective-permute-start | bytes 294920 | tf_op jit(solution)/shard_map/ppermute | solution.py:295
  14.9 24.7 %collective-permute-start.1 = (bf16[64,768]{1,0:T(8,128)(2,1)S(1)}, bf16[64,768]{1,0:T(8,128)(2,1)S(1)}, u32[]{:S(2)}, u32[]{:S(2)}) collective-permute-start(bf16[64,768]{1,0:T(8,128)(2,1)S(1)} %get-tuple-element.52), channel_id=1, source_target_pairs={{0,8},{1,9},{2,10},{3,11},{4,12},{5,13},{6,14},{7,15},{8,0},{9,1},... | collective-permute-start | bytes 294920 | tf_op jit(solution)/shard_map/ppermute | solution.py:295
  14.9 24.7 %collective-permute-start = (bf16[64,768]{1,0:T(8,128)(2,1)S(1)}, bf16[64,768]{1,0:T(8,128)(2,1)S(1)}, u32[]{:S(2)}, u32[]{:S(2)}) collective-permute-start(bf16[64,768]{1,0:T(8,128)(2,1)S(1)} %get-tuple-element.53), channel_id=1, source_target_pairs={{0,4},{1,5},{2,6},{3,7},{4,0},{5,1},{6,2},{7,3},{8,12},{9,13},{10,... | collective-permute-start | bytes 294920 | tf_op jit(solution)/shard_map/ppermute | solution.py:295
  39.6 18.0 %copy-start = (bf16[384,512]{1,0:T(8,128)(2,1)S(1)}, bf16[384,512]{1,0:T(8,128)(2,1)}, u32[]{:S(2)}) copy-start(bf16[384,512]{1,0:T(8,128)(2,1)} %get-tuple-element.37.refs_4_) | copy-start | bytes 1179652
  39.6 12.1 %collective-permute-start.3 = (bf16[256,768]{1,0:T(8,128)(2,1)S(1)}, bf16[256,768]{1,0:T(8,128)(2,1)S(1)}, u32[]{:S(2)}, u32[]{:S(2)}) collective-permute-start(bf16[256,768]{1,0:T(8,128)(2,1)S(1)} %pad_maximum_fusion.refs_0_), channel_id=1, source_target_pairs={{0,2},{1,3},{2,0},{3,1},{4,6},{5,7},{6,4},{7,5},{8,10},{9,11},{10,... | collective-permute-start | bytes 1179656 | tf_op jit(solution)/shard_map/ppermute | solution.py:295
  41.1 16.5 %collective-permute-start.6 = (bf16[384,512]{1,0:T(8,128)(2,1)}, bf16[384,512]{1,0:T(8,128)(2,1)S(1)}, u32[]{:S(2)}, u32[]{:S(2)}) collective-permute-start(bf16[384,512]{1,0:T(8,128)(2,1)} %get-tuple-element.34), channel_id=1, source_target_pairs={{0,2},{1,3},{2,0},{3,1},{4,6},{5,7},{6,4},{7,5},{8,10},{9,11},{10,... | collective-permute-start | bytes 1179656 | tf_op jit(solution)/shard_map/ppermute | solution.py:295
  41.7 15.8 %collective-permute-start.4 = (bf16[256,768]{1,0:T(8,128)(2,1)S(1)}, bf16[256,768]{1,0:T(8,128)(2,1)S(1)}, u32[]{:S(2)}, u32[]{:S(2)}) collective-permute-start(bf16[256,768]{1,0:T(8,128)(2,1)S(1)} %pad_maximum_fusion.refs_0_), channel_id=1, source_target_pairs={{0,1},{1,0},{2,3},{3,2},{4,5},{5,4},{6,7},{7,6},{8,9},{9,8},{10,11... | collective-permute-start | bytes 1179656 | tf_op jit(solution)/shard_map/ppermute | solution.py:295
  51.8 5.8 %collective-permute-start.5 = (bf16[256,768]{1,0:T(8,128)(2,1)S(1)}, bf16[256,768]{1,0:T(8,128)(2,1)S(1)}, u32[]{:S(2)}, u32[]{:S(2)}) collective-permute-start(bf16[256,768]{1,0:T(8,128)(2,1)S(1)} %collective-permute-done.3.refs_1_), channel_id=1, source_target_pairs={{0,1},{1,0},{2,3},{3,2},{4,5},{5,4},{6,7},{7,6},{8,9},{9,8},{10,11... | collective-permute-start | bytes 1179656 | tf_op jit(solution)/shard_map/ppermute | solution.py:295
  59.3 14.6 %collective-permute-start.10 = (bf16[1024,128]{1,0:T(8,128)(2,1)S(1)}, bf16[1024,128]{1,0:T(8,128)(2,1)S(1)}, u32[]{:S(2)}, u32[]{:S(2)}) collective-permute-start(bf16[1024,128]{1,0:T(8,128)(2,1)S(1)} %get-tuple-element.43), channel_id=1, source_target_pairs={{0,4},{1,5},{2,6},{3,7},{4,0},{5,1},{6,2},{7,3},{8,12},{9,13},{10,... | collective-permute-start | bytes 786440 | tf_op jit(solution)/shard_map/ppermute | solution.py:295
  59.4 14.6 %collective-permute-start.8 = (bf16[128,1024]{1,0:T(8,128)(2,1)S(1)}, bf16[128,1024]{1,0:T(8,128)(2,1)S(1)}, u32[]{:S(2)}, u32[]{:S(2)}) collective-permute-start(bf16[128,1024]{1,0:T(8,128)(2,1)S(1)} %get-tuple-element.33.refs_0_.out_ref), channel_id=1, source_target_pairs={{0,8},{1,9},{2,10},{3,11},{4,12},{5,13},{6,14},{7,15},{8,0},{9,1},... | collective-permute-start | bytes 786440 | tf_op jit(solution)/shard_map/ppermute | solution.py:295
  62.6 22.6 %collective-permute-start.7 = (bf16[128,1024]{1,0:T(8,128)(2,1)S(1)}, bf16[128,1024]{1,0:T(8,128)(2,1)S(1)}, u32[]{:S(2)}, u32[]{:S(2)}) collective-permute-start(bf16[128,1024]{1,0:T(8,128)(2,1)S(1)} %get-tuple-element.33.refs_0_.out_ref), channel_id=1, source_target_pairs={{0,4},{1,5},{2,6},{3,7},{4,0},{5,1},{6,2},{7,3},{8,12},{9,13},{10,... | collective-permute-start | bytes 786440 | tf_op jit(solution)/shard_map/ppermute | solution.py:295
  73.9 22.6 %collective-permute-start.11 = (bf16[1024,128]{1,0:T(8,128)(2,1)S(1)}, bf16[1024,128]{1,0:T(8,128)(2,1)S(1)}, u32[]{:S(2)}, u32[]{:S(2)}) collective-permute-start(bf16[1024,128]{1,0:T(8,128)(2,1)S(1)} %get-tuple-element.44), channel_id=1, source_target_pairs={{0,4},{1,5},{2,6},{3,7},{4,0},{5,1},{6,2},{7,3},{8,12},{9,13},{10,... | collective-permute-start | bytes 786440 | tf_op jit(solution)/shard_map/ppermute | solution.py:295
  73.9 21.3 %collective-permute-start.9 = (bf16[128,1024]{1,0:T(8,128)(2,1)S(1)}, bf16[128,1024]{1,0:T(8,128)(2,1)S(1)}, u32[]{:S(2)}, u32[]{:S(2)}) collective-permute-start(bf16[128,1024]{1,0:T(8,128)(2,1)S(1)} %collective-permute-done.8.refs_2_), channel_id=1, source_target_pairs={{0,4},{1,5},{2,6},{3,7},{4,0},{5,1},{6,2},{7,3},{8,12},{9,13},{10,... | collective-permute-start | bytes 786440 | tf_op jit(solution)/shard_map/ppermute | solution.py:295
  76.0 20.5 %collective-permute-start.12 = (bf16[1024,128]{1,0:T(8,128)(2,1)S(1)}, bf16[1024,128]{1,0:T(8,128)(2,1)S(1)}, u32[]{:S(2)}, u32[]{:S(2)}) collective-permute-start(bf16[1024,128]{1,0:T(8,128)(2,1)S(1)} %add_convert_fusion), channel_id=1, source_target_pairs={{0,8},{1,9},{2,10},{3,11},{4,12},{5,13},{6,14},{7,15},{8,0},{9,1},... | collective-permute-start | bytes 786440 | tf_op jit(solution)/shard_map/ppermute | solution.py:295
  101.0 24.5 %all-to-all-start.1 = ((bf16[8,384,128]{2,1,0:T(8,128)(2,1)}), bf16[8,384,128]{2,1,0:T(8,128)(2,1)S(1)}, u32[]{:S(2)}, u32[]{:S(2)}) async-start(bf16[8,384,128]{2,1,0:T(8,128)(2,1)} %shard_map.106), calls=%async_computation.1 | async-start | bytes 1572864 | tf_op jit(solution)/shard_map/all_to_all | solution.py:382
  105.7 18.3 %collective-permute-start.13 = (bf16[512,384]{1,0:T(8,128)(2,1)S(1)}, bf16[512,384]{1,0:T(8,128)(2,1)S(1)}, u32[]{:S(2)}, u32[]{:S(2)}) collective-permute-start(bf16[512,384]{1,0:T(8,128)(2,1)S(1)} %get-tuple-element.49), channel_id=1, source_target_pairs={{0,2},{1,3},{2,0},{3,1},{4,6},{5,7},{6,4},{7,5},{8,10},{9,11},{10,... | collective-permute-start | bytes 1179656 | tf_op jit(solution)/shard_map/ppermute | solution.py:295

commit v10 on v8

--- a/solution.py
+++ b/solution.py
@@ -236,8 +236,10 @@
 
 def weight_grad_kernel(cot_ref, *refs):
     *out_refs, own_ref, other_ref, outs = refs
-    for i, ref in enumerate(out_refs):
-        outs[i * HD : (i + 1) * HD, :] = ref[...]
+    first = 0
+    for ref in out_refs:
+        outs[first : first + ref.shape[0], :] = ref[...]
+        first += ref.shape[0]
     depth = own_ref.shape[1]
     y = lax.rem(lax.axis_index("seq"), 2)
     for ref, row in ((own_ref, y), (other_ref, 1 - y)):
@@ -298,15 +300,18 @@
     return lax.ppermute(array, ("seq", "fsdp"), pairs)
 
 
-def gather_cotangents(d_out):
+def send_cotangents(d_out):
     rows, width = d_out.shape
     part, columns = rows // 2, width // len(STEPS)
     z = lax.axis_index("seq") // 2
     first = lax.axis_index("fsdp") * part
-    along = [
+    return [
         exchange(lax.dynamic_slice(d_out, (first, (z ^ (step // 2)) * columns), (part, columns)), step)
         for step in STEPS
     ]
+
+
+def gather_cotangents(along):
     row = jnp.concatenate(along, axis=0)
     pieces = [row, exchange(row, 1)]
     return pieces + [exchange(piece, cores=True) for piece in pieces]
@@ -339,7 +344,7 @@
     )
     d_out, give = lax.optimization_barrier((d_out, give))
     given = exchange(give, 1)
-    pieces = gather_cotangents(d_out)
+    along = send_cotangents(d_out)
     (tok_out,) = call(
         pack_kernel,
         [shape((n, 3 * rows, HD), BF16)],
@@ -347,7 +352,8 @@
         moved=4 * 3 * rows * width,
         limit=big,
     )
-    tok_out, given = lax.optimization_barrier((tok_out, given))
+    tok_out, along[1] = lax.optimization_barrier((tok_out, along[1]))
+    pieces = gather_cotangents(along)
     tok_in = lax.all_to_all(tok_out, "seq", split_axis=0, concat_axis=0, tiled=True)
 
     probs, out_t, queries, keys_t, vals = call(
@@ -368,11 +374,14 @@
         moved=2 * image * columns,
     )
     near_far = exchange(near_far, 2)
-    far = exchange((far + near_far.astype(F32)).astype(BF16), 4)
+    far, out_t = lax.optimization_barrier(((far + near_far.astype(F32)).astype(BF16), out_t))
+    far = exchange(far, 4)
     near, _ = lax.optimization_barrier((near, near_far))
     near = exchange(near, 2)
+    out_near = exchange(out_t, 2)
+    half = HD // 2
     out_late, far = lax.optimization_barrier((out_t, far))
-    out_far = exchange(out_late, 4)
+    out_far = [exchange(out_late[:half], 4), exchange(out_late[half:], 4)]
     (grad_out,) = call(
         functools.partial(backward_kernel, chunk=chunk),
         [shape((n, 3 * rows, HD), BF16)],
@@ -381,9 +390,9 @@
         flops=8 * total * image * HD,
         moved=4 * total * image,
     )
-    grad_out, out_far = lax.optimization_barrier((grad_out, out_far))
+    grad_out, out_far[0] = lax.optimization_barrier((grad_out, out_far[0]))
     grad_in = lax.all_to_all(grad_out, "seq", split_axis=0, concat_axis=0, tiled=True)
-    outs = [out_t, exchange(out_t, 2), out_far, exchange(out_far, 2)]
+    outs = [out_t, out_near, *out_far, *(exchange(part, 2) for part in out_far)]
     dw_own, dw_other = call(
         weight_grad_kernel,
         [shape((4 * HD, depth), BF16)] * 2,

time: 120 us -> 131 us (1.092)
  waiting for transfers between devices: 68.4 us -> 78.9 us
  starting transfers between devices: 28.4 us -> 30.2 us
  local copies, waits for them, and re-layouts: 2.59 us -> 1.21 us
    ppermute x14 -> x16, waiting for transfers between devices: 68.4 us -> 78.9 us  [exchange(): return lax.ppermute(array, ('seq', 'fsdp'), pairs)]
    all_to_all x1, starting transfers between devices: 3.69 us -> 6.21 us  [local(): lax.all_to_all(grad_out, 'seq', split_axis=0, concat_axis=0, tiled=True)]
    all_to_all x1, starting transfers between devices: 6.78 us -> 5.31 us  [local(): lax.all_to_all(tok_out, 'seq', split_axis=0, concat_axis=0, tiled=True)]
    unnamed x10 -> x12, local copies, waits for them, and re-layouts: 2.56 us -> 1.16 us
    ppermute x14 -> x16, starting transfers between devices: 17.9 us -> 18.6 us  [exchange(): return lax.ppermute(array, ('seq', 'fsdp'), pairs)]
  transfers between devices with their start and end apart: 16 -> 18, of which waited for: 12 -> 10; matrix products, arithmetic and copies ran while one was open for 0% -> 0% of each run, Pallas kernels for 13% -> 8%
where the time goes in v10:
time: 131 us; the launch traced here: 130 us
  waiting for transfers between devices  78.9 us (60%)
  starting transfers between devices  30.2 us (23%)
  Pallas kernels  19.3 us (15%)
    ppermute x16, waiting for transfers between devices, exchange(): return lax.ppermute(array, ('seq', 'fsdp'), pairs)  78.9 us
    pallas_call x8, Pallas kernels, call(): pl.pallas_call(kernel, out_shape=outs, grid_spec=pltpu.PrefetchScalarGrid...  19.3 us
    ppermute x16, starting transfers between devices, exchange(): return lax.ppermute(array, ('seq', 'fsdp'), pairs)  18.6 us
    all_to_all x1, starting transfers between devices, local(): lax.all_to_all(grad_out, 'seq', split_axis=0, concat_axis=0, tiled=True)  6.21 us
    all_to_all x1, starting transfers between devices, local(): lax.all_to_all(tok_out, 'seq', split_axis=0, concat_axis=0, tiled=True)  5.31 us
  transfers between devices with their start and end apart: 18, of which 10 were waited for; matrix products, arithmetic and copies ran while one was open for 0% of the time, Pallas kernels for 8%

profile of v10, /device:TPU:0, one launch (start us, length us, event | category | flops | bytes accessed | tf_op | source)
XLA Modules:
  0.0 130.5 jit_solution(13582825080524572423)
XLA Ops:
  0.7 2.3 %shard_map.103 = (bf16[384,512]{1,0:T(8,128)(2,1)}, bf16[384,512]{1,0:T(8,128)(2,1)}, bf16[2,512,128]{2,1,0:T(8,128)(2,1)}) custom-call(s32[1]{0:T(128)} %bitcast.me_ref, bf16[384,1024]{1,0:T(8,128)(2,1)} %w_ref.1, bf16[512,1024]{1,0:T(8,128)(2,1)} %kt_ref.1, bf16[512,1024]{1,0:T(8,128)(2,1)} %vt_ref.1), custom_call_target="tpu_custom_call" | custom-call | bytes 1572864 | tf_op jit(solution)/shard_map/pallas_call | solution.py:147
  3.1 3.1 %collective-permute-start = (bf16[64,768]{1,0:T(8,128)(2,1)S(1)}, bf16[64,768]{1,0:T(8,128)(2,1)S(1)}, u32[]{:S(2)}, u32[]{:S(2)}) collective-permute-start(bf16[64,768]{1,0:T(8,128)(2,1)S(1)} %get-tuple-element.65), channel_id=1, source_target_pairs={{0,4},{1,5},{2,6},{3,7},{4,0},{5,1},{6,2},{7,3},{8,12},{9,13},{10,... | collective-permute-start | bytes 294920 | tf_op jit(solution)/shard_map/ppermute | solution.py:300
  6.1 2.5 %collective-permute-start.2 = (bf16[64,768]{1,0:T(8,128)(2,1)S(1)}, bf16[64,768]{1,0:T(8,128)(2,1)S(1)}, u32[]{:S(2)}, u32[]{:S(2)}) collective-permute-start(bf16[64,768]{1,0:T(8,128)(2,1)S(1)} %get-tuple-element.63), channel_id=1, source_target_pairs={{0,12},{1,13},{2,14},{3,15},{4,8},{5,9},{6,10},{7,11},{8,4},{9,5},... | collective-permute-start | bytes 294920 | tf_op jit(solution)/shard_map/ppermute | solution.py:300
  8.6 0.1 collective-permute-start.1
  8.7 2.1 %shard_map.102 = bf16[8,384,128]{2,1,0:T(8,128)(2,1)} custom-call(bf16[128,1024]{1,0:T(8,128)(2,1)} %q_ref.1, bf16[128,1024]{1,0:T(8,128)(2,1)} %k_ref.1, bf16[128,1024]{1,0:T(8,128)(2,1)} %v_ref.1), custom_call_target="tpu_custom_call" | custom-call | bytes 1572864 | tf_op jit(solution)/shard_map/pallas_call | solution.py:147
  10.9 0.0 collective-permute-done
  10.9 5.3 %all-to-all-start = ((bf16[8,384,128]{2,1,0:T(8,128)(2,1)}), bf16[8,384,128]{2,1,0:T(8,128)(2,1)S(1)}, u32[]{:S(2)}, u32[]{:S(2)}) async-start(bf16[8,384,128]{2,1,0:T(8,128)(2,1)} %shard_map.102), calls=%async_computation | async-start | bytes 1572864 | tf_op jit(solution)/shard_map/all_to_all | solution.py:357
  16.2 0.0 collective-permute-done.2
  16.2 1.4 %collective-permute-done.1 = bf16[64,768]{1,0:T(8,128)(2,1)S(1)} collective-permute-done((bf16[64,768]{1,0:T(8,128)(2,1)S(1)}, bf16[64,768]{1,0:T(8,128)(2,1)S(1)}, u32[]{:S(2)}, u32[]{:S(2)}) %collective-permute-start.1) | collective-permute-done | bytes 98336 | tf_op jit(solution)/shard_map/ppermute | solution.py:300
  17.6 1.6 %collective-permute-start.3 = (bf16[256,768]{1,0:T(8,128)(2,1)S(1)}, bf16[256,768]{1,0:T(8,128)(2,1)S(1)}, u32[]{:S(2)}, u32[]{:S(2)}) collective-permute-start(bf16[256,768]{1,0:T(8,128)(2,1)S(1)} %pad_maximum_fusion.refs_0_), channel_id=1, source_target_pairs={{0,2},{1,3},{2,0},{3,1},{4,6},{5,7},{6,4},{7,5},{8,10},{9,11},{10,... | collective-permute-start | bytes 1179656 | tf_op jit(solution)/shard_map/ppermute | solution.py:300
  19.2 0.5 collective-permute-start.6
  19.7 0.0 collective-permute-start.4
  19.7 16.8 %collective-permute-done.3.refs_1_ = bf16[256,768]{1,0:T(8,128)(2,1)S(1)} collective-permute-done((bf16[256,768]{1,0:T(8,128)(2,1)S(1)}, bf16[256,768]{1,0:T(8,128)(2,1)S(1)}, u32[]{:S(2)}, u32[]{:S(2)}) %collective-permute-start.3) | collective-permute-done | bytes 393248 | tf_op jit(solution)/shard_map/ppermute | solution.py:300
  36.5 0.0 collective-permute-start.5
  36.5 7.4 %collective-permute-done.6.refs_5_ = bf16[384,512]{1,0:T(8,128)(2,1)S(1)} collective-permute-done((bf16[384,512]{1,0:T(8,128)(2,1)S(1)}, bf16[384,512]{1,0:T(8,128)(2,1)S(1)}, u32[]{:S(2)}, u32[]{:S(2)}) %collective-permute-start.6) | collective-permute-done | bytes 393248 | tf_op jit(solution)/shard_map/ppermute | solution.py:300
  43.8 0.0 collective-permute-done.4.refs_2_
  43.8 0.0 collective-permute-done.5.refs_3_
  43.8 0.0 copy-start.1
  43.9 1.7 %shard_map.105 = (f32[1024,128]{1,0:T(8,128)S(1)}, f32[1024,128]{1,0:T(8,128)S(1)}, bf16[1024,128]{1,0:T(8,128)(2,1)S(1)}, bf16[1024,128]{1,0:T(8,128)(2,1)S(1)}, bf16[1024,768]{1,0:T(8,128)(2,1)S(1)}) custom-call(bf16[256,768]{1,0:T(8,128)(2,1)S(1)} %pad_maximum_fusion.refs_0_, bf16[256,768]{1,0:T(8,128)(2,1)S(1)} %collective-permute-done.3.refs_1_, ...), custom_call_target="tpu_custom_call" | custom-call | flops 805306368 | bytes 1572864 | tf_op jit(solution)/shard_map/pallas_call | solution.py:147
  45.5 0.0 copy-start.2
  45.5 1.1 copy-done.2
  46.7 0.6 collective-permute-start.7
  47.3 6.6 %collective-permute-done.7 = bf16[1024,128]{1,0:T(8,128)(2,1)S(1)} collective-permute-done((bf16[1024,128]{1,0:T(8,128)(2,1)S(1)}, bf16[1024,128]{1,0:T(8,128)(2,1)S(1)}, u32[]{:S(2)}, u32[]{:S(2)}) %collective-permute-start.7) | collective-permute-done | bytes 262176 | tf_op jit(solution)/shard_map/ppermute | solution.py:300
  53.9 0.1 add_convert_fusion
  54.0 0.0 all-to-all-done.tok_ref
  54.0 4.9 %shard_map.104 = (bf16[1536,1024]{1,0:T(8,128)(2,1)S(1)}, bf16[128,1024]{1,0:T(8,128)(2,1)S(1)}, bf16[1024,128]{1,0:T(8,128)(2,1)S(1)}, bf16[128,1536]{1,0:T(8,128)(2,1)S(1)}, bf16[1536,128]{1,0:T(8,128)(2,1)S(1)}) custom-call(bf16[8,384,128]{2,1,0:T(8,128)(2,1)S(1)} %all-to-all-done.tok_ref, bf16[2,512,128]{2,1,0:T(8,128)(2,1)S(1)} %copy-done.1), custom_call_target="tpu_custom_call" | custom-call | flops 805306368 | bytes 6291456 | tf_op jit(solution)/shard_map/pallas_call | solution.py:147
  58.9 1.4 %collective-permute-start.9 = (bf16[1024,128]{1,0:T(8,128)(2,1)S(1)}, bf16[1024,128]{1,0:T(8,128)(2,1)S(1)}, u32[]{:S(2)}, u32[]{:S(2)}) collective-permute-start(bf16[1024,128]{1,0:T(8,128)(2,1)S(1)} %add_convert_fusion), channel_id=1, source_target_pairs={{0,8},{1,9},{2,10},{3,11},{4,12},{5,13},{6,14},{7,15},{8,0},{9,1},... | collective-permute-start | bytes 786440 | tf_op jit(solution)/shard_map/ppermute | solution.py:300
  60.3 0.8 collective-permute-start.8
  61.1 11.1 %collective-permute-done.9.far_ref = bf16[1024,128]{1,0:T(8,128)(2,1)S(1)} collective-permute-done((bf16[1024,128]{1,0:T(8,128)(2,1)S(1)}, bf16[1024,128]{1,0:T(8,128)(2,1)S(1)}, u32[]{:S(2)}, u32[]{:S(2)}) %collective-permute-start.9) | collective-permute-done | bytes 262176 | tf_op jit(solution)/shard_map/ppermute | solution.py:300
  72.2 0.1 collective-permute-start.10
  72.3 0.0 collective-permute-done.8.near_ref
  72.3 4.5 %shard_map.106 = bf16[8,384,128]{2,1,0:T(8,128)(2,1)} custom-call(bf16[1024,128]{1,0:T(8,128)(2,1)S(1)} %get-tuple-element.37.queries_ref, bf16[128,1536]{1,0:T(8,128)(2,1)S(1)} %get-tuple-element.38.keys_t_ref, bf16[1536,128]{1,0:T(8,128)(2,1)S(1)} %get-tuple-element.39.vals_ref, bf16[1536,1024]{1,0:T(8,128)(2,1)S(1)} %get-tuple-element.40.probs_ref, ...), custom_call_target="tpu_custom_call" | custom-call | flops 1610612736 | bytes 6291456 | tf_op jit(solution)/shard_map/pallas_call | solution.py:147
  76.8 1.4 %collective-permute-done.10.refs_2_ = bf16[64,1024]{1,0:T(8,128)(2,1)S(1)} collective-permute-done((bf16[64,1024]{1,0:T(8,128)(2,1)S(1)}, bf16[64,1024]{1,0:T(8,128)(2,1)S(1)}, u32[]{:S(2)}, u32[]{:S(2)}) %collective-permute-start.10) | collective-permute-done | bytes 131104 | tf_op jit(solution)/shard_map/ppermute | solution.py:300
  78.1 6.2 %all-to-all-start.1 = ((bf16[8,384,128]{2,1,0:T(8,128)(2,1)}), bf16[8,384,128]{2,1,0:T(8,128)(2,1)S(1)}, u32[]{:S(2)}, u32[]{:S(2)}) async-start(bf16[8,384,128]{2,1,0:T(8,128)(2,1)} %shard_map.106), calls=%async_computation.1 | async-start | bytes 1572864 | tf_op jit(solution)/shard_map/all_to_all | solution.py:394
  84.4 2.9 %collective-permute-start.12 = (bf16[64,1024]{1,0:T(8,128)(2,1)S(1)}, bf16[64,1024]{1,0:T(8,128)(2,1)S(1)}, u32[]{:S(2)}, u32[]{:S(2)}) collective-permute-start(bf16[64,1024]{1,0:T(8,128)(2,1)S(1)} %get-tuple-element.66), channel_id=1, source_target_pairs={{0,8},{1,9},{2,10},{3,11},{4,12},{5,13},{6,14},{7,15},{8,0},{9,1},... | collective-permute-start | bytes 393224 | tf_op jit(solution)/shard_map/ppermute | solution.py:300
  87.3 1.5 %collective-permute-start.11 = (bf16[128,1024]{1,0:T(8,128)(2,1)S(1)}, bf16[128,1024]{1,0:T(8,128)(2,1)S(1)}, u32[]{:S(2)}, u32[]{:S(2)}) collective-permute-start(bf16[128,1024]{1,0:T(8,128)(2,1)S(1)} %get-tuple-element.53.out_ref.refs_0_), channel_id=1, source_target_pairs={{0,4},{1,5},{2,6},{3,7},{4,0},{5,1},{6,2},{7,3},{8,12},{9,13},{10,... | collective-permute-start | bytes 786440 | tf_op jit(solution)/shard_map/ppermute | solution.py:300
  88.7 21.6 %collective-permute-done.12.refs_3_ = bf16[64,1024]{1,0:T(8,128)(2,1)S(1)} collective-permute-done((bf16[64,1024]{1,0:T(8,128)(2,1)S(1)}, bf16[64,1024]{1,0:T(8,128)(2,1)S(1)}, u32[]{:S(2)}, u32[]{:S(2)}) %collective-permute-start.12) | collective-permute-done | bytes 131104 | tf_op jit(solution)/shard_map/ppermute | solution.py:300
  110.3 0.0 collective-permute-start.14
  110.4 2.0 %collective-permute-start.13 = (bf16[64,1024]{1,0:T(8,128)(2,1)S(1)}, bf16[64,1024]{1,0:T(8,128)(2,1)S(1)}, u32[]{:S(2)}, u32[]{:S(2)}) collective-permute-start(bf16[64,1024]{1,0:T(8,128)(2,1)S(1)} %collective-permute-done.10.refs_2_), channel_id=1, source_target_pairs={{0,4},{1,5},{2,6},{3,7},{4,0},{5,1},{6,2},{7,3},{8,12},{9,13},{10,... | collective-permute-start | bytes 393224 | tf_op jit(solution)/shard_map/ppermute | solution.py:300
  112.4 0.0 collective-permute-done.11.refs_1_
  112.4 3.7 %collective-permute-done.14.refs_5_ = bf16[64,1024]{1,0:T(8,128)(2,1)S(1)} collective-permute-done((bf16[64,1024]{1,0:T(8,128)(2,1)S(1)}, bf16[64,1024]{1,0:T(8,128)(2,1)S(1)}, u32[]{:S(2)}, u32[]{:S(2)}) %collective-permute-start.14) | collective-permute-done | bytes 131104 | tf_op jit(solution)/shard_map/ppermute | solution.py:300
  116.1 1.4 %collective-permute-done.13.refs_4_ = bf16[64,1024]{1,0:T(8,128)(2,1)S(1)} collective-permute-done((bf16[64,1024]{1,0:T(8,128)(2,1)S(1)}, bf16[64,1024]{1,0:T(8,128)(2,1)S(1)}, u32[]{:S(2)}, u32[]{:S(2)}) %collective-permute-start.13) | collective-permute-done | bytes 131104 | tf_op jit(solution)/shard_map/ppermute | solution.py:300
  117.5 1.3 shard_map.108
  118.8 1.6 %collective-permute-start.15 = (bf16[512,384]{1,0:T(8,128)(2,1)S(1)}, bf16[512,384]{1,0:T(8,128)(2,1)S(1)}, u32[]{:S(2)}, u32[]{:S(2)}) collective-permute-start(bf16[512,384]{1,0:T(8,128)(2,1)S(1)} %get-tuple-element.61), channel_id=1, source_target_pairs={{0,2},{1,3},{2,0},{3,1},{4,6},{5,7},{6,4},{7,5},{8,10},{9,11},{10,... | collective-permute-start | bytes 1179656 | tf_op jit(solution)/shard_map/ppermute | solution.py:300
  120.4 7.5 %collective-permute-done.15.other_ref = bf16[512,384]{1,0:T(8,128)(2,1)S(1)} collective-permute-done((bf16[512,384]{1,0:T(8,128)(2,1)S(1)}, bf16[512,384]{1,0:T(8,128)(2,1)S(1)}, u32[]{:S(2)}, u32[]{:S(2)}) %collective-permute-start.15) | collective-permute-done | bytes 393248 | tf_op jit(solution)/shard_map/ppermute | solution.py:300
  127.9 1.5 %shard_map.109 = f32[384,1024]{1,0:T(8,128)} custom-call(bf16[512,384]{1,0:T(8,128)(2,1)S(1)} %get-tuple-element.60.own_ref, bf16[512,384]{1,0:T(8,128)(2,1)S(1)} %collective-permute-done.15.other_ref), custom_call_target="tpu_custom_call" | custom-call | bytes 2359296 | tf_op jit(solution)/shard_map/pallas_call | solution.py:147
  129.4 0.0 all-to-all-done.1.tok_ref
  129.4 1.1 shard_map.107
  (12 shorter events, 0.1 us)
Async XLA Ops:
  0.6 2.4 %copy-start.4 = (bf16[128,3072]{1,0:T(8,128)(2,1)S(1)}, bf16[128,3072]{1,0:T(8,128)(2,1)}, u32[]{:S(2)}) copy-start(bf16[128,3072]{1,0:T(8,128)(2,1)} %param.13) | copy-start | bytes 2359300
  3.1 7.8 %collective-permute-start = (bf16[64,768]{1,0:T(8,128)(2,1)S(1)}, bf16[64,768]{1,0:T(8,128)(2,1)S(1)}, u32[]{:S(2)}, u32[]{:S(2)}) collective-permute-start(bf16[64,768]{1,0:T(8,128)(2,1)S(1)} %get-tuple-element.65), channel_id=1, source_target_pairs={{0,4},{1,5},{2,6},{3,7},{4,0},{5,1},{6,2},{7,3},{8,12},{9,13},{10,... | collective-permute-start | bytes 294920 | tf_op jit(solution)/shard_map/ppermute | solution.py:300
  6.1 10.1 %collective-permute-start.2 = (bf16[64,768]{1,0:T(8,128)(2,1)S(1)}, bf16[64,768]{1,0:T(8,128)(2,1)S(1)}, u32[]{:S(2)}, u32[]{:S(2)}) collective-permute-start(bf16[64,768]{1,0:T(8,128)(2,1)S(1)} %get-tuple-element.63), channel_id=1, source_target_pairs={{0,12},{1,13},{2,14},{3,15},{4,8},{5,9},{6,10},{7,11},{8,4},{9,5},... | collective-permute-start | bytes 294920 | tf_op jit(solution)/shard_map/ppermute | solution.py:300
  8.6 8.9 %collective-permute-start.1 = (bf16[64,768]{1,0:T(8,128)(2,1)S(1)}, bf16[64,768]{1,0:T(8,128)(2,1)S(1)}, u32[]{:S(2)}, u32[]{:S(2)}) collective-permute-start(bf16[64,768]{1,0:T(8,128)(2,1)S(1)} %get-tuple-element.64), channel_id=1, source_target_pairs={{0,8},{1,9},{2,10},{3,11},{4,12},{5,13},{6,14},{7,15},{8,0},{9,1},... | collective-permute-start | bytes 294920 | tf_op jit(solution)/shard_map/ppermute | solution.py:300
  10.9 8.3 %copy-start.5 = (bf16[384,512]{1,0:T(8,128)(2,1)S(1)}, bf16[384,512]{1,0:T(8,128)(2,1)}, u32[]{:S(2)}) copy-start(bf16[384,512]{1,0:T(8,128)(2,1)} %get-tuple-element.43) | copy-start | bytes 1179652
  10.9 33.0 %copy-start = (bf16[384,512]{1,0:T(8,128)(2,1)S(1)}, bf16[384,512]{1,0:T(8,128)(2,1)}, u32[]{:S(2)}) copy-start(bf16[384,512]{1,0:T(8,128)(2,1)} %get-tuple-element.42.refs_4_) | copy-start | bytes 1179652
  10.9 43.1 %all-to-all-start = ((bf16[8,384,128]{2,1,0:T(8,128)(2,1)}), bf16[8,384,128]{2,1,0:T(8,128)(2,1)S(1)}, u32[]{:S(2)}, u32[]{:S(2)}) async-start(bf16[8,384,128]{2,1,0:T(8,128)(2,1)} %shard_map.102), calls=%async_computation | async-start | bytes 1572864 | tf_op jit(solution)/shard_map/all_to_all | solution.py:357
  17.6 18.9 %collective-permute-start.3 = (bf16[256,768]{1,0:T(8,128)(2,1)S(1)}, bf16[256,768]{1,0:T(8,128)(2,1)S(1)}, u32[]{:S(2)}, u32[]{:S(2)}) collective-permute-start(bf16[256,768]{1,0:T(8,128)(2,1)S(1)} %pad_maximum_fusion.refs_0_), channel_id=1, source_target_pairs={{0,2},{1,3},{2,0},{3,1},{4,6},{5,7},{6,4},{7,5},{8,10},{9,11},{10,... | collective-permute-start | bytes 1179656 | tf_op jit(solution)/shard_map/ppermute | solution.py:300
  19.2 24.6 %collective-permute-start.6 = (bf16[384,512]{1,0:T(8,128)(2,1)S(1)}, bf16[384,512]{1,0:T(8,128)(2,1)S(1)}, u32[]{:S(2)}, u32[]{:S(2)}) collective-permute-start(bf16[384,512]{1,0:T(8,128)(2,1)S(1)} %copy-done.5), channel_id=1, source_target_pairs={{0,2},{1,3},{2,0},{3,1},{4,6},{5,7},{6,4},{7,5},{8,10},{9,11},{10,... | collective-permute-start | bytes 1179656 | tf_op jit(solution)/shard_map/ppermute | solution.py:300
  19.7 24.1 %collective-permute-start.4 = (bf16[256,768]{1,0:T(8,128)(2,1)S(1)}, bf16[256,768]{1,0:T(8,128)(2,1)S(1)}, u32[]{:S(2)}, u32[]{:S(2)}) collective-permute-start(bf16[256,768]{1,0:T(8,128)(2,1)S(1)} %pad_maximum_fusion.refs_0_), channel_id=1, source_target_pairs={{0,1},{1,0},{2,3},{3,2},{4,5},{5,4},{6,7},{7,6},{8,9},{9,8},{10,11... | collective-permute-start | bytes 1179656 | tf_op jit(solution)/shard_map/ppermute | solution.py:300
  36.5 7.4 %collective-permute-start.5 = (bf16[256,768]{1,0:T(8,128)(2,1)S(1)}, bf16[256,768]{1,0:T(8,128)(2,1)S(1)}, u32[]{:S(2)}, u32[]{:S(2)}) collective-permute-start(bf16[256,768]{1,0:T(8,128)(2,1)S(1)} %collective-permute-done.3.refs_1_), channel_id=1, source_target_pairs={{0,1},{1,0},{2,3},{3,2},{4,5},{5,4},{6,7},{7,6},{8,9},{9,8},{10,11... | collective-permute-start | bytes 1179656 | tf_op jit(solution)/shard_map/ppermute | solution.py:300
  43.8 10.2 %copy-start.1 = (bf16[2,512,128]{2,1,0:T(8,128)(2,1)S(1)}, bf16[2,512,128]{2,1,0:T(8,128)(2,1)}, u32[]{:S(2)}) copy-start(bf16[2,512,128]{2,1,0:T(8,128)(2,1)} %get-tuple-element.36.text_ref) | copy-start | bytes 786436
  45.5 1.1 copy-start.2
  46.7 7.3 %collective-permute-start.7 = (bf16[1024,128]{1,0:T(8,128)(2,1)S(1)}, bf16[1024,128]{1,0:T(8,128)(2,1)S(1)}, u32[]{:S(2)}, u32[]{:S(2)}) collective-permute-start(bf16[1024,128]{1,0:T(8,128)(2,1)S(1)} %get-tuple-element.45), channel_id=1, source_target_pairs={{0,4},{1,5},{2,6},{3,7},{4,0},{5,1},{6,2},{7,3},{8,12},{9,13},{10,... | collective-permute-start | bytes 786440 | tf_op jit(solution)/shard_map/ppermute | solution.py:300
  58.9 13.3 %collective-permute-start.9 = (bf16[1024,128]{1,0:T(8,128)(2,1)S(1)}, bf16[1024,128]{1,0:T(8,128)(2,1)S(1)}, u32[]{:S(2)}, u32[]{:S(2)}) collective-permute-start(bf16[1024,128]{1,0:T(8,128)(2,1)S(1)} %add_convert_fusion), channel_id=1, source_target_pairs={{0,8},{1,9},{2,10},{3,11},{4,12},{5,13},{6,14},{7,15},{8,0},{9,1},... | collective-permute-start | bytes 786440 | tf_op jit(solution)/shard_map/ppermute | solution.py:300
  60.3 12.0 %collective-permute-start.8 = (bf16[1024,128]{1,0:T(8,128)(2,1)S(1)}, bf16[1024,128]{1,0:T(8,128)(2,1)S(1)}, u32[]{:S(2)}, u32[]{:S(2)}) collective-permute-start(bf16[1024,128]{1,0:T(8,128)(2,1)S(1)} %get-tuple-element.50), channel_id=1, source_target_pairs={{0,4},{1,5},{2,6},{3,7},{4,0},{5,1},{6,2},{7,3},{8,12},{9,13},{10,... | collective-permute-start | bytes 786440 | tf_op jit(solution)/shard_map/ppermute | solution.py:300
  72.2 5.9 %collective-permute-start.10 = (bf16[64,1024]{1,0:T(8,128)(2,1)S(1)}, bf16[64,1024]{1,0:T(8,128)(2,1)S(1)}, u32[]{:S(2)}, u32[]{:S(2)}) collective-permute-start(bf16[64,1024]{1,0:T(8,128)(2,1)S(1)} %get-tuple-element.67), channel_id=1, source_target_pairs={{0,8},{1,9},{2,10},{3,11},{4,12},{5,13},{6,14},{7,15},{8,0},{9,1},... | collective-permute-start | bytes 393224 | tf_op jit(solution)/shard_map/ppermute | solution.py:300
  76.8 40.7 %copy-start.3 = (bf16[1024,768]{1,0:T(8,128)(2,1)S(1)}, bf16[1024,768]{1,0:T(8,128)(2,1)}, u32[]{:S(2)}) copy-start(bf16[1024,768]{1,0:T(8,128)(2,1)} %copy-done.2) | copy-start | bytes 4718596
  78.1 51.2 %all-to-all-start.1 = ((bf16[8,384,128]{2,1,0:T(8,128)(2,1)}), bf16[8,384,128]{2,1,0:T(8,128)(2,1)S(1)}, u32[]{:S(2)}, u32[]{:S(2)}) async-start(bf16[8,384,128]{2,1,0:T(8,128)(2,1)} %shard_map.106), calls=%async_computation.1 | async-start | bytes 1572864 | tf_op jit(solution)/shard_map/all_to_all | solution.py:394
  84.4 26.0 %collective-permute-start.12 = (bf16[64,1024]{1,0:T(8,128)(2,1)S(1)}, bf16[64,1024]{1,0:T(8,128)(2,1)S(1)}, u32[]{:S(2)}, u32[]{:S(2)}) collective-permute-start(bf16[64,1024]{1,0:T(8,128)(2,1)S(1)} %get-tuple-element.66), channel_id=1, source_target_pairs={{0,8},{1,9},{2,10},{3,11},{4,12},{5,13},{6,14},{7,15},{8,0},{9,1},... | collective-permute-start | bytes 393224 | tf_op jit(solution)/shard_map/ppermute | solution.py:300
  87.3 25.1 %collective-permute-start.11 = (bf16[128,1024]{1,0:T(8,128)(2,1)S(1)}, bf16[128,1024]{1,0:T(8,128)(2,1)S(1)}, u32[]{:S(2)}, u32[]{:S(2)}) collective-permute-start(bf16[128,1024]{1,0:T(8,128)(2,1)S(1)} %get-tuple-element.53.out_ref.refs_0_), channel_id=1, source_target_pairs={{0,4},{1,5},{2,6},{3,7},{4,0},{5,1},{6,2},{7,3},{8,12},{9,13},{10,... | collective-permute-start | bytes 786440 | tf_op jit(solution)/shard_map/ppermute | solution.py:300
  110.3 5.8 %collective-permute-start.14 = (bf16[64,1024]{1,0:T(8,128)(2,1)S(1)}, bf16[64,1024]{1,0:T(8,128)(2,1)S(1)}, u32[]{:S(2)}, u32[]{:S(2)}) collective-permute-start(bf16[64,1024]{1,0:T(8,128)(2,1)S(1)} %collective-permute-done.12.refs_3_), channel_id=1, source_target_pairs={{0,4},{1,5},{2,6},{3,7},{4,0},{5,1},{6,2},{7,3},{8,12},{9,13},{10,... | collective-permute-start | bytes 393224 | tf_op jit(solution)/shard_map/ppermute | solution.py:300
  110.4 7.2 %collective-permute-start.13 = (bf16[64,1024]{1,0:T(8,128)(2,1)S(1)}, bf16[64,1024]{1,0:T(8,128)(2,1)S(1)}, u32[]{:S(2)}, u32[]{:S(2)}) collective-permute-start(bf16[64,1024]{1,0:T(8,128)(2,1)S(1)} %collective-permute-done.10.refs_2_), channel_id=1, source_target_pairs={{0,4},{1,5},{2,6},{3,7},{4,0},{5,1},{6,2},{7,3},{8,12},{9,13},{10,... | collective-permute-start | bytes 393224 | tf_op jit(solution)/shard_map/ppermute | solution.py:300
  118.8 9.1 %collective-permute-start.15 = (bf16[512,384]{1,0:T(8,128)(2,1)S(1)}, bf16[512,384]{1,0:T(8,128)(2,1)S(1)}, u32[]{:S(2)}, u32[]{:S(2)}) collective-permute-start(bf16[512,384]{1,0:T(8,128)(2,1)S(1)} %get-tuple-element.61), channel_id=1, source_target_pairs={{0,2},{1,3},{2,0},{3,1},{4,6},{5,7},{6,4},{7,5},{8,10},{9,11},{10,... | collective-permute-start | bytes 1179656 | tf_op jit(solution)/shard_map/ppermute | solution.py:300

commit v11 on v10

--- a/solution.py
+++ b/solution.py
@@ -353,6 +353,7 @@
         limit=big,
     )
     tok_out, along[1] = lax.optimization_barrier((tok_out, along[1]))
+    along, given = lax.optimization_barrier((along, given))
     pieces = gather_cotangents(along)
     tok_in = lax.all_to_all(tok_out, "seq", split_axis=0, concat_axis=0, tiled=True)
 
@@ -379,9 +380,8 @@
     near, _ = lax.optimization_barrier((near, near_far))
     near = exchange(near, 2)
     out_near = exchange(out_t, 2)
-    half = HD // 2
-    out_late, far = lax.optimization_barrier((out_t, far))
-    out_far = [exchange(out_late[:half], 4), exchange(out_late[half:], 4)]
+    out_late, far, out_near = lax.optimization_barrier((out_t, far, out_near))
+    out_far = exchange(out_late, 4)
     (grad_out,) = call(
         functools.partial(backward_kernel, chunk=chunk),
         [shape((n, 3 * rows, HD), BF16)],
@@ -390,15 +390,14 @@
         flops=8 * total * image * HD,
         moved=4 * total * image,
     )
-    grad_out, out_far[0] = lax.optimization_barrier((grad_out, out_far[0]))
     grad_in = lax.all_to_all(grad_out, "seq", split_axis=0, concat_axis=0, tiled=True)
-    outs = [out_t, out_near, *out_far, *(exchange(part, 2) for part in out_far)]
+    outs = [out_t, out_near, out_far, exchange(out_far, 2)]
     dw_own, dw_other = call(
         weight_grad_kernel,
         [shape((4 * HD, depth), BF16)] * 2,
         [cot, *outs],
         scratch=[pltpu.VMEM((4 * HD, image), BF16)],
-        flops=8 * image * columns * HD,
+        flops=256 * image * columns * HD,
         moved=2 * image * columns,
     )
     grads = call(

time: 131 us -> 113 us (0.86)
  waiting for transfers between devices: 78.9 us -> 62.5 us
  starting transfers between devices: 30.2 us -> 27.1 us
  local copies, waits for them, and re-layouts: 1.21 us -> 2.62 us
    ppermute x16 -> x14, waiting for transfers between devices: 78.9 us -> 62.5 us  [exchange(): return lax.ppermute(array, ('seq', 'fsdp'), pairs)]
    all_to_all x1, starting transfers between devices: 6.21 us -> 4.55 us  [local(): lax.all_to_all(grad_out, 'seq', split_axis=0, concat_axis=0, tiled=True)]
    unnamed x12 -> x13, local copies, waits for them, and re-layouts: 1.16 us -> 2.58 us
    ppermute x16 -> x14, starting transfers between devices: 18.6 us -> 18.2 us  [exchange(): return lax.ppermute(array, ('seq', 'fsdp'), pairs)]
  transfers between devices with their start and end apart: 18 -> 16, of which waited for: 10 -> 9; matrix products, arithmetic and copies ran while one was open for 0% -> 0% of each run, Pallas kernels for 8% -> 10%
where the time goes in v11:
time: 113 us; the launch traced here: 112 us
  waiting for transfers between devices  62.5 us (55%)
  starting transfers between devices  27.1 us (24%)
  Pallas kernels  19.3 us (17%)
  local copies, waits for them, and re-layouts  2.62 us (2%)
    ppermute x14, waiting for transfers between devices, exchange(): return lax.ppermute(array, ('seq', 'fsdp'), pairs)  62.5 us
    pallas_call x8, Pallas kernels, call(): pl.pallas_call(kernel, out_shape=outs, grid_spec=pltpu.PrefetchScalarGrid...  19.3 us
    ppermute x14, starting transfers between devices, exchange(): return lax.ppermute(array, ('seq', 'fsdp'), pairs)  18.2 us
    all_to_all x1, starting transfers between devices, local(): lax.all_to_all(grad_out, 'seq', split_axis=0, concat_axis=0, tiled=True)  4.55 us
    all_to_all x1, starting transfers between devices, local(): lax.all_to_all(tok_out, 'seq', split_axis=0, concat_axis=0, tiled=True)  4.37 us
    unnamed x13, local copies, waits for them, and re-layouts  2.58 us
  transfers between devices with their start and end apart: 16, of which 9 were waited for; matrix products, arithmetic and copies ran while one was open for 0% of the time, Pallas kernels for 10%

profile of v11, /device:TPU:0, one launch (start us, length us, event | category | flops | bytes accessed | tf_op | source)
XLA Modules:
  0.0 112.5 jit_solution(6965559156142336157)
XLA Ops:
  0.6 0.0 copy-start.4
  0.6 2.3 %shard_map.103 = (bf16[384,512]{1,0:T(8,128)(2,1)}, bf16[384,512]{1,0:T(8,128)(2,1)}, bf16[2,512,128]{2,1,0:T(8,128)(2,1)}) custom-call(s32[1]{0:T(128)} %bitcast.me_ref, bf16[384,1024]{1,0:T(8,128)(2,1)} %w_ref.1, bf16[512,1024]{1,0:T(8,128)(2,1)} %kt_ref.1, bf16[512,1024]{1,0:T(8,128)(2,1)} %vt_ref.1), custom_call_target="tpu_custom_call" | custom-call | bytes 1572864 | tf_op jit(solution)/shard_map/pallas_call | solution.py:147
  3.0 3.0 %collective-permute-start.3 = (bf16[384,512]{1,0:T(8,128)(2,1)}, bf16[384,512]{1,0:T(8,128)(2,1)S(1)}, u32[]{:S(2)}, u32[]{:S(2)}) collective-permute-start(bf16[384,512]{1,0:T(8,128)(2,1)} %get-tuple-element.46), channel_id=1, source_target_pairs={{0,2},{1,3},{2,0},{3,1},{4,6},{5,7},{6,4},{7,5},{8,10},{9,11},{10,... | collective-permute-start | bytes 1179656 | tf_op jit(solution)/shard_map/ppermute | solution.py:300
  6.0 0.0 copy-done.4
  6.0 1.6 %collective-permute-start = (bf16[64,768]{1,0:T(8,128)(2,1)S(1)}, bf16[64,768]{1,0:T(8,128)(2,1)S(1)}, u32[]{:S(2)}, u32[]{:S(2)}) collective-permute-start(bf16[64,768]{1,0:T(8,128)(2,1)S(1)} %get-tuple-element.73), channel_id=1, source_target_pairs={{0,4},{1,5},{2,6},{3,7},{4,0},{5,1},{6,2},{7,3},{8,12},{9,13},{10,... | collective-permute-start | bytes 294920 | tf_op jit(solution)/shard_map/ppermute | solution.py:300
  7.6 2.5 %collective-permute-start.2 = (bf16[64,768]{1,0:T(8,128)(2,1)S(1)}, bf16[64,768]{1,0:T(8,128)(2,1)S(1)}, u32[]{:S(2)}, u32[]{:S(2)}) collective-permute-start(bf16[64,768]{1,0:T(8,128)(2,1)S(1)} %get-tuple-element.70), channel_id=1, source_target_pairs={{0,12},{1,13},{2,14},{3,15},{4,8},{5,9},{6,10},{7,11},{8,4},{9,5},... | collective-permute-start | bytes 294920 | tf_op jit(solution)/shard_map/ppermute | solution.py:300
  10.1 0.1 collective-permute-start.1
  10.2 2.1 %shard_map.102 = bf16[8,384,128]{2,1,0:T(8,128)(2,1)} custom-call(bf16[128,1024]{1,0:T(8,128)(2,1)} %q_ref.1, bf16[128,1024]{1,0:T(8,128)(2,1)} %k_ref.1, bf16[128,1024]{1,0:T(8,128)(2,1)} %v_ref.1), custom_call_target="tpu_custom_call" | custom-call | bytes 1572864 | tf_op jit(solution)/shard_map/pallas_call | solution.py:147
  12.4 0.0 collective-permute-done
  12.4 4.4 %all-to-all-start = ((bf16[8,384,128]{2,1,0:T(8,128)(2,1)}), bf16[8,384,128]{2,1,0:T(8,128)(2,1)S(1)}, u32[]{:S(2)}, u32[]{:S(2)}) async-start(bf16[8,384,128]{2,1,0:T(8,128)(2,1)} %shard_map.102), calls=%async_computation | async-start | bytes 1572864 | tf_op jit(solution)/shard_map/all_to_all | solution.py:358
  16.8 0.0 collective-permute-done.2
  16.8 2.1 %collective-permute-done.1 = bf16[64,768]{1,0:T(8,128)(2,1)S(1)} collective-permute-done((bf16[64,768]{1,0:T(8,128)(2,1)S(1)}, bf16[64,768]{1,0:T(8,128)(2,1)S(1)}, u32[]{:S(2)}, u32[]{:S(2)}) %collective-permute-start.1) | collective-permute-done | bytes 98336 | tf_op jit(solution)/shard_map/ppermute | solution.py:300
  18.9 0.0 collective-permute-done.3.refs_5_
  18.9 0.5 collective-permute-start.4
  19.4 0.0 collective-permute-start.5
  19.4 16.2 %collective-permute-done.4.refs_1_ = bf16[256,768]{1,0:T(8,128)(2,1)S(1)} collective-permute-done((bf16[256,768]{1,0:T(8,128)(2,1)S(1)}, bf16[256,768]{1,0:T(8,128)(2,1)S(1)}, u32[]{:S(2)}, u32[]{:S(2)}) %collective-permute-start.4) | collective-permute-done | bytes 393248 | tf_op jit(solution)/shard_map/ppermute | solution.py:300
  35.7 0.0 collective-permute-start.6
  35.7 0.0 collective-permute-done.5.refs_2_
  35.7 1.7 %collective-permute-done.6.refs_3_ = bf16[256,768]{1,0:T(8,128)(2,1)S(1)} collective-permute-done((bf16[256,768]{1,0:T(8,128)(2,1)S(1)}, bf16[256,768]{1,0:T(8,128)(2,1)S(1)}, u32[]{:S(2)}, u32[]{:S(2)}) %collective-permute-start.6) | collective-permute-done | bytes 393248 | tf_op jit(solution)/shard_map/ppermute | solution.py:300
  37.4 0.0 copy-done
  37.4 1.7 %shard_map.105 = (f32[1024,128]{1,0:T(8,128)S(1)}, f32[1024,128]{1,0:T(8,128)S(1)}, bf16[1024,128]{1,0:T(8,128)(2,1)S(1)}, bf16[1024,128]{1,0:T(8,128)(2,1)S(1)}, bf16[1024,768]{1,0:T(8,128)(2,1)S(1)}) custom-call(bf16[256,768]{1,0:T(8,128)(2,1)S(1)} %constant_dynamic-update-slice_fusion.refs_0_, bf16[256,768]{1,0:T(8,128)(2,1)S(1)} %collective-permute-done.4.refs_1_, ...), custom_call_target="tpu_custom_call" | custom-call | flops 805306368 | bytes 1572864 | tf_op jit(solution)/shard_map/pallas_call | solution.py:147
  39.0 0.0 copy-start.2
  39.1 1.1 %copy-done.2 = bf16[1024,768]{1,0:T(8,128)(2,1)} copy-done((bf16[1024,768]{1,0:T(8,128)(2,1)}, bf16[1024,768]{1,0:T(8,128)(2,1)S(1)}, u32[]{:S(2)}) %copy-start.2) | copy-done | bytes 1572888
  40.2 0.6 collective-permute-start.7
  40.8 7.7 %collective-permute-done.7 = bf16[1024,128]{1,0:T(8,128)(2,1)S(1)} collective-permute-done((bf16[1024,128]{1,0:T(8,128)(2,1)S(1)}, bf16[1024,128]{1,0:T(8,128)(2,1)S(1)}, u32[]{:S(2)}, u32[]{:S(2)}) %collective-permute-start.7) | collective-permute-done | bytes 262176 | tf_op jit(solution)/shard_map/ppermute | solution.py:300
  48.5 0.1 add_convert_fusion
  48.6 0.0 all-to-all-done.tok_ref
  48.6 4.9 %shard_map.104 = (bf16[1536,1024]{1,0:T(8,128)(2,1)S(1)}, bf16[128,1024]{1,0:T(8,128)(2,1)S(1)}, bf16[1024,128]{1,0:T(8,128)(2,1)S(1)}, bf16[128,1536]{1,0:T(8,128)(2,1)S(1)}, bf16[1536,128]{1,0:T(8,128)(2,1)S(1)}) custom-call(bf16[8,384,128]{2,1,0:T(8,128)(2,1)S(1)} %all-to-all-done.tok_ref, bf16[2,512,128]{2,1,0:T(8,128)(2,1)S(1)} %copy-done.1), custom_call_target="tpu_custom_call" | custom-call | flops 805306368 | bytes 6291456 | tf_op jit(solution)/shard_map/pallas_call | solution.py:147
  53.5 2.5 %collective-permute-start.9 = (bf16[1024,128]{1,0:T(8,128)(2,1)S(1)}, bf16[1024,128]{1,0:T(8,128)(2,1)S(1)}, u32[]{:S(2)}, u32[]{:S(2)}) collective-permute-start(bf16[1024,128]{1,0:T(8,128)(2,1)S(1)} %add_convert_fusion), channel_id=1, source_target_pairs={{0,8},{1,9},{2,10},{3,11},{4,12},{5,13},{6,14},{7,15},{8,0},{9,1},... | collective-permute-start | bytes 786440 | tf_op jit(solution)/shard_map/ppermute | solution.py:300
  56.0 1.7 %collective-permute-start.10 = (bf16[128,1024]{1,0:T(8,128)(2,1)S(1)}, bf16[128,1024]{1,0:T(8,128)(2,1)S(1)}, u32[]{:S(2)}, u32[]{:S(2)}) collective-permute-start(bf16[128,1024]{1,0:T(8,128)(2,1)S(1)} %get-tuple-element.67.out_ref.refs_0_), channel_id=1, source_target_pairs={{0,4},{1,5},{2,6},{3,7},{4,0},{5,1},{6,2},{7,3},{8,12},{9,13},{10,... | collective-permute-start | bytes 786440 | tf_op jit(solution)/shard_map/ppermute | solution.py:300
  57.8 10.1 %collective-permute-done.9.far_ref = bf16[1024,128]{1,0:T(8,128)(2,1)S(1)} collective-permute-done((bf16[1024,128]{1,0:T(8,128)(2,1)S(1)}, bf16[1024,128]{1,0:T(8,128)(2,1)S(1)}, u32[]{:S(2)}, u32[]{:S(2)}) %collective-permute-start.9) | collective-permute-done | bytes 262176 | tf_op jit(solution)/shard_map/ppermute | solution.py:300
  67.9 0.4 collective-permute-done.10.refs_1_
  68.3 1.0 collective-permute-start.11
  69.2 2.6 %collective-permute-start.8 = (bf16[1024,128]{1,0:T(8,128)(2,1)S(1)}, bf16[1024,128]{1,0:T(8,128)(2,1)S(1)}, u32[]{:S(2)}, u32[]{:S(2)}) collective-permute-start(bf16[1024,128]{1,0:T(8,128)(2,1)S(1)} %get-tuple-element.59), channel_id=1, source_target_pairs={{0,4},{1,5},{2,6},{3,7},{4,0},{5,1},{6,2},{7,3},{8,12},{9,13},{10,... | collective-permute-start | bytes 786440 | tf_op jit(solution)/shard_map/ppermute | solution.py:300
  71.8 9.9 %collective-permute-done.11.refs_2_ = bf16[128,1024]{1,0:T(8,128)(2,1)S(1)} collective-permute-done((bf16[128,1024]{1,0:T(8,128)(2,1)S(1)}, bf16[128,1024]{1,0:T(8,128)(2,1)S(1)}, u32[]{:S(2)}, u32[]{:S(2)}) %collective-permute-start.11) | collective-permute-done | bytes 262176 | tf_op jit(solution)/shard_map/ppermute | solution.py:300
  81.7 0.0 collective-permute-start.12
  81.7 0.1 collective-permute-done.8.near_ref
  81.8 4.5 %shard_map.106 = bf16[8,384,128]{2,1,0:T(8,128)(2,1)} custom-call(bf16[1024,128]{1,0:T(8,128)(2,1)S(1)} %get-tuple-element.41.queries_ref, bf16[128,1536]{1,0:T(8,128)(2,1)S(1)} %get-tuple-element.42.keys_t_ref, bf16[1536,128]{1,0:T(8,128)(2,1)S(1)} %get-tuple-element.43.vals_ref, bf16[1536,1024]{1,0:T(8,128)(2,1)S(1)} %get-tuple-element.44.probs_ref, ...), custom_call_target="tpu_custom_call" | custom-call | flops 1610612736 | bytes 6291456 | tf_op jit(solution)/shard_map/pallas_call | solution.py:147
  86.3 4.6 %all-to-all-start.1 = ((bf16[8,384,128]{2,1,0:T(8,128)(2,1)}), bf16[8,384,128]{2,1,0:T(8,128)(2,1)S(1)}, u32[]{:S(2)}, u32[]{:S(2)}) async-start(bf16[8,384,128]{2,1,0:T(8,128)(2,1)} %shard_map.106), calls=%async_computation.1 | async-start | bytes 1572864 | tf_op jit(solution)/shard_map/all_to_all | solution.py:393
  90.8 0.0 collective-permute-done.12.refs_3_
  90.8 0.0 copy-start.3
  90.8 1.4 %copy-done.3 = bf16[1024,768]{1,0:T(8,128)(2,1)S(1)} copy-done((bf16[1024,768]{1,0:T(8,128)(2,1)S(1)}, bf16[1024,768]{1,0:T(8,128)(2,1)}, u32[]{:S(2)}) %copy-start.3) | copy-done | bytes 1572888
  92.2 1.3 %shard_map.108 = (bf16[512,384]{1,0:T(8,128)(2,1)S(1)}, bf16[512,384]{1,0:T(8,128)(2,1)S(1)}) custom-call(bf16[1024,768]{1,0:T(8,128)(2,1)S(1)} %copy-done.3, bf16[128,1024]{1,0:T(8,128)(2,1)S(1)} %get-tuple-element.67.out_ref.refs_0_, bf16[128,1024]{1,0:T(8,128)(2,1)S(1)} %collective-permute-done.10.refs_1_, ...), custom_call_target="tpu_custom_call" | custom-call | flops 25769803776 | bytes 1572864 | tf_op jit(solution)/shard_map/pallas_call | solution.py:147
  93.5 2.1 %collective-permute-start.13 = (bf16[512,384]{1,0:T(8,128)(2,1)S(1)}, bf16[512,384]{1,0:T(8,128)(2,1)S(1)}, u32[]{:S(2)}, u32[]{:S(2)}) collective-permute-start(bf16[512,384]{1,0:T(8,128)(2,1)S(1)} %get-tuple-element.69), channel_id=1, source_target_pairs={{0,2},{1,3},{2,0},{3,1},{4,6},{5,7},{6,4},{7,5},{8,10},{9,11},{10,... | collective-permute-start | bytes 1179656 | tf_op jit(solution)/shard_map/ppermute | solution.py:300
  95.6 14.3 %collective-permute-done.13.other_ref = bf16[512,384]{1,0:T(8,128)(2,1)S(1)} collective-permute-done((bf16[512,384]{1,0:T(8,128)(2,1)S(1)}, bf16[512,384]{1,0:T(8,128)(2,1)S(1)}, u32[]{:S(2)}, u32[]{:S(2)}) %collective-permute-start.13) | collective-permute-done | bytes 393248 | tf_op jit(solution)/shard_map/ppermute | solution.py:300
  109.9 1.5 %shard_map.109 = f32[384,1024]{1,0:T(8,128)} custom-call(bf16[512,384]{1,0:T(8,128)(2,1)S(1)} %get-tuple-element.68.own_ref, bf16[512,384]{1,0:T(8,128)(2,1)S(1)} %collective-permute-done.13.other_ref), custom_call_target="tpu_custom_call" | custom-call | bytes 2359296 | tf_op jit(solution)/shard_map/pallas_call | solution.py:147
  111.4 0.0 all-to-all-done.1.tok_ref
  111.4 1.1 shard_map.107
  (8 shorter events, 0.1 us)
Async XLA Ops:
  0.6 5.3 %copy-start.4 = (bf16[128,3072]{1,0:T(8,128)(2,1)S(1)}, bf16[128,3072]{1,0:T(8,128)(2,1)}, u32[]{:S(2)}) copy-start(bf16[128,3072]{1,0:T(8,128)(2,1)} %param.13) | copy-start | bytes 2359300
  3.0 15.9 %collective-permute-start.3 = (bf16[384,512]{1,0:T(8,128)(2,1)}, bf16[384,512]{1,0:T(8,128)(2,1)S(1)}, u32[]{:S(2)}, u32[]{:S(2)}) collective-permute-start(bf16[384,512]{1,0:T(8,128)(2,1)} %get-tuple-element.46), channel_id=1, source_target_pairs={{0,2},{1,3},{2,0},{3,1},{4,6},{5,7},{6,4},{7,5},{8,10},{9,11},{10,... | collective-permute-start | bytes 1179656 | tf_op jit(solution)/shard_map/ppermute | solution.py:300
  6.0 6.4 %collective-permute-start = (bf16[64,768]{1,0:T(8,128)(2,1)S(1)}, bf16[64,768]{1,0:T(8,128)(2,1)S(1)}, u32[]{:S(2)}, u32[]{:S(2)}) collective-permute-start(bf16[64,768]{1,0:T(8,128)(2,1)S(1)} %get-tuple-element.73), channel_id=1, source_target_pairs={{0,4},{1,5},{2,6},{3,7},{4,0},{5,1},{6,2},{7,3},{8,12},{9,13},{10,... | collective-permute-start | bytes 294920 | tf_op jit(solution)/shard_map/ppermute | solution.py:300
  7.6 9.1 %collective-permute-start.2 = (bf16[64,768]{1,0:T(8,128)(2,1)S(1)}, bf16[64,768]{1,0:T(8,128)(2,1)S(1)}, u32[]{:S(2)}, u32[]{:S(2)}) collective-permute-start(bf16[64,768]{1,0:T(8,128)(2,1)S(1)} %get-tuple-element.70), channel_id=1, source_target_pairs={{0,12},{1,13},{2,14},{3,15},{4,8},{5,9},{6,10},{7,11},{8,4},{9,5},... | collective-permute-start | bytes 294920 | tf_op jit(solution)/shard_map/ppermute | solution.py:300
  10.1 8.8 %collective-permute-start.1 = (bf16[64,768]{1,0:T(8,128)(2,1)S(1)}, bf16[64,768]{1,0:T(8,128)(2,1)S(1)}, u32[]{:S(2)}, u32[]{:S(2)}) collective-permute-start(bf16[64,768]{1,0:T(8,128)(2,1)S(1)} %get-tuple-element.71), channel_id=1, source_target_pairs={{0,8},{1,9},{2,10},{3,11},{4,12},{5,13},{6,14},{7,15},{8,0},{9,1},... | collective-permute-start | bytes 294920 | tf_op jit(solution)/shard_map/ppermute | solution.py:300
  12.4 25.0 %copy-start = (bf16[384,512]{1,0:T(8,128)(2,1)S(1)}, bf16[384,512]{1,0:T(8,128)(2,1)}, u32[]{:S(2)}) copy-start(bf16[384,512]{1,0:T(8,128)(2,1)} %get-tuple-element.51.refs_4_) | copy-start | bytes 1179652
  12.4 36.2 %all-to-all-start = ((bf16[8,384,128]{2,1,0:T(8,128)(2,1)}), bf16[8,384,128]{2,1,0:T(8,128)(2,1)S(1)}, u32[]{:S(2)}, u32[]{:S(2)}) async-start(bf16[8,384,128]{2,1,0:T(8,128)(2,1)} %shard_map.102), calls=%async_computation | async-start | bytes 1572864 | tf_op jit(solution)/shard_map/all_to_all | solution.py:358
  18.9 16.7 %collective-permute-start.4 = (bf16[256,768]{1,0:T(8,128)(2,1)S(1)}, bf16[256,768]{1,0:T(8,128)(2,1)S(1)}, u32[]{:S(2)}, u32[]{:S(2)}) collective-permute-start(bf16[256,768]{1,0:T(8,128)(2,1)S(1)} %constant_dynamic-update-slice_fusion.refs_0_), channel_id=1, source_target_pairs={{0,2},{1,3},{2,0},{3,1},{4,6},{5,7},{6,4},{7,5},{8,10},{9,11},{10,... | collective-permute-start | bytes 1179656 | tf_op jit(solution)/shard_map/ppermute | solution.py:300
  19.4 16.2 %collective-permute-start.5 = (bf16[256,768]{1,0:T(8,128)(2,1)S(1)}, bf16[256,768]{1,0:T(8,128)(2,1)S(1)}, u32[]{:S(2)}, u32[]{:S(2)}) collective-permute-start(bf16[256,768]{1,0:T(8,128)(2,1)S(1)} %constant_dynamic-update-slice_fusion.refs_0_), channel_id=1, source_target_pairs={{0,1},{1,0},{2,3},{3,2},{4,5},{5,4},{6,7},{7,6},{8,9},{9,8},{10,11... | collective-permute-start | bytes 1179656 | tf_op jit(solution)/shard_map/ppermute | solution.py:300
  35.7 1.7 %collective-permute-start.6 = (bf16[256,768]{1,0:T(8,128)(2,1)S(1)}, bf16[256,768]{1,0:T(8,128)(2,1)S(1)}, u32[]{:S(2)}, u32[]{:S(2)}) collective-permute-start(bf16[256,768]{1,0:T(8,128)(2,1)S(1)} %collective-permute-done.4.refs_1_), channel_id=1, source_target_pairs={{0,1},{1,0},{2,3},{3,2},{4,5},{5,4},{6,7},{7,6},{8,9},{9,8},{10,11... | collective-permute-start | bytes 1179656 | tf_op jit(solution)/shard_map/ppermute | solution.py:300
  37.4 11.2 %copy-start.1 = (bf16[2,512,128]{2,1,0:T(8,128)(2,1)S(1)}, bf16[2,512,128]{2,1,0:T(8,128)(2,1)}, u32[]{:S(2)}) copy-start(bf16[2,512,128]{2,1,0:T(8,128)(2,1)} %get-tuple-element.40.text_ref) | copy-start | bytes 786436
  39.0 1.1 %copy-start.2 = (bf16[1024,768]{1,0:T(8,128)(2,1)}, bf16[1024,768]{1,0:T(8,128)(2,1)S(1)}, u32[]{:S(2)}) copy-start(bf16[1024,768]{1,0:T(8,128)(2,1)S(1)} %get-tuple-element.65.cot_ref) | copy-start | bytes 4718596
  40.2 8.3 %collective-permute-start.7 = (bf16[1024,128]{1,0:T(8,128)(2,1)S(1)}, bf16[1024,128]{1,0:T(8,128)(2,1)S(1)}, u32[]{:S(2)}, u32[]{:S(2)}) collective-permute-start(bf16[1024,128]{1,0:T(8,128)(2,1)S(1)} %get-tuple-element.54), channel_id=1, source_target_pairs={{0,4},{1,5},{2,6},{3,7},{4,0},{5,1},{6,2},{7,3},{8,12},{9,13},{10,... | collective-permute-start | bytes 786440 | tf_op jit(solution)/shard_map/ppermute | solution.py:300
  53.5 14.3 %collective-permute-start.9 = (bf16[1024,128]{1,0:T(8,128)(2,1)S(1)}, bf16[1024,128]{1,0:T(8,128)(2,1)S(1)}, u32[]{:S(2)}, u32[]{:S(2)}) collective-permute-start(bf16[1024,128]{1,0:T(8,128)(2,1)S(1)} %add_convert_fusion), channel_id=1, source_target_pairs={{0,8},{1,9},{2,10},{3,11},{4,12},{5,13},{6,14},{7,15},{8,0},{9,1},... | collective-permute-start | bytes 786440 | tf_op jit(solution)/shard_map/ppermute | solution.py:300
  56.0 12.2 %collective-permute-start.10 = (bf16[128,1024]{1,0:T(8,128)(2,1)S(1)}, bf16[128,1024]{1,0:T(8,128)(2,1)S(1)}, u32[]{:S(2)}, u32[]{:S(2)}) collective-permute-start(bf16[128,1024]{1,0:T(8,128)(2,1)S(1)} %get-tuple-element.67.out_ref.refs_0_), channel_id=1, source_target_pairs={{0,4},{1,5},{2,6},{3,7},{4,0},{5,1},{6,2},{7,3},{8,12},{9,13},{10,... | collective-permute-start | bytes 786440 | tf_op jit(solution)/shard_map/ppermute | solution.py:300
  68.3 13.5 %collective-permute-start.11 = (bf16[128,1024]{1,0:T(8,128)(2,1)S(1)}, bf16[128,1024]{1,0:T(8,128)(2,1)S(1)}, u32[]{:S(2)}, u32[]{:S(2)}) collective-permute-start(bf16[128,1024]{1,0:T(8,128)(2,1)S(1)} %get-tuple-element.67.out_ref.refs_0_), channel_id=1, source_target_pairs={{0,8},{1,9},{2,10},{3,11},{4,12},{5,13},{6,14},{7,15},{8,0},{9,1},... | collective-permute-start | bytes 786440 | tf_op jit(solution)/shard_map/ppermute | solution.py:300
  69.2 12.6 %collective-permute-start.8 = (bf16[1024,128]{1,0:T(8,128)(2,1)S(1)}, bf16[1024,128]{1,0:T(8,128)(2,1)S(1)}, u32[]{:S(2)}, u32[]{:S(2)}) collective-permute-start(bf16[1024,128]{1,0:T(8,128)(2,1)S(1)} %get-tuple-element.59), channel_id=1, source_target_pairs={{0,4},{1,5},{2,6},{3,7},{4,0},{5,1},{6,2},{7,3},{8,12},{9,13},{10,... | collective-permute-start | bytes 786440 | tf_op jit(solution)/shard_map/ppermute | solution.py:300
  81.7 9.1 %collective-permute-start.12 = (bf16[128,1024]{1,0:T(8,128)(2,1)S(1)}, bf16[128,1024]{1,0:T(8,128)(2,1)S(1)}, u32[]{:S(2)}, u32[]{:S(2)}) collective-permute-start(bf16[128,1024]{1,0:T(8,128)(2,1)S(1)} %collective-permute-done.11.refs_2_), channel_id=1, source_target_pairs={{0,4},{1,5},{2,6},{3,7},{4,0},{5,1},{6,2},{7,3},{8,12},{9,13},{10,... | collective-permute-start | bytes 786440 | tf_op jit(solution)/shard_map/ppermute | solution.py:300
  86.3 25.1 %all-to-all-start.1 = ((bf16[8,384,128]{2,1,0:T(8,128)(2,1)}), bf16[8,384,128]{2,1,0:T(8,128)(2,1)S(1)}, u32[]{:S(2)}, u32[]{:S(2)}) async-start(bf16[8,384,128]{2,1,0:T(8,128)(2,1)} %shard_map.106), calls=%async_computation.1 | async-start | bytes 1572864 | tf_op jit(solution)/shard_map/all_to_all | solution.py:393
  90.8 1.4 %copy-start.3 = (bf16[1024,768]{1,0:T(8,128)(2,1)S(1)}, bf16[1024,768]{1,0:T(8,128)(2,1)}, u32[]{:S(2)}) copy-start(bf16[1024,768]{1,0:T(8,128)(2,1)} %copy-done.2) | copy-start | bytes 4718596
  93.5 16.4 %collective-permute-start.13 = (bf16[512,384]{1,0:T(8,128)(2,1)S(1)}, bf16[512,384]{1,0:T(8,128)(2,1)S(1)}, u32[]{:S(2)}, u32[]{:S(2)}) collective-permute-start(bf16[512,384]{1,0:T(8,128)(2,1)S(1)} %get-tuple-element.69), channel_id=1, source_target_pairs={{0,2},{1,3},{2,0},{3,1},{4,6},{5,7},{6,4},{7,5},{8,10},{9,11},{10,... | collective-permute-start | bytes 1179656 | tf_op jit(solution)/shard_map/ppermute | solution.py:300

commit v12 on v11

--- a/solution.py
+++ b/solution.py
@@ -374,14 +374,23 @@
         flops=8 * image * columns * HD,
         moved=2 * image * columns,
     )
+    out_near, out_far = exchange(out_t, 2), exchange(out_t, 4)
+    near_far, _ = lax.optimization_barrier((near_far, out_t))
     near_far = exchange(near_far, 2)
-    far, out_t = lax.optimization_barrier(((far + near_far.astype(F32)).astype(BF16), out_t))
+    far, out_far = lax.optimization_barrier(((far + near_far.astype(F32)).astype(BF16), out_far))
     far = exchange(far, 4)
     near, _ = lax.optimization_barrier((near, near_far))
     near = exchange(near, 2)
-    out_near = exchange(out_t, 2)
-    out_late, far, out_near = lax.optimization_barrier((out_t, far, out_near))
-    out_far = exchange(out_late, 4)
+    outs = [out_t, out_near, out_far, exchange(out_far, 2)]
+    dw_own, dw_other = call(
+        weight_grad_kernel,
+        [shape((4 * HD, depth), BF16)] * 2,
+        [cot, *outs],
+        scratch=[pltpu.VMEM((4 * HD, image), BF16)],
+        flops=8 * image * columns * HD,
+        moved=2 * image * columns,
+    )
+    mine, _ = lax.optimization_barrier((mine, dw_own))
     (grad_out,) = call(
         functools.partial(backward_kernel, chunk=chunk),
         [shape((n, 3 * rows, HD), BF16)],
@@ -391,15 +400,6 @@
         moved=4 * total * image,
     )
     grad_in = lax.all_to_all(grad_out, "seq", split_axis=0, concat_axis=0, tiled=True)
-    outs = [out_t, out_near, out_far, exchange(out_far, 2)]
-    dw_own, dw_other = call(
-        weight_grad_kernel,
-        [shape((4 * HD, depth), BF16)] * 2,
-        [cot, *outs],
-        scratch=[pltpu.VMEM((4 * HD, image), BF16)],
-        flops=256 * image * columns * HD,
-        moved=2 * image * columns,
-    )
     grads = call(
         unpack_kernel,
         [shape((rows, width), BF16)] * 3,

time: 113 us -> 113 us (level)
  waiting for transfers between devices: 62.5 us -> 64.2 us
  local copies, waits for them, and re-layouts: 2.62 us -> 1.22 us
    ppermute x14, waiting for transfers between devices: 62.5 us -> 64.2 us  [exchange(): return lax.ppermute(array, ('seq', 'fsdp'), pairs)]
    unnamed x13, local copies, waits for them, and re-layouts: 2.58 us -> 1.18 us
  transfers between devices with their start and end apart: 16 -> 16, of which waited for: 9 -> 9; matrix products, arithmetic and copies ran while one was open for 0% -> 0% of each run, Pallas kernels for 10% -> 6%
where the time goes in v12:
time: 113 us; the launch traced here: 112 us
  waiting for transfers between devices  64.2 us (57%)
  starting transfers between devices  26.7 us (24%)
  Pallas kernels  19.3 us (17%)
  local copies, waits for them, and re-layouts  1.22 us (1%)
    ppermute x14, waiting for transfers between devices, exchange(): return lax.ppermute(array, ('seq', 'fsdp'), pairs)  64.2 us
    pallas_call x8, Pallas kernels, call(): pl.pallas_call(kernel, out_shape=outs, grid_spec=pltpu.PrefetchScalarGrid...  19.3 us
    ppermute x14, starting transfers between devices, exchange(): return lax.ppermute(array, ('seq', 'fsdp'), pairs)  17.4 us
    all_to_all x1, starting transfers between devices, local(): lax.all_to_all(grad_out, 'seq', split_axis=0, concat_axis=0, tiled=True)  4.91 us
    all_to_all x1, starting transfers between devices, local(): lax.all_to_all(tok_out, 'seq', split_axis=0, concat_axis=0, tiled=True)  4.37 us
  transfers between devices with their start and end apart: 16, of which 9 were waited for; matrix products, arithmetic and copies ran while one was open for 0% of the time, Pallas kernels for 6%

profile of v12, /device:TPU:0, one launch (start us, length us, event | category | flops | bytes accessed | tf_op | source)
XLA Modules:
  0.0 112.2 jit_solution(17126409878967831382)
XLA Ops:
  0.6 0.0 copy-start.4
  0.6 2.3 %shard_map.103 = (bf16[384,512]{1,0:T(8,128)(2,1)}, bf16[384,512]{1,0:T(8,128)(2,1)}, bf16[2,512,128]{2,1,0:T(8,128)(2,1)}) custom-call(s32[1]{0:T(128)} %bitcast.me_ref, bf16[384,1024]{1,0:T(8,128)(2,1)} %w_ref.1, bf16[512,1024]{1,0:T(8,128)(2,1)} %kt_ref.1, bf16[512,1024]{1,0:T(8,128)(2,1)} %vt_ref.1), custom_call_target="tpu_custom_call" | custom-call | bytes 1572864 | tf_op jit(solution)/shard_map/pallas_call | solution.py:147
  3.0 3.0 %collective-permute-start.3 = (bf16[384,512]{1,0:T(8,128)(2,1)}, bf16[384,512]{1,0:T(8,128)(2,1)S(1)}, u32[]{:S(2)}, u32[]{:S(2)}) collective-permute-start(bf16[384,512]{1,0:T(8,128)(2,1)} %get-tuple-element.46), channel_id=1, source_target_pairs={{0,2},{1,3},{2,0},{3,1},{4,6},{5,7},{6,4},{7,5},{8,10},{9,11},{10,... | collective-permute-start | bytes 1179656 | tf_op jit(solution)/shard_map/ppermute | solution.py:300
  6.0 0.0 copy-done.4
  6.0 1.6 %collective-permute-start = (bf16[64,768]{1,0:T(8,128)(2,1)S(1)}, bf16[64,768]{1,0:T(8,128)(2,1)S(1)}, u32[]{:S(2)}, u32[]{:S(2)}) collective-permute-start(bf16[64,768]{1,0:T(8,128)(2,1)S(1)} %get-tuple-element.71), channel_id=1, source_target_pairs={{0,4},{1,5},{2,6},{3,7},{4,0},{5,1},{6,2},{7,3},{8,12},{9,13},{10,... | collective-permute-start | bytes 294920 | tf_op jit(solution)/shard_map/ppermute | solution.py:300
  7.6 2.5 %collective-permute-start.2 = (bf16[64,768]{1,0:T(8,128)(2,1)S(1)}, bf16[64,768]{1,0:T(8,128)(2,1)S(1)}, u32[]{:S(2)}, u32[]{:S(2)}) collective-permute-start(bf16[64,768]{1,0:T(8,128)(2,1)S(1)} %get-tuple-element.68), channel_id=1, source_target_pairs={{0,12},{1,13},{2,14},{3,15},{4,8},{5,9},{6,10},{7,11},{8,4},{9,5},... | collective-permute-start | bytes 294920 | tf_op jit(solution)/shard_map/ppermute | solution.py:300
  10.1 0.1 collective-permute-start.1
  10.2 2.1 %shard_map.102 = bf16[8,384,128]{2,1,0:T(8,128)(2,1)} custom-call(bf16[128,1024]{1,0:T(8,128)(2,1)} %q_ref.1, bf16[128,1024]{1,0:T(8,128)(2,1)} %k_ref.1, bf16[128,1024]{1,0:T(8,128)(2,1)} %v_ref.1), custom_call_target="tpu_custom_call" | custom-call | bytes 1572864 | tf_op jit(solution)/shard_map/pallas_call | solution.py:147
  12.4 0.0 collective-permute-done
  12.4 4.4 %all-to-all-start = ((bf16[8,384,128]{2,1,0:T(8,128)(2,1)}), bf16[8,384,128]{2,1,0:T(8,128)(2,1)S(1)}, u32[]{:S(2)}, u32[]{:S(2)}) async-start(bf16[8,384,128]{2,1,0:T(8,128)(2,1)} %shard_map.102), calls=%async_computation | async-start | bytes 1572864 | tf_op jit(solution)/shard_map/all_to_all | solution.py:358
  16.8 0.0 collective-permute-done.2
  16.8 2.1 %collective-permute-done.1 = bf16[64,768]{1,0:T(8,128)(2,1)S(1)} collective-permute-done((bf16[64,768]{1,0:T(8,128)(2,1)S(1)}, bf16[64,768]{1,0:T(8,128)(2,1)S(1)}, u32[]{:S(2)}, u32[]{:S(2)}) %collective-permute-start.1) | collective-permute-done | bytes 98336 | tf_op jit(solution)/shard_map/ppermute | solution.py:300
  18.9 0.0 collective-permute-done.3.refs_5_
  18.9 0.0 copy-start.1
  19.0 0.5 collective-permute-start.4
  19.4 0.0 collective-permute-start.5
  19.4 16.2 %collective-permute-done.4.refs_1_ = bf16[256,768]{1,0:T(8,128)(2,1)S(1)} collective-permute-done((bf16[256,768]{1,0:T(8,128)(2,1)S(1)}, bf16[256,768]{1,0:T(8,128)(2,1)S(1)}, u32[]{:S(2)}, u32[]{:S(2)}) %collective-permute-start.4) | collective-permute-done | bytes 393248 | tf_op jit(solution)/shard_map/ppermute | solution.py:300
  35.7 0.0 collective-permute-start.6
  35.7 0.0 collective-permute-done.5.refs_2_
  35.7 1.7 %collective-permute-done.6.refs_3_ = bf16[256,768]{1,0:T(8,128)(2,1)S(1)} collective-permute-done((bf16[256,768]{1,0:T(8,128)(2,1)S(1)}, bf16[256,768]{1,0:T(8,128)(2,1)S(1)}, u32[]{:S(2)}, u32[]{:S(2)}) %collective-permute-start.6) | collective-permute-done | bytes 393248 | tf_op jit(solution)/shard_map/ppermute | solution.py:300
  37.4 0.0 copy-done
  37.4 1.7 %shard_map.105 = (f32[1024,128]{1,0:T(8,128)S(1)}, f32[1024,128]{1,0:T(8,128)S(1)}, bf16[1024,128]{1,0:T(8,128)(2,1)S(1)}, bf16[1024,128]{1,0:T(8,128)(2,1)S(1)}, bf16[1024,768]{1,0:T(8,128)(2,1)S(1)}) custom-call(bf16[256,768]{1,0:T(8,128)(2,1)S(1)} %constant_dynamic-update-slice_fusion.refs_0_, bf16[256,768]{1,0:T(8,128)(2,1)S(1)} %collective-permute-done.4.refs_1_, ...), custom_call_target="tpu_custom_call" | custom-call | flops 805306368 | bytes 1572864 | tf_op jit(solution)/shard_map/pallas_call | solution.py:147
  39.0 0.0 copy-start.2
  39.1 1.1 %copy-done.2 = bf16[1024,768]{1,0:T(8,128)(2,1)} copy-done((bf16[1024,768]{1,0:T(8,128)(2,1)}, bf16[1024,768]{1,0:T(8,128)(2,1)S(1)}, u32[]{:S(2)}) %copy-start.2) | copy-done | bytes 1572888
  40.2 0.0 all-to-all-done.tok_ref
  40.2 0.0 copy-done.1
  40.2 4.9 %shard_map.104 = (bf16[1536,1024]{1,0:T(8,128)(2,1)S(1)}, bf16[128,1024]{1,0:T(8,128)(2,1)S(1)}, bf16[1024,128]{1,0:T(8,128)(2,1)S(1)}, bf16[128,1536]{1,0:T(8,128)(2,1)S(1)}, bf16[1536,128]{1,0:T(8,128)(2,1)S(1)}) custom-call(bf16[8,384,128]{2,1,0:T(8,128)(2,1)S(1)} %all-to-all-done.tok_ref, bf16[2,512,128]{2,1,0:T(8,128)(2,1)S(1)} %copy-done.1), custom_call_target="tpu_custom_call" | custom-call | flops 805306368 | bytes 6291456 | tf_op jit(solution)/shard_map/pallas_call | solution.py:147
  45.1 0.7 collective-permute-start.8
  45.8 3.6 %collective-permute-start.9 = (bf16[128,1024]{1,0:T(8,128)(2,1)S(1)}, bf16[128,1024]{1,0:T(8,128)(2,1)S(1)}, u32[]{:S(2)}, u32[]{:S(2)}) collective-permute-start(bf16[128,1024]{1,0:T(8,128)(2,1)S(1)} %get-tuple-element.44.refs_0_.out_ref), channel_id=1, source_target_pairs={{0,8},{1,9},{2,10},{3,11},{4,12},{5,13},{6,14},{7,15},{8,0},{9,1},... | collective-permute-start | bytes 786440 | tf_op jit(solution)/shard_map/ppermute | solution.py:300
  49.4 0.1 collective-permute-start.7
  49.4 10.3 %collective-permute-done.8 = bf16[1024,128]{1,0:T(8,128)(2,1)S(1)} collective-permute-done((bf16[1024,128]{1,0:T(8,128)(2,1)S(1)}, bf16[1024,128]{1,0:T(8,128)(2,1)S(1)}, u32[]{:S(2)}, u32[]{:S(2)}) %collective-permute-start.8) | collective-permute-done | bytes 262176 | tf_op jit(solution)/shard_map/ppermute | solution.py:300
  59.7 0.1 add_convert_fusion
  59.8 1.4 %collective-permute-done.9.refs_2_ = bf16[128,1024]{1,0:T(8,128)(2,1)S(1)} collective-permute-done((bf16[128,1024]{1,0:T(8,128)(2,1)S(1)}, bf16[128,1024]{1,0:T(8,128)(2,1)S(1)}, u32[]{:S(2)}, u32[]{:S(2)}) %collective-permute-start.9) | collective-permute-done | bytes 262176 | tf_op jit(solution)/shard_map/ppermute | solution.py:300
  61.1 1.0 collective-permute-start.10
  62.1 1.1 collective-permute-start.11
  63.2 1.3 %collective-permute-start.12 = (bf16[1024,128]{1,0:T(8,128)(2,1)S(1)}, bf16[1024,128]{1,0:T(8,128)(2,1)S(1)}, u32[]{:S(2)}, u32[]{:S(2)}) collective-permute-start(bf16[1024,128]{1,0:T(8,128)(2,1)S(1)} %add_convert_fusion), channel_id=1, source_target_pairs={{0,8},{1,9},{2,10},{3,11},{4,12},{5,13},{6,14},{7,15},{8,0},{9,1},... | collective-permute-start | bytes 786440 | tf_op jit(solution)/shard_map/ppermute | solution.py:300
  64.5 6.7 %collective-permute-done.7.refs_1_ = bf16[128,1024]{1,0:T(8,128)(2,1)S(1)} collective-permute-done((bf16[128,1024]{1,0:T(8,128)(2,1)S(1)}, bf16[128,1024]{1,0:T(8,128)(2,1)S(1)}, u32[]{:S(2)}, u32[]{:S(2)}) %collective-permute-start.7) | collective-permute-done | bytes 262176 | tf_op jit(solution)/shard_map/ppermute | solution.py:300
  71.2 5.6 %collective-permute-done.10.refs_3_ = bf16[128,1024]{1,0:T(8,128)(2,1)S(1)} collective-permute-done((bf16[128,1024]{1,0:T(8,128)(2,1)S(1)}, bf16[128,1024]{1,0:T(8,128)(2,1)S(1)}, u32[]{:S(2)}, u32[]{:S(2)}) %collective-permute-start.10) | collective-permute-done | bytes 262176 | tf_op jit(solution)/shard_map/ppermute | solution.py:300
  76.8 1.3 %shard_map.106 = (bf16[512,384]{1,0:T(8,128)(2,1)S(1)}, bf16[512,384]{1,0:T(8,128)(2,1)S(1)}) custom-call(bf16[1024,768]{1,0:T(8,128)(2,1)S(1)} %copy-done.3, bf16[128,1024]{1,0:T(8,128)(2,1)S(1)} %get-tuple-element.44.refs_0_.out_ref, bf16[128,1024]{1,0:T(8,128)(2,1)S(1)} %collective-permute-done.7.refs_1_, ...), custom_call_target="tpu_custom_call" | custom-call | flops 805306368 | bytes 1572864 | tf_op jit(solution)/shard_map/pallas_call | solution.py:147
  78.1 3.5 %collective-permute-done.11.near_ref = bf16[1024,128]{1,0:T(8,128)(2,1)S(1)} collective-permute-done((bf16[1024,128]{1,0:T(8,128)(2,1)S(1)}, bf16[1024,128]{1,0:T(8,128)(2,1)S(1)}, u32[]{:S(2)}, u32[]{:S(2)}) %collective-permute-start.11) | collective-permute-done | bytes 262176 | tf_op jit(solution)/shard_map/ppermute | solution.py:300
  81.6 0.0 collective-permute-done.12.far_ref
  81.6 4.5 %shard_map.107 = bf16[8,384,128]{2,1,0:T(8,128)(2,1)} custom-call(bf16[1024,128]{1,0:T(8,128)(2,1)S(1)} %get-tuple-element.40.queries_ref, bf16[128,1536]{1,0:T(8,128)(2,1)S(1)} %get-tuple-element.41.keys_t_ref, bf16[1536,128]{1,0:T(8,128)(2,1)S(1)} %get-tuple-element.42.vals_ref, bf16[1536,1024]{1,0:T(8,128)(2,1)S(1)} %get-tuple-element.43.probs_ref, ...), custom_call_target="tpu_custom_call" | custom-call | flops 1610612736 | bytes 6291456 | tf_op jit(solution)/shard_map/pallas_call | solution.py:147
  86.1 4.9 %all-to-all-start.1 = ((bf16[8,384,128]{2,1,0:T(8,128)(2,1)}), bf16[8,384,128]{2,1,0:T(8,128)(2,1)S(1)}, u32[]{:S(2)}, u32[]{:S(2)}) async-start(bf16[8,384,128]{2,1,0:T(8,128)(2,1)} %shard_map.107), calls=%async_computation.1 | async-start | bytes 1572864 | tf_op jit(solution)/shard_map/all_to_all | solution.py:402
  91.0 2.0 %collective-permute-start.13 = (bf16[512,384]{1,0:T(8,128)(2,1)S(1)}, bf16[512,384]{1,0:T(8,128)(2,1)S(1)}, u32[]{:S(2)}, u32[]{:S(2)}) collective-permute-start(bf16[512,384]{1,0:T(8,128)(2,1)S(1)} %get-tuple-element.67), channel_id=1, source_target_pairs={{0,2},{1,3},{2,0},{3,1},{4,6},{5,7},{6,4},{7,5},{8,10},{9,11},{10,... | collective-permute-start | bytes 1179656 | tf_op jit(solution)/shard_map/ppermute | solution.py:300
  93.0 16.7 %collective-permute-done.13.other_ref = bf16[512,384]{1,0:T(8,128)(2,1)S(1)} collective-permute-done((bf16[512,384]{1,0:T(8,128)(2,1)S(1)}, bf16[512,384]{1,0:T(8,128)(2,1)S(1)}, u32[]{:S(2)}, u32[]{:S(2)}) %collective-permute-start.13) | collective-permute-done | bytes 393248 | tf_op jit(solution)/shard_map/ppermute | solution.py:300
  109.7 1.5 %shard_map.109 = f32[384,1024]{1,0:T(8,128)} custom-call(bf16[512,384]{1,0:T(8,128)(2,1)S(1)} %get-tuple-element.59.own_ref, bf16[512,384]{1,0:T(8,128)(2,1)S(1)} %collective-permute-done.13.other_ref), custom_call_target="tpu_custom_call" | custom-call | bytes 2359296 | tf_op jit(solution)/shard_map/pallas_call | solution.py:147
  111.1 0.0 all-to-all-done.1.tok_ref
  111.1 1.1 shard_map.108
  (8 shorter events, 0.1 us)
Async XLA Ops:
  0.6 5.3 %copy-start.4 = (bf16[128,3072]{1,0:T(8,128)(2,1)S(1)}, bf16[128,3072]{1,0:T(8,128)(2,1)}, u32[]{:S(2)}) copy-start(bf16[128,3072]{1,0:T(8,128)(2,1)} %param.13) | copy-start | bytes 2359300
  3.0 15.9 %collective-permute-start.3 = (bf16[384,512]{1,0:T(8,128)(2,1)}, bf16[384,512]{1,0:T(8,128)(2,1)S(1)}, u32[]{:S(2)}, u32[]{:S(2)}) collective-permute-start(bf16[384,512]{1,0:T(8,128)(2,1)} %get-tuple-element.46), channel_id=1, source_target_pairs={{0,2},{1,3},{2,0},{3,1},{4,6},{5,7},{6,4},{7,5},{8,10},{9,11},{10,... | collective-permute-start | bytes 1179656 | tf_op jit(solution)/shard_map/ppermute | solution.py:300
  6.0 6.4 %collective-permute-start = (bf16[64,768]{1,0:T(8,128)(2,1)S(1)}, bf16[64,768]{1,0:T(8,128)(2,1)S(1)}, u32[]{:S(2)}, u32[]{:S(2)}) collective-permute-start(bf16[64,768]{1,0:T(8,128)(2,1)S(1)} %get-tuple-element.71), channel_id=1, source_target_pairs={{0,4},{1,5},{2,6},{3,7},{4,0},{5,1},{6,2},{7,3},{8,12},{9,13},{10,... | collective-permute-start | bytes 294920 | tf_op jit(solution)/shard_map/ppermute | solution.py:300
  7.6 9.1 %collective-permute-start.2 = (bf16[64,768]{1,0:T(8,128)(2,1)S(1)}, bf16[64,768]{1,0:T(8,128)(2,1)S(1)}, u32[]{:S(2)}, u32[]{:S(2)}) collective-permute-start(bf16[64,768]{1,0:T(8,128)(2,1)S(1)} %get-tuple-element.68), channel_id=1, source_target_pairs={{0,12},{1,13},{2,14},{3,15},{4,8},{5,9},{6,10},{7,11},{8,4},{9,5},... | collective-permute-start | bytes 294920 | tf_op jit(solution)/shard_map/ppermute | solution.py:300
  10.1 8.8 %collective-permute-start.1 = (bf16[64,768]{1,0:T(8,128)(2,1)S(1)}, bf16[64,768]{1,0:T(8,128)(2,1)S(1)}, u32[]{:S(2)}, u32[]{:S(2)}) collective-permute-start(bf16[64,768]{1,0:T(8,128)(2,1)S(1)} %get-tuple-element.69), channel_id=1, source_target_pairs={{0,8},{1,9},{2,10},{3,11},{4,12},{5,13},{6,14},{7,15},{8,0},{9,1},... | collective-permute-start | bytes 294920 | tf_op jit(solution)/shard_map/ppermute | solution.py:300
  12.4 25.0 %copy-start = (bf16[384,512]{1,0:T(8,128)(2,1)S(1)}, bf16[384,512]{1,0:T(8,128)(2,1)}, u32[]{:S(2)}) copy-start(bf16[384,512]{1,0:T(8,128)(2,1)} %get-tuple-element.51.refs_4_) | copy-start | bytes 1179652
  12.4 27.8 %all-to-all-start = ((bf16[8,384,128]{2,1,0:T(8,128)(2,1)}), bf16[8,384,128]{2,1,0:T(8,128)(2,1)S(1)}, u32[]{:S(2)}, u32[]{:S(2)}) async-start(bf16[8,384,128]{2,1,0:T(8,128)(2,1)} %shard_map.102), calls=%async_computation | async-start | bytes 1572864 | tf_op jit(solution)/shard_map/all_to_all | solution.py:358
  18.9 21.3 %copy-start.1 = (bf16[2,512,128]{2,1,0:T(8,128)(2,1)S(1)}, bf16[2,512,128]{2,1,0:T(8,128)(2,1)}, u32[]{:S(2)}) copy-start(bf16[2,512,128]{2,1,0:T(8,128)(2,1)} %get-tuple-element.39.text_ref) | copy-start | bytes 786436
  19.0 16.7 %collective-permute-start.4 = (bf16[256,768]{1,0:T(8,128)(2,1)S(1)}, bf16[256,768]{1,0:T(8,128)(2,1)S(1)}, u32[]{:S(2)}, u32[]{:S(2)}) collective-permute-start(bf16[256,768]{1,0:T(8,128)(2,1)S(1)} %constant_dynamic-update-slice_fusion.refs_0_), channel_id=1, source_target_pairs={{0,2},{1,3},{2,0},{3,1},{4,6},{5,7},{6,4},{7,5},{8,10},{9,11},{10,... | collective-permute-start | bytes 1179656 | tf_op jit(solution)/shard_map/ppermute | solution.py:300
  19.4 16.2 %collective-permute-start.5 = (bf16[256,768]{1,0:T(8,128)(2,1)S(1)}, bf16[256,768]{1,0:T(8,128)(2,1)S(1)}, u32[]{:S(2)}, u32[]{:S(2)}) collective-permute-start(bf16[256,768]{1,0:T(8,128)(2,1)S(1)} %constant_dynamic-update-slice_fusion.refs_0_), channel_id=1, source_target_pairs={{0,1},{1,0},{2,3},{3,2},{4,5},{5,4},{6,7},{7,6},{8,9},{9,8},{10,11... | collective-permute-start | bytes 1179656 | tf_op jit(solution)/shard_map/ppermute | solution.py:300
  35.7 1.7 %collective-permute-start.6 = (bf16[256,768]{1,0:T(8,128)(2,1)S(1)}, bf16[256,768]{1,0:T(8,128)(2,1)S(1)}, u32[]{:S(2)}, u32[]{:S(2)}) collective-permute-start(bf16[256,768]{1,0:T(8,128)(2,1)S(1)} %collective-permute-done.4.refs_1_), channel_id=1, source_target_pairs={{0,1},{1,0},{2,3},{3,2},{4,5},{5,4},{6,7},{7,6},{8,9},{9,8},{10,11... | collective-permute-start | bytes 1179656 | tf_op jit(solution)/shard_map/ppermute | solution.py:300
  39.0 1.1 %copy-start.2 = (bf16[1024,768]{1,0:T(8,128)(2,1)}, bf16[1024,768]{1,0:T(8,128)(2,1)S(1)}, u32[]{:S(2)}) copy-start(bf16[1024,768]{1,0:T(8,128)(2,1)S(1)} %get-tuple-element.54.cot_ref) | copy-start | bytes 4718596
  40.2 36.6 %copy-start.3 = (bf16[1024,768]{1,0:T(8,128)(2,1)S(1)}, bf16[1024,768]{1,0:T(8,128)(2,1)}, u32[]{:S(2)}) copy-start(bf16[1024,768]{1,0:T(8,128)(2,1)} %copy-done.2) | copy-start | bytes 4718596
  45.1 14.6 %collective-permute-start.8 = (bf16[1024,128]{1,0:T(8,128)(2,1)S(1)}, bf16[1024,128]{1,0:T(8,128)(2,1)S(1)}, u32[]{:S(2)}, u32[]{:S(2)}) collective-permute-start(bf16[1024,128]{1,0:T(8,128)(2,1)S(1)} %get-tuple-element.57), channel_id=1, source_target_pairs={{0,4},{1,5},{2,6},{3,7},{4,0},{5,1},{6,2},{7,3},{8,12},{9,13},{10,... | collective-permute-start | bytes 786440 | tf_op jit(solution)/shard_map/ppermute | solution.py:300
  45.8 15.4 %collective-permute-start.9 = (bf16[128,1024]{1,0:T(8,128)(2,1)S(1)}, bf16[128,1024]{1,0:T(8,128)(2,1)S(1)}, u32[]{:S(2)}, u32[]{:S(2)}) collective-permute-start(bf16[128,1024]{1,0:T(8,128)(2,1)S(1)} %get-tuple-element.44.refs_0_.out_ref), channel_id=1, source_target_pairs={{0,8},{1,9},{2,10},{3,11},{4,12},{5,13},{6,14},{7,15},{8,0},{9,1},... | collective-permute-start | bytes 786440 | tf_op jit(solution)/shard_map/ppermute | solution.py:300
  49.4 21.8 %collective-permute-start.7 = (bf16[128,1024]{1,0:T(8,128)(2,1)S(1)}, bf16[128,1024]{1,0:T(8,128)(2,1)S(1)}, u32[]{:S(2)}, u32[]{:S(2)}) collective-permute-start(bf16[128,1024]{1,0:T(8,128)(2,1)S(1)} %get-tuple-element.44.refs_0_.out_ref), channel_id=1, source_target_pairs={{0,4},{1,5},{2,6},{3,7},{4,0},{5,1},{6,2},{7,3},{8,12},{9,13},{10,... | collective-permute-start | bytes 786440 | tf_op jit(solution)/shard_map/ppermute | solution.py:300
  61.1 15.6 %collective-permute-start.10 = (bf16[128,1024]{1,0:T(8,128)(2,1)S(1)}, bf16[128,1024]{1,0:T(8,128)(2,1)S(1)}, u32[]{:S(2)}, u32[]{:S(2)}) collective-permute-start(bf16[128,1024]{1,0:T(8,128)(2,1)S(1)} %collective-permute-done.9.refs_2_), channel_id=1, source_target_pairs={{0,4},{1,5},{2,6},{3,7},{4,0},{5,1},{6,2},{7,3},{8,12},{9,13},{10,... | collective-permute-start | bytes 786440 | tf_op jit(solution)/shard_map/ppermute | solution.py:300
  62.1 19.5 %collective-permute-start.11 = (bf16[1024,128]{1,0:T(8,128)(2,1)S(1)}, bf16[1024,128]{1,0:T(8,128)(2,1)S(1)}, u32[]{:S(2)}, u32[]{:S(2)}) collective-permute-start(bf16[1024,128]{1,0:T(8,128)(2,1)S(1)} %get-tuple-element.62), channel_id=1, source_target_pairs={{0,4},{1,5},{2,6},{3,7},{4,0},{5,1},{6,2},{7,3},{8,12},{9,13},{10,... | collective-permute-start | bytes 786440 | tf_op jit(solution)/shard_map/ppermute | solution.py:300
  63.2 18.4 %collective-permute-start.12 = (bf16[1024,128]{1,0:T(8,128)(2,1)S(1)}, bf16[1024,128]{1,0:T(8,128)(2,1)S(1)}, u32[]{:S(2)}, u32[]{:S(2)}) collective-permute-start(bf16[1024,128]{1,0:T(8,128)(2,1)S(1)} %add_convert_fusion), channel_id=1, source_target_pairs={{0,8},{1,9},{2,10},{3,11},{4,12},{5,13},{6,14},{7,15},{8,0},{9,1},... | collective-permute-start | bytes 786440 | tf_op jit(solution)/shard_map/ppermute | solution.py:300
  86.1 25.1 %all-to-all-start.1 = ((bf16[8,384,128]{2,1,0:T(8,128)(2,1)}), bf16[8,384,128]{2,1,0:T(8,128)(2,1)S(1)}, u32[]{:S(2)}, u32[]{:S(2)}) async-start(bf16[8,384,128]{2,1,0:T(8,128)(2,1)} %shard_map.107), calls=%async_computation.1 | async-start | bytes 1572864 | tf_op jit(solution)/shard_map/all_to_all | solution.py:402
  91.0 18.7 %collective-permute-start.13 = (bf16[512,384]{1,0:T(8,128)(2,1)S(1)}, bf16[512,384]{1,0:T(8,128)(2,1)S(1)}, u32[]{:S(2)}, u32[]{:S(2)}) collective-permute-start(bf16[512,384]{1,0:T(8,128)(2,1)S(1)} %get-tuple-element.67), channel_id=1, source_target_pairs={{0,2},{1,3},{2,0},{3,1},{4,6},{5,7},{6,4},{7,5},{8,10},{9,11},{10,... | collective-permute-start | bytes 1179656 | tf_op jit(solution)/shard_map/ppermute | solution.py:300

commit v13 on v11

--- a/solution.py
+++ b/solution.py
@@ -375,8 +375,7 @@
         moved=2 * image * columns,
     )
     near_far = exchange(near_far, 2)
-    far, out_t = lax.optimization_barrier(((far + near_far.astype(F32)).astype(BF16), out_t))
-    far = exchange(far, 4)
+    far = exchange((far + near_far.astype(F32)).astype(BF16), 4)
     near, _ = lax.optimization_barrier((near, near_far))
     near = exchange(near, 2)
     out_near = exchange(out_t, 2)
@@ -391,13 +390,14 @@
         moved=4 * total * image,
     )
     grad_in = lax.all_to_all(grad_out, "seq", split_axis=0, concat_axis=0, tiled=True)
+    out_far, _ = lax.optimization_barrier((out_far, grad_out))
     outs = [out_t, out_near, out_far, exchange(out_far, 2)]
     dw_own, dw_other = call(
         weight_grad_kernel,
         [shape((4 * HD, depth), BF16)] * 2,
         [cot, *outs],
         scratch=[pltpu.VMEM((4 * HD, image), BF16)],
-        flops=256 * image * columns * HD,
+        flops=96 * image * columns * HD,
         moved=2 * image * columns,
     )
     grads = call(

time: 113 us -> 109 us (0.965)
  starting transfers between devices: 27.1 us -> 22.5 us
    ppermute x14, starting transfers between devices: 18.2 us -> 14.5 us  [exchange(): return lax.ppermute(array, ('seq', 'fsdp'), pairs)]
  transfers between devices with their start and end apart: 16 -> 16, of which waited for: 9 -> 10; matrix products, arithmetic and copies ran while one was open for 0% -> 0% of each run, Pallas kernels for 10% -> 15%
where the time goes in v13:
time: 109 us
  waiting for transfers between devices  63.4 us (58%)
  starting transfers between devices  22.5 us (21%)
  Pallas kernels  19.3 us (18%)
  local copies, waits for them, and re-layouts  2.63 us (2%)
    ppermute x14, waiting for transfers between devices, exchange(): return lax.ppermute(array, ('seq', 'fsdp'), pairs)  63.4 us
    pallas_call x8, Pallas kernels, call(): pl.pallas_call(kernel, out_shape=outs, grid_spec=pltpu.PrefetchScalarGrid...  19.3 us
    ppermute x14, starting transfers between devices, exchange(): return lax.ppermute(array, ('seq', 'fsdp'), pairs)  14.5 us
    all_to_all x1, starting transfers between devices, local(): lax.all_to_all(tok_out, 'seq', split_axis=0, concat_axis=0, tiled=True)  4.37 us
    all_to_all x1, starting transfers between devices, local(): lax.all_to_all(grad_out, 'seq', split_axis=0, concat_axis=0, tiled=True)  3.55 us
    unnamed x13, local copies, waits for them, and re-layouts  2.58 us
  transfers between devices with their start and end apart: 16, of which 10 were waited for; matrix products, arithmetic and copies ran while one was open for 0% of the time, Pallas kernels for 15%

profile of v13, /device:TPU:0, one launch (start us, length us, event | category | flops | bytes accessed | tf_op | source)
XLA Modules:
  0.0 108.6 jit_solution(15683329899927912540)
XLA Ops:
  0.6 0.0 copy-start.4
  0.6 2.3 %shard_map.103 = (bf16[384,512]{1,0:T(8,128)(2,1)}, bf16[384,512]{1,0:T(8,128)(2,1)}, bf16[2,512,128]{2,1,0:T(8,128)(2,1)}) custom-call(s32[1]{0:T(128)} %bitcast.me_ref, bf16[384,1024]{1,0:T(8,128)(2,1)} %w_ref.1, bf16[512,1024]{1,0:T(8,128)(2,1)} %kt_ref.1, bf16[512,1024]{1,0:T(8,128)(2,1)} %vt_ref.1), custom_call_target="tpu_custom_call" | custom-call | bytes 1572864 | tf_op jit(solution)/shard_map/pallas_call | solution.py:147
  3.0 3.0 %collective-permute-start.3 = (bf16[384,512]{1,0:T(8,128)(2,1)}, bf16[384,512]{1,0:T(8,128)(2,1)S(1)}, u32[]{:S(2)}, u32[]{:S(2)}) collective-permute-start(bf16[384,512]{1,0:T(8,128)(2,1)} %get-tuple-element.46), channel_id=1, source_target_pairs={{0,2},{1,3},{2,0},{3,1},{4,6},{5,7},{6,4},{7,5},{8,10},{9,11},{10,... | collective-permute-start | bytes 1179656 | tf_op jit(solution)/shard_map/ppermute | solution.py:300
  6.0 0.0 copy-done.4
  6.0 1.6 %collective-permute-start = (bf16[64,768]{1,0:T(8,128)(2,1)S(1)}, bf16[64,768]{1,0:T(8,128)(2,1)S(1)}, u32[]{:S(2)}, u32[]{:S(2)}) collective-permute-start(bf16[64,768]{1,0:T(8,128)(2,1)S(1)} %get-tuple-element.71), channel_id=1, source_target_pairs={{0,4},{1,5},{2,6},{3,7},{4,0},{5,1},{6,2},{7,3},{8,12},{9,13},{10,... | collective-permute-start | bytes 294920 | tf_op jit(solution)/shard_map/ppermute | solution.py:300
  7.6 2.5 %collective-permute-start.2 = (bf16[64,768]{1,0:T(8,128)(2,1)S(1)}, bf16[64,768]{1,0:T(8,128)(2,1)S(1)}, u32[]{:S(2)}, u32[]{:S(2)}) collective-permute-start(bf16[64,768]{1,0:T(8,128)(2,1)S(1)} %get-tuple-element.68), channel_id=1, source_target_pairs={{0,12},{1,13},{2,14},{3,15},{4,8},{5,9},{6,10},{7,11},{8,4},{9,5},... | collective-permute-start | bytes 294920 | tf_op jit(solution)/shard_map/ppermute | solution.py:300
  10.1 0.1 collective-permute-start.1
  10.2 2.1 %shard_map.102 = bf16[8,384,128]{2,1,0:T(8,128)(2,1)} custom-call(bf16[128,1024]{1,0:T(8,128)(2,1)} %q_ref.1, bf16[128,1024]{1,0:T(8,128)(2,1)} %k_ref.1, bf16[128,1024]{1,0:T(8,128)(2,1)} %v_ref.1), custom_call_target="tpu_custom_call" | custom-call | bytes 1572864 | tf_op jit(solution)/shard_map/pallas_call | solution.py:147
  12.4 0.0 collective-permute-done
  12.4 4.4 %all-to-all-start = ((bf16[8,384,128]{2,1,0:T(8,128)(2,1)}), bf16[8,384,128]{2,1,0:T(8,128)(2,1)S(1)}, u32[]{:S(2)}, u32[]{:S(2)}) async-start(bf16[8,384,128]{2,1,0:T(8,128)(2,1)} %shard_map.102), calls=%async_computation | async-start | bytes 1572864 | tf_op jit(solution)/shard_map/all_to_all | solution.py:358
  16.8 0.0 collective-permute-done.2
  16.8 2.1 %collective-permute-done.1 = bf16[64,768]{1,0:T(8,128)(2,1)S(1)} collective-permute-done((bf16[64,768]{1,0:T(8,128)(2,1)S(1)}, bf16[64,768]{1,0:T(8,128)(2,1)S(1)}, u32[]{:S(2)}, u32[]{:S(2)}) %collective-permute-start.1) | collective-permute-done | bytes 98336 | tf_op jit(solution)/shard_map/ppermute | solution.py:300
  18.9 0.0 collective-permute-done.3.refs_5_
  18.9 0.5 collective-permute-start.4
  19.4 0.0 collective-permute-start.5
  19.4 16.2 %collective-permute-done.4.refs_1_ = bf16[256,768]{1,0:T(8,128)(2,1)S(1)} collective-permute-done((bf16[256,768]{1,0:T(8,128)(2,1)S(1)}, bf16[256,768]{1,0:T(8,128)(2,1)S(1)}, u32[]{:S(2)}, u32[]{:S(2)}) %collective-permute-start.4) | collective-permute-done | bytes 393248 | tf_op jit(solution)/shard_map/ppermute | solution.py:300
  35.7 0.0 collective-permute-start.6
  35.7 0.0 collective-permute-done.5.refs_2_
  35.7 1.7 %collective-permute-done.6.refs_3_ = bf16[256,768]{1,0:T(8,128)(2,1)S(1)} collective-permute-done((bf16[256,768]{1,0:T(8,128)(2,1)S(1)}, bf16[256,768]{1,0:T(8,128)(2,1)S(1)}, u32[]{:S(2)}, u32[]{:S(2)}) %collective-permute-start.6) | collective-permute-done | bytes 393248 | tf_op jit(solution)/shard_map/ppermute | solution.py:300
  37.4 0.0 copy-done
  37.4 1.7 %shard_map.105 = (f32[1024,128]{1,0:T(8,128)S(1)}, f32[1024,128]{1,0:T(8,128)S(1)}, bf16[1024,128]{1,0:T(8,128)(2,1)S(1)}, bf16[1024,128]{1,0:T(8,128)(2,1)S(1)}, bf16[1024,768]{1,0:T(8,128)(2,1)S(1)}) custom-call(bf16[256,768]{1,0:T(8,128)(2,1)S(1)} %constant_dynamic-update-slice_fusion.refs_0_, bf16[256,768]{1,0:T(8,128)(2,1)S(1)} %collective-permute-done.4.refs_1_, ...), custom_call_target="tpu_custom_call" | custom-call | flops 805306368 | bytes 1572864 | tf_op jit(solution)/shard_map/pallas_call | solution.py:147
  39.0 0.0 copy-start.2
  39.1 1.1 %copy-done.2 = bf16[1024,768]{1,0:T(8,128)(2,1)} copy-done((bf16[1024,768]{1,0:T(8,128)(2,1)}, bf16[1024,768]{1,0:T(8,128)(2,1)S(1)}, u32[]{:S(2)}) %copy-start.2) | copy-done | bytes 1572888
  40.2 0.6 collective-permute-start.7
  40.8 7.7 %collective-permute-done.7 = bf16[1024,128]{1,0:T(8,128)(2,1)S(1)} collective-permute-done((bf16[1024,128]{1,0:T(8,128)(2,1)S(1)}, bf16[1024,128]{1,0:T(8,128)(2,1)S(1)}, u32[]{:S(2)}, u32[]{:S(2)}) %collective-permute-start.7) | collective-permute-done | bytes 262176 | tf_op jit(solution)/shard_map/ppermute | solution.py:300
  48.5 0.1 add_convert_fusion
  48.6 2.5 %collective-permute-start.9 = (bf16[1024,128]{1,0:T(8,128)(2,1)S(1)}, bf16[1024,128]{1,0:T(8,128)(2,1)S(1)}, u32[]{:S(2)}, u32[]{:S(2)}) collective-permute-start(bf16[1024,128]{1,0:T(8,128)(2,1)S(1)} %add_convert_fusion), channel_id=1, source_target_pairs={{0,8},{1,9},{2,10},{3,11},{4,12},{5,13},{6,14},{7,15},{8,0},{9,1},... | collective-permute-start | bytes 786440 | tf_op jit(solution)/shard_map/ppermute | solution.py:300
  51.1 0.0 all-to-all-done.tok_ref
  51.1 0.0 copy-done.1
  51.1 4.9 %shard_map.104 = (bf16[1536,1024]{1,0:T(8,128)(2,1)S(1)}, bf16[128,1024]{1,0:T(8,128)(2,1)S(1)}, bf16[1024,128]{1,0:T(8,128)(2,1)S(1)}, bf16[128,1536]{1,0:T(8,128)(2,1)S(1)}, bf16[1536,128]{1,0:T(8,128)(2,1)S(1)}) custom-call(bf16[8,384,128]{2,1,0:T(8,128)(2,1)S(1)} %all-to-all-done.tok_ref, bf16[2,512,128]{2,1,0:T(8,128)(2,1)S(1)} %copy-done.1), custom_call_target="tpu_custom_call" | custom-call | flops 805306368 | bytes 6291456 | tf_op jit(solution)/shard_map/pallas_call | solution.py:147
  56.0 1.8 %collective-permute-start.10 = (bf16[128,1024]{1,0:T(8,128)(2,1)S(1)}, bf16[128,1024]{1,0:T(8,128)(2,1)S(1)}, u32[]{:S(2)}, u32[]{:S(2)}) collective-permute-start(bf16[128,1024]{1,0:T(8,128)(2,1)S(1)} %get-tuple-element.64.out_ref.refs_0_), channel_id=1, source_target_pairs={{0,4},{1,5},{2,6},{3,7},{4,0},{5,1},{6,2},{7,3},{8,12},{9,13},{10,... | collective-permute-start | bytes 786440 | tf_op jit(solution)/shard_map/ppermute | solution.py:300
  57.8 0.3 collective-permute-start.8
  58.1 4.8 %collective-permute-done.9.far_ref = bf16[1024,128]{1,0:T(8,128)(2,1)S(1)} collective-permute-done((bf16[1024,128]{1,0:T(8,128)(2,1)S(1)}, bf16[1024,128]{1,0:T(8,128)(2,1)S(1)}, u32[]{:S(2)}, u32[]{:S(2)}) %collective-permute-start.9) | collective-permute-done | bytes 262176 | tf_op jit(solution)/shard_map/ppermute | solution.py:300
  62.9 5.6 %collective-permute-done.10.refs_1_ = bf16[128,1024]{1,0:T(8,128)(2,1)S(1)} collective-permute-done((bf16[128,1024]{1,0:T(8,128)(2,1)S(1)}, bf16[128,1024]{1,0:T(8,128)(2,1)S(1)}, u32[]{:S(2)}, u32[]{:S(2)}) %collective-permute-start.10) | collective-permute-done | bytes 262176 | tf_op jit(solution)/shard_map/ppermute | solution.py:300
  68.5 1.6 %collective-permute-start.11 = (bf16[128,1024]{1,0:T(8,128)(2,1)S(1)}, bf16[128,1024]{1,0:T(8,128)(2,1)S(1)}, u32[]{:S(2)}, u32[]{:S(2)}) collective-permute-start(bf16[128,1024]{1,0:T(8,128)(2,1)S(1)} %get-tuple-element.64.out_ref.refs_0_), channel_id=1, source_target_pairs={{0,8},{1,9},{2,10},{3,11},{4,12},{5,13},{6,14},{7,15},{8,0},{9,1},... | collective-permute-start | bytes 786440 | tf_op jit(solution)/shard_map/ppermute | solution.py:300
  70.1 4.0 %collective-permute-done.8.near_ref = bf16[1024,128]{1,0:T(8,128)(2,1)S(1)} collective-permute-done((bf16[1024,128]{1,0:T(8,128)(2,1)S(1)}, bf16[1024,128]{1,0:T(8,128)(2,1)S(1)}, u32[]{:S(2)}, u32[]{:S(2)}) %collective-permute-start.8) | collective-permute-done | bytes 262176 | tf_op jit(solution)/shard_map/ppermute | solution.py:300
  74.1 4.5 %shard_map.106 = bf16[8,384,128]{2,1,0:T(8,128)(2,1)} custom-call(bf16[1024,128]{1,0:T(8,128)(2,1)S(1)} %get-tuple-element.40.queries_ref, bf16[128,1536]{1,0:T(8,128)(2,1)S(1)} %get-tuple-element.41.keys_t_ref, bf16[1536,128]{1,0:T(8,128)(2,1)S(1)} %get-tuple-element.42.vals_ref, bf16[1536,1024]{1,0:T(8,128)(2,1)S(1)} %get-tuple-element.43.probs_ref, ...), custom_call_target="tpu_custom_call" | custom-call | flops 1610612736 | bytes 6291456 | tf_op jit(solution)/shard_map/pallas_call | solution.py:147
  78.5 3.3 %collective-permute-done.11.refs_2_ = bf16[128,1024]{1,0:T(8,128)(2,1)S(1)} collective-permute-done((bf16[128,1024]{1,0:T(8,128)(2,1)S(1)}, bf16[128,1024]{1,0:T(8,128)(2,1)S(1)}, u32[]{:S(2)}, u32[]{:S(2)}) %collective-permute-start.11) | collective-permute-done | bytes 262176 | tf_op jit(solution)/shard_map/ppermute | solution.py:300
  81.8 0.0 collective-permute-start.12
  81.8 3.5 %all-to-all-start.1 = ((bf16[8,384,128]{2,1,0:T(8,128)(2,1)}), bf16[8,384,128]{2,1,0:T(8,128)(2,1)S(1)}, u32[]{:S(2)}, u32[]{:S(2)}) async-start(bf16[8,384,128]{2,1,0:T(8,128)(2,1)} %shard_map.106), calls=%async_computation.1 | async-start | bytes 1572864 | tf_op jit(solution)/shard_map/all_to_all | solution.py:392
  85.4 5.6 %collective-permute-done.12.refs_3_ = bf16[128,1024]{1,0:T(8,128)(2,1)S(1)} collective-permute-done((bf16[128,1024]{1,0:T(8,128)(2,1)S(1)}, bf16[128,1024]{1,0:T(8,128)(2,1)S(1)}, u32[]{:S(2)}, u32[]{:S(2)}) %collective-permute-start.12) | collective-permute-done | bytes 262176 | tf_op jit(solution)/shard_map/ppermute | solution.py:300
  91.0 1.4 %copy-done.3 = bf16[1024,768]{1,0:T(8,128)(2,1)S(1)} copy-done((bf16[1024,768]{1,0:T(8,128)(2,1)S(1)}, bf16[1024,768]{1,0:T(8,128)(2,1)}, u32[]{:S(2)}) %copy-start.3) | copy-done | bytes 1572888
  92.4 1.3 %shard_map.108 = (bf16[512,384]{1,0:T(8,128)(2,1)S(1)}, bf16[512,384]{1,0:T(8,128)(2,1)S(1)}) custom-call(bf16[1024,768]{1,0:T(8,128)(2,1)S(1)} %copy-done.3, bf16[128,1024]{1,0:T(8,128)(2,1)S(1)} %get-tuple-element.64.out_ref.refs_0_, bf16[128,1024]{1,0:T(8,128)(2,1)S(1)} %collective-permute-done.10.refs_1_, ...), custom_call_target="tpu_custom_call" | custom-call | flops 9663676416 | bytes 1572864 | tf_op jit(solution)/shard_map/pallas_call | solution.py:147
  93.6 0.1 collective-permute-start.13
  93.7 12.3 %collective-permute-done.13.other_ref = bf16[512,384]{1,0:T(8,128)(2,1)S(1)} collective-permute-done((bf16[512,384]{1,0:T(8,128)(2,1)S(1)}, bf16[512,384]{1,0:T(8,128)(2,1)S(1)}, u32[]{:S(2)}, u32[]{:S(2)}) %collective-permute-start.13) | collective-permute-done | bytes 393248 | tf_op jit(solution)/shard_map/ppermute | solution.py:300
  106.0 1.5 %shard_map.109 = f32[384,1024]{1,0:T(8,128)} custom-call(bf16[512,384]{1,0:T(8,128)(2,1)S(1)} %get-tuple-element.66.own_ref, bf16[512,384]{1,0:T(8,128)(2,1)S(1)} %collective-permute-done.13.other_ref), custom_call_target="tpu_custom_call" | custom-call | bytes 2359296 | tf_op jit(solution)/shard_map/pallas_call | solution.py:147
  107.5 0.0 all-to-all-done.1.tok_ref
  107.5 1.1 %shard_map.107 = (bf16[128,1024]{1,0:T(8,128)(2,1)}, bf16[128,1024]{1,0:T(8,128)(2,1)}, bf16[128,1024]{1,0:T(8,128)(2,1)}) custom-call(bf16[8,384,128]{2,1,0:T(8,128)(2,1)S(1)} %all-to-all-done.1.tok_ref), custom_call_target="tpu_custom_call" | custom-call | bytes 1572864 | tf_op jit(solution)/shard_map/pallas_call | solution.py:147
  (8 shorter events, 0.1 us)
Async XLA Ops:
  0.6 5.3 %copy-start.4 = (bf16[128,3072]{1,0:T(8,128)(2,1)S(1)}, bf16[128,3072]{1,0:T(8,128)(2,1)}, u32[]{:S(2)}) copy-start(bf16[128,3072]{1,0:T(8,128)(2,1)} %param.13) | copy-start | bytes 2359300
  3.0 15.9 %collective-permute-start.3 = (bf16[384,512]{1,0:T(8,128)(2,1)}, bf16[384,512]{1,0:T(8,128)(2,1)S(1)}, u32[]{:S(2)}, u32[]{:S(2)}) collective-permute-start(bf16[384,512]{1,0:T(8,128)(2,1)} %get-tuple-element.46), channel_id=1, source_target_pairs={{0,2},{1,3},{2,0},{3,1},{4,6},{5,7},{6,4},{7,5},{8,10},{9,11},{10,... | collective-permute-start | bytes 1179656 | tf_op jit(solution)/shard_map/ppermute | solution.py:300
  6.0 6.4 %collective-permute-start = (bf16[64,768]{1,0:T(8,128)(2,1)S(1)}, bf16[64,768]{1,0:T(8,128)(2,1)S(1)}, u32[]{:S(2)}, u32[]{:S(2)}) collective-permute-start(bf16[64,768]{1,0:T(8,128)(2,1)S(1)} %get-tuple-element.71), channel_id=1, source_target_pairs={{0,4},{1,5},{2,6},{3,7},{4,0},{5,1},{6,2},{7,3},{8,12},{9,13},{10,... | collective-permute-start | bytes 294920 | tf_op jit(solution)/shard_map/ppermute | solution.py:300
  7.6 9.1 %collective-permute-start.2 = (bf16[64,768]{1,0:T(8,128)(2,1)S(1)}, bf16[64,768]{1,0:T(8,128)(2,1)S(1)}, u32[]{:S(2)}, u32[]{:S(2)}) collective-permute-start(bf16[64,768]{1,0:T(8,128)(2,1)S(1)} %get-tuple-element.68), channel_id=1, source_target_pairs={{0,12},{1,13},{2,14},{3,15},{4,8},{5,9},{6,10},{7,11},{8,4},{9,5},... | collective-permute-start | bytes 294920 | tf_op jit(solution)/shard_map/ppermute | solution.py:300
  10.1 8.8 %collective-permute-start.1 = (bf16[64,768]{1,0:T(8,128)(2,1)S(1)}, bf16[64,768]{1,0:T(8,128)(2,1)S(1)}, u32[]{:S(2)}, u32[]{:S(2)}) collective-permute-start(bf16[64,768]{1,0:T(8,128)(2,1)S(1)} %get-tuple-element.69), channel_id=1, source_target_pairs={{0,8},{1,9},{2,10},{3,11},{4,12},{5,13},{6,14},{7,15},{8,0},{9,1},... | collective-permute-start | bytes 294920 | tf_op jit(solution)/shard_map/ppermute | solution.py:300
  12.4 25.0 %copy-start = (bf16[384,512]{1,0:T(8,128)(2,1)S(1)}, bf16[384,512]{1,0:T(8,128)(2,1)}, u32[]{:S(2)}) copy-start(bf16[384,512]{1,0:T(8,128)(2,1)} %get-tuple-element.51.refs_4_) | copy-start | bytes 1179652
  12.4 38.7 %all-to-all-start = ((bf16[8,384,128]{2,1,0:T(8,128)(2,1)}), bf16[8,384,128]{2,1,0:T(8,128)(2,1)S(1)}, u32[]{:S(2)}, u32[]{:S(2)}) async-start(bf16[8,384,128]{2,1,0:T(8,128)(2,1)} %shard_map.102), calls=%async_computation | async-start | bytes 1572864 | tf_op jit(solution)/shard_map/all_to_all | solution.py:358
  18.9 16.7 %collective-permute-start.4 = (bf16[256,768]{1,0:T(8,128)(2,1)S(1)}, bf16[256,768]{1,0:T(8,128)(2,1)S(1)}, u32[]{:S(2)}, u32[]{:S(2)}) collective-permute-start(bf16[256,768]{1,0:T(8,128)(2,1)S(1)} %constant_dynamic-update-slice_fusion.refs_0_), channel_id=1, source_target_pairs={{0,2},{1,3},{2,0},{3,1},{4,6},{5,7},{6,4},{7,5},{8,10},{9,11},{10,... | collective-permute-start | bytes 1179656 | tf_op jit(solution)/shard_map/ppermute | solution.py:300
  19.4 16.2 %collective-permute-start.5 = (bf16[256,768]{1,0:T(8,128)(2,1)S(1)}, bf16[256,768]{1,0:T(8,128)(2,1)S(1)}, u32[]{:S(2)}, u32[]{:S(2)}) collective-permute-start(bf16[256,768]{1,0:T(8,128)(2,1)S(1)} %constant_dynamic-update-slice_fusion.refs_0_), channel_id=1, source_target_pairs={{0,1},{1,0},{2,3},{3,2},{4,5},{5,4},{6,7},{7,6},{8,9},{9,8},{10,11... | collective-permute-start | bytes 1179656 | tf_op jit(solution)/shard_map/ppermute | solution.py:300
  35.7 1.7 %collective-permute-start.6 = (bf16[256,768]{1,0:T(8,128)(2,1)S(1)}, bf16[256,768]{1,0:T(8,128)(2,1)S(1)}, u32[]{:S(2)}, u32[]{:S(2)}) collective-permute-start(bf16[256,768]{1,0:T(8,128)(2,1)S(1)} %collective-permute-done.4.refs_1_), channel_id=1, source_target_pairs={{0,1},{1,0},{2,3},{3,2},{4,5},{5,4},{6,7},{7,6},{8,9},{9,8},{10,11... | collective-permute-start | bytes 1179656 | tf_op jit(solution)/shard_map/ppermute | solution.py:300
  37.4 13.7 %copy-start.1 = (bf16[2,512,128]{2,1,0:T(8,128)(2,1)S(1)}, bf16[2,512,128]{2,1,0:T(8,128)(2,1)}, u32[]{:S(2)}) copy-start(bf16[2,512,128]{2,1,0:T(8,128)(2,1)} %get-tuple-element.39.text_ref) | copy-start | bytes 786436
  39.0 1.1 %copy-start.2 = (bf16[1024,768]{1,0:T(8,128)(2,1)}, bf16[1024,768]{1,0:T(8,128)(2,1)S(1)}, u32[]{:S(2)}) copy-start(bf16[1024,768]{1,0:T(8,128)(2,1)S(1)} %get-tuple-element.62.cot_ref) | copy-start | bytes 4718596
  40.2 8.3 %collective-permute-start.7 = (bf16[1024,128]{1,0:T(8,128)(2,1)S(1)}, bf16[1024,128]{1,0:T(8,128)(2,1)S(1)}, u32[]{:S(2)}, u32[]{:S(2)}) collective-permute-start(bf16[1024,128]{1,0:T(8,128)(2,1)S(1)} %get-tuple-element.55), channel_id=1, source_target_pairs={{0,4},{1,5},{2,6},{3,7},{4,0},{5,1},{6,2},{7,3},{8,12},{9,13},{10,... | collective-permute-start | bytes 786440 | tf_op jit(solution)/shard_map/ppermute | solution.py:300
  48.6 14.3 %collective-permute-start.9 = (bf16[1024,128]{1,0:T(8,128)(2,1)S(1)}, bf16[1024,128]{1,0:T(8,128)(2,1)S(1)}, u32[]{:S(2)}, u32[]{:S(2)}) collective-permute-start(bf16[1024,128]{1,0:T(8,128)(2,1)S(1)} %add_convert_fusion), channel_id=1, source_target_pairs={{0,8},{1,9},{2,10},{3,11},{4,12},{5,13},{6,14},{7,15},{8,0},{9,1},... | collective-permute-start | bytes 786440 | tf_op jit(solution)/shard_map/ppermute | solution.py:300
  56.0 12.5 %collective-permute-start.10 = (bf16[128,1024]{1,0:T(8,128)(2,1)S(1)}, bf16[128,1024]{1,0:T(8,128)(2,1)S(1)}, u32[]{:S(2)}, u32[]{:S(2)}) collective-permute-start(bf16[128,1024]{1,0:T(8,128)(2,1)S(1)} %get-tuple-element.64.out_ref.refs_0_), channel_id=1, source_target_pairs={{0,4},{1,5},{2,6},{3,7},{4,0},{5,1},{6,2},{7,3},{8,12},{9,13},{10,... | collective-permute-start | bytes 786440 | tf_op jit(solution)/shard_map/ppermute | solution.py:300
  57.8 16.2 %collective-permute-start.8 = (bf16[1024,128]{1,0:T(8,128)(2,1)S(1)}, bf16[1024,128]{1,0:T(8,128)(2,1)S(1)}, u32[]{:S(2)}, u32[]{:S(2)}) collective-permute-start(bf16[1024,128]{1,0:T(8,128)(2,1)S(1)} %get-tuple-element.56), channel_id=1, source_target_pairs={{0,4},{1,5},{2,6},{3,7},{4,0},{5,1},{6,2},{7,3},{8,12},{9,13},{10,... | collective-permute-start | bytes 786440 | tf_op jit(solution)/shard_map/ppermute | solution.py:300
  68.5 13.3 %collective-permute-start.11 = (bf16[128,1024]{1,0:T(8,128)(2,1)S(1)}, bf16[128,1024]{1,0:T(8,128)(2,1)S(1)}, u32[]{:S(2)}, u32[]{:S(2)}) collective-permute-start(bf16[128,1024]{1,0:T(8,128)(2,1)S(1)} %get-tuple-element.64.out_ref.refs_0_), channel_id=1, source_target_pairs={{0,8},{1,9},{2,10},{3,11},{4,12},{5,13},{6,14},{7,15},{8,0},{9,1},... | collective-permute-start | bytes 786440 | tf_op jit(solution)/shard_map/ppermute | solution.py:300
  81.8 9.2 %collective-permute-start.12 = (bf16[128,1024]{1,0:T(8,128)(2,1)S(1)}, bf16[128,1024]{1,0:T(8,128)(2,1)S(1)}, u32[]{:S(2)}, u32[]{:S(2)}) collective-permute-start(bf16[128,1024]{1,0:T(8,128)(2,1)S(1)} %collective-permute-done.11.refs_2_), channel_id=1, source_target_pairs={{0,4},{1,5},{2,6},{3,7},{4,0},{5,1},{6,2},{7,3},{8,12},{9,13},{10,... | collective-permute-start | bytes 786440 | tf_op jit(solution)/shard_map/ppermute | solution.py:300
  81.8 25.7 %all-to-all-start.1 = ((bf16[8,384,128]{2,1,0:T(8,128)(2,1)}), bf16[8,384,128]{2,1,0:T(8,128)(2,1)S(1)}, u32[]{:S(2)}, u32[]{:S(2)}) async-start(bf16[8,384,128]{2,1,0:T(8,128)(2,1)} %shard_map.106), calls=%async_computation.1 | async-start | bytes 1572864 | tf_op jit(solution)/shard_map/all_to_all | solution.py:392
  91.0 1.4 %copy-start.3 = (bf16[1024,768]{1,0:T(8,128)(2,1)S(1)}, bf16[1024,768]{1,0:T(8,128)(2,1)}, u32[]{:S(2)}) copy-start(bf16[1024,768]{1,0:T(8,128)(2,1)} %copy-done.2) | copy-start | bytes 4718596
  93.6 12.4 %collective-permute-start.13 = (bf16[512,384]{1,0:T(8,128)(2,1)S(1)}, bf16[512,384]{1,0:T(8,128)(2,1)S(1)}, u32[]{:S(2)}, u32[]{:S(2)}) collective-permute-start(bf16[512,384]{1,0:T(8,128)(2,1)S(1)} %get-tuple-element.67), channel_id=1, source_target_pairs={{0,2},{1,3},{2,0},{3,1},{4,6},{5,7},{6,4},{7,5},{8,10},{9,11},{10,... | collective-permute-start | bytes 1179656 | tf_op jit(solution)/shard_map/ppermute | solution.py:300

commit v14 on v13

--- a/solution.py
+++ b/solution.py
@@ -375,12 +375,11 @@
         moved=2 * image * columns,
     )
     near_far = exchange(near_far, 2)
+    near_far, out_t, near = lax.optimization_barrier((near_far, out_t, near))
     far = exchange((far + near_far.astype(F32)).astype(BF16), 4)
-    near, _ = lax.optimization_barrier((near, near_far))
     near = exchange(near, 2)
-    out_near = exchange(out_t, 2)
-    out_late, far, out_near = lax.optimization_barrier((out_t, far, out_near))
-    out_far = exchange(out_late, 4)
+    out_late, far, near = lax.optimization_barrier((out_t, far, near))
+    out_near, out_far = exchange(out_late, 2), exchange(out_late, 4)
     (grad_out,) = call(
         functools.partial(backward_kernel, chunk=chunk),
         [shape((n, 3 * rows, HD), BF16)],
@@ -390,7 +389,7 @@
         moved=4 * total * image,
     )
     grad_in = lax.all_to_all(grad_out, "seq", split_axis=0, concat_axis=0, tiled=True)
-    out_far, _ = lax.optimization_barrier((out_far, grad_out))
+    out_far, out_near, _ = lax.optimization_barrier((out_far, out_near, grad_out))
     outs = [out_t, out_near, out_far, exchange(out_far, 2)]
     dw_own, dw_other = call(
         weight_grad_kernel,

time: 109 us -> 105 us (0.963)
  waiting for transfers between devices: 63.4 us -> 57.2 us
  starting transfers between devices: 22.5 us -> 24.8 us
    ppermute x14, waiting for transfers between devices: 63.4 us -> 57.2 us  [exchange(): return lax.ppermute(array, ('seq', 'fsdp'), pairs)]
    ppermute x14, starting transfers between devices: 14.5 us -> 16.5 us  [exchange(): return lax.ppermute(array, ('seq', 'fsdp'), pairs)]
where the time goes in v14:
time: 105 us
  waiting for transfers between devices  57.2 us (54%)
  starting transfers between devices  24.8 us (24%)
  Pallas kernels  19.3 us (18%)
  local copies, waits for them, and re-layouts  2.63 us (3%)
    ppermute x14, waiting for transfers between devices, exchange(): return lax.ppermute(array, ('seq', 'fsdp'), pairs)  57.2 us
    pallas_call x8, Pallas kernels, call(): pl.pallas_call(kernel, out_shape=outs, grid_spec=pltpu.PrefetchScalarGrid...  19.3 us
    ppermute x14, starting transfers between devices, exchange(): return lax.ppermute(array, ('seq', 'fsdp'), pairs)  16.5 us
    all_to_all x1, starting transfers between devices, local(): lax.all_to_all(tok_out, 'seq', split_axis=0, concat_axis=0, tiled=True)  4.37 us
    all_to_all x1, starting transfers between devices, local(): lax.all_to_all(grad_out, 'seq', split_axis=0, concat_axis=0, tiled=True)  3.87 us
    unnamed x13, local copies, waits for them, and re-layouts  2.58 us
  transfers between devices with their start and end apart: 16, of which 10 were waited for; matrix products, arithmetic and copies ran while one was open for 0% of the time, Pallas kernels for 15%

profile of v14, /device:TPU:0, one launch (start us, length us, event | category | flops | bytes accessed | tf_op | source)
XLA Modules:
  0.0 104.7 jit_solution(1399606507766238092)
XLA Ops:
  0.6 0.0 copy-start.4
  0.6 2.3 %shard_map.103 = (bf16[384,512]{1,0:T(8,128)(2,1)}, bf16[384,512]{1,0:T(8,128)(2,1)}, bf16[2,512,128]{2,1,0:T(8,128)(2,1)}) custom-call(s32[1]{0:T(128)} %bitcast.me_ref, bf16[384,1024]{1,0:T(8,128)(2,1)} %w_ref.1, bf16[512,1024]{1,0:T(8,128)(2,1)} %kt_ref.1, bf16[512,1024]{1,0:T(8,128)(2,1)} %vt_ref.1), custom_call_target="tpu_custom_call" | custom-call | bytes 1572864 | tf_op jit(solution)/shard_map/pallas_call | solution.py:147
  3.0 3.0 %collective-permute-start.3 = (bf16[384,512]{1,0:T(8,128)(2,1)}, bf16[384,512]{1,0:T(8,128)(2,1)S(1)}, u32[]{:S(2)}, u32[]{:S(2)}) collective-permute-start(bf16[384,512]{1,0:T(8,128)(2,1)} %get-tuple-element.48), channel_id=1, source_target_pairs={{0,2},{1,3},{2,0},{3,1},{4,6},{5,7},{6,4},{7,5},{8,10},{9,11},{10,... | collective-permute-start | bytes 1179656 | tf_op jit(solution)/shard_map/ppermute | solution.py:300
  6.0 0.0 copy-done.4
  6.0 1.6 %collective-permute-start = (bf16[64,768]{1,0:T(8,128)(2,1)S(1)}, bf16[64,768]{1,0:T(8,128)(2,1)S(1)}, u32[]{:S(2)}, u32[]{:S(2)}) collective-permute-start(bf16[64,768]{1,0:T(8,128)(2,1)S(1)} %get-tuple-element.77), channel_id=1, source_target_pairs={{0,4},{1,5},{2,6},{3,7},{4,0},{5,1},{6,2},{7,3},{8,12},{9,13},{10,... | collective-permute-start | bytes 294920 | tf_op jit(solution)/shard_map/ppermute | solution.py:300
  7.6 2.5 %collective-permute-start.2 = (bf16[64,768]{1,0:T(8,128)(2,1)S(1)}, bf16[64,768]{1,0:T(8,128)(2,1)S(1)}, u32[]{:S(2)}, u32[]{:S(2)}) collective-permute-start(bf16[64,768]{1,0:T(8,128)(2,1)S(1)} %get-tuple-element.74), channel_id=1, source_target_pairs={{0,12},{1,13},{2,14},{3,15},{4,8},{5,9},{6,10},{7,11},{8,4},{9,5},... | collective-permute-start | bytes 294920 | tf_op jit(solution)/shard_map/ppermute | solution.py:300
  10.1 0.1 collective-permute-start.1
  10.2 2.1 %shard_map.102 = bf16[8,384,128]{2,1,0:T(8,128)(2,1)} custom-call(bf16[128,1024]{1,0:T(8,128)(2,1)} %q_ref.1, bf16[128,1024]{1,0:T(8,128)(2,1)} %k_ref.1, bf16[128,1024]{1,0:T(8,128)(2,1)} %v_ref.1), custom_call_target="tpu_custom_call" | custom-call | bytes 1572864 | tf_op jit(solution)/shard_map/pallas_call | solution.py:147
  12.4 0.0 collective-permute-done
  12.4 4.4 %all-to-all-start = ((bf16[8,384,128]{2,1,0:T(8,128)(2,1)}), bf16[8,384,128]{2,1,0:T(8,128)(2,1)S(1)}, u32[]{:S(2)}, u32[]{:S(2)}) async-start(bf16[8,384,128]{2,1,0:T(8,128)(2,1)} %shard_map.102), calls=%async_computation | async-start | bytes 1572864 | tf_op jit(solution)/shard_map/all_to_all | solution.py:358
  16.8 0.0 collective-permute-done.2
  16.8 2.1 %collective-permute-done.1 = bf16[64,768]{1,0:T(8,128)(2,1)S(1)} collective-permute-done((bf16[64,768]{1,0:T(8,128)(2,1)S(1)}, bf16[64,768]{1,0:T(8,128)(2,1)S(1)}, u32[]{:S(2)}, u32[]{:S(2)}) %collective-permute-start.1) | collective-permute-done | bytes 98336 | tf_op jit(solution)/shard_map/ppermute | solution.py:300
  18.9 0.0 collective-permute-done.3.refs_5_
  18.9 0.0 copy-start.1
  19.0 0.5 collective-permute-start.4
  19.4 0.0 collective-permute-start.5
  19.4 16.2 %collective-permute-done.4.refs_1_ = bf16[256,768]{1,0:T(8,128)(2,1)S(1)} collective-permute-done((bf16[256,768]{1,0:T(8,128)(2,1)S(1)}, bf16[256,768]{1,0:T(8,128)(2,1)S(1)}, u32[]{:S(2)}, u32[]{:S(2)}) %collective-permute-start.4) | collective-permute-done | bytes 393248 | tf_op jit(solution)/shard_map/ppermute | solution.py:300
  35.7 0.0 collective-permute-start.6
  35.7 0.0 collective-permute-done.5.refs_2_
  35.7 1.7 %collective-permute-done.6.refs_3_ = bf16[256,768]{1,0:T(8,128)(2,1)S(1)} collective-permute-done((bf16[256,768]{1,0:T(8,128)(2,1)S(1)}, bf16[256,768]{1,0:T(8,128)(2,1)S(1)}, u32[]{:S(2)}, u32[]{:S(2)}) %collective-permute-start.6) | collective-permute-done | bytes 393248 | tf_op jit(solution)/shard_map/ppermute | solution.py:300
  37.4 0.0 copy-done
  37.4 1.7 %shard_map.105 = (f32[1024,128]{1,0:T(8,128)S(1)}, f32[1024,128]{1,0:T(8,128)S(1)}, bf16[1024,128]{1,0:T(8,128)(2,1)S(1)}, bf16[1024,128]{1,0:T(8,128)(2,1)S(1)}, bf16[1024,768]{1,0:T(8,128)(2,1)S(1)}) custom-call(bf16[256,768]{1,0:T(8,128)(2,1)S(1)} %constant_dynamic-update-slice_fusion.refs_0_, bf16[256,768]{1,0:T(8,128)(2,1)S(1)} %collective-permute-done.4.refs_1_, ...), custom_call_target="tpu_custom_call" | custom-call | flops 805306368 | bytes 1572864 | tf_op jit(solution)/shard_map/pallas_call | solution.py:147
  39.0 0.0 copy-start.2
  39.1 1.1 %copy-done.2 = bf16[1024,768]{1,0:T(8,128)(2,1)} copy-done((bf16[1024,768]{1,0:T(8,128)(2,1)}, bf16[1024,768]{1,0:T(8,128)(2,1)S(1)}, u32[]{:S(2)}) %copy-start.2) | copy-done | bytes 1572888
  40.2 0.6 collective-permute-start.7
  40.8 0.0 all-to-all-done.tok_ref
  40.8 4.9 %shard_map.104 = (bf16[1536,1024]{1,0:T(8,128)(2,1)S(1)}, bf16[128,1024]{1,0:T(8,128)(2,1)S(1)}, bf16[1024,128]{1,0:T(8,128)(2,1)S(1)}, bf16[128,1536]{1,0:T(8,128)(2,1)S(1)}, bf16[1536,128]{1,0:T(8,128)(2,1)S(1)}) custom-call(bf16[8,384,128]{2,1,0:T(8,128)(2,1)S(1)} %all-to-all-done.tok_ref, bf16[2,512,128]{2,1,0:T(8,128)(2,1)S(1)} %copy-done.1), custom_call_target="tpu_custom_call" | custom-call | flops 805306368 | bytes 6291456 | tf_op jit(solution)/shard_map/pallas_call | solution.py:147
  45.7 2.8 %collective-permute-done.7 = bf16[1024,128]{1,0:T(8,128)(2,1)S(1)} collective-permute-done((bf16[1024,128]{1,0:T(8,128)(2,1)S(1)}, bf16[1024,128]{1,0:T(8,128)(2,1)S(1)}, u32[]{:S(2)}, u32[]{:S(2)}) %collective-permute-start.7) | collective-permute-done | bytes 262176 | tf_op jit(solution)/shard_map/ppermute | solution.py:300
  48.5 0.1 add_convert_fusion
  48.6 2.5 %collective-permute-start.8 = (bf16[1024,128]{1,0:T(8,128)(2,1)S(1)}, bf16[1024,128]{1,0:T(8,128)(2,1)S(1)}, u32[]{:S(2)}, u32[]{:S(2)}) collective-permute-start(bf16[1024,128]{1,0:T(8,128)(2,1)S(1)} %add_convert_fusion), channel_id=1, source_target_pairs={{0,8},{1,9},{2,10},{3,11},{4,12},{5,13},{6,14},{7,15},{8,0},{9,1},... | collective-permute-start | bytes 786440 | tf_op jit(solution)/shard_map/ppermute | solution.py:300
  51.1 1.7 %collective-permute-start.9 = (bf16[1024,128]{1,0:T(8,128)(2,1)S(1)}, bf16[1024,128]{1,0:T(8,128)(2,1)S(1)}, u32[]{:S(2)}, u32[]{:S(2)}) collective-permute-start(bf16[1024,128]{1,0:T(8,128)(2,1)S(1)} %get-tuple-element.62), channel_id=1, source_target_pairs={{0,4},{1,5},{2,6},{3,7},{4,0},{5,1},{6,2},{7,3},{8,12},{9,13},{10,... | collective-permute-start | bytes 786440 | tf_op jit(solution)/shard_map/ppermute | solution.py:300
  52.9 10.1 %collective-permute-done.8.far_ref = bf16[1024,128]{1,0:T(8,128)(2,1)S(1)} collective-permute-done((bf16[1024,128]{1,0:T(8,128)(2,1)S(1)}, bf16[1024,128]{1,0:T(8,128)(2,1)S(1)}, u32[]{:S(2)}, u32[]{:S(2)}) %collective-permute-start.8) | collective-permute-done | bytes 262176 | tf_op jit(solution)/shard_map/ppermute | solution.py:300
  62.9 0.4 collective-permute-done.9.near_ref
  63.3 1.3 %collective-permute-start.11 = (bf16[128,1024]{1,0:T(8,128)(2,1)S(1)}, bf16[128,1024]{1,0:T(8,128)(2,1)S(1)}, u32[]{:S(2)}, u32[]{:S(2)}) collective-permute-start(bf16[128,1024]{1,0:T(8,128)(2,1)S(1)} %get-tuple-element.69.out_ref.refs_0_), channel_id=1, source_target_pairs={{0,4},{1,5},{2,6},{3,7},{4,0},{5,1},{6,2},{7,3},{8,12},{9,13},{10,... | collective-permute-start | bytes 786440 | tf_op jit(solution)/shard_map/ppermute | solution.py:300
  64.6 2.3 %collective-permute-start.10 = (bf16[128,1024]{1,0:T(8,128)(2,1)S(1)}, bf16[128,1024]{1,0:T(8,128)(2,1)S(1)}, u32[]{:S(2)}, u32[]{:S(2)}) collective-permute-start(bf16[128,1024]{1,0:T(8,128)(2,1)S(1)} %get-tuple-element.69.out_ref.refs_0_), channel_id=1, source_target_pairs={{0,8},{1,9},{2,10},{3,11},{4,12},{5,13},{6,14},{7,15},{8,0},{9,1},... | collective-permute-start | bytes 786440 | tf_op jit(solution)/shard_map/ppermute | solution.py:300
  66.9 4.5 %shard_map.106 = bf16[8,384,128]{2,1,0:T(8,128)(2,1)} custom-call(bf16[1024,128]{1,0:T(8,128)(2,1)S(1)} %get-tuple-element.43.queries_ref, bf16[128,1536]{1,0:T(8,128)(2,1)S(1)} %get-tuple-element.44.keys_t_ref, bf16[1536,128]{1,0:T(8,128)(2,1)S(1)} %get-tuple-element.45.vals_ref, bf16[1536,1024]{1,0:T(8,128)(2,1)S(1)} %get-tuple-element.46.probs_ref, ...), custom_call_target="tpu_custom_call" | custom-call | flops 1610612736 | bytes 6291456 | tf_op jit(solution)/shard_map/pallas_call | solution.py:147
  71.4 4.2 %collective-permute-done.11.refs_1_ = bf16[128,1024]{1,0:T(8,128)(2,1)S(1)} collective-permute-done((bf16[128,1024]{1,0:T(8,128)(2,1)S(1)}, bf16[128,1024]{1,0:T(8,128)(2,1)S(1)}, u32[]{:S(2)}, u32[]{:S(2)}) %collective-permute-start.11) | collective-permute-done | bytes 262176 | tf_op jit(solution)/shard_map/ppermute | solution.py:300
  75.6 3.2 %collective-permute-done.10.refs_2_ = bf16[128,1024]{1,0:T(8,128)(2,1)S(1)} collective-permute-done((bf16[128,1024]{1,0:T(8,128)(2,1)S(1)}, bf16[128,1024]{1,0:T(8,128)(2,1)S(1)}, u32[]{:S(2)}, u32[]{:S(2)}) %collective-permute-start.10) | collective-permute-done | bytes 262176 | tf_op jit(solution)/shard_map/ppermute | solution.py:300
  78.7 0.3 collective-permute-start.12
  79.1 3.9 %all-to-all-start.1 = ((bf16[8,384,128]{2,1,0:T(8,128)(2,1)}), bf16[8,384,128]{2,1,0:T(8,128)(2,1)S(1)}, u32[]{:S(2)}, u32[]{:S(2)}) async-start(bf16[8,384,128]{2,1,0:T(8,128)(2,1)} %shard_map.106), calls=%async_computation.1 | async-start | bytes 1572864 | tf_op jit(solution)/shard_map/all_to_all | solution.py:391
  82.9 2.9 %collective-permute-done.12.refs_3_ = bf16[128,1024]{1,0:T(8,128)(2,1)S(1)} collective-permute-done((bf16[128,1024]{1,0:T(8,128)(2,1)S(1)}, bf16[128,1024]{1,0:T(8,128)(2,1)S(1)}, u32[]{:S(2)}, u32[]{:S(2)}) %collective-permute-start.12) | collective-permute-done | bytes 262176 | tf_op jit(solution)/shard_map/ppermute | solution.py:300
  85.8 1.4 %copy-done.3 = bf16[1024,768]{1,0:T(8,128)(2,1)S(1)} copy-done((bf16[1024,768]{1,0:T(8,128)(2,1)S(1)}, bf16[1024,768]{1,0:T(8,128)(2,1)}, u32[]{:S(2)}) %copy-start.3) | copy-done | bytes 1572888
  87.2 1.3 %shard_map.108 = (bf16[512,384]{1,0:T(8,128)(2,1)S(1)}, bf16[512,384]{1,0:T(8,128)(2,1)S(1)}) custom-call(bf16[1024,768]{1,0:T(8,128)(2,1)S(1)} %copy-done.3, bf16[128,1024]{1,0:T(8,128)(2,1)S(1)} %get-tuple-element.69.out_ref.refs_0_, bf16[128,1024]{1,0:T(8,128)(2,1)S(1)} %collective-permute-done.11.refs_1_, ...), custom_call_target="tpu_custom_call" | custom-call | flops 9663676416 | bytes 1572864 | tf_op jit(solution)/shard_map/pallas_call | solution.py:147
  88.5 0.1 collective-permute-start.13
  88.6 13.6 %collective-permute-done.13.other_ref = bf16[512,384]{1,0:T(8,128)(2,1)S(1)} collective-permute-done((bf16[512,384]{1,0:T(8,128)(2,1)S(1)}, bf16[512,384]{1,0:T(8,128)(2,1)S(1)}, u32[]{:S(2)}, u32[]{:S(2)}) %collective-permute-start.13) | collective-permute-done | bytes 393248 | tf_op jit(solution)/shard_map/ppermute | solution.py:300
  102.1 1.5 %shard_map.109 = f32[384,1024]{1,0:T(8,128)} custom-call(bf16[512,384]{1,0:T(8,128)(2,1)S(1)} %get-tuple-element.72.own_ref, bf16[512,384]{1,0:T(8,128)(2,1)S(1)} %collective-permute-done.13.other_ref), custom_call_target="tpu_custom_call" | custom-call | bytes 2359296 | tf_op jit(solution)/shard_map/pallas_call | solution.py:147
  103.6 0.0 all-to-all-done.1.tok_ref
  103.6 1.1 %shard_map.107 = (bf16[128,1024]{1,0:T(8,128)(2,1)}, bf16[128,1024]{1,0:T(8,128)(2,1)}, bf16[128,1024]{1,0:T(8,128)(2,1)}) custom-call(bf16[8,384,128]{2,1,0:T(8,128)(2,1)S(1)} %all-to-all-done.1.tok_ref), custom_call_target="tpu_custom_call" | custom-call | bytes 1572864 | tf_op jit(solution)/shard_map/pallas_call | solution.py:147
  (8 shorter events, 0.1 us)
Async XLA Ops:
  0.6 5.3 %copy-start.4 = (bf16[128,3072]{1,0:T(8,128)(2,1)S(1)}, bf16[128,3072]{1,0:T(8,128)(2,1)}, u32[]{:S(2)}) copy-start(bf16[128,3072]{1,0:T(8,128)(2,1)} %param.13) | copy-start | bytes 2359300
  3.0 15.9 %collective-permute-start.3 = (bf16[384,512]{1,0:T(8,128)(2,1)}, bf16[384,512]{1,0:T(8,128)(2,1)S(1)}, u32[]{:S(2)}, u32[]{:S(2)}) collective-permute-start(bf16[384,512]{1,0:T(8,128)(2,1)} %get-tuple-element.48), channel_id=1, source_target_pairs={{0,2},{1,3},{2,0},{3,1},{4,6},{5,7},{6,4},{7,5},{8,10},{9,11},{10,... | collective-permute-start | bytes 1179656 | tf_op jit(solution)/shard_map/ppermute | solution.py:300
  6.0 6.4 %collective-permute-start = (bf16[64,768]{1,0:T(8,128)(2,1)S(1)}, bf16[64,768]{1,0:T(8,128)(2,1)S(1)}, u32[]{:S(2)}, u32[]{:S(2)}) collective-permute-start(bf16[64,768]{1,0:T(8,128)(2,1)S(1)} %get-tuple-element.77), channel_id=1, source_target_pairs={{0,4},{1,5},{2,6},{3,7},{4,0},{5,1},{6,2},{7,3},{8,12},{9,13},{10,... | collective-permute-start | bytes 294920 | tf_op jit(solution)/shard_map/ppermute | solution.py:300
  7.6 9.1 %collective-permute-start.2 = (bf16[64,768]{1,0:T(8,128)(2,1)S(1)}, bf16[64,768]{1,0:T(8,128)(2,1)S(1)}, u32[]{:S(2)}, u32[]{:S(2)}) collective-permute-start(bf16[64,768]{1,0:T(8,128)(2,1)S(1)} %get-tuple-element.74), channel_id=1, source_target_pairs={{0,12},{1,13},{2,14},{3,15},{4,8},{5,9},{6,10},{7,11},{8,4},{9,5},... | collective-permute-start | bytes 294920 | tf_op jit(solution)/shard_map/ppermute | solution.py:300
  10.1 8.8 %collective-permute-start.1 = (bf16[64,768]{1,0:T(8,128)(2,1)S(1)}, bf16[64,768]{1,0:T(8,128)(2,1)S(1)}, u32[]{:S(2)}, u32[]{:S(2)}) collective-permute-start(bf16[64,768]{1,0:T(8,128)(2,1)S(1)} %get-tuple-element.75), channel_id=1, source_target_pairs={{0,8},{1,9},{2,10},{3,11},{4,12},{5,13},{6,14},{7,15},{8,0},{9,1},... | collective-permute-start | bytes 294920 | tf_op jit(solution)/shard_map/ppermute | solution.py:300
  12.4 25.0 %copy-start = (bf16[384,512]{1,0:T(8,128)(2,1)S(1)}, bf16[384,512]{1,0:T(8,128)(2,1)}, u32[]{:S(2)}) copy-start(bf16[384,512]{1,0:T(8,128)(2,1)} %get-tuple-element.53.refs_4_) | copy-start | bytes 1179652
  12.4 28.4 %all-to-all-start = ((bf16[8,384,128]{2,1,0:T(8,128)(2,1)}), bf16[8,384,128]{2,1,0:T(8,128)(2,1)S(1)}, u32[]{:S(2)}, u32[]{:S(2)}) async-start(bf16[8,384,128]{2,1,0:T(8,128)(2,1)} %shard_map.102), calls=%async_computation | async-start | bytes 1572864 | tf_op jit(solution)/shard_map/all_to_all | solution.py:358
  18.9 21.9 %copy-start.1 = (bf16[2,512,128]{2,1,0:T(8,128)(2,1)S(1)}, bf16[2,512,128]{2,1,0:T(8,128)(2,1)}, u32[]{:S(2)}) copy-start(bf16[2,512,128]{2,1,0:T(8,128)(2,1)} %get-tuple-element.42.text_ref) | copy-start | bytes 786436
  19.0 16.7 %collective-permute-start.4 = (bf16[256,768]{1,0:T(8,128)(2,1)S(1)}, bf16[256,768]{1,0:T(8,128)(2,1)S(1)}, u32[]{:S(2)}, u32[]{:S(2)}) collective-permute-start(bf16[256,768]{1,0:T(8,128)(2,1)S(1)} %constant_dynamic-update-slice_fusion.refs_0_), channel_id=1, source_target_pairs={{0,2},{1,3},{2,0},{3,1},{4,6},{5,7},{6,4},{7,5},{8,10},{9,11},{10,... | collective-permute-start | bytes 1179656 | tf_op jit(solution)/shard_map/ppermute | solution.py:300
  19.4 16.2 %collective-permute-start.5 = (bf16[256,768]{1,0:T(8,128)(2,1)S(1)}, bf16[256,768]{1,0:T(8,128)(2,1)S(1)}, u32[]{:S(2)}, u32[]{:S(2)}) collective-permute-start(bf16[256,768]{1,0:T(8,128)(2,1)S(1)} %constant_dynamic-update-slice_fusion.refs_0_), channel_id=1, source_target_pairs={{0,1},{1,0},{2,3},{3,2},{4,5},{5,4},{6,7},{7,6},{8,9},{9,8},{10,11... | collective-permute-start | bytes 1179656 | tf_op jit(solution)/shard_map/ppermute | solution.py:300
  35.7 1.7 %collective-permute-start.6 = (bf16[256,768]{1,0:T(8,128)(2,1)S(1)}, bf16[256,768]{1,0:T(8,128)(2,1)S(1)}, u32[]{:S(2)}, u32[]{:S(2)}) collective-permute-start(bf16[256,768]{1,0:T(8,128)(2,1)S(1)} %collective-permute-done.4.refs_1_), channel_id=1, source_target_pairs={{0,1},{1,0},{2,3},{3,2},{4,5},{5,4},{6,7},{7,6},{8,9},{9,8},{10,11... | collective-permute-start | bytes 1179656 | tf_op jit(solution)/shard_map/ppermute | solution.py:300
  39.0 1.1 %copy-start.2 = (bf16[1024,768]{1,0:T(8,128)(2,1)}, bf16[1024,768]{1,0:T(8,128)(2,1)S(1)}, u32[]{:S(2)}) copy-start(bf16[1024,768]{1,0:T(8,128)(2,1)S(1)} %get-tuple-element.68.cot_ref) | copy-start | bytes 4718596
  40.2 8.3 %collective-permute-start.7 = (bf16[1024,128]{1,0:T(8,128)(2,1)S(1)}, bf16[1024,128]{1,0:T(8,128)(2,1)S(1)}, u32[]{:S(2)}, u32[]{:S(2)}) collective-permute-start(bf16[1024,128]{1,0:T(8,128)(2,1)S(1)} %get-tuple-element.55), channel_id=1, source_target_pairs={{0,4},{1,5},{2,6},{3,7},{4,0},{5,1},{6,2},{7,3},{8,12},{9,13},{10,... | collective-permute-start | bytes 786440 | tf_op jit(solution)/shard_map/ppermute | solution.py:300
  48.6 14.3 %collective-permute-start.8 = (bf16[1024,128]{1,0:T(8,128)(2,1)S(1)}, bf16[1024,128]{1,0:T(8,128)(2,1)S(1)}, u32[]{:S(2)}, u32[]{:S(2)}) collective-permute-start(bf16[1024,128]{1,0:T(8,128)(2,1)S(1)} %add_convert_fusion), channel_id=1, source_target_pairs={{0,8},{1,9},{2,10},{3,11},{4,12},{5,13},{6,14},{7,15},{8,0},{9,1},... | collective-permute-start | bytes 786440 | tf_op jit(solution)/shard_map/ppermute | solution.py:300
  51.1 12.2 %collective-permute-start.9 = (bf16[1024,128]{1,0:T(8,128)(2,1)S(1)}, bf16[1024,128]{1,0:T(8,128)(2,1)S(1)}, u32[]{:S(2)}, u32[]{:S(2)}) collective-permute-start(bf16[1024,128]{1,0:T(8,128)(2,1)S(1)} %get-tuple-element.62), channel_id=1, source_target_pairs={{0,4},{1,5},{2,6},{3,7},{4,0},{5,1},{6,2},{7,3},{8,12},{9,13},{10,... | collective-permute-start | bytes 786440 | tf_op jit(solution)/shard_map/ppermute | solution.py:300
  63.3 12.2 %collective-permute-start.11 = (bf16[128,1024]{1,0:T(8,128)(2,1)S(1)}, bf16[128,1024]{1,0:T(8,128)(2,1)S(1)}, u32[]{:S(2)}, u32[]{:S(2)}) collective-permute-start(bf16[128,1024]{1,0:T(8,128)(2,1)S(1)} %get-tuple-element.69.out_ref.refs_0_), channel_id=1, source_target_pairs={{0,4},{1,5},{2,6},{3,7},{4,0},{5,1},{6,2},{7,3},{8,12},{9,13},{10,... | collective-permute-start | bytes 786440 | tf_op jit(solution)/shard_map/ppermute | solution.py:300
  64.6 14.1 %collective-permute-start.10 = (bf16[128,1024]{1,0:T(8,128)(2,1)S(1)}, bf16[128,1024]{1,0:T(8,128)(2,1)S(1)}, u32[]{:S(2)}, u32[]{:S(2)}) collective-permute-start(bf16[128,1024]{1,0:T(8,128)(2,1)S(1)} %get-tuple-element.69.out_ref.refs_0_), channel_id=1, source_target_pairs={{0,8},{1,9},{2,10},{3,11},{4,12},{5,13},{6,14},{7,15},{8,0},{9,1},... | collective-permute-start | bytes 786440 | tf_op jit(solution)/shard_map/ppermute | solution.py:300
  78.7 7.1 %collective-permute-start.12 = (bf16[128,1024]{1,0:T(8,128)(2,1)S(1)}, bf16[128,1024]{1,0:T(8,128)(2,1)S(1)}, u32[]{:S(2)}, u32[]{:S(2)}) collective-permute-start(bf16[128,1024]{1,0:T(8,128)(2,1)S(1)} %collective-permute-done.10.refs_2_), channel_id=1, source_target_pairs={{0,4},{1,5},{2,6},{3,7},{4,0},{5,1},{6,2},{7,3},{8,12},{9,13},{10,... | collective-permute-start | bytes 786440 | tf_op jit(solution)/shard_map/ppermute | solution.py:300
  79.1 24.6 %all-to-all-start.1 = ((bf16[8,384,128]{2,1,0:T(8,128)(2,1)}), bf16[8,384,128]{2,1,0:T(8,128)(2,1)S(1)}, u32[]{:S(2)}, u32[]{:S(2)}) async-start(bf16[8,384,128]{2,1,0:T(8,128)(2,1)} %shard_map.106), calls=%async_computation.1 | async-start | bytes 1572864 | tf_op jit(solution)/shard_map/all_to_all | solution.py:391
  85.8 1.4 %copy-start.3 = (bf16[1024,768]{1,0:T(8,128)(2,1)S(1)}, bf16[1024,768]{1,0:T(8,128)(2,1)}, u32[]{:S(2)}) copy-start(bf16[1024,768]{1,0:T(8,128)(2,1)} %copy-done.2) | copy-start | bytes 4718596
  88.5 13.7 %collective-permute-start.13 = (bf16[512,384]{1,0:T(8,128)(2,1)S(1)}, bf16[512,384]{1,0:T(8,128)(2,1)S(1)}, u32[]{:S(2)}, u32[]{:S(2)}) collective-permute-start(bf16[512,384]{1,0:T(8,128)(2,1)S(1)} %get-tuple-element.73), channel_id=1, source_target_pairs={{0,2},{1,3},{2,0},{3,1},{4,6},{5,7},{6,4},{7,5},{8,10},{9,11},{10,... | collective-permute-start | bytes 1179656 | tf_op jit(solution)/shard_map/ppermute | solution.py:300

commit v15 on v14

--- a/solution.py
+++ b/solution.py
@@ -11,7 +11,7 @@
 HD = 128
 F32 = jnp.float32
 BF16 = jnp.bfloat16
-LIMIT = 28 * 1024 * 1024
+LIMIT = 16 * 1024 * 1024
 NT = (((1,), (1,)), ((), ()))
 
 
@@ -206,32 +206,33 @@
         out_ref[:, span] = jnp.dot(vals_t[...], low, preferred_element_type=F32).astype(BF16)
 
 
-def partial_kernel(*refs):
-    *pieces, own_ref, other_ref, mine_ref, far_ref, near_ref, near_far_ref, cot_ref, weight = refs
+def partial_kernel(*refs, kinds):
+    *pieces, own_ref, other_ref, mine_ref, far0_ref, far1_ref, near_ref, send0_ref, send1_ref, cot_ref, weight = refs
     me = lax.axis_index("seq")
     core = lax.axis_index("fsdp")
-    count = len(STEPS)
-    part = pieces[0].shape[0] // count
-    for p, piece in enumerate(pieces):
-        row, swapped = p % 2, p // 2
+    part = pieces[0].shape[0]
+    for piece, (first, row, swapped) in zip(pieces, kinds):
         shift = jnp.bitwise_xor(core, swapped) * part
-        for i, step in enumerate(STEPS):
-            at = pl.multiple_of(jnp.bitwise_xor(me, step + row) * (2 * part) + shift, 16)
+        for i in range(piece.shape[0] // part):
+            at = pl.multiple_of(jnp.bitwise_xor(me, STEPS[first + i] + row) * (2 * part) + shift, 16)
             cot_ref[pl.ds(at, part), :] = piece[i * part : (i + 1) * part, :]
     depth = own_ref.shape[0]
     y = lax.rem(me, 2)
     weight[pl.ds(pl.multiple_of(y * depth, 16), depth), :] = own_ref[...]
     weight[pl.ds(pl.multiple_of((1 - y) * depth, 16), depth), :] = other_ref[...]
     step = 256
-
-    @pl.loop(0, cot_ref.shape[0] // step)
-    def _(i):
-        at = pl.ds(pl.multiple_of(i * step, step), step)
-        part = jnp.dot(cot_ref[at, :], weight[...], preferred_element_type=F32)
-        mine_ref[at, :] = part[:, :HD]
-        near_ref[at, :] = part[:, HD : 2 * HD].astype(BF16)
-        far_ref[at, :] = part[:, 2 * HD : 3 * HD]
-        near_far_ref[at, :] = part[:, 3 * HD :].astype(BF16)
+    half = far0_ref.shape[0] // step
+    for h, (far_ref, send_ref) in enumerate(((far0_ref, send0_ref), (far1_ref, send1_ref))):
+
+        @pl.loop(0, half)
+        def _(i):
+            at = pl.ds(pl.multiple_of((h * half + i) * step, step), step)
+            within = pl.ds(pl.multiple_of(i * step, step), step)
+            part = jnp.dot(cot_ref[at, :], weight[...], preferred_element_type=F32)
+            mine_ref[at, :] = part[:, :HD]
+            near_ref[at, :] = part[:, HD : 2 * HD].astype(BF16)
+            far_ref[within, :] = part[:, 2 * HD : 3 * HD]
+            send_ref[within, :] = part[:, 3 * HD :].astype(BF16)
 
 
 def weight_grad_kernel(cot_ref, *refs):
@@ -248,7 +249,7 @@
 
 
 def backward_kernel(
-    queries_ref, keys_t_ref, vals_ref, probs_ref, out_ref, mine_ref, near_ref, far_ref, send_ref, dk, dv, *, chunk
+    queries_ref, keys_t_ref, vals_ref, probs_ref, out_ref, mine_ref, near_ref, far0_ref, far1_ref, send_ref, dk, dv, *, chunk
 ):
     n, three, _ = send_ref.shape
     rows = three // 3
@@ -257,7 +258,9 @@
     per = chunk // rows
     for c in range(image // chunk):
         span = slice(c * chunk, (c + 1) * chunk)
-        grads = mine_ref[span, :] + near_ref[span, :].astype(F32) + far_ref[span, :].astype(F32)
+        far_ref, within = (far0_ref, c) if 2 * c * chunk < image else (far1_ref, c - image // chunk // 2)
+        far = far_ref[within * chunk : (within + 1) * chunk, :].astype(F32)
+        grads = mine_ref[span, :] + near_ref[span, :].astype(F32) + far
         grads = grads.astype(BF16)
         row_dot = jnp.sum(
             grads.astype(F32).T * out_ref[:, span].astype(F32), axis=0, keepdims=True
@@ -305,16 +308,19 @@
     part, columns = rows // 2, width // len(STEPS)
     z = lax.axis_index("seq") // 2
     first = lax.axis_index("fsdp") * part
-    return [
+    along = [
         exchange(lax.dynamic_slice(d_out, (first, (z ^ (step // 2)) * columns), (part, columns)), step)
         for step in STEPS
     ]
-
-
-def gather_cotangents(along):
-    row = jnp.concatenate(along, axis=0)
-    pieces = [row, exchange(row, 1)]
-    return pieces + [exchange(piece, cores=True) for piece in pieces]
+    return along, lax.dynamic_slice(d_out, (part - first, z * columns), (part, columns))
+
+
+def gather_cotangents(own, own_swapped, own_y, rest):
+    rest = jnp.concatenate(rest, axis=0)
+    rest_y = exchange(rest, 1)
+    swapped = [exchange(piece, cores=True) for piece in (own_y, rest, rest_y)]
+    pieces = [own, own_swapped, own_y, rest, rest_y, *swapped]
+    return pieces, [(0, 0, 0), (0, 0, 1), (0, 1, 0), (1, 0, 0), (1, 1, 0), (0, 1, 1), (1, 0, 1), (1, 1, 1)]
 
 
 def local(q_img, k_img, v_img, k_txt, v_txt, out_weight, d_out):
@@ -344,7 +350,8 @@
     )
     d_out, give = lax.optimization_barrier((d_out, give))
     given = exchange(give, 1)
-    along = send_cotangents(d_out)
+    (own, *rest), own_swapped = send_cotangents(d_out)
+    own_y = exchange(own, 1)
     (tok_out,) = call(
         pack_kernel,
         [shape((n, 3 * rows, HD), BF16)],
@@ -352,9 +359,9 @@
         moved=4 * 3 * rows * width,
         limit=big,
     )
-    tok_out, along[1] = lax.optimization_barrier((tok_out, along[1]))
-    along, given = lax.optimization_barrier((along, given))
-    pieces = gather_cotangents(along)
+    tok_out, rest[0] = lax.optimization_barrier((tok_out, rest[0]))
+    rest, given = lax.optimization_barrier((rest, given))
+    pieces, kinds = gather_cotangents(own, own_swapped, own_y, rest)
     tok_in = lax.all_to_all(tok_out, "seq", split_axis=0, concat_axis=0, tiled=True)
 
     probs, out_t, queries, keys_t, vals = call(
@@ -366,24 +373,28 @@
         moved=4 * total * image,
     )
     columns = pieces[0].shape[1]
-    mine, far, near, near_far, cot = call(
-        partial_kernel,
-        [shape((image, HD), F32)] * 2 + [shape((image, HD), BF16)] * 2 + [shape((image, columns), BF16)],
+    mine, *far, near, send0, send1, cot = call(
+        functools.partial(partial_kernel, kinds=kinds),
+        [shape((image, HD), F32)]
+        + [shape((image // 2, HD), F32)] * 2
+        + [shape((image, HD), BF16)]
+        + [shape((image // 2, HD), BF16)] * 2
+        + [shape((image, columns), BF16)],
         [*pieces, keep, given],
         scratch=[pltpu.VMEM((columns, 4 * HD), BF16)],
         flops=8 * image * columns * HD,
         moved=2 * image * columns,
     )
-    near_far = exchange(near_far, 2)
+    near_far = [exchange(send0, 2), exchange(send1, 2)]
     near_far, out_t, near = lax.optimization_barrier((near_far, out_t, near))
-    far = exchange((far + near_far.astype(F32)).astype(BF16), 4)
+    far = [exchange((f + r.astype(F32)).astype(BF16), 4) for f, r in zip(far, near_far)]
     near = exchange(near, 2)
     out_late, far, near = lax.optimization_barrier((out_t, far, near))
     out_near, out_far = exchange(out_late, 2), exchange(out_late, 4)
     (grad_out,) = call(
         functools.partial(backward_kernel, chunk=chunk),
         [shape((n, 3 * rows, HD), BF16)],
-        [queries, keys_t, vals, probs, out_t, mine, near, far],
+        [queries, keys_t, vals, probs, out_t, mine, near, *far],
         scratch=[pltpu.VMEM((image, HD), F32), pltpu.VMEM((image, HD), F32)],
         flops=8 * total * image * HD,
         moved=4 * total * image,
@@ -396,7 +407,7 @@
         [shape((4 * HD, depth), BF16)] * 2,
         [cot, *outs],
         scratch=[pltpu.VMEM((4 * HD, image), BF16)],
-        flops=96 * image * columns * HD,
+        flops=40 * image * columns * HD,
         moved=2 * image * columns,
     )
     grads = call(

time: 105 us -> 142 us (1.35)
  waiting for transfers between devices: 57.2 us -> 87.1 us
  starting transfers between devices: 24.8 us -> 32.8 us
    ppermute x14 -> x18, waiting for transfers between devices: 57.2 us -> 87.1 us  [exchange(): return lax.ppermute(array, ('seq', 'fsdp'), pairs)]
    ppermute x14 -> x18, starting transfers between devices: 16.5 us -> 23.6 us  [exchange(): return lax.ppermute(array, ('seq', 'fsdp'), pairs)]
  transfers between devices with their start and end apart: 16 -> 20, of which waited for: 10 -> 13; matrix products, arithmetic and copies ran while one was open for 0% -> 0% of each run, Pallas kernels for 15% -> 8%
where the time goes in v15:
time: 142 us
  waiting for transfers between devices  87.1 us (61%)
  starting transfers between devices  32.8 us (23%)
  Pallas kernels  19.6 us (14%)
    ppermute x18, waiting for transfers between devices, exchange(): return lax.ppermute(array, ('seq', 'fsdp'), pairs)  87.1 us
    ppermute x18, starting transfers between devices, exchange(): return lax.ppermute(array, ('seq', 'fsdp'), pairs)  23.6 us
    pallas_call x8, Pallas kernels, call(): pl.pallas_call(kernel, out_shape=outs, grid_spec=pltpu.PrefetchScalarGrid...  19.6 us
    all_to_all x1, starting transfers between devices, local(): lax.all_to_all(tok_out, 'seq', split_axis=0, concat_axis=0, tiled=True)  5.21 us
    all_to_all x1, starting transfers between devices, local(): lax.all_to_all(grad_out, 'seq', split_axis=0, concat_axis=0, tiled=True)  4.02 us
  transfers between devices with their start and end apart: 20, of which 13 were waited for; matrix products, arithmetic and copies ran while one was open for 0% of the time, Pallas kernels for 8%

profile of v15, /device:TPU:0, one launch (start us, length us, event | category | flops | bytes accessed | tf_op | source)
XLA Modules:
  0.0 141.6 jit_solution(14237420100810011847)
XLA Ops:
  0.7 2.3 %shard_map.103 = (bf16[384,512]{1,0:T(8,128)(2,1)}, bf16[384,512]{1,0:T(8,128)(2,1)}, bf16[2,512,128]{2,1,0:T(8,128)(2,1)}) custom-call(s32[1]{0:T(128)} %bitcast.me_ref, bf16[384,1024]{1,0:T(8,128)(2,1)} %w_ref.1, bf16[512,1024]{1,0:T(8,128)(2,1)} %kt_ref.1, bf16[512,1024]{1,0:T(8,128)(2,1)} %vt_ref.1), custom_call_target="tpu_custom_call" | custom-call | bytes 1572864 | tf_op jit(solution)/shard_map/pallas_call | solution.py:147
  3.1 0.0 copy-start
  3.1 3.1 %collective-permute-start = (bf16[64,768]{1,0:T(8,128)(2,1)S(1)}, bf16[64,768]{1,0:T(8,128)(2,1)S(1)}, u32[]{:S(2)}, u32[]{:S(2)}) collective-permute-start(bf16[64,768]{1,0:T(8,128)(2,1)S(1)} %get-tuple-element.84), channel_id=1, source_target_pairs={{0,4},{1,5},{2,6},{3,7},{4,0},{5,1},{6,2},{7,3},{8,12},{9,13},{10,... | collective-permute-start | bytes 294920 | tf_op jit(solution)/shard_map/ppermute | solution.py:303
  6.2 1.5 %collective-permute-start.4 = (bf16[384,512]{1,0:T(8,128)(2,1)}, bf16[384,512]{1,0:T(8,128)(2,1)S(1)}, u32[]{:S(2)}, u32[]{:S(2)}) collective-permute-start(bf16[384,512]{1,0:T(8,128)(2,1)} %get-tuple-element.51), channel_id=1, source_target_pairs={{0,2},{1,3},{2,0},{3,1},{4,6},{5,7},{6,4},{7,5},{8,10},{9,11},{10,... | collective-permute-start | bytes 1179656 | tf_op jit(solution)/shard_map/ppermute | solution.py:303
  7.7 2.1 %shard_map.102 = bf16[8,384,128]{2,1,0:T(8,128)(2,1)} custom-call(bf16[128,1024]{1,0:T(8,128)(2,1)} %q_ref.1, bf16[128,1024]{1,0:T(8,128)(2,1)} %k_ref.1, bf16[128,1024]{1,0:T(8,128)(2,1)} %v_ref.1), custom_call_target="tpu_custom_call" | custom-call | bytes 1572864 | tf_op jit(solution)/shard_map/pallas_call | solution.py:147
  9.8 0.0 collective-permute-done
  9.8 5.2 %all-to-all-start = ((bf16[8,384,128]{2,1,0:T(8,128)(2,1)}), bf16[8,384,128]{2,1,0:T(8,128)(2,1)S(1)}, u32[]{:S(2)}, u32[]{:S(2)}) async-start(bf16[8,384,128]{2,1,0:T(8,128)(2,1)} %shard_map.102), calls=%async_computation | async-start | bytes 1572864 | tf_op jit(solution)/shard_map/all_to_all | solution.py:365
  15.0 3.8 %collective-permute-start.3 = (bf16[64,768]{1,0:T(8,128)(2,1)S(1)}, bf16[64,768]{1,0:T(8,128)(2,1)S(1)}, u32[]{:S(2)}, u32[]{:S(2)}) collective-permute-start(bf16[64,768]{1,0:T(8,128)(2,1)S(1)} %get-tuple-element.80), channel_id=1, source_target_pairs={{0,12},{1,13},{2,14},{3,15},{4,8},{5,9},{6,10},{7,11},{8,4},{9,5},... | collective-permute-start | bytes 294920 | tf_op jit(solution)/shard_map/ppermute | solution.py:303
  18.9 0.0 collective-permute-start.2
  18.9 15.2 %collective-permute-done.3 = bf16[64,768]{1,0:T(8,128)(2,1)S(1)} collective-permute-done((bf16[64,768]{1,0:T(8,128)(2,1)S(1)}, bf16[64,768]{1,0:T(8,128)(2,1)S(1)}, u32[]{:S(2)}, u32[]{:S(2)}) %collective-permute-start.3) | collective-permute-done | bytes 98336 | tf_op jit(solution)/shard_map/ppermute | solution.py:303
  34.1 8.5 %collective-permute-done.2 = bf16[64,768]{1,0:T(8,128)(2,1)S(1)} collective-permute-done((bf16[64,768]{1,0:T(8,128)(2,1)S(1)}, bf16[64,768]{1,0:T(8,128)(2,1)S(1)}, u32[]{:S(2)}, u32[]{:S(2)}) %collective-permute-start.2) | collective-permute-done | bytes 98336 | tf_op jit(solution)/shard_map/ppermute | solution.py:303
  42.6 0.0 collective-permute-done.4.refs_9_
  42.6 0.0 copy-start.1
  42.6 1.4 collective-permute-start.5
  44.0 0.0 collective-permute-start.7
  44.0 5.6 %collective-permute-done.5.refs_4_ = bf16[192,768]{1,0:T(8,128)(2,1)S(1)} collective-permute-done((bf16[192,768]{1,0:T(8,128)(2,1)S(1)}, bf16[192,768]{1,0:T(8,128)(2,1)S(1)}, u32[]{:S(2)}, u32[]{:S(2)}) %collective-permute-start.5) | collective-permute-done | bytes 294944 | tf_op jit(solution)/shard_map/ppermute | solution.py:303
  49.6 0.0 collective-permute-start.8
  49.6 1.6 %collective-permute-start.1 = (bf16[64,768]{1,0:T(8,128)(2,1)S(1)}, bf16[64,768]{1,0:T(8,128)(2,1)S(1)}, u32[]{:S(2)}, u32[]{:S(2)}) collective-permute-start(bf16[64,768]{1,0:T(8,128)(2,1)S(1)} %get-tuple-element.83.refs_0_), channel_id=1, source_target_pairs={{0,2},{1,3},{2,0},{3,1},{4,6},{5,7},{6,4},{7,5},{8,10},{9,11},{10,... | collective-permute-start | bytes 294920 | tf_op jit(solution)/shard_map/ppermute | solution.py:303
  51.2 3.6 %collective-permute-done.1.refs_2_ = bf16[64,768]{1,0:T(8,128)(2,1)S(1)} collective-permute-done((bf16[64,768]{1,0:T(8,128)(2,1)S(1)}, bf16[64,768]{1,0:T(8,128)(2,1)S(1)}, u32[]{:S(2)}, u32[]{:S(2)}) %collective-permute-start.1) | collective-permute-done | bytes 98336 | tf_op jit(solution)/shard_map/ppermute | solution.py:303
  54.8 0.0 collective-permute-start.6
  54.8 1.3 collective-permute-done.6.refs_5_
  56.1 0.0 collective-permute-done.8.refs_7_
  56.1 2.0 %shard_map.105 = (f32[1024,128]{1,0:T(8,128)S(1)}, f32[512,128]{1,0:T(8,128)S(1)}, f32[512,128]{1,0:T(8,128)S(1)}, bf16[1024,128]{1,0:T(8,128)(2,1)S(1)}, bf16[5...) custom-call(bf16[64,768]{1,0:T(8,128)(2,1)S(1)} %get-tuple-element.83.refs_0_, ...), custom_call_target="tpu_custom_call" | custom-call | flops 805306368 | bytes 1572864 | tf_op jit(solution)/shard_map/pallas_call | solution.py:147
  58.1 1.1 copy-done.2
  59.2 0.0 collective-permute-start.9
  59.2 2.0 %collective-permute-start.10 = (bf16[512,128]{1,0:T(8,128)(2,1)S(1)}, bf16[512,128]{1,0:T(8,128)(2,1)S(1)}, u32[]{:S(2)}, u32[]{:S(2)}) collective-permute-start(bf16[512,128]{1,0:T(8,128)(2,1)S(1)} %get-tuple-element.58), channel_id=1, source_target_pairs={{0,4},{1,5},{2,6},{3,7},{4,0},{5,1},{6,2},{7,3},{8,12},{9,13},{10,... | collective-permute-start | bytes 393224 | tf_op jit(solution)/shard_map/ppermute | solution.py:303
  61.3 4.9 %shard_map.104 = (bf16[1536,1024]{1,0:T(8,128)(2,1)S(1)}, bf16[128,1024]{1,0:T(8,128)(2,1)S(1)}, bf16[1024,128]{1,0:T(8,128)(2,1)S(1)}, bf16[128,1536]{1,0:T(8,128)(2,1)S(1)}, bf16[1536,128]{1,0:T(8,128)(2,1)S(1)}) custom-call(bf16[8,384,128]{2,1,0:T(8,128)(2,1)S(1)} %all-to-all-done.tok_ref, bf16[2,512,128]{2,1,0:T(8,128)(2,1)S(1)} %copy-done.1), custom_call_target="tpu_custom_call" | custom-call | flops 805306368 | bytes 6291456 | tf_op jit(solution)/shard_map/pallas_call | solution.py:147
  66.2 0.0 collective-permute-done.9
  66.2 1.6 %collective-permute-done.10 = bf16[512,128]{1,0:T(8,128)(2,1)S(1)} collective-permute-done((bf16[512,128]{1,0:T(8,128)(2,1)S(1)}, bf16[512,128]{1,0:T(8,128)(2,1)S(1)}, u32[]{:S(2)}, u32[]{:S(2)}) %collective-permute-start.10) | collective-permute-done | bytes 131104 | tf_op jit(solution)/shard_map/ppermute | solution.py:303
  67.8 1.6 %collective-permute-start.11 = (bf16[512,128]{1,0:T(8,128)(2,1)S(1)}, bf16[512,128]{1,0:T(8,128)(2,1)S(1)}, u32[]{:S(2)}, u32[]{:S(2)}) collective-permute-start(bf16[512,128]{1,0:T(8,128)(2,1)S(1)} %add_convert_fusion.1), channel_id=1, source_target_pairs={{0,8},{1,9},{2,10},{3,11},{4,12},{5,13},{6,14},{7,15},{8,0},{9,1},... | collective-permute-start | bytes 393224 | tf_op jit(solution)/shard_map/ppermute | solution.py:303
  69.5 1.7 %collective-permute-start.13 = (bf16[1024,128]{1,0:T(8,128)(2,1)S(1)}, bf16[1024,128]{1,0:T(8,128)(2,1)S(1)}, u32[]{:S(2)}, u32[]{:S(2)}) collective-permute-start(bf16[1024,128]{1,0:T(8,128)(2,1)S(1)} %get-tuple-element.67), channel_id=1, source_target_pairs={{0,4},{1,5},{2,6},{3,7},{4,0},{5,1},{6,2},{7,3},{8,12},{9,13},{10,... | collective-permute-start | bytes 786440 | tf_op jit(solution)/shard_map/ppermute | solution.py:303
  71.2 0.1 collective-permute-start.12
  71.4 5.2 %collective-permute-done.11.far0_ref = bf16[512,128]{1,0:T(8,128)(2,1)S(1)} collective-permute-done((bf16[512,128]{1,0:T(8,128)(2,1)S(1)}, bf16[512,128]{1,0:T(8,128)(2,1)S(1)}, u32[]{:S(2)}, u32[]{:S(2)}) %collective-permute-start.11) | collective-permute-done | bytes 131104 | tf_op jit(solution)/shard_map/ppermute | solution.py:303
  76.6 3.9 %collective-permute-done.12.far1_ref = bf16[512,128]{1,0:T(8,128)(2,1)S(1)} collective-permute-done((bf16[512,128]{1,0:T(8,128)(2,1)S(1)}, bf16[512,128]{1,0:T(8,128)(2,1)S(1)}, u32[]{:S(2)}, u32[]{:S(2)}) %collective-permute-start.12) | collective-permute-done | bytes 131104 | tf_op jit(solution)/shard_map/ppermute | solution.py:303
  80.5 2.0 %collective-permute-done.13.near_ref = bf16[1024,128]{1,0:T(8,128)(2,1)S(1)} collective-permute-done((bf16[1024,128]{1,0:T(8,128)(2,1)S(1)}, bf16[1024,128]{1,0:T(8,128)(2,1)S(1)}, u32[]{:S(2)}, u32[]{:S(2)}) %collective-permute-start.13) | collective-permute-done | bytes 262176 | tf_op jit(solution)/shard_map/ppermute | solution.py:303
  82.4 4.5 %shard_map.106 = bf16[8,384,128]{2,1,0:T(8,128)(2,1)} custom-call(bf16[1024,128]{1,0:T(8,128)(2,1)S(1)} %get-tuple-element.46.queries_ref, bf16[128,1536]{1,0:T(8,128)(2,1)S(1)} %get-tuple-element.47.keys_t_ref, bf16[1536,128]{1,0:T(8,128)(2,1)S(1)} %get-tuple-element.48.vals_ref, bf16[1536,1024]{1,0:T(8,128)(2,1)S(1)} %get-tuple-element.49.probs_ref, ...), custom_call_target="tpu_custom_call" | custom-call | flops 1610612736 | bytes 6291456 | tf_op jit(solution)/shard_map/pallas_call | solution.py:147
  86.9 4.0 %all-to-all-start.1 = ((bf16[8,384,128]{2,1,0:T(8,128)(2,1)}), bf16[8,384,128]{2,1,0:T(8,128)(2,1)S(1)}, u32[]{:S(2)}, u32[]{:S(2)}) async-start(bf16[8,384,128]{2,1,0:T(8,128)(2,1)} %shard_map.106), calls=%async_computation.1 | async-start | bytes 1572864 | tf_op jit(solution)/shard_map/all_to_all | solution.py:402
  90.9 2.0 %collective-permute-start.15 = (bf16[128,1024]{1,0:T(8,128)(2,1)S(1)}, bf16[128,1024]{1,0:T(8,128)(2,1)S(1)}, u32[]{:S(2)}, u32[]{:S(2)}) collective-permute-start(bf16[128,1024]{1,0:T(8,128)(2,1)S(1)} %get-tuple-element.75.out_ref.refs_0_), channel_id=1, source_target_pairs={{0,4},{1,5},{2,6},{3,7},{4,0},{5,1},{6,2},{7,3},{8,12},{9,13},{10,... | collective-permute-start | bytes 786440 | tf_op jit(solution)/shard_map/ppermute | solution.py:303
  93.0 2.4 %collective-permute-start.14 = (bf16[128,1024]{1,0:T(8,128)(2,1)S(1)}, bf16[128,1024]{1,0:T(8,128)(2,1)S(1)}, u32[]{:S(2)}, u32[]{:S(2)}) collective-permute-start(bf16[128,1024]{1,0:T(8,128)(2,1)S(1)} %get-tuple-element.75.out_ref.refs_0_), channel_id=1, source_target_pairs={{0,8},{1,9},{2,10},{3,11},{4,12},{5,13},{6,14},{7,15},{8,0},{9,1},... | collective-permute-start | bytes 786440 | tf_op jit(solution)/shard_map/ppermute | solution.py:303
  95.3 16.3 %collective-permute-done.15.refs_1_ = bf16[128,1024]{1,0:T(8,128)(2,1)S(1)} collective-permute-done((bf16[128,1024]{1,0:T(8,128)(2,1)S(1)}, bf16[128,1024]{1,0:T(8,128)(2,1)S(1)}, u32[]{:S(2)}, u32[]{:S(2)}) %collective-permute-start.15) | collective-permute-done | bytes 262176 | tf_op jit(solution)/shard_map/ppermute | solution.py:303
  111.6 10.1 %collective-permute-done.14.refs_2_ = bf16[128,1024]{1,0:T(8,128)(2,1)S(1)} collective-permute-done((bf16[128,1024]{1,0:T(8,128)(2,1)S(1)}, bf16[128,1024]{1,0:T(8,128)(2,1)S(1)}, u32[]{:S(2)}, u32[]{:S(2)}) %collective-permute-start.14) | collective-permute-done | bytes 262176 | tf_op jit(solution)/shard_map/ppermute | solution.py:303
  121.8 0.0 collective-permute-start.16
  121.8 6.4 %collective-permute-done.16.refs_3_ = bf16[128,1024]{1,0:T(8,128)(2,1)S(1)} collective-permute-done((bf16[128,1024]{1,0:T(8,128)(2,1)S(1)}, bf16[128,1024]{1,0:T(8,128)(2,1)S(1)}, u32[]{:S(2)}, u32[]{:S(2)}) %collective-permute-start.16) | collective-permute-done | bytes 262176 | tf_op jit(solution)/shard_map/ppermute | solution.py:303
  128.1 1.3 shard_map.108
  129.4 2.3 %collective-permute-start.17 = (bf16[512,384]{1,0:T(8,128)(2,1)S(1)}, bf16[512,384]{1,0:T(8,128)(2,1)S(1)}, u32[]{:S(2)}, u32[]{:S(2)}) collective-permute-start(bf16[512,384]{1,0:T(8,128)(2,1)S(1)} %get-tuple-element.79), channel_id=1, source_target_pairs={{0,2},{1,3},{2,0},{3,1},{4,6},{5,7},{6,4},{7,5},{8,10},{9,11},{10,... | collective-permute-start | bytes 1179656 | tf_op jit(solution)/shard_map/ppermute | solution.py:303
  131.6 7.4 %collective-permute-done.17.other_ref = bf16[512,384]{1,0:T(8,128)(2,1)S(1)} collective-permute-done((bf16[512,384]{1,0:T(8,128)(2,1)S(1)}, bf16[512,384]{1,0:T(8,128)(2,1)S(1)}, u32[]{:S(2)}, u32[]{:S(2)}) %collective-permute-start.17) | collective-permute-done | bytes 393248 | tf_op jit(solution)/shard_map/ppermute | solution.py:303
  139.0 1.5 %shard_map.109 = f32[384,1024]{1,0:T(8,128)} custom-call(bf16[512,384]{1,0:T(8,128)(2,1)S(1)} %get-tuple-element.78.own_ref, bf16[512,384]{1,0:T(8,128)(2,1)S(1)} %collective-permute-done.17.other_ref), custom_call_target="tpu_custom_call" | custom-call | bytes 2359296 | tf_op jit(solution)/shard_map/pallas_call | solution.py:147
  140.5 1.1 shard_map.107
  (16 shorter events, 0.1 us)
Async XLA Ops:
  0.6 2.4 %copy-start.4 = (bf16[128,3072]{1,0:T(8,128)(2,1)S(1)}, bf16[128,3072]{1,0:T(8,128)(2,1)}, u32[]{:S(2)}) copy-start(bf16[128,3072]{1,0:T(8,128)(2,1)} %param.13) | copy-start | bytes 2359300
  3.1 53.0 %copy-start = (bf16[384,512]{1,0:T(8,128)(2,1)S(1)}, bf16[384,512]{1,0:T(8,128)(2,1)}, u32[]{:S(2)}) copy-start(bf16[384,512]{1,0:T(8,128)(2,1)} %get-tuple-element.55.refs_8_) | copy-start | bytes 1179652
  3.1 6.8 %collective-permute-start = (bf16[64,768]{1,0:T(8,128)(2,1)S(1)}, bf16[64,768]{1,0:T(8,128)(2,1)S(1)}, u32[]{:S(2)}, u32[]{:S(2)}) collective-permute-start(bf16[64,768]{1,0:T(8,128)(2,1)S(1)} %get-tuple-element.84), channel_id=1, source_target_pairs={{0,4},{1,5},{2,6},{3,7},{4,0},{5,1},{6,2},{7,3},{8,12},{9,13},{10,... | collective-permute-start | bytes 294920 | tf_op jit(solution)/shard_map/ppermute | solution.py:303
  6.2 36.4 %collective-permute-start.4 = (bf16[384,512]{1,0:T(8,128)(2,1)}, bf16[384,512]{1,0:T(8,128)(2,1)S(1)}, u32[]{:S(2)}, u32[]{:S(2)}) collective-permute-start(bf16[384,512]{1,0:T(8,128)(2,1)} %get-tuple-element.51), channel_id=1, source_target_pairs={{0,2},{1,3},{2,0},{3,1},{4,6},{5,7},{6,4},{7,5},{8,10},{9,11},{10,... | collective-permute-start | bytes 1179656 | tf_op jit(solution)/shard_map/ppermute | solution.py:303
  9.8 51.4 %all-to-all-start = ((bf16[8,384,128]{2,1,0:T(8,128)(2,1)}), bf16[8,384,128]{2,1,0:T(8,128)(2,1)S(1)}, u32[]{:S(2)}, u32[]{:S(2)}) async-start(bf16[8,384,128]{2,1,0:T(8,128)(2,1)} %shard_map.102), calls=%async_computation | async-start | bytes 1572864 | tf_op jit(solution)/shard_map/all_to_all | solution.py:365
  15.0 19.0 %collective-permute-start.3 = (bf16[64,768]{1,0:T(8,128)(2,1)S(1)}, bf16[64,768]{1,0:T(8,128)(2,1)S(1)}, u32[]{:S(2)}, u32[]{:S(2)}) collective-permute-start(bf16[64,768]{1,0:T(8,128)(2,1)S(1)} %get-tuple-element.80), channel_id=1, source_target_pairs={{0,12},{1,13},{2,14},{3,15},{4,8},{5,9},{6,10},{7,11},{8,4},{9,5},... | collective-permute-start | bytes 294920 | tf_op jit(solution)/shard_map/ppermute | solution.py:303
  18.9 23.7 %collective-permute-start.2 = (bf16[64,768]{1,0:T(8,128)(2,1)S(1)}, bf16[64,768]{1,0:T(8,128)(2,1)S(1)}, u32[]{:S(2)}, u32[]{:S(2)}) collective-permute-start(bf16[64,768]{1,0:T(8,128)(2,1)S(1)} %get-tuple-element.81), channel_id=1, source_target_pairs={{0,8},{1,9},{2,10},{3,11},{4,12},{5,13},{6,14},{7,15},{8,0},{9,1},... | collective-permute-start | bytes 294920 | tf_op jit(solution)/shard_map/ppermute | solution.py:303
  42.6 18.7 %copy-start.1 = (bf16[2,512,128]{2,1,0:T(8,128)(2,1)S(1)}, bf16[2,512,128]{2,1,0:T(8,128)(2,1)}, u32[]{:S(2)}) copy-start(bf16[2,512,128]{2,1,0:T(8,128)(2,1)} %get-tuple-element.45.text_ref) | copy-start | bytes 786436
  42.6 7.0 %collective-permute-start.5 = (bf16[192,768]{1,0:T(8,128)(2,1)S(1)}, bf16[192,768]{1,0:T(8,128)(2,1)S(1)}, u32[]{:S(2)}, u32[]{:S(2)}) collective-permute-start(bf16[192,768]{1,0:T(8,128)(2,1)S(1)} %constant_dynamic-update-slice_fusion.refs_3_), channel_id=1, source_target_pairs={{0,2},{1,3},{2,0},{3,1},{4,6},{5,7},{6,4},{7,5},{8,10},{9,11},{10,... | collective-permute-start | bytes 884744 | tf_op jit(solution)/shard_map/ppermute | solution.py:303
  44.0 12.1 %collective-permute-start.7 = (bf16[192,768]{1,0:T(8,128)(2,1)S(1)}, bf16[192,768]{1,0:T(8,128)(2,1)S(1)}, u32[]{:S(2)}, u32[]{:S(2)}) collective-permute-start(bf16[192,768]{1,0:T(8,128)(2,1)S(1)} %constant_dynamic-update-slice_fusion.refs_3_), channel_id=1, source_target_pairs={{0,1},{1,0},{2,3},{3,2},{4,5},{5,4},{6,7},{7,6},{8,9},{9,8},{10,11... | collective-permute-start | bytes 884744 | tf_op jit(solution)/shard_map/ppermute | solution.py:303
  49.6 6.5 %collective-permute-start.8 = (bf16[192,768]{1,0:T(8,128)(2,1)S(1)}, bf16[192,768]{1,0:T(8,128)(2,1)S(1)}, u32[]{:S(2)}, u32[]{:S(2)}) collective-permute-start(bf16[192,768]{1,0:T(8,128)(2,1)S(1)} %collective-permute-done.5.refs_4_), channel_id=1, source_target_pairs={{0,1},{1,0},{2,3},{3,2},{4,5},{5,4},{6,7},{7,6},{8,9},{9,8},{10,11... | collective-permute-start | bytes 884744 | tf_op jit(solution)/shard_map/ppermute | solution.py:303
  49.6 5.2 %collective-permute-start.1 = (bf16[64,768]{1,0:T(8,128)(2,1)S(1)}, bf16[64,768]{1,0:T(8,128)(2,1)S(1)}, u32[]{:S(2)}, u32[]{:S(2)}) collective-permute-start(bf16[64,768]{1,0:T(8,128)(2,1)S(1)} %get-tuple-element.83.refs_0_), channel_id=1, source_target_pairs={{0,2},{1,3},{2,0},{3,1},{4,6},{5,7},{6,4},{7,5},{8,10},{9,11},{10,... | collective-permute-start | bytes 294920 | tf_op jit(solution)/shard_map/ppermute | solution.py:303
  54.8 1.3 collective-permute-start.6
  58.1 1.1 copy-start.2
  59.2 6.9 %collective-permute-start.9 = (bf16[512,128]{1,0:T(8,128)(2,1)}, bf16[512,128]{1,0:T(8,128)(2,1)S(1)}, u32[]{:S(2)}, u32[]{:S(2)}) collective-permute-start(bf16[512,128]{1,0:T(8,128)(2,1)} %get-tuple-element.57), channel_id=1, source_target_pairs={{0,4},{1,5},{2,6},{3,7},{4,0},{5,1},{6,2},{7,3},{8,12},{9,13},{10,... | collective-permute-start | bytes 393224 | tf_op jit(solution)/shard_map/ppermute | solution.py:303
  59.2 8.6 %collective-permute-start.10 = (bf16[512,128]{1,0:T(8,128)(2,1)S(1)}, bf16[512,128]{1,0:T(8,128)(2,1)S(1)}, u32[]{:S(2)}, u32[]{:S(2)}) collective-permute-start(bf16[512,128]{1,0:T(8,128)(2,1)S(1)} %get-tuple-element.58), channel_id=1, source_target_pairs={{0,4},{1,5},{2,6},{3,7},{4,0},{5,1},{6,2},{7,3},{8,12},{9,13},{10,... | collective-permute-start | bytes 393224 | tf_op jit(solution)/shard_map/ppermute | solution.py:303
  67.8 8.8 %collective-permute-start.11 = (bf16[512,128]{1,0:T(8,128)(2,1)S(1)}, bf16[512,128]{1,0:T(8,128)(2,1)S(1)}, u32[]{:S(2)}, u32[]{:S(2)}) collective-permute-start(bf16[512,128]{1,0:T(8,128)(2,1)S(1)} %add_convert_fusion.1), channel_id=1, source_target_pairs={{0,8},{1,9},{2,10},{3,11},{4,12},{5,13},{6,14},{7,15},{8,0},{9,1},... | collective-permute-start | bytes 393224 | tf_op jit(solution)/shard_map/ppermute | solution.py:303
  69.5 13.0 %collective-permute-start.13 = (bf16[1024,128]{1,0:T(8,128)(2,1)S(1)}, bf16[1024,128]{1,0:T(8,128)(2,1)S(1)}, u32[]{:S(2)}, u32[]{:S(2)}) collective-permute-start(bf16[1024,128]{1,0:T(8,128)(2,1)S(1)} %get-tuple-element.67), channel_id=1, source_target_pairs={{0,4},{1,5},{2,6},{3,7},{4,0},{5,1},{6,2},{7,3},{8,12},{9,13},{10,... | collective-permute-start | bytes 786440 | tf_op jit(solution)/shard_map/ppermute | solution.py:303
  71.2 9.3 %collective-permute-start.12 = (bf16[512,128]{1,0:T(8,128)(2,1)S(1)}, bf16[512,128]{1,0:T(8,128)(2,1)S(1)}, u32[]{:S(2)}, u32[]{:S(2)}) collective-permute-start(bf16[512,128]{1,0:T(8,128)(2,1)S(1)} %add_convert_fusion), channel_id=1, source_target_pairs={{0,8},{1,9},{2,10},{3,11},{4,12},{5,13},{6,14},{7,15},{8,0},{9,1},... | collective-permute-start | bytes 393224 | tf_op jit(solution)/shard_map/ppermute | solution.py:303
  86.9 41.2 %copy-start.3 = (bf16[1024,768]{1,0:T(8,128)(2,1)S(1)}, bf16[1024,768]{1,0:T(8,128)(2,1)}, u32[]{:S(2)}) copy-start(bf16[1024,768]{1,0:T(8,128)(2,1)} %copy-done.2) | copy-start | bytes 4718596
  86.9 53.6 %all-to-all-start.1 = ((bf16[8,384,128]{2,1,0:T(8,128)(2,1)}), bf16[8,384,128]{2,1,0:T(8,128)(2,1)S(1)}, u32[]{:S(2)}, u32[]{:S(2)}) async-start(bf16[8,384,128]{2,1,0:T(8,128)(2,1)} %shard_map.106), calls=%async_computation.1 | async-start | bytes 1572864 | tf_op jit(solution)/shard_map/all_to_all | solution.py:402
  90.9 20.7 %collective-permute-start.15 = (bf16[128,1024]{1,0:T(8,128)(2,1)S(1)}, bf16[128,1024]{1,0:T(8,128)(2,1)S(1)}, u32[]{:S(2)}, u32[]{:S(2)}) collective-permute-start(bf16[128,1024]{1,0:T(8,128)(2,1)S(1)} %get-tuple-element.75.out_ref.refs_0_), channel_id=1, source_target_pairs={{0,4},{1,5},{2,6},{3,7},{4,0},{5,1},{6,2},{7,3},{8,12},{9,13},{10,... | collective-permute-start | bytes 786440 | tf_op jit(solution)/shard_map/ppermute | solution.py:303
  93.0 28.8 %collective-permute-start.14 = (bf16[128,1024]{1,0:T(8,128)(2,1)S(1)}, bf16[128,1024]{1,0:T(8,128)(2,1)S(1)}, u32[]{:S(2)}, u32[]{:S(2)}) collective-permute-start(bf16[128,1024]{1,0:T(8,128)(2,1)S(1)} %get-tuple-element.75.out_ref.refs_0_), channel_id=1, source_target_pairs={{0,8},{1,9},{2,10},{3,11},{4,12},{5,13},{6,14},{7,15},{8,0},{9,1},... | collective-permute-start | bytes 786440 | tf_op jit(solution)/shard_map/ppermute | solution.py:303
  121.8 6.4 %collective-permute-start.16 = (bf16[128,1024]{1,0:T(8,128)(2,1)S(1)}, bf16[128,1024]{1,0:T(8,128)(2,1)S(1)}, u32[]{:S(2)}, u32[]{:S(2)}) collective-permute-start(bf16[128,1024]{1,0:T(8,128)(2,1)S(1)} %collective-permute-done.14.refs_2_), channel_id=1, source_target_pairs={{0,4},{1,5},{2,6},{3,7},{4,0},{5,1},{6,2},{7,3},{8,12},{9,13},{10,... | collective-permute-start | bytes 786440 | tf_op jit(solution)/shard_map/ppermute | solution.py:303
  129.4 9.6 %collective-permute-start.17 = (bf16[512,384]{1,0:T(8,128)(2,1)S(1)}, bf16[512,384]{1,0:T(8,128)(2,1)S(1)}, u32[]{:S(2)}, u32[]{:S(2)}) collective-permute-start(bf16[512,384]{1,0:T(8,128)(2,1)S(1)} %get-tuple-element.79), channel_id=1, source_target_pairs={{0,2},{1,3},{2,0},{3,1},{4,6},{5,7},{6,4},{7,5},{8,10},{9,11},{10,... | collective-permute-start | bytes 1179656 | tf_op jit(solution)/shard_map/ppermute | solution.py:303

commit v16 on v14

--- a/solution.py
+++ b/solution.py
@@ -182,12 +182,18 @@
     text_ref[1] = vt_ref[...]
 
 
+def query_order(n):
+    y = lax.rem(lax.axis_index("seq"), 2)
+    return [2 * z + y for z in range(n // 2)] + [2 * z + 1 - y for z in range(n // 2)]
+
+
 def forward_kernel(tok_ref, text_ref, probs_ref, out_ref, queries_ref, keys_t_ref, vals_ref, keys, vals_t, *, chunk):
     n, three, _ = tok_ref.shape
     rows = three // 3
     image = n * rows
     text = text_ref.shape[1]
-    queries_ref[...] = tok_ref[:, 0:rows, :].reshape(image, HD)
+    for i, source in enumerate(query_order(n)):
+        queries_ref[i * rows : (i + 1) * rows, :] = tok_ref[source, 0:rows, :]
     keys[0:image, :] = tok_ref[:, rows : 2 * rows, :].reshape(image, HD)
     keys[image : image + text, :] = text_ref[0]
     vals_ref[0:image, :] = tok_ref[:, 2 * rows : 3 * rows, :].reshape(image, HD)
@@ -206,17 +212,15 @@
         out_ref[:, span] = jnp.dot(vals_t[...], low, preferred_element_type=F32).astype(BF16)
 
 
-def partial_kernel(*refs):
-    *pieces, own_ref, other_ref, mine_ref, far_ref, near_ref, near_far_ref, cot_ref, weight = refs
+def partial_kernel(piece_ref, swapped_ref, own_ref, other_ref, *refs):
+    mine_ref, far_ref, near_ref, send_ref, cot_ref, weight = refs
     me = lax.axis_index("seq")
     core = lax.axis_index("fsdp")
-    count = len(STEPS)
-    part = pieces[0].shape[0] // count
-    for p, piece in enumerate(pieces):
-        row, swapped = p % 2, p // 2
-        shift = jnp.bitwise_xor(core, swapped) * part
+    part = piece_ref.shape[0] // len(STEPS)
+    for piece, shift in ((piece_ref, core), (swapped_ref, 1 - core)):
         for i, step in enumerate(STEPS):
-            at = pl.multiple_of(jnp.bitwise_xor(me, step + row) * (2 * part) + shift, 16)
+            z = jnp.bitwise_xor(me, step) // 2
+            at = pl.multiple_of(z * (2 * part) + shift * part, 16)
             cot_ref[pl.ds(at, part), :] = piece[i * part : (i + 1) * part, :]
     depth = own_ref.shape[0]
     y = lax.rem(me, 2)
@@ -231,33 +235,37 @@
         mine_ref[at, :] = part[:, :HD]
         near_ref[at, :] = part[:, HD : 2 * HD].astype(BF16)
         far_ref[at, :] = part[:, 2 * HD : 3 * HD]
-        near_far_ref[at, :] = part[:, 3 * HD :].astype(BF16)
-
-
-def weight_grad_kernel(cot_ref, *refs):
+        send_ref[at, :] = part[:, 3 * HD :].astype(BF16)
+
+
+def weight_grad_kernel(cot0_ref, cot1_ref, *refs):
     *out_refs, own_ref, other_ref, outs = refs
-    first = 0
-    for ref in out_refs:
-        outs[first : first + ref.shape[0], :] = ref[...]
-        first += ref.shape[0]
+    for i, ref in enumerate(out_refs):
+        outs[i * HD : (i + 1) * HD, :] = ref[...]
     depth = own_ref.shape[1]
+    tokens = cot0_ref.shape[0]
     y = lax.rem(lax.axis_index("seq"), 2)
     for ref, row in ((own_ref, y), (other_ref, 1 - y)):
-        at = pl.multiple_of(row * depth, HD)
-        ref[...] = jnp.dot(outs[...], cot_ref[:, pl.ds(at, depth)], preferred_element_type=F32).astype(BF16)
-
-
-def backward_kernel(
-    queries_ref, keys_t_ref, vals_ref, probs_ref, out_ref, mine_ref, near_ref, far_ref, send_ref, dk, dv, *, chunk
-):
+        cols = pl.ds(pl.multiple_of(row * depth, HD), depth)
+        total = jnp.dot(outs[:, :tokens], cot0_ref[:, cols], preferred_element_type=F32)
+        total += jnp.dot(outs[:, tokens:], cot1_ref[:, cols], preferred_element_type=F32)
+        ref[...] = total.astype(BF16)
+
+
+def backward_kernel(queries_ref, keys_t_ref, vals_ref, probs_ref, out_ref, *refs, chunk):
+    *grad_refs, send_ref, dk, dv = refs
     n, three, _ = send_ref.shape
     rows = three // 3
     image = n * rows
     scale = HD ** (-0.5)
     per = chunk // rows
+    order = query_order(n)
+    half = image // chunk // 2
     for c in range(image // chunk):
         span = slice(c * chunk, (c + 1) * chunk)
-        grads = mine_ref[span, :] + near_ref[span, :].astype(F32) + far_ref[span, :].astype(F32)
+        within = slice(c % half * chunk, (c % half + 1) * chunk)
+        mine_ref, near_ref, far_ref = grad_refs[c // half :: 2]
+        grads = mine_ref[within, :] + near_ref[within, :].astype(F32) + far_ref[within, :].astype(F32)
         grads = grads.astype(BF16)
         row_dot = jnp.sum(
             grads.astype(F32).T * out_ref[:, span].astype(F32), axis=0, keepdims=True
@@ -265,8 +273,9 @@
         prob_grad = lax.dot_general(vals_ref[...], grads, NT, preferred_element_type=F32)
         low = probs_ref[:, span]
         score_grad = (low.astype(F32) * (prob_grad - row_dot)).astype(BF16)
-        dq_t = jnp.dot(keys_t_ref[...], score_grad, preferred_element_type=F32) * scale
-        send_ref[c * per : (c + 1) * per, 0:rows, :] = dq_t.T.astype(BF16).reshape(per, rows, HD)
+        dq = (jnp.dot(keys_t_ref[...], score_grad, preferred_element_type=F32) * scale).T.astype(BF16)
+        for i in range(per):
+            send_ref[order[c * per + i], 0:rows, :] = dq[i * rows : (i + 1) * rows, :]
         dk_part = jnp.dot(score_grad[0:image, :], queries_ref[span, :], preferred_element_type=F32)
         dv_part = jnp.dot(low[0:image, :], grads, preferred_element_type=F32)
         if c == 0:
@@ -309,12 +318,6 @@
         exchange(lax.dynamic_slice(d_out, (first, (z ^ (step // 2)) * columns), (part, columns)), step)
         for step in STEPS
     ]
-
-
-def gather_cotangents(along):
-    row = jnp.concatenate(along, axis=0)
-    pieces = [row, exchange(row, 1)]
-    return pieces + [exchange(piece, cores=True) for piece in pieces]
 
 
 def local(q_img, k_img, v_img, k_txt, v_txt, out_weight, d_out):
@@ -354,7 +357,10 @@
     )
     tok_out, along[1] = lax.optimization_barrier((tok_out, along[1]))
     along, given = lax.optimization_barrier((along, given))
-    pieces = gather_cotangents(along)
+    row = jnp.concatenate(along, axis=0)
+    row_swapped = exchange(row, cores=True)
+    other_row = exchange(row, 1)
+    other_swapped = exchange(other_row, cores=True)
     tok_in = lax.all_to_all(tok_out, "seq", split_axis=0, concat_axis=0, tiled=True)
 
     probs, out_t, queries, keys_t, vals = call(
@@ -365,25 +371,37 @@
         flops=4 * total * image * HD,
         moved=4 * total * image,
     )
-    columns = pieces[0].shape[1]
-    mine, far, near, near_far, cot = call(
-        partial_kernel,
-        [shape((image, HD), F32)] * 2 + [shape((image, HD), BF16)] * 2 + [shape((image, columns), BF16)],
-        [*pieces, keep, given],
-        scratch=[pltpu.VMEM((columns, 4 * HD), BF16)],
-        flops=8 * image * columns * HD,
-        moved=2 * image * columns,
-    )
-    near_far = exchange(near_far, 2)
-    near_far, out_t, near = lax.optimization_barrier((near_far, out_t, near))
-    far = exchange((far + near_far.astype(F32)).astype(BF16), 4)
-    near = exchange(near, 2)
-    out_late, far, near = lax.optimization_barrier((out_t, far, near))
+    columns = row.shape[1]
+
+    def partial(*operands):
+        return call(
+            partial_kernel,
+            [shape((image // 2, HD), F32)] * 2
+            + [shape((image // 2, HD), BF16)] * 2
+            + [shape((image // 2, columns), BF16)],
+            [*operands, keep, given],
+            scratch=[pltpu.VMEM((columns, 4 * HD), BF16)],
+            flops=4 * image * columns * HD,
+            moved=image * columns,
+        )
+
+    def add(kept, received):
+        return (kept + received.astype(F32)).astype(BF16)
+
+    mine0, kept0, near0, send0, cot0 = partial(row, row_swapped)
+    far0 = exchange(add(kept0, exchange(send0, 2)), 4)
+    near0 = exchange(near0, 2)
+    other_row, far0, near0 = lax.optimization_barrier((other_row, far0, near0))
+    mine1, kept1, near1, send1, cot1 = partial(other_row, other_swapped)
+    send1, out_t, near1 = lax.optimization_barrier((exchange(send1, 2), out_t, near1))
+    far1 = exchange(add(kept1, send1), 4)
+    near1 = exchange(near1, 2)
+    out_late, far1, near1 = lax.optimization_barrier((out_t, far1, near1))
     out_near, out_far = exchange(out_late, 2), exchange(out_late, 4)
     (grad_out,) = call(
         functools.partial(backward_kernel, chunk=chunk),
         [shape((n, 3 * rows, HD), BF16)],
-        [queries, keys_t, vals, probs, out_t, mine, near, far],
+        [queries, keys_t, vals, probs, out_t, mine0, mine1, near0, near1, far0, far1],
         scratch=[pltpu.VMEM((image, HD), F32), pltpu.VMEM((image, HD), F32)],
         flops=8 * total * image * HD,
         moved=4 * total * image,
@@ -394,7 +412,7 @@
     dw_own, dw_other = call(
         weight_grad_kernel,
         [shape((4 * HD, depth), BF16)] * 2,
-        [cot, *outs],
+        [cot0, cot1, *outs],
         scratch=[pltpu.VMEM((4 * HD, image), BF16)],
         flops=96 * image * columns * HD,
         moved=2 * image * columns,

time: 105 us -> 103 us (0.981)
  waiting for transfers between devices: 57.2 us -> 48.7 us
  starting transfers between devices: 24.8 us -> 30.8 us
    ppermute x14 -> x17, waiting for transfers between devices: 57.2 us -> 48.7 us  [exchange(): return lax.ppermute(array, ('seq', 'fsdp'), pairs)]
    ppermute x14 -> x17, starting transfers between devices: 16.5 us -> 22.8 us  [exchange(): return lax.ppermute(array, ('seq', 'fsdp'), pairs)]
    unnamed x13 -> x17, local copies, waits for them, and re-layouts: 2.58 us -> 2.99 us
    pallas_call x8 -> x9, Pallas kernels: 19.3 us -> 19.4 us  [call(): pl.pallas_call(kernel, out_shape=outs, grid_spec=pltpu.PrefetchScalarGrid...]
  transfers between devices with their start and end apart: 16 -> 19, of which waited for: 10 -> 10; matrix products, arithmetic and copies ran while one was open for 0% -> 0% of each run, Pallas kernels for 15% -> 16%
where the time goes in v16:
time: 103 us
  waiting for transfers between devices  48.7 us (47%)
  starting transfers between devices  30.8 us (30%)
  Pallas kernels  19.4 us (19%)
  local copies, waits for them, and re-layouts  3.03 us (3%)
    ppermute x17, waiting for transfers between devices, exchange(): return lax.ppermute(array, ('seq', 'fsdp'), pairs)  48.7 us
    ppermute x17, starting transfers between devices, exchange(): return lax.ppermute(array, ('seq', 'fsdp'), pairs)  22.8 us
    pallas_call x9, Pallas kernels, call(): pl.pallas_call(kernel, out_shape=outs, grid_spec=pltpu.PrefetchScalarGrid...  19.4 us
    all_to_all x1, starting transfers between devices, local(): lax.all_to_all(tok_out, 'seq', split_axis=0, concat_axis=0, tiled=True)  4.38 us
    all_to_all x1, starting transfers between devices, local(): lax.all_to_all(grad_out, 'seq', split_axis=0, concat_axis=0, tiled=True)  3.56 us
    unnamed x17, local copies, waits for them, and re-layouts  2.99 us
  transfers between devices with their start and end apart: 19, of which 10 were waited for; matrix products, arithmetic and copies ran while one was open for 0% of the time, Pallas kernels for 16%

profile of v16, /device:TPU:0, one launch (start us, length us, event | category | flops | bytes accessed | tf_op | source)
XLA Modules:
  0.0 102.8 jit_solution(9382475691665322503)
XLA Ops:
  0.6 2.3 %shard_map.103 = (bf16[384,512]{1,0:T(8,128)(2,1)}, bf16[384,512]{1,0:T(8,128)(2,1)}, bf16[2,512,128]{2,1,0:T(8,128)(2,1)}) custom-call(s32[1]{0:T(128)} %bitcast.me_ref, bf16[384,1024]{1,0:T(8,128)(2,1)} %w_ref.1, bf16[512,1024]{1,0:T(8,128)(2,1)} %kt_ref.1, bf16[512,1024]{1,0:T(8,128)(2,1)} %vt_ref.1), custom_call_target="tpu_custom_call" | custom-call | bytes 1572864 | tf_op jit(solution)/shard_map/pallas_call | solution.py:147
  3.0 3.0 %collective-permute-start.3 = (bf16[384,512]{1,0:T(8,128)(2,1)}, bf16[384,512]{1,0:T(8,128)(2,1)S(1)}, u32[]{:S(2)}, u32[]{:S(2)}) collective-permute-start(bf16[384,512]{1,0:T(8,128)(2,1)} %get-tuple-element.56), channel_id=1, source_target_pairs={{0,2},{1,3},{2,0},{3,1},{4,6},{5,7},{6,4},{7,5},{8,10},{9,11},{10,... | collective-permute-start | bytes 1179656 | tf_op jit(solution)/shard_map/ppermute | solution.py:309
  6.0 1.6 %collective-permute-start = (bf16[64,768]{1,0:T(8,128)(2,1)S(1)}, bf16[64,768]{1,0:T(8,128)(2,1)S(1)}, u32[]{:S(2)}, u32[]{:S(2)}) collective-permute-start(bf16[64,768]{1,0:T(8,128)(2,1)S(1)} %get-tuple-element.93), channel_id=1, source_target_pairs={{0,4},{1,5},{2,6},{3,7},{4,0},{5,1},{6,2},{7,3},{8,12},{9,13},{10,... | collective-permute-start | bytes 294920 | tf_op jit(solution)/shard_map/ppermute | solution.py:309
  7.7 2.5 %collective-permute-start.2 = (bf16[64,768]{1,0:T(8,128)(2,1)S(1)}, bf16[64,768]{1,0:T(8,128)(2,1)S(1)}, u32[]{:S(2)}, u32[]{:S(2)}) collective-permute-start(bf16[64,768]{1,0:T(8,128)(2,1)S(1)} %get-tuple-element.90), channel_id=1, source_target_pairs={{0,12},{1,13},{2,14},{3,15},{4,8},{5,9},{6,10},{7,11},{8,4},{9,5},... | collective-permute-start | bytes 294920 | tf_op jit(solution)/shard_map/ppermute | solution.py:309
  10.1 0.1 collective-permute-start.1
  10.2 2.1 %shard_map.102 = bf16[8,384,128]{2,1,0:T(8,128)(2,1)} custom-call(bf16[128,1024]{1,0:T(8,128)(2,1)} %q_ref.1, bf16[128,1024]{1,0:T(8,128)(2,1)} %k_ref.1, bf16[128,1024]{1,0:T(8,128)(2,1)} %v_ref.1), custom_call_target="tpu_custom_call" | custom-call | bytes 1572864 | tf_op jit(solution)/shard_map/pallas_call | solution.py:147
  12.4 0.0 collective-permute-done
  12.4 4.4 %all-to-all-start = ((bf16[8,384,128]{2,1,0:T(8,128)(2,1)}), bf16[8,384,128]{2,1,0:T(8,128)(2,1)S(1)}, u32[]{:S(2)}, u32[]{:S(2)}) async-start(bf16[8,384,128]{2,1,0:T(8,128)(2,1)} %shard_map.102), calls=%async_computation | async-start | bytes 1572864 | tf_op jit(solution)/shard_map/all_to_all | solution.py:364
  16.8 2.1 %collective-permute-done.1 = bf16[64,768]{1,0:T(8,128)(2,1)S(1)} collective-permute-done((bf16[64,768]{1,0:T(8,128)(2,1)S(1)}, bf16[64,768]{1,0:T(8,128)(2,1)S(1)}, u32[]{:S(2)}, u32[]{:S(2)}) %collective-permute-start.1) | collective-permute-done | bytes 98336 | tf_op jit(solution)/shard_map/ppermute | solution.py:309
  18.9 0.0 collective-permute-done.3.other_ref
  18.9 0.1 collective-permute-start.5
  19.0 0.5 collective-permute-start.4
  19.5 1.2 %collective-permute-done.5.swapped_ref = bf16[256,768]{1,0:T(8,128)(2,1)S(1)} collective-permute-done((bf16[256,768]{1,0:T(8,128)(2,1)S(1)}, bf16[256,768]{1,0:T(8,128)(2,1)S(1)}, u32[]{:S(2)}, u32[]{:S(2)}) %collective-permute-start.5) | collective-permute-done | bytes 393248 | tf_op jit(solution)/shard_map/ppermute | solution.py:309
  20.7 0.9 shard_map.105
  21.6 0.9 copy-done.1
  22.6 4.0 %collective-permute-start.6 = (bf16[512,128]{1,0:T(8,128)(2,1)S(1)}, bf16[512,128]{1,0:T(8,128)(2,1)S(1)}, u32[]{:S(2)}, u32[]{:S(2)}) collective-permute-start(bf16[512,128]{1,0:T(8,128)(2,1)S(1)} %get-tuple-element.64), channel_id=1, source_target_pairs={{0,4},{1,5},{2,6},{3,7},{4,0},{5,1},{6,2},{7,3},{8,12},{9,13},{10,... | collective-permute-start | bytes 393224 | tf_op jit(solution)/shard_map/ppermute | solution.py:309
  26.6 9.1 %collective-permute-done.4.piece_ref = bf16[256,768]{1,0:T(8,128)(2,1)S(1)} collective-permute-done((bf16[256,768]{1,0:T(8,128)(2,1)S(1)}, bf16[256,768]{1,0:T(8,128)(2,1)S(1)}, u32[]{:S(2)}, u32[]{:S(2)}) %collective-permute-start.4) | collective-permute-done | bytes 393248 | tf_op jit(solution)/shard_map/ppermute | solution.py:309
  35.6 2.7 %collective-permute-start.8 = (bf16[512,128]{1,0:T(8,128)(2,1)S(1)}, bf16[512,128]{1,0:T(8,128)(2,1)S(1)}, u32[]{:S(2)}, u32[]{:S(2)}) collective-permute-start(bf16[512,128]{1,0:T(8,128)(2,1)S(1)} %get-tuple-element.65), channel_id=1, source_target_pairs={{0,4},{1,5},{2,6},{3,7},{4,0},{5,1},{6,2},{7,3},{8,12},{9,13},{10,... | collective-permute-start | bytes 393224 | tf_op jit(solution)/shard_map/ppermute | solution.py:309
  38.4 0.0 collective-permute-done.6
  38.4 2.1 %collective-permute-start.7 = (bf16[512,128]{1,0:T(8,128)(2,1)S(1)}, bf16[512,128]{1,0:T(8,128)(2,1)S(1)}, u32[]{:S(2)}, u32[]{:S(2)}) collective-permute-start(bf16[512,128]{1,0:T(8,128)(2,1)S(1)} %add_convert_fusion.1), channel_id=1, source_target_pairs={{0,8},{1,9},{2,10},{3,11},{4,12},{5,13},{6,14},{7,15},{8,0},{9,1},... | collective-permute-start | bytes 393224 | tf_op jit(solution)/shard_map/ppermute | solution.py:309
  40.5 3.9 %collective-permute-done.8.refs_2_ = bf16[512,128]{1,0:T(8,128)(2,1)S(1)} collective-permute-done((bf16[512,128]{1,0:T(8,128)(2,1)S(1)}, bf16[512,128]{1,0:T(8,128)(2,1)S(1)}, u32[]{:S(2)}, u32[]{:S(2)}) %collective-permute-start.8) | collective-permute-done | bytes 131104 | tf_op jit(solution)/shard_map/ppermute | solution.py:309
  44.4 3.4 %collective-permute-done.7.refs_4_ = bf16[512,128]{1,0:T(8,128)(2,1)S(1)} collective-permute-done((bf16[512,128]{1,0:T(8,128)(2,1)S(1)}, bf16[512,128]{1,0:T(8,128)(2,1)S(1)}, u32[]{:S(2)}, u32[]{:S(2)}) %collective-permute-start.7) | collective-permute-done | bytes 131104 | tf_op jit(solution)/shard_map/ppermute | solution.py:309
  47.8 0.0 collective-permute-done.9.swapped_ref
  47.8 0.9 shard_map.106
  48.7 0.9 copy-done.3
  49.6 0.0 collective-permute-start.10
  49.6 0.0 all-to-all-done.tok_ref
  49.6 4.9 %shard_map.104 = (bf16[1536,1024]{1,0:T(8,128)(2,1)S(1)}, bf16[128,1024]{1,0:T(8,128)(2,1)S(1)}, bf16[1024,128]{1,0:T(8,128)(2,1)S(1)}, bf16[128,1536]{1,0:T(8,128)(2,1)S(1)}, bf16[1536,128]{1,0:T(8,128)(2,1)S(1)}) custom-call(bf16[8,384,128]{2,1,0:T(8,128)(2,1)S(1)} %all-to-all-done.tok_ref, bf16[2,512,128]{2,1,0:T(8,128)(2,1)S(1)} %copy-done.5), custom_call_target="tpu_custom_call" | custom-call | flops 805306368 | bytes 6291456 | tf_op jit(solution)/shard_map/pallas_call | solution.py:147
  54.5 0.0 collective-permute-done.10
  54.6 2.4 %collective-permute-start.11 = (bf16[512,128]{1,0:T(8,128)(2,1)S(1)}, bf16[512,128]{1,0:T(8,128)(2,1)S(1)}, u32[]{:S(2)}, u32[]{:S(2)}) collective-permute-start(bf16[512,128]{1,0:T(8,128)(2,1)S(1)} %add_convert_fusion), channel_id=1, source_target_pairs={{0,8},{1,9},{2,10},{3,11},{4,12},{5,13},{6,14},{7,15},{8,0},{9,1},... | collective-permute-start | bytes 393224 | tf_op jit(solution)/shard_map/ppermute | solution.py:309
  57.0 0.2 collective-permute-start.12
  57.2 5.9 %collective-permute-done.11.refs_5_ = bf16[512,128]{1,0:T(8,128)(2,1)S(1)} collective-permute-done((bf16[512,128]{1,0:T(8,128)(2,1)S(1)}, bf16[512,128]{1,0:T(8,128)(2,1)S(1)}, u32[]{:S(2)}, u32[]{:S(2)}) %collective-permute-start.11) | collective-permute-done | bytes 131104 | tf_op jit(solution)/shard_map/ppermute | solution.py:309
  63.1 0.0 collective-permute-done.12.refs_3_
  63.1 1.6 %collective-permute-start.14 = (bf16[128,1024]{1,0:T(8,128)(2,1)S(1)}, bf16[128,1024]{1,0:T(8,128)(2,1)S(1)}, u32[]{:S(2)}, u32[]{:S(2)}) collective-permute-start(bf16[128,1024]{1,0:T(8,128)(2,1)S(1)} %get-tuple-element.85.out_ref.refs_0_), channel_id=1, source_target_pairs={{0,4},{1,5},{2,6},{3,7},{4,0},{5,1},{6,2},{7,3},{8,12},{9,13},{10,... | collective-permute-start | bytes 786440 | tf_op jit(solution)/shard_map/ppermute | solution.py:309
  64.7 1.2 %collective-permute-start.13 = (bf16[128,1024]{1,0:T(8,128)(2,1)S(1)}, bf16[128,1024]{1,0:T(8,128)(2,1)S(1)}, u32[]{:S(2)}, u32[]{:S(2)}) collective-permute-start(bf16[128,1024]{1,0:T(8,128)(2,1)S(1)} %get-tuple-element.85.out_ref.refs_0_), channel_id=1, source_target_pairs={{0,8},{1,9},{2,10},{3,11},{4,12},{5,13},{6,14},{7,15},{8,0},{9,1},... | collective-permute-start | bytes 786440 | tf_op jit(solution)/shard_map/ppermute | solution.py:309
  65.9 4.5 %shard_map.107 = bf16[8,384,128]{2,1,0:T(8,128)(2,1)} custom-call(bf16[1024,128]{1,0:T(8,128)(2,1)S(1)} %get-tuple-element.51.queries_ref, bf16[128,1536]{1,0:T(8,128)(2,1)S(1)} %get-tuple-element.52.keys_t_ref, bf16[1536,128]{1,0:T(8,128)(2,1)S(1)} %get-tuple-element.53.vals_ref, bf16[1536,1024]{1,0:T(8,128)(2,1)S(1)} %get-tuple-element.54.probs_ref, ...), custom_call_target="tpu_custom_call" | custom-call | flops 1610612736 | bytes 6291456 | tf_op jit(solution)/shard_map/pallas_call | solution.py:147
  70.4 3.5 %collective-permute-done.14.refs_1_ = bf16[128,1024]{1,0:T(8,128)(2,1)S(1)} collective-permute-done((bf16[128,1024]{1,0:T(8,128)(2,1)S(1)}, bf16[128,1024]{1,0:T(8,128)(2,1)S(1)}, u32[]{:S(2)}, u32[]{:S(2)}) %collective-permute-start.14) | collective-permute-done | bytes 262176 | tf_op jit(solution)/shard_map/ppermute | solution.py:309
  73.9 4.0 %collective-permute-done.13.refs_2_ = bf16[128,1024]{1,0:T(8,128)(2,1)S(1)} collective-permute-done((bf16[128,1024]{1,0:T(8,128)(2,1)S(1)}, bf16[128,1024]{1,0:T(8,128)(2,1)S(1)}, u32[]{:S(2)}, u32[]{:S(2)}) %collective-permute-start.13) | collective-permute-done | bytes 262176 | tf_op jit(solution)/shard_map/ppermute | solution.py:309
  77.9 0.0 collective-permute-start.15
  77.9 3.6 %all-to-all-start.1 = ((bf16[8,384,128]{2,1,0:T(8,128)(2,1)}), bf16[8,384,128]{2,1,0:T(8,128)(2,1)S(1)}, u32[]{:S(2)}, u32[]{:S(2)}) async-start(bf16[8,384,128]{2,1,0:T(8,128)(2,1)} %shard_map.107), calls=%async_computation.1 | async-start | bytes 1572864 | tf_op jit(solution)/shard_map/all_to_all | solution.py:409
  81.5 7.3 %collective-permute-done.15.refs_3_ = bf16[128,1024]{1,0:T(8,128)(2,1)S(1)} collective-permute-done((bf16[128,1024]{1,0:T(8,128)(2,1)S(1)}, bf16[128,1024]{1,0:T(8,128)(2,1)S(1)}, u32[]{:S(2)}, u32[]{:S(2)}) %collective-permute-start.15) | collective-permute-done | bytes 262176 | tf_op jit(solution)/shard_map/ppermute | solution.py:309
  88.8 1.1 %copy-done.4 = bf16[512,768]{1,0:T(8,128)(2,1)S(1)} copy-done((bf16[512,768]{1,0:T(8,128)(2,1)S(1)}, bf16[512,768]{1,0:T(8,128)(2,1)}, u32[]{:S(2)}) %copy-start.4) | copy-done | bytes 786456
  89.9 1.3 %shard_map.109 = (bf16[512,384]{1,0:T(8,128)(2,1)S(1)}, bf16[512,384]{1,0:T(8,128)(2,1)S(1)}) custom-call(bf16[512,768]{1,0:T(8,128)(2,1)S(1)} %copy-done.2, bf16[512,768]{1,0:T(8,128)(2,1)S(1)} %copy-done.4, bf16[128,1024]{1,0:T(8,128)(2,1)S(1)} %get-tuple-element.85.out_ref.refs_0_, bf16[128,1024]{1,0:T(8,128)(2,1)S(1)} %collective-permute-done.14.refs_1_, ...), custom_call_target="tpu_custom_call" | custom-call | flops 9663676416 | bytes 1572864 | tf_op jit(solution)/shard_map/pallas_call | solution.py:147
  91.2 0.8 collective-permute-start.16
  92.0 8.2 %collective-permute-done.16.other_ref = bf16[512,384]{1,0:T(8,128)(2,1)S(1)} collective-permute-done((bf16[512,384]{1,0:T(8,128)(2,1)S(1)}, bf16[512,384]{1,0:T(8,128)(2,1)S(1)}, u32[]{:S(2)}, u32[]{:S(2)}) %collective-permute-start.16) | collective-permute-done | bytes 393248 | tf_op jit(solution)/shard_map/ppermute | solution.py:309
  100.2 1.5 %shard_map.110 = f32[384,1024]{1,0:T(8,128)} custom-call(bf16[512,384]{1,0:T(8,128)(2,1)S(1)} %get-tuple-element.88.own_ref, bf16[512,384]{1,0:T(8,128)(2,1)S(1)} %collective-permute-done.16.other_ref), custom_call_target="tpu_custom_call" | custom-call | bytes 2359296 | tf_op jit(solution)/shard_map/pallas_call | solution.py:147
  101.7 0.0 all-to-all-done.1.tok_ref
  101.7 1.1 %shard_map.108 = (bf16[128,1024]{1,0:T(8,128)(2,1)}, bf16[128,1024]{1,0:T(8,128)(2,1)}, bf16[128,1024]{1,0:T(8,128)(2,1)}) custom-call(bf16[8,384,128]{2,1,0:T(8,128)(2,1)S(1)} %all-to-all-done.1.tok_ref), custom_call_target="tpu_custom_call" | custom-call | bytes 1572864 | tf_op jit(solution)/shard_map/pallas_call | solution.py:147
  (20 shorter events, 0.2 us)
Async XLA Ops:
  0.6 5.3 %copy-start.6 = (bf16[128,3072]{1,0:T(8,128)(2,1)S(1)}, bf16[128,3072]{1,0:T(8,128)(2,1)}, u32[]{:S(2)}) copy-start(bf16[128,3072]{1,0:T(8,128)(2,1)} %param.13) | copy-start | bytes 2359300
  3.0 17.7 %copy-start = (bf16[384,512]{1,0:T(8,128)(2,1)S(1)}, bf16[384,512]{1,0:T(8,128)(2,1)}, u32[]{:S(2)}) copy-start(bf16[384,512]{1,0:T(8,128)(2,1)} %get-tuple-element.61.own_ref) | copy-start | bytes 1179652
  3.0 15.9 %collective-permute-start.3 = (bf16[384,512]{1,0:T(8,128)(2,1)}, bf16[384,512]{1,0:T(8,128)(2,1)S(1)}, u32[]{:S(2)}, u32[]{:S(2)}) collective-permute-start(bf16[384,512]{1,0:T(8,128)(2,1)} %get-tuple-element.56), channel_id=1, source_target_pairs={{0,2},{1,3},{2,0},{3,1},{4,6},{5,7},{6,4},{7,5},{8,10},{9,11},{10,... | collective-permute-start | bytes 1179656 | tf_op jit(solution)/shard_map/ppermute | solution.py:309
  6.0 6.4 %collective-permute-start = (bf16[64,768]{1,0:T(8,128)(2,1)S(1)}, bf16[64,768]{1,0:T(8,128)(2,1)S(1)}, u32[]{:S(2)}, u32[]{:S(2)}) collective-permute-start(bf16[64,768]{1,0:T(8,128)(2,1)S(1)} %get-tuple-element.93), channel_id=1, source_target_pairs={{0,4},{1,5},{2,6},{3,7},{4,0},{5,1},{6,2},{7,3},{8,12},{9,13},{10,... | collective-permute-start | bytes 294920 | tf_op jit(solution)/shard_map/ppermute | solution.py:309
  7.7 9.1 %collective-permute-start.2 = (bf16[64,768]{1,0:T(8,128)(2,1)S(1)}, bf16[64,768]{1,0:T(8,128)(2,1)S(1)}, u32[]{:S(2)}, u32[]{:S(2)}) collective-permute-start(bf16[64,768]{1,0:T(8,128)(2,1)S(1)} %get-tuple-element.90), channel_id=1, source_target_pairs={{0,12},{1,13},{2,14},{3,15},{4,8},{5,9},{6,10},{7,11},{8,4},{9,5},... | collective-permute-start | bytes 294920 | tf_op jit(solution)/shard_map/ppermute | solution.py:309
  10.1 8.8 %collective-permute-start.1 = (bf16[64,768]{1,0:T(8,128)(2,1)S(1)}, bf16[64,768]{1,0:T(8,128)(2,1)S(1)}, u32[]{:S(2)}, u32[]{:S(2)}) collective-permute-start(bf16[64,768]{1,0:T(8,128)(2,1)S(1)} %get-tuple-element.91), channel_id=1, source_target_pairs={{0,8},{1,9},{2,10},{3,11},{4,12},{5,13},{6,14},{7,15},{8,0},{9,1},... | collective-permute-start | bytes 294920 | tf_op jit(solution)/shard_map/ppermute | solution.py:309
  12.4 37.2 %copy-start.5 = (bf16[2,512,128]{2,1,0:T(8,128)(2,1)S(1)}, bf16[2,512,128]{2,1,0:T(8,128)(2,1)}, u32[]{:S(2)}) copy-start(bf16[2,512,128]{2,1,0:T(8,128)(2,1)} %get-tuple-element.50.text_ref) | copy-start | bytes 786436
  12.4 37.2 %all-to-all-start = ((bf16[8,384,128]{2,1,0:T(8,128)(2,1)}), bf16[8,384,128]{2,1,0:T(8,128)(2,1)S(1)}, u32[]{:S(2)}, u32[]{:S(2)}) async-start(bf16[8,384,128]{2,1,0:T(8,128)(2,1)} %shard_map.102), calls=%async_computation | async-start | bytes 1572864 | tf_op jit(solution)/shard_map/all_to_all | solution.py:364
  18.9 1.8 %collective-permute-start.5 = (bf16[256,768]{1,0:T(8,128)(2,1)S(1)}, bf16[256,768]{1,0:T(8,128)(2,1)S(1)}, u32[]{:S(2)}, u32[]{:S(2)}) collective-permute-start(bf16[256,768]{1,0:T(8,128)(2,1)S(1)} %constant_dynamic-update-slice_fusion.piece_ref), channel_id=1, source_target_pairs={{0,1},{1,0},{2,3},{3,2},{4,5},{5,4},{6,7},{7,6},{8,9},{9,8},{10,11... | collective-permute-start | bytes 1179656 | tf_op jit(solution)/shard_map/ppermute | solution.py:309
  19.0 16.6 %collective-permute-start.4 = (bf16[256,768]{1,0:T(8,128)(2,1)S(1)}, bf16[256,768]{1,0:T(8,128)(2,1)S(1)}, u32[]{:S(2)}, u32[]{:S(2)}) collective-permute-start(bf16[256,768]{1,0:T(8,128)(2,1)S(1)} %constant_dynamic-update-slice_fusion.piece_ref), channel_id=1, source_target_pairs={{0,2},{1,3},{2,0},{3,1},{4,6},{5,7},{6,4},{7,5},{8,10},{9,11},{10,... | collective-permute-start | bytes 1179656 | tf_op jit(solution)/shard_map/ppermute | solution.py:309
  21.6 0.9 copy-start.1
  22.6 15.8 %collective-permute-start.6 = (bf16[512,128]{1,0:T(8,128)(2,1)S(1)}, bf16[512,128]{1,0:T(8,128)(2,1)S(1)}, u32[]{:S(2)}, u32[]{:S(2)}) collective-permute-start(bf16[512,128]{1,0:T(8,128)(2,1)S(1)} %get-tuple-element.64), channel_id=1, source_target_pairs={{0,4},{1,5},{2,6},{3,7},{4,0},{5,1},{6,2},{7,3},{8,12},{9,13},{10,... | collective-permute-start | bytes 393224 | tf_op jit(solution)/shard_map/ppermute | solution.py:309
  35.6 12.2 %collective-permute-start.9 = (bf16[256,768]{1,0:T(8,128)(2,1)S(1)}, bf16[256,768]{1,0:T(8,128)(2,1)S(1)}, u32[]{:S(2)}, u32[]{:S(2)}) collective-permute-start(bf16[256,768]{1,0:T(8,128)(2,1)S(1)} %collective-permute-done.4.piece_ref), channel_id=1, source_target_pairs={{0,1},{1,0},{2,3},{3,2},{4,5},{5,4},{6,7},{7,6},{8,9},{9,8},{10,11... | collective-permute-start | bytes 1179656 | tf_op jit(solution)/shard_map/ppermute | solution.py:309
  35.6 8.8 %collective-permute-start.8 = (bf16[512,128]{1,0:T(8,128)(2,1)S(1)}, bf16[512,128]{1,0:T(8,128)(2,1)S(1)}, u32[]{:S(2)}, u32[]{:S(2)}) collective-permute-start(bf16[512,128]{1,0:T(8,128)(2,1)S(1)} %get-tuple-element.65), channel_id=1, source_target_pairs={{0,4},{1,5},{2,6},{3,7},{4,0},{5,1},{6,2},{7,3},{8,12},{9,13},{10,... | collective-permute-start | bytes 393224 | tf_op jit(solution)/shard_map/ppermute | solution.py:309
  38.4 9.4 %collective-permute-start.7 = (bf16[512,128]{1,0:T(8,128)(2,1)S(1)}, bf16[512,128]{1,0:T(8,128)(2,1)S(1)}, u32[]{:S(2)}, u32[]{:S(2)}) collective-permute-start(bf16[512,128]{1,0:T(8,128)(2,1)S(1)} %add_convert_fusion.1), channel_id=1, source_target_pairs={{0,8},{1,9},{2,10},{3,11},{4,12},{5,13},{6,14},{7,15},{8,0},{9,1},... | collective-permute-start | bytes 393224 | tf_op jit(solution)/shard_map/ppermute | solution.py:309
  48.7 0.9 copy-start.3
  49.6 5.0 %collective-permute-start.10 = (bf16[512,128]{1,0:T(8,128)(2,1)S(1)}, bf16[512,128]{1,0:T(8,128)(2,1)S(1)}, u32[]{:S(2)}, u32[]{:S(2)}) collective-permute-start(bf16[512,128]{1,0:T(8,128)(2,1)S(1)} %get-tuple-element.67), channel_id=1, source_target_pairs={{0,4},{1,5},{2,6},{3,7},{4,0},{5,1},{6,2},{7,3},{8,12},{9,13},{10,... | collective-permute-start | bytes 393224 | tf_op jit(solution)/shard_map/ppermute | solution.py:309
  54.6 8.5 %collective-permute-start.11 = (bf16[512,128]{1,0:T(8,128)(2,1)S(1)}, bf16[512,128]{1,0:T(8,128)(2,1)S(1)}, u32[]{:S(2)}, u32[]{:S(2)}) collective-permute-start(bf16[512,128]{1,0:T(8,128)(2,1)S(1)} %add_convert_fusion), channel_id=1, source_target_pairs={{0,8},{1,9},{2,10},{3,11},{4,12},{5,13},{6,14},{7,15},{8,0},{9,1},... | collective-permute-start | bytes 393224 | tf_op jit(solution)/shard_map/ppermute | solution.py:309
  57.0 6.1 %collective-permute-start.12 = (bf16[512,128]{1,0:T(8,128)(2,1)S(1)}, bf16[512,128]{1,0:T(8,128)(2,1)S(1)}, u32[]{:S(2)}, u32[]{:S(2)}) collective-permute-start(bf16[512,128]{1,0:T(8,128)(2,1)S(1)} %get-tuple-element.76), channel_id=1, source_target_pairs={{0,4},{1,5},{2,6},{3,7},{4,0},{5,1},{6,2},{7,3},{8,12},{9,13},{10,... | collective-permute-start | bytes 393224 | tf_op jit(solution)/shard_map/ppermute | solution.py:309
  63.1 10.8 %collective-permute-start.14 = (bf16[128,1024]{1,0:T(8,128)(2,1)S(1)}, bf16[128,1024]{1,0:T(8,128)(2,1)S(1)}, u32[]{:S(2)}, u32[]{:S(2)}) collective-permute-start(bf16[128,1024]{1,0:T(8,128)(2,1)S(1)} %get-tuple-element.85.out_ref.refs_0_), channel_id=1, source_target_pairs={{0,4},{1,5},{2,6},{3,7},{4,0},{5,1},{6,2},{7,3},{8,12},{9,13},{10,... | collective-permute-start | bytes 786440 | tf_op jit(solution)/shard_map/ppermute | solution.py:309
  64.7 13.2 %collective-permute-start.13 = (bf16[128,1024]{1,0:T(8,128)(2,1)S(1)}, bf16[128,1024]{1,0:T(8,128)(2,1)S(1)}, u32[]{:S(2)}, u32[]{:S(2)}) collective-permute-start(bf16[128,1024]{1,0:T(8,128)(2,1)S(1)} %get-tuple-element.85.out_ref.refs_0_), channel_id=1, source_target_pairs={{0,8},{1,9},{2,10},{3,11},{4,12},{5,13},{6,14},{7,15},{8,0},{9,1},... | collective-permute-start | bytes 786440 | tf_op jit(solution)/shard_map/ppermute | solution.py:309
  65.9 22.9 %copy-start.2 = (bf16[512,768]{1,0:T(8,128)(2,1)S(1)}, bf16[512,768]{1,0:T(8,128)(2,1)}, u32[]{:S(2)}) copy-start(bf16[512,768]{1,0:T(8,128)(2,1)} %copy-done.1) | copy-start | bytes 2359300
  77.9 10.9 %collective-permute-start.15 = (bf16[128,1024]{1,0:T(8,128)(2,1)S(1)}, bf16[128,1024]{1,0:T(8,128)(2,1)S(1)}, u32[]{:S(2)}, u32[]{:S(2)}) collective-permute-start(bf16[128,1024]{1,0:T(8,128)(2,1)S(1)} %collective-permute-done.13.refs_2_), channel_id=1, source_target_pairs={{0,4},{1,5},{2,6},{3,7},{4,0},{5,1},{6,2},{7,3},{8,12},{9,13},{10,... | collective-permute-start | bytes 786440 | tf_op jit(solution)/shard_map/ppermute | solution.py:309
  77.9 23.8 %all-to-all-start.1 = ((bf16[8,384,128]{2,1,0:T(8,128)(2,1)}), bf16[8,384,128]{2,1,0:T(8,128)(2,1)S(1)}, u32[]{:S(2)}, u32[]{:S(2)}) async-start(bf16[8,384,128]{2,1,0:T(8,128)(2,1)} %shard_map.107), calls=%async_computation.1 | async-start | bytes 1572864 | tf_op jit(solution)/shard_map/all_to_all | solution.py:409
  88.8 1.1 %copy-start.4 = (bf16[512,768]{1,0:T(8,128)(2,1)S(1)}, bf16[512,768]{1,0:T(8,128)(2,1)}, u32[]{:S(2)}) copy-start(bf16[512,768]{1,0:T(8,128)(2,1)} %copy-done.3) | copy-start | bytes 2359300
  91.2 9.0 %collective-permute-start.16 = (bf16[512,384]{1,0:T(8,128)(2,1)S(1)}, bf16[512,384]{1,0:T(8,128)(2,1)S(1)}, u32[]{:S(2)}, u32[]{:S(2)}) collective-permute-start(bf16[512,384]{1,0:T(8,128)(2,1)S(1)} %get-tuple-element.89), channel_id=1, source_target_pairs={{0,2},{1,3},{2,0},{3,1},{4,6},{5,7},{6,4},{7,5},{8,10},{9,11},{10,... | collective-permute-start | bytes 1179656 | tf_op jit(solution)/shard_map/ppermute | solution.py:309

commit v17 on v16

--- a/solution.py
+++ b/solution.py
@@ -360,7 +360,6 @@
     row = jnp.concatenate(along, axis=0)
     row_swapped = exchange(row, cores=True)
     other_row = exchange(row, 1)
-    other_swapped = exchange(other_row, cores=True)
     tok_in = lax.all_to_all(tok_out, "seq", split_axis=0, concat_axis=0, tiled=True)
 
     probs, out_t, queries, keys_t, vals = call(
@@ -392,6 +391,7 @@
     far0 = exchange(add(kept0, exchange(send0, 2)), 4)
     near0 = exchange(near0, 2)
     other_row, far0, near0 = lax.optimization_barrier((other_row, far0, near0))
+    other_swapped = exchange(other_row, cores=True)
     mine1, kept1, near1, send1, cot1 = partial(other_row, other_swapped)
     send1, out_t, near1 = lax.optimization_barrier((exchange(send1, 2), out_t, near1))
     far1 = exchange(add(kept1, send1), 4)
@@ -414,7 +414,7 @@
         [shape((4 * HD, depth), BF16)] * 2,
         [cot0, cot1, *outs],
         scratch=[pltpu.VMEM((4 * HD, image), BF16)],
-        flops=96 * image * columns * HD,
+        flops=72 * image * columns * HD,
         moved=2 * image * columns,
     )
     grads = call(

time: 103 us -> 113 us (1.097)
  waiting for transfers between devices: 48.7 us -> 58.5 us
    ppermute x17, waiting for transfers between devices: 48.7 us -> 58.5 us  [exchange(): return lax.ppermute(array, ('seq', 'fsdp'), pairs)]
  transfers between devices with their start and end apart: 19 -> 19, of which waited for: 10 -> 11; matrix products, arithmetic and copies ran while one was open for 0% -> 0% of each run, Pallas kernels for 16% -> 15%
where the time goes in v17:
time: 113 us
  waiting for transfers between devices  58.5 us (52%)
  starting transfers between devices  30.2 us (27%)
  Pallas kernels  20.1 us (18%)
  local copies, waits for them, and re-layouts  3.04 us (3%)
    ppermute x17, waiting for transfers between devices, exchange(): return lax.ppermute(array, ('seq', 'fsdp'), pairs)  58.5 us
    ppermute x17, starting transfers between devices, exchange(): return lax.ppermute(array, ('seq', 'fsdp'), pairs)  22.2 us
    pallas_call x9, Pallas kernels, call(): pl.pallas_call(kernel, out_shape=outs, grid_spec=pltpu.PrefetchScalarGrid...  20.1 us
    all_to_all x1, starting transfers between devices, local(): lax.all_to_all(grad_out, 'seq', split_axis=0, concat_axis=0, tiled=True)  4.06 us
    all_to_all x1, starting transfers between devices, local(): lax.all_to_all(tok_out, 'seq', split_axis=0, concat_axis=0, tiled=True)  3.93 us
    unnamed x17, local copies, waits for them, and re-layouts  2.99 us
  transfers between devices with their start and end apart: 19, of which 11 were waited for; matrix products, arithmetic and copies ran while one was open for 0% of the time, Pallas kernels for 15%

profile of v17, /device:TPU:0, one launch (start us, length us, event | category | flops | bytes accessed | tf_op | source)
XLA Modules:
  0.0 112.7 jit_solution(15197978129004166307)
XLA Ops:
  0.6 2.3 %shard_map.103 = (bf16[384,512]{1,0:T(8,128)(2,1)}, bf16[384,512]{1,0:T(8,128)(2,1)}, bf16[2,512,128]{2,1,0:T(8,128)(2,1)}) custom-call(s32[1]{0:T(128)} %bitcast.me_ref, bf16[384,1024]{1,0:T(8,128)(2,1)} %w_ref.1, bf16[512,1024]{1,0:T(8,128)(2,1)} %kt_ref.1, bf16[512,1024]{1,0:T(8,128)(2,1)} %vt_ref.1), custom_call_target="tpu_custom_call" | custom-call | bytes 1572864 | tf_op jit(solution)/shard_map/pallas_call | solution.py:147
  3.0 3.0 %collective-permute-start.3 = (bf16[384,512]{1,0:T(8,128)(2,1)}, bf16[384,512]{1,0:T(8,128)(2,1)S(1)}, u32[]{:S(2)}, u32[]{:S(2)}) collective-permute-start(bf16[384,512]{1,0:T(8,128)(2,1)} %get-tuple-element.56), channel_id=1, source_target_pairs={{0,2},{1,3},{2,0},{3,1},{4,6},{5,7},{6,4},{7,5},{8,10},{9,11},{10,... | collective-permute-start | bytes 1179656 | tf_op jit(solution)/shard_map/ppermute | solution.py:309
  6.0 1.6 %collective-permute-start = (bf16[64,768]{1,0:T(8,128)(2,1)S(1)}, bf16[64,768]{1,0:T(8,128)(2,1)S(1)}, u32[]{:S(2)}, u32[]{:S(2)}) collective-permute-start(bf16[64,768]{1,0:T(8,128)(2,1)S(1)} %get-tuple-element.93), channel_id=1, source_target_pairs={{0,4},{1,5},{2,6},{3,7},{4,0},{5,1},{6,2},{7,3},{8,12},{9,13},{10,... | collective-permute-start | bytes 294920 | tf_op jit(solution)/shard_map/ppermute | solution.py:309
  7.7 2.5 %collective-permute-start.2 = (bf16[64,768]{1,0:T(8,128)(2,1)S(1)}, bf16[64,768]{1,0:T(8,128)(2,1)S(1)}, u32[]{:S(2)}, u32[]{:S(2)}) collective-permute-start(bf16[64,768]{1,0:T(8,128)(2,1)S(1)} %get-tuple-element.90), channel_id=1, source_target_pairs={{0,12},{1,13},{2,14},{3,15},{4,8},{5,9},{6,10},{7,11},{8,4},{9,5},... | collective-permute-start | bytes 294920 | tf_op jit(solution)/shard_map/ppermute | solution.py:309
  10.1 0.1 collective-permute-start.1
  10.2 2.1 %shard_map.102 = bf16[8,384,128]{2,1,0:T(8,128)(2,1)} custom-call(bf16[128,1024]{1,0:T(8,128)(2,1)} %q_ref.1, bf16[128,1024]{1,0:T(8,128)(2,1)} %k_ref.1, bf16[128,1024]{1,0:T(8,128)(2,1)} %v_ref.1), custom_call_target="tpu_custom_call" | custom-call | bytes 1572864 | tf_op jit(solution)/shard_map/pallas_call | solution.py:147
  12.4 0.0 collective-permute-done
  12.4 3.2 %collective-permute-done.2 = bf16[64,768]{1,0:T(8,128)(2,1)S(1)} collective-permute-done((bf16[64,768]{1,0:T(8,128)(2,1)S(1)}, bf16[64,768]{1,0:T(8,128)(2,1)S(1)}, u32[]{:S(2)}, u32[]{:S(2)}) %collective-permute-start.2) | collective-permute-done | bytes 98336 | tf_op jit(solution)/shard_map/ppermute | solution.py:309
  15.5 3.3 %collective-permute-done.1 = bf16[64,768]{1,0:T(8,128)(2,1)S(1)} collective-permute-done((bf16[64,768]{1,0:T(8,128)(2,1)S(1)}, bf16[64,768]{1,0:T(8,128)(2,1)S(1)}, u32[]{:S(2)}, u32[]{:S(2)}) %collective-permute-start.1) | collective-permute-done | bytes 98336 | tf_op jit(solution)/shard_map/ppermute | solution.py:309
  18.8 0.0 collective-permute-done.3.other_ref
  18.9 0.1 collective-permute-start.5
  18.9 3.9 %all-to-all-start = ((bf16[8,384,128]{2,1,0:T(8,128)(2,1)}), bf16[8,384,128]{2,1,0:T(8,128)(2,1)S(1)}, u32[]{:S(2)}, u32[]{:S(2)}) async-start(bf16[8,384,128]{2,1,0:T(8,128)(2,1)} %shard_map.102), calls=%async_computation | async-start | bytes 1572864 | tf_op jit(solution)/shard_map/all_to_all | solution.py:363
  22.9 0.0 collective-permute-done.5.swapped_ref
  22.9 0.9 shard_map.105
  23.8 0.9 copy-done.1
  24.7 2.0 %collective-permute-start.6 = (bf16[512,128]{1,0:T(8,128)(2,1)S(1)}, bf16[512,128]{1,0:T(8,128)(2,1)S(1)}, u32[]{:S(2)}, u32[]{:S(2)}) collective-permute-start(bf16[512,128]{1,0:T(8,128)(2,1)S(1)} %get-tuple-element.64), channel_id=1, source_target_pairs={{0,4},{1,5},{2,6},{3,7},{4,0},{5,1},{6,2},{7,3},{8,12},{9,13},{10,... | collective-permute-start | bytes 393224 | tf_op jit(solution)/shard_map/ppermute | solution.py:309
  26.7 1.5 %collective-permute-start.4 = (bf16[256,768]{1,0:T(8,128)(2,1)S(1)}, bf16[256,768]{1,0:T(8,128)(2,1)S(1)}, u32[]{:S(2)}, u32[]{:S(2)}) collective-permute-start(bf16[256,768]{1,0:T(8,128)(2,1)S(1)} %constant_dynamic-update-slice_fusion.piece_ref), channel_id=1, source_target_pairs={{0,2},{1,3},{2,0},{3,1},{4,6},{5,7},{6,4},{7,5},{8,10},{9,11},{10,... | collective-permute-start | bytes 1179656 | tf_op jit(solution)/shard_map/ppermute | solution.py:309
  28.2 0.6 collective-permute-start.8
  28.7 11.5 %collective-permute-done.6 = bf16[512,128]{1,0:T(8,128)(2,1)S(1)} collective-permute-done((bf16[512,128]{1,0:T(8,128)(2,1)S(1)}, bf16[512,128]{1,0:T(8,128)(2,1)S(1)}, u32[]{:S(2)}, u32[]{:S(2)}) %collective-permute-start.6) | collective-permute-done | bytes 131104 | tf_op jit(solution)/shard_map/ppermute | solution.py:309
  40.3 4.4 %collective-permute-start.7 = (bf16[512,128]{1,0:T(8,128)(2,1)S(1)}, bf16[512,128]{1,0:T(8,128)(2,1)S(1)}, u32[]{:S(2)}, u32[]{:S(2)}) collective-permute-start(bf16[512,128]{1,0:T(8,128)(2,1)S(1)} %add_convert_fusion.1), channel_id=1, source_target_pairs={{0,8},{1,9},{2,10},{3,11},{4,12},{5,13},{6,14},{7,15},{8,0},{9,1},... | collective-permute-start | bytes 393224 | tf_op jit(solution)/shard_map/ppermute | solution.py:309
  44.6 0.0 collective-permute-done.4.piece_ref
  44.6 0.0 collective-permute-done.8.refs_2_
  44.6 5.3 %collective-permute-done.7.refs_4_ = bf16[512,128]{1,0:T(8,128)(2,1)S(1)} collective-permute-done((bf16[512,128]{1,0:T(8,128)(2,1)S(1)}, bf16[512,128]{1,0:T(8,128)(2,1)S(1)}, u32[]{:S(2)}, u32[]{:S(2)}) %collective-permute-start.7) | collective-permute-done | bytes 131104 | tf_op jit(solution)/shard_map/ppermute | solution.py:309
  49.9 0.0 collective-permute-start.9
  49.9 1.7 %collective-permute-done.9.swapped_ref = bf16[256,768]{1,0:T(8,128)(2,1)S(1)} collective-permute-done((bf16[256,768]{1,0:T(8,128)(2,1)S(1)}, bf16[256,768]{1,0:T(8,128)(2,1)S(1)}, u32[]{:S(2)}, u32[]{:S(2)}) %collective-permute-start.9) | collective-permute-done | bytes 393248 | tf_op jit(solution)/shard_map/ppermute | solution.py:309
  51.7 1.5 %shard_map.106 = (f32[512,128]{1,0:T(8,128)S(1)}, f32[512,128]{1,0:T(8,128)S(1)}, bf16[512,128]{1,0:T(8,128)(2,1)S(1)}, bf16[512,128]{1,0:T(8,128)(2,1)}, bf16[512,768]{1,0:T(8,128)(2,1)S(1)}) custom-call(bf16[256,768]{1,0:T(8,128)(2,1)S(1)} %collective-permute-done.4.piece_ref, bf16[256,768]{1,0:T(8,128)(2,1)S(1)} %collective-permute-done.9.swapped_ref, ...), custom_call_target="tpu_custom_call" | custom-call | flops 402653184 | bytes 786432 | tf_op jit(solution)/shard_map/pallas_call | solution.py:147
  53.2 0.9 copy-done.3
  54.1 0.0 collective-permute-start.10
  54.1 4.9 %shard_map.104 = (bf16[1536,1024]{1,0:T(8,128)(2,1)S(1)}, bf16[128,1024]{1,0:T(8,128)(2,1)S(1)}, bf16[1024,128]{1,0:T(8,128)(2,1)S(1)}, bf16[128,1536]{1,0:T(8,128)(2,1)S(1)}, bf16[1536,128]{1,0:T(8,128)(2,1)S(1)}) custom-call(bf16[8,384,128]{2,1,0:T(8,128)(2,1)S(1)} %all-to-all-done.tok_ref, bf16[2,512,128]{2,1,0:T(8,128)(2,1)S(1)} %copy-done.5), custom_call_target="tpu_custom_call" | custom-call | flops 805306368 | bytes 6291456 | tf_op jit(solution)/shard_map/pallas_call | solution.py:147
  59.0 0.8 collective-permute-done.10
  59.9 1.8 %collective-permute-start.11 = (bf16[512,128]{1,0:T(8,128)(2,1)S(1)}, bf16[512,128]{1,0:T(8,128)(2,1)S(1)}, u32[]{:S(2)}, u32[]{:S(2)}) collective-permute-start(bf16[512,128]{1,0:T(8,128)(2,1)S(1)} %add_convert_fusion), channel_id=1, source_target_pairs={{0,8},{1,9},{2,10},{3,11},{4,12},{5,13},{6,14},{7,15},{8,0},{9,1},... | collective-permute-start | bytes 393224 | tf_op jit(solution)/shard_map/ppermute | solution.py:309
  61.6 0.8 collective-permute-start.12
  62.5 6.0 %collective-permute-done.11.refs_5_ = bf16[512,128]{1,0:T(8,128)(2,1)S(1)} collective-permute-done((bf16[512,128]{1,0:T(8,128)(2,1)S(1)}, bf16[512,128]{1,0:T(8,128)(2,1)S(1)}, u32[]{:S(2)}, u32[]{:S(2)}) %collective-permute-start.11) | collective-permute-done | bytes 131104 | tf_op jit(solution)/shard_map/ppermute | solution.py:309
  68.4 0.0 collective-permute-done.12.refs_3_
  68.4 1.4 %collective-permute-start.14 = (bf16[128,1024]{1,0:T(8,128)(2,1)S(1)}, bf16[128,1024]{1,0:T(8,128)(2,1)S(1)}, u32[]{:S(2)}, u32[]{:S(2)}) collective-permute-start(bf16[128,1024]{1,0:T(8,128)(2,1)S(1)} %get-tuple-element.85.out_ref.refs_0_), channel_id=1, source_target_pairs={{0,4},{1,5},{2,6},{3,7},{4,0},{5,1},{6,2},{7,3},{8,12},{9,13},{10,... | collective-permute-start | bytes 786440 | tf_op jit(solution)/shard_map/ppermute | solution.py:309
  69.8 1.1 %collective-permute-start.13 = (bf16[128,1024]{1,0:T(8,128)(2,1)S(1)}, bf16[128,1024]{1,0:T(8,128)(2,1)S(1)}, u32[]{:S(2)}, u32[]{:S(2)}) collective-permute-start(bf16[128,1024]{1,0:T(8,128)(2,1)S(1)} %get-tuple-element.85.out_ref.refs_0_), channel_id=1, source_target_pairs={{0,8},{1,9},{2,10},{3,11},{4,12},{5,13},{6,14},{7,15},{8,0},{9,1},... | collective-permute-start | bytes 786440 | tf_op jit(solution)/shard_map/ppermute | solution.py:309
  70.9 4.5 %shard_map.107 = bf16[8,384,128]{2,1,0:T(8,128)(2,1)} custom-call(bf16[1024,128]{1,0:T(8,128)(2,1)S(1)} %get-tuple-element.51.queries_ref, bf16[128,1536]{1,0:T(8,128)(2,1)S(1)} %get-tuple-element.52.keys_t_ref, bf16[1536,128]{1,0:T(8,128)(2,1)S(1)} %get-tuple-element.53.vals_ref, bf16[1536,1024]{1,0:T(8,128)(2,1)S(1)} %get-tuple-element.54.probs_ref, ...), custom_call_target="tpu_custom_call" | custom-call | flops 1610612736 | bytes 6291456 | tf_op jit(solution)/shard_map/pallas_call | solution.py:147
  75.4 4.1 %all-to-all-start.1 = ((bf16[8,384,128]{2,1,0:T(8,128)(2,1)}), bf16[8,384,128]{2,1,0:T(8,128)(2,1)S(1)}, u32[]{:S(2)}, u32[]{:S(2)}) async-start(bf16[8,384,128]{2,1,0:T(8,128)(2,1)} %shard_map.107), calls=%async_computation.1 | async-start | bytes 1572864 | tf_op jit(solution)/shard_map/all_to_all | solution.py:409
  79.4 0.8 collective-permute-done.14.refs_1_
  80.2 4.8 %collective-permute-done.13.refs_2_ = bf16[128,1024]{1,0:T(8,128)(2,1)S(1)} collective-permute-done((bf16[128,1024]{1,0:T(8,128)(2,1)S(1)}, bf16[128,1024]{1,0:T(8,128)(2,1)S(1)}, u32[]{:S(2)}, u32[]{:S(2)}) %collective-permute-start.13) | collective-permute-done | bytes 262176 | tf_op jit(solution)/shard_map/ppermute | solution.py:309
  85.0 0.0 collective-permute-start.15
  85.0 13.5 %collective-permute-done.15.refs_3_ = bf16[128,1024]{1,0:T(8,128)(2,1)S(1)} collective-permute-done((bf16[128,1024]{1,0:T(8,128)(2,1)S(1)}, bf16[128,1024]{1,0:T(8,128)(2,1)S(1)}, u32[]{:S(2)}, u32[]{:S(2)}) %collective-permute-start.15) | collective-permute-done | bytes 262176 | tf_op jit(solution)/shard_map/ppermute | solution.py:309
  98.5 1.1 %copy-done.4 = bf16[512,768]{1,0:T(8,128)(2,1)S(1)} copy-done((bf16[512,768]{1,0:T(8,128)(2,1)S(1)}, bf16[512,768]{1,0:T(8,128)(2,1)}, u32[]{:S(2)}) %copy-start.4) | copy-done | bytes 786456
  99.6 1.3 %shard_map.109 = (bf16[512,384]{1,0:T(8,128)(2,1)S(1)}, bf16[512,384]{1,0:T(8,128)(2,1)S(1)}) custom-call(bf16[512,768]{1,0:T(8,128)(2,1)S(1)} %copy-done.2, bf16[512,768]{1,0:T(8,128)(2,1)S(1)} %copy-done.4, bf16[128,1024]{1,0:T(8,128)(2,1)S(1)} %get-tuple-element.85.out_ref.refs_0_, bf16[128,1024]{1,0:T(8,128)(2,1)S(1)} %collective-permute-done.14.refs_1_, ...), custom_call_target="tpu_custom_call" | custom-call | flops 7247757312 | bytes 1572864 | tf_op jit(solution)/shard_map/pallas_call | solution.py:147
  100.9 1.5 %collective-permute-start.16 = (bf16[512,384]{1,0:T(8,128)(2,1)S(1)}, bf16[512,384]{1,0:T(8,128)(2,1)S(1)}, u32[]{:S(2)}, u32[]{:S(2)}) collective-permute-start(bf16[512,384]{1,0:T(8,128)(2,1)S(1)} %get-tuple-element.89), channel_id=1, source_target_pairs={{0,2},{1,3},{2,0},{3,1},{4,6},{5,7},{6,4},{7,5},{8,10},{9,11},{10,... | collective-permute-start | bytes 1179656 | tf_op jit(solution)/shard_map/ppermute | solution.py:309
  102.4 7.7 %collective-permute-done.16.other_ref = bf16[512,384]{1,0:T(8,128)(2,1)S(1)} collective-permute-done((bf16[512,384]{1,0:T(8,128)(2,1)S(1)}, bf16[512,384]{1,0:T(8,128)(2,1)S(1)}, u32[]{:S(2)}, u32[]{:S(2)}) %collective-permute-start.16) | collective-permute-done | bytes 393248 | tf_op jit(solution)/shard_map/ppermute | solution.py:309
  110.1 1.5 %shard_map.110 = f32[384,1024]{1,0:T(8,128)} custom-call(bf16[512,384]{1,0:T(8,128)(2,1)S(1)} %get-tuple-element.88.own_ref, bf16[512,384]{1,0:T(8,128)(2,1)S(1)} %collective-permute-done.16.other_ref), custom_call_target="tpu_custom_call" | custom-call | bytes 2359296 | tf_op jit(solution)/shard_map/pallas_call | solution.py:147
  111.6 1.1 shard_map.108
  (20 shorter events, 0.2 us)
Async XLA Ops:
  0.6 5.3 %copy-start.6 = (bf16[128,3072]{1,0:T(8,128)(2,1)S(1)}, bf16[128,3072]{1,0:T(8,128)(2,1)}, u32[]{:S(2)}) copy-start(bf16[128,3072]{1,0:T(8,128)(2,1)} %param.13) | copy-start | bytes 2359300
  3.0 19.9 %copy-start = (bf16[384,512]{1,0:T(8,128)(2,1)S(1)}, bf16[384,512]{1,0:T(8,128)(2,1)}, u32[]{:S(2)}) copy-start(bf16[384,512]{1,0:T(8,128)(2,1)} %get-tuple-element.61.own_ref) | copy-start | bytes 1179652
  3.0 15.8 %collective-permute-start.3 = (bf16[384,512]{1,0:T(8,128)(2,1)}, bf16[384,512]{1,0:T(8,128)(2,1)S(1)}, u32[]{:S(2)}, u32[]{:S(2)}) collective-permute-start(bf16[384,512]{1,0:T(8,128)(2,1)} %get-tuple-element.56), channel_id=1, source_target_pairs={{0,2},{1,3},{2,0},{3,1},{4,6},{5,7},{6,4},{7,5},{8,10},{9,11},{10,... | collective-permute-start | bytes 1179656 | tf_op jit(solution)/shard_map/ppermute | solution.py:309
  6.0 6.4 %collective-permute-start = (bf16[64,768]{1,0:T(8,128)(2,1)S(1)}, bf16[64,768]{1,0:T(8,128)(2,1)S(1)}, u32[]{:S(2)}, u32[]{:S(2)}) collective-permute-start(bf16[64,768]{1,0:T(8,128)(2,1)S(1)} %get-tuple-element.93), channel_id=1, source_target_pairs={{0,4},{1,5},{2,6},{3,7},{4,0},{5,1},{6,2},{7,3},{8,12},{9,13},{10,... | collective-permute-start | bytes 294920 | tf_op jit(solution)/shard_map/ppermute | solution.py:309
  7.7 7.9 %collective-permute-start.2 = (bf16[64,768]{1,0:T(8,128)(2,1)S(1)}, bf16[64,768]{1,0:T(8,128)(2,1)S(1)}, u32[]{:S(2)}, u32[]{:S(2)}) collective-permute-start(bf16[64,768]{1,0:T(8,128)(2,1)S(1)} %get-tuple-element.90), channel_id=1, source_target_pairs={{0,12},{1,13},{2,14},{3,15},{4,8},{5,9},{6,10},{7,11},{8,4},{9,5},... | collective-permute-start | bytes 294920 | tf_op jit(solution)/shard_map/ppermute | solution.py:309
  10.1 8.7 %collective-permute-start.1 = (bf16[64,768]{1,0:T(8,128)(2,1)S(1)}, bf16[64,768]{1,0:T(8,128)(2,1)S(1)}, u32[]{:S(2)}, u32[]{:S(2)}) collective-permute-start(bf16[64,768]{1,0:T(8,128)(2,1)S(1)} %get-tuple-element.91), channel_id=1, source_target_pairs={{0,8},{1,9},{2,10},{3,11},{4,12},{5,13},{6,14},{7,15},{8,0},{9,1},... | collective-permute-start | bytes 294920 | tf_op jit(solution)/shard_map/ppermute | solution.py:309
  12.4 41.7 %copy-start.5 = (bf16[2,512,128]{2,1,0:T(8,128)(2,1)S(1)}, bf16[2,512,128]{2,1,0:T(8,128)(2,1)}, u32[]{:S(2)}) copy-start(bf16[2,512,128]{2,1,0:T(8,128)(2,1)} %get-tuple-element.50.text_ref) | copy-start | bytes 786436
  18.9 4.0 %collective-permute-start.5 = (bf16[256,768]{1,0:T(8,128)(2,1)S(1)}, bf16[256,768]{1,0:T(8,128)(2,1)S(1)}, u32[]{:S(2)}, u32[]{:S(2)}) collective-permute-start(bf16[256,768]{1,0:T(8,128)(2,1)S(1)} %constant_dynamic-update-slice_fusion.piece_ref), channel_id=1, source_target_pairs={{0,1},{1,0},{2,3},{3,2},{4,5},{5,4},{6,7},{7,6},{8,9},{9,8},{10,11... | collective-permute-start | bytes 1179656 | tf_op jit(solution)/shard_map/ppermute | solution.py:309
  18.9 35.2 %all-to-all-start = ((bf16[8,384,128]{2,1,0:T(8,128)(2,1)}), bf16[8,384,128]{2,1,0:T(8,128)(2,1)S(1)}, u32[]{:S(2)}, u32[]{:S(2)}) async-start(bf16[8,384,128]{2,1,0:T(8,128)(2,1)} %shard_map.102), calls=%async_computation | async-start | bytes 1572864 | tf_op jit(solution)/shard_map/all_to_all | solution.py:363
  23.8 0.9 copy-start.1
  24.7 15.5 %collective-permute-start.6 = (bf16[512,128]{1,0:T(8,128)(2,1)S(1)}, bf16[512,128]{1,0:T(8,128)(2,1)S(1)}, u32[]{:S(2)}, u32[]{:S(2)}) collective-permute-start(bf16[512,128]{1,0:T(8,128)(2,1)S(1)} %get-tuple-element.64), channel_id=1, source_target_pairs={{0,4},{1,5},{2,6},{3,7},{4,0},{5,1},{6,2},{7,3},{8,12},{9,13},{10,... | collective-permute-start | bytes 393224 | tf_op jit(solution)/shard_map/ppermute | solution.py:309
  26.7 17.9 %collective-permute-start.4 = (bf16[256,768]{1,0:T(8,128)(2,1)S(1)}, bf16[256,768]{1,0:T(8,128)(2,1)S(1)}, u32[]{:S(2)}, u32[]{:S(2)}) collective-permute-start(bf16[256,768]{1,0:T(8,128)(2,1)S(1)} %constant_dynamic-update-slice_fusion.piece_ref), channel_id=1, source_target_pairs={{0,2},{1,3},{2,0},{3,1},{4,6},{5,7},{6,4},{7,5},{8,10},{9,11},{10,... | collective-permute-start | bytes 1179656 | tf_op jit(solution)/shard_map/ppermute | solution.py:309
  28.2 16.4 %collective-permute-start.8 = (bf16[512,128]{1,0:T(8,128)(2,1)S(1)}, bf16[512,128]{1,0:T(8,128)(2,1)S(1)}, u32[]{:S(2)}, u32[]{:S(2)}) collective-permute-start(bf16[512,128]{1,0:T(8,128)(2,1)S(1)} %get-tuple-element.65), channel_id=1, source_target_pairs={{0,4},{1,5},{2,6},{3,7},{4,0},{5,1},{6,2},{7,3},{8,12},{9,13},{10,... | collective-permute-start | bytes 393224 | tf_op jit(solution)/shard_map/ppermute | solution.py:309
  40.3 9.7 %collective-permute-start.7 = (bf16[512,128]{1,0:T(8,128)(2,1)S(1)}, bf16[512,128]{1,0:T(8,128)(2,1)S(1)}, u32[]{:S(2)}, u32[]{:S(2)}) collective-permute-start(bf16[512,128]{1,0:T(8,128)(2,1)S(1)} %add_convert_fusion.1), channel_id=1, source_target_pairs={{0,8},{1,9},{2,10},{3,11},{4,12},{5,13},{6,14},{7,15},{8,0},{9,1},... | collective-permute-start | bytes 393224 | tf_op jit(solution)/shard_map/ppermute | solution.py:309
  49.9 1.7 %collective-permute-start.9 = (bf16[256,768]{1,0:T(8,128)(2,1)S(1)}, bf16[256,768]{1,0:T(8,128)(2,1)S(1)}, u32[]{:S(2)}, u32[]{:S(2)}) collective-permute-start(bf16[256,768]{1,0:T(8,128)(2,1)S(1)} %collective-permute-done.4.piece_ref), channel_id=1, source_target_pairs={{0,1},{1,0},{2,3},{3,2},{4,5},{5,4},{6,7},{7,6},{8,9},{9,8},{10,11... | collective-permute-start | bytes 1179656 | tf_op jit(solution)/shard_map/ppermute | solution.py:309
  53.2 0.9 copy-start.3
  54.1 5.7 %collective-permute-start.10 = (bf16[512,128]{1,0:T(8,128)(2,1)}, bf16[512,128]{1,0:T(8,128)(2,1)S(1)}, u32[]{:S(2)}, u32[]{:S(2)}) collective-permute-start(bf16[512,128]{1,0:T(8,128)(2,1)} %get-tuple-element.67), channel_id=1, source_target_pairs={{0,4},{1,5},{2,6},{3,7},{4,0},{5,1},{6,2},{7,3},{8,12},{9,13},{10,... | collective-permute-start | bytes 393224 | tf_op jit(solution)/shard_map/ppermute | solution.py:309
  59.9 8.5 %collective-permute-start.11 = (bf16[512,128]{1,0:T(8,128)(2,1)S(1)}, bf16[512,128]{1,0:T(8,128)(2,1)S(1)}, u32[]{:S(2)}, u32[]{:S(2)}) collective-permute-start(bf16[512,128]{1,0:T(8,128)(2,1)S(1)} %add_convert_fusion), channel_id=1, source_target_pairs={{0,8},{1,9},{2,10},{3,11},{4,12},{5,13},{6,14},{7,15},{8,0},{9,1},... | collective-permute-start | bytes 393224 | tf_op jit(solution)/shard_map/ppermute | solution.py:309
  61.6 6.8 %collective-permute-start.12 = (bf16[512,128]{1,0:T(8,128)(2,1)S(1)}, bf16[512,128]{1,0:T(8,128)(2,1)S(1)}, u32[]{:S(2)}, u32[]{:S(2)}) collective-permute-start(bf16[512,128]{1,0:T(8,128)(2,1)S(1)} %get-tuple-element.76), channel_id=1, source_target_pairs={{0,4},{1,5},{2,6},{3,7},{4,0},{5,1},{6,2},{7,3},{8,12},{9,13},{10,... | collective-permute-start | bytes 393224 | tf_op jit(solution)/shard_map/ppermute | solution.py:309
  68.4 11.8 %collective-permute-start.14 = (bf16[128,1024]{1,0:T(8,128)(2,1)S(1)}, bf16[128,1024]{1,0:T(8,128)(2,1)S(1)}, u32[]{:S(2)}, u32[]{:S(2)}) collective-permute-start(bf16[128,1024]{1,0:T(8,128)(2,1)S(1)} %get-tuple-element.85.out_ref.refs_0_), channel_id=1, source_target_pairs={{0,4},{1,5},{2,6},{3,7},{4,0},{5,1},{6,2},{7,3},{8,12},{9,13},{10,... | collective-permute-start | bytes 786440 | tf_op jit(solution)/shard_map/ppermute | solution.py:309
  69.8 15.2 %collective-permute-start.13 = (bf16[128,1024]{1,0:T(8,128)(2,1)S(1)}, bf16[128,1024]{1,0:T(8,128)(2,1)S(1)}, u32[]{:S(2)}, u32[]{:S(2)}) collective-permute-start(bf16[128,1024]{1,0:T(8,128)(2,1)S(1)} %get-tuple-element.85.out_ref.refs_0_), channel_id=1, source_target_pairs={{0,8},{1,9},{2,10},{3,11},{4,12},{5,13},{6,14},{7,15},{8,0},{9,1},... | collective-permute-start | bytes 786440 | tf_op jit(solution)/shard_map/ppermute | solution.py:309
  70.9 27.6 %copy-start.2 = (bf16[512,768]{1,0:T(8,128)(2,1)S(1)}, bf16[512,768]{1,0:T(8,128)(2,1)}, u32[]{:S(2)}) copy-start(bf16[512,768]{1,0:T(8,128)(2,1)} %copy-done.1) | copy-start | bytes 2359300
  75.4 36.2 %all-to-all-start.1 = ((bf16[8,384,128]{2,1,0:T(8,128)(2,1)}), bf16[8,384,128]{2,1,0:T(8,128)(2,1)S(1)}, u32[]{:S(2)}, u32[]{:S(2)}) async-start(bf16[8,384,128]{2,1,0:T(8,128)(2,1)} %shard_map.107), calls=%async_computation.1 | async-start | bytes 1572864 | tf_op jit(solution)/shard_map/all_to_all | solution.py:409
  85.0 13.5 %collective-permute-start.15 = (bf16[128,1024]{1,0:T(8,128)(2,1)S(1)}, bf16[128,1024]{1,0:T(8,128)(2,1)S(1)}, u32[]{:S(2)}, u32[]{:S(2)}) collective-permute-start(bf16[128,1024]{1,0:T(8,128)(2,1)S(1)} %collective-permute-done.13.refs_2_), channel_id=1, source_target_pairs={{0,4},{1,5},{2,6},{3,7},{4,0},{5,1},{6,2},{7,3},{8,12},{9,13},{10,... | collective-permute-start | bytes 786440 | tf_op jit(solution)/shard_map/ppermute | solution.py:309
  98.5 1.1 %copy-start.4 = (bf16[512,768]{1,0:T(8,128)(2,1)S(1)}, bf16[512,768]{1,0:T(8,128)(2,1)}, u32[]{:S(2)}) copy-start(bf16[512,768]{1,0:T(8,128)(2,1)} %copy-done.3) | copy-start | bytes 2359300
  100.9 9.2 %collective-permute-start.16 = (bf16[512,384]{1,0:T(8,128)(2,1)S(1)}, bf16[512,384]{1,0:T(8,128)(2,1)S(1)}, u32[]{:S(2)}, u32[]{:S(2)}) collective-permute-start(bf16[512,384]{1,0:T(8,128)(2,1)S(1)} %get-tuple-element.89), channel_id=1, source_target_pairs={{0,2},{1,3},{2,0},{3,1},{4,6},{5,7},{6,4},{7,5},{8,10},{9,11},{10,... | collective-permute-start | bytes 1179656 | tf_op jit(solution)/shard_map/ppermute | solution.py:309

commit v18 on v16

--- a/solution.py
+++ b/solution.py
@@ -389,11 +389,11 @@
         return (kept + received.astype(F32)).astype(BF16)
 
     mine0, kept0, near0, send0, cot0 = partial(row, row_swapped)
-    far0 = exchange(add(kept0, exchange(send0, 2)), 4)
-    near0 = exchange(near0, 2)
-    other_row, far0, near0 = lax.optimization_barrier((other_row, far0, near0))
+    other_row, send0 = lax.optimization_barrier((other_row, exchange(send0, 2)))
     mine1, kept1, near1, send1, cot1 = partial(other_row, other_swapped)
-    send1, out_t, near1 = lax.optimization_barrier((exchange(send1, 2), out_t, near1))
+    send1, sum0, near0 = lax.optimization_barrier((send1, add(kept0, send0), near0))
+    far0, near0, send1 = exchange(sum0, 4), exchange(near0, 2), exchange(send1, 2)
+    send1, out_t, near1, far0, near0 = lax.optimization_barrier((send1, out_t, near1, far0, near0))
     far1 = exchange(add(kept1, send1), 4)
     near1 = exchange(near1, 2)
     out_late, far1, near1 = lax.optimization_barrier((out_t, far1, near1))

time: 103 us -> 108 us (1.049)
  local copies, waits for them, and re-layouts: 3.03 us -> 6.84 us
  starting transfers between devices: 30.8 us -> 28.6 us
  waiting for transfers between devices: 48.7 us -> 50.1 us
    unnamed x17 -> x29, local copies, waits for them, and re-layouts: 2.99 us -> 6.79 us
    ppermute x17, starting transfers between devices: 22.8 us -> 20.5 us  [exchange(): return lax.ppermute(array, ('seq', 'fsdp'), pairs)]
    ppermute x17, waiting for transfers between devices: 48.7 us -> 50 us  [exchange(): return lax.ppermute(array, ('seq', 'fsdp'), pairs)]
  transfers between devices with their start and end apart: 19 -> 19, of which waited for: 10 -> 10; matrix products, arithmetic and copies ran while one was open for 0% -> 1% of each run, Pallas kernels for 16% -> 16%
where the time goes in v18:
time: 108 us; the launch traced here: 107 us
  waiting for transfers between devices  50.1 us (46%)
  starting transfers between devices  28.6 us (26%)
  Pallas kernels  20.1 us (19%)
  local copies, waits for them, and re-layouts  6.84 us (6%)
    ppermute x17, waiting for transfers between devices, exchange(): return lax.ppermute(array, ('seq', 'fsdp'), pairs)  50 us
    ppermute x17, starting transfers between devices, exchange(): return lax.ppermute(array, ('seq', 'fsdp'), pairs)  20.5 us
    pallas_call x9, Pallas kernels, call(): pl.pallas_call(kernel, out_shape=outs, grid_spec=pltpu.PrefetchScalarGrid...  20.1 us
    unnamed x29, local copies, waits for them, and re-layouts  6.79 us
    all_to_all x1, starting transfers between devices, local(): lax.all_to_all(tok_out, 'seq', split_axis=0, concat_axis=0, tiled=True)  4.25 us
    all_to_all x1, starting transfers between devices, local(): lax.all_to_all(grad_out, 'seq', split_axis=0, concat_axis=0, tiled=True)  3.86 us
  transfers between devices with their start and end apart: 19, of which 10 were waited for; matrix products, arithmetic and copies ran while one was open for 1% of the time, Pallas kernels for 16%

profile of v18, /device:TPU:0, one launch (start us, length us, event | category | flops | bytes accessed | tf_op | source)
XLA Modules:
  0.0 107.1 jit_solution(6755023908818336169)
XLA Ops:
  0.6 2.3 %shard_map.103 = (bf16[384,512]{1,0:T(8,128)(2,1)}, bf16[384,512]{1,0:T(8,128)(2,1)}, bf16[2,512,128]{2,1,0:T(8,128)(2,1)}) custom-call(s32[1]{0:T(128)} %bitcast.me_ref, bf16[384,1024]{1,0:T(8,128)(2,1)} %w_ref.1, bf16[512,1024]{1,0:T(8,128)(2,1)} %kt_ref.1, bf16[512,1024]{1,0:T(8,128)(2,1)} %vt_ref.1), custom_call_target="tpu_custom_call" | custom-call | bytes 1572864 | tf_op jit(solution)/shard_map/pallas_call | solution.py:147
  3.0 3.0 %collective-permute-start.3 = (bf16[384,512]{1,0:T(8,128)(2,1)}, bf16[384,512]{1,0:T(8,128)(2,1)S(1)}, u32[]{:S(2)}, u32[]{:S(2)}) collective-permute-start(bf16[384,512]{1,0:T(8,128)(2,1)} %get-tuple-element.60), channel_id=1, source_target_pairs={{0,2},{1,3},{2,0},{3,1},{4,6},{5,7},{6,4},{7,5},{8,10},{9,11},{10,... | collective-permute-start | bytes 1179656 | tf_op jit(solution)/shard_map/ppermute | solution.py:309
  6.0 1.6 %collective-permute-start = (bf16[64,768]{1,0:T(8,128)(2,1)S(1)}, bf16[64,768]{1,0:T(8,128)(2,1)S(1)}, u32[]{:S(2)}, u32[]{:S(2)}) collective-permute-start(bf16[64,768]{1,0:T(8,128)(2,1)S(1)} %get-tuple-element.101), channel_id=1, source_target_pairs={{0,4},{1,5},{2,6},{3,7},{4,0},{5,1},{6,2},{7,3},{8,12},{9,13},{10,... | collective-permute-start | bytes 294920 | tf_op jit(solution)/shard_map/ppermute | solution.py:309
  7.7 2.5 %collective-permute-start.2 = (bf16[64,768]{1,0:T(8,128)(2,1)S(1)}, bf16[64,768]{1,0:T(8,128)(2,1)S(1)}, u32[]{:S(2)}, u32[]{:S(2)}) collective-permute-start(bf16[64,768]{1,0:T(8,128)(2,1)S(1)} %get-tuple-element.98), channel_id=1, source_target_pairs={{0,12},{1,13},{2,14},{3,15},{4,8},{5,9},{6,10},{7,11},{8,4},{9,5},... | collective-permute-start | bytes 294920 | tf_op jit(solution)/shard_map/ppermute | solution.py:309
  10.1 0.1 collective-permute-start.1
  10.2 2.1 %shard_map.102 = bf16[8,384,128]{2,1,0:T(8,128)(2,1)} custom-call(bf16[128,1024]{1,0:T(8,128)(2,1)} %q_ref.1, bf16[128,1024]{1,0:T(8,128)(2,1)} %k_ref.1, bf16[128,1024]{1,0:T(8,128)(2,1)} %v_ref.1), custom_call_target="tpu_custom_call" | custom-call | bytes 1572864 | tf_op jit(solution)/shard_map/pallas_call | solution.py:147
  12.4 4.3 %all-to-all-start = ((bf16[8,384,128]{2,1,0:T(8,128)(2,1)}), bf16[8,384,128]{2,1,0:T(8,128)(2,1)S(1)}, u32[]{:S(2)}, u32[]{:S(2)}) async-start(bf16[8,384,128]{2,1,0:T(8,128)(2,1)} %shard_map.102), calls=%async_computation | async-start | bytes 1572864 | tf_op jit(solution)/shard_map/all_to_all | solution.py:364
  16.6 2.3 %collective-permute-done.1 = bf16[64,768]{1,0:T(8,128)(2,1)S(1)} collective-permute-done((bf16[64,768]{1,0:T(8,128)(2,1)S(1)}, bf16[64,768]{1,0:T(8,128)(2,1)S(1)}, u32[]{:S(2)}, u32[]{:S(2)}) %collective-permute-start.1) | collective-permute-done | bytes 98336 | tf_op jit(solution)/shard_map/ppermute | solution.py:309
  19.0 0.5 collective-permute-start.4
  19.4 16.1 %collective-permute-done.4.piece_ref = bf16[256,768]{1,0:T(8,128)(2,1)S(1)} collective-permute-done((bf16[256,768]{1,0:T(8,128)(2,1)S(1)}, bf16[256,768]{1,0:T(8,128)(2,1)S(1)}, u32[]{:S(2)}, u32[]{:S(2)}) %collective-permute-start.4) | collective-permute-done | bytes 393248 | tf_op jit(solution)/shard_map/ppermute | solution.py:309
  35.5 0.0 collective-permute-start.7
  35.5 0.0 collective-permute-done.5.swapped_ref
  35.5 0.9 shard_map.105
  36.4 0.7 collective-permute-start.6
  37.1 5.3 %collective-permute-done.6 = bf16[512,128]{1,0:T(8,128)(2,1)S(1)} collective-permute-done((bf16[512,128]{1,0:T(8,128)(2,1)S(1)}, bf16[512,128]{1,0:T(8,128)(2,1)S(1)}, u32[]{:S(2)}, u32[]{:S(2)}) %collective-permute-start.6) | collective-permute-done | bytes 131104 | tf_op jit(solution)/shard_map/ppermute | solution.py:309
  42.4 0.7 add_convert_fusion.1
  43.1 0.0 collective-permute-done.7.swapped_ref
  43.1 1.5 %shard_map.106 = (f32[512,128]{1,0:T(8,128)S(1)}, f32[512,128]{1,0:T(8,128)S(1)}, bf16[512,128]{1,0:T(8,128)(2,1)S(1)}, bf16[512,128]{1,0:T(8,128)(2,1)}, bf16[512,768]{1,0:T(8,128)(2,1)S(1)}) custom-call(bf16[256,768]{1,0:T(8,128)(2,1)S(1)} %collective-permute-done.4.piece_ref, bf16[256,768]{1,0:T(8,128)(2,1)S(1)} %collective-permute-done.7.swapped_ref, ...), custom_call_target="tpu_custom_call" | custom-call | flops 402653184 | bytes 786432 | tf_op jit(solution)/shard_map/pallas_call | solution.py:147
  44.6 0.9 copy-done.1
  45.5 0.7 copy-done.10
  46.2 0.6 collective-permute-start.8
  46.8 3.6 %collective-permute-start.9 = (bf16[512,128]{1,0:T(8,128)(2,1)}, bf16[512,128]{1,0:T(8,128)(2,1)S(1)}, u32[]{:S(2)}, u32[]{:S(2)}) collective-permute-start(bf16[512,128]{1,0:T(8,128)(2,1)} %add_convert_fusion.1), channel_id=1, source_target_pairs={{0,8},{1,9},{2,10},{3,11},{4,12},{5,13},{6,14},{7,15},{8,0},{9,1},... | collective-permute-start | bytes 393224 | tf_op jit(solution)/shard_map/ppermute | solution.py:309
  50.4 0.3 collective-permute-start.10
  50.7 0.9 copy-done.3
  51.7 4.9 %shard_map.104 = (bf16[1536,1024]{1,0:T(8,128)(2,1)S(1)}, bf16[128,1024]{1,0:T(8,128)(2,1)S(1)}, bf16[1024,128]{1,0:T(8,128)(2,1)S(1)}, bf16[128,1536]{1,0:T(8,128)(2,1)S(1)}, bf16[1536,128]{1,0:T(8,128)(2,1)S(1)}) custom-call(bf16[8,384,128]{2,1,0:T(8,128)(2,1)S(1)} %all-to-all-done.tok_ref, bf16[2,512,128]{2,1,0:T(8,128)(2,1)S(1)} %copy-done.3), custom_call_target="tpu_custom_call" | custom-call | flops 805306368 | bytes 6291456 | tf_op jit(solution)/shard_map/pallas_call | solution.py:147
  56.6 0.5 collective-permute-done.10.refs_2_
  57.1 2.8 %collective-permute-start.11 = (bf16[512,128]{1,0:T(8,128)(2,1)S(1)}, bf16[512,128]{1,0:T(8,128)(2,1)S(1)}, u32[]{:S(2)}, u32[]{:S(2)}) collective-permute-start(bf16[512,128]{1,0:T(8,128)(2,1)S(1)} %add_convert_fusion), channel_id=1, source_target_pairs={{0,8},{1,9},{2,10},{3,11},{4,12},{5,13},{6,14},{7,15},{8,0},{9,1},... | collective-permute-start | bytes 393224 | tf_op jit(solution)/shard_map/ppermute | solution.py:309
  59.9 1.5 %collective-permute-start.12 = (bf16[512,128]{1,0:T(8,128)(2,1)S(1)}, bf16[512,128]{1,0:T(8,128)(2,1)S(1)}, u32[]{:S(2)}, u32[]{:S(2)}) collective-permute-start(bf16[512,128]{1,0:T(8,128)(2,1)S(1)} %copy-done.11), channel_id=1, source_target_pairs={{0,4},{1,5},{2,6},{3,7},{4,0},{5,1},{6,2},{7,3},{8,12},{9,13},{10,... | collective-permute-start | bytes 393224 | tf_op jit(solution)/shard_map/ppermute | solution.py:309
  61.5 4.6 %collective-permute-done.11.refs_5_ = bf16[512,128]{1,0:T(8,128)(2,1)S(1)} collective-permute-done((bf16[512,128]{1,0:T(8,128)(2,1)S(1)}, bf16[512,128]{1,0:T(8,128)(2,1)S(1)}, u32[]{:S(2)}, u32[]{:S(2)}) %collective-permute-start.11) | collective-permute-done | bytes 131104 | tf_op jit(solution)/shard_map/ppermute | solution.py:309
  66.1 0.5 collective-permute-done.12.refs_3_
  66.6 0.6 collective-permute-start.14
  67.2 2.2 %collective-permute-start.13 = (bf16[128,1024]{1,0:T(8,128)(2,1)S(1)}, bf16[128,1024]{1,0:T(8,128)(2,1)S(1)}, u32[]{:S(2)}, u32[]{:S(2)}) collective-permute-start(bf16[128,1024]{1,0:T(8,128)(2,1)S(1)} %get-tuple-element.93.out_ref.refs_0_), channel_id=1, source_target_pairs={{0,8},{1,9},{2,10},{3,11},{4,12},{5,13},{6,14},{7,15},{8,0},{9,1},... | collective-permute-start | bytes 786440 | tf_op jit(solution)/shard_map/ppermute | solution.py:309
  69.5 4.5 %shard_map.107 = bf16[8,384,128]{2,1,0:T(8,128)(2,1)} custom-call(bf16[1024,128]{1,0:T(8,128)(2,1)S(1)} %get-tuple-element.55.queries_ref, bf16[128,1536]{1,0:T(8,128)(2,1)S(1)} %get-tuple-element.56.keys_t_ref, bf16[1536,128]{1,0:T(8,128)(2,1)S(1)} %get-tuple-element.57.vals_ref, bf16[1536,1024]{1,0:T(8,128)(2,1)S(1)} %get-tuple-element.58.probs_ref, ...), custom_call_target="tpu_custom_call" | custom-call | flops 1610612736 | bytes 6291456 | tf_op jit(solution)/shard_map/pallas_call | solution.py:147
  73.9 5.5 %collective-permute-done.14.refs_1_ = bf16[128,1024]{1,0:T(8,128)(2,1)S(1)} collective-permute-done((bf16[128,1024]{1,0:T(8,128)(2,1)S(1)}, bf16[128,1024]{1,0:T(8,128)(2,1)S(1)}, u32[]{:S(2)}, u32[]{:S(2)}) %collective-permute-start.14) | collective-permute-done | bytes 262176 | tf_op jit(solution)/shard_map/ppermute | solution.py:309
  79.4 0.7 copy-done.4
  80.1 0.5 collective-permute-done.13.refs_2_
  80.7 0.3 collective-permute-start.15
  81.0 3.9 %all-to-all-start.1 = ((bf16[8,384,128]{2,1,0:T(8,128)(2,1)}), bf16[8,384,128]{2,1,0:T(8,128)(2,1)S(1)}, u32[]{:S(2)}, u32[]{:S(2)}) async-start(bf16[8,384,128]{2,1,0:T(8,128)(2,1)} %shard_map.107), calls=%async_computation.1 | async-start | bytes 1572864 | tf_op jit(solution)/shard_map/all_to_all | solution.py:409
  84.9 5.4 %collective-permute-done.15.refs_3_ = bf16[128,1024]{1,0:T(8,128)(2,1)S(1)} collective-permute-done((bf16[128,1024]{1,0:T(8,128)(2,1)S(1)}, bf16[128,1024]{1,0:T(8,128)(2,1)S(1)}, u32[]{:S(2)}, u32[]{:S(2)}) %collective-permute-start.15) | collective-permute-done | bytes 262176 | tf_op jit(solution)/shard_map/ppermute | solution.py:309
  90.2 0.7 copy-done.8
  90.9 0.9 copy-done.5
  91.9 0.9 copy-done.7
  92.8 0.9 copy-done.9
  93.8 1.3 %shard_map.109 = (bf16[512,384]{1,0:T(8,128)(2,1)S(1)}, bf16[512,384]{1,0:T(8,128)(2,1)S(1)}) custom-call(bf16[512,768]{1,0:T(8,128)(2,1)S(1)} %get-tuple-element.91.cot0_ref, bf16[512,768]{1,0:T(8,128)(2,1)S(1)} %copy-done.2, bf16[128,1024]{1,0:T(8,128)(2,1)S(1)} %get-tuple-element.93.out_ref.refs_0_, bf16[128,1024]{1,0:T(8,128)(2,1)S(1)} %copy-done.5, ...), custom_call_target="tpu_custom_call" | custom-call | flops 9663676416 | bytes 1572864 | tf_op jit(solution)/shard_map/pallas_call | solution.py:147
  95.1 0.1 collective-permute-start.16
  95.1 9.4 %collective-permute-done.16.other_ref = bf16[512,384]{1,0:T(8,128)(2,1)S(1)} collective-permute-done((bf16[512,384]{1,0:T(8,128)(2,1)S(1)}, bf16[512,384]{1,0:T(8,128)(2,1)S(1)}, u32[]{:S(2)}, u32[]{:S(2)}) %collective-permute-start.16) | collective-permute-done | bytes 393248 | tf_op jit(solution)/shard_map/ppermute | solution.py:309
  104.5 1.5 %shard_map.110 = f32[384,1024]{1,0:T(8,128)} custom-call(bf16[512,384]{1,0:T(8,128)(2,1)S(1)} %get-tuple-element.96.own_ref, bf16[512,384]{1,0:T(8,128)(2,1)S(1)} %collective-permute-done.16.other_ref), custom_call_target="tpu_custom_call" | custom-call | bytes 2359296 | tf_op jit(solution)/shard_map/pallas_call | solution.py:147
  106.0 1.1 %shard_map.108 = (bf16[128,1024]{1,0:T(8,128)(2,1)}, bf16[128,1024]{1,0:T(8,128)(2,1)}, bf16[128,1024]{1,0:T(8,128)(2,1)}) custom-call(bf16[8,384,128]{2,1,0:T(8,128)(2,1)S(1)} %all-to-all-done.1.tok_ref), custom_call_target="tpu_custom_call" | custom-call | bytes 1572864 | tf_op jit(solution)/shard_map/pallas_call | solution.py:147
  (32 shorter events, 0.2 us)
Async XLA Ops:
  0.6 5.3 %copy-start.12 = (bf16[128,3072]{1,0:T(8,128)(2,1)S(1)}, bf16[128,3072]{1,0:T(8,128)(2,1)}, u32[]{:S(2)}) copy-start(bf16[128,3072]{1,0:T(8,128)(2,1)} %param.13) | copy-start | bytes 2359300
  3.0 32.5 %copy-start = (bf16[384,512]{1,0:T(8,128)(2,1)S(1)}, bf16[384,512]{1,0:T(8,128)(2,1)}, u32[]{:S(2)}) copy-start(bf16[384,512]{1,0:T(8,128)(2,1)} %get-tuple-element.65.own_ref) | copy-start | bytes 1179652
  3.0 15.9 %collective-permute-start.3 = (bf16[384,512]{1,0:T(8,128)(2,1)}, bf16[384,512]{1,0:T(8,128)(2,1)S(1)}, u32[]{:S(2)}, u32[]{:S(2)}) collective-permute-start(bf16[384,512]{1,0:T(8,128)(2,1)} %get-tuple-element.60), channel_id=1, source_target_pairs={{0,2},{1,3},{2,0},{3,1},{4,6},{5,7},{6,4},{7,5},{8,10},{9,11},{10,... | collective-permute-start | bytes 1179656 | tf_op jit(solution)/shard_map/ppermute | solution.py:309
  6.0 6.4 %collective-permute-start = (bf16[64,768]{1,0:T(8,128)(2,1)S(1)}, bf16[64,768]{1,0:T(8,128)(2,1)S(1)}, u32[]{:S(2)}, u32[]{:S(2)}) collective-permute-start(bf16[64,768]{1,0:T(8,128)(2,1)S(1)} %get-tuple-element.101), channel_id=1, source_target_pairs={{0,4},{1,5},{2,6},{3,7},{4,0},{5,1},{6,2},{7,3},{8,12},{9,13},{10,... | collective-permute-start | bytes 294920 | tf_op jit(solution)/shard_map/ppermute | solution.py:309
  7.7 9.0 %collective-permute-start.2 = (bf16[64,768]{1,0:T(8,128)(2,1)S(1)}, bf16[64,768]{1,0:T(8,128)(2,1)S(1)}, u32[]{:S(2)}, u32[]{:S(2)}) collective-permute-start(bf16[64,768]{1,0:T(8,128)(2,1)S(1)} %get-tuple-element.98), channel_id=1, source_target_pairs={{0,12},{1,13},{2,14},{3,15},{4,8},{5,9},{6,10},{7,11},{8,4},{9,5},... | collective-permute-start | bytes 294920 | tf_op jit(solution)/shard_map/ppermute | solution.py:309
  10.1 8.8 %collective-permute-start.1 = (bf16[64,768]{1,0:T(8,128)(2,1)S(1)}, bf16[64,768]{1,0:T(8,128)(2,1)S(1)}, u32[]{:S(2)}, u32[]{:S(2)}) collective-permute-start(bf16[64,768]{1,0:T(8,128)(2,1)S(1)} %get-tuple-element.99), channel_id=1, source_target_pairs={{0,8},{1,9},{2,10},{3,11},{4,12},{5,13},{6,14},{7,15},{8,0},{9,1},... | collective-permute-start | bytes 294920 | tf_op jit(solution)/shard_map/ppermute | solution.py:309
  12.4 38.3 %all-to-all-start = ((bf16[8,384,128]{2,1,0:T(8,128)(2,1)}), bf16[8,384,128]{2,1,0:T(8,128)(2,1)S(1)}, u32[]{:S(2)}, u32[]{:S(2)}) async-start(bf16[8,384,128]{2,1,0:T(8,128)(2,1)} %shard_map.102), calls=%async_computation | async-start | bytes 1572864 | tf_op jit(solution)/shard_map/all_to_all | solution.py:364
  19.0 16.5 %collective-permute-start.4 = (bf16[256,768]{1,0:T(8,128)(2,1)S(1)}, bf16[256,768]{1,0:T(8,128)(2,1)S(1)}, u32[]{:S(2)}, u32[]{:S(2)}) collective-permute-start(bf16[256,768]{1,0:T(8,128)(2,1)S(1)} %constant_dynamic-update-slice_fusion.piece_ref), channel_id=1, source_target_pairs={{0,2},{1,3},{2,0},{3,1},{4,6},{5,7},{6,4},{7,5},{8,10},{9,11},{10,... | collective-permute-start | bytes 1179656 | tf_op jit(solution)/shard_map/ppermute | solution.py:309
  19.4 16.1 %collective-permute-start.5 = (bf16[256,768]{1,0:T(8,128)(2,1)S(1)}, bf16[256,768]{1,0:T(8,128)(2,1)S(1)}, u32[]{:S(2)}, u32[]{:S(2)}) collective-permute-start(bf16[256,768]{1,0:T(8,128)(2,1)S(1)} %constant_dynamic-update-slice_fusion.piece_ref), channel_id=1, source_target_pairs={{0,1},{1,0},{2,3},{3,2},{4,5},{5,4},{6,7},{7,6},{8,9},{9,8},{10,11... | collective-permute-start | bytes 1179656 | tf_op jit(solution)/shard_map/ppermute | solution.py:309
  35.5 7.6 %collective-permute-start.7 = (bf16[256,768]{1,0:T(8,128)(2,1)S(1)}, bf16[256,768]{1,0:T(8,128)(2,1)S(1)}, u32[]{:S(2)}, u32[]{:S(2)}) collective-permute-start(bf16[256,768]{1,0:T(8,128)(2,1)S(1)} %collective-permute-done.4.piece_ref), channel_id=1, source_target_pairs={{0,1},{1,0},{2,3},{3,2},{4,5},{5,4},{6,7},{7,6},{8,9},{9,8},{10,11... | collective-permute-start | bytes 1179656 | tf_op jit(solution)/shard_map/ppermute | solution.py:309
  36.4 6.0 %collective-permute-start.6 = (bf16[512,128]{1,0:T(8,128)(2,1)S(1)}, bf16[512,128]{1,0:T(8,128)(2,1)S(1)}, u32[]{:S(2)}, u32[]{:S(2)}) collective-permute-start(bf16[512,128]{1,0:T(8,128)(2,1)S(1)} %get-tuple-element.67), channel_id=1, source_target_pairs={{0,4},{1,5},{2,6},{3,7},{4,0},{5,1},{6,2},{7,3},{8,12},{9,13},{10,... | collective-permute-start | bytes 393224 | tf_op jit(solution)/shard_map/ppermute | solution.py:309
  44.6 0.9 copy-start.1
  45.5 0.7 copy-start.10
  46.2 10.4 %collective-permute-start.8 = (bf16[512,128]{1,0:T(8,128)(2,1)}, bf16[512,128]{1,0:T(8,128)(2,1)S(1)}, u32[]{:S(2)}, u32[]{:S(2)}) collective-permute-start(bf16[512,128]{1,0:T(8,128)(2,1)} %get-tuple-element.73), channel_id=1, source_target_pairs={{0,4},{1,5},{2,6},{3,7},{4,0},{5,1},{6,2},{7,3},{8,12},{9,13},{10,... | collective-permute-start | bytes 393224 | tf_op jit(solution)/shard_map/ppermute | solution.py:309
  46.8 9.8 %collective-permute-start.9 = (bf16[512,128]{1,0:T(8,128)(2,1)}, bf16[512,128]{1,0:T(8,128)(2,1)S(1)}, u32[]{:S(2)}, u32[]{:S(2)}) collective-permute-start(bf16[512,128]{1,0:T(8,128)(2,1)} %add_convert_fusion.1), channel_id=1, source_target_pairs={{0,8},{1,9},{2,10},{3,11},{4,12},{5,13},{6,14},{7,15},{8,0},{9,1},... | collective-permute-start | bytes 393224 | tf_op jit(solution)/shard_map/ppermute | solution.py:309
  50.4 6.7 %collective-permute-start.10 = (bf16[512,128]{1,0:T(8,128)(2,1)S(1)}, bf16[512,128]{1,0:T(8,128)(2,1)S(1)}, u32[]{:S(2)}, u32[]{:S(2)}) collective-permute-start(bf16[512,128]{1,0:T(8,128)(2,1)S(1)} %get-tuple-element.77), channel_id=1, source_target_pairs={{0,4},{1,5},{2,6},{3,7},{4,0},{5,1},{6,2},{7,3},{8,12},{9,13},{10,... | collective-permute-start | bytes 393224 | tf_op jit(solution)/shard_map/ppermute | solution.py:309
  50.7 1.0 copy-start.3
  51.7 8.3 %copy-start.11 = (bf16[512,128]{1,0:T(8,128)(2,1)S(1)}, bf16[512,128]{1,0:T(8,128)(2,1)}, u32[]{:S(2)}) copy-start(bf16[512,128]{1,0:T(8,128)(2,1)} %copy-done.10) | copy-start | bytes 393220
  57.1 8.9 %collective-permute-start.11 = (bf16[512,128]{1,0:T(8,128)(2,1)S(1)}, bf16[512,128]{1,0:T(8,128)(2,1)S(1)}, u32[]{:S(2)}, u32[]{:S(2)}) collective-permute-start(bf16[512,128]{1,0:T(8,128)(2,1)S(1)} %add_convert_fusion), channel_id=1, source_target_pairs={{0,8},{1,9},{2,10},{3,11},{4,12},{5,13},{6,14},{7,15},{8,0},{9,1},... | collective-permute-start | bytes 393224 | tf_op jit(solution)/shard_map/ppermute | solution.py:309
  59.9 6.7 %collective-permute-start.12 = (bf16[512,128]{1,0:T(8,128)(2,1)S(1)}, bf16[512,128]{1,0:T(8,128)(2,1)S(1)}, u32[]{:S(2)}, u32[]{:S(2)}) collective-permute-start(bf16[512,128]{1,0:T(8,128)(2,1)S(1)} %copy-done.11), channel_id=1, source_target_pairs={{0,4},{1,5},{2,6},{3,7},{4,0},{5,1},{6,2},{7,3},{8,12},{9,13},{10,... | collective-permute-start | bytes 393224 | tf_op jit(solution)/shard_map/ppermute | solution.py:309
  66.6 12.8 %collective-permute-start.14 = (bf16[128,1024]{1,0:T(8,128)(2,1)S(1)}, bf16[128,1024]{1,0:T(8,128)(2,1)S(1)}, u32[]{:S(2)}, u32[]{:S(2)}) collective-permute-start(bf16[128,1024]{1,0:T(8,128)(2,1)S(1)} %get-tuple-element.93.out_ref.refs_0_), channel_id=1, source_target_pairs={{0,4},{1,5},{2,6},{3,7},{4,0},{5,1},{6,2},{7,3},{8,12},{9,13},{10,... | collective-permute-start | bytes 786440 | tf_op jit(solution)/shard_map/ppermute | solution.py:309
  67.2 13.4 %collective-permute-start.13 = (bf16[128,1024]{1,0:T(8,128)(2,1)S(1)}, bf16[128,1024]{1,0:T(8,128)(2,1)S(1)}, u32[]{:S(2)}, u32[]{:S(2)}) collective-permute-start(bf16[128,1024]{1,0:T(8,128)(2,1)S(1)} %get-tuple-element.93.out_ref.refs_0_), channel_id=1, source_target_pairs={{0,8},{1,9},{2,10},{3,11},{4,12},{5,13},{6,14},{7,15},{8,0},{9,1},... | collective-permute-start | bytes 786440 | tf_op jit(solution)/shard_map/ppermute | solution.py:309
  69.4 21.5 %copy-start.2 = (bf16[512,768]{1,0:T(8,128)(2,1)S(1)}, bf16[512,768]{1,0:T(8,128)(2,1)}, u32[]{:S(2)}) copy-start(bf16[512,768]{1,0:T(8,128)(2,1)} %copy-done.1) | copy-start | bytes 2359300
  79.4 0.7 copy-start.4
  80.7 10.3 %copy-start.6 = (bf16[128,1024]{1,0:T(8,128)(2,1)}, bf16[128,1024]{1,0:T(8,128)(2,1)S(1)}, u32[]{:S(2)}) copy-start(bf16[128,1024]{1,0:T(8,128)(2,1)S(1)} %collective-permute-done.13.refs_2_) | copy-start | bytes 786436
  80.7 9.6 %collective-permute-start.15 = (bf16[128,1024]{1,0:T(8,128)(2,1)S(1)}, bf16[128,1024]{1,0:T(8,128)(2,1)S(1)}, u32[]{:S(2)}, u32[]{:S(2)}) collective-permute-start(bf16[128,1024]{1,0:T(8,128)(2,1)S(1)} %collective-permute-done.13.refs_2_), channel_id=1, source_target_pairs={{0,4},{1,5},{2,6},{3,7},{4,0},{5,1},{6,2},{7,3},{8,12},{9,13},{10,... | collective-permute-start | bytes 786440 | tf_op jit(solution)/shard_map/ppermute | solution.py:309
  81.0 25.0 %all-to-all-start.1 = ((bf16[8,384,128]{2,1,0:T(8,128)(2,1)}), bf16[8,384,128]{2,1,0:T(8,128)(2,1)S(1)}, u32[]{:S(2)}, u32[]{:S(2)}) async-start(bf16[8,384,128]{2,1,0:T(8,128)(2,1)} %shard_map.107), calls=%async_computation.1 | async-start | bytes 1572864 | tf_op jit(solution)/shard_map/all_to_all | solution.py:409
  90.2 0.7 copy-start.8
  90.9 1.0 copy-start.5
  91.9 0.9 copy-start.7
  92.8 0.9 copy-start.9
  95.1 9.5 %collective-permute-start.16 = (bf16[512,384]{1,0:T(8,128)(2,1)S(1)}, bf16[512,384]{1,0:T(8,128)(2,1)S(1)}, u32[]{:S(2)}, u32[]{:S(2)}) collective-permute-start(bf16[512,384]{1,0:T(8,128)(2,1)S(1)} %get-tuple-element.97), channel_id=1, source_target_pairs={{0,2},{1,3},{2,0},{3,1},{4,6},{5,7},{6,4},{7,5},{8,10},{9,11},{10,... | collective-permute-start | bytes 1179656 | tf_op jit(solution)/shard_map/ppermute | solution.py:309

commit v19 on v16

--- a/solution.py
+++ b/solution.py
@@ -391,13 +391,14 @@
     mine0, kept0, near0, send0, cot0 = partial(row, row_swapped)
     far0 = exchange(add(kept0, exchange(send0, 2)), 4)
     near0 = exchange(near0, 2)
-    other_row, far0, near0 = lax.optimization_barrier((other_row, far0, near0))
     mine1, kept1, near1, send1, cot1 = partial(other_row, other_swapped)
-    send1, out_t, near1 = lax.optimization_barrier((exchange(send1, 2), out_t, near1))
+    send1, far0, near0, out_t = lax.optimization_barrier((send1, far0, near0, out_t))
+    out_far = exchange(out_t, 4)
+    send1, near1 = lax.optimization_barrier((exchange(send1, 2), near1))
     far1 = exchange(add(kept1, send1), 4)
     near1 = exchange(near1, 2)
-    out_late, far1, near1 = lax.optimization_barrier((out_t, far1, near1))
-    out_near, out_far = exchange(out_late, 2), exchange(out_late, 4)
+    out_late, far1, near1, out_far = lax.optimization_barrier((out_t, far1, near1, out_far))
+    out_near = exchange(out_late, 2)
     (grad_out,) = call(
         functools.partial(backward_kernel, chunk=chunk),
         [shape((n, 3 * rows, HD), BF16)],

time: 103 us -> 107 us (1.039)
  waiting for transfers between devices: 48.7 us -> 54.3 us
  starting transfers between devices: 30.8 us -> 28.6 us
    ppermute x17, waiting for transfers between devices: 48.7 us -> 54.3 us  [exchange(): return lax.ppermute(array, ('seq', 'fsdp'), pairs)]
    ppermute x17, starting transfers between devices: 22.8 us -> 19.6 us  [exchange(): return lax.ppermute(array, ('seq', 'fsdp'), pairs)]
    all_to_all x1, starting transfers between devices: 3.56 us -> 4.66 us  [local(): lax.all_to_all(grad_out, 'seq', split_axis=0, concat_axis=0, tiled=True)]
  transfers between devices with their start and end apart: 19 -> 19, of which waited for: 10 -> 8; matrix products, arithmetic and copies ran while one was open for 0% -> 0% of each run, Pallas kernels for 16% -> 15%
where the time goes in v19:
time: 107 us; the launch traced here: 106 us
  waiting for transfers between devices  54.3 us (51%)
  starting transfers between devices  28.6 us (27%)
  Pallas kernels  19.4 us (18%)
  local copies, waits for them, and re-layouts  3.03 us (3%)
    ppermute x17, waiting for transfers between devices, exchange(): return lax.ppermute(array, ('seq', 'fsdp'), pairs)  54.3 us
    ppermute x17, starting transfers between devices, exchange(): return lax.ppermute(array, ('seq', 'fsdp'), pairs)  19.6 us
    pallas_call x9, Pallas kernels, call(): pl.pallas_call(kernel, out_shape=outs, grid_spec=pltpu.PrefetchScalarGrid...  19.4 us
    all_to_all x1, starting transfers between devices, local(): lax.all_to_all(grad_out, 'seq', split_axis=0, concat_axis=0, tiled=True)  4.66 us
    all_to_all x1, starting transfers between devices, local(): lax.all_to_all(tok_out, 'seq', split_axis=0, concat_axis=0, tiled=True)  4.38 us
    unnamed x17, local copies, waits for them, and re-layouts  2.99 us
  transfers between devices with their start and end apart: 19, of which 8 were waited for; matrix products, arithmetic and copies ran while one was open for 0% of the time, Pallas kernels for 15%

profile of v19, /device:TPU:0, one launch (start us, length us, event | category | flops | bytes accessed | tf_op | source)
XLA Modules:
  0.0 106.3 jit_solution(4899456362579228117)
XLA Ops:
  0.6 2.3 %shard_map.103 = (bf16[384,512]{1,0:T(8,128)(2,1)}, bf16[384,512]{1,0:T(8,128)(2,1)}, bf16[2,512,128]{2,1,0:T(8,128)(2,1)}) custom-call(s32[1]{0:T(128)} %bitcast.me_ref, bf16[384,1024]{1,0:T(8,128)(2,1)} %w_ref.1, bf16[512,1024]{1,0:T(8,128)(2,1)} %kt_ref.1, bf16[512,1024]{1,0:T(8,128)(2,1)} %vt_ref.1), custom_call_target="tpu_custom_call" | custom-call | bytes 1572864 | tf_op jit(solution)/shard_map/pallas_call | solution.py:147
  3.0 3.0 %collective-permute-start.3 = (bf16[384,512]{1,0:T(8,128)(2,1)}, bf16[384,512]{1,0:T(8,128)(2,1)S(1)}, u32[]{:S(2)}, u32[]{:S(2)}) collective-permute-start(bf16[384,512]{1,0:T(8,128)(2,1)} %get-tuple-element.57), channel_id=1, source_target_pairs={{0,2},{1,3},{2,0},{3,1},{4,6},{5,7},{6,4},{7,5},{8,10},{9,11},{10,... | collective-permute-start | bytes 1179656 | tf_op jit(solution)/shard_map/ppermute | solution.py:309
  6.0 1.6 %collective-permute-start = (bf16[64,768]{1,0:T(8,128)(2,1)S(1)}, bf16[64,768]{1,0:T(8,128)(2,1)S(1)}, u32[]{:S(2)}, u32[]{:S(2)}) collective-permute-start(bf16[64,768]{1,0:T(8,128)(2,1)S(1)} %get-tuple-element.95), channel_id=1, source_target_pairs={{0,4},{1,5},{2,6},{3,7},{4,0},{5,1},{6,2},{7,3},{8,12},{9,13},{10,... | collective-permute-start | bytes 294920 | tf_op jit(solution)/shard_map/ppermute | solution.py:309
  7.7 2.5 %collective-permute-start.2 = (bf16[64,768]{1,0:T(8,128)(2,1)S(1)}, bf16[64,768]{1,0:T(8,128)(2,1)S(1)}, u32[]{:S(2)}, u32[]{:S(2)}) collective-permute-start(bf16[64,768]{1,0:T(8,128)(2,1)S(1)} %get-tuple-element.92), channel_id=1, source_target_pairs={{0,12},{1,13},{2,14},{3,15},{4,8},{5,9},{6,10},{7,11},{8,4},{9,5},... | collective-permute-start | bytes 294920 | tf_op jit(solution)/shard_map/ppermute | solution.py:309
  10.1 0.1 collective-permute-start.1
  10.2 2.1 %shard_map.102 = bf16[8,384,128]{2,1,0:T(8,128)(2,1)} custom-call(bf16[128,1024]{1,0:T(8,128)(2,1)} %q_ref.1, bf16[128,1024]{1,0:T(8,128)(2,1)} %k_ref.1, bf16[128,1024]{1,0:T(8,128)(2,1)} %v_ref.1), custom_call_target="tpu_custom_call" | custom-call | bytes 1572864 | tf_op jit(solution)/shard_map/pallas_call | solution.py:147
  12.4 0.0 collective-permute-done
  12.4 4.4 %all-to-all-start = ((bf16[8,384,128]{2,1,0:T(8,128)(2,1)}), bf16[8,384,128]{2,1,0:T(8,128)(2,1)S(1)}, u32[]{:S(2)}, u32[]{:S(2)}) async-start(bf16[8,384,128]{2,1,0:T(8,128)(2,1)} %shard_map.102), calls=%async_computation | async-start | bytes 1572864 | tf_op jit(solution)/shard_map/all_to_all | solution.py:364
  16.8 0.0 collective-permute-done.2
  16.8 2.1 %collective-permute-done.1 = bf16[64,768]{1,0:T(8,128)(2,1)S(1)} collective-permute-done((bf16[64,768]{1,0:T(8,128)(2,1)S(1)}, bf16[64,768]{1,0:T(8,128)(2,1)S(1)}, u32[]{:S(2)}, u32[]{:S(2)}) %collective-permute-start.1) | collective-permute-done | bytes 98336 | tf_op jit(solution)/shard_map/ppermute | solution.py:309
  18.9 0.0 collective-permute-done.3.other_ref
  18.9 0.5 collective-permute-start.4
  19.4 0.0 collective-permute-start.6
  19.4 16.2 %collective-permute-done.4.piece_ref = bf16[256,768]{1,0:T(8,128)(2,1)S(1)} collective-permute-done((bf16[256,768]{1,0:T(8,128)(2,1)S(1)}, bf16[256,768]{1,0:T(8,128)(2,1)S(1)}, u32[]{:S(2)}, u32[]{:S(2)}) %collective-permute-start.4) | collective-permute-done | bytes 393248 | tf_op jit(solution)/shard_map/ppermute | solution.py:309
  35.6 0.0 collective-permute-done.6.swapped_ref
  35.6 0.9 shard_map.106
  36.6 0.9 copy-done.1
  37.5 0.6 collective-permute-start.7
  38.1 1.4 %collective-permute-start.9 = (bf16[512,128]{1,0:T(8,128)(2,1)S(1)}, bf16[512,128]{1,0:T(8,128)(2,1)S(1)}, u32[]{:S(2)}, u32[]{:S(2)}) collective-permute-start(bf16[512,128]{1,0:T(8,128)(2,1)S(1)} %get-tuple-element.67), channel_id=1, source_target_pairs={{0,4},{1,5},{2,6},{3,7},{4,0},{5,1},{6,2},{7,3},{8,12},{9,13},{10,... | collective-permute-start | bytes 393224 | tf_op jit(solution)/shard_map/ppermute | solution.py:309
  39.5 4.3 %collective-permute-done.7 = bf16[512,128]{1,0:T(8,128)(2,1)S(1)} collective-permute-done((bf16[512,128]{1,0:T(8,128)(2,1)S(1)}, bf16[512,128]{1,0:T(8,128)(2,1)S(1)}, u32[]{:S(2)}, u32[]{:S(2)}) %collective-permute-start.7) | collective-permute-done | bytes 131104 | tf_op jit(solution)/shard_map/ppermute | solution.py:309
  43.8 2.3 %collective-permute-start.8 = (bf16[512,128]{1,0:T(8,128)(2,1)S(1)}, bf16[512,128]{1,0:T(8,128)(2,1)S(1)}, u32[]{:S(2)}, u32[]{:S(2)}) collective-permute-start(bf16[512,128]{1,0:T(8,128)(2,1)S(1)} %add_convert_fusion.1), channel_id=1, source_target_pairs={{0,8},{1,9},{2,10},{3,11},{4,12},{5,13},{6,14},{7,15},{8,0},{9,1},... | collective-permute-start | bytes 393224 | tf_op jit(solution)/shard_map/ppermute | solution.py:309
  46.1 0.0 collective-permute-done.5.swapped_ref
  46.1 0.9 shard_map.105
  47.0 0.9 copy-done.3
  47.9 0.0 all-to-all-done.tok_ref
  47.9 4.9 %shard_map.104 = (bf16[1536,1024]{1,0:T(8,128)(2,1)S(1)}, bf16[128,1024]{1,0:T(8,128)(2,1)S(1)}, bf16[1024,128]{1,0:T(8,128)(2,1)S(1)}, bf16[128,1536]{1,0:T(8,128)(2,1)S(1)}, bf16[1536,128]{1,0:T(8,128)(2,1)S(1)}) custom-call(bf16[8,384,128]{2,1,0:T(8,128)(2,1)S(1)} %all-to-all-done.tok_ref, bf16[2,512,128]{2,1,0:T(8,128)(2,1)S(1)} %copy-done.5), custom_call_target="tpu_custom_call" | custom-call | flops 805306368 | bytes 6291456 | tf_op jit(solution)/shard_map/pallas_call | solution.py:147
  52.9 0.0 collective-permute-done.9.refs_2_
  52.9 2.0 %collective-permute-start.10 = (bf16[512,128]{1,0:T(8,128)(2,1)S(1)}, bf16[512,128]{1,0:T(8,128)(2,1)S(1)}, u32[]{:S(2)}, u32[]{:S(2)}) collective-permute-start(bf16[512,128]{1,0:T(8,128)(2,1)S(1)} %get-tuple-element.74), channel_id=1, source_target_pairs={{0,4},{1,5},{2,6},{3,7},{4,0},{5,1},{6,2},{7,3},{8,12},{9,13},{10,... | collective-permute-start | bytes 393224 | tf_op jit(solution)/shard_map/ppermute | solution.py:309
  54.9 1.5 %collective-permute-start.13 = (bf16[128,1024]{1,0:T(8,128)(2,1)S(1)}, bf16[128,1024]{1,0:T(8,128)(2,1)S(1)}, u32[]{:S(2)}, u32[]{:S(2)}) collective-permute-start(bf16[128,1024]{1,0:T(8,128)(2,1)S(1)} %get-tuple-element.87.out_ref.refs_0_), channel_id=1, source_target_pairs={{0,8},{1,9},{2,10},{3,11},{4,12},{5,13},{6,14},{7,15},{8,0},{9,1},... | collective-permute-start | bytes 786440 | tf_op jit(solution)/shard_map/ppermute | solution.py:309
  56.4 3.9 %collective-permute-done.10 = bf16[512,128]{1,0:T(8,128)(2,1)S(1)} collective-permute-done((bf16[512,128]{1,0:T(8,128)(2,1)S(1)}, bf16[512,128]{1,0:T(8,128)(2,1)S(1)}, u32[]{:S(2)}, u32[]{:S(2)}) %collective-permute-start.10) | collective-permute-done | bytes 131104 | tf_op jit(solution)/shard_map/ppermute | solution.py:309
  60.4 1.4 %collective-permute-start.11 = (bf16[512,128]{1,0:T(8,128)(2,1)S(1)}, bf16[512,128]{1,0:T(8,128)(2,1)S(1)}, u32[]{:S(2)}, u32[]{:S(2)}) collective-permute-start(bf16[512,128]{1,0:T(8,128)(2,1)S(1)} %add_convert_fusion), channel_id=1, source_target_pairs={{0,8},{1,9},{2,10},{3,11},{4,12},{5,13},{6,14},{7,15},{8,0},{9,1},... | collective-permute-start | bytes 393224 | tf_op jit(solution)/shard_map/ppermute | solution.py:309
  61.8 2.5 %collective-permute-start.12 = (bf16[512,128]{1,0:T(8,128)(2,1)S(1)}, bf16[512,128]{1,0:T(8,128)(2,1)S(1)}, u32[]{:S(2)}, u32[]{:S(2)}) collective-permute-start(bf16[512,128]{1,0:T(8,128)(2,1)S(1)} %get-tuple-element.77), channel_id=1, source_target_pairs={{0,4},{1,5},{2,6},{3,7},{4,0},{5,1},{6,2},{7,3},{8,12},{9,13},{10,... | collective-permute-start | bytes 393224 | tf_op jit(solution)/shard_map/ppermute | solution.py:309
  64.3 9.8 %collective-permute-done.11.refs_5_ = bf16[512,128]{1,0:T(8,128)(2,1)S(1)} collective-permute-done((bf16[512,128]{1,0:T(8,128)(2,1)S(1)}, bf16[512,128]{1,0:T(8,128)(2,1)S(1)}, u32[]{:S(2)}, u32[]{:S(2)}) %collective-permute-start.11) | collective-permute-done | bytes 131104 | tf_op jit(solution)/shard_map/ppermute | solution.py:309
  74.0 0.0 collective-permute-done.12.refs_3_
  74.0 0.0 collective-permute-done.13.refs_2_
  74.0 0.0 collective-permute-start.14
  74.1 4.5 %shard_map.107 = bf16[8,384,128]{2,1,0:T(8,128)(2,1)} custom-call(bf16[1024,128]{1,0:T(8,128)(2,1)S(1)} %get-tuple-element.52.queries_ref, bf16[128,1536]{1,0:T(8,128)(2,1)S(1)} %get-tuple-element.53.keys_t_ref, bf16[1536,128]{1,0:T(8,128)(2,1)S(1)} %get-tuple-element.54.vals_ref, bf16[1536,1024]{1,0:T(8,128)(2,1)S(1)} %get-tuple-element.55.probs_ref, ...), custom_call_target="tpu_custom_call" | custom-call | flops 1610612736 | bytes 6291456 | tf_op jit(solution)/shard_map/pallas_call | solution.py:147
  78.5 2.3 %collective-permute-done.14.refs_1_ = bf16[128,1024]{1,0:T(8,128)(2,1)S(1)} collective-permute-done((bf16[128,1024]{1,0:T(8,128)(2,1)S(1)}, bf16[128,1024]{1,0:T(8,128)(2,1)S(1)}, u32[]{:S(2)}, u32[]{:S(2)}) %collective-permute-start.14) | collective-permute-done | bytes 262176 | tf_op jit(solution)/shard_map/ppermute | solution.py:309
  80.8 0.0 collective-permute-start.15
  80.8 4.7 %all-to-all-start.1 = ((bf16[8,384,128]{2,1,0:T(8,128)(2,1)}), bf16[8,384,128]{2,1,0:T(8,128)(2,1)S(1)}, u32[]{:S(2)}, u32[]{:S(2)}) async-start(bf16[8,384,128]{2,1,0:T(8,128)(2,1)} %shard_map.107), calls=%async_computation.1 | async-start | bytes 1572864 | tf_op jit(solution)/shard_map/all_to_all | solution.py:410
  85.5 2.8 %collective-permute-done.15.refs_3_ = bf16[128,1024]{1,0:T(8,128)(2,1)S(1)} collective-permute-done((bf16[128,1024]{1,0:T(8,128)(2,1)S(1)}, bf16[128,1024]{1,0:T(8,128)(2,1)S(1)}, u32[]{:S(2)}, u32[]{:S(2)}) %collective-permute-start.15) | collective-permute-done | bytes 262176 | tf_op jit(solution)/shard_map/ppermute | solution.py:309
  88.3 1.1 %copy-done.4 = bf16[512,768]{1,0:T(8,128)(2,1)S(1)} copy-done((bf16[512,768]{1,0:T(8,128)(2,1)S(1)}, bf16[512,768]{1,0:T(8,128)(2,1)}, u32[]{:S(2)}) %copy-start.4) | copy-done | bytes 786456
  89.4 1.3 %shard_map.109 = (bf16[512,384]{1,0:T(8,128)(2,1)S(1)}, bf16[512,384]{1,0:T(8,128)(2,1)S(1)}) custom-call(bf16[512,768]{1,0:T(8,128)(2,1)S(1)} %copy-done.2, bf16[512,768]{1,0:T(8,128)(2,1)S(1)} %copy-done.4, bf16[128,1024]{1,0:T(8,128)(2,1)S(1)} %get-tuple-element.87.out_ref.refs_0_, bf16[128,1024]{1,0:T(8,128)(2,1)S(1)} %collective-permute-done.14.refs_1_, ...), custom_call_target="tpu_custom_call" | custom-call | flops 9663676416 | bytes 1572864 | tf_op jit(solution)/shard_map/pallas_call | solution.py:147
  90.7 0.1 collective-permute-start.16
  90.8 12.9 %collective-permute-done.16.other_ref = bf16[512,384]{1,0:T(8,128)(2,1)S(1)} collective-permute-done((bf16[512,384]{1,0:T(8,128)(2,1)S(1)}, bf16[512,384]{1,0:T(8,128)(2,1)S(1)}, u32[]{:S(2)}, u32[]{:S(2)}) %collective-permute-start.16) | collective-permute-done | bytes 393248 | tf_op jit(solution)/shard_map/ppermute | solution.py:309
  103.7 1.5 %shard_map.110 = f32[384,1024]{1,0:T(8,128)} custom-call(bf16[512,384]{1,0:T(8,128)(2,1)S(1)} %get-tuple-element.90.own_ref, bf16[512,384]{1,0:T(8,128)(2,1)S(1)} %collective-permute-done.16.other_ref), custom_call_target="tpu_custom_call" | custom-call | bytes 2359296 | tf_op jit(solution)/shard_map/pallas_call | solution.py:147
  105.2 0.0 all-to-all-done.1.tok_ref
  105.2 1.1 %shard_map.108 = (bf16[128,1024]{1,0:T(8,128)(2,1)}, bf16[128,1024]{1,0:T(8,128)(2,1)}, bf16[128,1024]{1,0:T(8,128)(2,1)}) custom-call(bf16[8,384,128]{2,1,0:T(8,128)(2,1)S(1)} %all-to-all-done.1.tok_ref), custom_call_target="tpu_custom_call" | custom-call | bytes 1572864 | tf_op jit(solution)/shard_map/pallas_call | solution.py:147
  (20 shorter events, 0.2 us)
Async XLA Ops:
  0.6 5.3 %copy-start.6 = (bf16[128,3072]{1,0:T(8,128)(2,1)S(1)}, bf16[128,3072]{1,0:T(8,128)(2,1)}, u32[]{:S(2)}) copy-start(bf16[128,3072]{1,0:T(8,128)(2,1)} %param.13) | copy-start | bytes 2359300
  3.0 32.6 %copy-start = (bf16[384,512]{1,0:T(8,128)(2,1)S(1)}, bf16[384,512]{1,0:T(8,128)(2,1)}, u32[]{:S(2)}) copy-start(bf16[384,512]{1,0:T(8,128)(2,1)} %get-tuple-element.62.own_ref) | copy-start | bytes 1179652
  3.0 15.9 %collective-permute-start.3 = (bf16[384,512]{1,0:T(8,128)(2,1)}, bf16[384,512]{1,0:T(8,128)(2,1)S(1)}, u32[]{:S(2)}, u32[]{:S(2)}) collective-permute-start(bf16[384,512]{1,0:T(8,128)(2,1)} %get-tuple-element.57), channel_id=1, source_target_pairs={{0,2},{1,3},{2,0},{3,1},{4,6},{5,7},{6,4},{7,5},{8,10},{9,11},{10,... | collective-permute-start | bytes 1179656 | tf_op jit(solution)/shard_map/ppermute | solution.py:309
  6.0 6.4 %collective-permute-start = (bf16[64,768]{1,0:T(8,128)(2,1)S(1)}, bf16[64,768]{1,0:T(8,128)(2,1)S(1)}, u32[]{:S(2)}, u32[]{:S(2)}) collective-permute-start(bf16[64,768]{1,0:T(8,128)(2,1)S(1)} %get-tuple-element.95), channel_id=1, source_target_pairs={{0,4},{1,5},{2,6},{3,7},{4,0},{5,1},{6,2},{7,3},{8,12},{9,13},{10,... | collective-permute-start | bytes 294920 | tf_op jit(solution)/shard_map/ppermute | solution.py:309
  7.7 9.1 %collective-permute-start.2 = (bf16[64,768]{1,0:T(8,128)(2,1)S(1)}, bf16[64,768]{1,0:T(8,128)(2,1)S(1)}, u32[]{:S(2)}, u32[]{:S(2)}) collective-permute-start(bf16[64,768]{1,0:T(8,128)(2,1)S(1)} %get-tuple-element.92), channel_id=1, source_target_pairs={{0,12},{1,13},{2,14},{3,15},{4,8},{5,9},{6,10},{7,11},{8,4},{9,5},... | collective-permute-start | bytes 294920 | tf_op jit(solution)/shard_map/ppermute | solution.py:309
  10.1 8.8 %collective-permute-start.1 = (bf16[64,768]{1,0:T(8,128)(2,1)S(1)}, bf16[64,768]{1,0:T(8,128)(2,1)S(1)}, u32[]{:S(2)}, u32[]{:S(2)}) collective-permute-start(bf16[64,768]{1,0:T(8,128)(2,1)S(1)} %get-tuple-element.93), channel_id=1, source_target_pairs={{0,8},{1,9},{2,10},{3,11},{4,12},{5,13},{6,14},{7,15},{8,0},{9,1},... | collective-permute-start | bytes 294920 | tf_op jit(solution)/shard_map/ppermute | solution.py:309
  12.4 35.6 %copy-start.5 = (bf16[2,512,128]{2,1,0:T(8,128)(2,1)S(1)}, bf16[2,512,128]{2,1,0:T(8,128)(2,1)}, u32[]{:S(2)}) copy-start(bf16[2,512,128]{2,1,0:T(8,128)(2,1)} %get-tuple-element.51.text_ref) | copy-start | bytes 786436
  12.4 35.6 %all-to-all-start = ((bf16[8,384,128]{2,1,0:T(8,128)(2,1)}), bf16[8,384,128]{2,1,0:T(8,128)(2,1)S(1)}, u32[]{:S(2)}, u32[]{:S(2)}) async-start(bf16[8,384,128]{2,1,0:T(8,128)(2,1)} %shard_map.102), calls=%async_computation | async-start | bytes 1572864 | tf_op jit(solution)/shard_map/all_to_all | solution.py:364
  18.9 16.7 %collective-permute-start.4 = (bf16[256,768]{1,0:T(8,128)(2,1)S(1)}, bf16[256,768]{1,0:T(8,128)(2,1)S(1)}, u32[]{:S(2)}, u32[]{:S(2)}) collective-permute-start(bf16[256,768]{1,0:T(8,128)(2,1)S(1)} %constant_dynamic-update-slice_fusion.piece_ref), channel_id=1, source_target_pairs={{0,2},{1,3},{2,0},{3,1},{4,6},{5,7},{6,4},{7,5},{8,10},{9,11},{10,... | collective-permute-start | bytes 1179656 | tf_op jit(solution)/shard_map/ppermute | solution.py:309
  19.4 16.2 %collective-permute-start.6 = (bf16[256,768]{1,0:T(8,128)(2,1)S(1)}, bf16[256,768]{1,0:T(8,128)(2,1)S(1)}, u32[]{:S(2)}, u32[]{:S(2)}) collective-permute-start(bf16[256,768]{1,0:T(8,128)(2,1)S(1)} %constant_dynamic-update-slice_fusion.piece_ref), channel_id=1, source_target_pairs={{0,1},{1,0},{2,3},{3,2},{4,5},{5,4},{6,7},{7,6},{8,9},{9,8},{10,11... | collective-permute-start | bytes 1179656 | tf_op jit(solution)/shard_map/ppermute | solution.py:309
  35.6 10.5 %collective-permute-start.5 = (bf16[256,768]{1,0:T(8,128)(2,1)S(1)}, bf16[256,768]{1,0:T(8,128)(2,1)S(1)}, u32[]{:S(2)}, u32[]{:S(2)}) collective-permute-start(bf16[256,768]{1,0:T(8,128)(2,1)S(1)} %collective-permute-done.4.piece_ref), channel_id=1, source_target_pairs={{0,1},{1,0},{2,3},{3,2},{4,5},{5,4},{6,7},{7,6},{8,9},{9,8},{10,11... | collective-permute-start | bytes 1179656 | tf_op jit(solution)/shard_map/ppermute | solution.py:309
  36.5 0.9 copy-start.1
  37.5 6.3 %collective-permute-start.7 = (bf16[512,128]{1,0:T(8,128)(2,1)S(1)}, bf16[512,128]{1,0:T(8,128)(2,1)S(1)}, u32[]{:S(2)}, u32[]{:S(2)}) collective-permute-start(bf16[512,128]{1,0:T(8,128)(2,1)S(1)} %get-tuple-element.66), channel_id=1, source_target_pairs={{0,4},{1,5},{2,6},{3,7},{4,0},{5,1},{6,2},{7,3},{8,12},{9,13},{10,... | collective-permute-start | bytes 393224 | tf_op jit(solution)/shard_map/ppermute | solution.py:309
  38.1 14.8 %collective-permute-start.9 = (bf16[512,128]{1,0:T(8,128)(2,1)S(1)}, bf16[512,128]{1,0:T(8,128)(2,1)S(1)}, u32[]{:S(2)}, u32[]{:S(2)}) collective-permute-start(bf16[512,128]{1,0:T(8,128)(2,1)S(1)} %get-tuple-element.67), channel_id=1, source_target_pairs={{0,4},{1,5},{2,6},{3,7},{4,0},{5,1},{6,2},{7,3},{8,12},{9,13},{10,... | collective-permute-start | bytes 393224 | tf_op jit(solution)/shard_map/ppermute | solution.py:309
  43.8 9.1 %collective-permute-start.8 = (bf16[512,128]{1,0:T(8,128)(2,1)S(1)}, bf16[512,128]{1,0:T(8,128)(2,1)S(1)}, u32[]{:S(2)}, u32[]{:S(2)}) collective-permute-start(bf16[512,128]{1,0:T(8,128)(2,1)S(1)} %add_convert_fusion.1), channel_id=1, source_target_pairs={{0,8},{1,9},{2,10},{3,11},{4,12},{5,13},{6,14},{7,15},{8,0},{9,1},... | collective-permute-start | bytes 393224 | tf_op jit(solution)/shard_map/ppermute | solution.py:309
  47.0 0.9 copy-start.3
  52.9 7.5 %collective-permute-start.10 = (bf16[512,128]{1,0:T(8,128)(2,1)S(1)}, bf16[512,128]{1,0:T(8,128)(2,1)S(1)}, u32[]{:S(2)}, u32[]{:S(2)}) collective-permute-start(bf16[512,128]{1,0:T(8,128)(2,1)S(1)} %get-tuple-element.74), channel_id=1, source_target_pairs={{0,4},{1,5},{2,6},{3,7},{4,0},{5,1},{6,2},{7,3},{8,12},{9,13},{10,... | collective-permute-start | bytes 393224 | tf_op jit(solution)/shard_map/ppermute | solution.py:309
  54.9 19.2 %collective-permute-start.13 = (bf16[128,1024]{1,0:T(8,128)(2,1)S(1)}, bf16[128,1024]{1,0:T(8,128)(2,1)S(1)}, u32[]{:S(2)}, u32[]{:S(2)}) collective-permute-start(bf16[128,1024]{1,0:T(8,128)(2,1)S(1)} %get-tuple-element.87.out_ref.refs_0_), channel_id=1, source_target_pairs={{0,8},{1,9},{2,10},{3,11},{4,12},{5,13},{6,14},{7,15},{8,0},{9,1},... | collective-permute-start | bytes 786440 | tf_op jit(solution)/shard_map/ppermute | solution.py:309
  60.4 13.6 %collective-permute-start.11 = (bf16[512,128]{1,0:T(8,128)(2,1)S(1)}, bf16[512,128]{1,0:T(8,128)(2,1)S(1)}, u32[]{:S(2)}, u32[]{:S(2)}) collective-permute-start(bf16[512,128]{1,0:T(8,128)(2,1)S(1)} %add_convert_fusion), channel_id=1, source_target_pairs={{0,8},{1,9},{2,10},{3,11},{4,12},{5,13},{6,14},{7,15},{8,0},{9,1},... | collective-permute-start | bytes 393224 | tf_op jit(solution)/shard_map/ppermute | solution.py:309
  61.8 12.2 %collective-permute-start.12 = (bf16[512,128]{1,0:T(8,128)(2,1)S(1)}, bf16[512,128]{1,0:T(8,128)(2,1)S(1)}, u32[]{:S(2)}, u32[]{:S(2)}) collective-permute-start(bf16[512,128]{1,0:T(8,128)(2,1)S(1)} %get-tuple-element.77), channel_id=1, source_target_pairs={{0,4},{1,5},{2,6},{3,7},{4,0},{5,1},{6,2},{7,3},{8,12},{9,13},{10,... | collective-permute-start | bytes 393224 | tf_op jit(solution)/shard_map/ppermute | solution.py:309
  74.0 6.8 %collective-permute-start.14 = (bf16[128,1024]{1,0:T(8,128)(2,1)S(1)}, bf16[128,1024]{1,0:T(8,128)(2,1)S(1)}, u32[]{:S(2)}, u32[]{:S(2)}) collective-permute-start(bf16[128,1024]{1,0:T(8,128)(2,1)S(1)} %get-tuple-element.87.out_ref.refs_0_), channel_id=1, source_target_pairs={{0,4},{1,5},{2,6},{3,7},{4,0},{5,1},{6,2},{7,3},{8,12},{9,13},{10,... | collective-permute-start | bytes 786440 | tf_op jit(solution)/shard_map/ppermute | solution.py:309
  74.1 14.2 %copy-start.2 = (bf16[512,768]{1,0:T(8,128)(2,1)S(1)}, bf16[512,768]{1,0:T(8,128)(2,1)}, u32[]{:S(2)}) copy-start(bf16[512,768]{1,0:T(8,128)(2,1)} %copy-done.1) | copy-start | bytes 2359300
  80.8 7.5 %collective-permute-start.15 = (bf16[128,1024]{1,0:T(8,128)(2,1)S(1)}, bf16[128,1024]{1,0:T(8,128)(2,1)S(1)}, u32[]{:S(2)}, u32[]{:S(2)}) collective-permute-start(bf16[128,1024]{1,0:T(8,128)(2,1)S(1)} %collective-permute-done.13.refs_2_), channel_id=1, source_target_pairs={{0,4},{1,5},{2,6},{3,7},{4,0},{5,1},{6,2},{7,3},{8,12},{9,13},{10,... | collective-permute-start | bytes 786440 | tf_op jit(solution)/shard_map/ppermute | solution.py:309
  80.8 24.3 %all-to-all-start.1 = ((bf16[8,384,128]{2,1,0:T(8,128)(2,1)}), bf16[8,384,128]{2,1,0:T(8,128)(2,1)S(1)}, u32[]{:S(2)}, u32[]{:S(2)}) async-start(bf16[8,384,128]{2,1,0:T(8,128)(2,1)} %shard_map.107), calls=%async_computation.1 | async-start | bytes 1572864 | tf_op jit(solution)/shard_map/all_to_all | solution.py:410
  88.3 1.1 %copy-start.4 = (bf16[512,768]{1,0:T(8,128)(2,1)S(1)}, bf16[512,768]{1,0:T(8,128)(2,1)}, u32[]{:S(2)}) copy-start(bf16[512,768]{1,0:T(8,128)(2,1)} %copy-done.3) | copy-start | bytes 2359300
  90.7 13.0 %collective-permute-start.16 = (bf16[512,384]{1,0:T(8,128)(2,1)S(1)}, bf16[512,384]{1,0:T(8,128)(2,1)S(1)}, u32[]{:S(2)}, u32[]{:S(2)}) collective-permute-start(bf16[512,384]{1,0:T(8,128)(2,1)S(1)} %get-tuple-element.91), channel_id=1, source_target_pairs={{0,2},{1,3},{2,0},{3,1},{4,6},{5,7},{6,4},{7,5},{8,10},{9,11},{10,... | collective-permute-start | bytes 1179656 | tf_op jit(solution)/shard_map/ppermute | solution.py:309

commit v20 on v18

--- a/solution.py
+++ b/solution.py
@@ -166,18 +166,11 @@
     return pl.ds(pl.multiple_of(jnp.bitwise_xor(lax.axis_index("seq"), step + other_row) * HD, HD), HD)
 
 
-def pack_kernel(q_ref, k_ref, v_ref, tok_ref):
+def pack_kernel(me_ref, q_ref, k_ref, v_ref, kt_ref, vt_ref, tok_ref, text_ref):
     rows = q_ref.shape[0]
     for h in range(tok_ref.shape[0]):
         for i, ref in enumerate((q_ref, k_ref, v_ref)):
             tok_ref[h, i * rows : (i + 1) * rows, :] = ref[:, h * HD : (h + 1) * HD]
-
-
-def pack_weight_kernel(me_ref, w_ref, kt_ref, vt_ref, keep_ref, give_ref, text_ref):
-    for i, step in enumerate(STEPS):
-        cols = slice(i * HD, (i + 1) * HD)
-        keep_ref[:, cols] = w_ref[:, head_columns(step, 0)]
-        give_ref[:, cols] = w_ref[:, head_columns(step, 1)]
     text_ref[0] = kt_ref[...]
     text_ref[1] = vt_ref[...]
 
@@ -212,44 +205,42 @@
         out_ref[:, span] = jnp.dot(vals_t[...], low, preferred_element_type=F32).astype(BF16)
 
 
-def partial_kernel(piece_ref, swapped_ref, own_ref, other_ref, *refs):
-    mine_ref, far_ref, near_ref, send_ref, cot_ref, weight = refs
+def place_rows(piece_ref, swapped_ref, cot, start):
     me = lax.axis_index("seq")
     core = lax.axis_index("fsdp")
     part = piece_ref.shape[0] // len(STEPS)
     for piece, shift in ((piece_ref, core), (swapped_ref, 1 - core)):
         for i, step in enumerate(STEPS):
             z = jnp.bitwise_xor(me, step) // 2
-            at = pl.multiple_of(z * (2 * part) + shift * part, 16)
-            cot_ref[pl.ds(at, part), :] = piece[i * part : (i + 1) * part, :]
+            at = pl.multiple_of(start + z * (2 * part) + shift * part, 16)
+            cot[pl.ds(at, part), :] = piece[i * part : (i + 1) * part, :]
+
+
+def partial_kernel(piece_ref, swapped_ref, own_ref, other_ref, mine_ref, near_ref, far_ref, send_ref, cot, weight):
+    place_rows(piece_ref, swapped_ref, cot, 0)
+    me = lax.axis_index("seq")
     depth = own_ref.shape[0]
     y = lax.rem(me, 2)
     weight[pl.ds(pl.multiple_of(y * depth, 16), depth), :] = own_ref[...]
     weight[pl.ds(pl.multiple_of((1 - y) * depth, 16), depth), :] = other_ref[...]
-    step = 256
-
-    @pl.loop(0, cot_ref.shape[0] // step)
-    def _(i):
-        at = pl.ds(pl.multiple_of(i * step, step), step)
-        part = jnp.dot(cot_ref[at, :], weight[...], preferred_element_type=F32)
-        mine_ref[at, :] = part[:, :HD]
-        near_ref[at, :] = part[:, HD : 2 * HD].astype(BF16)
-        far_ref[at, :] = part[:, 2 * HD : 3 * HD]
-        send_ref[at, :] = part[:, 3 * HD :].astype(BF16)
-
-
-def weight_grad_kernel(cot0_ref, cot1_ref, *refs):
-    *out_refs, own_ref, other_ref, outs = refs
-    for i, ref in enumerate(out_refs):
+    for step, ref in zip(STEPS, (mine_ref, near_ref, far_ref, send_ref)):
+        z = jnp.bitwise_xor(me, step) // 2
+        cols = pl.ds(pl.multiple_of(z * 2 * HD, 2 * HD), 2 * HD)
+        ref[...] = jnp.dot(cot[...], weight[:, cols], preferred_element_type=F32).astype(ref.dtype)
+
+
+def weight_grad_kernel(*refs):
+    *pieces, out0, out1, out2, out3, own_ref, other_ref, cot, outs = refs
+    tokens = cot.shape[0]
+    place_rows(pieces[0], pieces[1], cot, 0)
+    place_rows(pieces[2], pieces[3], cot, tokens // 2)
+    for i, ref in enumerate((out0, out1, out2, out3)):
         outs[i * HD : (i + 1) * HD, :] = ref[...]
     depth = own_ref.shape[1]
-    tokens = cot0_ref.shape[0]
     y = lax.rem(lax.axis_index("seq"), 2)
     for ref, row in ((own_ref, y), (other_ref, 1 - y)):
         cols = pl.ds(pl.multiple_of(row * depth, HD), depth)
-        total = jnp.dot(outs[:, :tokens], cot0_ref[:, cols], preferred_element_type=F32)
-        total += jnp.dot(outs[:, tokens:], cot1_ref[:, cols], preferred_element_type=F32)
-        ref[...] = total.astype(BF16)
+        ref[...] = jnp.dot(outs[...], cot[:, cols], preferred_element_type=F32).astype(BF16)
 
 
 def backward_kernel(queries_ref, keys_t_ref, vals_ref, probs_ref, out_ref, *refs, chunk):
@@ -264,9 +255,7 @@
     for c in range(image // chunk):
         span = slice(c * chunk, (c + 1) * chunk)
         within = slice(c % half * chunk, (c % half + 1) * chunk)
-        mine_ref, near_ref, far_ref = grad_refs[c // half :: 2]
-        grads = mine_ref[within, :] + near_ref[within, :].astype(F32) + far_ref[within, :].astype(F32)
-        grads = grads.astype(BF16)
+        grads = grad_refs[c // half][within, :]
         row_dot = jnp.sum(
             grads.astype(F32).T * out_ref[:, span].astype(F32), axis=0, keepdims=True
         )
@@ -335,32 +324,21 @@
     vmem = pl.BlockSpec(memory_space=pltpu.VMEM)
 
     head = pl.BlockSpec((text, HD), lambda i, me_ref: (0, me_ref[0]))
-    big = 60 * 1024 * 1024
-    keep, give, text_head = call(
-        pack_weight_kernel,
-        [shape((depth, 4 * HD), BF16)] * 2 + [shape((2, text, HD), BF16)],
-        [lax.axis_index("seq").astype(jnp.int32)[None], out_weight, k_txt, v_txt],
-        specs=[vmem] + [head] * 2,
+    given = exchange(out_weight, 1)
+    along = send_cotangents(d_out)
+    tok_out, text_head = call(
+        pack_kernel,
+        [shape((n, 3 * rows, HD), BF16), shape((2, text, HD), BF16)],
+        [lax.axis_index("seq").astype(jnp.int32)[None], q_img, k_img, v_img, k_txt, v_txt],
+        specs=[vmem] * 3 + [head] * 2,
         scalars=1,
-        moved=4 * depth * width,
-        limit=big,
-    )
-    d_out, give = lax.optimization_barrier((d_out, give))
-    given = exchange(give, 1)
-    along = send_cotangents(d_out)
-    (tok_out,) = call(
-        pack_kernel,
-        [shape((n, 3 * rows, HD), BF16)],
-        [q_img, k_img, v_img],
         moved=4 * 3 * rows * width,
-        limit=big,
+        limit=60 * 1024 * 1024,
     )
     tok_out, along[1] = lax.optimization_barrier((tok_out, along[1]))
     along, given = lax.optimization_barrier((along, given))
     row = jnp.concatenate(along, axis=0)
     row_swapped = exchange(row, cores=True)
-    other_row = exchange(row, 1)
-    other_swapped = exchange(other_row, cores=True)
     tok_in = lax.all_to_all(tok_out, "seq", split_axis=0, concat_axis=0, tiled=True)
 
     probs, out_t, queries, keys_t, vals = call(
@@ -372,36 +350,30 @@
         moved=4 * total * image,
     )
     columns = row.shape[1]
-
-    def partial(*operands):
-        return call(
-            partial_kernel,
-            [shape((image // 2, HD), F32)] * 2
-            + [shape((image // 2, HD), BF16)] * 2
-            + [shape((image // 2, columns), BF16)],
-            [*operands, keep, given],
-            scratch=[pltpu.VMEM((columns, 4 * HD), BF16)],
-            flops=4 * image * columns * HD,
-            moved=image * columns,
-        )
-
-    def add(kept, received):
-        return (kept + received.astype(F32)).astype(BF16)
-
-    mine0, kept0, near0, send0, cot0 = partial(row, row_swapped)
-    other_row, send0 = lax.optimization_barrier((other_row, exchange(send0, 2)))
-    mine1, kept1, near1, send1, cot1 = partial(other_row, other_swapped)
-    send1, sum0, near0 = lax.optimization_barrier((send1, add(kept0, send0), near0))
-    far0, near0, send1 = exchange(sum0, 4), exchange(near0, 2), exchange(send1, 2)
-    send1, out_t, near1, far0, near0 = lax.optimization_barrier((send1, out_t, near1, far0, near0))
-    far1 = exchange(add(kept1, send1), 4)
-    near1 = exchange(near1, 2)
-    out_late, far1, near1 = lax.optimization_barrier((out_t, far1, near1))
+    mine, near, far, send = call(
+        partial_kernel,
+        [shape((image // 2, 2 * HD), kind) for kind in (F32, BF16, F32, BF16)],
+        [row, row_swapped, out_weight, given],
+        scratch=[pltpu.VMEM((image // 2, columns), BF16), pltpu.VMEM((columns, width), BF16)],
+        flops=8 * image * columns * HD,
+        moved=2 * image * columns,
+    )
+    send, out_t, near = lax.optimization_barrier((exchange(send, 2), out_t, near))
+    far = exchange((far + send.astype(F32)).astype(BF16), 4)
+    near = exchange(near, 2)
+    heads = mine + near.astype(F32) + far.astype(F32)
+    first_row = lax.axis_index("seq") % 2 == 0
+    kept = jnp.where(first_row, heads[:, :HD], heads[:, HD:]).astype(BF16)
+    got = exchange(jnp.where(first_row, heads[:, HD:], heads[:, :HD]).astype(BF16), 1)
+    row, _ = lax.optimization_barrier((row, out_t))
+    other_row = exchange(row, 1)
+    out_late, got, other_row = lax.optimization_barrier((out_t, got, other_row))
+    other_swapped = exchange(other_row, cores=True)
     out_near, out_far = exchange(out_late, 2), exchange(out_late, 4)
     (grad_out,) = call(
         functools.partial(backward_kernel, chunk=chunk),
         [shape((n, 3 * rows, HD), BF16)],
-        [queries, keys_t, vals, probs, out_t, mine0, mine1, near0, near1, far0, far1],
+        [queries, keys_t, vals, probs, out_t, kept, got],
         scratch=[pltpu.VMEM((image, HD), F32), pltpu.VMEM((image, HD), F32)],
         flops=8 * total * image * HD,
         moved=4 * total * image,
@@ -412,8 +384,8 @@
     dw_own, dw_other = call(
         weight_grad_kernel,
         [shape((4 * HD, depth), BF16)] * 2,
-        [cot0, cot1, *outs],
-        scratch=[pltpu.VMEM((4 * HD, image), BF16)],
+        [row, row_swapped, other_row, other_swapped, *outs],
+        scratch=[pltpu.VMEM((image, columns), BF16), pltpu.VMEM((4 * HD, image), BF16)],
         flops=96 * image * columns * HD,
         moved=2 * image * columns,
     )

time: 108 us -> 119 us (1.10)
  local copies, waits for them, and re-layouts: 6.84 us -> 13.7 us
  waiting for transfers between devices: 50.1 us -> 53.5 us
  starting transfers between devices: 28.6 us -> 30.9 us
  Pallas kernels: 20.1 us -> 18.4 us
    unnamed x29 -> x39, local copies, waits for them, and re-layouts: 6.79 us -> 12.7 us
    ppermute x17 -> x15, waiting for transfers between devices: 50 us -> 53.5 us  [exchange(): return lax.ppermute(array, ('seq', 'fsdp'), pairs)]
    pallas_call x9 -> x7, Pallas kernels: 20.1 us -> 18.4 us  [call(): pl.pallas_call(kernel, out_shape=outs, grid_spec=pltpu.PrefetchScalarGrid...]
    ppermute x17 -> x15, starting transfers between devices: 20.5 us -> 21.5 us  [exchange(): return lax.ppermute(array, ('seq', 'fsdp'), pairs)]
  transfers between devices with their start and end apart: 19 -> 17, of which waited for: 10 -> 9; matrix products, arithmetic and copies ran while one was open for 1% -> 1% of each run, Pallas kernels for 16% -> 15%
where the time goes in v20:
time: 119 us
  waiting for transfers between devices  53.5 us (45%)
  starting transfers between devices  30.9 us (26%)
  Pallas kernels  18.4 us (15%)
  local copies, waits for them, and re-layouts  13.7 us (12%)
  other arithmetic  1.3 us (1%)
    ppermute x15, waiting for transfers between devices, exchange(): return lax.ppermute(array, ('seq', 'fsdp'), pairs)  53.5 us
    ppermute x15, starting transfers between devices, exchange(): return lax.ppermute(array, ('seq', 'fsdp'), pairs)  21.5 us
    pallas_call x7, Pallas kernels, call(): pl.pallas_call(kernel, out_shape=outs, grid_spec=pltpu.PrefetchScalarGrid...  18.4 us
    unnamed x39, local copies, waits for them, and re-layouts  12.7 us
    all_to_all x1, starting transfers between devices, local(): lax.all_to_all(tok_out, 'seq', split_axis=0, concat_axis=0, tiled=True)  4.88 us
    all_to_all x1, starting transfers between devices, local(): lax.all_to_all(grad_out, 'seq', split_axis=0, concat_axis=0, tiled=True)  4.44 us
  transfers between devices with their start and end apart: 17, of which 9 were waited for; matrix products, arithmetic and copies ran while one was open for 1% of the time, Pallas kernels for 15%

profile of v20, /device:TPU:0, one launch (start us, length us, event | category | flops | bytes accessed | tf_op | source)
XLA Modules:
  0.0 118.6 jit_solution(7701165234816843005)
XLA Ops:
  0.6 3.0 %collective-permute-start.3 = (bf16[384,1024]{1,0:T(8,128)(2,1)}, bf16[384,1024]{1,0:T(8,128)(2,1)S(1)}, u32[]{:S(2)}, u32[]{:S(2)}) collective-permute-start(bf16[384,1024]{1,0:T(8,128)(2,1)} %own_ref.1), channel_id=1, source_target_pairs={{0,2},{1,3},{2,0},{3,1},{4,6},{5,7},{6,4},{7,5},{8,10},{9,11},{10,... | collective-permute-start | bytes 2359304 | tf_op jit(solution)/shard_map/ppermute | solution.py:298
  3.7 1.1 fusion
  4.7 1.6 %collective-permute-start = (bf16[64,768]{1,0:T(8,128)(2,1)S(1)}, bf16[64,768]{1,0:T(8,128)(2,1)S(1)}, u32[]{:S(2)}, u32[]{:S(2)}) collective-permute-start(bf16[64,768]{1,0:T(8,128)(2,1)S(1)} %get-tuple-element.70), channel_id=1, source_target_pairs={{0,4},{1,5},{2,6},{3,7},{4,0},{5,1},{6,2},{7,3},{8,12},{9,13},{10,... | collective-permute-start | bytes 294920 | tf_op jit(solution)/shard_map/ppermute | solution.py:298
  6.4 2.3 %shard_map.102 = (bf16[8,384,128]{2,1,0:T(8,128)(2,1)}, bf16[2,512,128]{2,1,0:T(8,128)(2,1)}) custom-call(s32[1]{0:T(128)} %bitcast.me_ref, bf16[128,1024]{1,0:T(8,128)(2,1)} %q_ref.1, bf16[128,1024]{1,0:T(8,128)(2,1)} %k_ref.1, bf16[128,1024]{1,0:T(8,128)(2,1)} %v_ref.1, bf16[512,1024]{1,0:T(8,128)(2,1)} %kt_ref.1, bf16[512,1024]{1,0:T(8,128)(2,1)} %vt_ref.1), custom_call_target="tpu_custom_call" | custom-call | bytes 1572864 | tf_op jit(solution)/shard_map/pallas_call | solution.py:147
  8.7 0.7 collective-permute-done
  9.4 4.9 %all-to-all-start = ((bf16[8,384,128]{2,1,0:T(8,128)(2,1)}), bf16[8,384,128]{2,1,0:T(8,128)(2,1)S(1)}, u32[]{:S(2)}, u32[]{:S(2)}) async-start(bf16[8,384,128]{2,1,0:T(8,128)(2,1)} %get-tuple-element.37), calls=%async_computation | async-start | bytes 1572864 | tf_op jit(solution)/shard_map/all_to_all | solution.py:342
  14.3 2.9 %collective-permute-start.1 = (bf16[64,768]{1,0:T(8,128)(2,1)S(1)}, bf16[64,768]{1,0:T(8,128)(2,1)S(1)}, u32[]{:S(2)}, u32[]{:S(2)}) collective-permute-start(bf16[64,768]{1,0:T(8,128)(2,1)S(1)} %get-tuple-element.71), channel_id=1, source_target_pairs={{0,8},{1,9},{2,10},{3,11},{4,12},{5,13},{6,14},{7,15},{8,0},{9,1},... | collective-permute-start | bytes 294920 | tf_op jit(solution)/shard_map/ppermute | solution.py:298
  17.2 1.5 %collective-permute-start.2 = (bf16[64,768]{1,0:T(8,128)(2,1)S(1)}, bf16[64,768]{1,0:T(8,128)(2,1)S(1)}, u32[]{:S(2)}, u32[]{:S(2)}) collective-permute-start(bf16[64,768]{1,0:T(8,128)(2,1)S(1)} %get-tuple-element.68), channel_id=1, source_target_pairs={{0,12},{1,13},{2,14},{3,15},{4,8},{5,9},{6,10},{7,11},{8,4},{9,5},... | collective-permute-start | bytes 294920 | tf_op jit(solution)/shard_map/ppermute | solution.py:298
  18.7 22.1 %collective-permute-done.1 = bf16[64,768]{1,0:T(8,128)(2,1)S(1)} collective-permute-done((bf16[64,768]{1,0:T(8,128)(2,1)S(1)}, bf16[64,768]{1,0:T(8,128)(2,1)S(1)}, u32[]{:S(2)}, u32[]{:S(2)}) %collective-permute-start.1) | collective-permute-done | bytes 98336 | tf_op jit(solution)/shard_map/ppermute | solution.py:298
  40.9 0.1 collective-permute-start.4
  40.9 0.8 copy-done.1
  41.7 1.0 collective-permute-done.4.swapped_ref.refs_1_
  42.7 1.1 copy-done.2
  43.8 1.9 %shard_map.104 = (f32[512,256]{1,0:T(8,128)S(1)}, bf16[512,256]{1,0:T(8,128)(2,1)S(1)}, f32[512,256]{1,0:T(8,128)S(1)}, bf16[512,256]{1,0:T(8,128)(2,1)}) custom-call(bf16[256,768]{1,0:T(8,128)(2,1)S(1)} %constant_dynamic-update-slice_fusion.piece_ref.refs_0_, bf16[256,768]{1,0:T(8,128)(2,1)S(1)} %collective-permute-done.4.swapped_ref.refs_1_, ...), custom_call_target="tpu_custom_call" | custom-call | flops 805306368 | bytes 1572864 | tf_op jit(solution)/shard_map/pallas_call | solution.py:147
  45.7 0.7 copy-done.4
  46.4 1.6 %collective-permute-start.5 = (bf16[512,256]{1,0:T(8,128)(2,1)}, bf16[512,256]{1,0:T(8,128)(2,1)}, u32[]{:S(2)}, u32[]{:S(2)}) collective-permute-start(bf16[512,256]{1,0:T(8,128)(2,1)} %get-tuple-element.49), channel_id=1, source_target_pairs={{0,4},{1,5},{2,6},{3,7},{4,0},{5,1},{6,2},{7,3},{8,12},{9,13},{10,... | collective-permute-start | bytes 786440 | tf_op jit(solution)/shard_map/ppermute | solution.py:298
  48.0 0.0 all-to-all-done.tok_ref
  48.0 0.9 copy-done.3
  48.9 4.9 %shard_map.103 = (bf16[1536,1024]{1,0:T(8,128)(2,1)S(1)}, bf16[128,1024]{1,0:T(8,128)(2,1)S(1)}, bf16[1024,128]{1,0:T(8,128)(2,1)S(1)}, bf16[128,1536]{1,0:T(8,128)(2,1)S(1)}, bf16[1536,128]{1,0:T(8,128)(2,1)S(1)}) custom-call(bf16[8,384,128]{2,1,0:T(8,128)(2,1)S(1)} %all-to-all-done.tok_ref, bf16[2,512,128]{2,1,0:T(8,128)(2,1)S(1)} %copy-done.3), custom_call_target="tpu_custom_call" | custom-call | flops 805306368 | bytes 6291456 | tf_op jit(solution)/shard_map/pallas_call | solution.py:147
  53.8 1.6 %copy-done.10 = bf16[1536,1024]{1,0:T(8,128)(2,1)} copy-done((bf16[1536,1024]{1,0:T(8,128)(2,1)}, bf16[1536,1024]{1,0:T(8,128)(2,1)S(1)}, u32[]{:S(2)}) %copy-start.10) | copy-done | bytes 3145752
  55.5 1.2 %add_convert_fusion = bf16[512,256]{1,0:T(8,128)(2,1)S(1)} fusion(f32[512,256]{1,0:T(8,128)S(1)} %get-tuple-element.55, bf16[512,256]{1,0:T(8,128)(2,1)} %collective-permute-done.5), kind=kLoop, calls=%fused_computation.1 | loop fusion | flops 393216 | bytes 1048576 | tf_op jit(solution)/shard_map/convert_element_type | solution.py:362
  56.7 0.6 collective-permute-start.7
  57.3 1.2 collective-permute-start.6
  58.5 1.7 %collective-permute-start.9 = (bf16[256,768]{1,0:T(8,128)(2,1)S(1)}, bf16[256,768]{1,0:T(8,128)(2,1)S(1)}, u32[]{:S(2)}, u32[]{:S(2)}) collective-permute-start(bf16[256,768]{1,0:T(8,128)(2,1)S(1)} %constant_dynamic-update-slice_fusion.piece_ref.refs_0_), channel_id=1, source_target_pairs={{0,2},{1,3},{2,0},{3,1},{4,6},{5,7},{6,4},{7,5},{8,10},{9,11},{10,... | collective-permute-start | bytes 1179656 | tf_op jit(solution)/shard_map/ppermute | solution.py:298
  60.2 11.1 %collective-permute-done.7 = bf16[512,256]{1,0:T(8,128)(2,1)S(1)} collective-permute-done((bf16[512,256]{1,0:T(8,128)(2,1)S(1)}, bf16[512,256]{1,0:T(8,128)(2,1)S(1)}, u32[]{:S(2)}, u32[]{:S(2)}) %collective-permute-start.7) | collective-permute-done | bytes 262176 | tf_op jit(solution)/shard_map/ppermute | solution.py:298
  71.4 0.1 convert_add_fusion
  71.5 1.4 %collective-permute-start.8 = (bf16[512,128]{1,0:T(8,128)(2,1)S(1)}, bf16[512,128]{1,0:T(8,128)(2,1)S(1)}, u32[]{:S(2)}, u32[]{:S(2)}) collective-permute-start(bf16[512,128]{1,0:T(8,128)(2,1)S(1)} %get-tuple-element.72), channel_id=1, source_target_pairs={{0,2},{1,3},{2,0},{3,1},{4,6},{5,7},{6,4},{7,5},{8,10},{9,11},{10,... | collective-permute-start | bytes 393224 | tf_op jit(solution)/shard_map/ppermute | solution.py:298
  72.9 4.1 %collective-permute-done.8.refs_1_ = bf16[512,128]{1,0:T(8,128)(2,1)S(1)} collective-permute-done((bf16[512,128]{1,0:T(8,128)(2,1)S(1)}, bf16[512,128]{1,0:T(8,128)(2,1)S(1)}, u32[]{:S(2)}, u32[]{:S(2)}) %collective-permute-start.8) | collective-permute-done | bytes 131104 | tf_op jit(solution)/shard_map/ppermute | solution.py:298
  76.9 0.2 collective-permute-start.11
  77.1 1.6 %collective-permute-start.12 = (bf16[128,1024]{1,0:T(8,128)(2,1)S(1)}, bf16[128,1024]{1,0:T(8,128)(2,1)S(1)}, u32[]{:S(2)}, u32[]{:S(2)}) collective-permute-start(bf16[128,1024]{1,0:T(8,128)(2,1)S(1)} %get-tuple-element.63.out_ref.refs_4_), channel_id=1, source_target_pairs={{0,4},{1,5},{2,6},{3,7},{4,0},{5,1},{6,2},{7,3},{8,12},{9,13},{10,... | collective-permute-start | bytes 786440 | tf_op jit(solution)/shard_map/ppermute | solution.py:298
  78.7 1.9 %copy-done.11 = bf16[1536,1024]{1,0:T(8,128)(2,1)S(1)} copy-done((bf16[1536,1024]{1,0:T(8,128)(2,1)S(1)}, bf16[1536,1024]{1,0:T(8,128)(2,1)}, u32[]{:S(2)}) %copy-start.11) | copy-done | bytes 3145752
  80.6 1.0 copy-done.13
  81.6 1.0 copy-done.15
  82.6 0.9 copy-done.17
  83.6 4.5 %shard_map.105 = bf16[8,384,128]{2,1,0:T(8,128)(2,1)} custom-call(bf16[1024,128]{1,0:T(8,128)(2,1)S(1)} %copy-done.17, bf16[128,1536]{1,0:T(8,128)(2,1)S(1)} %copy-done.13, bf16[1536,128]{1,0:T(8,128)(2,1)S(1)} %copy-done.15, bf16[1536,1024]{1,0:T(8,128)(2,1)S(1)} %copy-done.11, bf16[128,1024]{1,0:T(8,128)(2,1)S(1)} %get-tuple-element.63.out_ref.refs_4_, ...), custom_call_target="tpu_custom_call" | custom-call | flops 1610612736 | bytes 6291456 | tf_op jit(solution)/shard_map/pallas_call | solution.py:147
  88.0 0.6 collective-permute-done.11.refs_6_
  88.6 1.3 %collective-permute-done.12.refs_5_ = bf16[128,1024]{1,0:T(8,128)(2,1)S(1)} collective-permute-done((bf16[128,1024]{1,0:T(8,128)(2,1)S(1)}, bf16[128,1024]{1,0:T(8,128)(2,1)S(1)}, u32[]{:S(2)}, u32[]{:S(2)}) %collective-permute-start.12) | collective-permute-done | bytes 262176 | tf_op jit(solution)/shard_map/ppermute | solution.py:298
  89.9 0.7 copy-done.8
  90.6 0.3 collective-permute-start.13
  90.9 4.4 %all-to-all-start.1 = ((bf16[8,384,128]{2,1,0:T(8,128)(2,1)}), bf16[8,384,128]{2,1,0:T(8,128)(2,1)S(1)}, u32[]{:S(2)}, u32[]{:S(2)}) async-start(bf16[8,384,128]{2,1,0:T(8,128)(2,1)} %shard_map.105), calls=%async_computation.1 | async-start | bytes 1572864 | tf_op jit(solution)/shard_map/all_to_all | solution.py:381
  95.4 2.2 %collective-permute-done.13.refs_7_ = bf16[128,1024]{1,0:T(8,128)(2,1)} collective-permute-done((bf16[128,1024]{1,0:T(8,128)(2,1)S(1)}, bf16[128,1024]{1,0:T(8,128)(2,1)}, u32[]{:S(2)}, u32[]{:S(2)}) %collective-permute-start.13) | collective-permute-done | bytes 262176 | tf_op jit(solution)/shard_map/ppermute | solution.py:298
  97.6 0.9 copy-done.7
  98.6 0.9 copy-done.9
  99.5 2.3 %shard_map.107 = (bf16[512,384]{1,0:T(8,128)(2,1)S(1)}, bf16[512,384]{1,0:T(8,128)(2,1)S(1)}) custom-call(bf16[256,768]{1,0:T(8,128)(2,1)S(1)} %constant_dynamic-update-slice_fusion.piece_ref.refs_0_, bf16[256,768]{1,0:T(8,128)(2,1)S(1)} %collective-permute-done.4.swapped_ref.refs_1_, bf16[256,768]{1,0:T(8,128)(2,1)S(1)} %collective-permute-done.9.refs_2_, ...), custom_call_target="tpu_custom_call" | custom-call | flops 9663676416 | bytes 1572864 | tf_op jit(solution)/shard_map/pallas_call | solution.py:147
  101.8 3.8 %collective-permute-start.14 = (bf16[512,384]{1,0:T(8,128)(2,1)S(1)}, bf16[512,384]{1,0:T(8,128)(2,1)S(1)}, u32[]{:S(2)}, u32[]{:S(2)}) collective-permute-start(bf16[512,384]{1,0:T(8,128)(2,1)S(1)} %get-tuple-element.67), channel_id=1, source_target_pairs={{0,2},{1,3},{2,0},{3,1},{4,6},{5,7},{6,4},{7,5},{8,10},{9,11},{10,... | collective-permute-start | bytes 1179656 | tf_op jit(solution)/shard_map/ppermute | solution.py:298
  105.6 10.4 %collective-permute-done.14.other_ref = bf16[512,384]{1,0:T(8,128)(2,1)S(1)} collective-permute-done((bf16[512,384]{1,0:T(8,128)(2,1)S(1)}, bf16[512,384]{1,0:T(8,128)(2,1)S(1)}, u32[]{:S(2)}, u32[]{:S(2)}) %collective-permute-start.14) | collective-permute-done | bytes 393248 | tf_op jit(solution)/shard_map/ppermute | solution.py:298
  116.1 1.5 %shard_map.108 = f32[384,1024]{1,0:T(8,128)} custom-call(bf16[512,384]{1,0:T(8,128)(2,1)S(1)} %get-tuple-element.66.own_ref, bf16[512,384]{1,0:T(8,128)(2,1)S(1)} %collective-permute-done.14.other_ref), custom_call_target="tpu_custom_call" | custom-call | bytes 2359296 | tf_op jit(solution)/shard_map/pallas_call | solution.py:147
  117.5 1.1 shard_map.106
  (37 shorter events, 0.1 us)
Async XLA Ops:
  0.6 42.0 %copy-start = (bf16[384,1024]{1,0:T(8,128)(2,1)S(1)}, bf16[384,1024]{1,0:T(8,128)(2,1)}, u32[]{:S(2)}) copy-start(bf16[384,1024]{1,0:T(8,128)(2,1)} %own_ref.1) | copy-start | bytes 2359300
  0.6 40.1 %collective-permute-start.3 = (bf16[384,1024]{1,0:T(8,128)(2,1)}, bf16[384,1024]{1,0:T(8,128)(2,1)S(1)}, u32[]{:S(2)}, u32[]{:S(2)}) collective-permute-start(bf16[384,1024]{1,0:T(8,128)(2,1)} %own_ref.1), channel_id=1, source_target_pairs={{0,2},{1,3},{2,0},{3,1},{4,6},{5,7},{6,4},{7,5},{8,10},{9,11},{10,... | collective-permute-start | bytes 2359304 | tf_op jit(solution)/shard_map/ppermute | solution.py:298
  4.7 4.7 %collective-permute-start = (bf16[64,768]{1,0:T(8,128)(2,1)S(1)}, bf16[64,768]{1,0:T(8,128)(2,1)S(1)}, u32[]{:S(2)}, u32[]{:S(2)}) collective-permute-start(bf16[64,768]{1,0:T(8,128)(2,1)S(1)} %get-tuple-element.70), channel_id=1, source_target_pairs={{0,4},{1,5},{2,6},{3,7},{4,0},{5,1},{6,2},{7,3},{8,12},{9,13},{10,... | collective-permute-start | bytes 294920 | tf_op jit(solution)/shard_map/ppermute | solution.py:298
  9.4 38.5 %all-to-all-start = ((bf16[8,384,128]{2,1,0:T(8,128)(2,1)}), bf16[8,384,128]{2,1,0:T(8,128)(2,1)S(1)}, u32[]{:S(2)}, u32[]{:S(2)}) async-start(bf16[8,384,128]{2,1,0:T(8,128)(2,1)} %get-tuple-element.37), calls=%async_computation | async-start | bytes 1572864 | tf_op jit(solution)/shard_map/all_to_all | solution.py:342
  14.3 26.5 %collective-permute-start.1 = (bf16[64,768]{1,0:T(8,128)(2,1)S(1)}, bf16[64,768]{1,0:T(8,128)(2,1)S(1)}, u32[]{:S(2)}, u32[]{:S(2)}) collective-permute-start(bf16[64,768]{1,0:T(8,128)(2,1)S(1)} %get-tuple-element.71), channel_id=1, source_target_pairs={{0,8},{1,9},{2,10},{3,11},{4,12},{5,13},{6,14},{7,15},{8,0},{9,1},... | collective-permute-start | bytes 294920 | tf_op jit(solution)/shard_map/ppermute | solution.py:298
  17.2 23.6 %collective-permute-start.2 = (bf16[64,768]{1,0:T(8,128)(2,1)S(1)}, bf16[64,768]{1,0:T(8,128)(2,1)S(1)}, u32[]{:S(2)}, u32[]{:S(2)}) collective-permute-start(bf16[64,768]{1,0:T(8,128)(2,1)S(1)} %get-tuple-element.68), channel_id=1, source_target_pairs={{0,12},{1,13},{2,14},{3,15},{4,8},{5,9},{6,10},{7,11},{8,4},{9,5},... | collective-permute-start | bytes 294920 | tf_op jit(solution)/shard_map/ppermute | solution.py:298
  40.8 0.9 copy-start.1
  40.9 1.8 %collective-permute-start.4 = (bf16[256,768]{1,0:T(8,128)(2,1)S(1)}, bf16[256,768]{1,0:T(8,128)(2,1)S(1)}, u32[]{:S(2)}, u32[]{:S(2)}) collective-permute-start(bf16[256,768]{1,0:T(8,128)(2,1)S(1)} %constant_dynamic-update-slice_fusion.piece_ref.refs_0_), channel_id=1, source_target_pairs={{0,1},{1,0},{2,3},{3,2},{4,5},{5,4},{6,7},{7,6},{8,9},{9,8},{10,11... | collective-permute-start | bytes 1179656 | tf_op jit(solution)/shard_map/ppermute | solution.py:298
  42.6 1.1 copy-start.2
  45.6 0.7 copy-start.4
  46.4 9.1 %collective-permute-start.5 = (bf16[512,256]{1,0:T(8,128)(2,1)}, bf16[512,256]{1,0:T(8,128)(2,1)}, u32[]{:S(2)}, u32[]{:S(2)}) collective-permute-start(bf16[512,256]{1,0:T(8,128)(2,1)} %get-tuple-element.49), channel_id=1, source_target_pairs={{0,4},{1,5},{2,6},{3,7},{4,0},{5,1},{6,2},{7,3},{8,12},{9,13},{10,... | collective-permute-start | bytes 786440 | tf_op jit(solution)/shard_map/ppermute | solution.py:298
  48.0 1.0 copy-start.3
  48.9 8.4 %copy-start.5 = (bf16[512,256]{1,0:T(8,128)(2,1)S(1)}, bf16[512,256]{1,0:T(8,128)(2,1)}, u32[]{:S(2)}) copy-start(bf16[512,256]{1,0:T(8,128)(2,1)} %copy-done.4) | copy-start | bytes 786436
  53.8 1.6 %copy-start.10 = (bf16[1536,1024]{1,0:T(8,128)(2,1)}, bf16[1536,1024]{1,0:T(8,128)(2,1)S(1)}, u32[]{:S(2)}) copy-start(bf16[1536,1024]{1,0:T(8,128)(2,1)S(1)} %get-tuple-element.42.probs_ref) | copy-start | bytes 9437188
  55.5 1.2 %copy-start.12 = (bf16[128,1536]{1,0:T(8,128)(2,1)}, bf16[128,1536]{1,0:T(8,128)(2,1)S(1)}, u32[]{:S(2)}) copy-start(bf16[128,1536]{1,0:T(8,128)(2,1)S(1)} %get-tuple-element.40.keys_t_ref) | copy-start | bytes 1179652
  55.5 1.9 %copy-start.14 = (bf16[1536,128]{1,0:T(8,128)(2,1)}, bf16[1536,128]{1,0:T(8,128)(2,1)S(1)}, u32[]{:S(2)}) copy-start(bf16[1536,128]{1,0:T(8,128)(2,1)S(1)} %get-tuple-element.41.vals_ref) | copy-start | bytes 1179652
  55.5 1.9 %copy-start.16 = (bf16[1024,128]{1,0:T(8,128)(2,1)}, bf16[1024,128]{1,0:T(8,128)(2,1)S(1)}, u32[]{:S(2)}) copy-start(bf16[1024,128]{1,0:T(8,128)(2,1)S(1)} %get-tuple-element.39.queries_ref) | copy-start | bytes 786436
  56.7 14.7 %collective-permute-start.7 = (bf16[512,256]{1,0:T(8,128)(2,1)S(1)}, bf16[512,256]{1,0:T(8,128)(2,1)S(1)}, u32[]{:S(2)}, u32[]{:S(2)}) collective-permute-start(bf16[512,256]{1,0:T(8,128)(2,1)S(1)} %add_convert_fusion), channel_id=1, source_target_pairs={{0,8},{1,9},{2,10},{3,11},{4,12},{5,13},{6,14},{7,15},{8,0},{9,1},... | collective-permute-start | bytes 786440 | tf_op jit(solution)/shard_map/ppermute | solution.py:298
  57.3 14.0 %collective-permute-start.6 = (bf16[512,256]{1,0:T(8,128)(2,1)S(1)}, bf16[512,256]{1,0:T(8,128)(2,1)S(1)}, u32[]{:S(2)}, u32[]{:S(2)}) collective-permute-start(bf16[512,256]{1,0:T(8,128)(2,1)S(1)} %copy-done.5), channel_id=1, source_target_pairs={{0,4},{1,5},{2,6},{3,7},{4,0},{5,1},{6,2},{7,3},{8,12},{9,13},{10,... | collective-permute-start | bytes 786440 | tf_op jit(solution)/shard_map/ppermute | solution.py:298
  58.5 18.4 %collective-permute-start.9 = (bf16[256,768]{1,0:T(8,128)(2,1)S(1)}, bf16[256,768]{1,0:T(8,128)(2,1)S(1)}, u32[]{:S(2)}, u32[]{:S(2)}) collective-permute-start(bf16[256,768]{1,0:T(8,128)(2,1)S(1)} %constant_dynamic-update-slice_fusion.piece_ref.refs_0_), channel_id=1, source_target_pairs={{0,2},{1,3},{2,0},{3,1},{4,6},{5,7},{6,4},{7,5},{8,10},{9,11},{10,... | collective-permute-start | bytes 1179656 | tf_op jit(solution)/shard_map/ppermute | solution.py:298
  71.5 5.5 %collective-permute-start.8 = (bf16[512,128]{1,0:T(8,128)(2,1)S(1)}, bf16[512,128]{1,0:T(8,128)(2,1)S(1)}, u32[]{:S(2)}, u32[]{:S(2)}) collective-permute-start(bf16[512,128]{1,0:T(8,128)(2,1)S(1)} %get-tuple-element.72), channel_id=1, source_target_pairs={{0,2},{1,3},{2,0},{3,1},{4,6},{5,7},{6,4},{7,5},{8,10},{9,11},{10,... | collective-permute-start | bytes 393224 | tf_op jit(solution)/shard_map/ppermute | solution.py:298
  76.9 11.7 %collective-permute-start.11 = (bf16[128,1024]{1,0:T(8,128)(2,1)S(1)}, bf16[128,1024]{1,0:T(8,128)(2,1)S(1)}, u32[]{:S(2)}, u32[]{:S(2)}) collective-permute-start(bf16[128,1024]{1,0:T(8,128)(2,1)S(1)} %get-tuple-element.63.out_ref.refs_4_), channel_id=1, source_target_pairs={{0,8},{1,9},{2,10},{3,11},{4,12},{5,13},{6,14},{7,15},{8,0},{9,1},... | collective-permute-start | bytes 786440 | tf_op jit(solution)/shard_map/ppermute | solution.py:298
  77.1 12.8 %collective-permute-start.12 = (bf16[128,1024]{1,0:T(8,128)(2,1)S(1)}, bf16[128,1024]{1,0:T(8,128)(2,1)S(1)}, u32[]{:S(2)}, u32[]{:S(2)}) collective-permute-start(bf16[128,1024]{1,0:T(8,128)(2,1)S(1)} %get-tuple-element.63.out_ref.refs_4_), channel_id=1, source_target_pairs={{0,4},{1,5},{2,6},{3,7},{4,0},{5,1},{6,2},{7,3},{8,12},{9,13},{10,... | collective-permute-start | bytes 786440 | tf_op jit(solution)/shard_map/ppermute | solution.py:298
  78.7 16.7 %collective-permute-start.10 = (bf16[256,768]{1,0:T(8,128)(2,1)S(1)}, bf16[256,768]{1,0:T(8,128)(2,1)S(1)}, u32[]{:S(2)}, u32[]{:S(2)}) collective-permute-start(bf16[256,768]{1,0:T(8,128)(2,1)S(1)} %collective-permute-done.9.refs_2_), channel_id=1, source_target_pairs={{0,1},{1,0},{2,3},{3,2},{4,5},{5,4},{6,7},{7,6},{8,9},{9,8},{10,11... | collective-permute-start | bytes 1179656 | tf_op jit(solution)/shard_map/ppermute | solution.py:298
  78.7 1.9 %copy-start.11 = (bf16[1536,1024]{1,0:T(8,128)(2,1)S(1)}, bf16[1536,1024]{1,0:T(8,128)(2,1)}, u32[]{:S(2)}) copy-start(bf16[1536,1024]{1,0:T(8,128)(2,1)} %copy-done.10) | copy-start | bytes 9437188
  80.6 1.0 copy-start.13
  81.6 1.0 copy-start.15
  82.6 0.9 copy-start.17
  88.6 6.8 %copy-start.6 = (bf16[128,1024]{1,0:T(8,128)(2,1)}, bf16[128,1024]{1,0:T(8,128)(2,1)S(1)}, u32[]{:S(2)}) copy-start(bf16[128,1024]{1,0:T(8,128)(2,1)S(1)} %collective-permute-done.11.refs_6_) | copy-start | bytes 786436
  89.9 0.7 copy-start.8
  90.6 7.0 %collective-permute-start.13 = (bf16[128,1024]{1,0:T(8,128)(2,1)S(1)}, bf16[128,1024]{1,0:T(8,128)(2,1)}, u32[]{:S(2)}, u32[]{:S(2)}) collective-permute-start(bf16[128,1024]{1,0:T(8,128)(2,1)S(1)} %collective-permute-done.11.refs_6_), channel_id=1, source_target_pairs={{0,4},{1,5},{2,6},{3,7},{4,0},{5,1},{6,2},{7,3},{8,12},{9,13},{10,... | collective-permute-start | bytes 786440 | tf_op jit(solution)/shard_map/ppermute | solution.py:298
  90.9 26.6 %all-to-all-start.1 = ((bf16[8,384,128]{2,1,0:T(8,128)(2,1)}), bf16[8,384,128]{2,1,0:T(8,128)(2,1)S(1)}, u32[]{:S(2)}, u32[]{:S(2)}) async-start(bf16[8,384,128]{2,1,0:T(8,128)(2,1)} %shard_map.105), calls=%async_computation.1 | async-start | bytes 1572864 | tf_op jit(solution)/shard_map/all_to_all | solution.py:381
  97.6 1.0 copy-start.7
  98.6 0.9 copy-start.9
  101.8 14.2 %collective-permute-start.14 = (bf16[512,384]{1,0:T(8,128)(2,1)S(1)}, bf16[512,384]{1,0:T(8,128)(2,1)S(1)}, u32[]{:S(2)}, u32[]{:S(2)}) collective-permute-start(bf16[512,384]{1,0:T(8,128)(2,1)S(1)} %get-tuple-element.67), channel_id=1, source_target_pairs={{0,2},{1,3},{2,0},{3,1},{4,6},{5,7},{6,4},{7,5},{8,10},{9,11},{10,... | collective-permute-start | bytes 1179656 | tf_op jit(solution)/shard_map/ppermute | solution.py:298

commit v21 on v20

--- a/solution.py
+++ b/solution.py
@@ -11,7 +11,7 @@
 HD = 128
 F32 = jnp.float32
 BF16 = jnp.bfloat16
-LIMIT = 28 * 1024 * 1024
+LIMIT = 16 * 1024 * 1024
 NT = (((1,), (1,)), ((), ()))
 
 
@@ -335,7 +335,7 @@
         moved=4 * 3 * rows * width,
         limit=60 * 1024 * 1024,
     )
-    tok_out, along[1] = lax.optimization_barrier((tok_out, along[1]))
+    tok_out, along = lax.optimization_barrier((tok_out, along))
     along, given = lax.optimization_barrier((along, given))
     row = jnp.concatenate(along, axis=0)
     row_swapped = exchange(row, cores=True)

time: 119 us -> 109 us (0.916)
  waiting for transfers between devices: 53.5 us -> 45.3 us
  starting transfers between devices: 30.9 us -> 28.8 us
    ppermute x15, waiting for transfers between devices: 53.5 us -> 37.3 us  [exchange(): return lax.ppermute(array, ('seq', 'fsdp'), pairs)]
    all_to_all x1, waiting for transfers between devices: 0.01 us -> 8.01 us  [local(): lax.all_to_all(tok_out, 'seq', split_axis=0, concat_axis=0, tiled=True)]
  transfers between devices with their start and end apart: 17 -> 17, of which waited for: 9 -> 11; matrix products, arithmetic and copies ran while one was open for 1% -> 1% of each run, Pallas kernels for 15% -> 16%
where the time goes in v21:
time: 109 us; the launch traced here: 108 us
  waiting for transfers between devices  45.3 us (42%)
  starting transfers between devices  28.8 us (26%)
  Pallas kernels  18.4 us (17%)
  local copies, waits for them, and re-layouts  13.9 us (13%)
  other arithmetic  1.3 us (1%)
    ppermute x15, waiting for transfers between devices, exchange(): return lax.ppermute(array, ('seq', 'fsdp'), pairs)  37.3 us
    ppermute x15, starting transfers between devices, exchange(): return lax.ppermute(array, ('seq', 'fsdp'), pairs)  20.7 us
    pallas_call x7, Pallas kernels, call(): pl.pallas_call(kernel, out_shape=outs, grid_spec=pltpu.PrefetchScalarGrid...  18.4 us
    unnamed x39, local copies, waits for them, and re-layouts  12.8 us
    all_to_all x1, waiting for transfers between devices, local(): lax.all_to_all(tok_out, 'seq', split_axis=0, concat_axis=0, tiled=True)  8.01 us
    all_to_all x1, starting transfers between devices, local(): lax.all_to_all(grad_out, 'seq', split_axis=0, concat_axis=0, tiled=True)  4.22 us
    all_to_all x1, starting transfers between devices, local(): lax.all_to_all(tok_out, 'seq', split_axis=0, concat_axis=0, tiled=True)  3.9 us
  transfers between devices with their start and end apart: 17, of which 11 were waited for; matrix products, arithmetic and copies ran while one was open for 1% of the time, Pallas kernels for 16%

profile of v21, /device:TPU:0, one launch (start us, length us, event | category | flops | bytes accessed | tf_op | source)
XLA Modules:
  0.0 108.5 jit_solution(2003314771255627511)
XLA Ops:
  0.6 3.0 %collective-permute-start.3 = (bf16[384,1024]{1,0:T(8,128)(2,1)}, bf16[384,1024]{1,0:T(8,128)(2,1)S(1)}, u32[]{:S(2)}, u32[]{:S(2)}) collective-permute-start(bf16[384,1024]{1,0:T(8,128)(2,1)} %own_ref.1), channel_id=1, source_target_pairs={{0,2},{1,3},{2,0},{3,1},{4,6},{5,7},{6,4},{7,5},{8,10},{9,11},{10,... | collective-permute-start | bytes 2359304 | tf_op jit(solution)/shard_map/ppermute | solution.py:298
  3.7 1.1 fusion
  4.7 1.6 %collective-permute-start = (bf16[64,768]{1,0:T(8,128)(2,1)S(1)}, bf16[64,768]{1,0:T(8,128)(2,1)S(1)}, u32[]{:S(2)}, u32[]{:S(2)}) collective-permute-start(bf16[64,768]{1,0:T(8,128)(2,1)S(1)} %get-tuple-element.75), channel_id=1, source_target_pairs={{0,4},{1,5},{2,6},{3,7},{4,0},{5,1},{6,2},{7,3},{8,12},{9,13},{10,... | collective-permute-start | bytes 294920 | tf_op jit(solution)/shard_map/ppermute | solution.py:298
  6.4 2.6 %collective-permute-start.1 = (bf16[64,768]{1,0:T(8,128)(2,1)S(1)}, bf16[64,768]{1,0:T(8,128)(2,1)S(1)}, u32[]{:S(2)}, u32[]{:S(2)}) collective-permute-start(bf16[64,768]{1,0:T(8,128)(2,1)S(1)} %get-tuple-element.77), channel_id=1, source_target_pairs={{0,8},{1,9},{2,10},{3,11},{4,12},{5,13},{6,14},{7,15},{8,0},{9,1},... | collective-permute-start | bytes 294920 | tf_op jit(solution)/shard_map/ppermute | solution.py:298
  9.0 0.2 collective-permute-start.2
  9.2 2.3 %shard_map.102 = (bf16[8,384,128]{2,1,0:T(8,128)(2,1)}, bf16[2,512,128]{2,1,0:T(8,128)(2,1)}) custom-call(s32[1]{0:T(128)} %bitcast.me_ref, bf16[128,1024]{1,0:T(8,128)(2,1)} %q_ref.1, bf16[128,1024]{1,0:T(8,128)(2,1)} %k_ref.1, bf16[128,1024]{1,0:T(8,128)(2,1)} %v_ref.1, bf16[512,1024]{1,0:T(8,128)(2,1)} %kt_ref.1, bf16[512,1024]{1,0:T(8,128)(2,1)} %vt_ref.1), custom_call_target="tpu_custom_call" | custom-call | bytes 1572864 | tf_op jit(solution)/shard_map/pallas_call | solution.py:147
  11.5 5.0 %collective-permute-done.1 = bf16[64,768]{1,0:T(8,128)(2,1)S(1)} collective-permute-done((bf16[64,768]{1,0:T(8,128)(2,1)S(1)}, bf16[64,768]{1,0:T(8,128)(2,1)S(1)}, u32[]{:S(2)}, u32[]{:S(2)}) %collective-permute-start.1) | collective-permute-done | bytes 98336 | tf_op jit(solution)/shard_map/ppermute | solution.py:298
  16.5 3.9 %all-to-all-start = ((bf16[8,384,128]{2,1,0:T(8,128)(2,1)}), bf16[8,384,128]{2,1,0:T(8,128)(2,1)S(1)}, u32[]{:S(2)}, u32[]{:S(2)}) async-start(bf16[8,384,128]{2,1,0:T(8,128)(2,1)} %get-tuple-element.40), calls=%async_computation | async-start | bytes 1572864 | tf_op jit(solution)/shard_map/all_to_all | solution.py:342
  20.4 2.4 %collective-permute-done.3.other_ref = bf16[384,1024]{1,0:T(8,128)(2,1)S(1)} collective-permute-done((bf16[384,1024]{1,0:T(8,128)(2,1)}, bf16[384,1024]{1,0:T(8,128)(2,1)S(1)}, u32[]{:S(2)}, u32[]{:S(2)}) %collective-permute-start.3) | collective-permute-done | bytes 786464 | tf_op jit(solution)/shard_map/ppermute | solution.py:298
  22.9 0.9 copy-done.1
  23.8 0.1 collective-permute-start.4
  23.9 1.7 %collective-permute-done.4.swapped_ref.refs_1_ = bf16[256,768]{1,0:T(8,128)(2,1)S(1)} collective-permute-done((bf16[256,768]{1,0:T(8,128)(2,1)S(1)}, bf16[256,768]{1,0:T(8,128)(2,1)S(1)}, u32[]{:S(2)}, u32[]{:S(2)}) %collective-permute-start.4) | collective-permute-done | bytes 393248 | tf_op jit(solution)/shard_map/ppermute | solution.py:298
  25.6 1.1 %copy-done.2 = bf16[384,1024]{1,0:T(8,128)(2,1)S(1)} copy-done((bf16[384,1024]{1,0:T(8,128)(2,1)S(1)}, bf16[384,1024]{1,0:T(8,128)(2,1)}, u32[]{:S(2)}) %copy-start.2) | copy-done | bytes 786456
  26.7 1.9 %shard_map.104 = (f32[512,256]{1,0:T(8,128)S(1)}, bf16[512,256]{1,0:T(8,128)(2,1)S(1)}, f32[512,256]{1,0:T(8,128)S(1)}, bf16[512,256]{1,0:T(8,128)(2,1)}) custom-call(bf16[256,768]{1,0:T(8,128)(2,1)S(1)} %constant_dynamic-update-slice_fusion.piece_ref.refs_0_, bf16[256,768]{1,0:T(8,128)(2,1)S(1)} %collective-permute-done.4.swapped_ref.refs_1_, ...), custom_call_target="tpu_custom_call" | custom-call | flops 805306368 | bytes 1572864 | tf_op jit(solution)/shard_map/pallas_call | solution.py:147
  28.6 0.7 copy-done.4
  29.3 2.5 %collective-permute-start.5 = (bf16[512,256]{1,0:T(8,128)(2,1)}, bf16[512,256]{1,0:T(8,128)(2,1)}, u32[]{:S(2)}, u32[]{:S(2)}) collective-permute-start(bf16[512,256]{1,0:T(8,128)(2,1)} %get-tuple-element.55), channel_id=1, source_target_pairs={{0,4},{1,5},{2,6},{3,7},{4,0},{5,1},{6,2},{7,3},{8,12},{9,13},{10,... | collective-permute-start | bytes 786440 | tf_op jit(solution)/shard_map/ppermute | solution.py:298
  31.8 8.0 %all-to-all-done.tok_ref = bf16[8,384,128]{2,1,0:T(8,128)(2,1)S(1)} async-done(((bf16[8,384,128]{2,1,0:T(8,128)(2,1)}), bf16[8,384,128]{2,1,0:T(8,128)(2,1)S(1)}, u32[]{:S(2)}, u32[]{:S(2)}) %all-to-all-start) | async-done | bytes 786464 | tf_op jit(solution)/shard_map/all_to_all | solution.py:342
  39.8 0.9 copy-done.3
  40.7 4.9 %shard_map.103 = (bf16[1536,1024]{1,0:T(8,128)(2,1)S(1)}, bf16[128,1024]{1,0:T(8,128)(2,1)S(1)}, bf16[1024,128]{1,0:T(8,128)(2,1)S(1)}, bf16[128,1536]{1,0:T(8,128)(2,1)S(1)}, bf16[1536,128]{1,0:T(8,128)(2,1)S(1)}) custom-call(bf16[8,384,128]{2,1,0:T(8,128)(2,1)S(1)} %all-to-all-done.tok_ref, bf16[2,512,128]{2,1,0:T(8,128)(2,1)S(1)} %copy-done.3), custom_call_target="tpu_custom_call" | custom-call | flops 805306368 | bytes 6291456 | tf_op jit(solution)/shard_map/pallas_call | solution.py:147
  45.7 1.6 %copy-done.10 = bf16[1536,1024]{1,0:T(8,128)(2,1)} copy-done((bf16[1536,1024]{1,0:T(8,128)(2,1)}, bf16[1536,1024]{1,0:T(8,128)(2,1)S(1)}, u32[]{:S(2)}) %copy-start.10) | copy-done | bytes 3145752
  47.3 1.2 %add_convert_fusion = bf16[512,256]{1,0:T(8,128)(2,1)S(1)} fusion(f32[512,256]{1,0:T(8,128)S(1)} %get-tuple-element.61, bf16[512,256]{1,0:T(8,128)(2,1)} %collective-permute-done.5), kind=kLoop, calls=%fused_computation.1 | loop fusion | flops 393216 | bytes 1048576 | tf_op jit(solution)/shard_map/convert_element_type | solution.py:362
  48.5 0.1 collective-permute-start.7
  48.6 1.7 %collective-permute-start.6 = (bf16[512,256]{1,0:T(8,128)(2,1)S(1)}, bf16[512,256]{1,0:T(8,128)(2,1)S(1)}, u32[]{:S(2)}, u32[]{:S(2)}) collective-permute-start(bf16[512,256]{1,0:T(8,128)(2,1)S(1)} %copy-done.5), channel_id=1, source_target_pairs={{0,4},{1,5},{2,6},{3,7},{4,0},{5,1},{6,2},{7,3},{8,12},{9,13},{10,... | collective-permute-start | bytes 786440 | tf_op jit(solution)/shard_map/ppermute | solution.py:298
  50.3 1.7 %collective-permute-start.9 = (bf16[256,768]{1,0:T(8,128)(2,1)S(1)}, bf16[256,768]{1,0:T(8,128)(2,1)S(1)}, u32[]{:S(2)}, u32[]{:S(2)}) collective-permute-start(bf16[256,768]{1,0:T(8,128)(2,1)S(1)} %constant_dynamic-update-slice_fusion.piece_ref.refs_0_), channel_id=1, source_target_pairs={{0,2},{1,3},{2,0},{3,1},{4,6},{5,7},{6,4},{7,5},{8,10},{9,11},{10,... | collective-permute-start | bytes 1179656 | tf_op jit(solution)/shard_map/ppermute | solution.py:298
  52.0 8.4 %collective-permute-done.7 = bf16[512,256]{1,0:T(8,128)(2,1)S(1)} collective-permute-done((bf16[512,256]{1,0:T(8,128)(2,1)S(1)}, bf16[512,256]{1,0:T(8,128)(2,1)S(1)}, u32[]{:S(2)}, u32[]{:S(2)}) %collective-permute-start.7) | collective-permute-done | bytes 262176 | tf_op jit(solution)/shard_map/ppermute | solution.py:298
  60.4 0.8 collective-permute-done.6
  61.2 0.1 convert_add_fusion
  61.3 2.5 %collective-permute-start.8 = (bf16[512,128]{1,0:T(8,128)(2,1)S(1)}, bf16[512,128]{1,0:T(8,128)(2,1)S(1)}, u32[]{:S(2)}, u32[]{:S(2)}) collective-permute-start(bf16[512,128]{1,0:T(8,128)(2,1)S(1)} %get-tuple-element.78), channel_id=1, source_target_pairs={{0,2},{1,3},{2,0},{3,1},{4,6},{5,7},{6,4},{7,5},{8,10},{9,11},{10,... | collective-permute-start | bytes 393224 | tf_op jit(solution)/shard_map/ppermute | solution.py:298
  63.8 3.4 %collective-permute-done.8.refs_1_ = bf16[512,128]{1,0:T(8,128)(2,1)S(1)} collective-permute-done((bf16[512,128]{1,0:T(8,128)(2,1)S(1)}, bf16[512,128]{1,0:T(8,128)(2,1)S(1)}, u32[]{:S(2)}, u32[]{:S(2)}) %collective-permute-start.8) | collective-permute-done | bytes 131104 | tf_op jit(solution)/shard_map/ppermute | solution.py:298
  67.2 1.8 %collective-permute-start.12 = (bf16[128,1024]{1,0:T(8,128)(2,1)S(1)}, bf16[128,1024]{1,0:T(8,128)(2,1)S(1)}, u32[]{:S(2)}, u32[]{:S(2)}) collective-permute-start(bf16[128,1024]{1,0:T(8,128)(2,1)S(1)} %get-tuple-element.69.out_ref.refs_4_), channel_id=1, source_target_pairs={{0,4},{1,5},{2,6},{3,7},{4,0},{5,1},{6,2},{7,3},{8,12},{9,13},{10,... | collective-permute-start | bytes 786440 | tf_op jit(solution)/shard_map/ppermute | solution.py:298
  68.9 1.9 %copy-done.11 = bf16[1536,1024]{1,0:T(8,128)(2,1)S(1)} copy-done((bf16[1536,1024]{1,0:T(8,128)(2,1)S(1)}, bf16[1536,1024]{1,0:T(8,128)(2,1)}, u32[]{:S(2)}) %copy-start.11) | copy-done | bytes 3145752
  70.8 1.0 copy-done.13
  71.8 1.0 copy-done.15
  72.8 0.9 copy-done.17
  73.8 4.5 %shard_map.105 = bf16[8,384,128]{2,1,0:T(8,128)(2,1)} custom-call(bf16[1024,128]{1,0:T(8,128)(2,1)S(1)} %copy-done.17, bf16[128,1536]{1,0:T(8,128)(2,1)S(1)} %copy-done.13, bf16[1536,128]{1,0:T(8,128)(2,1)S(1)} %copy-done.15, bf16[1536,1024]{1,0:T(8,128)(2,1)S(1)} %copy-done.11, bf16[128,1024]{1,0:T(8,128)(2,1)S(1)} %get-tuple-element.69.out_ref.refs_4_, ...), custom_call_target="tpu_custom_call" | custom-call | flops 1610612736 | bytes 6291456 | tf_op jit(solution)/shard_map/pallas_call | solution.py:147
  78.2 1.1 %collective-permute-done.11.refs_6_ = bf16[128,1024]{1,0:T(8,128)(2,1)S(1)} collective-permute-done((bf16[128,1024]{1,0:T(8,128)(2,1)S(1)}, bf16[128,1024]{1,0:T(8,128)(2,1)S(1)}, u32[]{:S(2)}, u32[]{:S(2)}) %collective-permute-start.11) | collective-permute-done | bytes 262176 | tf_op jit(solution)/shard_map/ppermute | solution.py:298
  79.4 0.8 collective-permute-done.12.refs_5_
  80.2 0.7 copy-done.8
  80.9 0.3 collective-permute-start.13
  81.2 4.2 %all-to-all-start.1 = ((bf16[8,384,128]{2,1,0:T(8,128)(2,1)}), bf16[8,384,128]{2,1,0:T(8,128)(2,1)S(1)}, u32[]{:S(2)}, u32[]{:S(2)}) async-start(bf16[8,384,128]{2,1,0:T(8,128)(2,1)} %shard_map.105), calls=%async_computation.1 | async-start | bytes 1572864 | tf_op jit(solution)/shard_map/all_to_all | solution.py:381
  85.4 3.4 %collective-permute-done.13.refs_7_ = bf16[128,1024]{1,0:T(8,128)(2,1)} collective-permute-done((bf16[128,1024]{1,0:T(8,128)(2,1)S(1)}, bf16[128,1024]{1,0:T(8,128)(2,1)}, u32[]{:S(2)}, u32[]{:S(2)}) %collective-permute-start.13) | collective-permute-done | bytes 262176 | tf_op jit(solution)/shard_map/ppermute | solution.py:298
  88.8 0.9 copy-done.7
  89.8 0.9 copy-done.9
  90.7 2.3 %shard_map.107 = (bf16[512,384]{1,0:T(8,128)(2,1)S(1)}, bf16[512,384]{1,0:T(8,128)(2,1)S(1)}) custom-call(bf16[256,768]{1,0:T(8,128)(2,1)S(1)} %constant_dynamic-update-slice_fusion.piece_ref.refs_0_, bf16[256,768]{1,0:T(8,128)(2,1)S(1)} %collective-permute-done.4.swapped_ref.refs_1_, bf16[256,768]{1,0:T(8,128)(2,1)S(1)} %collective-permute-done.9.refs_2_, ...), custom_call_target="tpu_custom_call" | custom-call | flops 9663676416 | bytes 1572864 | tf_op jit(solution)/shard_map/pallas_call | solution.py:147
  93.1 2.6 %collective-permute-start.14 = (bf16[512,384]{1,0:T(8,128)(2,1)S(1)}, bf16[512,384]{1,0:T(8,128)(2,1)S(1)}, u32[]{:S(2)}, u32[]{:S(2)}) collective-permute-start(bf16[512,384]{1,0:T(8,128)(2,1)S(1)} %get-tuple-element.73), channel_id=1, source_target_pairs={{0,2},{1,3},{2,0},{3,1},{4,6},{5,7},{6,4},{7,5},{8,10},{9,11},{10,... | collective-permute-start | bytes 1179656 | tf_op jit(solution)/shard_map/ppermute | solution.py:298
  95.7 10.2 %collective-permute-done.14.other_ref = bf16[512,384]{1,0:T(8,128)(2,1)S(1)} collective-permute-done((bf16[512,384]{1,0:T(8,128)(2,1)S(1)}, bf16[512,384]{1,0:T(8,128)(2,1)S(1)}, u32[]{:S(2)}, u32[]{:S(2)}) %collective-permute-start.14) | collective-permute-done | bytes 393248 | tf_op jit(solution)/shard_map/ppermute | solution.py:298
  105.9 1.5 %shard_map.108 = f32[384,1024]{1,0:T(8,128)} custom-call(bf16[512,384]{1,0:T(8,128)(2,1)S(1)} %get-tuple-element.72.own_ref, bf16[512,384]{1,0:T(8,128)(2,1)S(1)} %collective-permute-done.14.other_ref), custom_call_target="tpu_custom_call" | custom-call | bytes 2359296 | tf_op jit(solution)/shard_map/pallas_call | solution.py:147
  107.4 1.1 %shard_map.106 = (bf16[128,1024]{1,0:T(8,128)(2,1)}, bf16[128,1024]{1,0:T(8,128)(2,1)}, bf16[128,1024]{1,0:T(8,128)(2,1)}) custom-call(bf16[8,384,128]{2,1,0:T(8,128)(2,1)S(1)} %all-to-all-done.1.tok_ref), custom_call_target="tpu_custom_call" | custom-call | bytes 1572864 | tf_op jit(solution)/shard_map/pallas_call | solution.py:147
  (37 shorter events, 0.1 us)
Async XLA Ops:
  0.6 25.0 %copy-start = (bf16[384,1024]{1,0:T(8,128)(2,1)S(1)}, bf16[384,1024]{1,0:T(8,128)(2,1)}, u32[]{:S(2)}) copy-start(bf16[384,1024]{1,0:T(8,128)(2,1)} %own_ref.1) | copy-start | bytes 2359300
  0.6 22.2 %collective-permute-start.3 = (bf16[384,1024]{1,0:T(8,128)(2,1)}, bf16[384,1024]{1,0:T(8,128)(2,1)S(1)}, u32[]{:S(2)}, u32[]{:S(2)}) collective-permute-start(bf16[384,1024]{1,0:T(8,128)(2,1)} %own_ref.1), channel_id=1, source_target_pairs={{0,2},{1,3},{2,0},{3,1},{4,6},{5,7},{6,4},{7,5},{8,10},{9,11},{10,... | collective-permute-start | bytes 2359304 | tf_op jit(solution)/shard_map/ppermute | solution.py:298
  4.7 6.8 %collective-permute-start = (bf16[64,768]{1,0:T(8,128)(2,1)S(1)}, bf16[64,768]{1,0:T(8,128)(2,1)S(1)}, u32[]{:S(2)}, u32[]{:S(2)}) collective-permute-start(bf16[64,768]{1,0:T(8,128)(2,1)S(1)} %get-tuple-element.75), channel_id=1, source_target_pairs={{0,4},{1,5},{2,6},{3,7},{4,0},{5,1},{6,2},{7,3},{8,12},{9,13},{10,... | collective-permute-start | bytes 294920 | tf_op jit(solution)/shard_map/ppermute | solution.py:298
  6.4 10.1 %collective-permute-start.1 = (bf16[64,768]{1,0:T(8,128)(2,1)S(1)}, bf16[64,768]{1,0:T(8,128)(2,1)S(1)}, u32[]{:S(2)}, u32[]{:S(2)}) collective-permute-start(bf16[64,768]{1,0:T(8,128)(2,1)S(1)} %get-tuple-element.77), channel_id=1, source_target_pairs={{0,8},{1,9},{2,10},{3,11},{4,12},{5,13},{6,14},{7,15},{8,0},{9,1},... | collective-permute-start | bytes 294920 | tf_op jit(solution)/shard_map/ppermute | solution.py:298
  9.0 7.6 %collective-permute-start.2 = (bf16[64,768]{1,0:T(8,128)(2,1)S(1)}, bf16[64,768]{1,0:T(8,128)(2,1)S(1)}, u32[]{:S(2)}, u32[]{:S(2)}) collective-permute-start(bf16[64,768]{1,0:T(8,128)(2,1)S(1)} %get-tuple-element.74), channel_id=1, source_target_pairs={{0,12},{1,13},{2,14},{3,15},{4,8},{5,9},{6,10},{7,11},{8,4},{9,5},... | collective-permute-start | bytes 294920 | tf_op jit(solution)/shard_map/ppermute | solution.py:298
  16.5 23.3 %all-to-all-start = ((bf16[8,384,128]{2,1,0:T(8,128)(2,1)}), bf16[8,384,128]{2,1,0:T(8,128)(2,1)S(1)}, u32[]{:S(2)}, u32[]{:S(2)}) async-start(bf16[8,384,128]{2,1,0:T(8,128)(2,1)} %get-tuple-element.40), calls=%async_computation | async-start | bytes 1572864 | tf_op jit(solution)/shard_map/all_to_all | solution.py:342
  22.9 0.9 copy-start.1
  23.8 1.8 %collective-permute-start.4 = (bf16[256,768]{1,0:T(8,128)(2,1)S(1)}, bf16[256,768]{1,0:T(8,128)(2,1)S(1)}, u32[]{:S(2)}, u32[]{:S(2)}) collective-permute-start(bf16[256,768]{1,0:T(8,128)(2,1)S(1)} %constant_dynamic-update-slice_fusion.piece_ref.refs_0_), channel_id=1, source_target_pairs={{0,1},{1,0},{2,3},{3,2},{4,5},{5,4},{6,7},{7,6},{8,9},{9,8},{10,11... | collective-permute-start | bytes 1179656 | tf_op jit(solution)/shard_map/ppermute | solution.py:298
  25.6 1.1 %copy-start.2 = (bf16[384,1024]{1,0:T(8,128)(2,1)S(1)}, bf16[384,1024]{1,0:T(8,128)(2,1)}, u32[]{:S(2)}) copy-start(bf16[384,1024]{1,0:T(8,128)(2,1)} %copy-done.1) | copy-start | bytes 2359300
  28.6 0.7 copy-start.4
  29.3 18.0 %collective-permute-start.5 = (bf16[512,256]{1,0:T(8,128)(2,1)}, bf16[512,256]{1,0:T(8,128)(2,1)}, u32[]{:S(2)}, u32[]{:S(2)}) collective-permute-start(bf16[512,256]{1,0:T(8,128)(2,1)} %get-tuple-element.55), channel_id=1, source_target_pairs={{0,4},{1,5},{2,6},{3,7},{4,0},{5,1},{6,2},{7,3},{8,12},{9,13},{10,... | collective-permute-start | bytes 786440 | tf_op jit(solution)/shard_map/ppermute | solution.py:298
  39.8 1.0 copy-start.3
  40.7 7.9 %copy-start.5 = (bf16[512,256]{1,0:T(8,128)(2,1)S(1)}, bf16[512,256]{1,0:T(8,128)(2,1)}, u32[]{:S(2)}) copy-start(bf16[512,256]{1,0:T(8,128)(2,1)} %copy-done.4) | copy-start | bytes 786436
  45.7 1.6 %copy-start.10 = (bf16[1536,1024]{1,0:T(8,128)(2,1)}, bf16[1536,1024]{1,0:T(8,128)(2,1)S(1)}, u32[]{:S(2)}) copy-start(bf16[1536,1024]{1,0:T(8,128)(2,1)S(1)} %get-tuple-element.45.probs_ref) | copy-start | bytes 9437188
  47.3 1.2 %copy-start.12 = (bf16[128,1536]{1,0:T(8,128)(2,1)}, bf16[128,1536]{1,0:T(8,128)(2,1)S(1)}, u32[]{:S(2)}) copy-start(bf16[128,1536]{1,0:T(8,128)(2,1)S(1)} %get-tuple-element.43.keys_t_ref) | copy-start | bytes 1179652
  47.3 1.3 %copy-start.14 = (bf16[1536,128]{1,0:T(8,128)(2,1)}, bf16[1536,128]{1,0:T(8,128)(2,1)S(1)}, u32[]{:S(2)}) copy-start(bf16[1536,128]{1,0:T(8,128)(2,1)S(1)} %get-tuple-element.44.vals_ref) | copy-start | bytes 1179652
  47.3 1.3 %copy-start.16 = (bf16[1024,128]{1,0:T(8,128)(2,1)}, bf16[1024,128]{1,0:T(8,128)(2,1)S(1)}, u32[]{:S(2)}) copy-start(bf16[1024,128]{1,0:T(8,128)(2,1)S(1)} %get-tuple-element.42.queries_ref) | copy-start | bytes 786436
  48.5 11.9 %collective-permute-start.7 = (bf16[512,256]{1,0:T(8,128)(2,1)S(1)}, bf16[512,256]{1,0:T(8,128)(2,1)S(1)}, u32[]{:S(2)}, u32[]{:S(2)}) collective-permute-start(bf16[512,256]{1,0:T(8,128)(2,1)S(1)} %add_convert_fusion), channel_id=1, source_target_pairs={{0,8},{1,9},{2,10},{3,11},{4,12},{5,13},{6,14},{7,15},{8,0},{9,1},... | collective-permute-start | bytes 786440 | tf_op jit(solution)/shard_map/ppermute | solution.py:298
  48.6 12.6 %collective-permute-start.6 = (bf16[512,256]{1,0:T(8,128)(2,1)S(1)}, bf16[512,256]{1,0:T(8,128)(2,1)S(1)}, u32[]{:S(2)}, u32[]{:S(2)}) collective-permute-start(bf16[512,256]{1,0:T(8,128)(2,1)S(1)} %copy-done.5), channel_id=1, source_target_pairs={{0,4},{1,5},{2,6},{3,7},{4,0},{5,1},{6,2},{7,3},{8,12},{9,13},{10,... | collective-permute-start | bytes 786440 | tf_op jit(solution)/shard_map/ppermute | solution.py:298
  50.3 16.9 %collective-permute-start.9 = (bf16[256,768]{1,0:T(8,128)(2,1)S(1)}, bf16[256,768]{1,0:T(8,128)(2,1)S(1)}, u32[]{:S(2)}, u32[]{:S(2)}) collective-permute-start(bf16[256,768]{1,0:T(8,128)(2,1)S(1)} %constant_dynamic-update-slice_fusion.piece_ref.refs_0_), channel_id=1, source_target_pairs={{0,2},{1,3},{2,0},{3,1},{4,6},{5,7},{6,4},{7,5},{8,10},{9,11},{10,... | collective-permute-start | bytes 1179656 | tf_op jit(solution)/shard_map/ppermute | solution.py:298
  61.3 5.9 %collective-permute-start.8 = (bf16[512,128]{1,0:T(8,128)(2,1)S(1)}, bf16[512,128]{1,0:T(8,128)(2,1)S(1)}, u32[]{:S(2)}, u32[]{:S(2)}) collective-permute-start(bf16[512,128]{1,0:T(8,128)(2,1)S(1)} %get-tuple-element.78), channel_id=1, source_target_pairs={{0,2},{1,3},{2,0},{3,1},{4,6},{5,7},{6,4},{7,5},{8,10},{9,11},{10,... | collective-permute-start | bytes 393224 | tf_op jit(solution)/shard_map/ppermute | solution.py:298
  67.2 12.2 %collective-permute-start.11 = (bf16[128,1024]{1,0:T(8,128)(2,1)S(1)}, bf16[128,1024]{1,0:T(8,128)(2,1)S(1)}, u32[]{:S(2)}, u32[]{:S(2)}) collective-permute-start(bf16[128,1024]{1,0:T(8,128)(2,1)S(1)} %get-tuple-element.69.out_ref.refs_4_), channel_id=1, source_target_pairs={{0,8},{1,9},{2,10},{3,11},{4,12},{5,13},{6,14},{7,15},{8,0},{9,1},... | collective-permute-start | bytes 786440 | tf_op jit(solution)/shard_map/ppermute | solution.py:298
  67.2 13.0 %collective-permute-start.12 = (bf16[128,1024]{1,0:T(8,128)(2,1)S(1)}, bf16[128,1024]{1,0:T(8,128)(2,1)S(1)}, u32[]{:S(2)}, u32[]{:S(2)}) collective-permute-start(bf16[128,1024]{1,0:T(8,128)(2,1)S(1)} %get-tuple-element.69.out_ref.refs_4_), channel_id=1, source_target_pairs={{0,4},{1,5},{2,6},{3,7},{4,0},{5,1},{6,2},{7,3},{8,12},{9,13},{10,... | collective-permute-start | bytes 786440 | tf_op jit(solution)/shard_map/ppermute | solution.py:298
  68.9 16.5 %collective-permute-start.10 = (bf16[256,768]{1,0:T(8,128)(2,1)S(1)}, bf16[256,768]{1,0:T(8,128)(2,1)S(1)}, u32[]{:S(2)}, u32[]{:S(2)}) collective-permute-start(bf16[256,768]{1,0:T(8,128)(2,1)S(1)} %collective-permute-done.9.refs_2_), channel_id=1, source_target_pairs={{0,1},{1,0},{2,3},{3,2},{4,5},{5,4},{6,7},{7,6},{8,9},{9,8},{10,11... | collective-permute-start | bytes 1179656 | tf_op jit(solution)/shard_map/ppermute | solution.py:298
  68.9 1.9 %copy-start.11 = (bf16[1536,1024]{1,0:T(8,128)(2,1)S(1)}, bf16[1536,1024]{1,0:T(8,128)(2,1)}, u32[]{:S(2)}) copy-start(bf16[1536,1024]{1,0:T(8,128)(2,1)} %copy-done.10) | copy-start | bytes 9437188
  70.8 1.0 copy-start.13
  71.8 1.0 copy-start.15
  72.8 0.9 copy-start.17
  79.4 6.1 %copy-start.6 = (bf16[128,1024]{1,0:T(8,128)(2,1)}, bf16[128,1024]{1,0:T(8,128)(2,1)S(1)}, u32[]{:S(2)}) copy-start(bf16[128,1024]{1,0:T(8,128)(2,1)S(1)} %collective-permute-done.11.refs_6_) | copy-start | bytes 786436
  80.2 0.7 copy-start.8
  80.9 7.9 %collective-permute-start.13 = (bf16[128,1024]{1,0:T(8,128)(2,1)S(1)}, bf16[128,1024]{1,0:T(8,128)(2,1)}, u32[]{:S(2)}, u32[]{:S(2)}) collective-permute-start(bf16[128,1024]{1,0:T(8,128)(2,1)S(1)} %collective-permute-done.11.refs_6_), channel_id=1, source_target_pairs={{0,4},{1,5},{2,6},{3,7},{4,0},{5,1},{6,2},{7,3},{8,12},{9,13},{10,... | collective-permute-start | bytes 786440 | tf_op jit(solution)/shard_map/ppermute | solution.py:298
  81.2 26.2 %all-to-all-start.1 = ((bf16[8,384,128]{2,1,0:T(8,128)(2,1)}), bf16[8,384,128]{2,1,0:T(8,128)(2,1)S(1)}, u32[]{:S(2)}, u32[]{:S(2)}) async-start(bf16[8,384,128]{2,1,0:T(8,128)(2,1)} %shard_map.105), calls=%async_computation.1 | async-start | bytes 1572864 | tf_op jit(solution)/shard_map/all_to_all | solution.py:381
  88.8 1.0 copy-start.7
  89.8 0.9 copy-start.9
  93.1 12.8 %collective-permute-start.14 = (bf16[512,384]{1,0:T(8,128)(2,1)S(1)}, bf16[512,384]{1,0:T(8,128)(2,1)S(1)}, u32[]{:S(2)}, u32[]{:S(2)}) collective-permute-start(bf16[512,384]{1,0:T(8,128)(2,1)S(1)} %get-tuple-element.73), channel_id=1, source_target_pairs={{0,2},{1,3},{2,0},{3,1},{4,6},{5,7},{6,4},{7,5},{8,10},{9,11},{10,... | collective-permute-start | bytes 1179656 | tf_op jit(solution)/shard_map/ppermute | solution.py:298

commit v22 on v21

--- a/solution.py
+++ b/solution.py
@@ -227,6 +227,25 @@
         z = jnp.bitwise_xor(me, step) // 2
         cols = pl.ds(pl.multiple_of(z * 2 * HD, 2 * HD), 2 * HD)
         ref[...] = jnp.dot(cot[...], weight[:, cols], preferred_element_type=F32).astype(ref.dtype)
+
+
+def concat_kernel(*refs):
+    *pieces, out_ref = refs
+    part = pieces[0].shape[0]
+    for i, piece in enumerate(pieces):
+        out_ref[i * part : (i + 1) * part, :] = piece[...]
+
+
+def add_kernel(kept_ref, received_ref, out_ref):
+    out_ref[...] = (kept_ref[...] + received_ref[...].astype(F32)).astype(BF16)
+
+
+def finish_kernel(mine_ref, near_ref, far_ref, kept_ref, give_ref):
+    heads = mine_ref[...] + near_ref[...].astype(F32) + far_ref[...].astype(F32)
+    first, second = heads[:, :HD].astype(BF16), heads[:, HD:].astype(BF16)
+    first_row = lax.rem(lax.axis_index("seq"), 2) == 0
+    kept_ref[...] = jnp.where(first_row, first, second)
+    give_ref[...] = jnp.where(first_row, second, first)
 
 
 def weight_grad_kernel(*refs):
@@ -337,7 +356,7 @@
     )
     tok_out, along = lax.optimization_barrier((tok_out, along))
     along, given = lax.optimization_barrier((along, given))
-    row = jnp.concatenate(along, axis=0)
+    (row,) = call(concat_kernel, [shape((4 * along[0].shape[0], along[0].shape[1]), BF16)], along)
     row_swapped = exchange(row, cores=True)
     tok_in = lax.all_to_all(tok_out, "seq", split_axis=0, concat_axis=0, tiled=True)
 
@@ -359,12 +378,11 @@
         moved=2 * image * columns,
     )
     send, out_t, near = lax.optimization_barrier((exchange(send, 2), out_t, near))
-    far = exchange((far + send.astype(F32)).astype(BF16), 4)
+    (far,) = call(add_kernel, [shape(far.shape, BF16)], [far, send])
+    far = exchange(far, 4)
     near = exchange(near, 2)
-    heads = mine + near.astype(F32) + far.astype(F32)
-    first_row = lax.axis_index("seq") % 2 == 0
-    kept = jnp.where(first_row, heads[:, :HD], heads[:, HD:]).astype(BF16)
-    got = exchange(jnp.where(first_row, heads[:, HD:], heads[:, :HD]).astype(BF16), 1)
+    kept, give = call(finish_kernel, [shape((image // 2, HD), BF16)] * 2, [mine, near, far])
+    got = exchange(give, 1)
     row, _ = lax.optimization_barrier((row, out_t))
     other_row = exchange(row, 1)
     out_late, got, other_row = lax.optimization_barrier((out_t, got, other_row))

time: 109 us -> 107 us (0.982)
  local copies, waits for them, and re-layouts: 13.9 us -> 7.44 us
  starting transfers between devices: 28.8 us -> 32.5 us
  waiting for transfers between devices: 45.3 us -> 47.8 us
  other arithmetic: 1.3 us -> 0 us
    ppermute x15, waiting for transfers between devices: 37.3 us -> 47.4 us  [exchange(): return lax.ppermute(array, ('seq', 'fsdp'), pairs)]
    all_to_all x1, waiting for transfers between devices: 8.01 us -> 0.38 us  [local(): lax.all_to_all(tok_out, 'seq', split_axis=0, concat_axis=0, tiled=True)]
    unnamed x39 -> x18, local copies, waits for them, and re-layouts: 12.8 us -> 6.3 us
    all_to_all x1, starting transfers between devices: 4.22 us -> 5.59 us  [local(): lax.all_to_all(grad_out, 'seq', split_axis=0, concat_axis=0, tiled=True)]
    ppermute x15, starting transfers between devices: 20.7 us -> 22 us  [exchange(): return lax.ppermute(array, ('seq', 'fsdp'), pairs)]
    convert_element_type x2 -> x0, other arithmetic: 1.22 us -> none  [the longest x1 1.2 us: local(): far = exchange((far + send.astype(F32)).astype(BF16), 4)]
    pallas_call x7 -> x10, Pallas kernels: 18.4 us -> 17.7 us  [call(): pl.pallas_call(kernel, out_shape=outs, grid_spec=pltpu.PrefetchScalarGrid...]
  transfers between devices with their start and end apart: 17 -> 17, of which waited for: 11 -> 11; matrix products, arithmetic and copies ran while one was open for 1% -> 0% of each run, Pallas kernels for 16% -> 16%
where the time goes in v22:
time: 107 us; the launch traced here: 106 us
  waiting for transfers between devices  47.8 us (45%)
  starting transfers between devices  32.5 us (30%)
  Pallas kernels  17.7 us (17%)
  local copies, waits for them, and re-layouts  7.44 us (7%)
    ppermute x15, waiting for transfers between devices, exchange(): return lax.ppermute(array, ('seq', 'fsdp'), pairs)  47.4 us
    ppermute x15, starting transfers between devices, exchange(): return lax.ppermute(array, ('seq', 'fsdp'), pairs)  22 us
    pallas_call x10, Pallas kernels, call(): pl.pallas_call(kernel, out_shape=outs, grid_spec=pltpu.PrefetchScalarGrid...  17.7 us
    unnamed x18, local copies, waits for them, and re-layouts  6.3 us
    all_to_all x1, starting transfers between devices, local(): lax.all_to_all(grad_out, 'seq', split_axis=0, concat_axis=0, tiled=True)  5.59 us
    all_to_all x1, starting transfers between devices, local(): lax.all_to_all(tok_out, 'seq', split_axis=0, concat_axis=0, tiled=True)  4.86 us
  transfers between devices with their start and end apart: 17, of which 11 were waited for; matrix products, arithmetic and copies ran while one was open for 0% of the time, Pallas kernels for 16%

profile of v22, /device:TPU:0, one launch (start us, length us, event | category | flops | bytes accessed | tf_op | source)
XLA Modules:
  0.0 106.1 jit_solution(8713876202938594669)
XLA Ops:
  0.6 0.0 copy-start
  0.7 1.1 %fusion = (bf16[64,768]{1,0:T(8,128)(2,1)S(1)}, bf16[64,768]{1,0:T(8,128)(2,1)S(1)}, bf16[64,768]{1,0:T(8,128)(2,1)S(1)}, bf16[64,768]{1,0:T(8,128)(2,1)S(1)}) fusion(bf16[128,3072]{1,0:T(8,128)(2,1)} %param.13, s32[]{:T(128)S(6)} %select_n.23, s32[]{:T(128)S(6)} %select_n.28, s32[]{:T(128)S(6)} %select_n.26, s32[]{:T(128)S(6)} %select_n.25, s32[]{:T(128)S(6)} %select_n.27), kind=kLoop, calls=%fused_computation | loop fusion | bytes 786452 | tf_op jit(solution)/shard_map/dynamic_slice | solution.py:326
  1.8 3.1 %collective-permute-start = (bf16[64,768]{1,0:T(8,128)(2,1)S(1)}, bf16[64,768]{1,0:T(8,128)(2,1)S(1)}, u32[]{:S(2)}, u32[]{:S(2)}) collective-permute-start(bf16[64,768]{1,0:T(8,128)(2,1)S(1)} %get-tuple-element.79), channel_id=1, source_target_pairs={{0,4},{1,5},{2,6},{3,7},{4,0},{5,1},{6,2},{7,3},{8,12},{9,13},{10,... | collective-permute-start | bytes 294920 | tf_op jit(solution)/shard_map/ppermute | solution.py:317
  4.9 2.6 %collective-permute-start.1 = (bf16[64,768]{1,0:T(8,128)(2,1)S(1)}, bf16[64,768]{1,0:T(8,128)(2,1)S(1)}, u32[]{:S(2)}, u32[]{:S(2)}) collective-permute-start(bf16[64,768]{1,0:T(8,128)(2,1)S(1)} %get-tuple-element.81), channel_id=1, source_target_pairs={{0,8},{1,9},{2,10},{3,11},{4,12},{5,13},{6,14},{7,15},{8,0},{9,1},... | collective-permute-start | bytes 294920 | tf_op jit(solution)/shard_map/ppermute | solution.py:317
  7.5 0.0 collective-permute-start.2
  7.5 1.7 %collective-permute-start.3 = (bf16[384,1024]{1,0:T(8,128)(2,1)}, bf16[384,1024]{1,0:T(8,128)(2,1)S(1)}, u32[]{:S(2)}, u32[]{:S(2)}) collective-permute-start(bf16[384,1024]{1,0:T(8,128)(2,1)} %own_ref.1), channel_id=1, source_target_pairs={{0,2},{1,3},{2,0},{3,1},{4,6},{5,7},{6,4},{7,5},{8,10},{9,11},{10,... | collective-permute-start | bytes 2359304 | tf_op jit(solution)/shard_map/ppermute | solution.py:317
  9.2 2.3 %shard_map.102 = (bf16[8,384,128]{2,1,0:T(8,128)(2,1)}, bf16[2,512,128]{2,1,0:T(8,128)(2,1)}) custom-call(s32[1]{0:T(128)} %bitcast.me_ref, bf16[128,1024]{1,0:T(8,128)(2,1)} %q_ref.1, bf16[128,1024]{1,0:T(8,128)(2,1)} %k_ref.1, bf16[128,1024]{1,0:T(8,128)(2,1)} %v_ref.1, bf16[512,1024]{1,0:T(8,128)(2,1)} %kt_ref.1, bf16[512,1024]{1,0:T(8,128)(2,1)} %vt_ref.1), custom_call_target="tpu_custom_call" | custom-call | bytes 1572864 | tf_op jit(solution)/shard_map/pallas_call | solution.py:147
  11.6 0.0 collective-permute-done.refs_1_
  11.6 3.8 %collective-permute-done.1.refs_2_ = bf16[64,768]{1,0:T(8,128)(2,1)S(1)} collective-permute-done((bf16[64,768]{1,0:T(8,128)(2,1)S(1)}, bf16[64,768]{1,0:T(8,128)(2,1)S(1)}, u32[]{:S(2)}, u32[]{:S(2)}) %collective-permute-start.1) | collective-permute-done | bytes 98336 | tf_op jit(solution)/shard_map/ppermute | solution.py:317
  15.3 0.0 collective-permute-done.2.refs_3_
  15.3 4.9 %all-to-all-start = ((bf16[8,384,128]{2,1,0:T(8,128)(2,1)}), bf16[8,384,128]{2,1,0:T(8,128)(2,1)S(1)}, u32[]{:S(2)}, u32[]{:S(2)}) async-start(bf16[8,384,128]{2,1,0:T(8,128)(2,1)} %get-tuple-element.42), calls=%async_computation | async-start | bytes 1572864 | tf_op jit(solution)/shard_map/all_to_all | solution.py:361
  20.2 12.6 %collective-permute-done.3.other_ref = bf16[384,1024]{1,0:T(8,128)(2,1)S(1)} collective-permute-done((bf16[384,1024]{1,0:T(8,128)(2,1)}, bf16[384,1024]{1,0:T(8,128)(2,1)S(1)}, u32[]{:S(2)}, u32[]{:S(2)}) %collective-permute-start.3) | collective-permute-done | bytes 786464 | tf_op jit(solution)/shard_map/ppermute | solution.py:317
  32.7 0.9 copy-done.1
  33.7 0.1 collective-permute-start.4
  33.8 1.7 %collective-permute-done.4.swapped_ref.refs_1_ = bf16[256,768]{1,0:T(8,128)(2,1)S(1)} collective-permute-done((bf16[256,768]{1,0:T(8,128)(2,1)S(1)}, bf16[256,768]{1,0:T(8,128)(2,1)S(1)}, u32[]{:S(2)}, u32[]{:S(2)}) %collective-permute-start.4) | collective-permute-done | bytes 393248 | tf_op jit(solution)/shard_map/ppermute | solution.py:317
  35.5 1.1 %copy-done.2 = bf16[384,1024]{1,0:T(8,128)(2,1)S(1)} copy-done((bf16[384,1024]{1,0:T(8,128)(2,1)S(1)}, bf16[384,1024]{1,0:T(8,128)(2,1)}, u32[]{:S(2)}) %copy-start.2) | copy-done | bytes 786456
  36.6 1.9 %shard_map.105 = (f32[512,256]{1,0:T(8,128)S(1)}, bf16[512,256]{1,0:T(8,128)(2,1)S(1)}, f32[512,256]{1,0:T(8,128)S(1)}, bf16[512,256]{1,0:T(8,128)(2,1)}) custom-call(bf16[256,768]{1,0:T(8,128)(2,1)S(1)} %shard_map.104.piece_ref.refs_0_, bf16[256,768]{1,0:T(8,128)(2,1)S(1)} %collective-permute-done.4.swapped_ref.refs_1_, bf16[384,1024]{1,0:T(8,128)(2,1)S(1)} %copy-done, ...), custom_call_target="tpu_custom_call" | custom-call | flops 805306368 | bytes 1572864 | tf_op jit(solution)/shard_map/pallas_call | solution.py:147
  38.5 0.7 copy-done.8
  39.2 0.0 collective-permute-start.5
  39.2 0.4 all-to-all-done.tok_ref
  39.6 0.9 copy-done.3
  40.5 4.9 %shard_map.103 = (bf16[1536,1024]{1,0:T(8,128)(2,1)S(1)}, bf16[128,1024]{1,0:T(8,128)(2,1)S(1)}, bf16[1024,128]{1,0:T(8,128)(2,1)S(1)}, bf16[128,1536]{1,0:T(8,128)(2,1)S(1)}, bf16[1536,128]{1,0:T(8,128)(2,1)S(1)}) custom-call(bf16[8,384,128]{2,1,0:T(8,128)(2,1)S(1)} %all-to-all-done.tok_ref, bf16[2,512,128]{2,1,0:T(8,128)(2,1)S(1)} %copy-done.3), custom_call_target="tpu_custom_call" | custom-call | flops 805306368 | bytes 6291456 | tf_op jit(solution)/shard_map/pallas_call | solution.py:147
  45.4 2.3 %collective-permute-done.5.received_ref = bf16[512,256]{1,0:T(8,128)(2,1)S(1)} collective-permute-done((bf16[512,256]{1,0:T(8,128)(2,1)}, bf16[512,256]{1,0:T(8,128)(2,1)S(1)}, u32[]{:S(2)}, u32[]{:S(2)}) %collective-permute-start.5) | collective-permute-done | bytes 262176 | tf_op jit(solution)/shard_map/ppermute | solution.py:317
  47.7 0.3 collective-permute-start.6
  48.1 4.9 %collective-permute-start.7 = (bf16[512,256]{1,0:T(8,128)(2,1)S(1)}, bf16[512,256]{1,0:T(8,128)(2,1)S(1)}, u32[]{:S(2)}, u32[]{:S(2)}) collective-permute-start(bf16[512,256]{1,0:T(8,128)(2,1)S(1)} %shard_map.106), channel_id=1, source_target_pairs={{0,8},{1,9},{2,10},{3,11},{4,12},{5,13},{6,14},{7,15},{8,0},{9,1},... | collective-permute-start | bytes 786440 | tf_op jit(solution)/shard_map/ppermute | solution.py:317
  53.0 0.1 collective-permute-start.9
  53.1 7.9 %collective-permute-done.6.near_ref = bf16[512,256]{1,0:T(8,128)(2,1)S(1)} collective-permute-done((bf16[512,256]{1,0:T(8,128)(2,1)}, bf16[512,256]{1,0:T(8,128)(2,1)S(1)}, u32[]{:S(2)}, u32[]{:S(2)}) %collective-permute-start.6) | collective-permute-done | bytes 262176 | tf_op jit(solution)/shard_map/ppermute | solution.py:317
  61.1 0.0 collective-permute-done.7.far_ref
  61.1 0.1 shard_map.107
  61.2 1.6 %collective-permute-start.8 = (bf16[512,128]{1,0:T(8,128)(2,1)S(1)}, bf16[512,128]{1,0:T(8,128)(2,1)S(1)}, u32[]{:S(2)}, u32[]{:S(2)}) collective-permute-start(bf16[512,128]{1,0:T(8,128)(2,1)S(1)} %get-tuple-element.66), channel_id=1, source_target_pairs={{0,2},{1,3},{2,0},{3,1},{4,6},{5,7},{6,4},{7,5},{8,10},{9,11},{10,... | collective-permute-start | bytes 393224 | tf_op jit(solution)/shard_map/ppermute | solution.py:317
  62.8 3.5 %collective-permute-done.8.refs_1_ = bf16[512,128]{1,0:T(8,128)(2,1)S(1)} collective-permute-done((bf16[512,128]{1,0:T(8,128)(2,1)S(1)}, bf16[512,128]{1,0:T(8,128)(2,1)S(1)}, u32[]{:S(2)}, u32[]{:S(2)}) %collective-permute-start.8) | collective-permute-done | bytes 131104 | tf_op jit(solution)/shard_map/ppermute | solution.py:317
  66.2 1.6 %collective-permute-start.11 = (bf16[128,1024]{1,0:T(8,128)(2,1)S(1)}, bf16[128,1024]{1,0:T(8,128)(2,1)S(1)}, u32[]{:S(2)}, u32[]{:S(2)}) collective-permute-start(bf16[128,1024]{1,0:T(8,128)(2,1)S(1)} %get-tuple-element.73.out_ref.refs_4_), channel_id=1, source_target_pairs={{0,8},{1,9},{2,10},{3,11},{4,12},{5,13},{6,14},{7,15},{8,0},{9,1},... | collective-permute-start | bytes 786440 | tf_op jit(solution)/shard_map/ppermute | solution.py:317
  67.8 4.7 %collective-permute-start.12 = (bf16[128,1024]{1,0:T(8,128)(2,1)S(1)}, bf16[128,1024]{1,0:T(8,128)(2,1)S(1)}, u32[]{:S(2)}, u32[]{:S(2)}) collective-permute-start(bf16[128,1024]{1,0:T(8,128)(2,1)S(1)} %get-tuple-element.73.out_ref.refs_4_), channel_id=1, source_target_pairs={{0,4},{1,5},{2,6},{3,7},{4,0},{5,1},{6,2},{7,3},{8,12},{9,13},{10,... | collective-permute-start | bytes 786440 | tf_op jit(solution)/shard_map/ppermute | solution.py:317
  72.5 0.0 collective-permute-start.10
  72.5 4.5 %shard_map.108 = bf16[8,384,128]{2,1,0:T(8,128)(2,1)} custom-call(bf16[1024,128]{1,0:T(8,128)(2,1)S(1)} %get-tuple-element.44.queries_ref, bf16[128,1536]{1,0:T(8,128)(2,1)S(1)} %get-tuple-element.45.keys_t_ref, bf16[1536,128]{1,0:T(8,128)(2,1)S(1)} %get-tuple-element.46.vals_ref, bf16[1536,1024]{1,0:T(8,128)(2,1)S(1)} %get-tuple-element.47.probs_ref, ...), custom_call_target="tpu_custom_call" | custom-call | flops 1610612736 | bytes 6291456 | tf_op jit(solution)/shard_map/pallas_call | solution.py:147
  77.0 1.2 %collective-permute-done.11.refs_6_ = bf16[128,1024]{1,0:T(8,128)(2,1)S(1)} collective-permute-done((bf16[128,1024]{1,0:T(8,128)(2,1)S(1)}, bf16[128,1024]{1,0:T(8,128)(2,1)S(1)}, u32[]{:S(2)}, u32[]{:S(2)}) %collective-permute-start.11) | collective-permute-done | bytes 262176 | tf_op jit(solution)/shard_map/ppermute | solution.py:317
  78.2 0.9 collective-permute-done.12.refs_5_
  79.1 0.7 copy-done.6
  79.8 0.7 collective-permute-start.13
  80.6 5.6 %all-to-all-start.1 = ((bf16[8,384,128]{2,1,0:T(8,128)(2,1)}), bf16[8,384,128]{2,1,0:T(8,128)(2,1)S(1)}, u32[]{:S(2)}, u32[]{:S(2)}) async-start(bf16[8,384,128]{2,1,0:T(8,128)(2,1)} %shard_map.108), calls=%async_computation.1 | async-start | bytes 1572864 | tf_op jit(solution)/shard_map/all_to_all | solution.py:399
  86.2 1.5 %collective-permute-done.13.refs_7_ = bf16[128,1024]{1,0:T(8,128)(2,1)S(1)} collective-permute-done((bf16[128,1024]{1,0:T(8,128)(2,1)S(1)}, bf16[128,1024]{1,0:T(8,128)(2,1)S(1)}, u32[]{:S(2)}, u32[]{:S(2)}) %collective-permute-start.13) | collective-permute-done | bytes 262176 | tf_op jit(solution)/shard_map/ppermute | solution.py:317
  87.7 0.9 copy-done.5
  88.6 0.9 copy-done.7
  89.6 1.4 %shard_map.110 = (bf16[512,384]{1,0:T(8,128)(2,1)S(1)}, bf16[512,384]{1,0:T(8,128)(2,1)S(1)}) custom-call(bf16[256,768]{1,0:T(8,128)(2,1)S(1)} %shard_map.104.piece_ref.refs_0_, bf16[256,768]{1,0:T(8,128)(2,1)S(1)} %collective-permute-done.4.swapped_ref.refs_1_, bf16[256,768]{1,0:T(8,128)(2,1)S(1)} %collective-permute-done.9.refs_2_, ...), custom_call_target="tpu_custom_call" | custom-call | flops 9663676416 | bytes 1572864 | tf_op jit(solution)/shard_map/pallas_call | solution.py:147
  91.0 0.6 collective-permute-start.14
  91.6 12.0 %collective-permute-done.14.other_ref = bf16[512,384]{1,0:T(8,128)(2,1)S(1)} collective-permute-done((bf16[512,384]{1,0:T(8,128)(2,1)S(1)}, bf16[512,384]{1,0:T(8,128)(2,1)S(1)}, u32[]{:S(2)}, u32[]{:S(2)}) %collective-permute-start.14) | collective-permute-done | bytes 393248 | tf_op jit(solution)/shard_map/ppermute | solution.py:317
  103.6 1.5 %shard_map.111 = f32[384,1024]{1,0:T(8,128)} custom-call(bf16[512,384]{1,0:T(8,128)(2,1)S(1)} %get-tuple-element.76.own_ref, bf16[512,384]{1,0:T(8,128)(2,1)S(1)} %collective-permute-done.14.other_ref), custom_call_target="tpu_custom_call" | custom-call | bytes 2359296 | tf_op jit(solution)/shard_map/pallas_call | solution.py:147
  105.1 1.1 %shard_map.109 = (bf16[128,1024]{1,0:T(8,128)(2,1)}, bf16[128,1024]{1,0:T(8,128)(2,1)}, bf16[128,1024]{1,0:T(8,128)(2,1)}) custom-call(bf16[8,384,128]{2,1,0:T(8,128)(2,1)S(1)} %all-to-all-done.1.tok_ref), custom_call_target="tpu_custom_call" | custom-call | bytes 1572864 | tf_op jit(solution)/shard_map/pallas_call | solution.py:147
  (15 shorter events, 0.1 us)
Async XLA Ops:
  0.6 34.8 %copy-start = (bf16[384,1024]{1,0:T(8,128)(2,1)S(1)}, bf16[384,1024]{1,0:T(8,128)(2,1)}, u32[]{:S(2)}) copy-start(bf16[384,1024]{1,0:T(8,128)(2,1)} %own_ref.1) | copy-start | bytes 2359300
  1.8 9.7 %collective-permute-start = (bf16[64,768]{1,0:T(8,128)(2,1)S(1)}, bf16[64,768]{1,0:T(8,128)(2,1)S(1)}, u32[]{:S(2)}, u32[]{:S(2)}) collective-permute-start(bf16[64,768]{1,0:T(8,128)(2,1)S(1)} %get-tuple-element.79), channel_id=1, source_target_pairs={{0,4},{1,5},{2,6},{3,7},{4,0},{5,1},{6,2},{7,3},{8,12},{9,13},{10,... | collective-permute-start | bytes 294920 | tf_op jit(solution)/shard_map/ppermute | solution.py:317
  4.9 10.4 %collective-permute-start.1 = (bf16[64,768]{1,0:T(8,128)(2,1)S(1)}, bf16[64,768]{1,0:T(8,128)(2,1)S(1)}, u32[]{:S(2)}, u32[]{:S(2)}) collective-permute-start(bf16[64,768]{1,0:T(8,128)(2,1)S(1)} %get-tuple-element.81), channel_id=1, source_target_pairs={{0,8},{1,9},{2,10},{3,11},{4,12},{5,13},{6,14},{7,15},{8,0},{9,1},... | collective-permute-start | bytes 294920 | tf_op jit(solution)/shard_map/ppermute | solution.py:317
  7.5 7.8 %collective-permute-start.2 = (bf16[64,768]{1,0:T(8,128)(2,1)S(1)}, bf16[64,768]{1,0:T(8,128)(2,1)S(1)}, u32[]{:S(2)}, u32[]{:S(2)}) collective-permute-start(bf16[64,768]{1,0:T(8,128)(2,1)S(1)} %get-tuple-element.78), channel_id=1, source_target_pairs={{0,12},{1,13},{2,14},{3,15},{4,8},{5,9},{6,10},{7,11},{8,4},{9,5},... | collective-permute-start | bytes 294920 | tf_op jit(solution)/shard_map/ppermute | solution.py:317
  7.5 25.2 %collective-permute-start.3 = (bf16[384,1024]{1,0:T(8,128)(2,1)}, bf16[384,1024]{1,0:T(8,128)(2,1)S(1)}, u32[]{:S(2)}, u32[]{:S(2)}) collective-permute-start(bf16[384,1024]{1,0:T(8,128)(2,1)} %own_ref.1), channel_id=1, source_target_pairs={{0,2},{1,3},{2,0},{3,1},{4,6},{5,7},{6,4},{7,5},{8,10},{9,11},{10,... | collective-permute-start | bytes 2359304 | tf_op jit(solution)/shard_map/ppermute | solution.py:317
  15.3 24.2 %all-to-all-start = ((bf16[8,384,128]{2,1,0:T(8,128)(2,1)}), bf16[8,384,128]{2,1,0:T(8,128)(2,1)S(1)}, u32[]{:S(2)}, u32[]{:S(2)}) async-start(bf16[8,384,128]{2,1,0:T(8,128)(2,1)} %get-tuple-element.42), calls=%async_computation | async-start | bytes 1572864 | tf_op jit(solution)/shard_map/all_to_all | solution.py:361
  32.7 0.9 copy-start.1
  33.7 1.8 %collective-permute-start.4 = (bf16[256,768]{1,0:T(8,128)(2,1)S(1)}, bf16[256,768]{1,0:T(8,128)(2,1)S(1)}, u32[]{:S(2)}, u32[]{:S(2)}) collective-permute-start(bf16[256,768]{1,0:T(8,128)(2,1)S(1)} %shard_map.104.piece_ref.refs_0_), channel_id=1, source_target_pairs={{0,1},{1,0},{2,3},{3,2},{4,5},{5,4},{6,7},{7,6},{8,9},{9,8},{10,11... | collective-permute-start | bytes 1179656 | tf_op jit(solution)/shard_map/ppermute | solution.py:317
  35.5 1.1 %copy-start.2 = (bf16[384,1024]{1,0:T(8,128)(2,1)S(1)}, bf16[384,1024]{1,0:T(8,128)(2,1)}, u32[]{:S(2)}) copy-start(bf16[384,1024]{1,0:T(8,128)(2,1)} %copy-done.1) | copy-start | bytes 2359300
  38.5 0.7 copy-start.8
  39.2 8.6 %collective-permute-start.5 = (bf16[512,256]{1,0:T(8,128)(2,1)}, bf16[512,256]{1,0:T(8,128)(2,1)S(1)}, u32[]{:S(2)}, u32[]{:S(2)}) collective-permute-start(bf16[512,256]{1,0:T(8,128)(2,1)} %get-tuple-element.57), channel_id=1, source_target_pairs={{0,4},{1,5},{2,6},{3,7},{4,0},{5,1},{6,2},{7,3},{8,12},{9,13},{10,... | collective-permute-start | bytes 786440 | tf_op jit(solution)/shard_map/ppermute | solution.py:317
  39.6 1.0 copy-start.3
  47.7 13.3 %collective-permute-start.6 = (bf16[512,256]{1,0:T(8,128)(2,1)}, bf16[512,256]{1,0:T(8,128)(2,1)S(1)}, u32[]{:S(2)}, u32[]{:S(2)}) collective-permute-start(bf16[512,256]{1,0:T(8,128)(2,1)} %copy-done.8), channel_id=1, source_target_pairs={{0,4},{1,5},{2,6},{3,7},{4,0},{5,1},{6,2},{7,3},{8,12},{9,13},{10,... | collective-permute-start | bytes 786440 | tf_op jit(solution)/shard_map/ppermute | solution.py:317
  48.1 13.0 %collective-permute-start.7 = (bf16[512,256]{1,0:T(8,128)(2,1)S(1)}, bf16[512,256]{1,0:T(8,128)(2,1)S(1)}, u32[]{:S(2)}, u32[]{:S(2)}) collective-permute-start(bf16[512,256]{1,0:T(8,128)(2,1)S(1)} %shard_map.106), channel_id=1, source_target_pairs={{0,8},{1,9},{2,10},{3,11},{4,12},{5,13},{6,14},{7,15},{8,0},{9,1},... | collective-permute-start | bytes 786440 | tf_op jit(solution)/shard_map/ppermute | solution.py:317
  53.0 13.2 %collective-permute-start.9 = (bf16[256,768]{1,0:T(8,128)(2,1)S(1)}, bf16[256,768]{1,0:T(8,128)(2,1)S(1)}, u32[]{:S(2)}, u32[]{:S(2)}) collective-permute-start(bf16[256,768]{1,0:T(8,128)(2,1)S(1)} %shard_map.104.piece_ref.refs_0_), channel_id=1, source_target_pairs={{0,2},{1,3},{2,0},{3,1},{4,6},{5,7},{6,4},{7,5},{8,10},{9,11},{10,... | collective-permute-start | bytes 1179656 | tf_op jit(solution)/shard_map/ppermute | solution.py:317
  61.2 5.0 %collective-permute-start.8 = (bf16[512,128]{1,0:T(8,128)(2,1)S(1)}, bf16[512,128]{1,0:T(8,128)(2,1)S(1)}, u32[]{:S(2)}, u32[]{:S(2)}) collective-permute-start(bf16[512,128]{1,0:T(8,128)(2,1)S(1)} %get-tuple-element.66), channel_id=1, source_target_pairs={{0,2},{1,3},{2,0},{3,1},{4,6},{5,7},{6,4},{7,5},{8,10},{9,11},{10,... | collective-permute-start | bytes 393224 | tf_op jit(solution)/shard_map/ppermute | solution.py:317
  66.2 12.0 %collective-permute-start.11 = (bf16[128,1024]{1,0:T(8,128)(2,1)S(1)}, bf16[128,1024]{1,0:T(8,128)(2,1)S(1)}, u32[]{:S(2)}, u32[]{:S(2)}) collective-permute-start(bf16[128,1024]{1,0:T(8,128)(2,1)S(1)} %get-tuple-element.73.out_ref.refs_4_), channel_id=1, source_target_pairs={{0,8},{1,9},{2,10},{3,11},{4,12},{5,13},{6,14},{7,15},{8,0},{9,1},... | collective-permute-start | bytes 786440 | tf_op jit(solution)/shard_map/ppermute | solution.py:317
  67.8 11.3 %collective-permute-start.12 = (bf16[128,1024]{1,0:T(8,128)(2,1)S(1)}, bf16[128,1024]{1,0:T(8,128)(2,1)S(1)}, u32[]{:S(2)}, u32[]{:S(2)}) collective-permute-start(bf16[128,1024]{1,0:T(8,128)(2,1)S(1)} %get-tuple-element.73.out_ref.refs_4_), channel_id=1, source_target_pairs={{0,4},{1,5},{2,6},{3,7},{4,0},{5,1},{6,2},{7,3},{8,12},{9,13},{10,... | collective-permute-start | bytes 786440 | tf_op jit(solution)/shard_map/ppermute | solution.py:317
  72.5 13.7 %collective-permute-start.10 = (bf16[256,768]{1,0:T(8,128)(2,1)S(1)}, bf16[256,768]{1,0:T(8,128)(2,1)S(1)}, u32[]{:S(2)}, u32[]{:S(2)}) collective-permute-start(bf16[256,768]{1,0:T(8,128)(2,1)S(1)} %collective-permute-done.9.refs_2_), channel_id=1, source_target_pairs={{0,1},{1,0},{2,3},{3,2},{4,5},{5,4},{6,7},{7,6},{8,9},{9,8},{10,11... | collective-permute-start | bytes 1179656 | tf_op jit(solution)/shard_map/ppermute | solution.py:317
  78.2 8.0 %copy-start.4 = (bf16[128,1024]{1,0:T(8,128)(2,1)}, bf16[128,1024]{1,0:T(8,128)(2,1)S(1)}, u32[]{:S(2)}) copy-start(bf16[128,1024]{1,0:T(8,128)(2,1)S(1)} %collective-permute-done.11.refs_6_) | copy-start | bytes 786436
  79.1 0.7 copy-start.6
  79.8 7.9 %collective-permute-start.13 = (bf16[128,1024]{1,0:T(8,128)(2,1)S(1)}, bf16[128,1024]{1,0:T(8,128)(2,1)S(1)}, u32[]{:S(2)}, u32[]{:S(2)}) collective-permute-start(bf16[128,1024]{1,0:T(8,128)(2,1)S(1)} %collective-permute-done.11.refs_6_), channel_id=1, source_target_pairs={{0,4},{1,5},{2,6},{3,7},{4,0},{5,1},{6,2},{7,3},{8,12},{9,13},{10,... | collective-permute-start | bytes 786440 | tf_op jit(solution)/shard_map/ppermute | solution.py:317
  80.6 24.5 %all-to-all-start.1 = ((bf16[8,384,128]{2,1,0:T(8,128)(2,1)}), bf16[8,384,128]{2,1,0:T(8,128)(2,1)S(1)}, u32[]{:S(2)}, u32[]{:S(2)}) async-start(bf16[8,384,128]{2,1,0:T(8,128)(2,1)} %shard_map.108), calls=%async_computation.1 | async-start | bytes 1572864 | tf_op jit(solution)/shard_map/all_to_all | solution.py:399
  87.7 1.0 copy-start.5
  88.6 0.9 copy-start.7
  91.0 12.6 %collective-permute-start.14 = (bf16[512,384]{1,0:T(8,128)(2,1)S(1)}, bf16[512,384]{1,0:T(8,128)(2,1)S(1)}, u32[]{:S(2)}, u32[]{:S(2)}) collective-permute-start(bf16[512,384]{1,0:T(8,128)(2,1)S(1)} %get-tuple-element.77), channel_id=1, source_target_pairs={{0,2},{1,3},{2,0},{3,1},{4,6},{5,7},{6,4},{7,5},{8,10},{9,11},{10,... | collective-permute-start | bytes 1179656 | tf_op jit(solution)/shard_map/ppermute | solution.py:317

commit v23 on v22

--- a/solution.py
+++ b/solution.py
@@ -227,13 +227,6 @@
         z = jnp.bitwise_xor(me, step) // 2
         cols = pl.ds(pl.multiple_of(z * 2 * HD, 2 * HD), 2 * HD)
         ref[...] = jnp.dot(cot[...], weight[:, cols], preferred_element_type=F32).astype(ref.dtype)
-
-
-def concat_kernel(*refs):
-    *pieces, out_ref = refs
-    part = pieces[0].shape[0]
-    for i, piece in enumerate(pieces):
-        out_ref[i * part : (i + 1) * part, :] = piece[...]
 
 
 def add_kernel(kept_ref, received_ref, out_ref):
@@ -356,7 +349,7 @@
     )
     tok_out, along = lax.optimization_barrier((tok_out, along))
     along, given = lax.optimization_barrier((along, given))
-    (row,) = call(concat_kernel, [shape((4 * along[0].shape[0], along[0].shape[1]), BF16)], along)
+    row = jnp.concatenate(along, axis=0)
     row_swapped = exchange(row, cores=True)
     tok_in = lax.all_to_all(tok_out, "seq", split_axis=0, concat_axis=0, tiled=True)
 
@@ -377,17 +370,16 @@
         flops=8 * image * columns * HD,
         moved=2 * image * columns,
     )
-    send, out_t, near = lax.optimization_barrier((exchange(send, 2), out_t, near))
+    send, near = lax.optimization_barrier((exchange(send, 2), near))
     (far,) = call(add_kernel, [shape(far.shape, BF16)], [far, send])
-    far = exchange(far, 4)
-    near = exchange(near, 2)
+    far, near = exchange(far, 4), exchange(near, 2)
+    out_late, far, near = lax.optimization_barrier((out_t, far, near))
     kept, give = call(finish_kernel, [shape((image // 2, HD), BF16)] * 2, [mine, near, far])
     got = exchange(give, 1)
+    out_near, out_far = exchange(out_late, 2), exchange(out_late, 4)
     row, _ = lax.optimization_barrier((row, out_t))
     other_row = exchange(row, 1)
-    out_late, got, other_row = lax.optimization_barrier((out_t, got, other_row))
     other_swapped = exchange(other_row, cores=True)
-    out_near, out_far = exchange(out_late, 2), exchange(out_late, 4)
     (grad_out,) = call(
         functools.partial(backward_kernel, chunk=chunk),
         [shape((n, 3 * rows, HD), BF16)],
@@ -397,7 +389,7 @@
         moved=4 * total * image,
     )
     grad_in = lax.all_to_all(grad_out, "seq", split_axis=0, concat_axis=0, tiled=True)
-    out_far, out_near, _ = lax.optimization_barrier((out_far, out_near, grad_out))
+    out_far, out_near, other_row, _ = lax.optimization_barrier((out_far, out_near, other_row, grad_out))
     outs = [out_t, out_near, out_far, exchange(out_far, 2)]
     dw_own, dw_other = call(
         weight_grad_kernel,

time: 107 us -> 97.6 us (0.912)
  starting transfers between devices: 32.5 us -> 27.1 us
  local copies, waits for them, and re-layouts: 7.44 us -> 3.72 us
    unnamed x18 -> x19, local copies, waits for them, and re-layouts: 6.3 us -> 2.65 us
    ppermute x15, starting transfers between devices: 22 us -> 19 us  [exchange(): return lax.ppermute(array, ('seq', 'fsdp'), pairs)]
    all_to_all x1, starting transfers between devices: 5.59 us -> 3.84 us  [local(): lax.all_to_all(grad_out, 'seq', split_axis=0, concat_axis=0, tiled=True)]
    pallas_call x10 -> x9, Pallas kernels: 17.7 us -> 17.3 us  [call(): pl.pallas_call(kernel, out_shape=outs, grid_spec=pltpu.PrefetchScalarGrid...]
  transfers between devices with their start and end apart: 17 -> 17, of which waited for: 11 -> 14; matrix products, arithmetic and copies ran while one was open for 0% -> 1% of each run, Pallas kernels for 16% -> 17%
where the time goes in v23:
time: 97.6 us; the launch traced here: 97.3 us
  waiting for transfers between devices  48.5 us (50%)
  starting transfers between devices  27.1 us (28%)
  Pallas kernels  17.3 us (18%)
  local copies, waits for them, and re-layouts  3.72 us (4%)
    ppermute x15, waiting for transfers between devices, exchange(): return lax.ppermute(array, ('seq', 'fsdp'), pairs)  48.5 us
    ppermute x15, starting transfers between devices, exchange(): return lax.ppermute(array, ('seq', 'fsdp'), pairs)  19 us
    pallas_call x9, Pallas kernels, call(): pl.pallas_call(kernel, out_shape=outs, grid_spec=pltpu.PrefetchScalarGrid...  17.3 us
    all_to_all x1, starting transfers between devices, local(): lax.all_to_all(tok_out, 'seq', split_axis=0, concat_axis=0, tiled=True)  4.25 us
    all_to_all x1, starting transfers between devices, local(): lax.all_to_all(grad_out, 'seq', split_axis=0, concat_axis=0, tiled=True)  3.84 us
    unnamed x19, local copies, waits for them, and re-layouts  2.65 us
  transfers between devices with their start and end apart: 17, of which 14 were waited for; matrix products, arithmetic and copies ran while one was open for 1% of the time, Pallas kernels for 17%

profile of v23, /device:TPU:0, one launch (start us, length us, event | category | flops | bytes accessed | tf_op | source)
XLA Modules:
  0.0 97.3 jit_solution(5422338716717487173)
XLA Ops:
  0.6 3.0 %collective-permute-start.3 = (bf16[384,1024]{1,0:T(8,128)(2,1)}, bf16[384,1024]{1,0:T(8,128)(2,1)S(1)}, u32[]{:S(2)}, u32[]{:S(2)}) collective-permute-start(bf16[384,1024]{1,0:T(8,128)(2,1)} %own_ref.1), channel_id=1, source_target_pairs={{0,2},{1,3},{2,0},{3,1},{4,6},{5,7},{6,4},{7,5},{8,10},{9,11},{10,... | collective-permute-start | bytes 2359304 | tf_op jit(solution)/shard_map/ppermute | solution.py:310
  3.7 1.1 %fusion = (bf16[64,768]{1,0:T(8,128)(2,1)S(1)}, bf16[64,768]{1,0:T(8,128)(2,1)S(1)}, bf16[64,768]{1,0:T(8,128)(2,1)S(1)}, bf16[64,768]{1,0:T(8,128)(2,1)S(1)}) fusion(bf16[128,3072]{1,0:T(8,128)(2,1)} %param.13, s32[]{:T(128)S(6)} %select_n.23, s32[]{:T(128)S(6)} %select_n.28, s32[]{:T(128)S(6)} %select_n.26, s32[]{:T(128)S(6)} %select_n.25, s32[]{:T(128)S(6)} %select_n.27), kind=kLoop, calls=%fused_computation.4 | loop fusion | bytes 786452 | tf_op jit(solution)/shard_map/dynamic_slice | solution.py:319
  4.7 3.7 %collective-permute-start.2 = (bf16[64,768]{1,0:T(8,128)(2,1)S(1)}, bf16[64,768]{1,0:T(8,128)(2,1)S(1)}, u32[]{:S(2)}, u32[]{:S(2)}) collective-permute-start(bf16[64,768]{1,0:T(8,128)(2,1)S(1)} %get-tuple-element.78), channel_id=1, source_target_pairs={{0,12},{1,13},{2,14},{3,15},{4,8},{5,9},{6,10},{7,11},{8,4},{9,5},... | collective-permute-start | bytes 294920 | tf_op jit(solution)/shard_map/ppermute | solution.py:310
  8.4 0.0 collective-permute-start
  8.4 0.8 collective-permute-start.1
  9.2 2.3 %shard_map.102 = (bf16[8,384,128]{2,1,0:T(8,128)(2,1)}, bf16[2,512,128]{2,1,0:T(8,128)(2,1)}) custom-call(s32[1]{0:T(128)} %bitcast.me_ref, bf16[128,1024]{1,0:T(8,128)(2,1)} %q_ref.1, bf16[128,1024]{1,0:T(8,128)(2,1)} %k_ref.1, bf16[128,1024]{1,0:T(8,128)(2,1)} %v_ref.1, bf16[512,1024]{1,0:T(8,128)(2,1)} %kt_ref.1, bf16[512,1024]{1,0:T(8,128)(2,1)} %vt_ref.1), custom_call_target="tpu_custom_call" | custom-call | bytes 1572864 | tf_op jit(solution)/shard_map/pallas_call | solution.py:147
  11.5 0.6 collective-permute-done.2
  12.1 2.4 %collective-permute-done = bf16[64,768]{1,0:T(8,128)(2,1)S(1)} collective-permute-done((bf16[64,768]{1,0:T(8,128)(2,1)S(1)}, bf16[64,768]{1,0:T(8,128)(2,1)S(1)}, u32[]{:S(2)}, u32[]{:S(2)}) %collective-permute-start) | collective-permute-done | bytes 98336 | tf_op jit(solution)/shard_map/ppermute | solution.py:310
  14.5 1.9 %collective-permute-done.1 = bf16[64,768]{1,0:T(8,128)(2,1)S(1)} collective-permute-done((bf16[64,768]{1,0:T(8,128)(2,1)S(1)}, bf16[64,768]{1,0:T(8,128)(2,1)S(1)}, u32[]{:S(2)}, u32[]{:S(2)}) %collective-permute-start.1) | collective-permute-done | bytes 98336 | tf_op jit(solution)/shard_map/ppermute | solution.py:310
  16.4 4.2 %all-to-all-start = ((bf16[8,384,128]{2,1,0:T(8,128)(2,1)}), bf16[8,384,128]{2,1,0:T(8,128)(2,1)S(1)}, u32[]{:S(2)}, u32[]{:S(2)}) async-start(bf16[8,384,128]{2,1,0:T(8,128)(2,1)} %get-tuple-element.42), calls=%async_computation | async-start | bytes 1572864 | tf_op jit(solution)/shard_map/all_to_all | solution.py:354
  20.6 0.8 collective-permute-done.3.other_ref
  21.5 0.1 collective-permute-start.4
  21.6 1.7 %collective-permute-done.4.swapped_ref.refs_1_ = bf16[256,768]{1,0:T(8,128)(2,1)S(1)} collective-permute-done((bf16[256,768]{1,0:T(8,128)(2,1)S(1)}, bf16[256,768]{1,0:T(8,128)(2,1)S(1)}, u32[]{:S(2)}, u32[]{:S(2)}) %collective-permute-start.4) | collective-permute-done | bytes 393248 | tf_op jit(solution)/shard_map/ppermute | solution.py:310
  23.3 1.5 %shard_map.104 = (f32[512,256]{1,0:T(8,128)S(1)}, bf16[512,256]{1,0:T(8,128)(2,1)}, f32[512,256]{1,0:T(8,128)S(1)}, bf16[512,256]{1,0:T(8,128)(2,1)S(1)}) custom-call(bf16[256,768]{1,0:T(8,128)(2,1)S(1)} %constant_dynamic-update-slice_fusion.piece_ref.refs_0_, bf16[256,768]{1,0:T(8,128)(2,1)S(1)} %collective-permute-done.4.swapped_ref.refs_1_, ...), custom_call_target="tpu_custom_call" | custom-call | flops 805306368 | bytes 1572864 | tf_op jit(solution)/shard_map/pallas_call | solution.py:147
  24.7 1.8 %collective-permute-start.5 = (bf16[512,256]{1,0:T(8,128)(2,1)S(1)}, bf16[512,256]{1,0:T(8,128)(2,1)S(1)}, u32[]{:S(2)}, u32[]{:S(2)}) collective-permute-start(bf16[512,256]{1,0:T(8,128)(2,1)S(1)} %get-tuple-element.60), channel_id=1, source_target_pairs={{0,4},{1,5},{2,6},{3,7},{4,0},{5,1},{6,2},{7,3},{8,12},{9,13},{10,... | collective-permute-start | bytes 786440 | tf_op jit(solution)/shard_map/ppermute | solution.py:310
  26.5 14.5 %collective-permute-done.5.received_ref = bf16[512,256]{1,0:T(8,128)(2,1)S(1)} collective-permute-done((bf16[512,256]{1,0:T(8,128)(2,1)S(1)}, bf16[512,256]{1,0:T(8,128)(2,1)S(1)}, u32[]{:S(2)}, u32[]{:S(2)}) %collective-permute-start.5) | collective-permute-done | bytes 262176 | tf_op jit(solution)/shard_map/ppermute | solution.py:310
  41.1 2.6 %collective-permute-start.6 = (bf16[512,256]{1,0:T(8,128)(2,1)S(1)}, bf16[512,256]{1,0:T(8,128)(2,1)S(1)}, u32[]{:S(2)}, u32[]{:S(2)}) collective-permute-start(bf16[512,256]{1,0:T(8,128)(2,1)S(1)} %shard_map.105), channel_id=1, source_target_pairs={{0,8},{1,9},{2,10},{3,11},{4,12},{5,13},{6,14},{7,15},{8,0},{9,1},... | collective-permute-start | bytes 786440 | tf_op jit(solution)/shard_map/ppermute | solution.py:310
  43.7 0.4 collective-permute-start.7
  44.1 0.0 all-to-all-done.tok_ref
  44.1 0.0 copy-done.3
  44.1 4.9 %shard_map.103 = (bf16[1536,1024]{1,0:T(8,128)(2,1)S(1)}, bf16[128,1024]{1,0:T(8,128)(2,1)S(1)}, bf16[1024,128]{1,0:T(8,128)(2,1)S(1)}, bf16[128,1536]{1,0:T(8,128)(2,1)S(1)}, bf16[1536,128]{1,0:T(8,128)(2,1)S(1)}) custom-call(bf16[8,384,128]{2,1,0:T(8,128)(2,1)S(1)} %all-to-all-done.tok_ref, bf16[2,512,128]{2,1,0:T(8,128)(2,1)S(1)} %copy-done.3), custom_call_target="tpu_custom_call" | custom-call | flops 805306368 | bytes 6291456 | tf_op jit(solution)/shard_map/pallas_call | solution.py:147
  49.0 1.5 %collective-permute-start.11 = (bf16[256,768]{1,0:T(8,128)(2,1)S(1)}, bf16[256,768]{1,0:T(8,128)(2,1)S(1)}, u32[]{:S(2)}, u32[]{:S(2)}) collective-permute-start(bf16[256,768]{1,0:T(8,128)(2,1)S(1)} %constant_dynamic-update-slice_fusion.piece_ref.refs_0_), channel_id=1, source_target_pairs={{0,2},{1,3},{2,0},{3,1},{4,6},{5,7},{6,4},{7,5},{8,10},{9,11},{10,... | collective-permute-start | bytes 1179656 | tf_op jit(solution)/shard_map/ppermute | solution.py:310
  50.5 3.9 %collective-permute-done.6.far_ref = bf16[512,256]{1,0:T(8,128)(2,1)S(1)} collective-permute-done((bf16[512,256]{1,0:T(8,128)(2,1)S(1)}, bf16[512,256]{1,0:T(8,128)(2,1)S(1)}, u32[]{:S(2)}, u32[]{:S(2)}) %collective-permute-start.6) | collective-permute-done | bytes 262176 | tf_op jit(solution)/shard_map/ppermute | solution.py:310
  54.5 0.7 collective-permute-done.7.near_ref
  55.2 0.1 shard_map.106
  55.3 1.0 %collective-permute-start.8 = (bf16[512,128]{1,0:T(8,128)(2,1)S(1)}, bf16[512,128]{1,0:T(8,128)(2,1)S(1)}, u32[]{:S(2)}, u32[]{:S(2)}) collective-permute-start(bf16[512,128]{1,0:T(8,128)(2,1)S(1)} %get-tuple-element.67), channel_id=1, source_target_pairs={{0,2},{1,3},{2,0},{3,1},{4,6},{5,7},{6,4},{7,5},{8,10},{9,11},{10,... | collective-permute-start | bytes 393224 | tf_op jit(solution)/shard_map/ppermute | solution.py:310
  56.3 1.3 %collective-permute-start.10 = (bf16[128,1024]{1,0:T(8,128)(2,1)S(1)}, bf16[128,1024]{1,0:T(8,128)(2,1)S(1)}, u32[]{:S(2)}, u32[]{:S(2)}) collective-permute-start(bf16[128,1024]{1,0:T(8,128)(2,1)S(1)} %get-tuple-element.72.out_ref.refs_4_), channel_id=1, source_target_pairs={{0,4},{1,5},{2,6},{3,7},{4,0},{5,1},{6,2},{7,3},{8,12},{9,13},{10,... | collective-permute-start | bytes 786440 | tf_op jit(solution)/shard_map/ppermute | solution.py:310
  57.6 2.3 %collective-permute-start.9 = (bf16[128,1024]{1,0:T(8,128)(2,1)S(1)}, bf16[128,1024]{1,0:T(8,128)(2,1)S(1)}, u32[]{:S(2)}, u32[]{:S(2)}) collective-permute-start(bf16[128,1024]{1,0:T(8,128)(2,1)S(1)} %get-tuple-element.72.out_ref.refs_4_), channel_id=1, source_target_pairs={{0,8},{1,9},{2,10},{3,11},{4,12},{5,13},{6,14},{7,15},{8,0},{9,1},... | collective-permute-start | bytes 786440 | tf_op jit(solution)/shard_map/ppermute | solution.py:310
  60.0 0.5 collective-permute-done.11.refs_2_
  60.5 0.0 collective-permute-start.12
  60.5 1.4 %collective-permute-done.8.refs_1_ = bf16[512,128]{1,0:T(8,128)(2,1)S(1)} collective-permute-done((bf16[512,128]{1,0:T(8,128)(2,1)S(1)}, bf16[512,128]{1,0:T(8,128)(2,1)S(1)}, u32[]{:S(2)}, u32[]{:S(2)}) %collective-permute-start.8) | collective-permute-done | bytes 131104 | tf_op jit(solution)/shard_map/ppermute | solution.py:310
  61.9 4.5 %shard_map.107 = bf16[8,384,128]{2,1,0:T(8,128)(2,1)} custom-call(bf16[1024,128]{1,0:T(8,128)(2,1)S(1)} %get-tuple-element.44.queries_ref, bf16[128,1536]{1,0:T(8,128)(2,1)S(1)} %get-tuple-element.45.keys_t_ref, bf16[1536,128]{1,0:T(8,128)(2,1)S(1)} %get-tuple-element.46.vals_ref, bf16[1536,1024]{1,0:T(8,128)(2,1)S(1)} %get-tuple-element.47.probs_ref, ...), custom_call_target="tpu_custom_call" | custom-call | flops 1610612736 | bytes 6291456 | tf_op jit(solution)/shard_map/pallas_call | solution.py:147
  66.3 1.8 %collective-permute-done.10.refs_5_ = bf16[128,1024]{1,0:T(8,128)(2,1)S(1)} collective-permute-done((bf16[128,1024]{1,0:T(8,128)(2,1)S(1)}, bf16[128,1024]{1,0:T(8,128)(2,1)S(1)}, u32[]{:S(2)}, u32[]{:S(2)}) %collective-permute-start.10) | collective-permute-done | bytes 262176 | tf_op jit(solution)/shard_map/ppermute | solution.py:310
  68.2 3.4 %collective-permute-done.9.refs_6_ = bf16[128,1024]{1,0:T(8,128)(2,1)S(1)} collective-permute-done((bf16[128,1024]{1,0:T(8,128)(2,1)S(1)}, bf16[128,1024]{1,0:T(8,128)(2,1)S(1)}, u32[]{:S(2)}, u32[]{:S(2)}) %collective-permute-start.9) | collective-permute-done | bytes 262176 | tf_op jit(solution)/shard_map/ppermute | solution.py:310
  71.5 0.4 collective-permute-start.13
  71.9 3.8 %all-to-all-start.1 = ((bf16[8,384,128]{2,1,0:T(8,128)(2,1)}), bf16[8,384,128]{2,1,0:T(8,128)(2,1)S(1)}, u32[]{:S(2)}, u32[]{:S(2)}) async-start(bf16[8,384,128]{2,1,0:T(8,128)(2,1)} %shard_map.107), calls=%async_computation.1 | async-start | bytes 1572864 | tf_op jit(solution)/shard_map/all_to_all | solution.py:391
  75.7 3.0 %collective-permute-done.13.refs_7_ = bf16[128,1024]{1,0:T(8,128)(2,1)S(1)} collective-permute-done((bf16[128,1024]{1,0:T(8,128)(2,1)S(1)}, bf16[128,1024]{1,0:T(8,128)(2,1)S(1)}, u32[]{:S(2)}, u32[]{:S(2)}) %collective-permute-start.13) | collective-permute-done | bytes 262176 | tf_op jit(solution)/shard_map/ppermute | solution.py:310
  78.8 0.7 copy-done.6
  79.5 0.0 collective-permute-done.12.refs_3_
  79.5 0.0 copy-done.2
  79.5 0.9 copy-done.5
  80.5 0.9 copy-done.7
  81.4 1.4 %shard_map.109 = (bf16[512,384]{1,0:T(8,128)(2,1)S(1)}, bf16[512,384]{1,0:T(8,128)(2,1)S(1)}) custom-call(bf16[256,768]{1,0:T(8,128)(2,1)S(1)} %constant_dynamic-update-slice_fusion.piece_ref.refs_0_, bf16[256,768]{1,0:T(8,128)(2,1)S(1)} %copy-done.2, bf16[256,768]{1,0:T(8,128)(2,1)S(1)} %collective-permute-done.11.refs_2_, ...), custom_call_target="tpu_custom_call" | custom-call | flops 9663676416 | bytes 1572864 | tf_op jit(solution)/shard_map/pallas_call | solution.py:147
  82.8 0.1 collective-permute-start.14
  82.9 11.8 %collective-permute-done.14.other_ref = bf16[512,384]{1,0:T(8,128)(2,1)S(1)} collective-permute-done((bf16[512,384]{1,0:T(8,128)(2,1)S(1)}, bf16[512,384]{1,0:T(8,128)(2,1)S(1)}, u32[]{:S(2)}, u32[]{:S(2)}) %collective-permute-start.14) | collective-permute-done | bytes 393248 | tf_op jit(solution)/shard_map/ppermute | solution.py:310
  94.7 1.5 %shard_map.110 = f32[384,1024]{1,0:T(8,128)} custom-call(bf16[512,384]{1,0:T(8,128)(2,1)S(1)} %get-tuple-element.76.own_ref, bf16[512,384]{1,0:T(8,128)(2,1)S(1)} %collective-permute-done.14.other_ref), custom_call_target="tpu_custom_call" | custom-call | bytes 2359296 | tf_op jit(solution)/shard_map/pallas_call | solution.py:147
  96.2 0.0 all-to-all-done.1.tok_ref
  96.2 1.1 %shard_map.108 = (bf16[128,1024]{1,0:T(8,128)(2,1)}, bf16[128,1024]{1,0:T(8,128)(2,1)}, bf16[128,1024]{1,0:T(8,128)(2,1)}) custom-call(bf16[8,384,128]{2,1,0:T(8,128)(2,1)S(1)} %all-to-all-done.1.tok_ref), custom_call_target="tpu_custom_call" | custom-call | bytes 1572864 | tf_op jit(solution)/shard_map/pallas_call | solution.py:147
  (16 shorter events, 0.1 us)
Async XLA Ops:
  0.6 22.6 %copy-start = (bf16[384,1024]{1,0:T(8,128)(2,1)S(1)}, bf16[384,1024]{1,0:T(8,128)(2,1)}, u32[]{:S(2)}) copy-start(bf16[384,1024]{1,0:T(8,128)(2,1)} %own_ref.1) | copy-start | bytes 2359300
  0.6 20.8 %collective-permute-start.3 = (bf16[384,1024]{1,0:T(8,128)(2,1)}, bf16[384,1024]{1,0:T(8,128)(2,1)S(1)}, u32[]{:S(2)}, u32[]{:S(2)}) collective-permute-start(bf16[384,1024]{1,0:T(8,128)(2,1)} %own_ref.1), channel_id=1, source_target_pairs={{0,2},{1,3},{2,0},{3,1},{4,6},{5,7},{6,4},{7,5},{8,10},{9,11},{10,... | collective-permute-start | bytes 2359304 | tf_op jit(solution)/shard_map/ppermute | solution.py:310
  4.7 7.3 %collective-permute-start.2 = (bf16[64,768]{1,0:T(8,128)(2,1)S(1)}, bf16[64,768]{1,0:T(8,128)(2,1)S(1)}, u32[]{:S(2)}, u32[]{:S(2)}) collective-permute-start(bf16[64,768]{1,0:T(8,128)(2,1)S(1)} %get-tuple-element.78), channel_id=1, source_target_pairs={{0,12},{1,13},{2,14},{3,15},{4,8},{5,9},{6,10},{7,11},{8,4},{9,5},... | collective-permute-start | bytes 294920 | tf_op jit(solution)/shard_map/ppermute | solution.py:310
  8.4 6.1 %collective-permute-start = (bf16[64,768]{1,0:T(8,128)(2,1)S(1)}, bf16[64,768]{1,0:T(8,128)(2,1)S(1)}, u32[]{:S(2)}, u32[]{:S(2)}) collective-permute-start(bf16[64,768]{1,0:T(8,128)(2,1)S(1)} %get-tuple-element.79), channel_id=1, source_target_pairs={{0,4},{1,5},{2,6},{3,7},{4,0},{5,1},{6,2},{7,3},{8,12},{9,13},{10,... | collective-permute-start | bytes 294920 | tf_op jit(solution)/shard_map/ppermute | solution.py:310
  8.4 8.0 %collective-permute-start.1 = (bf16[64,768]{1,0:T(8,128)(2,1)S(1)}, bf16[64,768]{1,0:T(8,128)(2,1)S(1)}, u32[]{:S(2)}, u32[]{:S(2)}) collective-permute-start(bf16[64,768]{1,0:T(8,128)(2,1)S(1)} %get-tuple-element.81), channel_id=1, source_target_pairs={{0,8},{1,9},{2,10},{3,11},{4,12},{5,13},{6,14},{7,15},{8,0},{9,1},... | collective-permute-start | bytes 294920 | tf_op jit(solution)/shard_map/ppermute | solution.py:310
  16.4 27.7 %copy-start.3 = (bf16[2,512,128]{2,1,0:T(8,128)(2,1)S(1)}, bf16[2,512,128]{2,1,0:T(8,128)(2,1)}, u32[]{:S(2)}) copy-start(bf16[2,512,128]{2,1,0:T(8,128)(2,1)} %get-tuple-element.43.text_ref) | copy-start | bytes 786436
  16.4 27.7 %all-to-all-start = ((bf16[8,384,128]{2,1,0:T(8,128)(2,1)}), bf16[8,384,128]{2,1,0:T(8,128)(2,1)S(1)}, u32[]{:S(2)}, u32[]{:S(2)}) async-start(bf16[8,384,128]{2,1,0:T(8,128)(2,1)} %get-tuple-element.42), calls=%async_computation | async-start | bytes 1572864 | tf_op jit(solution)/shard_map/all_to_all | solution.py:354
  21.5 1.8 %collective-permute-start.4 = (bf16[256,768]{1,0:T(8,128)(2,1)S(1)}, bf16[256,768]{1,0:T(8,128)(2,1)S(1)}, u32[]{:S(2)}, u32[]{:S(2)}) collective-permute-start(bf16[256,768]{1,0:T(8,128)(2,1)S(1)} %constant_dynamic-update-slice_fusion.piece_ref.refs_0_), channel_id=1, source_target_pairs={{0,1},{1,0},{2,3},{3,2},{4,5},{5,4},{6,7},{7,6},{8,9},{9,8},{10,11... | collective-permute-start | bytes 1179656 | tf_op jit(solution)/shard_map/ppermute | solution.py:310
  23.3 1.5 %copy-start.1 = (bf16[256,768]{1,0:T(8,128)(2,1)}, bf16[256,768]{1,0:T(8,128)(2,1)S(1)}, u32[]{:S(2)}) copy-start(bf16[256,768]{1,0:T(8,128)(2,1)S(1)} %collective-permute-done.4.swapped_ref.refs_1_) | copy-start | bytes 1179652
  24.7 16.3 %collective-permute-start.5 = (bf16[512,256]{1,0:T(8,128)(2,1)S(1)}, bf16[512,256]{1,0:T(8,128)(2,1)S(1)}, u32[]{:S(2)}, u32[]{:S(2)}) collective-permute-start(bf16[512,256]{1,0:T(8,128)(2,1)S(1)} %get-tuple-element.60), channel_id=1, source_target_pairs={{0,4},{1,5},{2,6},{3,7},{4,0},{5,1},{6,2},{7,3},{8,12},{9,13},{10,... | collective-permute-start | bytes 786440 | tf_op jit(solution)/shard_map/ppermute | solution.py:310
  41.1 13.4 %collective-permute-start.6 = (bf16[512,256]{1,0:T(8,128)(2,1)S(1)}, bf16[512,256]{1,0:T(8,128)(2,1)S(1)}, u32[]{:S(2)}, u32[]{:S(2)}) collective-permute-start(bf16[512,256]{1,0:T(8,128)(2,1)S(1)} %shard_map.105), channel_id=1, source_target_pairs={{0,8},{1,9},{2,10},{3,11},{4,12},{5,13},{6,14},{7,15},{8,0},{9,1},... | collective-permute-start | bytes 786440 | tf_op jit(solution)/shard_map/ppermute | solution.py:310
  43.7 11.5 %collective-permute-start.7 = (bf16[512,256]{1,0:T(8,128)(2,1)}, bf16[512,256]{1,0:T(8,128)(2,1)S(1)}, u32[]{:S(2)}, u32[]{:S(2)}) collective-permute-start(bf16[512,256]{1,0:T(8,128)(2,1)} %get-tuple-element.63), channel_id=1, source_target_pairs={{0,4},{1,5},{2,6},{3,7},{4,0},{5,1},{6,2},{7,3},{8,12},{9,13},{10,... | collective-permute-start | bytes 786440 | tf_op jit(solution)/shard_map/ppermute | solution.py:310
  49.0 11.4 %collective-permute-start.11 = (bf16[256,768]{1,0:T(8,128)(2,1)S(1)}, bf16[256,768]{1,0:T(8,128)(2,1)S(1)}, u32[]{:S(2)}, u32[]{:S(2)}) collective-permute-start(bf16[256,768]{1,0:T(8,128)(2,1)S(1)} %constant_dynamic-update-slice_fusion.piece_ref.refs_0_), channel_id=1, source_target_pairs={{0,2},{1,3},{2,0},{3,1},{4,6},{5,7},{6,4},{7,5},{8,10},{9,11},{10,... | collective-permute-start | bytes 1179656 | tf_op jit(solution)/shard_map/ppermute | solution.py:310
  55.3 6.6 %collective-permute-start.8 = (bf16[512,128]{1,0:T(8,128)(2,1)S(1)}, bf16[512,128]{1,0:T(8,128)(2,1)S(1)}, u32[]{:S(2)}, u32[]{:S(2)}) collective-permute-start(bf16[512,128]{1,0:T(8,128)(2,1)S(1)} %get-tuple-element.67), channel_id=1, source_target_pairs={{0,2},{1,3},{2,0},{3,1},{4,6},{5,7},{6,4},{7,5},{8,10},{9,11},{10,... | collective-permute-start | bytes 393224 | tf_op jit(solution)/shard_map/ppermute | solution.py:310
  56.3 11.9 %collective-permute-start.10 = (bf16[128,1024]{1,0:T(8,128)(2,1)S(1)}, bf16[128,1024]{1,0:T(8,128)(2,1)S(1)}, u32[]{:S(2)}, u32[]{:S(2)}) collective-permute-start(bf16[128,1024]{1,0:T(8,128)(2,1)S(1)} %get-tuple-element.72.out_ref.refs_4_), channel_id=1, source_target_pairs={{0,4},{1,5},{2,6},{3,7},{4,0},{5,1},{6,2},{7,3},{8,12},{9,13},{10,... | collective-permute-start | bytes 786440 | tf_op jit(solution)/shard_map/ppermute | solution.py:310
  57.6 13.9 %collective-permute-start.9 = (bf16[128,1024]{1,0:T(8,128)(2,1)S(1)}, bf16[128,1024]{1,0:T(8,128)(2,1)S(1)}, u32[]{:S(2)}, u32[]{:S(2)}) collective-permute-start(bf16[128,1024]{1,0:T(8,128)(2,1)S(1)} %get-tuple-element.72.out_ref.refs_4_), channel_id=1, source_target_pairs={{0,8},{1,9},{2,10},{3,11},{4,12},{5,13},{6,14},{7,15},{8,0},{9,1},... | collective-permute-start | bytes 786440 | tf_op jit(solution)/shard_map/ppermute | solution.py:310
  60.5 19.1 %collective-permute-start.12 = (bf16[256,768]{1,0:T(8,128)(2,1)S(1)}, bf16[256,768]{1,0:T(8,128)(2,1)S(1)}, u32[]{:S(2)}, u32[]{:S(2)}) collective-permute-start(bf16[256,768]{1,0:T(8,128)(2,1)S(1)} %collective-permute-done.11.refs_2_), channel_id=1, source_target_pairs={{0,1},{1,0},{2,3},{3,2},{4,5},{5,4},{6,7},{7,6},{8,9},{9,8},{10,11... | collective-permute-start | bytes 1179656 | tf_op jit(solution)/shard_map/ppermute | solution.py:310
  61.9 17.6 %copy-start.2 = (bf16[256,768]{1,0:T(8,128)(2,1)S(1)}, bf16[256,768]{1,0:T(8,128)(2,1)}, u32[]{:S(2)}) copy-start(bf16[256,768]{1,0:T(8,128)(2,1)} %copy-done.1) | copy-start | bytes 1179652
  71.5 7.3 %copy-start.4 = (bf16[128,1024]{1,0:T(8,128)(2,1)}, bf16[128,1024]{1,0:T(8,128)(2,1)S(1)}, u32[]{:S(2)}) copy-start(bf16[128,1024]{1,0:T(8,128)(2,1)S(1)} %collective-permute-done.9.refs_6_) | copy-start | bytes 786436
  71.5 7.2 %collective-permute-start.13 = (bf16[128,1024]{1,0:T(8,128)(2,1)S(1)}, bf16[128,1024]{1,0:T(8,128)(2,1)S(1)}, u32[]{:S(2)}, u32[]{:S(2)}) collective-permute-start(bf16[128,1024]{1,0:T(8,128)(2,1)S(1)} %collective-permute-done.9.refs_6_), channel_id=1, source_target_pairs={{0,4},{1,5},{2,6},{3,7},{4,0},{5,1},{6,2},{7,3},{8,12},{9,13},{10,... | collective-permute-start | bytes 786440 | tf_op jit(solution)/shard_map/ppermute | solution.py:310
  71.9 24.3 %all-to-all-start.1 = ((bf16[8,384,128]{2,1,0:T(8,128)(2,1)}), bf16[8,384,128]{2,1,0:T(8,128)(2,1)S(1)}, u32[]{:S(2)}, u32[]{:S(2)}) async-start(bf16[8,384,128]{2,1,0:T(8,128)(2,1)} %shard_map.107), calls=%async_computation.1 | async-start | bytes 1572864 | tf_op jit(solution)/shard_map/all_to_all | solution.py:391
  78.8 0.7 copy-start.6
  79.5 1.0 copy-start.5
  80.5 0.9 copy-start.7
  82.8 11.9 %collective-permute-start.14 = (bf16[512,384]{1,0:T(8,128)(2,1)S(1)}, bf16[512,384]{1,0:T(8,128)(2,1)S(1)}, u32[]{:S(2)}, u32[]{:S(2)}) collective-permute-start(bf16[512,384]{1,0:T(8,128)(2,1)S(1)} %get-tuple-element.77), channel_id=1, source_target_pairs={{0,2},{1,3},{2,0},{3,1},{4,6},{5,7},{6,4},{7,5},{8,10},{9,11},{10,... | collective-permute-start | bytes 1179656 | tf_op jit(solution)/shard_map/ppermute | solution.py:310

commit v24 on v23

--- a/solution.py
+++ b/solution.py
@@ -255,37 +255,53 @@
         ref[...] = jnp.dot(outs[...], cot[:, cols], preferred_element_type=F32).astype(BF16)
 
 
-def backward_kernel(queries_ref, keys_t_ref, vals_ref, probs_ref, out_ref, *refs, chunk):
-    *grad_refs, send_ref, dk, dv = refs
-    n, three, _ = send_ref.shape
-    rows = three // 3
-    image = n * rows
+def backward_half(first, queries_ref, keys_t_ref, vals_ref, probs_ref, out_ref, grads_ref, dq_ref, dk, dv, chunk):
+    image = dk.shape[0]
     scale = HD ** (-0.5)
-    per = chunk // rows
-    order = query_order(n)
-    half = image // chunk // 2
-    for c in range(image // chunk):
-        span = slice(c * chunk, (c + 1) * chunk)
-        within = slice(c % half * chunk, (c % half + 1) * chunk)
-        grads = grad_refs[c // half][within, :]
+    tokens = grads_ref.shape[0]
+    start = 0 if first else tokens
+    for c in range(tokens // chunk):
+        span = slice(start + c * chunk, start + (c + 1) * chunk)
+        within = slice(c * chunk, (c + 1) * chunk)
+        grads = grads_ref[within, :]
         row_dot = jnp.sum(
             grads.astype(F32).T * out_ref[:, span].astype(F32), axis=0, keepdims=True
         )
         prob_grad = lax.dot_general(vals_ref[...], grads, NT, preferred_element_type=F32)
         low = probs_ref[:, span]
         score_grad = (low.astype(F32) * (prob_grad - row_dot)).astype(BF16)
-        dq = (jnp.dot(keys_t_ref[...], score_grad, preferred_element_type=F32) * scale).T.astype(BF16)
-        for i in range(per):
-            send_ref[order[c * per + i], 0:rows, :] = dq[i * rows : (i + 1) * rows, :]
+        dq = jnp.dot(keys_t_ref[...], score_grad, preferred_element_type=F32) * scale
+        dq_ref[within, :] = dq.T.astype(BF16)
         dk_part = jnp.dot(score_grad[0:image, :], queries_ref[span, :], preferred_element_type=F32)
         dv_part = jnp.dot(low[0:image, :], grads, preferred_element_type=F32)
-        if c == 0:
+        if first and c == 0:
             dk[...] = dk_part
             dv[...] = dv_part
         else:
             dk[...] += dk_part
             dv[...] += dv_part
-    send_ref[:, rows : 2 * rows, :] = (dk[...] * scale).astype(BF16).reshape(n, rows, HD)
+
+
+def backward_first_kernel(queries_ref, keys_t_ref, vals_ref, probs_ref, out_ref, grads_ref, dq_ref, dk_ref, dv_ref, *, chunk):
+    backward_half(
+        True, queries_ref, keys_t_ref, vals_ref, probs_ref, out_ref, grads_ref, dq_ref, dk_ref, dv_ref, chunk
+    )
+
+
+def backward_second_kernel(
+    queries_ref, keys_t_ref, vals_ref, probs_ref, out_ref, grads_ref, dq0_ref, dk_ref, dv_ref, send_ref, dq1_ref, dk, dv, *, chunk
+):
+    n, three, _ = send_ref.shape
+    rows = three // 3
+    dk[...] = dk_ref[...]
+    dv[...] = dv_ref[...]
+    backward_half(
+        False, queries_ref, keys_t_ref, vals_ref, probs_ref, out_ref, grads_ref, dq1_ref, dk, dv, chunk
+    )
+    for i, source in enumerate(query_order(n)):
+        ref, at = (dq0_ref, i) if 2 * i < n else (dq1_ref, i - n // 2)
+        send_ref[source, 0:rows, :] = ref[at * rows : (at + 1) * rows, :]
+    send_ref[:, rows : 2 * rows, :] = (dk[...] * HD ** (-0.5)).astype(BF16).reshape(n, rows, HD)
     send_ref[:, 2 * rows : 3 * rows, :] = dv[...].astype(BF16).reshape(n, rows, HD)
 
 
@@ -377,16 +393,23 @@
     kept, give = call(finish_kernel, [shape((image // 2, HD), BF16)] * 2, [mine, near, far])
     got = exchange(give, 1)
     out_near, out_far = exchange(out_late, 2), exchange(out_late, 4)
-    row, _ = lax.optimization_barrier((row, out_t))
+    row, got = lax.optimization_barrier((row, got))
     other_row = exchange(row, 1)
     other_swapped = exchange(other_row, cores=True)
+    dq, dk, dv = call(
+        functools.partial(backward_first_kernel, chunk=chunk),
+        [shape((image // 2, HD), BF16)] + [shape((image, HD), F32)] * 2,
+        [queries, keys_t, vals, probs, out_t, kept],
+        flops=4 * total * image * HD,
+        moved=2 * total * image,
+    )
     (grad_out,) = call(
-        functools.partial(backward_kernel, chunk=chunk),
+        functools.partial(backward_second_kernel, chunk=chunk),
         [shape((n, 3 * rows, HD), BF16)],
-        [queries, keys_t, vals, probs, out_t, kept, got],
-        scratch=[pltpu.VMEM((image, HD), F32), pltpu.VMEM((image, HD), F32)],
-        flops=8 * total * image * HD,
-        moved=4 * total * image,
+        [queries, keys_t, vals, probs, out_t, got, dq, dk, dv],
+        scratch=[pltpu.VMEM((image // 2, HD), BF16)] + [pltpu.VMEM((image, HD), F32)] * 2,
+        flops=4 * total * image * HD,
+        moved=2 * total * image,
     )
     grad_in = lax.all_to_all(grad_out, "seq", split_axis=0, concat_axis=0, tiled=True)
     out_far, out_near, other_row, _ = lax.optimization_barrier((out_far, out_near, other_row, grad_out))

time: 97.6 us -> 104 us (1.066)
  starting transfers between devices: 27.1 us -> 32.2 us
  waiting for transfers between devices: 48.5 us -> 51.8 us
  local copies, waits for them, and re-layouts: 3.72 us -> 2.06 us
    ppermute x15, starting transfers between devices: 19 us -> 23.8 us  [exchange(): return lax.ppermute(array, ('seq', 'fsdp'), pairs)]
    ppermute x15, waiting for transfers between devices: 48.5 us -> 51.8 us  [exchange(): return lax.ppermute(array, ('seq', 'fsdp'), pairs)]
    unnamed x19 -> x11, local copies, waits for them, and re-layouts: 2.65 us -> 0.99 us
    pallas_call x9 -> x10, Pallas kernels: 17.3 us -> 17.4 us  [call(): pl.pallas_call(kernel, out_shape=outs, grid_spec=pltpu.PrefetchScalarGrid...]
  transfers between devices with their start and end apart: 17 -> 17, of which waited for: 14 -> 11; matrix products, arithmetic and copies ran while one was open for 1% -> 1% of each run, Pallas kernels for 17% -> 16%
where the time goes in v24:
time: 104 us
  waiting for transfers between devices  51.8 us (50%)
  starting transfers between devices  32.2 us (31%)
  Pallas kernels  17.4 us (17%)
  local copies, waits for them, and re-layouts  2.06 us (2%)
    ppermute x15, waiting for transfers between devices, exchange(): return lax.ppermute(array, ('seq', 'fsdp'), pairs)  51.8 us
    ppermute x15, starting transfers between devices, exchange(): return lax.ppermute(array, ('seq', 'fsdp'), pairs)  23.8 us
    pallas_call x10, Pallas kernels, call(): pl.pallas_call(kernel, out_shape=outs, grid_spec=pltpu.PrefetchScalarGrid...  17.4 us
    all_to_all x1, starting transfers between devices, local(): lax.all_to_all(grad_out, 'seq', split_axis=0, concat_axis=0, tiled=True)  4.46 us
    all_to_all x1, starting transfers between devices, local(): lax.all_to_all(tok_out, 'seq', split_axis=0, concat_axis=0, tiled=True)  3.9 us
  transfers between devices with their start and end apart: 17, of which 11 were waited for; matrix products, arithmetic and copies ran while one was open for 1% of the time, Pallas kernels for 16%

profile of v24, /device:TPU:0, one launch (start us, length us, event | category | flops | bytes accessed | tf_op | source)
XLA Modules:
  0.0 104.1 jit_solution(10769257821008740691)
XLA Ops:
  0.6 0.0 copy-start
  0.6 3.0 %collective-permute-start.3 = (bf16[384,1024]{1,0:T(8,128)(2,1)}, bf16[384,1024]{1,0:T(8,128)(2,1)S(1)}, u32[]{:S(2)}, u32[]{:S(2)}) collective-permute-start(bf16[384,1024]{1,0:T(8,128)(2,1)} %own_ref.1), channel_id=1, source_target_pairs={{0,2},{1,3},{2,0},{3,1},{4,6},{5,7},{6,4},{7,5},{8,10},{9,11},{10,... | collective-permute-start | bytes 2359304 | tf_op jit(solution)/shard_map/ppermute | solution.py:326
  3.7 1.1 %fusion = (bf16[64,768]{1,0:T(8,128)(2,1)S(1)}, bf16[64,768]{1,0:T(8,128)(2,1)S(1)}, bf16[64,768]{1,0:T(8,128)(2,1)S(1)}, bf16[64,768]{1,0:T(8,128)(2,1)S(1)}) fusion(bf16[128,3072]{1,0:T(8,128)(2,1)} %param.13, s32[]{:T(128)S(6)} %select_n.23, s32[]{:T(128)S(6)} %select_n.28, s32[]{:T(128)S(6)} %select_n.26, s32[]{:T(128)S(6)} %select_n.25, s32[]{:T(128)S(6)} %select_n.27), kind=kLoop, calls=%fused_computation.4 | loop fusion | bytes 786452 | tf_op jit(solution)/shard_map/dynamic_slice | solution.py:335
  4.7 1.6 %collective-permute-start = (bf16[64,768]{1,0:T(8,128)(2,1)S(1)}, bf16[64,768]{1,0:T(8,128)(2,1)S(1)}, u32[]{:S(2)}, u32[]{:S(2)}) collective-permute-start(bf16[64,768]{1,0:T(8,128)(2,1)S(1)} %get-tuple-element.87), channel_id=1, source_target_pairs={{0,4},{1,5},{2,6},{3,7},{4,0},{5,1},{6,2},{7,3},{8,12},{9,13},{10,... | collective-permute-start | bytes 294920 | tf_op jit(solution)/shard_map/ppermute | solution.py:326
  6.4 2.6 %collective-permute-start.1 = (bf16[64,768]{1,0:T(8,128)(2,1)S(1)}, bf16[64,768]{1,0:T(8,128)(2,1)S(1)}, u32[]{:S(2)}, u32[]{:S(2)}) collective-permute-start(bf16[64,768]{1,0:T(8,128)(2,1)S(1)} %get-tuple-element.89), channel_id=1, source_target_pairs={{0,8},{1,9},{2,10},{3,11},{4,12},{5,13},{6,14},{7,15},{8,0},{9,1},... | collective-permute-start | bytes 294920 | tf_op jit(solution)/shard_map/ppermute | solution.py:326
  9.0 0.2 collective-permute-start.2
  9.2 2.3 %shard_map.102 = (bf16[8,384,128]{2,1,0:T(8,128)(2,1)}, bf16[2,512,128]{2,1,0:T(8,128)(2,1)}) custom-call(s32[1]{0:T(128)} %bitcast.me_ref, bf16[128,1024]{1,0:T(8,128)(2,1)} %q_ref.1, bf16[128,1024]{1,0:T(8,128)(2,1)} %k_ref.1, bf16[128,1024]{1,0:T(8,128)(2,1)} %v_ref.1, bf16[512,1024]{1,0:T(8,128)(2,1)} %kt_ref.1, bf16[512,1024]{1,0:T(8,128)(2,1)} %vt_ref.1), custom_call_target="tpu_custom_call" | custom-call | bytes 1572864 | tf_op jit(solution)/shard_map/pallas_call | solution.py:147
  11.5 0.0 collective-permute-done
  11.5 5.0 %collective-permute-done.1 = bf16[64,768]{1,0:T(8,128)(2,1)S(1)} collective-permute-done((bf16[64,768]{1,0:T(8,128)(2,1)S(1)}, bf16[64,768]{1,0:T(8,128)(2,1)S(1)}, u32[]{:S(2)}, u32[]{:S(2)}) %collective-permute-start.1) | collective-permute-done | bytes 98336 | tf_op jit(solution)/shard_map/ppermute | solution.py:326
  16.5 0.0 collective-permute-done.2
  16.5 3.9 %all-to-all-start = ((bf16[8,384,128]{2,1,0:T(8,128)(2,1)}), bf16[8,384,128]{2,1,0:T(8,128)(2,1)S(1)}, u32[]{:S(2)}, u32[]{:S(2)}) async-start(bf16[8,384,128]{2,1,0:T(8,128)(2,1)} %get-tuple-element.46), calls=%async_computation | async-start | bytes 1572864 | tf_op jit(solution)/shard_map/all_to_all | solution.py:370
  20.4 2.4 %collective-permute-done.3.other_ref = bf16[384,1024]{1,0:T(8,128)(2,1)S(1)} collective-permute-done((bf16[384,1024]{1,0:T(8,128)(2,1)}, bf16[384,1024]{1,0:T(8,128)(2,1)S(1)}, u32[]{:S(2)}, u32[]{:S(2)}) %collective-permute-start.3) | collective-permute-done | bytes 786464 | tf_op jit(solution)/shard_map/ppermute | solution.py:326
  22.9 0.1 collective-permute-start.4
  23.0 1.7 %collective-permute-done.4.swapped_ref.refs_1_ = bf16[256,768]{1,0:T(8,128)(2,1)S(1)} collective-permute-done((bf16[256,768]{1,0:T(8,128)(2,1)S(1)}, bf16[256,768]{1,0:T(8,128)(2,1)S(1)}, u32[]{:S(2)}, u32[]{:S(2)}) %collective-permute-start.4) | collective-permute-done | bytes 393248 | tf_op jit(solution)/shard_map/ppermute | solution.py:326
  24.7 0.0 copy-done
  24.7 1.5 %shard_map.104 = (f32[512,256]{1,0:T(8,128)S(1)}, bf16[512,256]{1,0:T(8,128)(2,1)}, f32[512,256]{1,0:T(8,128)S(1)}, bf16[512,256]{1,0:T(8,128)(2,1)S(1)}) custom-call(bf16[256,768]{1,0:T(8,128)(2,1)S(1)} %constant_dynamic-update-slice_fusion.piece_ref.refs_0_, bf16[256,768]{1,0:T(8,128)(2,1)S(1)} %collective-permute-done.4.swapped_ref.refs_1_, ...), custom_call_target="tpu_custom_call" | custom-call | flops 805306368 | bytes 1572864 | tf_op jit(solution)/shard_map/pallas_call | solution.py:147
  26.2 2.5 %collective-permute-start.5 = (bf16[512,256]{1,0:T(8,128)(2,1)S(1)}, bf16[512,256]{1,0:T(8,128)(2,1)S(1)}, u32[]{:S(2)}, u32[]{:S(2)}) collective-permute-start(bf16[512,256]{1,0:T(8,128)(2,1)S(1)} %get-tuple-element.64), channel_id=1, source_target_pairs={{0,4},{1,5},{2,6},{3,7},{4,0},{5,1},{6,2},{7,3},{8,12},{9,13},{10,... | collective-permute-start | bytes 786440 | tf_op jit(solution)/shard_map/ppermute | solution.py:326
  28.6 11.8 %collective-permute-done.5.received_ref = bf16[512,256]{1,0:T(8,128)(2,1)S(1)} collective-permute-done((bf16[512,256]{1,0:T(8,128)(2,1)S(1)}, bf16[512,256]{1,0:T(8,128)(2,1)S(1)}, u32[]{:S(2)}, u32[]{:S(2)}) %collective-permute-start.5) | collective-permute-done | bytes 262176 | tf_op jit(solution)/shard_map/ppermute | solution.py:326
  40.4 2.4 %collective-permute-start.6 = (bf16[512,256]{1,0:T(8,128)(2,1)S(1)}, bf16[512,256]{1,0:T(8,128)(2,1)S(1)}, u32[]{:S(2)}, u32[]{:S(2)}) collective-permute-start(bf16[512,256]{1,0:T(8,128)(2,1)S(1)} %shard_map.105), channel_id=1, source_target_pairs={{0,8},{1,9},{2,10},{3,11},{4,12},{5,13},{6,14},{7,15},{8,0},{9,1},... | collective-permute-start | bytes 786440 | tf_op jit(solution)/shard_map/ppermute | solution.py:326
  42.9 0.0 copy-done.1
  42.9 2.5 %collective-permute-start.7 = (bf16[512,256]{1,0:T(8,128)(2,1)}, bf16[512,256]{1,0:T(8,128)(2,1)S(1)}, u32[]{:S(2)}, u32[]{:S(2)}) collective-permute-start(bf16[512,256]{1,0:T(8,128)(2,1)} %get-tuple-element.67), channel_id=1, source_target_pairs={{0,4},{1,5},{2,6},{3,7},{4,0},{5,1},{6,2},{7,3},{8,12},{9,13},{10,... | collective-permute-start | bytes 786440 | tf_op jit(solution)/shard_map/ppermute | solution.py:326
  45.3 0.0 all-to-all-done.tok_ref
  45.3 0.9 copy-done.3
  46.3 4.9 %shard_map.103 = (bf16[1536,1024]{1,0:T(8,128)(2,1)S(1)}, bf16[128,1024]{1,0:T(8,128)(2,1)S(1)}, bf16[1024,128]{1,0:T(8,128)(2,1)S(1)}, bf16[128,1536]{1,0:T(8,128)(2,1)S(1)}, bf16[1536,128]{1,0:T(8,128)(2,1)S(1)}) custom-call(bf16[8,384,128]{2,1,0:T(8,128)(2,1)S(1)} %all-to-all-done.tok_ref, bf16[2,512,128]{2,1,0:T(8,128)(2,1)S(1)} %copy-done.3), custom_call_target="tpu_custom_call" | custom-call | flops 805306368 | bytes 6291456 | tf_op jit(solution)/shard_map/pallas_call | solution.py:147
  51.2 4.0 %collective-permute-done.6.far_ref = bf16[512,256]{1,0:T(8,128)(2,1)S(1)} collective-permute-done((bf16[512,256]{1,0:T(8,128)(2,1)S(1)}, bf16[512,256]{1,0:T(8,128)(2,1)S(1)}, u32[]{:S(2)}, u32[]{:S(2)}) %collective-permute-start.6) | collective-permute-done | bytes 262176 | tf_op jit(solution)/shard_map/ppermute | solution.py:326
  55.2 0.3 collective-permute-done.7.near_ref
  55.5 0.1 shard_map.106
  55.6 2.3 %collective-permute-start.8 = (bf16[512,128]{1,0:T(8,128)(2,1)S(1)}, bf16[512,128]{1,0:T(8,128)(2,1)S(1)}, u32[]{:S(2)}, u32[]{:S(2)}) collective-permute-start(bf16[512,128]{1,0:T(8,128)(2,1)S(1)} %get-tuple-element.70), channel_id=1, source_target_pairs={{0,2},{1,3},{2,0},{3,1},{4,6},{5,7},{6,4},{7,5},{8,10},{9,11},{10,... | collective-permute-start | bytes 393224 | tf_op jit(solution)/shard_map/ppermute | solution.py:326
  57.9 3.2 %collective-permute-done.8.grads_ref = bf16[512,128]{1,0:T(8,128)(2,1)S(1)} collective-permute-done((bf16[512,128]{1,0:T(8,128)(2,1)S(1)}, bf16[512,128]{1,0:T(8,128)(2,1)S(1)}, u32[]{:S(2)}, u32[]{:S(2)}) %collective-permute-start.8) | collective-permute-done | bytes 131104 | tf_op jit(solution)/shard_map/ppermute | solution.py:326
  61.1 1.8 %collective-permute-start.11 = (bf16[256,768]{1,0:T(8,128)(2,1)S(1)}, bf16[256,768]{1,0:T(8,128)(2,1)S(1)}, u32[]{:S(2)}, u32[]{:S(2)}) collective-permute-start(bf16[256,768]{1,0:T(8,128)(2,1)S(1)} %constant_dynamic-update-slice_fusion.piece_ref.refs_0_), channel_id=1, source_target_pairs={{0,2},{1,3},{2,0},{3,1},{4,6},{5,7},{6,4},{7,5},{8,10},{9,11},{10,... | collective-permute-start | bytes 1179656 | tf_op jit(solution)/shard_map/ppermute | solution.py:326
  62.9 0.0 collective-permute-start.10
  62.9 2.4 %collective-permute-start.9 = (bf16[128,1024]{1,0:T(8,128)(2,1)S(1)}, bf16[128,1024]{1,0:T(8,128)(2,1)S(1)}, u32[]{:S(2)}, u32[]{:S(2)}) collective-permute-start(bf16[128,1024]{1,0:T(8,128)(2,1)S(1)} %get-tuple-element.80.out_ref.refs_4_), channel_id=1, source_target_pairs={{0,8},{1,9},{2,10},{3,11},{4,12},{5,13},{6,14},{7,15},{8,0},{9,1},... | collective-permute-start | bytes 786440 | tf_op jit(solution)/shard_map/ppermute | solution.py:326
  65.3 5.8 %collective-permute-done.11.refs_2_ = bf16[256,768]{1,0:T(8,128)(2,1)S(1)} collective-permute-done((bf16[256,768]{1,0:T(8,128)(2,1)S(1)}, bf16[256,768]{1,0:T(8,128)(2,1)S(1)}, u32[]{:S(2)}, u32[]{:S(2)}) %collective-permute-start.11) | collective-permute-done | bytes 393248 | tf_op jit(solution)/shard_map/ppermute | solution.py:326
  71.1 0.0 collective-permute-start.12
  71.1 1.8 %shard_map.107 = (bf16[512,128]{1,0:T(8,128)(2,1)S(1)}, f32[1024,128]{1,0:T(8,128)S(1)}, f32[1024,128]{1,0:T(8,128)S(1)}) custom-call(bf16[1024,128]{1,0:T(8,128)(2,1)S(1)} %get-tuple-element.48.queries_ref, bf16[128,1536]{1,0:T(8,128)(2,1)S(1)} %get-tuple-element.49.keys_t_ref, bf16[1536,128]{1,0:T(8,128)(2,1)S(1)} %get-tuple-element.50.vals_ref, ...), custom_call_target="tpu_custom_call" | custom-call | flops 805306368 | bytes 3145728 | tf_op jit(solution)/shard_map/pallas_call | solution.py:147
  73.0 2.8 %shard_map.108 = bf16[8,384,128]{2,1,0:T(8,128)(2,1)} custom-call(bf16[1024,128]{1,0:T(8,128)(2,1)S(1)} %get-tuple-element.48.queries_ref, bf16[128,1536]{1,0:T(8,128)(2,1)S(1)} %get-tuple-element.49.keys_t_ref, bf16[1536,128]{1,0:T(8,128)(2,1)S(1)} %get-tuple-element.50.vals_ref, bf16[1536,1024]{1,0:T(8,128)(2,1)S(1)} %get-tuple-element.51.probs_ref, ...), custom_call_target="tpu_custom_call" | custom-call | flops 805306368 | bytes 3145728 | tf_op jit(solution)/shard_map/pallas_call | solution.py:147
  75.7 0.0 collective-permute-done.10.refs_5_
  75.7 0.1 collective-permute-done.9.refs_6_
  75.8 0.2 collective-permute-start.13
  76.0 4.5 %all-to-all-start.1 = ((bf16[8,384,128]{2,1,0:T(8,128)(2,1)}), bf16[8,384,128]{2,1,0:T(8,128)(2,1)S(1)}, u32[]{:S(2)}, u32[]{:S(2)}) async-start(bf16[8,384,128]{2,1,0:T(8,128)(2,1)} %shard_map.108), calls=%async_computation.1 | async-start | bytes 1572864 | tf_op jit(solution)/shard_map/all_to_all | solution.py:414
  80.4 4.5 %collective-permute-done.13.refs_7_ = bf16[128,1024]{1,0:T(8,128)(2,1)S(1)} collective-permute-done((bf16[128,1024]{1,0:T(8,128)(2,1)S(1)}, bf16[128,1024]{1,0:T(8,128)(2,1)S(1)}, u32[]{:S(2)}, u32[]{:S(2)}) %collective-permute-start.13) | collective-permute-done | bytes 262176 | tf_op jit(solution)/shard_map/ppermute | solution.py:326
  84.9 0.0 collective-permute-done.12.refs_3_
  84.9 1.4 %shard_map.110 = (bf16[512,384]{1,0:T(8,128)(2,1)S(1)}, bf16[512,384]{1,0:T(8,128)(2,1)S(1)}) custom-call(bf16[256,768]{1,0:T(8,128)(2,1)S(1)} %constant_dynamic-update-slice_fusion.piece_ref.refs_0_, bf16[256,768]{1,0:T(8,128)(2,1)S(1)} %copy-done.2, bf16[256,768]{1,0:T(8,128)(2,1)S(1)} %collective-permute-done.11.refs_2_, ...), custom_call_target="tpu_custom_call" | custom-call | flops 9663676416 | bytes 1572864 | tf_op jit(solution)/shard_map/pallas_call | solution.py:147
  86.3 2.2 %collective-permute-start.14 = (bf16[512,384]{1,0:T(8,128)(2,1)S(1)}, bf16[512,384]{1,0:T(8,128)(2,1)S(1)}, u32[]{:S(2)}, u32[]{:S(2)}) collective-permute-start(bf16[512,384]{1,0:T(8,128)(2,1)S(1)} %get-tuple-element.85), channel_id=1, source_target_pairs={{0,2},{1,3},{2,0},{3,1},{4,6},{5,7},{6,4},{7,5},{8,10},{9,11},{10,... | collective-permute-start | bytes 1179656 | tf_op jit(solution)/shard_map/ppermute | solution.py:326
  88.5 13.1 %collective-permute-done.14.other_ref = bf16[512,384]{1,0:T(8,128)(2,1)S(1)} collective-permute-done((bf16[512,384]{1,0:T(8,128)(2,1)S(1)}, bf16[512,384]{1,0:T(8,128)(2,1)S(1)}, u32[]{:S(2)}, u32[]{:S(2)}) %collective-permute-start.14) | collective-permute-done | bytes 393248 | tf_op jit(solution)/shard_map/ppermute | solution.py:326
  101.6 1.5 %shard_map.111 = f32[384,1024]{1,0:T(8,128)} custom-call(bf16[512,384]{1,0:T(8,128)(2,1)S(1)} %get-tuple-element.84.own_ref, bf16[512,384]{1,0:T(8,128)(2,1)S(1)} %collective-permute-done.14.other_ref), custom_call_target="tpu_custom_call" | custom-call | bytes 2359296 | tf_op jit(solution)/shard_map/pallas_call | solution.py:147
  103.0 0.0 all-to-all-done.1.tok_ref
  103.1 1.1 %shard_map.109 = (bf16[128,1024]{1,0:T(8,128)(2,1)}, bf16[128,1024]{1,0:T(8,128)(2,1)}, bf16[128,1024]{1,0:T(8,128)(2,1)}) custom-call(bf16[8,384,128]{2,1,0:T(8,128)(2,1)S(1)} %all-to-all-done.1.tok_ref), custom_call_target="tpu_custom_call" | custom-call | bytes 1572864 | tf_op jit(solution)/shard_map/pallas_call | solution.py:147
  (9 shorter events, 0.1 us)
Async XLA Ops:
  0.6 24.1 %copy-start = (bf16[384,1024]{1,0:T(8,128)(2,1)S(1)}, bf16[384,1024]{1,0:T(8,128)(2,1)}, u32[]{:S(2)}) copy-start(bf16[384,1024]{1,0:T(8,128)(2,1)} %own_ref.1) | copy-start | bytes 2359300
  0.6 22.2 %collective-permute-start.3 = (bf16[384,1024]{1,0:T(8,128)(2,1)}, bf16[384,1024]{1,0:T(8,128)(2,1)S(1)}, u32[]{:S(2)}, u32[]{:S(2)}) collective-permute-start(bf16[384,1024]{1,0:T(8,128)(2,1)} %own_ref.1), channel_id=1, source_target_pairs={{0,2},{1,3},{2,0},{3,1},{4,6},{5,7},{6,4},{7,5},{8,10},{9,11},{10,... | collective-permute-start | bytes 2359304 | tf_op jit(solution)/shard_map/ppermute | solution.py:326
  4.7 6.8 %collective-permute-start = (bf16[64,768]{1,0:T(8,128)(2,1)S(1)}, bf16[64,768]{1,0:T(8,128)(2,1)S(1)}, u32[]{:S(2)}, u32[]{:S(2)}) collective-permute-start(bf16[64,768]{1,0:T(8,128)(2,1)S(1)} %get-tuple-element.87), channel_id=1, source_target_pairs={{0,4},{1,5},{2,6},{3,7},{4,0},{5,1},{6,2},{7,3},{8,12},{9,13},{10,... | collective-permute-start | bytes 294920 | tf_op jit(solution)/shard_map/ppermute | solution.py:326
  6.4 10.1 %collective-permute-start.1 = (bf16[64,768]{1,0:T(8,128)(2,1)S(1)}, bf16[64,768]{1,0:T(8,128)(2,1)S(1)}, u32[]{:S(2)}, u32[]{:S(2)}) collective-permute-start(bf16[64,768]{1,0:T(8,128)(2,1)S(1)} %get-tuple-element.89), channel_id=1, source_target_pairs={{0,8},{1,9},{2,10},{3,11},{4,12},{5,13},{6,14},{7,15},{8,0},{9,1},... | collective-permute-start | bytes 294920 | tf_op jit(solution)/shard_map/ppermute | solution.py:326
  9.0 7.6 %collective-permute-start.2 = (bf16[64,768]{1,0:T(8,128)(2,1)S(1)}, bf16[64,768]{1,0:T(8,128)(2,1)S(1)}, u32[]{:S(2)}, u32[]{:S(2)}) collective-permute-start(bf16[64,768]{1,0:T(8,128)(2,1)S(1)} %get-tuple-element.86), channel_id=1, source_target_pairs={{0,12},{1,13},{2,14},{3,15},{4,8},{5,9},{6,10},{7,11},{8,4},{9,5},... | collective-permute-start | bytes 294920 | tf_op jit(solution)/shard_map/ppermute | solution.py:326
  16.5 28.8 %all-to-all-start = ((bf16[8,384,128]{2,1,0:T(8,128)(2,1)}), bf16[8,384,128]{2,1,0:T(8,128)(2,1)S(1)}, u32[]{:S(2)}, u32[]{:S(2)}) async-start(bf16[8,384,128]{2,1,0:T(8,128)(2,1)} %get-tuple-element.46), calls=%async_computation | async-start | bytes 1572864 | tf_op jit(solution)/shard_map/all_to_all | solution.py:370
  22.9 1.8 %collective-permute-start.4 = (bf16[256,768]{1,0:T(8,128)(2,1)S(1)}, bf16[256,768]{1,0:T(8,128)(2,1)S(1)}, u32[]{:S(2)}, u32[]{:S(2)}) collective-permute-start(bf16[256,768]{1,0:T(8,128)(2,1)S(1)} %constant_dynamic-update-slice_fusion.piece_ref.refs_0_), channel_id=1, source_target_pairs={{0,1},{1,0},{2,3},{3,2},{4,5},{5,4},{6,7},{7,6},{8,9},{9,8},{10,11... | collective-permute-start | bytes 1179656 | tf_op jit(solution)/shard_map/ppermute | solution.py:326
  24.7 18.1 %copy-start.1 = (bf16[256,768]{1,0:T(8,128)(2,1)}, bf16[256,768]{1,0:T(8,128)(2,1)S(1)}, u32[]{:S(2)}) copy-start(bf16[256,768]{1,0:T(8,128)(2,1)S(1)} %collective-permute-done.4.swapped_ref.refs_1_) | copy-start | bytes 1179652
  26.2 14.2 %collective-permute-start.5 = (bf16[512,256]{1,0:T(8,128)(2,1)S(1)}, bf16[512,256]{1,0:T(8,128)(2,1)S(1)}, u32[]{:S(2)}, u32[]{:S(2)}) collective-permute-start(bf16[512,256]{1,0:T(8,128)(2,1)S(1)} %get-tuple-element.64), channel_id=1, source_target_pairs={{0,4},{1,5},{2,6},{3,7},{4,0},{5,1},{6,2},{7,3},{8,12},{9,13},{10,... | collective-permute-start | bytes 786440 | tf_op jit(solution)/shard_map/ppermute | solution.py:326
  40.4 14.7 %collective-permute-start.6 = (bf16[512,256]{1,0:T(8,128)(2,1)S(1)}, bf16[512,256]{1,0:T(8,128)(2,1)S(1)}, u32[]{:S(2)}, u32[]{:S(2)}) collective-permute-start(bf16[512,256]{1,0:T(8,128)(2,1)S(1)} %shard_map.105), channel_id=1, source_target_pairs={{0,8},{1,9},{2,10},{3,11},{4,12},{5,13},{6,14},{7,15},{8,0},{9,1},... | collective-permute-start | bytes 786440 | tf_op jit(solution)/shard_map/ppermute | solution.py:326
  42.9 12.6 %collective-permute-start.7 = (bf16[512,256]{1,0:T(8,128)(2,1)}, bf16[512,256]{1,0:T(8,128)(2,1)S(1)}, u32[]{:S(2)}, u32[]{:S(2)}) collective-permute-start(bf16[512,256]{1,0:T(8,128)(2,1)} %get-tuple-element.67), channel_id=1, source_target_pairs={{0,4},{1,5},{2,6},{3,7},{4,0},{5,1},{6,2},{7,3},{8,12},{9,13},{10,... | collective-permute-start | bytes 786440 | tf_op jit(solution)/shard_map/ppermute | solution.py:326
  45.3 1.0 copy-start.3
  55.6 5.5 %collective-permute-start.8 = (bf16[512,128]{1,0:T(8,128)(2,1)S(1)}, bf16[512,128]{1,0:T(8,128)(2,1)S(1)}, u32[]{:S(2)}, u32[]{:S(2)}) collective-permute-start(bf16[512,128]{1,0:T(8,128)(2,1)S(1)} %get-tuple-element.70), channel_id=1, source_target_pairs={{0,2},{1,3},{2,0},{3,1},{4,6},{5,7},{6,4},{7,5},{8,10},{9,11},{10,... | collective-permute-start | bytes 393224 | tf_op jit(solution)/shard_map/ppermute | solution.py:326
  61.1 10.0 %collective-permute-start.11 = (bf16[256,768]{1,0:T(8,128)(2,1)S(1)}, bf16[256,768]{1,0:T(8,128)(2,1)S(1)}, u32[]{:S(2)}, u32[]{:S(2)}) collective-permute-start(bf16[256,768]{1,0:T(8,128)(2,1)S(1)} %constant_dynamic-update-slice_fusion.piece_ref.refs_0_), channel_id=1, source_target_pairs={{0,2},{1,3},{2,0},{3,1},{4,6},{5,7},{6,4},{7,5},{8,10},{9,11},{10,... | collective-permute-start | bytes 1179656 | tf_op jit(solution)/shard_map/ppermute | solution.py:326
  62.9 12.8 %collective-permute-start.10 = (bf16[128,1024]{1,0:T(8,128)(2,1)S(1)}, bf16[128,1024]{1,0:T(8,128)(2,1)S(1)}, u32[]{:S(2)}, u32[]{:S(2)}) collective-permute-start(bf16[128,1024]{1,0:T(8,128)(2,1)S(1)} %get-tuple-element.80.out_ref.refs_4_), channel_id=1, source_target_pairs={{0,4},{1,5},{2,6},{3,7},{4,0},{5,1},{6,2},{7,3},{8,12},{9,13},{10,... | collective-permute-start | bytes 786440 | tf_op jit(solution)/shard_map/ppermute | solution.py:326
  62.9 12.9 %collective-permute-start.9 = (bf16[128,1024]{1,0:T(8,128)(2,1)S(1)}, bf16[128,1024]{1,0:T(8,128)(2,1)S(1)}, u32[]{:S(2)}, u32[]{:S(2)}) collective-permute-start(bf16[128,1024]{1,0:T(8,128)(2,1)S(1)} %get-tuple-element.80.out_ref.refs_4_), channel_id=1, source_target_pairs={{0,8},{1,9},{2,10},{3,11},{4,12},{5,13},{6,14},{7,15},{8,0},{9,1},... | collective-permute-start | bytes 786440 | tf_op jit(solution)/shard_map/ppermute | solution.py:326
  71.1 13.8 %collective-permute-start.12 = (bf16[256,768]{1,0:T(8,128)(2,1)S(1)}, bf16[256,768]{1,0:T(8,128)(2,1)S(1)}, u32[]{:S(2)}, u32[]{:S(2)}) collective-permute-start(bf16[256,768]{1,0:T(8,128)(2,1)S(1)} %collective-permute-done.11.refs_2_), channel_id=1, source_target_pairs={{0,1},{1,0},{2,3},{3,2},{4,5},{5,4},{6,7},{7,6},{8,9},{9,8},{10,11... | collective-permute-start | bytes 1179656 | tf_op jit(solution)/shard_map/ppermute | solution.py:326
  72.9 12.0 %copy-start.2 = (bf16[256,768]{1,0:T(8,128)(2,1)S(1)}, bf16[256,768]{1,0:T(8,128)(2,1)}, u32[]{:S(2)}) copy-start(bf16[256,768]{1,0:T(8,128)(2,1)} %copy-done.1) | copy-start | bytes 1179652
  75.8 9.1 %collective-permute-start.13 = (bf16[128,1024]{1,0:T(8,128)(2,1)S(1)}, bf16[128,1024]{1,0:T(8,128)(2,1)S(1)}, u32[]{:S(2)}, u32[]{:S(2)}) collective-permute-start(bf16[128,1024]{1,0:T(8,128)(2,1)S(1)} %collective-permute-done.9.refs_6_), channel_id=1, source_target_pairs={{0,4},{1,5},{2,6},{3,7},{4,0},{5,1},{6,2},{7,3},{8,12},{9,13},{10,... | collective-permute-start | bytes 786440 | tf_op jit(solution)/shard_map/ppermute | solution.py:326
  76.0 27.1 %all-to-all-start.1 = ((bf16[8,384,128]{2,1,0:T(8,128)(2,1)}), bf16[8,384,128]{2,1,0:T(8,128)(2,1)S(1)}, u32[]{:S(2)}, u32[]{:S(2)}) async-start(bf16[8,384,128]{2,1,0:T(8,128)(2,1)} %shard_map.108), calls=%async_computation.1 | async-start | bytes 1572864 | tf_op jit(solution)/shard_map/all_to_all | solution.py:414
  86.3 15.3 %collective-permute-start.14 = (bf16[512,384]{1,0:T(8,128)(2,1)S(1)}, bf16[512,384]{1,0:T(8,128)(2,1)S(1)}, u32[]{:S(2)}, u32[]{:S(2)}) collective-permute-start(bf16[512,384]{1,0:T(8,128)(2,1)S(1)} %get-tuple-element.85), channel_id=1, source_target_pairs={{0,2},{1,3},{2,0},{3,1},{4,6},{5,7},{6,4},{7,5},{8,10},{9,11},{10,... | collective-permute-start | bytes 1179656 | tf_op jit(solution)/shard_map/ppermute | solution.py:326

commit v25 on v23

--- a/solution.py
+++ b/solution.py
@@ -370,26 +370,23 @@
         flops=8 * image * columns * HD,
         moved=2 * image * columns,
     )
-    send, near = lax.optimization_barrier((exchange(send, 2), near))
+    row, send = lax.optimization_barrier((row, send))
+    other_row = exchange(row, 1)
+    send, near, other_row = lax.optimization_barrier((exchange(send, 2), near, other_row))
     (far,) = call(add_kernel, [shape(far.shape, BF16)], [far, send])
     far, near = exchange(far, 4), exchange(near, 2)
-    out_late, far, near = lax.optimization_barrier((out_t, far, near))
+    out_near, out_far = exchange(out_t, 2), exchange(out_t, 4)
     kept, give = call(finish_kernel, [shape((image // 2, HD), BF16)] * 2, [mine, near, far])
     got = exchange(give, 1)
-    out_near, out_far = exchange(out_late, 2), exchange(out_late, 4)
-    row, _ = lax.optimization_barrier((row, out_t))
-    other_row = exchange(row, 1)
     other_swapped = exchange(other_row, cores=True)
     (grad_out,) = call(
         functools.partial(backward_kernel, chunk=chunk),
         [shape((n, 3 * rows, HD), BF16)],
         [queries, keys_t, vals, probs, out_t, kept, got],
         scratch=[pltpu.VMEM((image, HD), F32), pltpu.VMEM((image, HD), F32)],
-        flops=8 * total * image * HD,
-        moved=4 * total * image,
     )
     grad_in = lax.all_to_all(grad_out, "seq", split_axis=0, concat_axis=0, tiled=True)
-    out_far, out_near, other_row, _ = lax.optimization_barrier((out_far, out_near, other_row, grad_out))
+    out_far, out_near, _ = lax.optimization_barrier((out_far, out_near, grad_out))
     outs = [out_t, out_near, out_far, exchange(out_far, 2)]
     dw_own, dw_other = call(
         weight_grad_kernel,

time: 97.6 us -> 98.6 us (1.010)
  local copies, waits for them, and re-layouts: 3.72 us -> 5.36 us
  waiting for transfers between devices: 48.5 us -> 47 us
    unnamed x19, local copies, waits for them, and re-layouts: 2.65 us -> 4.29 us
    ppermute x15, waiting for transfers between devices: 48.5 us -> 47 us  [exchange(): return lax.ppermute(array, ('seq', 'fsdp'), pairs)]
    ppermute x15, starting transfers between devices: 19 us -> 20.4 us  [exchange(): return lax.ppermute(array, ('seq', 'fsdp'), pairs)]
  transfers between devices with their start and end apart: 17 -> 17, of which waited for: 14 -> 10; matrix products, arithmetic and copies ran while one was open for 1% -> 1% of each run, Pallas kernels for 17% -> 16%
where the time goes in v25:
time: 98.6 us; the launch traced here: 98.2 us
  waiting for transfers between devices  47 us (48%)
  starting transfers between devices  27.8 us (28%)
  Pallas kernels  17.2 us (17%)
  local copies, waits for them, and re-layouts  5.36 us (5%)
    ppermute x15, waiting for transfers between devices, exchange(): return lax.ppermute(array, ('seq', 'fsdp'), pairs)  47 us
    ppermute x15, starting transfers between devices, exchange(): return lax.ppermute(array, ('seq', 'fsdp'), pairs)  20.4 us
    pallas_call x9, Pallas kernels, call(): pl.pallas_call(kernel, out_shape=outs, grid_spec=pltpu.PrefetchScalarGrid...  17.2 us
    unnamed x19, local copies, waits for them, and re-layouts  4.29 us
    all_to_all x1, starting transfers between devices, local(): lax.all_to_all(tok_out, 'seq', split_axis=0, concat_axis=0, tiled=True)  3.9 us
    all_to_all x1, starting transfers between devices, local(): lax.all_to_all(grad_out, 'seq', split_axis=0, concat_axis=0, tiled=True)  3.55 us
  transfers between devices with their start and end apart: 17, of which 10 were waited for; matrix products, arithmetic and copies ran while one was open for 1% of the time, Pallas kernels for 16%

profile of v25, /device:TPU:0, one launch (start us, length us, event | category | flops | bytes accessed | tf_op | source)
XLA Modules:
  0.0 98.2 jit_solution(5287532658963617107)
XLA Ops:
  0.6 3.0 %collective-permute-start.3 = (bf16[384,1024]{1,0:T(8,128)(2,1)}, bf16[384,1024]{1,0:T(8,128)(2,1)S(1)}, u32[]{:S(2)}, u32[]{:S(2)}) collective-permute-start(bf16[384,1024]{1,0:T(8,128)(2,1)} %own_ref.1), channel_id=1, source_target_pairs={{0,2},{1,3},{2,0},{3,1},{4,6},{5,7},{6,4},{7,5},{8,10},{9,11},{10,... | collective-permute-start | bytes 2359304 | tf_op jit(solution)/shard_map/ppermute | solution.py:310
  3.7 1.1 %fusion = (bf16[64,768]{1,0:T(8,128)(2,1)S(1)}, bf16[64,768]{1,0:T(8,128)(2,1)S(1)}, bf16[64,768]{1,0:T(8,128)(2,1)S(1)}, bf16[64,768]{1,0:T(8,128)(2,1)S(1)}) fusion(bf16[128,3072]{1,0:T(8,128)(2,1)} %param.13, s32[]{:T(128)S(6)} %select_n.23, s32[]{:T(128)S(6)} %select_n.28, s32[]{:T(128)S(6)} %select_n.26, s32[]{:T(128)S(6)} %select_n.25, s32[]{:T(128)S(6)} %select_n.27), kind=kLoop, calls=%fused_computation.4 | loop fusion | bytes 786452 | tf_op jit(solution)/shard_map/dynamic_slice | solution.py:319
  4.7 1.6 %collective-permute-start = (bf16[64,768]{1,0:T(8,128)(2,1)S(1)}, bf16[64,768]{1,0:T(8,128)(2,1)S(1)}, u32[]{:S(2)}, u32[]{:S(2)}) collective-permute-start(bf16[64,768]{1,0:T(8,128)(2,1)S(1)} %get-tuple-element.75), channel_id=1, source_target_pairs={{0,4},{1,5},{2,6},{3,7},{4,0},{5,1},{6,2},{7,3},{8,12},{9,13},{10,... | collective-permute-start | bytes 294920 | tf_op jit(solution)/shard_map/ppermute | solution.py:310
  6.4 2.6 %collective-permute-start.1 = (bf16[64,768]{1,0:T(8,128)(2,1)S(1)}, bf16[64,768]{1,0:T(8,128)(2,1)S(1)}, u32[]{:S(2)}, u32[]{:S(2)}) collective-permute-start(bf16[64,768]{1,0:T(8,128)(2,1)S(1)} %get-tuple-element.77), channel_id=1, source_target_pairs={{0,8},{1,9},{2,10},{3,11},{4,12},{5,13},{6,14},{7,15},{8,0},{9,1},... | collective-permute-start | bytes 294920 | tf_op jit(solution)/shard_map/ppermute | solution.py:310
  9.0 0.2 collective-permute-start.2
  9.2 2.3 %shard_map.102 = (bf16[8,384,128]{2,1,0:T(8,128)(2,1)}, bf16[2,512,128]{2,1,0:T(8,128)(2,1)}) custom-call(s32[1]{0:T(128)} %bitcast.me_ref, bf16[128,1024]{1,0:T(8,128)(2,1)} %q_ref.1, bf16[128,1024]{1,0:T(8,128)(2,1)} %k_ref.1, bf16[128,1024]{1,0:T(8,128)(2,1)} %v_ref.1, bf16[512,1024]{1,0:T(8,128)(2,1)} %kt_ref.1, bf16[512,1024]{1,0:T(8,128)(2,1)} %vt_ref.1), custom_call_target="tpu_custom_call" | custom-call | bytes 1572864 | tf_op jit(solution)/shard_map/pallas_call | solution.py:147
  11.5 0.0 collective-permute-done
  11.5 5.0 %collective-permute-done.1 = bf16[64,768]{1,0:T(8,128)(2,1)S(1)} collective-permute-done((bf16[64,768]{1,0:T(8,128)(2,1)S(1)}, bf16[64,768]{1,0:T(8,128)(2,1)S(1)}, u32[]{:S(2)}, u32[]{:S(2)}) %collective-permute-start.1) | collective-permute-done | bytes 98336 | tf_op jit(solution)/shard_map/ppermute | solution.py:310
  16.5 0.0 collective-permute-done.2
  16.5 3.9 %all-to-all-start = ((bf16[8,384,128]{2,1,0:T(8,128)(2,1)}), bf16[8,384,128]{2,1,0:T(8,128)(2,1)S(1)}, u32[]{:S(2)}, u32[]{:S(2)}) async-start(bf16[8,384,128]{2,1,0:T(8,128)(2,1)} %get-tuple-element.40), calls=%async_computation | async-start | bytes 1572864 | tf_op jit(solution)/shard_map/all_to_all | solution.py:354
  20.4 2.4 %collective-permute-done.3.other_ref = bf16[384,1024]{1,0:T(8,128)(2,1)S(1)} collective-permute-done((bf16[384,1024]{1,0:T(8,128)(2,1)}, bf16[384,1024]{1,0:T(8,128)(2,1)S(1)}, u32[]{:S(2)}, u32[]{:S(2)}) %collective-permute-start.3) | collective-permute-done | bytes 786464 | tf_op jit(solution)/shard_map/ppermute | solution.py:310
  22.9 0.1 collective-permute-start.4
  23.0 1.7 %collective-permute-done.4.swapped_ref.refs_1_ = bf16[256,768]{1,0:T(8,128)(2,1)S(1)} collective-permute-done((bf16[256,768]{1,0:T(8,128)(2,1)S(1)}, bf16[256,768]{1,0:T(8,128)(2,1)S(1)}, u32[]{:S(2)}, u32[]{:S(2)}) %collective-permute-start.4) | collective-permute-done | bytes 393248 | tf_op jit(solution)/shard_map/ppermute | solution.py:310
  24.7 1.5 %shard_map.104 = (f32[512,256]{1,0:T(8,128)S(1)}, bf16[512,256]{1,0:T(8,128)(2,1)}, f32[512,256]{1,0:T(8,128)S(1)}, bf16[512,256]{1,0:T(8,128)(2,1)S(1)}) custom-call(bf16[256,768]{1,0:T(8,128)(2,1)S(1)} %constant_dynamic-update-slice_fusion.piece_ref.refs_0_, bf16[256,768]{1,0:T(8,128)(2,1)S(1)} %collective-permute-done.4.swapped_ref.refs_1_, ...), custom_call_target="tpu_custom_call" | custom-call | flops 805306368 | bytes 1572864 | tf_op jit(solution)/shard_map/pallas_call | solution.py:147
  26.2 2.4 %collective-permute-start.6 = (bf16[256,768]{1,0:T(8,128)(2,1)S(1)}, bf16[256,768]{1,0:T(8,128)(2,1)S(1)}, u32[]{:S(2)}, u32[]{:S(2)}) collective-permute-start(bf16[256,768]{1,0:T(8,128)(2,1)S(1)} %constant_dynamic-update-slice_fusion.piece_ref.refs_0_), channel_id=1, source_target_pairs={{0,2},{1,3},{2,0},{3,1},{4,6},{5,7},{6,4},{7,5},{8,10},{9,11},{10,... | collective-permute-start | bytes 1179656 | tf_op jit(solution)/shard_map/ppermute | solution.py:310
  28.6 2.5 %collective-permute-start.5 = (bf16[512,256]{1,0:T(8,128)(2,1)S(1)}, bf16[512,256]{1,0:T(8,128)(2,1)S(1)}, u32[]{:S(2)}, u32[]{:S(2)}) collective-permute-start(bf16[512,256]{1,0:T(8,128)(2,1)S(1)} %get-tuple-element.58), channel_id=1, source_target_pairs={{0,4},{1,5},{2,6},{3,7},{4,0},{5,1},{6,2},{7,3},{8,12},{9,13},{10,... | collective-permute-start | bytes 786440 | tf_op jit(solution)/shard_map/ppermute | solution.py:310
  31.0 10.2 %collective-permute-done.5.received_ref = bf16[512,256]{1,0:T(8,128)(2,1)S(1)} collective-permute-done((bf16[512,256]{1,0:T(8,128)(2,1)S(1)}, bf16[512,256]{1,0:T(8,128)(2,1)S(1)}, u32[]{:S(2)}, u32[]{:S(2)}) %collective-permute-start.5) | collective-permute-done | bytes 262176 | tf_op jit(solution)/shard_map/ppermute | solution.py:310
  41.2 0.0 collective-permute-done.6.refs_2_
  41.3 5.0 %collective-permute-start.8 = (bf16[512,256]{1,0:T(8,128)(2,1)S(1)}, bf16[512,256]{1,0:T(8,128)(2,1)S(1)}, u32[]{:S(2)}, u32[]{:S(2)}) collective-permute-start(bf16[512,256]{1,0:T(8,128)(2,1)S(1)} %shard_map.105), channel_id=1, source_target_pairs={{0,8},{1,9},{2,10},{3,11},{4,12},{5,13},{6,14},{7,15},{8,0},{9,1},... | collective-permute-start | bytes 786440 | tf_op jit(solution)/shard_map/ppermute | solution.py:310
  46.3 0.8 collective-permute-start.7
  47.1 0.0 all-to-all-done.tok_ref
  47.1 0.9 copy-done.3
  48.0 4.9 %shard_map.103 = (bf16[1536,1024]{1,0:T(8,128)(2,1)S(1)}, bf16[128,1024]{1,0:T(8,128)(2,1)S(1)}, bf16[1024,128]{1,0:T(8,128)(2,1)S(1)}, bf16[128,1536]{1,0:T(8,128)(2,1)S(1)}, bf16[1536,128]{1,0:T(8,128)(2,1)S(1)}) custom-call(bf16[8,384,128]{2,1,0:T(8,128)(2,1)S(1)} %all-to-all-done.tok_ref, bf16[2,512,128]{2,1,0:T(8,128)(2,1)S(1)} %copy-done.3), custom_call_target="tpu_custom_call" | custom-call | flops 805306368 | bytes 6291456 | tf_op jit(solution)/shard_map/pallas_call | solution.py:147
  52.9 0.1 collective-permute-start.11
  53.1 1.3 %collective-permute-start.12 = (bf16[128,1024]{1,0:T(8,128)(2,1)S(1)}, bf16[128,1024]{1,0:T(8,128)(2,1)S(1)}, u32[]{:S(2)}, u32[]{:S(2)}) collective-permute-start(bf16[128,1024]{1,0:T(8,128)(2,1)S(1)} %get-tuple-element.46.out_ref.refs_4_), channel_id=1, source_target_pairs={{0,4},{1,5},{2,6},{3,7},{4,0},{5,1},{6,2},{7,3},{8,12},{9,13},{10,... | collective-permute-start | bytes 786440 | tf_op jit(solution)/shard_map/ppermute | solution.py:310
  54.3 5.0 %collective-permute-done.8.far_ref = bf16[512,256]{1,0:T(8,128)(2,1)S(1)} collective-permute-done((bf16[512,256]{1,0:T(8,128)(2,1)S(1)}, bf16[512,256]{1,0:T(8,128)(2,1)S(1)}, u32[]{:S(2)}, u32[]{:S(2)}) %collective-permute-start.8) | collective-permute-done | bytes 262176 | tf_op jit(solution)/shard_map/ppermute | solution.py:310
  59.4 1.8 %collective-permute-done.7.near_ref = bf16[512,256]{1,0:T(8,128)(2,1)S(1)} collective-permute-done((bf16[512,256]{1,0:T(8,128)(2,1)}, bf16[512,256]{1,0:T(8,128)(2,1)S(1)}, u32[]{:S(2)}, u32[]{:S(2)}) %collective-permute-start.7) | collective-permute-done | bytes 262176 | tf_op jit(solution)/shard_map/ppermute | solution.py:310
  61.1 0.1 shard_map.106
  61.2 0.1 collective-permute-start.9
  61.3 0.1 collective-permute-start.10
  61.4 4.9 %collective-permute-done.9.refs_1_ = bf16[512,128]{1,0:T(8,128)(2,1)S(1)} collective-permute-done((bf16[512,128]{1,0:T(8,128)(2,1)S(1)}, bf16[512,128]{1,0:T(8,128)(2,1)S(1)}, u32[]{:S(2)}, u32[]{:S(2)}) %collective-permute-start.9) | collective-permute-done | bytes 131104 | tf_op jit(solution)/shard_map/ppermute | solution.py:310
  66.3 4.5 %shard_map.107 = bf16[8,384,128]{2,1,0:T(8,128)(2,1)} custom-call(bf16[1024,128]{1,0:T(8,128)(2,1)S(1)} %get-tuple-element.42.queries_ref, bf16[128,1536]{1,0:T(8,128)(2,1)S(1)} %get-tuple-element.43.keys_t_ref, bf16[1536,128]{1,0:T(8,128)(2,1)S(1)} %get-tuple-element.44.vals_ref, bf16[1536,1024]{1,0:T(8,128)(2,1)S(1)} %get-tuple-element.45.probs_ref, ...), custom_call_target="tpu_custom_call" | custom-call | tf_op jit(solution)/shard_map/pallas_call | solution.py:147
  70.7 0.0 collective-permute-done.11.refs_6_
  70.7 0.1 collective-permute-done.12.refs_5_
  70.9 0.7 copy-done.4
  71.6 0.5 collective-permute-start.13
  72.1 3.5 %all-to-all-start.1 = ((bf16[8,384,128]{2,1,0:T(8,128)(2,1)}), bf16[8,384,128]{2,1,0:T(8,128)(2,1)S(1)}, u32[]{:S(2)}, u32[]{:S(2)}) async-start(bf16[8,384,128]{2,1,0:T(8,128)(2,1)} %shard_map.107), calls=%async_computation.1 | async-start | bytes 1572864 | tf_op jit(solution)/shard_map/all_to_all | solution.py:388
  75.7 0.0 collective-permute-done.10.refs_3_
  75.7 4.6 %collective-permute-done.13.refs_7_ = bf16[128,1024]{1,0:T(8,128)(2,1)S(1)} collective-permute-done((bf16[128,1024]{1,0:T(8,128)(2,1)S(1)}, bf16[128,1024]{1,0:T(8,128)(2,1)S(1)}, u32[]{:S(2)}, u32[]{:S(2)}) %collective-permute-start.13) | collective-permute-done | bytes 262176 | tf_op jit(solution)/shard_map/ppermute | solution.py:310
  80.2 0.7 copy-done.6
  80.9 0.9 copy-done.5
  81.9 0.9 copy-done.7
  82.8 1.4 %shard_map.109 = (bf16[512,384]{1,0:T(8,128)(2,1)S(1)}, bf16[512,384]{1,0:T(8,128)(2,1)S(1)}) custom-call(bf16[256,768]{1,0:T(8,128)(2,1)S(1)} %constant_dynamic-update-slice_fusion.piece_ref.refs_0_, bf16[256,768]{1,0:T(8,128)(2,1)S(1)} %copy-done.2, bf16[256,768]{1,0:T(8,128)(2,1)S(1)} %collective-permute-done.6.refs_2_, ...), custom_call_target="tpu_custom_call" | custom-call | flops 9663676416 | bytes 1572864 | tf_op jit(solution)/shard_map/pallas_call | solution.py:147
  84.2 0.1 collective-permute-start.14
  84.3 11.3 %collective-permute-done.14.other_ref = bf16[512,384]{1,0:T(8,128)(2,1)S(1)} collective-permute-done((bf16[512,384]{1,0:T(8,128)(2,1)S(1)}, bf16[512,384]{1,0:T(8,128)(2,1)S(1)}, u32[]{:S(2)}, u32[]{:S(2)}) %collective-permute-start.14) | collective-permute-done | bytes 393248 | tf_op jit(solution)/shard_map/ppermute | solution.py:310
  95.6 1.5 %shard_map.110 = f32[384,1024]{1,0:T(8,128)} custom-call(bf16[512,384]{1,0:T(8,128)(2,1)S(1)} %get-tuple-element.72.own_ref, bf16[512,384]{1,0:T(8,128)(2,1)S(1)} %collective-permute-done.14.other_ref), custom_call_target="tpu_custom_call" | custom-call | bytes 2359296 | tf_op jit(solution)/shard_map/pallas_call | solution.py:147
  97.1 0.0 all-to-all-done.1.tok_ref
  97.1 1.1 %shard_map.108 = (bf16[128,1024]{1,0:T(8,128)(2,1)}, bf16[128,1024]{1,0:T(8,128)(2,1)}, bf16[128,1024]{1,0:T(8,128)(2,1)}) custom-call(bf16[8,384,128]{2,1,0:T(8,128)(2,1)S(1)} %all-to-all-done.1.tok_ref), custom_call_target="tpu_custom_call" | custom-call | bytes 1572864 | tf_op jit(solution)/shard_map/pallas_call | solution.py:147
  (16 shorter events, 0.1 us)
Async XLA Ops:
  0.6 24.1 %copy-start = (bf16[384,1024]{1,0:T(8,128)(2,1)S(1)}, bf16[384,1024]{1,0:T(8,128)(2,1)}, u32[]{:S(2)}) copy-start(bf16[384,1024]{1,0:T(8,128)(2,1)} %own_ref.1) | copy-start | bytes 2359300
  0.6 22.2 %collective-permute-start.3 = (bf16[384,1024]{1,0:T(8,128)(2,1)}, bf16[384,1024]{1,0:T(8,128)(2,1)S(1)}, u32[]{:S(2)}, u32[]{:S(2)}) collective-permute-start(bf16[384,1024]{1,0:T(8,128)(2,1)} %own_ref.1), channel_id=1, source_target_pairs={{0,2},{1,3},{2,0},{3,1},{4,6},{5,7},{6,4},{7,5},{8,10},{9,11},{10,... | collective-permute-start | bytes 2359304 | tf_op jit(solution)/shard_map/ppermute | solution.py:310
  4.7 6.8 %collective-permute-start = (bf16[64,768]{1,0:T(8,128)(2,1)S(1)}, bf16[64,768]{1,0:T(8,128)(2,1)S(1)}, u32[]{:S(2)}, u32[]{:S(2)}) collective-permute-start(bf16[64,768]{1,0:T(8,128)(2,1)S(1)} %get-tuple-element.75), channel_id=1, source_target_pairs={{0,4},{1,5},{2,6},{3,7},{4,0},{5,1},{6,2},{7,3},{8,12},{9,13},{10,... | collective-permute-start | bytes 294920 | tf_op jit(solution)/shard_map/ppermute | solution.py:310
  6.4 10.1 %collective-permute-start.1 = (bf16[64,768]{1,0:T(8,128)(2,1)S(1)}, bf16[64,768]{1,0:T(8,128)(2,1)S(1)}, u32[]{:S(2)}, u32[]{:S(2)}) collective-permute-start(bf16[64,768]{1,0:T(8,128)(2,1)S(1)} %get-tuple-element.77), channel_id=1, source_target_pairs={{0,8},{1,9},{2,10},{3,11},{4,12},{5,13},{6,14},{7,15},{8,0},{9,1},... | collective-permute-start | bytes 294920 | tf_op jit(solution)/shard_map/ppermute | solution.py:310
  9.0 7.6 %collective-permute-start.2 = (bf16[64,768]{1,0:T(8,128)(2,1)S(1)}, bf16[64,768]{1,0:T(8,128)(2,1)S(1)}, u32[]{:S(2)}, u32[]{:S(2)}) collective-permute-start(bf16[64,768]{1,0:T(8,128)(2,1)S(1)} %get-tuple-element.74), channel_id=1, source_target_pairs={{0,12},{1,13},{2,14},{3,15},{4,8},{5,9},{6,10},{7,11},{8,4},{9,5},... | collective-permute-start | bytes 294920 | tf_op jit(solution)/shard_map/ppermute | solution.py:310
  16.5 30.5 %all-to-all-start = ((bf16[8,384,128]{2,1,0:T(8,128)(2,1)}), bf16[8,384,128]{2,1,0:T(8,128)(2,1)S(1)}, u32[]{:S(2)}, u32[]{:S(2)}) async-start(bf16[8,384,128]{2,1,0:T(8,128)(2,1)} %get-tuple-element.40), calls=%async_computation | async-start | bytes 1572864 | tf_op jit(solution)/shard_map/all_to_all | solution.py:354
  22.9 1.8 %collective-permute-start.4 = (bf16[256,768]{1,0:T(8,128)(2,1)S(1)}, bf16[256,768]{1,0:T(8,128)(2,1)S(1)}, u32[]{:S(2)}, u32[]{:S(2)}) collective-permute-start(bf16[256,768]{1,0:T(8,128)(2,1)S(1)} %constant_dynamic-update-slice_fusion.piece_ref.refs_0_), channel_id=1, source_target_pairs={{0,1},{1,0},{2,3},{3,2},{4,5},{5,4},{6,7},{7,6},{8,9},{9,8},{10,11... | collective-permute-start | bytes 1179656 | tf_op jit(solution)/shard_map/ppermute | solution.py:310
  24.7 1.5 %copy-start.1 = (bf16[256,768]{1,0:T(8,128)(2,1)}, bf16[256,768]{1,0:T(8,128)(2,1)S(1)}, u32[]{:S(2)}) copy-start(bf16[256,768]{1,0:T(8,128)(2,1)S(1)} %collective-permute-done.4.swapped_ref.refs_1_) | copy-start | bytes 1179652
  26.2 15.1 %collective-permute-start.6 = (bf16[256,768]{1,0:T(8,128)(2,1)S(1)}, bf16[256,768]{1,0:T(8,128)(2,1)S(1)}, u32[]{:S(2)}, u32[]{:S(2)}) collective-permute-start(bf16[256,768]{1,0:T(8,128)(2,1)S(1)} %constant_dynamic-update-slice_fusion.piece_ref.refs_0_), channel_id=1, source_target_pairs={{0,2},{1,3},{2,0},{3,1},{4,6},{5,7},{6,4},{7,5},{8,10},{9,11},{10,... | collective-permute-start | bytes 1179656 | tf_op jit(solution)/shard_map/ppermute | solution.py:310
  28.6 12.7 %collective-permute-start.5 = (bf16[512,256]{1,0:T(8,128)(2,1)S(1)}, bf16[512,256]{1,0:T(8,128)(2,1)S(1)}, u32[]{:S(2)}, u32[]{:S(2)}) collective-permute-start(bf16[512,256]{1,0:T(8,128)(2,1)S(1)} %get-tuple-element.58), channel_id=1, source_target_pairs={{0,4},{1,5},{2,6},{3,7},{4,0},{5,1},{6,2},{7,3},{8,12},{9,13},{10,... | collective-permute-start | bytes 786440 | tf_op jit(solution)/shard_map/ppermute | solution.py:310
  41.3 18.1 %collective-permute-start.8 = (bf16[512,256]{1,0:T(8,128)(2,1)S(1)}, bf16[512,256]{1,0:T(8,128)(2,1)S(1)}, u32[]{:S(2)}, u32[]{:S(2)}) collective-permute-start(bf16[512,256]{1,0:T(8,128)(2,1)S(1)} %shard_map.105), channel_id=1, source_target_pairs={{0,8},{1,9},{2,10},{3,11},{4,12},{5,13},{6,14},{7,15},{8,0},{9,1},... | collective-permute-start | bytes 786440 | tf_op jit(solution)/shard_map/ppermute | solution.py:310
  46.3 14.8 %collective-permute-start.7 = (bf16[512,256]{1,0:T(8,128)(2,1)}, bf16[512,256]{1,0:T(8,128)(2,1)S(1)}, u32[]{:S(2)}, u32[]{:S(2)}) collective-permute-start(bf16[512,256]{1,0:T(8,128)(2,1)} %get-tuple-element.61), channel_id=1, source_target_pairs={{0,4},{1,5},{2,6},{3,7},{4,0},{5,1},{6,2},{7,3},{8,12},{9,13},{10,... | collective-permute-start | bytes 786440 | tf_op jit(solution)/shard_map/ppermute | solution.py:310
  47.1 1.0 copy-start.3
  52.9 17.8 %collective-permute-start.11 = (bf16[128,1024]{1,0:T(8,128)(2,1)S(1)}, bf16[128,1024]{1,0:T(8,128)(2,1)S(1)}, u32[]{:S(2)}, u32[]{:S(2)}) collective-permute-start(bf16[128,1024]{1,0:T(8,128)(2,1)S(1)} %get-tuple-element.46.out_ref.refs_4_), channel_id=1, source_target_pairs={{0,8},{1,9},{2,10},{3,11},{4,12},{5,13},{6,14},{7,15},{8,0},{9,1},... | collective-permute-start | bytes 786440 | tf_op jit(solution)/shard_map/ppermute | solution.py:310
  53.1 17.8 %collective-permute-start.12 = (bf16[128,1024]{1,0:T(8,128)(2,1)S(1)}, bf16[128,1024]{1,0:T(8,128)(2,1)S(1)}, u32[]{:S(2)}, u32[]{:S(2)}) collective-permute-start(bf16[128,1024]{1,0:T(8,128)(2,1)S(1)} %get-tuple-element.46.out_ref.refs_4_), channel_id=1, source_target_pairs={{0,4},{1,5},{2,6},{3,7},{4,0},{5,1},{6,2},{7,3},{8,12},{9,13},{10,... | collective-permute-start | bytes 786440 | tf_op jit(solution)/shard_map/ppermute | solution.py:310
  61.2 5.0 %collective-permute-start.9 = (bf16[512,128]{1,0:T(8,128)(2,1)S(1)}, bf16[512,128]{1,0:T(8,128)(2,1)S(1)}, u32[]{:S(2)}, u32[]{:S(2)}) collective-permute-start(bf16[512,128]{1,0:T(8,128)(2,1)S(1)} %get-tuple-element.65), channel_id=1, source_target_pairs={{0,2},{1,3},{2,0},{3,1},{4,6},{5,7},{6,4},{7,5},{8,10},{9,11},{10,... | collective-permute-start | bytes 393224 | tf_op jit(solution)/shard_map/ppermute | solution.py:310
  61.3 14.3 %collective-permute-start.10 = (bf16[256,768]{1,0:T(8,128)(2,1)S(1)}, bf16[256,768]{1,0:T(8,128)(2,1)S(1)}, u32[]{:S(2)}, u32[]{:S(2)}) collective-permute-start(bf16[256,768]{1,0:T(8,128)(2,1)S(1)} %collective-permute-done.6.refs_2_), channel_id=1, source_target_pairs={{0,1},{1,0},{2,3},{3,2},{4,5},{5,4},{6,7},{7,6},{8,9},{9,8},{10,11... | collective-permute-start | bytes 1179656 | tf_op jit(solution)/shard_map/ppermute | solution.py:310
  66.3 14.7 %copy-start.2 = (bf16[256,768]{1,0:T(8,128)(2,1)S(1)}, bf16[256,768]{1,0:T(8,128)(2,1)}, u32[]{:S(2)}) copy-start(bf16[256,768]{1,0:T(8,128)(2,1)} %copy-done.1) | copy-start | bytes 1179652
  70.9 0.7 copy-start.4
  71.6 8.7 %collective-permute-start.13 = (bf16[128,1024]{1,0:T(8,128)(2,1)S(1)}, bf16[128,1024]{1,0:T(8,128)(2,1)S(1)}, u32[]{:S(2)}, u32[]{:S(2)}) collective-permute-start(bf16[128,1024]{1,0:T(8,128)(2,1)S(1)} %collective-permute-done.11.refs_6_), channel_id=1, source_target_pairs={{0,4},{1,5},{2,6},{3,7},{4,0},{5,1},{6,2},{7,3},{8,12},{9,13},{10,... | collective-permute-start | bytes 786440 | tf_op jit(solution)/shard_map/ppermute | solution.py:310
  72.1 25.0 %all-to-all-start.1 = ((bf16[8,384,128]{2,1,0:T(8,128)(2,1)}), bf16[8,384,128]{2,1,0:T(8,128)(2,1)S(1)}, u32[]{:S(2)}, u32[]{:S(2)}) async-start(bf16[8,384,128]{2,1,0:T(8,128)(2,1)} %shard_map.107), calls=%async_computation.1 | async-start | bytes 1572864 | tf_op jit(solution)/shard_map/all_to_all | solution.py:388
  80.2 0.7 copy-start.6
  80.9 1.0 copy-start.5
  81.9 0.9 copy-start.7
  84.2 11.4 %collective-permute-start.14 = (bf16[512,384]{1,0:T(8,128)(2,1)S(1)}, bf16[512,384]{1,0:T(8,128)(2,1)S(1)}, u32[]{:S(2)}, u32[]{:S(2)}) collective-permute-start(bf16[512,384]{1,0:T(8,128)(2,1)S(1)} %get-tuple-element.73), channel_id=1, source_target_pairs={{0,2},{1,3},{2,0},{3,1},{4,6},{5,7},{6,4},{7,5},{8,10},{9,11},{10,... | collective-permute-start | bytes 1179656 | tf_op jit(solution)/shard_map/ppermute | solution.py:310

commit v26 on v25

--- a/solution.py
+++ b/solution.py
@@ -370,14 +370,14 @@
         flops=8 * image * columns * HD,
         moved=2 * image * columns,
     )
-    row, send = lax.optimization_barrier((row, send))
-    other_row = exchange(row, 1)
-    send, near, other_row = lax.optimization_barrier((exchange(send, 2), near, other_row))
+    send, near = lax.optimization_barrier((exchange(send, 2), near))
     (far,) = call(add_kernel, [shape(far.shape, BF16)], [far, send])
     far, near = exchange(far, 4), exchange(near, 2)
     out_near, out_far = exchange(out_t, 2), exchange(out_t, 4)
     kept, give = call(finish_kernel, [shape((image // 2, HD), BF16)] * 2, [mine, near, far])
     got = exchange(give, 1)
+    row, _ = lax.optimization_barrier((row, out_t))
+    other_row = exchange(row, 1)
     other_swapped = exchange(other_row, cores=True)
     (grad_out,) = call(
         functools.partial(backward_kernel, chunk=chunk),

time: 98.6 us -> 102 us (1.034)
  waiting for transfers between devices: 47 us -> 50.3 us
  starting transfers between devices: 27.8 us -> 25.3 us
  local copies, waits for them, and re-layouts: 5.36 us -> 7.39 us
    all_to_all x1, waiting for transfers between devices: 0.01 us -> 11 us  [local(): lax.all_to_all(tok_out, 'seq', split_axis=0, concat_axis=0, tiled=True)]
    ppermute x15, waiting for transfers between devices: 47 us -> 39.4 us  [exchange(): return lax.ppermute(array, ('seq', 'fsdp'), pairs)]
    ppermute x15, starting transfers between devices: 20.4 us -> 17.6 us  [exchange(): return lax.ppermute(array, ('seq', 'fsdp'), pairs)]
    unnamed x19 -> x25, local copies, waits for them, and re-layouts: 4.29 us -> 6.31 us
where the time goes in v26:
time: 102 us; the launch traced here: 101 us
  waiting for transfers between devices  50.3 us (49%)
  starting transfers between devices  25.3 us (25%)
  Pallas kernels  17.6 us (17%)
  local copies, waits for them, and re-layouts  7.39 us (7%)
    ppermute x15, waiting for transfers between devices, exchange(): return lax.ppermute(array, ('seq', 'fsdp'), pairs)  39.4 us
    pallas_call x9, Pallas kernels, call(): pl.pallas_call(kernel, out_shape=outs, grid_spec=pltpu.PrefetchScalarGrid...  17.6 us
    ppermute x15, starting transfers between devices, exchange(): return lax.ppermute(array, ('seq', 'fsdp'), pairs)  17.6 us
    all_to_all x1, waiting for transfers between devices, local(): lax.all_to_all(tok_out, 'seq', split_axis=0, concat_axis=0, tiled=True)  11 us
    unnamed x25, local copies, waits for them, and re-layouts  6.31 us
    all_to_all x1, starting transfers between devices, local(): lax.all_to_all(tok_out, 'seq', split_axis=0, concat_axis=0, tiled=True)  4.11 us
    all_to_all x1, starting transfers between devices, local(): lax.all_to_all(grad_out, 'seq', split_axis=0, concat_axis=0, tiled=True)  3.56 us
  transfers between devices with their start and end apart: 17, of which 10 were waited for; matrix products, arithmetic and copies ran while one was open for 1% of the time, Pallas kernels for 16%

profile of v26, /device:TPU:0, one launch (start us, length us, event | category | flops | bytes accessed | tf_op | source)
XLA Modules:
  0.0 101.4 jit_solution(1348968280811560408)
XLA Ops:
  0.6 3.0 %collective-permute-start.3 = (bf16[384,1024]{1,0:T(8,128)(2,1)}, bf16[384,1024]{1,0:T(8,128)(2,1)S(1)}, u32[]{:S(2)}, u32[]{:S(2)}) collective-permute-start(bf16[384,1024]{1,0:T(8,128)(2,1)} %own_ref.1), channel_id=1, source_target_pairs={{0,2},{1,3},{2,0},{3,1},{4,6},{5,7},{6,4},{7,5},{8,10},{9,11},{10,... | collective-permute-start | bytes 2359304 | tf_op jit(solution)/shard_map/ppermute | solution.py:310
  3.7 1.1 %fusion = (bf16[64,768]{1,0:T(8,128)(2,1)S(1)}, bf16[64,768]{1,0:T(8,128)(2,1)S(1)}, bf16[64,768]{1,0:T(8,128)(2,1)S(1)}, bf16[64,768]{1,0:T(8,128)(2,1)S(1)}) fusion(bf16[128,3072]{1,0:T(8,128)(2,1)} %param.13, s32[]{:T(128)S(6)} %select_n.23, s32[]{:T(128)S(6)} %select_n.28, s32[]{:T(128)S(6)} %select_n.26, s32[]{:T(128)S(6)} %select_n.25, s32[]{:T(128)S(6)} %select_n.27), kind=kLoop, calls=%fused_computation.4 | loop fusion | bytes 786452 | tf_op jit(solution)/shard_map/dynamic_slice | solution.py:319
  4.7 3.7 %collective-permute-start.2 = (bf16[64,768]{1,0:T(8,128)(2,1)S(1)}, bf16[64,768]{1,0:T(8,128)(2,1)S(1)}, u32[]{:S(2)}, u32[]{:S(2)}) collective-permute-start(bf16[64,768]{1,0:T(8,128)(2,1)S(1)} %get-tuple-element.70), channel_id=1, source_target_pairs={{0,12},{1,13},{2,14},{3,15},{4,8},{5,9},{6,10},{7,11},{8,4},{9,5},... | collective-permute-start | bytes 294920 | tf_op jit(solution)/shard_map/ppermute | solution.py:310
  8.4 0.0 collective-permute-start
  8.4 0.8 collective-permute-start.1
  9.2 2.3 %shard_map.102 = (bf16[8,384,128]{2,1,0:T(8,128)(2,1)}, bf16[2,512,128]{2,1,0:T(8,128)(2,1)}) custom-call(s32[1]{0:T(128)} %bitcast.me_ref, bf16[128,1024]{1,0:T(8,128)(2,1)} %q_ref.1, bf16[128,1024]{1,0:T(8,128)(2,1)} %k_ref.1, bf16[128,1024]{1,0:T(8,128)(2,1)} %v_ref.1, bf16[512,1024]{1,0:T(8,128)(2,1)} %kt_ref.1, bf16[512,1024]{1,0:T(8,128)(2,1)} %vt_ref.1), custom_call_target="tpu_custom_call" | custom-call | bytes 1572864 | tf_op jit(solution)/shard_map/pallas_call | solution.py:147
  11.5 0.6 collective-permute-done.2
  12.1 2.4 %collective-permute-done = bf16[64,768]{1,0:T(8,128)(2,1)S(1)} collective-permute-done((bf16[64,768]{1,0:T(8,128)(2,1)S(1)}, bf16[64,768]{1,0:T(8,128)(2,1)S(1)}, u32[]{:S(2)}, u32[]{:S(2)}) %collective-permute-start) | collective-permute-done | bytes 98336 | tf_op jit(solution)/shard_map/ppermute | solution.py:310
  14.5 1.9 %collective-permute-done.1 = bf16[64,768]{1,0:T(8,128)(2,1)S(1)} collective-permute-done((bf16[64,768]{1,0:T(8,128)(2,1)S(1)}, bf16[64,768]{1,0:T(8,128)(2,1)S(1)}, u32[]{:S(2)}, u32[]{:S(2)}) %collective-permute-start.1) | collective-permute-done | bytes 98336 | tf_op jit(solution)/shard_map/ppermute | solution.py:310
  16.4 4.1 %all-to-all-start = ((bf16[8,384,128]{2,1,0:T(8,128)(2,1)}), bf16[8,384,128]{2,1,0:T(8,128)(2,1)S(1)}, u32[]{:S(2)}, u32[]{:S(2)}) async-start(bf16[8,384,128]{2,1,0:T(8,128)(2,1)} %get-tuple-element.38), calls=%async_computation | async-start | bytes 1572864 | tf_op jit(solution)/shard_map/all_to_all | solution.py:354
  20.5 0.9 collective-permute-done.3.other_ref
  21.4 0.9 copy-done.1
  22.4 0.1 collective-permute-start.4
  22.4 1.7 %collective-permute-done.4.swapped_ref.refs_1_ = bf16[256,768]{1,0:T(8,128)(2,1)S(1)} collective-permute-done((bf16[256,768]{1,0:T(8,128)(2,1)S(1)}, bf16[256,768]{1,0:T(8,128)(2,1)S(1)}, u32[]{:S(2)}, u32[]{:S(2)}) %collective-permute-start.4) | collective-permute-done | bytes 393248 | tf_op jit(solution)/shard_map/ppermute | solution.py:310
  24.2 1.1 %copy-done.2 = bf16[384,1024]{1,0:T(8,128)(2,1)S(1)} copy-done((bf16[384,1024]{1,0:T(8,128)(2,1)S(1)}, bf16[384,1024]{1,0:T(8,128)(2,1)}, u32[]{:S(2)}) %copy-start.2) | copy-done | bytes 786456
  25.3 1.9 %shard_map.104 = (f32[512,256]{1,0:T(8,128)S(1)}, bf16[512,256]{1,0:T(8,128)(2,1)S(1)}, f32[512,256]{1,0:T(8,128)S(1)}, bf16[512,256]{1,0:T(8,128)(2,1)}) custom-call(bf16[256,768]{1,0:T(8,128)(2,1)S(1)} %constant_dynamic-update-slice_fusion.piece_ref.refs_0_, bf16[256,768]{1,0:T(8,128)(2,1)S(1)} %collective-permute-done.4.swapped_ref.refs_1_, ...), custom_call_target="tpu_custom_call" | custom-call | flops 805306368 | bytes 1572864 | tf_op jit(solution)/shard_map/pallas_call | solution.py:147
  27.2 0.7 copy-done.8
  27.9 1.8 %collective-permute-start.5 = (bf16[512,256]{1,0:T(8,128)(2,1)}, bf16[512,256]{1,0:T(8,128)(2,1)S(1)}, u32[]{:S(2)}, u32[]{:S(2)}) collective-permute-start(bf16[512,256]{1,0:T(8,128)(2,1)} %get-tuple-element.55), channel_id=1, source_target_pairs={{0,4},{1,5},{2,6},{3,7},{4,0},{5,1},{6,2},{7,3},{8,12},{9,13},{10,... | collective-permute-start | bytes 786440 | tf_op jit(solution)/shard_map/ppermute | solution.py:310
  29.7 11.0 %all-to-all-done.tok_ref = bf16[8,384,128]{2,1,0:T(8,128)(2,1)S(1)} async-done(((bf16[8,384,128]{2,1,0:T(8,128)(2,1)}), bf16[8,384,128]{2,1,0:T(8,128)(2,1)S(1)}, u32[]{:S(2)}, u32[]{:S(2)}) %all-to-all-start) | async-done | bytes 786464 | tf_op jit(solution)/shard_map/all_to_all | solution.py:354
  40.6 0.9 copy-done.7
  41.6 4.9 %shard_map.103 = (bf16[1536,1024]{1,0:T(8,128)(2,1)S(1)}, bf16[128,1024]{1,0:T(8,128)(2,1)S(1)}, bf16[1024,128]{1,0:T(8,128)(2,1)S(1)}, bf16[128,1536]{1,0:T(8,128)(2,1)S(1)}, bf16[1536,128]{1,0:T(8,128)(2,1)S(1)}) custom-call(bf16[8,384,128]{2,1,0:T(8,128)(2,1)S(1)} %all-to-all-done.tok_ref, bf16[2,512,128]{2,1,0:T(8,128)(2,1)S(1)} %copy-done.7), custom_call_target="tpu_custom_call" | custom-call | flops 805306368 | bytes 6291456 | tf_op jit(solution)/shard_map/pallas_call | solution.py:147
  46.5 1.4 %collective-permute-start.9 = (bf16[256,768]{1,0:T(8,128)(2,1)S(1)}, bf16[256,768]{1,0:T(8,128)(2,1)S(1)}, u32[]{:S(2)}, u32[]{:S(2)}) collective-permute-start(bf16[256,768]{1,0:T(8,128)(2,1)S(1)} %constant_dynamic-update-slice_fusion.piece_ref.refs_0_), channel_id=1, source_target_pairs={{0,2},{1,3},{2,0},{3,1},{4,6},{5,7},{6,4},{7,5},{8,10},{9,11},{10,... | collective-permute-start | bytes 1179656 | tf_op jit(solution)/shard_map/ppermute | solution.py:310
  47.9 0.0 collective-permute-done.5.received_ref
  47.9 0.0 collective-permute-start.6
  48.0 2.1 %collective-permute-start.7 = (bf16[512,256]{1,0:T(8,128)(2,1)S(1)}, bf16[512,256]{1,0:T(8,128)(2,1)S(1)}, u32[]{:S(2)}, u32[]{:S(2)}) collective-permute-start(bf16[512,256]{1,0:T(8,128)(2,1)S(1)} %shard_map.105), channel_id=1, source_target_pairs={{0,8},{1,9},{2,10},{3,11},{4,12},{5,13},{6,14},{7,15},{8,0},{9,1},... | collective-permute-start | bytes 786440 | tf_op jit(solution)/shard_map/ppermute | solution.py:310
  50.1 0.1 collective-permute-start.12
  50.1 2.8 %collective-permute-start.11 = (bf16[128,1024]{1,0:T(8,128)(2,1)S(1)}, bf16[128,1024]{1,0:T(8,128)(2,1)S(1)}, u32[]{:S(2)}, u32[]{:S(2)}) collective-permute-start(bf16[128,1024]{1,0:T(8,128)(2,1)S(1)} %get-tuple-element.44.out_ref.refs_4_), channel_id=1, source_target_pairs={{0,8},{1,9},{2,10},{3,11},{4,12},{5,13},{6,14},{7,15},{8,0},{9,1},... | collective-permute-start | bytes 786440 | tf_op jit(solution)/shard_map/ppermute | solution.py:310
  53.0 13.2 %collective-permute-done.6.near_ref = bf16[512,256]{1,0:T(8,128)(2,1)S(1)} collective-permute-done((bf16[512,256]{1,0:T(8,128)(2,1)}, bf16[512,256]{1,0:T(8,128)(2,1)S(1)}, u32[]{:S(2)}, u32[]{:S(2)}) %collective-permute-start.6) | collective-permute-done | bytes 262176 | tf_op jit(solution)/shard_map/ppermute | solution.py:310
  66.1 0.0 collective-permute-done.7.far_ref
  66.1 0.1 shard_map.106
  66.2 0.5 collective-permute-start.8
  66.8 0.0 collective-permute-done.9.refs_2_
  66.8 0.0 collective-permute-start.10
  66.8 4.5 %collective-permute-done.8.refs_1_ = bf16[512,128]{1,0:T(8,128)(2,1)S(1)} collective-permute-done((bf16[512,128]{1,0:T(8,128)(2,1)S(1)}, bf16[512,128]{1,0:T(8,128)(2,1)S(1)}, u32[]{:S(2)}, u32[]{:S(2)}) %collective-permute-start.8) | collective-permute-done | bytes 131104 | tf_op jit(solution)/shard_map/ppermute | solution.py:310
  71.3 4.4 %shard_map.107 = bf16[8,384,128]{2,1,0:T(8,128)(2,1)} custom-call(bf16[1024,128]{1,0:T(8,128)(2,1)S(1)} %get-tuple-element.40.queries_ref, bf16[128,1536]{1,0:T(8,128)(2,1)S(1)} %get-tuple-element.41.keys_t_ref, bf16[1536,128]{1,0:T(8,128)(2,1)S(1)} %get-tuple-element.42.vals_ref, bf16[1536,1024]{1,0:T(8,128)(2,1)S(1)} %get-tuple-element.43.probs_ref, ...), custom_call_target="tpu_custom_call" | custom-call | tf_op jit(solution)/shard_map/pallas_call | solution.py:147
  75.7 0.0 collective-permute-done.12.refs_5_
  75.7 0.0 collective-permute-done.11.refs_6_
  75.7 0.1 collective-permute-start.13
  75.8 3.6 %all-to-all-start.1 = ((bf16[8,384,128]{2,1,0:T(8,128)(2,1)}), bf16[8,384,128]{2,1,0:T(8,128)(2,1)S(1)}, u32[]{:S(2)}, u32[]{:S(2)}) async-start(bf16[8,384,128]{2,1,0:T(8,128)(2,1)} %shard_map.107), calls=%async_computation.1 | async-start | bytes 1572864 | tf_op jit(solution)/shard_map/all_to_all | solution.py:388
  79.4 7.6 %collective-permute-done.13.refs_7_ = bf16[128,1024]{1,0:T(8,128)(2,1)S(1)} collective-permute-done((bf16[128,1024]{1,0:T(8,128)(2,1)S(1)}, bf16[128,1024]{1,0:T(8,128)(2,1)S(1)}, u32[]{:S(2)}, u32[]{:S(2)}) %collective-permute-start.13) | collective-permute-done | bytes 262176 | tf_op jit(solution)/shard_map/ppermute | solution.py:310
  87.0 0.7 copy-done.9
  87.7 0.9 copy-done.6
  88.7 0.9 copy-done.10
  89.6 1.4 %shard_map.109 = (bf16[512,384]{1,0:T(8,128)(2,1)S(1)}, bf16[512,384]{1,0:T(8,128)(2,1)S(1)}) custom-call(bf16[256,768]{1,0:T(8,128)(2,1)S(1)} %constant_dynamic-update-slice_fusion.piece_ref.refs_0_, bf16[256,768]{1,0:T(8,128)(2,1)S(1)} %copy-done.4, bf16[256,768]{1,0:T(8,128)(2,1)S(1)} %collective-permute-done.9.refs_2_, ...), custom_call_target="tpu_custom_call" | custom-call | flops 9663676416 | bytes 1572864 | tf_op jit(solution)/shard_map/pallas_call | solution.py:147
  91.0 1.3 %collective-permute-start.14 = (bf16[512,384]{1,0:T(8,128)(2,1)S(1)}, bf16[512,384]{1,0:T(8,128)(2,1)S(1)}, u32[]{:S(2)}, u32[]{:S(2)}) collective-permute-start(bf16[512,384]{1,0:T(8,128)(2,1)S(1)} %get-tuple-element.69), channel_id=1, source_target_pairs={{0,2},{1,3},{2,0},{3,1},{4,6},{5,7},{6,4},{7,5},{8,10},{9,11},{10,... | collective-permute-start | bytes 1179656 | tf_op jit(solution)/shard_map/ppermute | solution.py:310
  92.3 6.6 %collective-permute-done.14.other_ref = bf16[512,384]{1,0:T(8,128)(2,1)S(1)} collective-permute-done((bf16[512,384]{1,0:T(8,128)(2,1)S(1)}, bf16[512,384]{1,0:T(8,128)(2,1)S(1)}, u32[]{:S(2)}, u32[]{:S(2)}) %collective-permute-start.14) | collective-permute-done | bytes 393248 | tf_op jit(solution)/shard_map/ppermute | solution.py:310
  98.8 1.5 %shard_map.110 = f32[384,1024]{1,0:T(8,128)} custom-call(bf16[512,384]{1,0:T(8,128)(2,1)S(1)} %get-tuple-element.68.own_ref, bf16[512,384]{1,0:T(8,128)(2,1)S(1)} %collective-permute-done.14.other_ref), custom_call_target="tpu_custom_call" | custom-call | bytes 2359296 | tf_op jit(solution)/shard_map/pallas_call | solution.py:147
  100.3 1.1 %shard_map.108 = (bf16[128,1024]{1,0:T(8,128)(2,1)}, bf16[128,1024]{1,0:T(8,128)(2,1)}, bf16[128,1024]{1,0:T(8,128)(2,1)}) custom-call(bf16[8,384,128]{2,1,0:T(8,128)(2,1)S(1)} %all-to-all-done.1.tok_ref), custom_call_target="tpu_custom_call" | custom-call | bytes 1572864 | tf_op jit(solution)/shard_map/pallas_call | solution.py:147
  (22 shorter events, 0.1 us)
Async XLA Ops:
  0.6 23.5 %copy-start = (bf16[384,1024]{1,0:T(8,128)(2,1)S(1)}, bf16[384,1024]{1,0:T(8,128)(2,1)}, u32[]{:S(2)}) copy-start(bf16[384,1024]{1,0:T(8,128)(2,1)} %own_ref.1) | copy-start | bytes 2359300
  0.6 20.8 %collective-permute-start.3 = (bf16[384,1024]{1,0:T(8,128)(2,1)}, bf16[384,1024]{1,0:T(8,128)(2,1)S(1)}, u32[]{:S(2)}, u32[]{:S(2)}) collective-permute-start(bf16[384,1024]{1,0:T(8,128)(2,1)} %own_ref.1), channel_id=1, source_target_pairs={{0,2},{1,3},{2,0},{3,1},{4,6},{5,7},{6,4},{7,5},{8,10},{9,11},{10,... | collective-permute-start | bytes 2359304 | tf_op jit(solution)/shard_map/ppermute | solution.py:310
  4.7 7.3 %collective-permute-start.2 = (bf16[64,768]{1,0:T(8,128)(2,1)S(1)}, bf16[64,768]{1,0:T(8,128)(2,1)S(1)}, u32[]{:S(2)}, u32[]{:S(2)}) collective-permute-start(bf16[64,768]{1,0:T(8,128)(2,1)S(1)} %get-tuple-element.70), channel_id=1, source_target_pairs={{0,12},{1,13},{2,14},{3,15},{4,8},{5,9},{6,10},{7,11},{8,4},{9,5},... | collective-permute-start | bytes 294920 | tf_op jit(solution)/shard_map/ppermute | solution.py:310
  8.4 6.1 %collective-permute-start = (bf16[64,768]{1,0:T(8,128)(2,1)S(1)}, bf16[64,768]{1,0:T(8,128)(2,1)S(1)}, u32[]{:S(2)}, u32[]{:S(2)}) collective-permute-start(bf16[64,768]{1,0:T(8,128)(2,1)S(1)} %get-tuple-element.71), channel_id=1, source_target_pairs={{0,4},{1,5},{2,6},{3,7},{4,0},{5,1},{6,2},{7,3},{8,12},{9,13},{10,... | collective-permute-start | bytes 294920 | tf_op jit(solution)/shard_map/ppermute | solution.py:310
  8.4 8.0 %collective-permute-start.1 = (bf16[64,768]{1,0:T(8,128)(2,1)S(1)}, bf16[64,768]{1,0:T(8,128)(2,1)S(1)}, u32[]{:S(2)}, u32[]{:S(2)}) collective-permute-start(bf16[64,768]{1,0:T(8,128)(2,1)S(1)} %get-tuple-element.73), channel_id=1, source_target_pairs={{0,8},{1,9},{2,10},{3,11},{4,12},{5,13},{6,14},{7,15},{8,0},{9,1},... | collective-permute-start | bytes 294920 | tf_op jit(solution)/shard_map/ppermute | solution.py:310
  16.4 24.3 %all-to-all-start = ((bf16[8,384,128]{2,1,0:T(8,128)(2,1)}), bf16[8,384,128]{2,1,0:T(8,128)(2,1)S(1)}, u32[]{:S(2)}, u32[]{:S(2)}) async-start(bf16[8,384,128]{2,1,0:T(8,128)(2,1)} %get-tuple-element.38), calls=%async_computation | async-start | bytes 1572864 | tf_op jit(solution)/shard_map/all_to_all | solution.py:354
  21.4 0.9 copy-start.1
  22.4 1.8 %collective-permute-start.4 = (bf16[256,768]{1,0:T(8,128)(2,1)S(1)}, bf16[256,768]{1,0:T(8,128)(2,1)S(1)}, u32[]{:S(2)}, u32[]{:S(2)}) collective-permute-start(bf16[256,768]{1,0:T(8,128)(2,1)S(1)} %constant_dynamic-update-slice_fusion.piece_ref.refs_0_), channel_id=1, source_target_pairs={{0,1},{1,0},{2,3},{3,2},{4,5},{5,4},{6,7},{7,6},{8,9},{9,8},{10,11... | collective-permute-start | bytes 1179656 | tf_op jit(solution)/shard_map/ppermute | solution.py:310
  24.2 1.1 %copy-start.2 = (bf16[384,1024]{1,0:T(8,128)(2,1)S(1)}, bf16[384,1024]{1,0:T(8,128)(2,1)}, u32[]{:S(2)}) copy-start(bf16[384,1024]{1,0:T(8,128)(2,1)} %copy-done.1) | copy-start | bytes 2359300
  25.3 2.6 %copy-start.3 = (bf16[256,768]{1,0:T(8,128)(2,1)}, bf16[256,768]{1,0:T(8,128)(2,1)S(1)}, u32[]{:S(2)}) copy-start(bf16[256,768]{1,0:T(8,128)(2,1)S(1)} %collective-permute-done.4.swapped_ref.refs_1_) | copy-start | bytes 1179652
  27.2 0.7 copy-start.8
  27.9 20.0 %collective-permute-start.5 = (bf16[512,256]{1,0:T(8,128)(2,1)}, bf16[512,256]{1,0:T(8,128)(2,1)S(1)}, u32[]{:S(2)}, u32[]{:S(2)}) collective-permute-start(bf16[512,256]{1,0:T(8,128)(2,1)} %get-tuple-element.55), channel_id=1, source_target_pairs={{0,4},{1,5},{2,6},{3,7},{4,0},{5,1},{6,2},{7,3},{8,12},{9,13},{10,... | collective-permute-start | bytes 786440 | tf_op jit(solution)/shard_map/ppermute | solution.py:310
  40.6 1.0 copy-start.7
  46.5 20.3 %collective-permute-start.9 = (bf16[256,768]{1,0:T(8,128)(2,1)S(1)}, bf16[256,768]{1,0:T(8,128)(2,1)S(1)}, u32[]{:S(2)}, u32[]{:S(2)}) collective-permute-start(bf16[256,768]{1,0:T(8,128)(2,1)S(1)} %constant_dynamic-update-slice_fusion.piece_ref.refs_0_), channel_id=1, source_target_pairs={{0,2},{1,3},{2,0},{3,1},{4,6},{5,7},{6,4},{7,5},{8,10},{9,11},{10,... | collective-permute-start | bytes 1179656 | tf_op jit(solution)/shard_map/ppermute | solution.py:310
  47.9 18.2 %collective-permute-start.6 = (bf16[512,256]{1,0:T(8,128)(2,1)}, bf16[512,256]{1,0:T(8,128)(2,1)S(1)}, u32[]{:S(2)}, u32[]{:S(2)}) collective-permute-start(bf16[512,256]{1,0:T(8,128)(2,1)} %copy-done.8), channel_id=1, source_target_pairs={{0,4},{1,5},{2,6},{3,7},{4,0},{5,1},{6,2},{7,3},{8,12},{9,13},{10,... | collective-permute-start | bytes 786440 | tf_op jit(solution)/shard_map/ppermute | solution.py:310
  48.0 18.2 %collective-permute-start.7 = (bf16[512,256]{1,0:T(8,128)(2,1)S(1)}, bf16[512,256]{1,0:T(8,128)(2,1)S(1)}, u32[]{:S(2)}, u32[]{:S(2)}) collective-permute-start(bf16[512,256]{1,0:T(8,128)(2,1)S(1)} %shard_map.105), channel_id=1, source_target_pairs={{0,8},{1,9},{2,10},{3,11},{4,12},{5,13},{6,14},{7,15},{8,0},{9,1},... | collective-permute-start | bytes 786440 | tf_op jit(solution)/shard_map/ppermute | solution.py:310
  50.1 25.7 %collective-permute-start.12 = (bf16[128,1024]{1,0:T(8,128)(2,1)S(1)}, bf16[128,1024]{1,0:T(8,128)(2,1)S(1)}, u32[]{:S(2)}, u32[]{:S(2)}) collective-permute-start(bf16[128,1024]{1,0:T(8,128)(2,1)S(1)} %get-tuple-element.44.out_ref.refs_4_), channel_id=1, source_target_pairs={{0,4},{1,5},{2,6},{3,7},{4,0},{5,1},{6,2},{7,3},{8,12},{9,13},{10,... | collective-permute-start | bytes 786440 | tf_op jit(solution)/shard_map/ppermute | solution.py:310
  50.1 25.6 %collective-permute-start.11 = (bf16[128,1024]{1,0:T(8,128)(2,1)S(1)}, bf16[128,1024]{1,0:T(8,128)(2,1)S(1)}, u32[]{:S(2)}, u32[]{:S(2)}) collective-permute-start(bf16[128,1024]{1,0:T(8,128)(2,1)S(1)} %get-tuple-element.44.out_ref.refs_4_), channel_id=1, source_target_pairs={{0,8},{1,9},{2,10},{3,11},{4,12},{5,13},{6,14},{7,15},{8,0},{9,1},... | collective-permute-start | bytes 786440 | tf_op jit(solution)/shard_map/ppermute | solution.py:310
  66.2 5.0 %collective-permute-start.8 = (bf16[512,128]{1,0:T(8,128)(2,1)S(1)}, bf16[512,128]{1,0:T(8,128)(2,1)S(1)}, u32[]{:S(2)}, u32[]{:S(2)}) collective-permute-start(bf16[512,128]{1,0:T(8,128)(2,1)S(1)} %get-tuple-element.61), channel_id=1, source_target_pairs={{0,2},{1,3},{2,0},{3,1},{4,6},{5,7},{6,4},{7,5},{8,10},{9,11},{10,... | collective-permute-start | bytes 393224 | tf_op jit(solution)/shard_map/ppermute | solution.py:310
  66.8 20.9 %collective-permute-start.10 = (bf16[256,768]{1,0:T(8,128)(2,1)S(1)}, bf16[256,768]{1,0:T(8,128)(2,1)S(1)}, u32[]{:S(2)}, u32[]{:S(2)}) collective-permute-start(bf16[256,768]{1,0:T(8,128)(2,1)S(1)} %collective-permute-done.9.refs_2_), channel_id=1, source_target_pairs={{0,1},{1,0},{2,3},{3,2},{4,5},{5,4},{6,7},{7,6},{8,9},{9,8},{10,11... | collective-permute-start | bytes 1179656 | tf_op jit(solution)/shard_map/ppermute | solution.py:310
  71.3 16.4 %copy-start.4 = (bf16[256,768]{1,0:T(8,128)(2,1)S(1)}, bf16[256,768]{1,0:T(8,128)(2,1)}, u32[]{:S(2)}) copy-start(bf16[256,768]{1,0:T(8,128)(2,1)} %copy-done.3) | copy-start | bytes 1179652
  75.7 11.3 %copy-start.5 = (bf16[128,1024]{1,0:T(8,128)(2,1)}, bf16[128,1024]{1,0:T(8,128)(2,1)S(1)}, u32[]{:S(2)}) copy-start(bf16[128,1024]{1,0:T(8,128)(2,1)S(1)} %collective-permute-done.11.refs_6_) | copy-start | bytes 786436
  75.7 11.2 %collective-permute-start.13 = (bf16[128,1024]{1,0:T(8,128)(2,1)S(1)}, bf16[128,1024]{1,0:T(8,128)(2,1)S(1)}, u32[]{:S(2)}, u32[]{:S(2)}) collective-permute-start(bf16[128,1024]{1,0:T(8,128)(2,1)S(1)} %collective-permute-done.11.refs_6_), channel_id=1, source_target_pairs={{0,4},{1,5},{2,6},{3,7},{4,0},{5,1},{6,2},{7,3},{8,12},{9,13},{10,... | collective-permute-start | bytes 786440 | tf_op jit(solution)/shard_map/ppermute | solution.py:310
  75.8 24.5 %all-to-all-start.1 = ((bf16[8,384,128]{2,1,0:T(8,128)(2,1)}), bf16[8,384,128]{2,1,0:T(8,128)(2,1)S(1)}, u32[]{:S(2)}, u32[]{:S(2)}) async-start(bf16[8,384,128]{2,1,0:T(8,128)(2,1)} %shard_map.107), calls=%async_computation.1 | async-start | bytes 1572864 | tf_op jit(solution)/shard_map/all_to_all | solution.py:388
  87.0 0.7 copy-start.9
  87.7 1.0 copy-start.6
  88.7 0.9 copy-start.10
  91.0 7.8 %collective-permute-start.14 = (bf16[512,384]{1,0:T(8,128)(2,1)S(1)}, bf16[512,384]{1,0:T(8,128)(2,1)S(1)}, u32[]{:S(2)}, u32[]{:S(2)}) collective-permute-start(bf16[512,384]{1,0:T(8,128)(2,1)S(1)} %get-tuple-element.69), channel_id=1, source_target_pairs={{0,2},{1,3},{2,0},{3,1},{4,6},{5,7},{6,4},{7,5},{8,10},{9,11},{10,... | collective-permute-start | bytes 1179656 | tf_op jit(solution)/shard_map/ppermute | solution.py:310

commit v27 on v23

--- a/solution.py
+++ b/solution.py
@@ -242,12 +242,12 @@
 
 
 def weight_grad_kernel(*refs):
-    *pieces, out0, out1, out2, out3, own_ref, other_ref, cot, outs = refs
+    *pieces, out0, out1, own_ref, other_ref, cot, outs = refs
     tokens = cot.shape[0]
     place_rows(pieces[0], pieces[1], cot, 0)
     place_rows(pieces[2], pieces[3], cot, tokens // 2)
-    for i, ref in enumerate((out0, out1, out2, out3)):
-        outs[i * HD : (i + 1) * HD, :] = ref[...]
+    outs[0:HD, :] = out0[...]
+    outs[HD : 2 * HD, :] = out1[...]
     depth = own_ref.shape[1]
     y = lax.rem(lax.axis_index("seq"), 2)
     for ref, row in ((own_ref, y), (other_ref, 1 - y)):
@@ -296,10 +296,11 @@
             ref[:, h * HD : (h + 1) * HD] = tok_ref[h, i * rows : (i + 1) * rows, :]
 
 
-def unpack_weight_kernel(own_ref, other_ref, w_ref):
-    for other_row, ref in enumerate((own_ref, other_ref)):
-        for i, step in enumerate(STEPS):
-            w_ref[:, head_columns(step, other_row)] = ref[i * HD : (i + 1) * HD, :].astype(F32).T
+def unpack_weight_kernel(own0_ref, other0_ref, own1_ref, other1_ref, w_ref):
+    for i, step in enumerate(STEPS):
+        rows = slice(i % 2 * HD, (i % 2 + 1) * HD)
+        for other_row, ref in enumerate((own0_ref, other0_ref) if i < 2 else (own1_ref, other1_ref)):
+            w_ref[:, head_columns(step, other_row)] = ref[rows, :].astype(F32).T
 
 
 def exchange(array, distance=0, cores=False):
@@ -389,16 +390,23 @@
         moved=4 * total * image,
     )
     grad_in = lax.all_to_all(grad_out, "seq", split_axis=0, concat_axis=0, tiled=True)
-    out_far, out_near, other_row, _ = lax.optimization_barrier((out_far, out_near, other_row, grad_out))
-    outs = [out_t, out_near, out_far, exchange(out_far, 2)]
-    dw_own, dw_other = call(
-        weight_grad_kernel,
-        [shape((4 * HD, depth), BF16)] * 2,
-        [row, row_swapped, other_row, other_swapped, *outs],
-        scratch=[pltpu.VMEM((image, columns), BF16), pltpu.VMEM((4 * HD, image), BF16)],
-        flops=96 * image * columns * HD,
-        moved=2 * image * columns,
-    )
+
+    def weight_grad(flops, *outs):
+        return call(
+            weight_grad_kernel,
+            [shape((2 * HD, depth), BF16)] * 2,
+            [row, row_swapped, other_row, other_swapped, *outs],
+            scratch=[pltpu.VMEM((image, columns), BF16), pltpu.VMEM((2 * HD, image), BF16)],
+            flops=flops,
+            moved=image * columns,
+        )
+
+    own0, other0 = weight_grad(0, out_t, out_near)
+    out_far, other0, _ = lax.optimization_barrier((out_far, other0, grad_out))
+    other0 = exchange(other0, 1)
+    last = exchange(out_far, 2)
+    last, other0 = lax.optimization_barrier((last, other0))
+    own1, other1 = weight_grad(96 * image * columns * HD, out_far, last)
     grads = call(
         unpack_kernel,
         [shape((rows, width), BF16)] * 3,
@@ -408,7 +416,7 @@
     (d_weight,) = call(
         unpack_weight_kernel,
         [shape((depth, width), F32)],
-        [dw_own, exchange(dw_other, 1)],
+        [own0, other0, own1, exchange(other1, 1)],
         moved=6 * depth * width,
     )
     return (*grads, d_weight)

time: 97.6 us -> 104 us (1.066)
  waiting for transfers between devices: 48.5 us -> 53.1 us
  local copies, waits for them, and re-layouts: 3.72 us -> 4.79 us
    all_to_all x1, waiting for transfers between devices: 0.01 us -> 11 us  [local(): lax.all_to_all(tok_out, 'seq', split_axis=0, concat_axis=0, tiled=True)]
    ppermute x15 -> x16, waiting for transfers between devices: 48.5 us -> 42.1 us  [exchange(): return lax.ppermute(array, ('seq', 'fsdp'), pairs)]
    unnamed x19 -> x15, local copies, waits for them, and re-layouts: 2.65 us -> 3.72 us
    pallas_call x9 -> x10, Pallas kernels: 17.3 us -> 18 us  [call(): pl.pallas_call(kernel, out_shape=outs, grid_spec=pltpu.PrefetchScalarGrid...]
    ppermute x15 -> x16, starting transfers between devices: 19 us -> 19.7 us  [exchange(): return lax.ppermute(array, ('seq', 'fsdp'), pairs)]
  transfers between devices with their start and end apart: 17 -> 18, of which waited for: 14 -> 14; matrix products, arithmetic and copies ran while one was open for 1% -> 1% of each run, Pallas kernels for 17% -> 16%
where the time goes in v27:
time: 104 us
  waiting for transfers between devices  53.1 us (51%)
  starting transfers between devices  27.3 us (26%)
  Pallas kernels  18 us (17%)
  local copies, waits for them, and re-layouts  4.79 us (5%)
    ppermute x16, waiting for transfers between devices, exchange(): return lax.ppermute(array, ('seq', 'fsdp'), pairs)  42.1 us
    ppermute x16, starting transfers between devices, exchange(): return lax.ppermute(array, ('seq', 'fsdp'), pairs)  19.7 us
    pallas_call x10, Pallas kernels, call(): pl.pallas_call(kernel, out_shape=outs, grid_spec=pltpu.PrefetchScalarGrid...  18 us
    all_to_all x1, waiting for transfers between devices, local(): lax.all_to_all(tok_out, 'seq', split_axis=0, concat_axis=0, tiled=True)  11 us
    all_to_all x1, starting transfers between devices, local(): lax.all_to_all(tok_out, 'seq', split_axis=0, concat_axis=0, tiled=True)  4.11 us
    unnamed x15, local copies, waits for them, and re-layouts  3.72 us
    all_to_all x1, starting transfers between devices, local(): lax.all_to_all(grad_out, 'seq', split_axis=0, concat_axis=0, tiled=True)  3.55 us
  transfers between devices with their start and end apart: 18, of which 14 were waited for; matrix products, arithmetic and copies ran while one was open for 1% of the time, Pallas kernels for 16%

profile of v27, /device:TPU:0, one launch (start us, length us, event | category | flops | bytes accessed | tf_op | source)
XLA Modules:
  0.0 103.9 jit_solution(11766012937862774819)
XLA Ops:
  0.6 3.0 %collective-permute-start.3 = (bf16[384,1024]{1,0:T(8,128)(2,1)}, bf16[384,1024]{1,0:T(8,128)(2,1)S(1)}, u32[]{:S(2)}, u32[]{:S(2)}) collective-permute-start(bf16[384,1024]{1,0:T(8,128)(2,1)} %own_ref.1), channel_id=1, source_target_pairs={{0,2},{1,3},{2,0},{3,1},{4,6},{5,7},{6,4},{7,5},{8,10},{9,11},{10,... | collective-permute-start | bytes 2359304 | tf_op jit(solution)/shard_map/ppermute | solution.py:311
  3.7 1.1 %fusion = (bf16[64,768]{1,0:T(8,128)(2,1)S(1)}, bf16[64,768]{1,0:T(8,128)(2,1)S(1)}, bf16[64,768]{1,0:T(8,128)(2,1)S(1)}, bf16[64,768]{1,0:T(8,128)(2,1)S(1)}) fusion(bf16[128,3072]{1,0:T(8,128)(2,1)} %param.13, s32[]{:T(128)S(6)} %select_n.23, s32[]{:T(128)S(6)} %select_n.28, s32[]{:T(128)S(6)} %select_n.26, s32[]{:T(128)S(6)} %select_n.25, s32[]{:T(128)S(6)} %select_n.27), kind=kLoop, calls=%fused_computation.4 | loop fusion | bytes 786452 | tf_op jit(solution)/shard_map/dynamic_slice | solution.py:320
  4.7 3.7 %collective-permute-start.2 = (bf16[64,768]{1,0:T(8,128)(2,1)S(1)}, bf16[64,768]{1,0:T(8,128)(2,1)S(1)}, u32[]{:S(2)}, u32[]{:S(2)}) collective-permute-start(bf16[64,768]{1,0:T(8,128)(2,1)S(1)} %get-tuple-element.84), channel_id=1, source_target_pairs={{0,12},{1,13},{2,14},{3,15},{4,8},{5,9},{6,10},{7,11},{8,4},{9,5},... | collective-permute-start | bytes 294920 | tf_op jit(solution)/shard_map/ppermute | solution.py:311
  8.4 0.0 collective-permute-start
  8.4 0.8 collective-permute-start.1
  9.2 2.3 %shard_map.102 = (bf16[8,384,128]{2,1,0:T(8,128)(2,1)}, bf16[2,512,128]{2,1,0:T(8,128)(2,1)}) custom-call(s32[1]{0:T(128)} %bitcast.me_ref, bf16[128,1024]{1,0:T(8,128)(2,1)} %q_ref.1, bf16[128,1024]{1,0:T(8,128)(2,1)} %k_ref.1, bf16[128,1024]{1,0:T(8,128)(2,1)} %v_ref.1, bf16[512,1024]{1,0:T(8,128)(2,1)} %kt_ref.1, bf16[512,1024]{1,0:T(8,128)(2,1)} %vt_ref.1), custom_call_target="tpu_custom_call" | custom-call | bytes 1572864 | tf_op jit(solution)/shard_map/pallas_call | solution.py:147
  11.5 0.6 collective-permute-done.2
  12.1 2.4 %collective-permute-done = bf16[64,768]{1,0:T(8,128)(2,1)S(1)} collective-permute-done((bf16[64,768]{1,0:T(8,128)(2,1)S(1)}, bf16[64,768]{1,0:T(8,128)(2,1)S(1)}, u32[]{:S(2)}, u32[]{:S(2)}) %collective-permute-start) | collective-permute-done | bytes 98336 | tf_op jit(solution)/shard_map/ppermute | solution.py:311
  14.5 1.9 %collective-permute-done.1 = bf16[64,768]{1,0:T(8,128)(2,1)S(1)} collective-permute-done((bf16[64,768]{1,0:T(8,128)(2,1)S(1)}, bf16[64,768]{1,0:T(8,128)(2,1)S(1)}, u32[]{:S(2)}, u32[]{:S(2)}) %collective-permute-start.1) | collective-permute-done | bytes 98336 | tf_op jit(solution)/shard_map/ppermute | solution.py:311
  16.4 4.1 %all-to-all-start = ((bf16[8,384,128]{2,1,0:T(8,128)(2,1)}), bf16[8,384,128]{2,1,0:T(8,128)(2,1)S(1)}, u32[]{:S(2)}, u32[]{:S(2)}) async-start(bf16[8,384,128]{2,1,0:T(8,128)(2,1)} %get-tuple-element.45), calls=%async_computation | async-start | bytes 1572864 | tf_op jit(solution)/shard_map/all_to_all | solution.py:355
  20.5 0.9 collective-permute-done.3.other_ref
  21.4 0.9 copy-done.1
  22.4 0.1 collective-permute-start.4
  22.5 1.7 %collective-permute-done.4.swapped_ref.refs_1_ = bf16[256,768]{1,0:T(8,128)(2,1)S(1)} collective-permute-done((bf16[256,768]{1,0:T(8,128)(2,1)S(1)}, bf16[256,768]{1,0:T(8,128)(2,1)S(1)}, u32[]{:S(2)}, u32[]{:S(2)}) %collective-permute-start.4) | collective-permute-done | bytes 393248 | tf_op jit(solution)/shard_map/ppermute | solution.py:311
  24.2 1.1 %copy-done.2 = bf16[384,1024]{1,0:T(8,128)(2,1)S(1)} copy-done((bf16[384,1024]{1,0:T(8,128)(2,1)S(1)}, bf16[384,1024]{1,0:T(8,128)(2,1)}, u32[]{:S(2)}) %copy-start.2) | copy-done | bytes 786456
  25.3 1.9 %shard_map.104 = (f32[512,256]{1,0:T(8,128)S(1)}, bf16[512,256]{1,0:T(8,128)(2,1)S(1)}, f32[512,256]{1,0:T(8,128)S(1)}, bf16[512,256]{1,0:T(8,128)(2,1)}) custom-call(bf16[256,768]{1,0:T(8,128)(2,1)S(1)} %constant_dynamic-update-slice_fusion.piece_ref.refs_0_, bf16[256,768]{1,0:T(8,128)(2,1)S(1)} %collective-permute-done.4.swapped_ref.refs_1_, ...), custom_call_target="tpu_custom_call" | custom-call | flops 805306368 | bytes 1572864 | tf_op jit(solution)/shard_map/pallas_call | solution.py:147
  27.2 0.7 copy-done.4
  27.9 1.8 %collective-permute-start.5 = (bf16[512,256]{1,0:T(8,128)(2,1)}, bf16[512,256]{1,0:T(8,128)(2,1)S(1)}, u32[]{:S(2)}, u32[]{:S(2)}) collective-permute-start(bf16[512,256]{1,0:T(8,128)(2,1)} %get-tuple-element.63), channel_id=1, source_target_pairs={{0,4},{1,5},{2,6},{3,7},{4,0},{5,1},{6,2},{7,3},{8,12},{9,13},{10,... | collective-permute-start | bytes 786440 | tf_op jit(solution)/shard_map/ppermute | solution.py:311
  29.7 11.0 %all-to-all-done.tok_ref = bf16[8,384,128]{2,1,0:T(8,128)(2,1)S(1)} async-done(((bf16[8,384,128]{2,1,0:T(8,128)(2,1)}), bf16[8,384,128]{2,1,0:T(8,128)(2,1)S(1)}, u32[]{:S(2)}, u32[]{:S(2)}) %all-to-all-start) | async-done | bytes 786464 | tf_op jit(solution)/shard_map/all_to_all | solution.py:355
  40.6 0.9 copy-done.3
  41.6 4.9 %shard_map.103 = (bf16[1536,1024]{1,0:T(8,128)(2,1)S(1)}, bf16[128,1024]{1,0:T(8,128)(2,1)S(1)}, bf16[1024,128]{1,0:T(8,128)(2,1)S(1)}, bf16[128,1536]{1,0:T(8,128)(2,1)S(1)}, bf16[1536,128]{1,0:T(8,128)(2,1)S(1)}) custom-call(bf16[8,384,128]{2,1,0:T(8,128)(2,1)S(1)} %all-to-all-done.tok_ref, bf16[2,512,128]{2,1,0:T(8,128)(2,1)S(1)} %copy-done.3), custom_call_target="tpu_custom_call" | custom-call | flops 805306368 | bytes 6291456 | tf_op jit(solution)/shard_map/pallas_call | solution.py:147
  46.5 1.4 %collective-permute-start.9 = (bf16[256,768]{1,0:T(8,128)(2,1)S(1)}, bf16[256,768]{1,0:T(8,128)(2,1)S(1)}, u32[]{:S(2)}, u32[]{:S(2)}) collective-permute-start(bf16[256,768]{1,0:T(8,128)(2,1)S(1)} %constant_dynamic-update-slice_fusion.piece_ref.refs_0_), channel_id=1, source_target_pairs={{0,2},{1,3},{2,0},{3,1},{4,6},{5,7},{6,4},{7,5},{8,10},{9,11},{10,... | collective-permute-start | bytes 1179656 | tf_op jit(solution)/shard_map/ppermute | solution.py:311
  47.9 0.0 collective-permute-done.5.received_ref
  48.0 0.1 collective-permute-start.6
  48.0 2.0 %collective-permute-start.7 = (bf16[512,256]{1,0:T(8,128)(2,1)S(1)}, bf16[512,256]{1,0:T(8,128)(2,1)S(1)}, u32[]{:S(2)}, u32[]{:S(2)}) collective-permute-start(bf16[512,256]{1,0:T(8,128)(2,1)S(1)} %copy-done.5), channel_id=1, source_target_pairs={{0,4},{1,5},{2,6},{3,7},{4,0},{5,1},{6,2},{7,3},{8,12},{9,13},{10,... | collective-permute-start | bytes 786440 | tf_op jit(solution)/shard_map/ppermute | solution.py:311
  50.1 6.1 %collective-permute-done.9.refs_2_ = bf16[256,768]{1,0:T(8,128)(2,1)S(1)} collective-permute-done((bf16[256,768]{1,0:T(8,128)(2,1)S(1)}, bf16[256,768]{1,0:T(8,128)(2,1)S(1)}, u32[]{:S(2)}, u32[]{:S(2)}) %collective-permute-start.9) | collective-permute-done | bytes 393248 | tf_op jit(solution)/shard_map/ppermute | solution.py:311
  56.1 0.0 collective-permute-start.10
  56.1 5.2 %collective-permute-done.6.far_ref = bf16[512,256]{1,0:T(8,128)(2,1)S(1)} collective-permute-done((bf16[512,256]{1,0:T(8,128)(2,1)S(1)}, bf16[512,256]{1,0:T(8,128)(2,1)S(1)}, u32[]{:S(2)}, u32[]{:S(2)}) %collective-permute-start.6) | collective-permute-done | bytes 262176 | tf_op jit(solution)/shard_map/ppermute | solution.py:311
  61.4 0.2 collective-permute-done.7.near_ref
  61.5 0.1 shard_map.106
  61.6 0.4 collective-permute-start.8
  62.0 0.0 collective-permute-start.11
  62.0 2.1 %collective-permute-start.12 = (bf16[128,1024]{1,0:T(8,128)(2,1)S(1)}, bf16[128,1024]{1,0:T(8,128)(2,1)S(1)}, u32[]{:S(2)}, u32[]{:S(2)}) collective-permute-start(bf16[128,1024]{1,0:T(8,128)(2,1)S(1)} %get-tuple-element.75.out_ref.refs_4_), channel_id=1, source_target_pairs={{0,8},{1,9},{2,10},{3,11},{4,12},{5,13},{6,14},{7,15},{8,0},{9,1},... | collective-permute-start | bytes 786440 | tf_op jit(solution)/shard_map/ppermute | solution.py:311
  64.1 2.8 %collective-permute-done.8.refs_1_ = bf16[512,128]{1,0:T(8,128)(2,1)S(1)} collective-permute-done((bf16[512,128]{1,0:T(8,128)(2,1)S(1)}, bf16[512,128]{1,0:T(8,128)(2,1)S(1)}, u32[]{:S(2)}, u32[]{:S(2)}) %collective-permute-start.8) | collective-permute-done | bytes 131104 | tf_op jit(solution)/shard_map/ppermute | solution.py:311
  66.9 4.5 %shard_map.107 = bf16[8,384,128]{2,1,0:T(8,128)(2,1)} custom-call(bf16[1024,128]{1,0:T(8,128)(2,1)S(1)} %get-tuple-element.47.queries_ref, bf16[128,1536]{1,0:T(8,128)(2,1)S(1)} %get-tuple-element.48.keys_t_ref, bf16[1536,128]{1,0:T(8,128)(2,1)S(1)} %get-tuple-element.49.vals_ref, bf16[1536,1024]{1,0:T(8,128)(2,1)S(1)} %get-tuple-element.50.probs_ref, ...), custom_call_target="tpu_custom_call" | custom-call | flops 1610612736 | bytes 6291456 | tf_op jit(solution)/shard_map/pallas_call | solution.py:147
  71.4 3.5 %all-to-all-start.1 = ((bf16[8,384,128]{2,1,0:T(8,128)(2,1)}), bf16[8,384,128]{2,1,0:T(8,128)(2,1)S(1)}, u32[]{:S(2)}, u32[]{:S(2)}) async-start(bf16[8,384,128]{2,1,0:T(8,128)(2,1)} %shard_map.107), calls=%async_computation.1 | async-start | bytes 1572864 | tf_op jit(solution)/shard_map/all_to_all | solution.py:392
  74.9 0.0 collective-permute-done.11.refs_5_
  74.9 0.8 shard_map.109
  75.8 0.6 collective-permute-done.12.refs_4_
  76.4 1.3 %collective-permute-start.13 = (bf16[128,1024]{1,0:T(8,128)(2,1)S(1)}, bf16[128,1024]{1,0:T(8,128)(2,1)S(1)}, u32[]{:S(2)}, u32[]{:S(2)}) collective-permute-start(bf16[128,1024]{1,0:T(8,128)(2,1)S(1)} %collective-permute-done.12.refs_4_), channel_id=1, source_target_pairs={{0,4},{1,5},{2,6},{3,7},{4,0},{5,1},{6,2},{7,3},{8,12},{9,13},{10,... | collective-permute-start | bytes 786440 | tf_op jit(solution)/shard_map/ppermute | solution.py:311
  77.8 1.5 %collective-permute-start.14 = (bf16[256,384]{1,0:T(8,128)(2,1)S(1)}, bf16[256,384]{1,0:T(8,128)(2,1)S(1)}, u32[]{:S(2)}, u32[]{:S(2)}) collective-permute-start(bf16[256,384]{1,0:T(8,128)(2,1)S(1)} %get-tuple-element.79), channel_id=1, source_target_pairs={{0,2},{1,3},{2,0},{3,1},{4,6},{5,7},{6,4},{7,5},{8,10},{9,11},{10,... | collective-permute-start | bytes 589832 | tf_op jit(solution)/shard_map/ppermute | solution.py:311
  79.2 9.7 %collective-permute-done.14.other0_ref = bf16[256,384]{1,0:T(8,128)(2,1)S(1)} collective-permute-done((bf16[256,384]{1,0:T(8,128)(2,1)S(1)}, bf16[256,384]{1,0:T(8,128)(2,1)S(1)}, u32[]{:S(2)}, u32[]{:S(2)}) %collective-permute-start.14) | collective-permute-done | bytes 196640 | tf_op jit(solution)/shard_map/ppermute | solution.py:311
  89.0 5.8 %collective-permute-done.13.refs_5_ = bf16[128,1024]{1,0:T(8,128)(2,1)S(1)} collective-permute-done((bf16[128,1024]{1,0:T(8,128)(2,1)S(1)}, bf16[128,1024]{1,0:T(8,128)(2,1)S(1)}, u32[]{:S(2)}, u32[]{:S(2)}) %collective-permute-start.13) | collective-permute-done | bytes 262176 | tf_op jit(solution)/shard_map/ppermute | solution.py:311
  94.8 0.8 shard_map.110
  95.6 1.6 %collective-permute-start.15 = (bf16[256,384]{1,0:T(8,128)(2,1)S(1)}, bf16[256,384]{1,0:T(8,128)(2,1)S(1)}, u32[]{:S(2)}, u32[]{:S(2)}) collective-permute-start(bf16[256,384]{1,0:T(8,128)(2,1)S(1)} %get-tuple-element.83), channel_id=1, source_target_pairs={{0,2},{1,3},{2,0},{3,1},{4,6},{5,7},{6,4},{7,5},{8,10},{9,11},{10,... | collective-permute-start | bytes 589832 | tf_op jit(solution)/shard_map/ppermute | solution.py:311
  97.2 4.2 %collective-permute-done.15.other1_ref = bf16[256,384]{1,0:T(8,128)(2,1)S(1)} collective-permute-done((bf16[256,384]{1,0:T(8,128)(2,1)S(1)}, bf16[256,384]{1,0:T(8,128)(2,1)S(1)}, u32[]{:S(2)}, u32[]{:S(2)}) %collective-permute-start.15) | collective-permute-done | bytes 196640 | tf_op jit(solution)/shard_map/ppermute | solution.py:311
  101.4 1.5 %shard_map.111 = f32[384,1024]{1,0:T(8,128)} custom-call(bf16[256,384]{1,0:T(8,128)(2,1)S(1)} %get-tuple-element.76.own0_ref, bf16[256,384]{1,0:T(8,128)(2,1)S(1)} %collective-permute-done.14.other0_ref, bf16[256,384]{1,0:T(8,128)(2,1)S(1)} %get-tuple-element.82.own1_ref, bf16[256,384]{1,0:T(8,128)(2,1)S(1)} %collective-permute-done.15.other1_ref), custom_call_target="tpu_custom_call" | custom-call | bytes 2359296 | tf_op jit(solution)/shard_map/pallas_call | solution.py:147
  102.9 1.1 %shard_map.108 = (bf16[128,1024]{1,0:T(8,128)(2,1)}, bf16[128,1024]{1,0:T(8,128)(2,1)}, bf16[128,1024]{1,0:T(8,128)(2,1)}) custom-call(bf16[8,384,128]{2,1,0:T(8,128)(2,1)S(1)} %all-to-all-done.1.tok_ref), custom_call_target="tpu_custom_call" | custom-call | bytes 1572864 | tf_op jit(solution)/shard_map/pallas_call | solution.py:147
  (15 shorter events, 0.1 us)
Async XLA Ops:
  0.6 23.5 %copy-start = (bf16[384,1024]{1,0:T(8,128)(2,1)S(1)}, bf16[384,1024]{1,0:T(8,128)(2,1)}, u32[]{:S(2)}) copy-start(bf16[384,1024]{1,0:T(8,128)(2,1)} %own_ref.1) | copy-start | bytes 2359300
  0.6 20.8 %collective-permute-start.3 = (bf16[384,1024]{1,0:T(8,128)(2,1)}, bf16[384,1024]{1,0:T(8,128)(2,1)S(1)}, u32[]{:S(2)}, u32[]{:S(2)}) collective-permute-start(bf16[384,1024]{1,0:T(8,128)(2,1)} %own_ref.1), channel_id=1, source_target_pairs={{0,2},{1,3},{2,0},{3,1},{4,6},{5,7},{6,4},{7,5},{8,10},{9,11},{10,... | collective-permute-start | bytes 2359304 | tf_op jit(solution)/shard_map/ppermute | solution.py:311
  4.7 7.3 %collective-permute-start.2 = (bf16[64,768]{1,0:T(8,128)(2,1)S(1)}, bf16[64,768]{1,0:T(8,128)(2,1)S(1)}, u32[]{:S(2)}, u32[]{:S(2)}) collective-permute-start(bf16[64,768]{1,0:T(8,128)(2,1)S(1)} %get-tuple-element.84), channel_id=1, source_target_pairs={{0,12},{1,13},{2,14},{3,15},{4,8},{5,9},{6,10},{7,11},{8,4},{9,5},... | collective-permute-start | bytes 294920 | tf_op jit(solution)/shard_map/ppermute | solution.py:311
  8.4 6.1 %collective-permute-start = (bf16[64,768]{1,0:T(8,128)(2,1)S(1)}, bf16[64,768]{1,0:T(8,128)(2,1)S(1)}, u32[]{:S(2)}, u32[]{:S(2)}) collective-permute-start(bf16[64,768]{1,0:T(8,128)(2,1)S(1)} %get-tuple-element.85), channel_id=1, source_target_pairs={{0,4},{1,5},{2,6},{3,7},{4,0},{5,1},{6,2},{7,3},{8,12},{9,13},{10,... | collective-permute-start | bytes 294920 | tf_op jit(solution)/shard_map/ppermute | solution.py:311
  8.4 8.0 %collective-permute-start.1 = (bf16[64,768]{1,0:T(8,128)(2,1)S(1)}, bf16[64,768]{1,0:T(8,128)(2,1)S(1)}, u32[]{:S(2)}, u32[]{:S(2)}) collective-permute-start(bf16[64,768]{1,0:T(8,128)(2,1)S(1)} %get-tuple-element.87), channel_id=1, source_target_pairs={{0,8},{1,9},{2,10},{3,11},{4,12},{5,13},{6,14},{7,15},{8,0},{9,1},... | collective-permute-start | bytes 294920 | tf_op jit(solution)/shard_map/ppermute | solution.py:311
  16.4 24.3 %all-to-all-start = ((bf16[8,384,128]{2,1,0:T(8,128)(2,1)}), bf16[8,384,128]{2,1,0:T(8,128)(2,1)S(1)}, u32[]{:S(2)}, u32[]{:S(2)}) async-start(bf16[8,384,128]{2,1,0:T(8,128)(2,1)} %get-tuple-element.45), calls=%async_computation | async-start | bytes 1572864 | tf_op jit(solution)/shard_map/all_to_all | solution.py:355
  21.4 0.9 copy-start.1
  22.4 1.8 %collective-permute-start.4 = (bf16[256,768]{1,0:T(8,128)(2,1)S(1)}, bf16[256,768]{1,0:T(8,128)(2,1)S(1)}, u32[]{:S(2)}, u32[]{:S(2)}) collective-permute-start(bf16[256,768]{1,0:T(8,128)(2,1)S(1)} %constant_dynamic-update-slice_fusion.piece_ref.refs_0_), channel_id=1, source_target_pairs={{0,1},{1,0},{2,3},{3,2},{4,5},{5,4},{6,7},{7,6},{8,9},{9,8},{10,11... | collective-permute-start | bytes 1179656 | tf_op jit(solution)/shard_map/ppermute | solution.py:311
  24.2 1.1 %copy-start.2 = (bf16[384,1024]{1,0:T(8,128)(2,1)S(1)}, bf16[384,1024]{1,0:T(8,128)(2,1)}, u32[]{:S(2)}) copy-start(bf16[384,1024]{1,0:T(8,128)(2,1)} %copy-done.1) | copy-start | bytes 2359300
  27.2 0.7 copy-start.4
  27.9 20.0 %collective-permute-start.5 = (bf16[512,256]{1,0:T(8,128)(2,1)}, bf16[512,256]{1,0:T(8,128)(2,1)S(1)}, u32[]{:S(2)}, u32[]{:S(2)}) collective-permute-start(bf16[512,256]{1,0:T(8,128)(2,1)} %get-tuple-element.63), channel_id=1, source_target_pairs={{0,4},{1,5},{2,6},{3,7},{4,0},{5,1},{6,2},{7,3},{8,12},{9,13},{10,... | collective-permute-start | bytes 786440 | tf_op jit(solution)/shard_map/ppermute | solution.py:311
  40.6 1.0 copy-start.3
  41.6 6.4 %copy-start.5 = (bf16[512,256]{1,0:T(8,128)(2,1)S(1)}, bf16[512,256]{1,0:T(8,128)(2,1)}, u32[]{:S(2)}) copy-start(bf16[512,256]{1,0:T(8,128)(2,1)} %copy-done.4) | copy-start | bytes 786436
  46.5 9.6 %collective-permute-start.9 = (bf16[256,768]{1,0:T(8,128)(2,1)S(1)}, bf16[256,768]{1,0:T(8,128)(2,1)S(1)}, u32[]{:S(2)}, u32[]{:S(2)}) collective-permute-start(bf16[256,768]{1,0:T(8,128)(2,1)S(1)} %constant_dynamic-update-slice_fusion.piece_ref.refs_0_), channel_id=1, source_target_pairs={{0,2},{1,3},{2,0},{3,1},{4,6},{5,7},{6,4},{7,5},{8,10},{9,11},{10,... | collective-permute-start | bytes 1179656 | tf_op jit(solution)/shard_map/ppermute | solution.py:311
  48.0 13.4 %collective-permute-start.6 = (bf16[512,256]{1,0:T(8,128)(2,1)S(1)}, bf16[512,256]{1,0:T(8,128)(2,1)S(1)}, u32[]{:S(2)}, u32[]{:S(2)}) collective-permute-start(bf16[512,256]{1,0:T(8,128)(2,1)S(1)} %shard_map.105), channel_id=1, source_target_pairs={{0,8},{1,9},{2,10},{3,11},{4,12},{5,13},{6,14},{7,15},{8,0},{9,1},... | collective-permute-start | bytes 786440 | tf_op jit(solution)/shard_map/ppermute | solution.py:311
  48.0 13.5 %collective-permute-start.7 = (bf16[512,256]{1,0:T(8,128)(2,1)S(1)}, bf16[512,256]{1,0:T(8,128)(2,1)S(1)}, u32[]{:S(2)}, u32[]{:S(2)}) collective-permute-start(bf16[512,256]{1,0:T(8,128)(2,1)S(1)} %copy-done.5), channel_id=1, source_target_pairs={{0,4},{1,5},{2,6},{3,7},{4,0},{5,1},{6,2},{7,3},{8,12},{9,13},{10,... | collective-permute-start | bytes 786440 | tf_op jit(solution)/shard_map/ppermute | solution.py:311
  56.1 18.8 %collective-permute-start.10 = (bf16[256,768]{1,0:T(8,128)(2,1)S(1)}, bf16[256,768]{1,0:T(8,128)(2,1)S(1)}, u32[]{:S(2)}, u32[]{:S(2)}) collective-permute-start(bf16[256,768]{1,0:T(8,128)(2,1)S(1)} %collective-permute-done.9.refs_2_), channel_id=1, source_target_pairs={{0,1},{1,0},{2,3},{3,2},{4,5},{5,4},{6,7},{7,6},{8,9},{9,8},{10,11... | collective-permute-start | bytes 1179656 | tf_op jit(solution)/shard_map/ppermute | solution.py:311
  61.6 5.3 %collective-permute-start.8 = (bf16[512,128]{1,0:T(8,128)(2,1)S(1)}, bf16[512,128]{1,0:T(8,128)(2,1)S(1)}, u32[]{:S(2)}, u32[]{:S(2)}) collective-permute-start(bf16[512,128]{1,0:T(8,128)(2,1)S(1)} %get-tuple-element.70), channel_id=1, source_target_pairs={{0,2},{1,3},{2,0},{3,1},{4,6},{5,7},{6,4},{7,5},{8,10},{9,11},{10,... | collective-permute-start | bytes 393224 | tf_op jit(solution)/shard_map/ppermute | solution.py:311
  62.0 12.9 %collective-permute-start.11 = (bf16[128,1024]{1,0:T(8,128)(2,1)S(1)}, bf16[128,1024]{1,0:T(8,128)(2,1)S(1)}, u32[]{:S(2)}, u32[]{:S(2)}) collective-permute-start(bf16[128,1024]{1,0:T(8,128)(2,1)S(1)} %get-tuple-element.75.out_ref.refs_4_), channel_id=1, source_target_pairs={{0,4},{1,5},{2,6},{3,7},{4,0},{5,1},{6,2},{7,3},{8,12},{9,13},{10,... | collective-permute-start | bytes 786440 | tf_op jit(solution)/shard_map/ppermute | solution.py:311
  62.0 14.4 %collective-permute-start.12 = (bf16[128,1024]{1,0:T(8,128)(2,1)S(1)}, bf16[128,1024]{1,0:T(8,128)(2,1)S(1)}, u32[]{:S(2)}, u32[]{:S(2)}) collective-permute-start(bf16[128,1024]{1,0:T(8,128)(2,1)S(1)} %get-tuple-element.75.out_ref.refs_4_), channel_id=1, source_target_pairs={{0,8},{1,9},{2,10},{3,11},{4,12},{5,13},{6,14},{7,15},{8,0},{9,1},... | collective-permute-start | bytes 786440 | tf_op jit(solution)/shard_map/ppermute | solution.py:311
  71.4 31.5 %all-to-all-start.1 = ((bf16[8,384,128]{2,1,0:T(8,128)(2,1)}), bf16[8,384,128]{2,1,0:T(8,128)(2,1)S(1)}, u32[]{:S(2)}, u32[]{:S(2)}) async-start(bf16[8,384,128]{2,1,0:T(8,128)(2,1)} %shard_map.107), calls=%async_computation.1 | async-start | bytes 1572864 | tf_op jit(solution)/shard_map/all_to_all | solution.py:392
  76.4 18.4 %collective-permute-start.13 = (bf16[128,1024]{1,0:T(8,128)(2,1)S(1)}, bf16[128,1024]{1,0:T(8,128)(2,1)S(1)}, u32[]{:S(2)}, u32[]{:S(2)}) collective-permute-start(bf16[128,1024]{1,0:T(8,128)(2,1)S(1)} %collective-permute-done.12.refs_4_), channel_id=1, source_target_pairs={{0,4},{1,5},{2,6},{3,7},{4,0},{5,1},{6,2},{7,3},{8,12},{9,13},{10,... | collective-permute-start | bytes 786440 | tf_op jit(solution)/shard_map/ppermute | solution.py:311
  77.8 11.2 %collective-permute-start.14 = (bf16[256,384]{1,0:T(8,128)(2,1)S(1)}, bf16[256,384]{1,0:T(8,128)(2,1)S(1)}, u32[]{:S(2)}, u32[]{:S(2)}) collective-permute-start(bf16[256,384]{1,0:T(8,128)(2,1)S(1)} %get-tuple-element.79), channel_id=1, source_target_pairs={{0,2},{1,3},{2,0},{3,1},{4,6},{5,7},{6,4},{7,5},{8,10},{9,11},{10,... | collective-permute-start | bytes 589832 | tf_op jit(solution)/shard_map/ppermute | solution.py:311
  95.6 5.7 %collective-permute-start.15 = (bf16[256,384]{1,0:T(8,128)(2,1)S(1)}, bf16[256,384]{1,0:T(8,128)(2,1)S(1)}, u32[]{:S(2)}, u32[]{:S(2)}) collective-permute-start(bf16[256,384]{1,0:T(8,128)(2,1)S(1)} %get-tuple-element.83), channel_id=1, source_target_pairs={{0,2},{1,3},{2,0},{3,1},{4,6},{5,7},{6,4},{7,5},{8,10},{9,11},{10,... | collective-permute-start | bytes 589832 | tf_op jit(solution)/shard_map/ppermute | solution.py:311

commit v28 on v26

--- a/solution.py
+++ b/solution.py
@@ -353,14 +353,6 @@
     row_swapped = exchange(row, cores=True)
     tok_in = lax.all_to_all(tok_out, "seq", split_axis=0, concat_axis=0, tiled=True)
 
-    probs, out_t, queries, keys_t, vals = call(
-        functools.partial(forward_kernel, chunk=chunk),
-        [shape(dims, BF16) for dims in ((total, image), (HD, image), (image, HD), (HD, total), (total, HD))],
-        [tok_in, text_head],
-        scratch=[pltpu.VMEM((total, HD), BF16), pltpu.VMEM((HD, total), BF16)],
-        flops=4 * total * image * HD,
-        moved=4 * total * image,
-    )
     columns = row.shape[1]
     mine, near, far, send = call(
         partial_kernel,
@@ -370,7 +362,15 @@
         flops=8 * image * columns * HD,
         moved=2 * image * columns,
     )
-    send, near = lax.optimization_barrier((exchange(send, 2), near))
+    send, near, tok_in = lax.optimization_barrier((exchange(send, 2), near, tok_in))
+    probs, out_t, queries, keys_t, vals = call(
+        functools.partial(forward_kernel, chunk=chunk),
+        [shape(dims, BF16) for dims in ((total, image), (HD, image), (image, HD), (HD, total), (total, HD))],
+        [tok_in, text_head],
+        scratch=[pltpu.VMEM((total, HD), BF16), pltpu.VMEM((HD, total), BF16)],
+        flops=4 * total * image * HD,
+        moved=4 * total * image,
+    )
     (far,) = call(add_kernel, [shape(far.shape, BF16)], [far, send])
     far, near = exchange(far, 4), exchange(near, 2)
     out_near, out_far = exchange(out_t, 2), exchange(out_t, 4)

time: 102 us -> 102 us (level)
  starting transfers between devices: 25.3 us -> 27.1 us
    all_to_all x1, waiting for transfers between devices: 11 us -> 0.01 us  [local(): lax.all_to_all(tok_out, 'seq', split_axis=0, concat_axis=0, tiled=True)]
    ppermute x15, waiting for transfers between devices: 39.4 us -> 49.8 us  [exchange(): return lax.ppermute(array, ('seq', 'fsdp'), pairs)]
  transfers between devices with their start and end apart: 17 -> 17, of which waited for: 10 -> 11; matrix products, arithmetic and copies ran while one was open for 1% -> 1% of each run, Pallas kernels for 16% -> 11%
where the time goes in v28:
time: 102 us
  waiting for transfers between devices  49.8 us (49%)
  starting transfers between devices  27.1 us (27%)
  Pallas kernels  16.9 us (17%)
  local copies, waits for them, and re-layouts  7.38 us (7%)
    ppermute x15, waiting for transfers between devices, exchange(): return lax.ppermute(array, ('seq', 'fsdp'), pairs)  49.8 us
    ppermute x15, starting transfers between devices, exchange(): return lax.ppermute(array, ('seq', 'fsdp'), pairs)  18.5 us
    pallas_call x9, Pallas kernels, call(): pl.pallas_call(kernel, out_shape=outs, grid_spec=pltpu.PrefetchScalarGrid...  16.9 us
    unnamed x25, local copies, waits for them, and re-layouts  6.31 us
    all_to_all x1, starting transfers between devices, local(): lax.all_to_all(grad_out, 'seq', split_axis=0, concat_axis=0, tiled=True)  4.49 us
    all_to_all x1, starting transfers between devices, local(): lax.all_to_all(tok_out, 'seq', split_axis=0, concat_axis=0, tiled=True)  4.11 us
  transfers between devices with their start and end apart: 17, of which 11 were waited for; matrix products, arithmetic and copies ran while one was open for 1% of the time, Pallas kernels for 11%

profile of v28, /device:TPU:0, one launch (start us, length us, event | category | flops | bytes accessed | tf_op | source)
XLA Modules:
  0.0 101.9 jit_solution(16142297837069812562)
XLA Ops:
  0.6 3.0 %collective-permute-start.3 = (bf16[384,1024]{1,0:T(8,128)(2,1)}, bf16[384,1024]{1,0:T(8,128)(2,1)S(1)}, u32[]{:S(2)}, u32[]{:S(2)}) collective-permute-start(bf16[384,1024]{1,0:T(8,128)(2,1)} %own_ref.1), channel_id=1, source_target_pairs={{0,2},{1,3},{2,0},{3,1},{4,6},{5,7},{6,4},{7,5},{8,10},{9,11},{10,... | collective-permute-start | bytes 2359304 | tf_op jit(solution)/shard_map/ppermute | solution.py:310
  3.7 1.1 %fusion = (bf16[64,768]{1,0:T(8,128)(2,1)S(1)}, bf16[64,768]{1,0:T(8,128)(2,1)S(1)}, bf16[64,768]{1,0:T(8,128)(2,1)S(1)}, bf16[64,768]{1,0:T(8,128)(2,1)S(1)}) fusion(bf16[128,3072]{1,0:T(8,128)(2,1)} %param.13, s32[]{:T(128)S(6)} %select_n.23, s32[]{:T(128)S(6)} %select_n.28, s32[]{:T(128)S(6)} %select_n.26, s32[]{:T(128)S(6)} %select_n.25, s32[]{:T(128)S(6)} %select_n.27), kind=kLoop, calls=%fused_computation.4 | loop fusion | bytes 786452 | tf_op jit(solution)/shard_map/dynamic_slice | solution.py:319
  4.7 3.7 %collective-permute-start.2 = (bf16[64,768]{1,0:T(8,128)(2,1)S(1)}, bf16[64,768]{1,0:T(8,128)(2,1)S(1)}, u32[]{:S(2)}, u32[]{:S(2)}) collective-permute-start(bf16[64,768]{1,0:T(8,128)(2,1)S(1)} %get-tuple-element.72), channel_id=1, source_target_pairs={{0,12},{1,13},{2,14},{3,15},{4,8},{5,9},{6,10},{7,11},{8,4},{9,5},... | collective-permute-start | bytes 294920 | tf_op jit(solution)/shard_map/ppermute | solution.py:310
  8.4 0.0 collective-permute-start
  8.4 0.8 collective-permute-start.1
  9.2 2.3 %shard_map.102 = (bf16[8,384,128]{2,1,0:T(8,128)(2,1)}, bf16[2,512,128]{2,1,0:T(8,128)(2,1)}) custom-call(s32[1]{0:T(128)} %bitcast.me_ref, bf16[128,1024]{1,0:T(8,128)(2,1)} %q_ref.1, bf16[128,1024]{1,0:T(8,128)(2,1)} %k_ref.1, bf16[128,1024]{1,0:T(8,128)(2,1)} %v_ref.1, bf16[512,1024]{1,0:T(8,128)(2,1)} %kt_ref.1, bf16[512,1024]{1,0:T(8,128)(2,1)} %vt_ref.1), custom_call_target="tpu_custom_call" | custom-call | bytes 1572864 | tf_op jit(solution)/shard_map/pallas_call | solution.py:147
  11.5 0.6 collective-permute-done.2
  12.1 2.4 %collective-permute-done = bf16[64,768]{1,0:T(8,128)(2,1)S(1)} collective-permute-done((bf16[64,768]{1,0:T(8,128)(2,1)S(1)}, bf16[64,768]{1,0:T(8,128)(2,1)S(1)}, u32[]{:S(2)}, u32[]{:S(2)}) %collective-permute-start) | collective-permute-done | bytes 98336 | tf_op jit(solution)/shard_map/ppermute | solution.py:310
  14.5 1.9 %collective-permute-done.1 = bf16[64,768]{1,0:T(8,128)(2,1)S(1)} collective-permute-done((bf16[64,768]{1,0:T(8,128)(2,1)S(1)}, bf16[64,768]{1,0:T(8,128)(2,1)S(1)}, u32[]{:S(2)}, u32[]{:S(2)}) %collective-permute-start.1) | collective-permute-done | bytes 98336 | tf_op jit(solution)/shard_map/ppermute | solution.py:310
  16.4 4.1 %all-to-all-start = ((bf16[8,384,128]{2,1,0:T(8,128)(2,1)}), bf16[8,384,128]{2,1,0:T(8,128)(2,1)S(1)}, u32[]{:S(2)}, u32[]{:S(2)}) async-start(bf16[8,384,128]{2,1,0:T(8,128)(2,1)} %get-tuple-element.50), calls=%async_computation | async-start | bytes 1572864 | tf_op jit(solution)/shard_map/all_to_all | solution.py:354
  20.5 0.9 collective-permute-done.3.other_ref
  21.4 0.9 copy-done.1
  22.4 0.1 collective-permute-start.4
  22.4 1.7 %collective-permute-done.4.swapped_ref.refs_1_ = bf16[256,768]{1,0:T(8,128)(2,1)S(1)} collective-permute-done((bf16[256,768]{1,0:T(8,128)(2,1)S(1)}, bf16[256,768]{1,0:T(8,128)(2,1)S(1)}, u32[]{:S(2)}, u32[]{:S(2)}) %collective-permute-start.4) | collective-permute-done | bytes 393248 | tf_op jit(solution)/shard_map/ppermute | solution.py:310
  24.2 1.1 %copy-done.2 = bf16[384,1024]{1,0:T(8,128)(2,1)S(1)} copy-done((bf16[384,1024]{1,0:T(8,128)(2,1)S(1)}, bf16[384,1024]{1,0:T(8,128)(2,1)}, u32[]{:S(2)}) %copy-start.2) | copy-done | bytes 786456
  25.3 1.2 %shard_map.103 = (f32[512,256]{1,0:T(8,128)S(1)}, bf16[512,256]{1,0:T(8,128)(2,1)S(1)}, f32[512,256]{1,0:T(8,128)S(1)}, bf16[512,256]{1,0:T(8,128)(2,1)S(1)}) custom-call(bf16[256,768]{1,0:T(8,128)(2,1)S(1)} %constant_dynamic-update-slice_fusion.piece_ref.refs_0_, bf16[256,768]{1,0:T(8,128)(2,1)S(1)} %collective-permute-done.4.swapped_ref.refs_1_, ...), custom_call_target="tpu_custom_call" | custom-call | flops 805306368 | bytes 1572864 | tf_op jit(solution)/shard_map/pallas_call | solution.py:147
  26.5 0.0 copy-start.8
  26.5 0.7 copy-done.8
  27.2 1.8 %collective-permute-start.5 = (bf16[512,256]{1,0:T(8,128)(2,1)S(1)}, bf16[512,256]{1,0:T(8,128)(2,1)S(1)}, u32[]{:S(2)}, u32[]{:S(2)}) collective-permute-start(bf16[512,256]{1,0:T(8,128)(2,1)S(1)} %get-tuple-element.48), channel_id=1, source_target_pairs={{0,4},{1,5},{2,6},{3,7},{4,0},{5,1},{6,2},{7,3},{8,12},{9,13},{10,... | collective-permute-start | bytes 786440 | tf_op jit(solution)/shard_map/ppermute | solution.py:310
  29.0 12.2 %collective-permute-done.5.received_ref = bf16[512,256]{1,0:T(8,128)(2,1)S(1)} collective-permute-done((bf16[512,256]{1,0:T(8,128)(2,1)S(1)}, bf16[512,256]{1,0:T(8,128)(2,1)S(1)}, u32[]{:S(2)}, u32[]{:S(2)}) %collective-permute-start.5) | collective-permute-done | bytes 262176 | tf_op jit(solution)/shard_map/ppermute | solution.py:310
  41.1 0.0 all-to-all-done.tok_ref
  41.1 0.9 copy-done.7
  42.1 4.9 %shard_map.104 = (bf16[1536,1024]{1,0:T(8,128)(2,1)S(1)}, bf16[128,1024]{1,0:T(8,128)(2,1)S(1)}, bf16[1024,128]{1,0:T(8,128)(2,1)S(1)}, bf16[128,1536]{1,0:T(8,128)(2,1)S(1)}, bf16[1536,128]{1,0:T(8,128)(2,1)S(1)}) custom-call(bf16[8,384,128]{2,1,0:T(8,128)(2,1)S(1)} %all-to-all-done.tok_ref, bf16[2,512,128]{2,1,0:T(8,128)(2,1)S(1)} %copy-done.7), custom_call_target="tpu_custom_call" | custom-call | flops 805306368 | bytes 6291456 | tf_op jit(solution)/shard_map/pallas_call | solution.py:147
  47.0 1.6 %collective-permute-start.9 = (bf16[256,768]{1,0:T(8,128)(2,1)S(1)}, bf16[256,768]{1,0:T(8,128)(2,1)S(1)}, u32[]{:S(2)}, u32[]{:S(2)}) collective-permute-start(bf16[256,768]{1,0:T(8,128)(2,1)S(1)} %constant_dynamic-update-slice_fusion.piece_ref.refs_0_), channel_id=1, source_target_pairs={{0,2},{1,3},{2,0},{3,1},{4,6},{5,7},{6,4},{7,5},{8,10},{9,11},{10,... | collective-permute-start | bytes 1179656 | tf_op jit(solution)/shard_map/ppermute | solution.py:310
  48.6 0.3 collective-permute-start.6
  49.0 4.6 %collective-permute-start.7 = (bf16[512,256]{1,0:T(8,128)(2,1)S(1)}, bf16[512,256]{1,0:T(8,128)(2,1)S(1)}, u32[]{:S(2)}, u32[]{:S(2)}) collective-permute-start(bf16[512,256]{1,0:T(8,128)(2,1)S(1)} %shard_map.105), channel_id=1, source_target_pairs={{0,8},{1,9},{2,10},{3,11},{4,12},{5,13},{6,14},{7,15},{8,0},{9,1},... | collective-permute-start | bytes 786440 | tf_op jit(solution)/shard_map/ppermute | solution.py:310
  53.6 0.0 collective-permute-start.12
  53.6 0.2 collective-permute-start.11
  53.8 10.6 %collective-permute-done.6.near_ref = bf16[512,256]{1,0:T(8,128)(2,1)S(1)} collective-permute-done((bf16[512,256]{1,0:T(8,128)(2,1)}, bf16[512,256]{1,0:T(8,128)(2,1)S(1)}, u32[]{:S(2)}, u32[]{:S(2)}) %collective-permute-start.6) | collective-permute-done | bytes 262176 | tf_op jit(solution)/shard_map/ppermute | solution.py:310
  64.4 2.2 %collective-permute-done.7.far_ref = bf16[512,256]{1,0:T(8,128)(2,1)S(1)} collective-permute-done((bf16[512,256]{1,0:T(8,128)(2,1)S(1)}, bf16[512,256]{1,0:T(8,128)(2,1)S(1)}, u32[]{:S(2)}, u32[]{:S(2)}) %collective-permute-start.7) | collective-permute-done | bytes 262176 | tf_op jit(solution)/shard_map/ppermute | solution.py:310
  66.6 0.1 shard_map.106
  66.7 0.9 collective-permute-start.8
  67.6 0.0 collective-permute-start.10
  67.6 4.1 %collective-permute-done.8.refs_1_ = bf16[512,128]{1,0:T(8,128)(2,1)S(1)} collective-permute-done((bf16[512,128]{1,0:T(8,128)(2,1)S(1)}, bf16[512,128]{1,0:T(8,128)(2,1)S(1)}, u32[]{:S(2)}, u32[]{:S(2)}) %collective-permute-start.8) | collective-permute-done | bytes 131104 | tf_op jit(solution)/shard_map/ppermute | solution.py:310
  71.7 4.4 %shard_map.107 = bf16[8,384,128]{2,1,0:T(8,128)(2,1)} custom-call(bf16[1024,128]{1,0:T(8,128)(2,1)S(1)} %get-tuple-element.53.queries_ref, bf16[128,1536]{1,0:T(8,128)(2,1)S(1)} %get-tuple-element.54.keys_t_ref, bf16[1536,128]{1,0:T(8,128)(2,1)S(1)} %get-tuple-element.55.vals_ref, bf16[1536,1024]{1,0:T(8,128)(2,1)S(1)} %get-tuple-element.56.probs_ref, ...), custom_call_target="tpu_custom_call" | custom-call | tf_op jit(solution)/shard_map/pallas_call | solution.py:147
  76.2 0.1 collective-permute-start.13
  76.3 4.5 %all-to-all-start.1 = ((bf16[8,384,128]{2,1,0:T(8,128)(2,1)}), bf16[8,384,128]{2,1,0:T(8,128)(2,1)S(1)}, u32[]{:S(2)}, u32[]{:S(2)}) async-start(bf16[8,384,128]{2,1,0:T(8,128)(2,1)} %shard_map.107), calls=%async_computation.1 | async-start | bytes 1572864 | tf_op jit(solution)/shard_map/all_to_all | solution.py:388
  80.8 3.3 %collective-permute-done.13.refs_7_ = bf16[128,1024]{1,0:T(8,128)(2,1)S(1)} collective-permute-done((bf16[128,1024]{1,0:T(8,128)(2,1)S(1)}, bf16[128,1024]{1,0:T(8,128)(2,1)S(1)}, u32[]{:S(2)}, u32[]{:S(2)}) %collective-permute-start.13) | collective-permute-done | bytes 262176 | tf_op jit(solution)/shard_map/ppermute | solution.py:310
  84.1 0.7 copy-done.9
  84.8 0.0 collective-permute-done.10.refs_3_
  84.8 0.9 copy-done.6
  85.7 0.9 copy-done.10
  86.7 1.4 %shard_map.109 = (bf16[512,384]{1,0:T(8,128)(2,1)S(1)}, bf16[512,384]{1,0:T(8,128)(2,1)S(1)}) custom-call(bf16[256,768]{1,0:T(8,128)(2,1)S(1)} %constant_dynamic-update-slice_fusion.piece_ref.refs_0_, bf16[256,768]{1,0:T(8,128)(2,1)S(1)} %copy-done.4, bf16[256,768]{1,0:T(8,128)(2,1)S(1)} %collective-permute-done.9.refs_2_, ...), custom_call_target="tpu_custom_call" | custom-call | flops 9663676416 | bytes 1572864 | tf_op jit(solution)/shard_map/pallas_call | solution.py:147
  88.1 1.3 %collective-permute-start.14 = (bf16[512,384]{1,0:T(8,128)(2,1)S(1)}, bf16[512,384]{1,0:T(8,128)(2,1)S(1)}, u32[]{:S(2)}, u32[]{:S(2)}) collective-permute-start(bf16[512,384]{1,0:T(8,128)(2,1)S(1)} %get-tuple-element.71), channel_id=1, source_target_pairs={{0,2},{1,3},{2,0},{3,1},{4,6},{5,7},{6,4},{7,5},{8,10},{9,11},{10,... | collective-permute-start | bytes 1179656 | tf_op jit(solution)/shard_map/ppermute | solution.py:310
  89.4 9.9 %collective-permute-done.14.other_ref = bf16[512,384]{1,0:T(8,128)(2,1)S(1)} collective-permute-done((bf16[512,384]{1,0:T(8,128)(2,1)S(1)}, bf16[512,384]{1,0:T(8,128)(2,1)S(1)}, u32[]{:S(2)}, u32[]{:S(2)}) %collective-permute-start.14) | collective-permute-done | bytes 393248 | tf_op jit(solution)/shard_map/ppermute | solution.py:310
  99.3 1.5 %shard_map.110 = f32[384,1024]{1,0:T(8,128)} custom-call(bf16[512,384]{1,0:T(8,128)(2,1)S(1)} %get-tuple-element.70.own_ref, bf16[512,384]{1,0:T(8,128)(2,1)S(1)} %collective-permute-done.14.other_ref), custom_call_target="tpu_custom_call" | custom-call | bytes 2359296 | tf_op jit(solution)/shard_map/pallas_call | solution.py:147
  100.8 0.0 all-to-all-done.1.tok_ref
  100.8 1.1 %shard_map.108 = (bf16[128,1024]{1,0:T(8,128)(2,1)}, bf16[128,1024]{1,0:T(8,128)(2,1)}, bf16[128,1024]{1,0:T(8,128)(2,1)}) custom-call(bf16[8,384,128]{2,1,0:T(8,128)(2,1)S(1)} %all-to-all-done.1.tok_ref), custom_call_target="tpu_custom_call" | custom-call | bytes 1572864 | tf_op jit(solution)/shard_map/pallas_call | solution.py:147
  (22 shorter events, 0.1 us)
Async XLA Ops:
  0.6 23.5 %copy-start = (bf16[384,1024]{1,0:T(8,128)(2,1)S(1)}, bf16[384,1024]{1,0:T(8,128)(2,1)}, u32[]{:S(2)}) copy-start(bf16[384,1024]{1,0:T(8,128)(2,1)} %own_ref.1) | copy-start | bytes 2359300
  0.6 20.8 %collective-permute-start.3 = (bf16[384,1024]{1,0:T(8,128)(2,1)}, bf16[384,1024]{1,0:T(8,128)(2,1)S(1)}, u32[]{:S(2)}, u32[]{:S(2)}) collective-permute-start(bf16[384,1024]{1,0:T(8,128)(2,1)} %own_ref.1), channel_id=1, source_target_pairs={{0,2},{1,3},{2,0},{3,1},{4,6},{5,7},{6,4},{7,5},{8,10},{9,11},{10,... | collective-permute-start | bytes 2359304 | tf_op jit(solution)/shard_map/ppermute | solution.py:310
  4.7 7.3 %collective-permute-start.2 = (bf16[64,768]{1,0:T(8,128)(2,1)S(1)}, bf16[64,768]{1,0:T(8,128)(2,1)S(1)}, u32[]{:S(2)}, u32[]{:S(2)}) collective-permute-start(bf16[64,768]{1,0:T(8,128)(2,1)S(1)} %get-tuple-element.72), channel_id=1, source_target_pairs={{0,12},{1,13},{2,14},{3,15},{4,8},{5,9},{6,10},{7,11},{8,4},{9,5},... | collective-permute-start | bytes 294920 | tf_op jit(solution)/shard_map/ppermute | solution.py:310
  8.4 6.1 %collective-permute-start = (bf16[64,768]{1,0:T(8,128)(2,1)S(1)}, bf16[64,768]{1,0:T(8,128)(2,1)S(1)}, u32[]{:S(2)}, u32[]{:S(2)}) collective-permute-start(bf16[64,768]{1,0:T(8,128)(2,1)S(1)} %get-tuple-element.73), channel_id=1, source_target_pairs={{0,4},{1,5},{2,6},{3,7},{4,0},{5,1},{6,2},{7,3},{8,12},{9,13},{10,... | collective-permute-start | bytes 294920 | tf_op jit(solution)/shard_map/ppermute | solution.py:310
  8.4 8.0 %collective-permute-start.1 = (bf16[64,768]{1,0:T(8,128)(2,1)S(1)}, bf16[64,768]{1,0:T(8,128)(2,1)S(1)}, u32[]{:S(2)}, u32[]{:S(2)}) collective-permute-start(bf16[64,768]{1,0:T(8,128)(2,1)S(1)} %get-tuple-element.75), channel_id=1, source_target_pairs={{0,8},{1,9},{2,10},{3,11},{4,12},{5,13},{6,14},{7,15},{8,0},{9,1},... | collective-permute-start | bytes 294920 | tf_op jit(solution)/shard_map/ppermute | solution.py:310
  16.4 24.8 %all-to-all-start = ((bf16[8,384,128]{2,1,0:T(8,128)(2,1)}), bf16[8,384,128]{2,1,0:T(8,128)(2,1)S(1)}, u32[]{:S(2)}, u32[]{:S(2)}) async-start(bf16[8,384,128]{2,1,0:T(8,128)(2,1)} %get-tuple-element.50), calls=%async_computation | async-start | bytes 1572864 | tf_op jit(solution)/shard_map/all_to_all | solution.py:354
  21.4 0.9 copy-start.1
  22.4 1.8 %collective-permute-start.4 = (bf16[256,768]{1,0:T(8,128)(2,1)S(1)}, bf16[256,768]{1,0:T(8,128)(2,1)S(1)}, u32[]{:S(2)}, u32[]{:S(2)}) collective-permute-start(bf16[256,768]{1,0:T(8,128)(2,1)S(1)} %constant_dynamic-update-slice_fusion.piece_ref.refs_0_), channel_id=1, source_target_pairs={{0,1},{1,0},{2,3},{3,2},{4,5},{5,4},{6,7},{7,6},{8,9},{9,8},{10,11... | collective-permute-start | bytes 1179656 | tf_op jit(solution)/shard_map/ppermute | solution.py:310
  24.2 1.1 %copy-start.2 = (bf16[384,1024]{1,0:T(8,128)(2,1)S(1)}, bf16[384,1024]{1,0:T(8,128)(2,1)}, u32[]{:S(2)}) copy-start(bf16[384,1024]{1,0:T(8,128)(2,1)} %copy-done.1) | copy-start | bytes 2359300
  25.3 3.7 %copy-start.3 = (bf16[256,768]{1,0:T(8,128)(2,1)}, bf16[256,768]{1,0:T(8,128)(2,1)S(1)}, u32[]{:S(2)}) copy-start(bf16[256,768]{1,0:T(8,128)(2,1)S(1)} %collective-permute-done.4.swapped_ref.refs_1_) | copy-start | bytes 1179652
  26.5 0.7 copy-start.8
  27.2 14.0 %collective-permute-start.5 = (bf16[512,256]{1,0:T(8,128)(2,1)S(1)}, bf16[512,256]{1,0:T(8,128)(2,1)S(1)}, u32[]{:S(2)}, u32[]{:S(2)}) collective-permute-start(bf16[512,256]{1,0:T(8,128)(2,1)S(1)} %get-tuple-element.48), channel_id=1, source_target_pairs={{0,4},{1,5},{2,6},{3,7},{4,0},{5,1},{6,2},{7,3},{8,12},{9,13},{10,... | collective-permute-start | bytes 786440 | tf_op jit(solution)/shard_map/ppermute | solution.py:310
  41.1 1.0 copy-start.7
  47.0 20.6 %collective-permute-start.9 = (bf16[256,768]{1,0:T(8,128)(2,1)S(1)}, bf16[256,768]{1,0:T(8,128)(2,1)S(1)}, u32[]{:S(2)}, u32[]{:S(2)}) collective-permute-start(bf16[256,768]{1,0:T(8,128)(2,1)S(1)} %constant_dynamic-update-slice_fusion.piece_ref.refs_0_), channel_id=1, source_target_pairs={{0,2},{1,3},{2,0},{3,1},{4,6},{5,7},{6,4},{7,5},{8,10},{9,11},{10,... | collective-permute-start | bytes 1179656 | tf_op jit(solution)/shard_map/ppermute | solution.py:310
  48.6 15.8 %collective-permute-start.6 = (bf16[512,256]{1,0:T(8,128)(2,1)}, bf16[512,256]{1,0:T(8,128)(2,1)S(1)}, u32[]{:S(2)}, u32[]{:S(2)}) collective-permute-start(bf16[512,256]{1,0:T(8,128)(2,1)} %copy-done.8), channel_id=1, source_target_pairs={{0,4},{1,5},{2,6},{3,7},{4,0},{5,1},{6,2},{7,3},{8,12},{9,13},{10,... | collective-permute-start | bytes 786440 | tf_op jit(solution)/shard_map/ppermute | solution.py:310
  49.0 17.6 %collective-permute-start.7 = (bf16[512,256]{1,0:T(8,128)(2,1)S(1)}, bf16[512,256]{1,0:T(8,128)(2,1)S(1)}, u32[]{:S(2)}, u32[]{:S(2)}) collective-permute-start(bf16[512,256]{1,0:T(8,128)(2,1)S(1)} %shard_map.105), channel_id=1, source_target_pairs={{0,8},{1,9},{2,10},{3,11},{4,12},{5,13},{6,14},{7,15},{8,0},{9,1},... | collective-permute-start | bytes 786440 | tf_op jit(solution)/shard_map/ppermute | solution.py:310
  53.6 22.5 %collective-permute-start.12 = (bf16[128,1024]{1,0:T(8,128)(2,1)S(1)}, bf16[128,1024]{1,0:T(8,128)(2,1)S(1)}, u32[]{:S(2)}, u32[]{:S(2)}) collective-permute-start(bf16[128,1024]{1,0:T(8,128)(2,1)S(1)} %get-tuple-element.57.out_ref.refs_4_), channel_id=1, source_target_pairs={{0,4},{1,5},{2,6},{3,7},{4,0},{5,1},{6,2},{7,3},{8,12},{9,13},{10,... | collective-permute-start | bytes 786440 | tf_op jit(solution)/shard_map/ppermute | solution.py:310
  53.6 22.5 %collective-permute-start.11 = (bf16[128,1024]{1,0:T(8,128)(2,1)S(1)}, bf16[128,1024]{1,0:T(8,128)(2,1)S(1)}, u32[]{:S(2)}, u32[]{:S(2)}) collective-permute-start(bf16[128,1024]{1,0:T(8,128)(2,1)S(1)} %get-tuple-element.57.out_ref.refs_4_), channel_id=1, source_target_pairs={{0,8},{1,9},{2,10},{3,11},{4,12},{5,13},{6,14},{7,15},{8,0},{9,1},... | collective-permute-start | bytes 786440 | tf_op jit(solution)/shard_map/ppermute | solution.py:310
  66.7 5.0 %collective-permute-start.8 = (bf16[512,128]{1,0:T(8,128)(2,1)S(1)}, bf16[512,128]{1,0:T(8,128)(2,1)S(1)}, u32[]{:S(2)}, u32[]{:S(2)}) collective-permute-start(bf16[512,128]{1,0:T(8,128)(2,1)S(1)} %get-tuple-element.63), channel_id=1, source_target_pairs={{0,2},{1,3},{2,0},{3,1},{4,6},{5,7},{6,4},{7,5},{8,10},{9,11},{10,... | collective-permute-start | bytes 393224 | tf_op jit(solution)/shard_map/ppermute | solution.py:310
  67.6 17.1 %collective-permute-start.10 = (bf16[256,768]{1,0:T(8,128)(2,1)S(1)}, bf16[256,768]{1,0:T(8,128)(2,1)S(1)}, u32[]{:S(2)}, u32[]{:S(2)}) collective-permute-start(bf16[256,768]{1,0:T(8,128)(2,1)S(1)} %collective-permute-done.9.refs_2_), channel_id=1, source_target_pairs={{0,1},{1,0},{2,3},{3,2},{4,5},{5,4},{6,7},{7,6},{8,9},{9,8},{10,11... | collective-permute-start | bytes 1179656 | tf_op jit(solution)/shard_map/ppermute | solution.py:310
  71.7 13.0 %copy-start.4 = (bf16[256,768]{1,0:T(8,128)(2,1)S(1)}, bf16[256,768]{1,0:T(8,128)(2,1)}, u32[]{:S(2)}) copy-start(bf16[256,768]{1,0:T(8,128)(2,1)} %copy-done.3) | copy-start | bytes 1179652
  76.2 7.9 %copy-start.5 = (bf16[128,1024]{1,0:T(8,128)(2,1)}, bf16[128,1024]{1,0:T(8,128)(2,1)S(1)}, u32[]{:S(2)}) copy-start(bf16[128,1024]{1,0:T(8,128)(2,1)S(1)} %collective-permute-done.11.refs_6_) | copy-start | bytes 786436
  76.2 7.9 %collective-permute-start.13 = (bf16[128,1024]{1,0:T(8,128)(2,1)S(1)}, bf16[128,1024]{1,0:T(8,128)(2,1)S(1)}, u32[]{:S(2)}, u32[]{:S(2)}) collective-permute-start(bf16[128,1024]{1,0:T(8,128)(2,1)S(1)} %collective-permute-done.11.refs_6_), channel_id=1, source_target_pairs={{0,4},{1,5},{2,6},{3,7},{4,0},{5,1},{6,2},{7,3},{8,12},{9,13},{10,... | collective-permute-start | bytes 786440 | tf_op jit(solution)/shard_map/ppermute | solution.py:310
  76.3 24.5 %all-to-all-start.1 = ((bf16[8,384,128]{2,1,0:T(8,128)(2,1)}), bf16[8,384,128]{2,1,0:T(8,128)(2,1)S(1)}, u32[]{:S(2)}, u32[]{:S(2)}) async-start(bf16[8,384,128]{2,1,0:T(8,128)(2,1)} %shard_map.107), calls=%async_computation.1 | async-start | bytes 1572864 | tf_op jit(solution)/shard_map/all_to_all | solution.py:388
  84.1 0.7 copy-start.9
  84.8 1.0 copy-start.6
  85.7 0.9 copy-start.10
  88.1 11.3 %collective-permute-start.14 = (bf16[512,384]{1,0:T(8,128)(2,1)S(1)}, bf16[512,384]{1,0:T(8,128)(2,1)S(1)}, u32[]{:S(2)}, u32[]{:S(2)}) collective-permute-start(bf16[512,384]{1,0:T(8,128)(2,1)S(1)} %get-tuple-element.71), channel_id=1, source_target_pairs={{0,2},{1,3},{2,0},{3,1},{4,6},{5,7},{6,4},{7,5},{8,10},{9,11},{10,... | collective-permute-start | bytes 1179656 | tf_op jit(solution)/shard_map/ppermute | solution.py:310

commit v29 on v26

--- a/solution.py
+++ b/solution.py
@@ -372,12 +372,12 @@
     )
     send, near = lax.optimization_barrier((exchange(send, 2), near))
     (far,) = call(add_kernel, [shape(far.shape, BF16)], [far, send])
-    far, near = exchange(far, 4), exchange(near, 2)
+    row, far = lax.optimization_barrier((row, far))
+    far, near, other_row = exchange(far, 4), exchange(near, 2), exchange(row, 1)
     out_near, out_far = exchange(out_t, 2), exchange(out_t, 4)
+    far, near, other_row = lax.optimization_barrier((far, near, other_row))
     kept, give = call(finish_kernel, [shape((image // 2, HD), BF16)] * 2, [mine, near, far])
     got = exchange(give, 1)
-    row, _ = lax.optimization_barrier((row, out_t))
-    other_row = exchange(row, 1)
     other_swapped = exchange(other_row, cores=True)
     (grad_out,) = call(
         functools.partial(backward_kernel, chunk=chunk),

time: 102 us -> 98.2 us (0.963)
  waiting for transfers between devices: 50.3 us -> 47.4 us
  local copies, waits for them, and re-layouts: 7.39 us -> 5.36 us
  starting transfers between devices: 25.3 us -> 27.1 us
    all_to_all x1, waiting for transfers between devices: 11 us -> 0.01 us  [local(): lax.all_to_all(tok_out, 'seq', split_axis=0, concat_axis=0, tiled=True)]
    ppermute x15, waiting for transfers between devices: 39.4 us -> 47.4 us  [exchange(): return lax.ppermute(array, ('seq', 'fsdp'), pairs)]
    unnamed x25 -> x19, local copies, waits for them, and re-layouts: 6.31 us -> 4.29 us
    ppermute x15, starting transfers between devices: 17.6 us -> 19 us  [exchange(): return lax.ppermute(array, ('seq', 'fsdp'), pairs)]
  transfers between devices with their start and end apart: 17 -> 17, of which waited for: 10 -> 8; matrix products, arithmetic and copies ran while one was open for 1% -> 1% of each run, Pallas kernels for 16% -> 17%
where the time goes in v29:
time: 98.2 us; the launch traced here: 97.8 us
  waiting for transfers between devices  47.4 us (48%)
  starting transfers between devices  27.1 us (28%)
  Pallas kernels  17.3 us (18%)
  local copies, waits for them, and re-layouts  5.36 us (5%)
    ppermute x15, waiting for transfers between devices, exchange(): return lax.ppermute(array, ('seq', 'fsdp'), pairs)  47.4 us
    ppermute x15, starting transfers between devices, exchange(): return lax.ppermute(array, ('seq', 'fsdp'), pairs)  19 us
    pallas_call x9, Pallas kernels, call(): pl.pallas_call(kernel, out_shape=outs, grid_spec=pltpu.PrefetchScalarGrid...  17.3 us
    unnamed x19, local copies, waits for them, and re-layouts  4.29 us
    all_to_all x1, starting transfers between devices, local(): lax.all_to_all(grad_out, 'seq', split_axis=0, concat_axis=0, tiled=True)  4.14 us
    all_to_all x1, starting transfers between devices, local(): lax.all_to_all(tok_out, 'seq', split_axis=0, concat_axis=0, tiled=True)  3.9 us
  transfers between devices with their start and end apart: 17, of which 8 were waited for; matrix products, arithmetic and copies ran while one was open for 1% of the time, Pallas kernels for 17%

profile of v29, /device:TPU:0, one launch (start us, length us, event | category | flops | bytes accessed | tf_op | source)
XLA Modules:
  0.0 97.8 jit_solution(9980241219422378138)
XLA Ops:
  0.6 3.0 %collective-permute-start.3 = (bf16[384,1024]{1,0:T(8,128)(2,1)}, bf16[384,1024]{1,0:T(8,128)(2,1)S(1)}, u32[]{:S(2)}, u32[]{:S(2)}) collective-permute-start(bf16[384,1024]{1,0:T(8,128)(2,1)} %own_ref.1), channel_id=1, source_target_pairs={{0,2},{1,3},{2,0},{3,1},{4,6},{5,7},{6,4},{7,5},{8,10},{9,11},{10,... | collective-permute-start | bytes 2359304 | tf_op jit(solution)/shard_map/ppermute | solution.py:310
  3.7 1.1 %fusion = (bf16[64,768]{1,0:T(8,128)(2,1)S(1)}, bf16[64,768]{1,0:T(8,128)(2,1)S(1)}, bf16[64,768]{1,0:T(8,128)(2,1)S(1)}, bf16[64,768]{1,0:T(8,128)(2,1)S(1)}) fusion(bf16[128,3072]{1,0:T(8,128)(2,1)} %param.13, s32[]{:T(128)S(6)} %select_n.23, s32[]{:T(128)S(6)} %select_n.28, s32[]{:T(128)S(6)} %select_n.26, s32[]{:T(128)S(6)} %select_n.25, s32[]{:T(128)S(6)} %select_n.27), kind=kLoop, calls=%fused_computation.4 | loop fusion | bytes 786452 | tf_op jit(solution)/shard_map/dynamic_slice | solution.py:319
  4.7 1.6 %collective-permute-start = (bf16[64,768]{1,0:T(8,128)(2,1)S(1)}, bf16[64,768]{1,0:T(8,128)(2,1)S(1)}, u32[]{:S(2)}, u32[]{:S(2)}) collective-permute-start(bf16[64,768]{1,0:T(8,128)(2,1)S(1)} %get-tuple-element.79), channel_id=1, source_target_pairs={{0,4},{1,5},{2,6},{3,7},{4,0},{5,1},{6,2},{7,3},{8,12},{9,13},{10,... | collective-permute-start | bytes 294920 | tf_op jit(solution)/shard_map/ppermute | solution.py:310
  6.4 2.6 %collective-permute-start.1 = (bf16[64,768]{1,0:T(8,128)(2,1)S(1)}, bf16[64,768]{1,0:T(8,128)(2,1)S(1)}, u32[]{:S(2)}, u32[]{:S(2)}) collective-permute-start(bf16[64,768]{1,0:T(8,128)(2,1)S(1)} %get-tuple-element.81), channel_id=1, source_target_pairs={{0,8},{1,9},{2,10},{3,11},{4,12},{5,13},{6,14},{7,15},{8,0},{9,1},... | collective-permute-start | bytes 294920 | tf_op jit(solution)/shard_map/ppermute | solution.py:310
  9.0 0.2 collective-permute-start.2
  9.2 2.3 %shard_map.102 = (bf16[8,384,128]{2,1,0:T(8,128)(2,1)}, bf16[2,512,128]{2,1,0:T(8,128)(2,1)}) custom-call(s32[1]{0:T(128)} %bitcast.me_ref, bf16[128,1024]{1,0:T(8,128)(2,1)} %q_ref.1, bf16[128,1024]{1,0:T(8,128)(2,1)} %k_ref.1, bf16[128,1024]{1,0:T(8,128)(2,1)} %v_ref.1, bf16[512,1024]{1,0:T(8,128)(2,1)} %kt_ref.1, bf16[512,1024]{1,0:T(8,128)(2,1)} %vt_ref.1), custom_call_target="tpu_custom_call" | custom-call | bytes 1572864 | tf_op jit(solution)/shard_map/pallas_call | solution.py:147
  11.5 0.0 collective-permute-done
  11.5 5.0 %collective-permute-done.1 = bf16[64,768]{1,0:T(8,128)(2,1)S(1)} collective-permute-done((bf16[64,768]{1,0:T(8,128)(2,1)S(1)}, bf16[64,768]{1,0:T(8,128)(2,1)S(1)}, u32[]{:S(2)}, u32[]{:S(2)}) %collective-permute-start.1) | collective-permute-done | bytes 98336 | tf_op jit(solution)/shard_map/ppermute | solution.py:310
  16.5 0.0 collective-permute-done.2
  16.5 3.9 %all-to-all-start = ((bf16[8,384,128]{2,1,0:T(8,128)(2,1)}), bf16[8,384,128]{2,1,0:T(8,128)(2,1)S(1)}, u32[]{:S(2)}, u32[]{:S(2)}) async-start(bf16[8,384,128]{2,1,0:T(8,128)(2,1)} %get-tuple-element.42), calls=%async_computation | async-start | bytes 1572864 | tf_op jit(solution)/shard_map/all_to_all | solution.py:354
  20.4 2.4 %collective-permute-done.3.other_ref = bf16[384,1024]{1,0:T(8,128)(2,1)S(1)} collective-permute-done((bf16[384,1024]{1,0:T(8,128)(2,1)}, bf16[384,1024]{1,0:T(8,128)(2,1)S(1)}, u32[]{:S(2)}, u32[]{:S(2)}) %collective-permute-start.3) | collective-permute-done | bytes 786464 | tf_op jit(solution)/shard_map/ppermute | solution.py:310
  22.9 0.1 collective-permute-start.4
  23.0 1.7 %collective-permute-done.4.swapped_ref.refs_1_ = bf16[256,768]{1,0:T(8,128)(2,1)S(1)} collective-permute-done((bf16[256,768]{1,0:T(8,128)(2,1)S(1)}, bf16[256,768]{1,0:T(8,128)(2,1)S(1)}, u32[]{:S(2)}, u32[]{:S(2)}) %collective-permute-start.4) | collective-permute-done | bytes 393248 | tf_op jit(solution)/shard_map/ppermute | solution.py:310
  24.7 1.5 %shard_map.104 = (f32[512,256]{1,0:T(8,128)S(1)}, bf16[512,256]{1,0:T(8,128)(2,1)}, f32[512,256]{1,0:T(8,128)S(1)}, bf16[512,256]{1,0:T(8,128)(2,1)S(1)}) custom-call(bf16[256,768]{1,0:T(8,128)(2,1)S(1)} %constant_dynamic-update-slice_fusion.piece_ref.refs_0_, bf16[256,768]{1,0:T(8,128)(2,1)S(1)} %collective-permute-done.4.swapped_ref.refs_1_, ...), custom_call_target="tpu_custom_call" | custom-call | flops 805306368 | bytes 1572864 | tf_op jit(solution)/shard_map/pallas_call | solution.py:147
  26.2 2.5 %collective-permute-start.5 = (bf16[512,256]{1,0:T(8,128)(2,1)S(1)}, bf16[512,256]{1,0:T(8,128)(2,1)S(1)}, u32[]{:S(2)}, u32[]{:S(2)}) collective-permute-start(bf16[512,256]{1,0:T(8,128)(2,1)S(1)} %get-tuple-element.60), channel_id=1, source_target_pairs={{0,4},{1,5},{2,6},{3,7},{4,0},{5,1},{6,2},{7,3},{8,12},{9,13},{10,... | collective-permute-start | bytes 786440 | tf_op jit(solution)/shard_map/ppermute | solution.py:310
  28.6 11.8 %collective-permute-done.5.received_ref = bf16[512,256]{1,0:T(8,128)(2,1)S(1)} collective-permute-done((bf16[512,256]{1,0:T(8,128)(2,1)S(1)}, bf16[512,256]{1,0:T(8,128)(2,1)S(1)}, u32[]{:S(2)}, u32[]{:S(2)}) %collective-permute-start.5) | collective-permute-done | bytes 262176 | tf_op jit(solution)/shard_map/ppermute | solution.py:310
  40.4 2.1 %collective-permute-start.8 = (bf16[256,768]{1,0:T(8,128)(2,1)S(1)}, bf16[256,768]{1,0:T(8,128)(2,1)S(1)}, u32[]{:S(2)}, u32[]{:S(2)}) collective-permute-start(bf16[256,768]{1,0:T(8,128)(2,1)S(1)} %constant_dynamic-update-slice_fusion.piece_ref.refs_0_), channel_id=1, source_target_pairs={{0,2},{1,3},{2,0},{3,1},{4,6},{5,7},{6,4},{7,5},{8,10},{9,11},{10,... | collective-permute-start | bytes 1179656 | tf_op jit(solution)/shard_map/ppermute | solution.py:310
  42.6 1.6 %collective-permute-start.6 = (bf16[512,256]{1,0:T(8,128)(2,1)S(1)}, bf16[512,256]{1,0:T(8,128)(2,1)S(1)}, u32[]{:S(2)}, u32[]{:S(2)}) collective-permute-start(bf16[512,256]{1,0:T(8,128)(2,1)S(1)} %shard_map.105), channel_id=1, source_target_pairs={{0,8},{1,9},{2,10},{3,11},{4,12},{5,13},{6,14},{7,15},{8,0},{9,1},... | collective-permute-start | bytes 786440 | tf_op jit(solution)/shard_map/ppermute | solution.py:310
  44.2 2.5 %collective-permute-start.7 = (bf16[512,256]{1,0:T(8,128)(2,1)}, bf16[512,256]{1,0:T(8,128)(2,1)S(1)}, u32[]{:S(2)}, u32[]{:S(2)}) collective-permute-start(bf16[512,256]{1,0:T(8,128)(2,1)} %get-tuple-element.64), channel_id=1, source_target_pairs={{0,4},{1,5},{2,6},{3,7},{4,0},{5,1},{6,2},{7,3},{8,12},{9,13},{10,... | collective-permute-start | bytes 786440 | tf_op jit(solution)/shard_map/ppermute | solution.py:310
  46.6 0.0 all-to-all-done.tok_ref
  46.6 0.9 copy-done.3
  47.6 4.9 %shard_map.103 = (bf16[1536,1024]{1,0:T(8,128)(2,1)S(1)}, bf16[128,1024]{1,0:T(8,128)(2,1)S(1)}, bf16[1024,128]{1,0:T(8,128)(2,1)S(1)}, bf16[128,1536]{1,0:T(8,128)(2,1)S(1)}, bf16[1536,128]{1,0:T(8,128)(2,1)S(1)}) custom-call(bf16[8,384,128]{2,1,0:T(8,128)(2,1)S(1)} %all-to-all-done.tok_ref, bf16[2,512,128]{2,1,0:T(8,128)(2,1)S(1)} %copy-done.3), custom_call_target="tpu_custom_call" | custom-call | flops 805306368 | bytes 6291456 | tf_op jit(solution)/shard_map/pallas_call | solution.py:147
  52.5 0.1 collective-permute-start.11
  52.6 0.9 collective-permute-start.12
  53.5 5.6 %collective-permute-done.6.far_ref = bf16[512,256]{1,0:T(8,128)(2,1)S(1)} collective-permute-done((bf16[512,256]{1,0:T(8,128)(2,1)S(1)}, bf16[512,256]{1,0:T(8,128)(2,1)S(1)}, u32[]{:S(2)}, u32[]{:S(2)}) %collective-permute-start.6) | collective-permute-done | bytes 262176 | tf_op jit(solution)/shard_map/ppermute | solution.py:310
  59.0 0.0 collective-permute-done.7.near_ref
  59.0 0.0 collective-permute-done.8.refs_2_
  59.0 0.1 shard_map.106
  59.2 0.8 collective-permute-start.9
  59.9 0.0 collective-permute-start.10
  59.9 4.3 %collective-permute-done.9.refs_1_ = bf16[512,128]{1,0:T(8,128)(2,1)S(1)} collective-permute-done((bf16[512,128]{1,0:T(8,128)(2,1)S(1)}, bf16[512,128]{1,0:T(8,128)(2,1)S(1)}, u32[]{:S(2)}, u32[]{:S(2)}) %collective-permute-start.9) | collective-permute-done | bytes 131104 | tf_op jit(solution)/shard_map/ppermute | solution.py:310
  64.2 4.5 %shard_map.107 = bf16[8,384,128]{2,1,0:T(8,128)(2,1)} custom-call(bf16[1024,128]{1,0:T(8,128)(2,1)S(1)} %get-tuple-element.44.queries_ref, bf16[128,1536]{1,0:T(8,128)(2,1)S(1)} %get-tuple-element.45.keys_t_ref, bf16[1536,128]{1,0:T(8,128)(2,1)S(1)} %get-tuple-element.46.vals_ref, bf16[1536,1024]{1,0:T(8,128)(2,1)S(1)} %get-tuple-element.47.probs_ref, ...), custom_call_target="tpu_custom_call" | custom-call | tf_op jit(solution)/shard_map/pallas_call | solution.py:147
  68.7 0.0 collective-permute-done.11.refs_6_
  68.7 0.0 collective-permute-done.12.refs_5_
  68.7 0.7 copy-done.4
  69.4 0.0 collective-permute-start.13
  69.4 4.1 %all-to-all-start.1 = ((bf16[8,384,128]{2,1,0:T(8,128)(2,1)}), bf16[8,384,128]{2,1,0:T(8,128)(2,1)S(1)}, u32[]{:S(2)}, u32[]{:S(2)}) async-start(bf16[8,384,128]{2,1,0:T(8,128)(2,1)} %shard_map.107), calls=%async_computation.1 | async-start | bytes 1572864 | tf_op jit(solution)/shard_map/all_to_all | solution.py:388
  73.5 5.1 %collective-permute-done.13.refs_7_ = bf16[128,1024]{1,0:T(8,128)(2,1)S(1)} collective-permute-done((bf16[128,1024]{1,0:T(8,128)(2,1)S(1)}, bf16[128,1024]{1,0:T(8,128)(2,1)S(1)}, u32[]{:S(2)}, u32[]{:S(2)}) %collective-permute-start.13) | collective-permute-done | bytes 262176 | tf_op jit(solution)/shard_map/ppermute | solution.py:310
  78.6 0.7 copy-done.6
  79.3 0.0 collective-permute-done.10.refs_3_
  79.3 0.9 copy-done.5
  80.3 0.9 copy-done.7
  81.2 1.4 %shard_map.109 = (bf16[512,384]{1,0:T(8,128)(2,1)S(1)}, bf16[512,384]{1,0:T(8,128)(2,1)S(1)}) custom-call(bf16[256,768]{1,0:T(8,128)(2,1)S(1)} %constant_dynamic-update-slice_fusion.piece_ref.refs_0_, bf16[256,768]{1,0:T(8,128)(2,1)S(1)} %copy-done.2, bf16[256,768]{1,0:T(8,128)(2,1)S(1)} %collective-permute-done.8.refs_2_, ...), custom_call_target="tpu_custom_call" | custom-call | flops 9663676416 | bytes 1572864 | tf_op jit(solution)/shard_map/pallas_call | solution.py:147
  82.6 1.1 %collective-permute-start.14 = (bf16[512,384]{1,0:T(8,128)(2,1)S(1)}, bf16[512,384]{1,0:T(8,128)(2,1)S(1)}, u32[]{:S(2)}, u32[]{:S(2)}) collective-permute-start(bf16[512,384]{1,0:T(8,128)(2,1)S(1)} %get-tuple-element.77), channel_id=1, source_target_pairs={{0,2},{1,3},{2,0},{3,1},{4,6},{5,7},{6,4},{7,5},{8,10},{9,11},{10,... | collective-permute-start | bytes 1179656 | tf_op jit(solution)/shard_map/ppermute | solution.py:310
  83.7 11.5 %collective-permute-done.14.other_ref = bf16[512,384]{1,0:T(8,128)(2,1)S(1)} collective-permute-done((bf16[512,384]{1,0:T(8,128)(2,1)S(1)}, bf16[512,384]{1,0:T(8,128)(2,1)S(1)}, u32[]{:S(2)}, u32[]{:S(2)}) %collective-permute-start.14) | collective-permute-done | bytes 393248 | tf_op jit(solution)/shard_map/ppermute | solution.py:310
  95.2 1.5 %shard_map.110 = f32[384,1024]{1,0:T(8,128)} custom-call(bf16[512,384]{1,0:T(8,128)(2,1)S(1)} %get-tuple-element.76.own_ref, bf16[512,384]{1,0:T(8,128)(2,1)S(1)} %collective-permute-done.14.other_ref), custom_call_target="tpu_custom_call" | custom-call | bytes 2359296 | tf_op jit(solution)/shard_map/pallas_call | solution.py:147
  96.7 0.0 all-to-all-done.1.tok_ref
  96.7 1.1 %shard_map.108 = (bf16[128,1024]{1,0:T(8,128)(2,1)}, bf16[128,1024]{1,0:T(8,128)(2,1)}, bf16[128,1024]{1,0:T(8,128)(2,1)}) custom-call(bf16[8,384,128]{2,1,0:T(8,128)(2,1)S(1)} %all-to-all-done.1.tok_ref), custom_call_target="tpu_custom_call" | custom-call | bytes 1572864 | tf_op jit(solution)/shard_map/pallas_call | solution.py:147
  (16 shorter events, 0.1 us)
Async XLA Ops:
  0.6 24.1 %copy-start = (bf16[384,1024]{1,0:T(8,128)(2,1)S(1)}, bf16[384,1024]{1,0:T(8,128)(2,1)}, u32[]{:S(2)}) copy-start(bf16[384,1024]{1,0:T(8,128)(2,1)} %own_ref.1) | copy-start | bytes 2359300
  0.6 22.2 %collective-permute-start.3 = (bf16[384,1024]{1,0:T(8,128)(2,1)}, bf16[384,1024]{1,0:T(8,128)(2,1)S(1)}, u32[]{:S(2)}, u32[]{:S(2)}) collective-permute-start(bf16[384,1024]{1,0:T(8,128)(2,1)} %own_ref.1), channel_id=1, source_target_pairs={{0,2},{1,3},{2,0},{3,1},{4,6},{5,7},{6,4},{7,5},{8,10},{9,11},{10,... | collective-permute-start | bytes 2359304 | tf_op jit(solution)/shard_map/ppermute | solution.py:310
  4.7 6.8 %collective-permute-start = (bf16[64,768]{1,0:T(8,128)(2,1)S(1)}, bf16[64,768]{1,0:T(8,128)(2,1)S(1)}, u32[]{:S(2)}, u32[]{:S(2)}) collective-permute-start(bf16[64,768]{1,0:T(8,128)(2,1)S(1)} %get-tuple-element.79), channel_id=1, source_target_pairs={{0,4},{1,5},{2,6},{3,7},{4,0},{5,1},{6,2},{7,3},{8,12},{9,13},{10,... | collective-permute-start | bytes 294920 | tf_op jit(solution)/shard_map/ppermute | solution.py:310
  6.4 10.1 %collective-permute-start.1 = (bf16[64,768]{1,0:T(8,128)(2,1)S(1)}, bf16[64,768]{1,0:T(8,128)(2,1)S(1)}, u32[]{:S(2)}, u32[]{:S(2)}) collective-permute-start(bf16[64,768]{1,0:T(8,128)(2,1)S(1)} %get-tuple-element.81), channel_id=1, source_target_pairs={{0,8},{1,9},{2,10},{3,11},{4,12},{5,13},{6,14},{7,15},{8,0},{9,1},... | collective-permute-start | bytes 294920 | tf_op jit(solution)/shard_map/ppermute | solution.py:310
  9.0 7.6 %collective-permute-start.2 = (bf16[64,768]{1,0:T(8,128)(2,1)S(1)}, bf16[64,768]{1,0:T(8,128)(2,1)S(1)}, u32[]{:S(2)}, u32[]{:S(2)}) collective-permute-start(bf16[64,768]{1,0:T(8,128)(2,1)S(1)} %get-tuple-element.78), channel_id=1, source_target_pairs={{0,12},{1,13},{2,14},{3,15},{4,8},{5,9},{6,10},{7,11},{8,4},{9,5},... | collective-permute-start | bytes 294920 | tf_op jit(solution)/shard_map/ppermute | solution.py:310
  16.5 30.1 %all-to-all-start = ((bf16[8,384,128]{2,1,0:T(8,128)(2,1)}), bf16[8,384,128]{2,1,0:T(8,128)(2,1)S(1)}, u32[]{:S(2)}, u32[]{:S(2)}) async-start(bf16[8,384,128]{2,1,0:T(8,128)(2,1)} %get-tuple-element.42), calls=%async_computation | async-start | bytes 1572864 | tf_op jit(solution)/shard_map/all_to_all | solution.py:354
  22.9 1.8 %collective-permute-start.4 = (bf16[256,768]{1,0:T(8,128)(2,1)S(1)}, bf16[256,768]{1,0:T(8,128)(2,1)S(1)}, u32[]{:S(2)}, u32[]{:S(2)}) collective-permute-start(bf16[256,768]{1,0:T(8,128)(2,1)S(1)} %constant_dynamic-update-slice_fusion.piece_ref.refs_0_), channel_id=1, source_target_pairs={{0,1},{1,0},{2,3},{3,2},{4,5},{5,4},{6,7},{7,6},{8,9},{9,8},{10,11... | collective-permute-start | bytes 1179656 | tf_op jit(solution)/shard_map/ppermute | solution.py:310
  24.7 1.5 %copy-start.1 = (bf16[256,768]{1,0:T(8,128)(2,1)}, bf16[256,768]{1,0:T(8,128)(2,1)S(1)}, u32[]{:S(2)}) copy-start(bf16[256,768]{1,0:T(8,128)(2,1)S(1)} %collective-permute-done.4.swapped_ref.refs_1_) | copy-start | bytes 1179652
  26.2 14.2 %collective-permute-start.5 = (bf16[512,256]{1,0:T(8,128)(2,1)S(1)}, bf16[512,256]{1,0:T(8,128)(2,1)S(1)}, u32[]{:S(2)}, u32[]{:S(2)}) collective-permute-start(bf16[512,256]{1,0:T(8,128)(2,1)S(1)} %get-tuple-element.60), channel_id=1, source_target_pairs={{0,4},{1,5},{2,6},{3,7},{4,0},{5,1},{6,2},{7,3},{8,12},{9,13},{10,... | collective-permute-start | bytes 786440 | tf_op jit(solution)/shard_map/ppermute | solution.py:310
  40.4 18.6 %collective-permute-start.8 = (bf16[256,768]{1,0:T(8,128)(2,1)S(1)}, bf16[256,768]{1,0:T(8,128)(2,1)S(1)}, u32[]{:S(2)}, u32[]{:S(2)}) collective-permute-start(bf16[256,768]{1,0:T(8,128)(2,1)S(1)} %constant_dynamic-update-slice_fusion.piece_ref.refs_0_), channel_id=1, source_target_pairs={{0,2},{1,3},{2,0},{3,1},{4,6},{5,7},{6,4},{7,5},{8,10},{9,11},{10,... | collective-permute-start | bytes 1179656 | tf_op jit(solution)/shard_map/ppermute | solution.py:310
  42.6 16.5 %collective-permute-start.6 = (bf16[512,256]{1,0:T(8,128)(2,1)S(1)}, bf16[512,256]{1,0:T(8,128)(2,1)S(1)}, u32[]{:S(2)}, u32[]{:S(2)}) collective-permute-start(bf16[512,256]{1,0:T(8,128)(2,1)S(1)} %shard_map.105), channel_id=1, source_target_pairs={{0,8},{1,9},{2,10},{3,11},{4,12},{5,13},{6,14},{7,15},{8,0},{9,1},... | collective-permute-start | bytes 786440 | tf_op jit(solution)/shard_map/ppermute | solution.py:310
  44.2 14.9 %collective-permute-start.7 = (bf16[512,256]{1,0:T(8,128)(2,1)}, bf16[512,256]{1,0:T(8,128)(2,1)S(1)}, u32[]{:S(2)}, u32[]{:S(2)}) collective-permute-start(bf16[512,256]{1,0:T(8,128)(2,1)} %get-tuple-element.64), channel_id=1, source_target_pairs={{0,4},{1,5},{2,6},{3,7},{4,0},{5,1},{6,2},{7,3},{8,12},{9,13},{10,... | collective-permute-start | bytes 786440 | tf_op jit(solution)/shard_map/ppermute | solution.py:310
  46.6 1.0 copy-start.3
  52.5 16.1 %collective-permute-start.11 = (bf16[128,1024]{1,0:T(8,128)(2,1)S(1)}, bf16[128,1024]{1,0:T(8,128)(2,1)S(1)}, u32[]{:S(2)}, u32[]{:S(2)}) collective-permute-start(bf16[128,1024]{1,0:T(8,128)(2,1)S(1)} %get-tuple-element.48.out_ref.refs_4_), channel_id=1, source_target_pairs={{0,8},{1,9},{2,10},{3,11},{4,12},{5,13},{6,14},{7,15},{8,0},{9,1},... | collective-permute-start | bytes 786440 | tf_op jit(solution)/shard_map/ppermute | solution.py:310
  52.6 16.1 %collective-permute-start.12 = (bf16[128,1024]{1,0:T(8,128)(2,1)S(1)}, bf16[128,1024]{1,0:T(8,128)(2,1)S(1)}, u32[]{:S(2)}, u32[]{:S(2)}) collective-permute-start(bf16[128,1024]{1,0:T(8,128)(2,1)S(1)} %get-tuple-element.48.out_ref.refs_4_), channel_id=1, source_target_pairs={{0,4},{1,5},{2,6},{3,7},{4,0},{5,1},{6,2},{7,3},{8,12},{9,13},{10,... | collective-permute-start | bytes 786440 | tf_op jit(solution)/shard_map/ppermute | solution.py:310
  59.2 5.0 %collective-permute-start.9 = (bf16[512,128]{1,0:T(8,128)(2,1)S(1)}, bf16[512,128]{1,0:T(8,128)(2,1)S(1)}, u32[]{:S(2)}, u32[]{:S(2)}) collective-permute-start(bf16[512,128]{1,0:T(8,128)(2,1)S(1)} %get-tuple-element.69), channel_id=1, source_target_pairs={{0,2},{1,3},{2,0},{3,1},{4,6},{5,7},{6,4},{7,5},{8,10},{9,11},{10,... | collective-permute-start | bytes 393224 | tf_op jit(solution)/shard_map/ppermute | solution.py:310
  59.9 19.4 %collective-permute-start.10 = (bf16[256,768]{1,0:T(8,128)(2,1)S(1)}, bf16[256,768]{1,0:T(8,128)(2,1)S(1)}, u32[]{:S(2)}, u32[]{:S(2)}) collective-permute-start(bf16[256,768]{1,0:T(8,128)(2,1)S(1)} %collective-permute-done.8.refs_2_), channel_id=1, source_target_pairs={{0,1},{1,0},{2,3},{3,2},{4,5},{5,4},{6,7},{7,6},{8,9},{9,8},{10,11... | collective-permute-start | bytes 1179656 | tf_op jit(solution)/shard_map/ppermute | solution.py:310
  64.2 15.1 %copy-start.2 = (bf16[256,768]{1,0:T(8,128)(2,1)S(1)}, bf16[256,768]{1,0:T(8,128)(2,1)}, u32[]{:S(2)}) copy-start(bf16[256,768]{1,0:T(8,128)(2,1)} %copy-done.1) | copy-start | bytes 1179652
  68.7 0.7 copy-start.4
  69.4 9.2 %collective-permute-start.13 = (bf16[128,1024]{1,0:T(8,128)(2,1)S(1)}, bf16[128,1024]{1,0:T(8,128)(2,1)S(1)}, u32[]{:S(2)}, u32[]{:S(2)}) collective-permute-start(bf16[128,1024]{1,0:T(8,128)(2,1)S(1)} %collective-permute-done.11.refs_6_), channel_id=1, source_target_pairs={{0,4},{1,5},{2,6},{3,7},{4,0},{5,1},{6,2},{7,3},{8,12},{9,13},{10,... | collective-permute-start | bytes 786440 | tf_op jit(solution)/shard_map/ppermute | solution.py:310
  69.4 27.3 %all-to-all-start.1 = ((bf16[8,384,128]{2,1,0:T(8,128)(2,1)}), bf16[8,384,128]{2,1,0:T(8,128)(2,1)S(1)}, u32[]{:S(2)}, u32[]{:S(2)}) async-start(bf16[8,384,128]{2,1,0:T(8,128)(2,1)} %shard_map.107), calls=%async_computation.1 | async-start | bytes 1572864 | tf_op jit(solution)/shard_map/all_to_all | solution.py:388
  78.6 0.7 copy-start.6
  79.3 1.0 copy-start.5
  80.3 0.9 copy-start.7
  82.6 12.6 %collective-permute-start.14 = (bf16[512,384]{1,0:T(8,128)(2,1)S(1)}, bf16[512,384]{1,0:T(8,128)(2,1)S(1)}, u32[]{:S(2)}, u32[]{:S(2)}) collective-permute-start(bf16[512,384]{1,0:T(8,128)(2,1)S(1)} %get-tuple-element.77), channel_id=1, source_target_pairs={{0,2},{1,3},{2,0},{3,1},{4,6},{5,7},{6,4},{7,5},{8,10},{9,11},{10,... | collective-permute-start | bytes 1179656 | tf_op jit(solution)/shard_map/ppermute | solution.py:310

commit v30 on v29

--- a/solution.py
+++ b/solution.py
@@ -345,7 +345,6 @@
         specs=[vmem] * 3 + [head] * 2,
         scalars=1,
         moved=4 * 3 * rows * width,
-        limit=60 * 1024 * 1024,
     )
     tok_out, along = lax.optimization_barrier((tok_out, along))
     along, given = lax.optimization_barrier((along, given))

time: 98.2 us -> 98.3 us (level)
  local copies, waits for them, and re-layouts: 5.36 us -> 10.7 us
  waiting for transfers between devices: 47.4 us -> 43.4 us
  Pallas kernels: 17.3 us -> 16 us
    unnamed x19 -> x31, local copies, waits for them, and re-layouts: 4.29 us -> 9.59 us
    ppermute x15, waiting for transfers between devices: 47.4 us -> 43.4 us  [exchange(): return lax.ppermute(array, ('seq', 'fsdp'), pairs)]
    pallas_call x9, Pallas kernels: 17.3 us -> 16 us  [call(): pl.pallas_call(kernel, out_shape=outs, grid_spec=pltpu.PrefetchScalarGrid...]
  transfers between devices with their start and end apart: 17 -> 17, of which waited for: 8 -> 9; matrix products, arithmetic and copies ran while one was open for 1% -> 1% of each run, Pallas kernels for 17% -> 15%
where the time goes in v30:
time: 98.3 us; the launch traced here: 97.8 us
  waiting for transfers between devices  43.4 us (44%)
  starting transfers between devices  26.9 us (27%)
  Pallas kernels  16 us (16%)
  local copies, waits for them, and re-layouts  10.7 us (11%)
    ppermute x15, waiting for transfers between devices, exchange(): return lax.ppermute(array, ('seq', 'fsdp'), pairs)  43.4 us
    ppermute x15, starting transfers between devices, exchange(): return lax.ppermute(array, ('seq', 'fsdp'), pairs)  18.9 us
    pallas_call x9, Pallas kernels, call(): pl.pallas_call(kernel, out_shape=outs, grid_spec=pltpu.PrefetchScalarGrid...  16 us
    unnamed x31, local copies, waits for them, and re-layouts  9.59 us
    all_to_all x1, starting transfers between devices, local(): lax.all_to_all(grad_out, 'seq', split_axis=0, concat_axis=0, tiled=True)  4.07 us
    all_to_all x1, starting transfers between devices, local(): lax.all_to_all(tok_out, 'seq', split_axis=0, concat_axis=0, tiled=True)  3.97 us
  transfers between devices with their start and end apart: 17, of which 9 were waited for; matrix products, arithmetic and copies ran while one was open for 1% of the time, Pallas kernels for 15%

profile of v30, /device:TPU:0, one launch (start us, length us, event | category | flops | bytes accessed | tf_op | source)
XLA Modules:
  0.0 97.8 jit_solution(18025746663633326706)
XLA Ops:
  0.6 3.0 %collective-permute-start.3 = (bf16[384,1024]{1,0:T(8,128)(2,1)}, bf16[384,1024]{1,0:T(8,128)(2,1)S(1)}, u32[]{:S(2)}, u32[]{:S(2)}) collective-permute-start(bf16[384,1024]{1,0:T(8,128)(2,1)} %own_ref.1), channel_id=1, source_target_pairs={{0,2},{1,3},{2,0},{3,1},{4,6},{5,7},{6,4},{7,5},{8,10},{9,11},{10,... | collective-permute-start | bytes 2359304 | tf_op jit(solution)/shard_map/ppermute | solution.py:310
  3.7 1.1 %fusion = (bf16[64,768]{1,0:T(8,128)(2,1)S(1)}, bf16[64,768]{1,0:T(8,128)(2,1)S(1)}, bf16[64,768]{1,0:T(8,128)(2,1)S(1)}, bf16[64,768]{1,0:T(8,128)(2,1)S(1)}) fusion(bf16[128,3072]{1,0:T(8,128)(2,1)} %param.13, s32[]{:T(128)S(6)} %select_n.23, s32[]{:T(128)S(6)} %select_n.28, s32[]{:T(128)S(6)} %select_n.26, s32[]{:T(128)S(6)} %select_n.25, s32[]{:T(128)S(6)} %select_n.27), kind=kLoop, calls=%fused_computation.4 | loop fusion | bytes 786452 | tf_op jit(solution)/shard_map/dynamic_slice | solution.py:319
  4.7 1.6 %collective-permute-start = (bf16[64,768]{1,0:T(8,128)(2,1)S(1)}, bf16[64,768]{1,0:T(8,128)(2,1)S(1)}, u32[]{:S(2)}, u32[]{:S(2)}) collective-permute-start(bf16[64,768]{1,0:T(8,128)(2,1)S(1)} %get-tuple-element.79), channel_id=1, source_target_pairs={{0,4},{1,5},{2,6},{3,7},{4,0},{5,1},{6,2},{7,3},{8,12},{9,13},{10,... | collective-permute-start | bytes 294920 | tf_op jit(solution)/shard_map/ppermute | solution.py:310
  6.4 2.6 %collective-permute-start.1 = (bf16[64,768]{1,0:T(8,128)(2,1)S(1)}, bf16[64,768]{1,0:T(8,128)(2,1)S(1)}, u32[]{:S(2)}, u32[]{:S(2)}) collective-permute-start(bf16[64,768]{1,0:T(8,128)(2,1)S(1)} %get-tuple-element.81), channel_id=1, source_target_pairs={{0,8},{1,9},{2,10},{3,11},{4,12},{5,13},{6,14},{7,15},{8,0},{9,1},... | collective-permute-start | bytes 294920 | tf_op jit(solution)/shard_map/ppermute | solution.py:310
  9.0 0.2 collective-permute-start.2
  9.2 1.2 %copy-done = bf16[512,1024]{1,0:T(8,128)(2,1)S(1)} copy-done((bf16[512,1024]{1,0:T(8,128)(2,1)S(1)}, bf16[512,1024]{1,0:T(8,128)(2,1)}, u32[]{:S(2)}) %copy-start) | copy-done | bytes 1048600
  10.4 1.2 %copy-done.1 = bf16[512,1024]{1,0:T(8,128)(2,1)S(1)} copy-done((bf16[512,1024]{1,0:T(8,128)(2,1)S(1)}, bf16[512,1024]{1,0:T(8,128)(2,1)}, u32[]{:S(2)}) %copy-start.1) | copy-done | bytes 1048600
  11.6 0.9 copy-done.2
  12.6 0.9 copy-done.3
  13.5 0.9 copy-done.4
  14.5 1.1 %shard_map.102 = (bf16[8,384,128]{2,1,0:T(8,128)(2,1)}, bf16[2,512,128]{2,1,0:T(8,128)(2,1)S(1)}) custom-call(s32[1]{0:T(128)} %bitcast.me_ref, bf16[128,1024]{1,0:T(8,128)(2,1)S(1)} %copy-done.2, bf16[128,1024]{1,0:T(8,128)(2,1)S(1)} %copy-done.3, bf16[128,1024]{1,0:T(8,128)(2,1)S(1)} %copy-done.4, bf16[512,1024]{1,0:T(8,128)(2,1)S(1)} %copy-done, ...), custom_call_target="tpu_custom_call" | custom-call | bytes 1572864 | tf_op jit(solution)/shard_map/pallas_call | solution.py:147
  15.6 0.0 collective-permute-done
  15.6 0.9 collective-permute-done.1
  16.5 0.0 collective-permute-done.2
  16.5 4.0 %all-to-all-start = ((bf16[8,384,128]{2,1,0:T(8,128)(2,1)}), bf16[8,384,128]{2,1,0:T(8,128)(2,1)S(1)}, u32[]{:S(2)}, u32[]{:S(2)}) async-start(bf16[8,384,128]{2,1,0:T(8,128)(2,1)} %get-tuple-element.42), calls=%async_computation | async-start | bytes 1572864 | tf_op jit(solution)/shard_map/all_to_all | solution.py:353
  20.5 2.4 %collective-permute-done.3.other_ref = bf16[384,1024]{1,0:T(8,128)(2,1)S(1)} collective-permute-done((bf16[384,1024]{1,0:T(8,128)(2,1)}, bf16[384,1024]{1,0:T(8,128)(2,1)S(1)}, u32[]{:S(2)}, u32[]{:S(2)}) %collective-permute-start.3) | collective-permute-done | bytes 786464 | tf_op jit(solution)/shard_map/ppermute | solution.py:310
  22.9 0.1 collective-permute-start.4
  23.0 1.7 %collective-permute-done.4.swapped_ref.refs_1_ = bf16[256,768]{1,0:T(8,128)(2,1)S(1)} collective-permute-done((bf16[256,768]{1,0:T(8,128)(2,1)S(1)}, bf16[256,768]{1,0:T(8,128)(2,1)S(1)}, u32[]{:S(2)}, u32[]{:S(2)}) %collective-permute-start.4) | collective-permute-done | bytes 393248 | tf_op jit(solution)/shard_map/ppermute | solution.py:310
  24.7 1.5 %shard_map.104 = (f32[512,256]{1,0:T(8,128)S(1)}, bf16[512,256]{1,0:T(8,128)(2,1)}, f32[512,256]{1,0:T(8,128)S(1)}, bf16[512,256]{1,0:T(8,128)(2,1)S(1)}) custom-call(bf16[256,768]{1,0:T(8,128)(2,1)S(1)} %constant_dynamic-update-slice_fusion.piece_ref.refs_0_, bf16[256,768]{1,0:T(8,128)(2,1)S(1)} %collective-permute-done.4.swapped_ref.refs_1_, ...), custom_call_target="tpu_custom_call" | custom-call | flops 805306368 | bytes 1572864 | tf_op jit(solution)/shard_map/pallas_call | solution.py:147
  26.2 2.5 %collective-permute-start.5 = (bf16[512,256]{1,0:T(8,128)(2,1)S(1)}, bf16[512,256]{1,0:T(8,128)(2,1)S(1)}, u32[]{:S(2)}, u32[]{:S(2)}) collective-permute-start(bf16[512,256]{1,0:T(8,128)(2,1)S(1)} %get-tuple-element.60), channel_id=1, source_target_pairs={{0,4},{1,5},{2,6},{3,7},{4,0},{5,1},{6,2},{7,3},{8,12},{9,13},{10,... | collective-permute-start | bytes 786440 | tf_op jit(solution)/shard_map/ppermute | solution.py:310
  28.6 11.8 %collective-permute-done.5.received_ref = bf16[512,256]{1,0:T(8,128)(2,1)S(1)} collective-permute-done((bf16[512,256]{1,0:T(8,128)(2,1)S(1)}, bf16[512,256]{1,0:T(8,128)(2,1)S(1)}, u32[]{:S(2)}, u32[]{:S(2)}) %collective-permute-start.5) | collective-permute-done | bytes 262176 | tf_op jit(solution)/shard_map/ppermute | solution.py:310
  40.5 2.0 %collective-permute-start.8 = (bf16[256,768]{1,0:T(8,128)(2,1)S(1)}, bf16[256,768]{1,0:T(8,128)(2,1)S(1)}, u32[]{:S(2)}, u32[]{:S(2)}) collective-permute-start(bf16[256,768]{1,0:T(8,128)(2,1)S(1)} %constant_dynamic-update-slice_fusion.piece_ref.refs_0_), channel_id=1, source_target_pairs={{0,2},{1,3},{2,0},{3,1},{4,6},{5,7},{6,4},{7,5},{8,10},{9,11},{10,... | collective-permute-start | bytes 1179656 | tf_op jit(solution)/shard_map/ppermute | solution.py:310
  42.6 1.6 %collective-permute-start.6 = (bf16[512,256]{1,0:T(8,128)(2,1)S(1)}, bf16[512,256]{1,0:T(8,128)(2,1)S(1)}, u32[]{:S(2)}, u32[]{:S(2)}) collective-permute-start(bf16[512,256]{1,0:T(8,128)(2,1)S(1)} %shard_map.105), channel_id=1, source_target_pairs={{0,8},{1,9},{2,10},{3,11},{4,12},{5,13},{6,14},{7,15},{8,0},{9,1},... | collective-permute-start | bytes 786440 | tf_op jit(solution)/shard_map/ppermute | solution.py:310
  44.2 2.5 %collective-permute-start.7 = (bf16[512,256]{1,0:T(8,128)(2,1)}, bf16[512,256]{1,0:T(8,128)(2,1)S(1)}, u32[]{:S(2)}, u32[]{:S(2)}) collective-permute-start(bf16[512,256]{1,0:T(8,128)(2,1)} %get-tuple-element.64), channel_id=1, source_target_pairs={{0,4},{1,5},{2,6},{3,7},{4,0},{5,1},{6,2},{7,3},{8,12},{9,13},{10,... | collective-permute-start | bytes 786440 | tf_op jit(solution)/shard_map/ppermute | solution.py:310
  46.7 0.0 all-to-all-done.tok_ref
  46.7 0.9 copy-done.9
  47.6 4.9 %shard_map.103 = (bf16[1536,1024]{1,0:T(8,128)(2,1)S(1)}, bf16[128,1024]{1,0:T(8,128)(2,1)S(1)}, bf16[1024,128]{1,0:T(8,128)(2,1)S(1)}, bf16[128,1536]{1,0:T(8,128)(2,1)S(1)}, bf16[1536,128]{1,0:T(8,128)(2,1)S(1)}) custom-call(bf16[8,384,128]{2,1,0:T(8,128)(2,1)S(1)} %all-to-all-done.tok_ref, bf16[2,512,128]{2,1,0:T(8,128)(2,1)S(1)} %copy-done.9), custom_call_target="tpu_custom_call" | custom-call | flops 805306368 | bytes 6291456 | tf_op jit(solution)/shard_map/pallas_call | solution.py:147
  52.5 0.1 collective-permute-start.11
  52.6 0.9 collective-permute-start.12
  53.5 5.6 %collective-permute-done.6.far_ref = bf16[512,256]{1,0:T(8,128)(2,1)S(1)} collective-permute-done((bf16[512,256]{1,0:T(8,128)(2,1)S(1)}, bf16[512,256]{1,0:T(8,128)(2,1)S(1)}, u32[]{:S(2)}, u32[]{:S(2)}) %collective-permute-start.6) | collective-permute-done | bytes 262176 | tf_op jit(solution)/shard_map/ppermute | solution.py:310
  59.0 0.0 collective-permute-done.7.near_ref
  59.0 0.1 shard_map.106
  59.2 0.7 collective-permute-start.9
  59.9 4.3 %collective-permute-done.9.refs_1_ = bf16[512,128]{1,0:T(8,128)(2,1)S(1)} collective-permute-done((bf16[512,128]{1,0:T(8,128)(2,1)S(1)}, bf16[512,128]{1,0:T(8,128)(2,1)S(1)}, u32[]{:S(2)}, u32[]{:S(2)}) %collective-permute-start.9) | collective-permute-done | bytes 131104 | tf_op jit(solution)/shard_map/ppermute | solution.py:310
  64.2 4.4 %shard_map.107 = bf16[8,384,128]{2,1,0:T(8,128)(2,1)} custom-call(bf16[1024,128]{1,0:T(8,128)(2,1)S(1)} %get-tuple-element.44.queries_ref, bf16[128,1536]{1,0:T(8,128)(2,1)S(1)} %get-tuple-element.45.keys_t_ref, bf16[1536,128]{1,0:T(8,128)(2,1)S(1)} %get-tuple-element.46.vals_ref, bf16[1536,1024]{1,0:T(8,128)(2,1)S(1)} %get-tuple-element.47.probs_ref, ...), custom_call_target="tpu_custom_call" | custom-call | tf_op jit(solution)/shard_map/pallas_call | solution.py:147
  68.6 0.0 collective-permute-done.11.refs_6_
  68.6 0.1 collective-permute-done.12.refs_5_
  68.7 0.7 copy-done.10
  69.4 4.1 %all-to-all-start.1 = ((bf16[8,384,128]{2,1,0:T(8,128)(2,1)}), bf16[8,384,128]{2,1,0:T(8,128)(2,1)S(1)}, u32[]{:S(2)}, u32[]{:S(2)}) async-start(bf16[8,384,128]{2,1,0:T(8,128)(2,1)} %shard_map.107), calls=%async_computation.1 | async-start | bytes 1572864 | tf_op jit(solution)/shard_map/all_to_all | solution.py:387
  73.5 5.1 %collective-permute-done.13.refs_7_ = bf16[128,1024]{1,0:T(8,128)(2,1)S(1)} collective-permute-done((bf16[128,1024]{1,0:T(8,128)(2,1)S(1)}, bf16[128,1024]{1,0:T(8,128)(2,1)S(1)}, u32[]{:S(2)}, u32[]{:S(2)}) %collective-permute-start.13) | collective-permute-done | bytes 262176 | tf_op jit(solution)/shard_map/ppermute | solution.py:310
  78.6 0.7 copy-done.12
  79.3 0.9 copy-done.11
  80.3 0.9 copy-done.13
  81.2 1.4 %shard_map.109 = (bf16[512,384]{1,0:T(8,128)(2,1)S(1)}, bf16[512,384]{1,0:T(8,128)(2,1)S(1)}) custom-call(bf16[256,768]{1,0:T(8,128)(2,1)S(1)} %constant_dynamic-update-slice_fusion.piece_ref.refs_0_, bf16[256,768]{1,0:T(8,128)(2,1)S(1)} %copy-done.7, bf16[256,768]{1,0:T(8,128)(2,1)S(1)} %collective-permute-done.8.refs_2_, ...), custom_call_target="tpu_custom_call" | custom-call | flops 9663676416 | bytes 1572864 | tf_op jit(solution)/shard_map/pallas_call | solution.py:147
  82.6 1.1 %collective-permute-start.14 = (bf16[512,384]{1,0:T(8,128)(2,1)S(1)}, bf16[512,384]{1,0:T(8,128)(2,1)S(1)}, u32[]{:S(2)}, u32[]{:S(2)}) collective-permute-start(bf16[512,384]{1,0:T(8,128)(2,1)S(1)} %get-tuple-element.77), channel_id=1, source_target_pairs={{0,2},{1,3},{2,0},{3,1},{4,6},{5,7},{6,4},{7,5},{8,10},{9,11},{10,... | collective-permute-start | bytes 1179656 | tf_op jit(solution)/shard_map/ppermute | solution.py:310
  83.7 11.5 %collective-permute-done.14.other_ref = bf16[512,384]{1,0:T(8,128)(2,1)S(1)} collective-permute-done((bf16[512,384]{1,0:T(8,128)(2,1)S(1)}, bf16[512,384]{1,0:T(8,128)(2,1)S(1)}, u32[]{:S(2)}, u32[]{:S(2)}) %collective-permute-start.14) | collective-permute-done | bytes 393248 | tf_op jit(solution)/shard_map/ppermute | solution.py:310
  95.2 1.5 %shard_map.110 = f32[384,1024]{1,0:T(8,128)} custom-call(bf16[512,384]{1,0:T(8,128)(2,1)S(1)} %get-tuple-element.76.own_ref, bf16[512,384]{1,0:T(8,128)(2,1)S(1)} %collective-permute-done.14.other_ref), custom_call_target="tpu_custom_call" | custom-call | bytes 2359296 | tf_op jit(solution)/shard_map/pallas_call | solution.py:147
  96.7 1.1 %shard_map.108 = (bf16[128,1024]{1,0:T(8,128)(2,1)}, bf16[128,1024]{1,0:T(8,128)(2,1)}, bf16[128,1024]{1,0:T(8,128)(2,1)}) custom-call(bf16[8,384,128]{2,1,0:T(8,128)(2,1)S(1)} %all-to-all-done.1.tok_ref), custom_call_target="tpu_custom_call" | custom-call | bytes 1572864 | tf_op jit(solution)/shard_map/pallas_call | solution.py:147
  (28 shorter events, 0.1 us)
Async XLA Ops:
  0.6 24.1 %copy-start.5 = (bf16[384,1024]{1,0:T(8,128)(2,1)S(1)}, bf16[384,1024]{1,0:T(8,128)(2,1)}, u32[]{:S(2)}) copy-start(bf16[384,1024]{1,0:T(8,128)(2,1)} %own_ref.1) | copy-start | bytes 2359300
  0.6 22.2 %collective-permute-start.3 = (bf16[384,1024]{1,0:T(8,128)(2,1)}, bf16[384,1024]{1,0:T(8,128)(2,1)S(1)}, u32[]{:S(2)}, u32[]{:S(2)}) collective-permute-start(bf16[384,1024]{1,0:T(8,128)(2,1)} %own_ref.1), channel_id=1, source_target_pairs={{0,2},{1,3},{2,0},{3,1},{4,6},{5,7},{6,4},{7,5},{8,10},{9,11},{10,... | collective-permute-start | bytes 2359304 | tf_op jit(solution)/shard_map/ppermute | solution.py:310
  4.7 10.9 %collective-permute-start = (bf16[64,768]{1,0:T(8,128)(2,1)S(1)}, bf16[64,768]{1,0:T(8,128)(2,1)S(1)}, u32[]{:S(2)}, u32[]{:S(2)}) collective-permute-start(bf16[64,768]{1,0:T(8,128)(2,1)S(1)} %get-tuple-element.79), channel_id=1, source_target_pairs={{0,4},{1,5},{2,6},{3,7},{4,0},{5,1},{6,2},{7,3},{8,12},{9,13},{10,... | collective-permute-start | bytes 294920 | tf_op jit(solution)/shard_map/ppermute | solution.py:310
  6.4 10.1 %collective-permute-start.1 = (bf16[64,768]{1,0:T(8,128)(2,1)S(1)}, bf16[64,768]{1,0:T(8,128)(2,1)S(1)}, u32[]{:S(2)}, u32[]{:S(2)}) collective-permute-start(bf16[64,768]{1,0:T(8,128)(2,1)S(1)} %get-tuple-element.81), channel_id=1, source_target_pairs={{0,8},{1,9},{2,10},{3,11},{4,12},{5,13},{6,14},{7,15},{8,0},{9,1},... | collective-permute-start | bytes 294920 | tf_op jit(solution)/shard_map/ppermute | solution.py:310
  9.0 7.6 %collective-permute-start.2 = (bf16[64,768]{1,0:T(8,128)(2,1)S(1)}, bf16[64,768]{1,0:T(8,128)(2,1)S(1)}, u32[]{:S(2)}, u32[]{:S(2)}) collective-permute-start(bf16[64,768]{1,0:T(8,128)(2,1)S(1)} %get-tuple-element.78), channel_id=1, source_target_pairs={{0,12},{1,13},{2,14},{3,15},{4,8},{5,9},{6,10},{7,11},{8,4},{9,5},... | collective-permute-start | bytes 294920 | tf_op jit(solution)/shard_map/ppermute | solution.py:310
  9.2 1.2 %copy-start = (bf16[512,1024]{1,0:T(8,128)(2,1)S(1)}, bf16[512,1024]{1,0:T(8,128)(2,1)}, u32[]{:S(2)}) copy-start(bf16[512,1024]{1,0:T(8,128)(2,1)} %kt_ref.1) | copy-start | bytes 3145732
  10.4 1.2 %copy-start.1 = (bf16[512,1024]{1,0:T(8,128)(2,1)S(1)}, bf16[512,1024]{1,0:T(8,128)(2,1)}, u32[]{:S(2)}) copy-start(bf16[512,1024]{1,0:T(8,128)(2,1)} %vt_ref.1) | copy-start | bytes 3145732
  11.6 0.9 copy-start.2
  12.6 0.9 copy-start.3
  13.5 0.9 copy-start.4
  15.6 24.9 %copy-start.8 = (bf16[2,512,128]{2,1,0:T(8,128)(2,1)}, bf16[2,512,128]{2,1,0:T(8,128)(2,1)S(1)}, u32[]{:S(2)}) copy-start(bf16[2,512,128]{2,1,0:T(8,128)(2,1)S(1)} %get-tuple-element.43.text_ref) | copy-start | bytes 786436
  16.5 30.1 %all-to-all-start = ((bf16[8,384,128]{2,1,0:T(8,128)(2,1)}), bf16[8,384,128]{2,1,0:T(8,128)(2,1)S(1)}, u32[]{:S(2)}, u32[]{:S(2)}) async-start(bf16[8,384,128]{2,1,0:T(8,128)(2,1)} %get-tuple-element.42), calls=%async_computation | async-start | bytes 1572864 | tf_op jit(solution)/shard_map/all_to_all | solution.py:353
  22.9 1.8 %collective-permute-start.4 = (bf16[256,768]{1,0:T(8,128)(2,1)S(1)}, bf16[256,768]{1,0:T(8,128)(2,1)S(1)}, u32[]{:S(2)}, u32[]{:S(2)}) collective-permute-start(bf16[256,768]{1,0:T(8,128)(2,1)S(1)} %constant_dynamic-update-slice_fusion.piece_ref.refs_0_), channel_id=1, source_target_pairs={{0,1},{1,0},{2,3},{3,2},{4,5},{5,4},{6,7},{7,6},{8,9},{9,8},{10,11... | collective-permute-start | bytes 1179656 | tf_op jit(solution)/shard_map/ppermute | solution.py:310
  24.7 1.5 %copy-start.6 = (bf16[256,768]{1,0:T(8,128)(2,1)}, bf16[256,768]{1,0:T(8,128)(2,1)S(1)}, u32[]{:S(2)}) copy-start(bf16[256,768]{1,0:T(8,128)(2,1)S(1)} %collective-permute-done.4.swapped_ref.refs_1_) | copy-start | bytes 1179652
  26.2 14.3 %collective-permute-start.5 = (bf16[512,256]{1,0:T(8,128)(2,1)S(1)}, bf16[512,256]{1,0:T(8,128)(2,1)S(1)}, u32[]{:S(2)}, u32[]{:S(2)}) collective-permute-start(bf16[512,256]{1,0:T(8,128)(2,1)S(1)} %get-tuple-element.60), channel_id=1, source_target_pairs={{0,4},{1,5},{2,6},{3,7},{4,0},{5,1},{6,2},{7,3},{8,12},{9,13},{10,... | collective-permute-start | bytes 786440 | tf_op jit(solution)/shard_map/ppermute | solution.py:310
  40.5 18.5 %collective-permute-start.8 = (bf16[256,768]{1,0:T(8,128)(2,1)S(1)}, bf16[256,768]{1,0:T(8,128)(2,1)S(1)}, u32[]{:S(2)}, u32[]{:S(2)}) collective-permute-start(bf16[256,768]{1,0:T(8,128)(2,1)S(1)} %constant_dynamic-update-slice_fusion.piece_ref.refs_0_), channel_id=1, source_target_pairs={{0,2},{1,3},{2,0},{3,1},{4,6},{5,7},{6,4},{7,5},{8,10},{9,11},{10,... | collective-permute-start | bytes 1179656 | tf_op jit(solution)/shard_map/ppermute | solution.py:310
  42.6 16.5 %collective-permute-start.6 = (bf16[512,256]{1,0:T(8,128)(2,1)S(1)}, bf16[512,256]{1,0:T(8,128)(2,1)S(1)}, u32[]{:S(2)}, u32[]{:S(2)}) collective-permute-start(bf16[512,256]{1,0:T(8,128)(2,1)S(1)} %shard_map.105), channel_id=1, source_target_pairs={{0,8},{1,9},{2,10},{3,11},{4,12},{5,13},{6,14},{7,15},{8,0},{9,1},... | collective-permute-start | bytes 786440 | tf_op jit(solution)/shard_map/ppermute | solution.py:310
  44.2 14.9 %collective-permute-start.7 = (bf16[512,256]{1,0:T(8,128)(2,1)}, bf16[512,256]{1,0:T(8,128)(2,1)S(1)}, u32[]{:S(2)}, u32[]{:S(2)}) collective-permute-start(bf16[512,256]{1,0:T(8,128)(2,1)} %get-tuple-element.64), channel_id=1, source_target_pairs={{0,4},{1,5},{2,6},{3,7},{4,0},{5,1},{6,2},{7,3},{8,12},{9,13},{10,... | collective-permute-start | bytes 786440 | tf_op jit(solution)/shard_map/ppermute | solution.py:310
  46.7 1.0 copy-start.9
  52.5 16.1 %collective-permute-start.11 = (bf16[128,1024]{1,0:T(8,128)(2,1)S(1)}, bf16[128,1024]{1,0:T(8,128)(2,1)S(1)}, u32[]{:S(2)}, u32[]{:S(2)}) collective-permute-start(bf16[128,1024]{1,0:T(8,128)(2,1)S(1)} %get-tuple-element.48.out_ref.refs_4_), channel_id=1, source_target_pairs={{0,8},{1,9},{2,10},{3,11},{4,12},{5,13},{6,14},{7,15},{8,0},{9,1},... | collective-permute-start | bytes 786440 | tf_op jit(solution)/shard_map/ppermute | solution.py:310
  52.6 16.1 %collective-permute-start.12 = (bf16[128,1024]{1,0:T(8,128)(2,1)S(1)}, bf16[128,1024]{1,0:T(8,128)(2,1)S(1)}, u32[]{:S(2)}, u32[]{:S(2)}) collective-permute-start(bf16[128,1024]{1,0:T(8,128)(2,1)S(1)} %get-tuple-element.48.out_ref.refs_4_), channel_id=1, source_target_pairs={{0,4},{1,5},{2,6},{3,7},{4,0},{5,1},{6,2},{7,3},{8,12},{9,13},{10,... | collective-permute-start | bytes 786440 | tf_op jit(solution)/shard_map/ppermute | solution.py:310
  59.2 5.0 %collective-permute-start.9 = (bf16[512,128]{1,0:T(8,128)(2,1)S(1)}, bf16[512,128]{1,0:T(8,128)(2,1)S(1)}, u32[]{:S(2)}, u32[]{:S(2)}) collective-permute-start(bf16[512,128]{1,0:T(8,128)(2,1)S(1)} %get-tuple-element.69), channel_id=1, source_target_pairs={{0,2},{1,3},{2,0},{3,1},{4,6},{5,7},{6,4},{7,5},{8,10},{9,11},{10,... | collective-permute-start | bytes 393224 | tf_op jit(solution)/shard_map/ppermute | solution.py:310
  59.9 19.4 %collective-permute-start.10 = (bf16[256,768]{1,0:T(8,128)(2,1)S(1)}, bf16[256,768]{1,0:T(8,128)(2,1)S(1)}, u32[]{:S(2)}, u32[]{:S(2)}) collective-permute-start(bf16[256,768]{1,0:T(8,128)(2,1)S(1)} %collective-permute-done.8.refs_2_), channel_id=1, source_target_pairs={{0,1},{1,0},{2,3},{3,2},{4,5},{5,4},{6,7},{7,6},{8,9},{9,8},{10,11... | collective-permute-start | bytes 1179656 | tf_op jit(solution)/shard_map/ppermute | solution.py:310
  64.2 15.1 %copy-start.7 = (bf16[256,768]{1,0:T(8,128)(2,1)S(1)}, bf16[256,768]{1,0:T(8,128)(2,1)}, u32[]{:S(2)}) copy-start(bf16[256,768]{1,0:T(8,128)(2,1)} %copy-done.6) | copy-start | bytes 1179652
  68.7 0.7 copy-start.10
  69.4 9.2 %collective-permute-start.13 = (bf16[128,1024]{1,0:T(8,128)(2,1)S(1)}, bf16[128,1024]{1,0:T(8,128)(2,1)S(1)}, u32[]{:S(2)}, u32[]{:S(2)}) collective-permute-start(bf16[128,1024]{1,0:T(8,128)(2,1)S(1)} %collective-permute-done.11.refs_6_), channel_id=1, source_target_pairs={{0,4},{1,5},{2,6},{3,7},{4,0},{5,1},{6,2},{7,3},{8,12},{9,13},{10,... | collective-permute-start | bytes 786440 | tf_op jit(solution)/shard_map/ppermute | solution.py:310
  69.4 27.3 %all-to-all-start.1 = ((bf16[8,384,128]{2,1,0:T(8,128)(2,1)}), bf16[8,384,128]{2,1,0:T(8,128)(2,1)S(1)}, u32[]{:S(2)}, u32[]{:S(2)}) async-start(bf16[8,384,128]{2,1,0:T(8,128)(2,1)} %shard_map.107), calls=%async_computation.1 | async-start | bytes 1572864 | tf_op jit(solution)/shard_map/all_to_all | solution.py:387
  78.6 0.7 copy-start.12
  79.3 1.0 copy-start.11
  80.3 0.9 copy-start.13
  82.6 12.6 %collective-permute-start.14 = (bf16[512,384]{1,0:T(8,128)(2,1)S(1)}, bf16[512,384]{1,0:T(8,128)(2,1)S(1)}, u32[]{:S(2)}, u32[]{:S(2)}) collective-permute-start(bf16[512,384]{1,0:T(8,128)(2,1)S(1)} %get-tuple-element.77), channel_id=1, source_target_pairs={{0,2},{1,3},{2,0},{3,1},{4,6},{5,7},{6,4},{7,5},{8,10},{9,11},{10,... | collective-permute-start | bytes 1179656 | tf_op jit(solution)/shard_map/ppermute | solution.py:310

commit v31 on v24

--- a/solution.py
+++ b/solution.py
@@ -388,31 +388,26 @@
     )
     send, near = lax.optimization_barrier((exchange(send, 2), near))
     (far,) = call(add_kernel, [shape(far.shape, BF16)], [far, send])
-    far, near = exchange(far, 4), exchange(near, 2)
-    out_late, far, near = lax.optimization_barrier((out_t, far, near))
+    row, far = lax.optimization_barrier((row, far))
+    far, near, other_row = exchange(far, 4), exchange(near, 2), exchange(row, 1)
+    out_near, out_far = exchange(out_t, 2), exchange(out_t, 4)
+    far, near, other_row = lax.optimization_barrier((far, near, other_row))
     kept, give = call(finish_kernel, [shape((image // 2, HD), BF16)] * 2, [mine, near, far])
     got = exchange(give, 1)
-    out_near, out_far = exchange(out_late, 2), exchange(out_late, 4)
-    row, got = lax.optimization_barrier((row, got))
-    other_row = exchange(row, 1)
     other_swapped = exchange(other_row, cores=True)
     dq, dk, dv = call(
         functools.partial(backward_first_kernel, chunk=chunk),
         [shape((image // 2, HD), BF16)] + [shape((image, HD), F32)] * 2,
         [queries, keys_t, vals, probs, out_t, kept],
-        flops=4 * total * image * HD,
-        moved=2 * total * image,
     )
     (grad_out,) = call(
         functools.partial(backward_second_kernel, chunk=chunk),
         [shape((n, 3 * rows, HD), BF16)],
         [queries, keys_t, vals, probs, out_t, got, dq, dk, dv],
         scratch=[pltpu.VMEM((image // 2, HD), BF16)] + [pltpu.VMEM((image, HD), F32)] * 2,
-        flops=4 * total * image * HD,
-        moved=2 * total * image,
     )
     grad_in = lax.all_to_all(grad_out, "seq", split_axis=0, concat_axis=0, tiled=True)
-    out_far, out_near, other_row, _ = lax.optimization_barrier((out_far, out_near, other_row, grad_out))
+    out_far, out_near, _ = lax.optimization_barrier((out_far, out_near, grad_out))
     outs = [out_t, out_near, out_far, exchange(out_far, 2)]
     dw_own, dw_other = call(
         weight_grad_kernel,

time: 104 us -> 98.2 us (0.944)
  starting transfers between devices: 32.2 us -> 26.8 us
  waiting for transfers between devices: 51.8 us -> 47.5 us
  local copies, waits for them, and re-layouts: 2.06 us -> 5.36 us
    ppermute x15, starting transfers between devices: 23.8 us -> 19 us  [exchange(): return lax.ppermute(array, ('seq', 'fsdp'), pairs)]
    ppermute x15, waiting for transfers between devices: 51.8 us -> 47.5 us  [exchange(): return lax.ppermute(array, ('seq', 'fsdp'), pairs)]
    unnamed x11 -> x19, local copies, waits for them, and re-layouts: 0.99 us -> 4.29 us
  transfers between devices with their start and end apart: 17 -> 17, of which waited for: 11 -> 10; matrix products, arithmetic and copies ran while one was open for 1% -> 1% of each run, Pallas kernels for 16% -> 17%
where the time goes in v31:
time: 98.2 us; the launch traced here: 97.8 us
  waiting for transfers between devices  47.5 us (48%)
  starting transfers between devices  26.8 us (27%)
  Pallas kernels  17.4 us (18%)
  local copies, waits for them, and re-layouts  5.36 us (5%)
    ppermute x15, waiting for transfers between devices, exchange(): return lax.ppermute(array, ('seq', 'fsdp'), pairs)  47.5 us
    ppermute x15, starting transfers between devices, exchange(): return lax.ppermute(array, ('seq', 'fsdp'), pairs)  19 us
    pallas_call x10, Pallas kernels, call(): pl.pallas_call(kernel, out_shape=outs, grid_spec=pltpu.PrefetchScalarGrid...  17.4 us
    unnamed x19, local copies, waits for them, and re-layouts  4.29 us
    all_to_all x1, starting transfers between devices, local(): lax.all_to_all(tok_out, 'seq', split_axis=0, concat_axis=0, tiled=True)  3.9 us
    all_to_all x1, starting transfers between devices, local(): lax.all_to_all(grad_out, 'seq', split_axis=0, concat_axis=0, tiled=True)  3.89 us
  transfers between devices with their start and end apart: 17, of which 10 were waited for; matrix products, arithmetic and copies ran while one was open for 1% of the time, Pallas kernels for 17%

profile of v31, /device:TPU:0, one launch (start us, length us, event | category | flops | bytes accessed | tf_op | source)
XLA Modules:
  0.0 97.8 jit_solution(3179528346465835572)
XLA Ops:
  0.6 3.0 %collective-permute-start.3 = (bf16[384,1024]{1,0:T(8,128)(2,1)}, bf16[384,1024]{1,0:T(8,128)(2,1)S(1)}, u32[]{:S(2)}, u32[]{:S(2)}) collective-permute-start(bf16[384,1024]{1,0:T(8,128)(2,1)} %own_ref.1), channel_id=1, source_target_pairs={{0,2},{1,3},{2,0},{3,1},{4,6},{5,7},{6,4},{7,5},{8,10},{9,11},{10,... | collective-permute-start | bytes 2359304 | tf_op jit(solution)/shard_map/ppermute | solution.py:326
  3.7 1.1 %fusion = (bf16[64,768]{1,0:T(8,128)(2,1)S(1)}, bf16[64,768]{1,0:T(8,128)(2,1)S(1)}, bf16[64,768]{1,0:T(8,128)(2,1)S(1)}, bf16[64,768]{1,0:T(8,128)(2,1)S(1)}) fusion(bf16[128,3072]{1,0:T(8,128)(2,1)} %param.13, s32[]{:T(128)S(6)} %select_n.23, s32[]{:T(128)S(6)} %select_n.28, s32[]{:T(128)S(6)} %select_n.26, s32[]{:T(128)S(6)} %select_n.25, s32[]{:T(128)S(6)} %select_n.27), kind=kLoop, calls=%fused_computation.4 | loop fusion | bytes 786452 | tf_op jit(solution)/shard_map/dynamic_slice | solution.py:335
  4.7 1.6 %collective-permute-start = (bf16[64,768]{1,0:T(8,128)(2,1)S(1)}, bf16[64,768]{1,0:T(8,128)(2,1)S(1)}, u32[]{:S(2)}, u32[]{:S(2)}) collective-permute-start(bf16[64,768]{1,0:T(8,128)(2,1)S(1)} %get-tuple-element.85), channel_id=1, source_target_pairs={{0,4},{1,5},{2,6},{3,7},{4,0},{5,1},{6,2},{7,3},{8,12},{9,13},{10,... | collective-permute-start | bytes 294920 | tf_op jit(solution)/shard_map/ppermute | solution.py:326
  6.4 2.6 %collective-permute-start.1 = (bf16[64,768]{1,0:T(8,128)(2,1)S(1)}, bf16[64,768]{1,0:T(8,128)(2,1)S(1)}, u32[]{:S(2)}, u32[]{:S(2)}) collective-permute-start(bf16[64,768]{1,0:T(8,128)(2,1)S(1)} %get-tuple-element.87), channel_id=1, source_target_pairs={{0,8},{1,9},{2,10},{3,11},{4,12},{5,13},{6,14},{7,15},{8,0},{9,1},... | collective-permute-start | bytes 294920 | tf_op jit(solution)/shard_map/ppermute | solution.py:326
  9.0 0.2 collective-permute-start.2
  9.2 2.3 %shard_map.102 = (bf16[8,384,128]{2,1,0:T(8,128)(2,1)}, bf16[2,512,128]{2,1,0:T(8,128)(2,1)}) custom-call(s32[1]{0:T(128)} %bitcast.me_ref, bf16[128,1024]{1,0:T(8,128)(2,1)} %q_ref.1, bf16[128,1024]{1,0:T(8,128)(2,1)} %k_ref.1, bf16[128,1024]{1,0:T(8,128)(2,1)} %v_ref.1, bf16[512,1024]{1,0:T(8,128)(2,1)} %kt_ref.1, bf16[512,1024]{1,0:T(8,128)(2,1)} %vt_ref.1), custom_call_target="tpu_custom_call" | custom-call | bytes 1572864 | tf_op jit(solution)/shard_map/pallas_call | solution.py:147
  11.5 0.0 collective-permute-done
  11.5 5.0 %collective-permute-done.1 = bf16[64,768]{1,0:T(8,128)(2,1)S(1)} collective-permute-done((bf16[64,768]{1,0:T(8,128)(2,1)S(1)}, bf16[64,768]{1,0:T(8,128)(2,1)S(1)}, u32[]{:S(2)}, u32[]{:S(2)}) %collective-permute-start.1) | collective-permute-done | bytes 98336 | tf_op jit(solution)/shard_map/ppermute | solution.py:326
  16.5 0.0 collective-permute-done.2
  16.5 3.9 %all-to-all-start = ((bf16[8,384,128]{2,1,0:T(8,128)(2,1)}), bf16[8,384,128]{2,1,0:T(8,128)(2,1)S(1)}, u32[]{:S(2)}, u32[]{:S(2)}) async-start(bf16[8,384,128]{2,1,0:T(8,128)(2,1)} %get-tuple-element.45), calls=%async_computation | async-start | bytes 1572864 | tf_op jit(solution)/shard_map/all_to_all | solution.py:370
  20.4 2.4 %collective-permute-done.3.other_ref = bf16[384,1024]{1,0:T(8,128)(2,1)S(1)} collective-permute-done((bf16[384,1024]{1,0:T(8,128)(2,1)}, bf16[384,1024]{1,0:T(8,128)(2,1)S(1)}, u32[]{:S(2)}, u32[]{:S(2)}) %collective-permute-start.3) | collective-permute-done | bytes 786464 | tf_op jit(solution)/shard_map/ppermute | solution.py:326
  22.9 0.1 collective-permute-start.4
  23.0 1.7 %collective-permute-done.4.swapped_ref.refs_1_ = bf16[256,768]{1,0:T(8,128)(2,1)S(1)} collective-permute-done((bf16[256,768]{1,0:T(8,128)(2,1)S(1)}, bf16[256,768]{1,0:T(8,128)(2,1)S(1)}, u32[]{:S(2)}, u32[]{:S(2)}) %collective-permute-start.4) | collective-permute-done | bytes 393248 | tf_op jit(solution)/shard_map/ppermute | solution.py:326
  24.7 1.5 %shard_map.104 = (f32[512,256]{1,0:T(8,128)S(1)}, bf16[512,256]{1,0:T(8,128)(2,1)}, f32[512,256]{1,0:T(8,128)S(1)}, bf16[512,256]{1,0:T(8,128)(2,1)S(1)}) custom-call(bf16[256,768]{1,0:T(8,128)(2,1)S(1)} %constant_dynamic-update-slice_fusion.piece_ref.refs_0_, bf16[256,768]{1,0:T(8,128)(2,1)S(1)} %collective-permute-done.4.swapped_ref.refs_1_, ...), custom_call_target="tpu_custom_call" | custom-call | flops 805306368 | bytes 1572864 | tf_op jit(solution)/shard_map/pallas_call | solution.py:147
  26.2 2.5 %collective-permute-start.5 = (bf16[512,256]{1,0:T(8,128)(2,1)S(1)}, bf16[512,256]{1,0:T(8,128)(2,1)S(1)}, u32[]{:S(2)}, u32[]{:S(2)}) collective-permute-start(bf16[512,256]{1,0:T(8,128)(2,1)S(1)} %get-tuple-element.63), channel_id=1, source_target_pairs={{0,4},{1,5},{2,6},{3,7},{4,0},{5,1},{6,2},{7,3},{8,12},{9,13},{10,... | collective-permute-start | bytes 786440 | tf_op jit(solution)/shard_map/ppermute | solution.py:326
  28.6 11.8 %collective-permute-done.5.received_ref = bf16[512,256]{1,0:T(8,128)(2,1)S(1)} collective-permute-done((bf16[512,256]{1,0:T(8,128)(2,1)S(1)}, bf16[512,256]{1,0:T(8,128)(2,1)S(1)}, u32[]{:S(2)}, u32[]{:S(2)}) %collective-permute-start.5) | collective-permute-done | bytes 262176 | tf_op jit(solution)/shard_map/ppermute | solution.py:326
  40.4 2.1 %collective-permute-start.8 = (bf16[256,768]{1,0:T(8,128)(2,1)S(1)}, bf16[256,768]{1,0:T(8,128)(2,1)S(1)}, u32[]{:S(2)}, u32[]{:S(2)}) collective-permute-start(bf16[256,768]{1,0:T(8,128)(2,1)S(1)} %constant_dynamic-update-slice_fusion.piece_ref.refs_0_), channel_id=1, source_target_pairs={{0,2},{1,3},{2,0},{3,1},{4,6},{5,7},{6,4},{7,5},{8,10},{9,11},{10,... | collective-permute-start | bytes 1179656 | tf_op jit(solution)/shard_map/ppermute | solution.py:326
  42.6 1.6 %collective-permute-start.6 = (bf16[512,256]{1,0:T(8,128)(2,1)S(1)}, bf16[512,256]{1,0:T(8,128)(2,1)S(1)}, u32[]{:S(2)}, u32[]{:S(2)}) collective-permute-start(bf16[512,256]{1,0:T(8,128)(2,1)S(1)} %shard_map.105), channel_id=1, source_target_pairs={{0,8},{1,9},{2,10},{3,11},{4,12},{5,13},{6,14},{7,15},{8,0},{9,1},... | collective-permute-start | bytes 786440 | tf_op jit(solution)/shard_map/ppermute | solution.py:326
  44.2 2.5 %collective-permute-start.7 = (bf16[512,256]{1,0:T(8,128)(2,1)}, bf16[512,256]{1,0:T(8,128)(2,1)S(1)}, u32[]{:S(2)}, u32[]{:S(2)}) collective-permute-start(bf16[512,256]{1,0:T(8,128)(2,1)} %get-tuple-element.67), channel_id=1, source_target_pairs={{0,4},{1,5},{2,6},{3,7},{4,0},{5,1},{6,2},{7,3},{8,12},{9,13},{10,... | collective-permute-start | bytes 786440 | tf_op jit(solution)/shard_map/ppermute | solution.py:326
  46.6 0.0 all-to-all-done.tok_ref
  46.6 0.9 copy-done.3
  47.6 4.9 %shard_map.103 = (bf16[1536,1024]{1,0:T(8,128)(2,1)S(1)}, bf16[128,1024]{1,0:T(8,128)(2,1)S(1)}, bf16[1024,128]{1,0:T(8,128)(2,1)S(1)}, bf16[128,1536]{1,0:T(8,128)(2,1)S(1)}, bf16[1536,128]{1,0:T(8,128)(2,1)S(1)}) custom-call(bf16[8,384,128]{2,1,0:T(8,128)(2,1)S(1)} %all-to-all-done.tok_ref, bf16[2,512,128]{2,1,0:T(8,128)(2,1)S(1)} %copy-done.3), custom_call_target="tpu_custom_call" | custom-call | flops 805306368 | bytes 6291456 | tf_op jit(solution)/shard_map/pallas_call | solution.py:147
  52.5 0.1 collective-permute-start.11
  52.6 0.9 collective-permute-start.12
  53.5 5.6 %collective-permute-done.6.far_ref = bf16[512,256]{1,0:T(8,128)(2,1)S(1)} collective-permute-done((bf16[512,256]{1,0:T(8,128)(2,1)S(1)}, bf16[512,256]{1,0:T(8,128)(2,1)S(1)}, u32[]{:S(2)}, u32[]{:S(2)}) %collective-permute-start.6) | collective-permute-done | bytes 262176 | tf_op jit(solution)/shard_map/ppermute | solution.py:326
  59.0 0.0 collective-permute-done.7.near_ref
  59.0 0.0 collective-permute-done.8.refs_2_
  59.0 0.1 shard_map.106
  59.1 0.8 collective-permute-start.9
  59.9 0.0 collective-permute-start.10
  59.9 1.8 %shard_map.107 = (bf16[512,128]{1,0:T(8,128)(2,1)S(1)}, f32[1024,128]{1,0:T(8,128)S(1)}, f32[1024,128]{1,0:T(8,128)S(1)}) custom-call(bf16[1024,128]{1,0:T(8,128)(2,1)S(1)} %get-tuple-element.47.queries_ref, bf16[128,1536]{1,0:T(8,128)(2,1)S(1)} %get-tuple-element.48.keys_t_ref, bf16[1536,128]{1,0:T(8,128)(2,1)S(1)} %get-tuple-element.49.vals_ref, ...), custom_call_target="tpu_custom_call" | custom-call | tf_op jit(solution)/shard_map/pallas_call | solution.py:147
  61.8 2.4 %collective-permute-done.9.grads_ref = bf16[512,128]{1,0:T(8,128)(2,1)S(1)} collective-permute-done((bf16[512,128]{1,0:T(8,128)(2,1)S(1)}, bf16[512,128]{1,0:T(8,128)(2,1)S(1)}, u32[]{:S(2)}, u32[]{:S(2)}) %collective-permute-start.9) | collective-permute-done | bytes 131104 | tf_op jit(solution)/shard_map/ppermute | solution.py:326
  64.2 2.8 %shard_map.108 = bf16[8,384,128]{2,1,0:T(8,128)(2,1)} custom-call(bf16[1024,128]{1,0:T(8,128)(2,1)S(1)} %get-tuple-element.47.queries_ref, bf16[128,1536]{1,0:T(8,128)(2,1)S(1)} %get-tuple-element.48.keys_t_ref, bf16[1536,128]{1,0:T(8,128)(2,1)S(1)} %get-tuple-element.49.vals_ref, bf16[1536,1024]{1,0:T(8,128)(2,1)S(1)} %get-tuple-element.50.probs_ref, ...), custom_call_target="tpu_custom_call" | custom-call | tf_op jit(solution)/shard_map/pallas_call | solution.py:147
  67.0 1.5 %collective-permute-done.11.refs_6_ = bf16[128,1024]{1,0:T(8,128)(2,1)S(1)} collective-permute-done((bf16[128,1024]{1,0:T(8,128)(2,1)S(1)}, bf16[128,1024]{1,0:T(8,128)(2,1)S(1)}, u32[]{:S(2)}, u32[]{:S(2)}) %collective-permute-start.11) | collective-permute-done | bytes 262176 | tf_op jit(solution)/shard_map/ppermute | solution.py:326
  68.5 0.2 collective-permute-done.12.refs_5_
  68.7 0.7 copy-done.4
  69.4 3.9 %all-to-all-start.1 = ((bf16[8,384,128]{2,1,0:T(8,128)(2,1)}), bf16[8,384,128]{2,1,0:T(8,128)(2,1)S(1)}, u32[]{:S(2)}, u32[]{:S(2)}) async-start(bf16[8,384,128]{2,1,0:T(8,128)(2,1)} %shard_map.108), calls=%async_computation.1 | async-start | bytes 1572864 | tf_op jit(solution)/shard_map/all_to_all | solution.py:409
  73.3 5.3 %collective-permute-done.13.refs_7_ = bf16[128,1024]{1,0:T(8,128)(2,1)S(1)} collective-permute-done((bf16[128,1024]{1,0:T(8,128)(2,1)S(1)}, bf16[128,1024]{1,0:T(8,128)(2,1)S(1)}, u32[]{:S(2)}, u32[]{:S(2)}) %collective-permute-start.13) | collective-permute-done | bytes 262176 | tf_op jit(solution)/shard_map/ppermute | solution.py:326
  78.6 0.7 copy-done.6
  79.3 0.0 collective-permute-done.10.refs_3_
  79.3 0.9 copy-done.5
  80.3 0.9 copy-done.7
  81.2 1.4 %shard_map.110 = (bf16[512,384]{1,0:T(8,128)(2,1)S(1)}, bf16[512,384]{1,0:T(8,128)(2,1)S(1)}) custom-call(bf16[256,768]{1,0:T(8,128)(2,1)S(1)} %constant_dynamic-update-slice_fusion.piece_ref.refs_0_, bf16[256,768]{1,0:T(8,128)(2,1)S(1)} %copy-done.2, bf16[256,768]{1,0:T(8,128)(2,1)S(1)} %collective-permute-done.8.refs_2_, ...), custom_call_target="tpu_custom_call" | custom-call | flops 9663676416 | bytes 1572864 | tf_op jit(solution)/shard_map/pallas_call | solution.py:147
  82.6 1.1 %collective-permute-start.14 = (bf16[512,384]{1,0:T(8,128)(2,1)S(1)}, bf16[512,384]{1,0:T(8,128)(2,1)S(1)}, u32[]{:S(2)}, u32[]{:S(2)}) collective-permute-start(bf16[512,384]{1,0:T(8,128)(2,1)S(1)} %get-tuple-element.83), channel_id=1, source_target_pairs={{0,2},{1,3},{2,0},{3,1},{4,6},{5,7},{6,4},{7,5},{8,10},{9,11},{10,... | collective-permute-start | bytes 1179656 | tf_op jit(solution)/shard_map/ppermute | solution.py:326
  83.7 11.5 %collective-permute-done.14.other_ref = bf16[512,384]{1,0:T(8,128)(2,1)S(1)} collective-permute-done((bf16[512,384]{1,0:T(8,128)(2,1)S(1)}, bf16[512,384]{1,0:T(8,128)(2,1)S(1)}, u32[]{:S(2)}, u32[]{:S(2)}) %collective-permute-start.14) | collective-permute-done | bytes 393248 | tf_op jit(solution)/shard_map/ppermute | solution.py:326
  95.2 1.5 %shard_map.111 = f32[384,1024]{1,0:T(8,128)} custom-call(bf16[512,384]{1,0:T(8,128)(2,1)S(1)} %get-tuple-element.82.own_ref, bf16[512,384]{1,0:T(8,128)(2,1)S(1)} %collective-permute-done.14.other_ref), custom_call_target="tpu_custom_call" | custom-call | bytes 2359296 | tf_op jit(solution)/shard_map/pallas_call | solution.py:147
  96.7 0.0 all-to-all-done.1.tok_ref
  96.7 1.1 %shard_map.109 = (bf16[128,1024]{1,0:T(8,128)(2,1)}, bf16[128,1024]{1,0:T(8,128)(2,1)}, bf16[128,1024]{1,0:T(8,128)(2,1)}) custom-call(bf16[8,384,128]{2,1,0:T(8,128)(2,1)S(1)} %all-to-all-done.1.tok_ref), custom_call_target="tpu_custom_call" | custom-call | bytes 1572864 | tf_op jit(solution)/shard_map/pallas_call | solution.py:147
  (17 shorter events, 0.1 us)
Async XLA Ops:
  0.6 24.1 %copy-start = (bf16[384,1024]{1,0:T(8,128)(2,1)S(1)}, bf16[384,1024]{1,0:T(8,128)(2,1)}, u32[]{:S(2)}) copy-start(bf16[384,1024]{1,0:T(8,128)(2,1)} %own_ref.1) | copy-start | bytes 2359300
  0.6 22.2 %collective-permute-start.3 = (bf16[384,1024]{1,0:T(8,128)(2,1)}, bf16[384,1024]{1,0:T(8,128)(2,1)S(1)}, u32[]{:S(2)}, u32[]{:S(2)}) collective-permute-start(bf16[384,1024]{1,0:T(8,128)(2,1)} %own_ref.1), channel_id=1, source_target_pairs={{0,2},{1,3},{2,0},{3,1},{4,6},{5,7},{6,4},{7,5},{8,10},{9,11},{10,... | collective-permute-start | bytes 2359304 | tf_op jit(solution)/shard_map/ppermute | solution.py:326
  4.7 6.8 %collective-permute-start = (bf16[64,768]{1,0:T(8,128)(2,1)S(1)}, bf16[64,768]{1,0:T(8,128)(2,1)S(1)}, u32[]{:S(2)}, u32[]{:S(2)}) collective-permute-start(bf16[64,768]{1,0:T(8,128)(2,1)S(1)} %get-tuple-element.85), channel_id=1, source_target_pairs={{0,4},{1,5},{2,6},{3,7},{4,0},{5,1},{6,2},{7,3},{8,12},{9,13},{10,... | collective-permute-start | bytes 294920 | tf_op jit(solution)/shard_map/ppermute | solution.py:326
  6.4 10.1 %collective-permute-start.1 = (bf16[64,768]{1,0:T(8,128)(2,1)S(1)}, bf16[64,768]{1,0:T(8,128)(2,1)S(1)}, u32[]{:S(2)}, u32[]{:S(2)}) collective-permute-start(bf16[64,768]{1,0:T(8,128)(2,1)S(1)} %get-tuple-element.87), channel_id=1, source_target_pairs={{0,8},{1,9},{2,10},{3,11},{4,12},{5,13},{6,14},{7,15},{8,0},{9,1},... | collective-permute-start | bytes 294920 | tf_op jit(solution)/shard_map/ppermute | solution.py:326
  9.0 7.6 %collective-permute-start.2 = (bf16[64,768]{1,0:T(8,128)(2,1)S(1)}, bf16[64,768]{1,0:T(8,128)(2,1)S(1)}, u32[]{:S(2)}, u32[]{:S(2)}) collective-permute-start(bf16[64,768]{1,0:T(8,128)(2,1)S(1)} %get-tuple-element.84), channel_id=1, source_target_pairs={{0,12},{1,13},{2,14},{3,15},{4,8},{5,9},{6,10},{7,11},{8,4},{9,5},... | collective-permute-start | bytes 294920 | tf_op jit(solution)/shard_map/ppermute | solution.py:326
  16.5 30.1 %all-to-all-start = ((bf16[8,384,128]{2,1,0:T(8,128)(2,1)}), bf16[8,384,128]{2,1,0:T(8,128)(2,1)S(1)}, u32[]{:S(2)}, u32[]{:S(2)}) async-start(bf16[8,384,128]{2,1,0:T(8,128)(2,1)} %get-tuple-element.45), calls=%async_computation | async-start | bytes 1572864 | tf_op jit(solution)/shard_map/all_to_all | solution.py:370
  22.9 1.8 %collective-permute-start.4 = (bf16[256,768]{1,0:T(8,128)(2,1)S(1)}, bf16[256,768]{1,0:T(8,128)(2,1)S(1)}, u32[]{:S(2)}, u32[]{:S(2)}) collective-permute-start(bf16[256,768]{1,0:T(8,128)(2,1)S(1)} %constant_dynamic-update-slice_fusion.piece_ref.refs_0_), channel_id=1, source_target_pairs={{0,1},{1,0},{2,3},{3,2},{4,5},{5,4},{6,7},{7,6},{8,9},{9,8},{10,11... | collective-permute-start | bytes 1179656 | tf_op jit(solution)/shard_map/ppermute | solution.py:326
  24.7 19.5 %copy-start.1 = (bf16[256,768]{1,0:T(8,128)(2,1)}, bf16[256,768]{1,0:T(8,128)(2,1)S(1)}, u32[]{:S(2)}) copy-start(bf16[256,768]{1,0:T(8,128)(2,1)S(1)} %collective-permute-done.4.swapped_ref.refs_1_) | copy-start | bytes 1179652
  26.2 14.2 %collective-permute-start.5 = (bf16[512,256]{1,0:T(8,128)(2,1)S(1)}, bf16[512,256]{1,0:T(8,128)(2,1)S(1)}, u32[]{:S(2)}, u32[]{:S(2)}) collective-permute-start(bf16[512,256]{1,0:T(8,128)(2,1)S(1)} %get-tuple-element.63), channel_id=1, source_target_pairs={{0,4},{1,5},{2,6},{3,7},{4,0},{5,1},{6,2},{7,3},{8,12},{9,13},{10,... | collective-permute-start | bytes 786440 | tf_op jit(solution)/shard_map/ppermute | solution.py:326
  40.4 18.6 %collective-permute-start.8 = (bf16[256,768]{1,0:T(8,128)(2,1)S(1)}, bf16[256,768]{1,0:T(8,128)(2,1)S(1)}, u32[]{:S(2)}, u32[]{:S(2)}) collective-permute-start(bf16[256,768]{1,0:T(8,128)(2,1)S(1)} %constant_dynamic-update-slice_fusion.piece_ref.refs_0_), channel_id=1, source_target_pairs={{0,2},{1,3},{2,0},{3,1},{4,6},{5,7},{6,4},{7,5},{8,10},{9,11},{10,... | collective-permute-start | bytes 1179656 | tf_op jit(solution)/shard_map/ppermute | solution.py:326
  42.6 16.5 %collective-permute-start.6 = (bf16[512,256]{1,0:T(8,128)(2,1)S(1)}, bf16[512,256]{1,0:T(8,128)(2,1)S(1)}, u32[]{:S(2)}, u32[]{:S(2)}) collective-permute-start(bf16[512,256]{1,0:T(8,128)(2,1)S(1)} %shard_map.105), channel_id=1, source_target_pairs={{0,8},{1,9},{2,10},{3,11},{4,12},{5,13},{6,14},{7,15},{8,0},{9,1},... | collective-permute-start | bytes 786440 | tf_op jit(solution)/shard_map/ppermute | solution.py:326
  44.2 14.9 %collective-permute-start.7 = (bf16[512,256]{1,0:T(8,128)(2,1)}, bf16[512,256]{1,0:T(8,128)(2,1)S(1)}, u32[]{:S(2)}, u32[]{:S(2)}) collective-permute-start(bf16[512,256]{1,0:T(8,128)(2,1)} %get-tuple-element.67), channel_id=1, source_target_pairs={{0,4},{1,5},{2,6},{3,7},{4,0},{5,1},{6,2},{7,3},{8,12},{9,13},{10,... | collective-permute-start | bytes 786440 | tf_op jit(solution)/shard_map/ppermute | solution.py:326
  46.6 1.0 copy-start.3
  52.5 15.9 %collective-permute-start.11 = (bf16[128,1024]{1,0:T(8,128)(2,1)S(1)}, bf16[128,1024]{1,0:T(8,128)(2,1)S(1)}, u32[]{:S(2)}, u32[]{:S(2)}) collective-permute-start(bf16[128,1024]{1,0:T(8,128)(2,1)S(1)} %get-tuple-element.51.out_ref.refs_4_), channel_id=1, source_target_pairs={{0,8},{1,9},{2,10},{3,11},{4,12},{5,13},{6,14},{7,15},{8,0},{9,1},... | collective-permute-start | bytes 786440 | tf_op jit(solution)/shard_map/ppermute | solution.py:326
  52.6 16.1 %collective-permute-start.12 = (bf16[128,1024]{1,0:T(8,128)(2,1)S(1)}, bf16[128,1024]{1,0:T(8,128)(2,1)S(1)}, u32[]{:S(2)}, u32[]{:S(2)}) collective-permute-start(bf16[128,1024]{1,0:T(8,128)(2,1)S(1)} %get-tuple-element.51.out_ref.refs_4_), channel_id=1, source_target_pairs={{0,4},{1,5},{2,6},{3,7},{4,0},{5,1},{6,2},{7,3},{8,12},{9,13},{10,... | collective-permute-start | bytes 786440 | tf_op jit(solution)/shard_map/ppermute | solution.py:326
  59.1 5.0 %collective-permute-start.9 = (bf16[512,128]{1,0:T(8,128)(2,1)S(1)}, bf16[512,128]{1,0:T(8,128)(2,1)S(1)}, u32[]{:S(2)}, u32[]{:S(2)}) collective-permute-start(bf16[512,128]{1,0:T(8,128)(2,1)S(1)} %get-tuple-element.71), channel_id=1, source_target_pairs={{0,2},{1,3},{2,0},{3,1},{4,6},{5,7},{6,4},{7,5},{8,10},{9,11},{10,... | collective-permute-start | bytes 393224 | tf_op jit(solution)/shard_map/ppermute | solution.py:326
  59.9 19.4 %collective-permute-start.10 = (bf16[256,768]{1,0:T(8,128)(2,1)S(1)}, bf16[256,768]{1,0:T(8,128)(2,1)S(1)}, u32[]{:S(2)}, u32[]{:S(2)}) collective-permute-start(bf16[256,768]{1,0:T(8,128)(2,1)S(1)} %collective-permute-done.8.refs_2_), channel_id=1, source_target_pairs={{0,1},{1,0},{2,3},{3,2},{4,5},{5,4},{6,7},{7,6},{8,9},{9,8},{10,11... | collective-permute-start | bytes 1179656 | tf_op jit(solution)/shard_map/ppermute | solution.py:326
  64.2 15.1 %copy-start.2 = (bf16[256,768]{1,0:T(8,128)(2,1)S(1)}, bf16[256,768]{1,0:T(8,128)(2,1)}, u32[]{:S(2)}) copy-start(bf16[256,768]{1,0:T(8,128)(2,1)} %copy-done.1) | copy-start | bytes 1179652
  68.7 0.7 copy-start.4
  69.4 9.2 %collective-permute-start.13 = (bf16[128,1024]{1,0:T(8,128)(2,1)S(1)}, bf16[128,1024]{1,0:T(8,128)(2,1)S(1)}, u32[]{:S(2)}, u32[]{:S(2)}) collective-permute-start(bf16[128,1024]{1,0:T(8,128)(2,1)S(1)} %collective-permute-done.11.refs_6_), channel_id=1, source_target_pairs={{0,4},{1,5},{2,6},{3,7},{4,0},{5,1},{6,2},{7,3},{8,12},{9,13},{10,... | collective-permute-start | bytes 786440 | tf_op jit(solution)/shard_map/ppermute | solution.py:326
  69.4 27.3 %all-to-all-start.1 = ((bf16[8,384,128]{2,1,0:T(8,128)(2,1)}), bf16[8,384,128]{2,1,0:T(8,128)(2,1)S(1)}, u32[]{:S(2)}, u32[]{:S(2)}) async-start(bf16[8,384,128]{2,1,0:T(8,128)(2,1)} %shard_map.108), calls=%async_computation.1 | async-start | bytes 1572864 | tf_op jit(solution)/shard_map/all_to_all | solution.py:409
  78.6 0.7 copy-start.6
  79.3 1.0 copy-start.5
  80.3 0.9 copy-start.7
  82.6 12.6 %collective-permute-start.14 = (bf16[512,384]{1,0:T(8,128)(2,1)S(1)}, bf16[512,384]{1,0:T(8,128)(2,1)S(1)}, u32[]{:S(2)}, u32[]{:S(2)}) collective-permute-start(bf16[512,384]{1,0:T(8,128)(2,1)S(1)} %get-tuple-element.83), channel_id=1, source_target_pairs={{0,2},{1,3},{2,0},{3,1},{4,6},{5,7},{6,4},{7,5},{8,10},{9,11},{10,... | collective-permute-start | bytes 1179656 | tf_op jit(solution)/shard_map/ppermute | solution.py:326

commit v32 on v29

--- a/solution.py
+++ b/solution.py
@@ -402,10 +402,11 @@
         [grad_in],
         moved=4 * 3 * rows * width,
     )
+    dw_other, *grads = lax.optimization_barrier((exchange(dw_other, 1), *grads))
     (d_weight,) = call(
         unpack_weight_kernel,
         [shape((depth, width), F32)],
-        [dw_own, exchange(dw_other, 1)],
+        [dw_own, dw_other],
         moved=6 * depth * width,
     )
     return (*grads, d_weight)

time: 98.2 us -> 97.1 us (0.989)
  waiting for transfers between devices: 47.4 us -> 45.4 us
    ppermute x15, waiting for transfers between devices: 47.4 us -> 36.7 us  [exchange(): return lax.ppermute(array, ('seq', 'fsdp'), pairs)]
    all_to_all x1, waiting for transfers between devices: 0.01 us -> 8.69 us  [local(): lax.all_to_all(grad_out, 'seq', split_axis=0, concat_axis=0, tiled=True)]
    unnamed x19 -> x23, local copies, waits for them, and re-layouts: 4.29 us -> 5.26 us
  transfers between devices with their start and end apart: 17 -> 17, of which waited for: 8 -> 10; matrix products, arithmetic and copies ran while one was open for 1% -> 1% of each run, Pallas kernels for 17% -> 16%
where the time goes in v32:
time: 97.1 us; the launch traced here: 96.7 us
  waiting for transfers between devices  45.4 us (47%)
  starting transfers between devices  27 us (28%)
  Pallas kernels  17.2 us (18%)
  local copies, waits for them, and re-layouts  6.33 us (7%)
    ppermute x15, waiting for transfers between devices, exchange(): return lax.ppermute(array, ('seq', 'fsdp'), pairs)  36.7 us
    ppermute x15, starting transfers between devices, exchange(): return lax.ppermute(array, ('seq', 'fsdp'), pairs)  19 us
    pallas_call x9, Pallas kernels, call(): pl.pallas_call(kernel, out_shape=outs, grid_spec=pltpu.PrefetchScalarGrid...  17.2 us
    all_to_all x1, waiting for transfers between devices, local(): lax.all_to_all(grad_out, 'seq', split_axis=0, concat_axis=0, tiled=True)  8.69 us
    unnamed x23, local copies, waits for them, and re-layouts  5.26 us
    all_to_all x1, starting transfers between devices, local(): lax.all_to_all(grad_out, 'seq', split_axis=0, concat_axis=0, tiled=True)  4.14 us
    all_to_all x1, starting transfers between devices, local(): lax.all_to_all(tok_out, 'seq', split_axis=0, concat_axis=0, tiled=True)  3.9 us
  transfers between devices with their start and end apart: 17, of which 10 were waited for; matrix products, arithmetic and copies ran while one was open for 1% of the time, Pallas kernels for 16%

profile of v32, /device:TPU:0, one launch (start us, length us, event | category | flops | bytes accessed | tf_op | source)
XLA Modules:
  0.0 96.7 jit_solution(10808264864915379852)
XLA Ops:
  0.6 3.0 %collective-permute-start.3 = (bf16[384,1024]{1,0:T(8,128)(2,1)}, bf16[384,1024]{1,0:T(8,128)(2,1)S(1)}, u32[]{:S(2)}, u32[]{:S(2)}) collective-permute-start(bf16[384,1024]{1,0:T(8,128)(2,1)} %own_ref.1), channel_id=1, source_target_pairs={{0,2},{1,3},{2,0},{3,1},{4,6},{5,7},{6,4},{7,5},{8,10},{9,11},{10,... | collective-permute-start | bytes 2359304 | tf_op jit(solution)/shard_map/ppermute | solution.py:310
  3.7 1.1 %fusion = (bf16[64,768]{1,0:T(8,128)(2,1)S(1)}, bf16[64,768]{1,0:T(8,128)(2,1)S(1)}, bf16[64,768]{1,0:T(8,128)(2,1)S(1)}, bf16[64,768]{1,0:T(8,128)(2,1)S(1)}) fusion(bf16[128,3072]{1,0:T(8,128)(2,1)} %param.13, s32[]{:T(128)S(6)} %select_n.23, s32[]{:T(128)S(6)} %select_n.28, s32[]{:T(128)S(6)} %select_n.26, s32[]{:T(128)S(6)} %select_n.25, s32[]{:T(128)S(6)} %select_n.27), kind=kLoop, calls=%fused_computation.4 | loop fusion | bytes 786452 | tf_op jit(solution)/shard_map/dynamic_slice | solution.py:319
  4.7 1.6 %collective-permute-start = (bf16[64,768]{1,0:T(8,128)(2,1)S(1)}, bf16[64,768]{1,0:T(8,128)(2,1)S(1)}, u32[]{:S(2)}, u32[]{:S(2)}) collective-permute-start(bf16[64,768]{1,0:T(8,128)(2,1)S(1)} %get-tuple-element.87), channel_id=1, source_target_pairs={{0,4},{1,5},{2,6},{3,7},{4,0},{5,1},{6,2},{7,3},{8,12},{9,13},{10,... | collective-permute-start | bytes 294920 | tf_op jit(solution)/shard_map/ppermute | solution.py:310
  6.4 2.6 %collective-permute-start.1 = (bf16[64,768]{1,0:T(8,128)(2,1)S(1)}, bf16[64,768]{1,0:T(8,128)(2,1)S(1)}, u32[]{:S(2)}, u32[]{:S(2)}) collective-permute-start(bf16[64,768]{1,0:T(8,128)(2,1)S(1)} %get-tuple-element.89), channel_id=1, source_target_pairs={{0,8},{1,9},{2,10},{3,11},{4,12},{5,13},{6,14},{7,15},{8,0},{9,1},... | collective-permute-start | bytes 294920 | tf_op jit(solution)/shard_map/ppermute | solution.py:310
  9.0 0.2 collective-permute-start.2
  9.2 2.3 %shard_map.102 = (bf16[8,384,128]{2,1,0:T(8,128)(2,1)}, bf16[2,512,128]{2,1,0:T(8,128)(2,1)}) custom-call(s32[1]{0:T(128)} %bitcast.me_ref, bf16[128,1024]{1,0:T(8,128)(2,1)} %q_ref.1, bf16[128,1024]{1,0:T(8,128)(2,1)} %k_ref.1, bf16[128,1024]{1,0:T(8,128)(2,1)} %v_ref.1, bf16[512,1024]{1,0:T(8,128)(2,1)} %kt_ref.1, bf16[512,1024]{1,0:T(8,128)(2,1)} %vt_ref.1), custom_call_target="tpu_custom_call" | custom-call | bytes 1572864 | tf_op jit(solution)/shard_map/pallas_call | solution.py:147
  11.5 0.0 collective-permute-done
  11.5 5.0 %collective-permute-done.1 = bf16[64,768]{1,0:T(8,128)(2,1)S(1)} collective-permute-done((bf16[64,768]{1,0:T(8,128)(2,1)S(1)}, bf16[64,768]{1,0:T(8,128)(2,1)S(1)}, u32[]{:S(2)}, u32[]{:S(2)}) %collective-permute-start.1) | collective-permute-done | bytes 98336 | tf_op jit(solution)/shard_map/ppermute | solution.py:310
  16.5 0.0 collective-permute-done.2
  16.5 3.9 %all-to-all-start = ((bf16[8,384,128]{2,1,0:T(8,128)(2,1)}), bf16[8,384,128]{2,1,0:T(8,128)(2,1)S(1)}, u32[]{:S(2)}, u32[]{:S(2)}) async-start(bf16[8,384,128]{2,1,0:T(8,128)(2,1)} %get-tuple-element.63), calls=%async_computation | async-start | bytes 1572864 | tf_op jit(solution)/shard_map/all_to_all | solution.py:354
  20.4 2.4 %collective-permute-done.3.other_ref = bf16[384,1024]{1,0:T(8,128)(2,1)S(1)} collective-permute-done((bf16[384,1024]{1,0:T(8,128)(2,1)}, bf16[384,1024]{1,0:T(8,128)(2,1)S(1)}, u32[]{:S(2)}, u32[]{:S(2)}) %collective-permute-start.3) | collective-permute-done | bytes 786464 | tf_op jit(solution)/shard_map/ppermute | solution.py:310
  22.9 0.1 collective-permute-start.4
  23.0 1.7 %collective-permute-done.4.swapped_ref.refs_1_ = bf16[256,768]{1,0:T(8,128)(2,1)S(1)} collective-permute-done((bf16[256,768]{1,0:T(8,128)(2,1)S(1)}, bf16[256,768]{1,0:T(8,128)(2,1)S(1)}, u32[]{:S(2)}, u32[]{:S(2)}) %collective-permute-start.4) | collective-permute-done | bytes 393248 | tf_op jit(solution)/shard_map/ppermute | solution.py:310
  24.7 1.5 %shard_map.103 = (f32[512,256]{1,0:T(8,128)S(1)}, bf16[512,256]{1,0:T(8,128)(2,1)}, f32[512,256]{1,0:T(8,128)S(1)}, bf16[512,256]{1,0:T(8,128)(2,1)S(1)}) custom-call(bf16[256,768]{1,0:T(8,128)(2,1)S(1)} %constant_dynamic-update-slice_fusion.piece_ref.refs_0_, bf16[256,768]{1,0:T(8,128)(2,1)S(1)} %collective-permute-done.4.swapped_ref.refs_1_, ...), custom_call_target="tpu_custom_call" | custom-call | flops 805306368 | bytes 1572864 | tf_op jit(solution)/shard_map/pallas_call | solution.py:147
  26.2 2.5 %collective-permute-start.5 = (bf16[512,256]{1,0:T(8,128)(2,1)S(1)}, bf16[512,256]{1,0:T(8,128)(2,1)S(1)}, u32[]{:S(2)}, u32[]{:S(2)}) collective-permute-start(bf16[512,256]{1,0:T(8,128)(2,1)S(1)} %get-tuple-element.56), channel_id=1, source_target_pairs={{0,4},{1,5},{2,6},{3,7},{4,0},{5,1},{6,2},{7,3},{8,12},{9,13},{10,... | collective-permute-start | bytes 786440 | tf_op jit(solution)/shard_map/ppermute | solution.py:310
  28.6 11.8 %collective-permute-done.5.received_ref = bf16[512,256]{1,0:T(8,128)(2,1)S(1)} collective-permute-done((bf16[512,256]{1,0:T(8,128)(2,1)S(1)}, bf16[512,256]{1,0:T(8,128)(2,1)S(1)}, u32[]{:S(2)}, u32[]{:S(2)}) %collective-permute-start.5) | collective-permute-done | bytes 262176 | tf_op jit(solution)/shard_map/ppermute | solution.py:310
  40.4 2.1 %collective-permute-start.8 = (bf16[256,768]{1,0:T(8,128)(2,1)S(1)}, bf16[256,768]{1,0:T(8,128)(2,1)S(1)}, u32[]{:S(2)}, u32[]{:S(2)}) collective-permute-start(bf16[256,768]{1,0:T(8,128)(2,1)S(1)} %constant_dynamic-update-slice_fusion.piece_ref.refs_0_), channel_id=1, source_target_pairs={{0,2},{1,3},{2,0},{3,1},{4,6},{5,7},{6,4},{7,5},{8,10},{9,11},{10,... | collective-permute-start | bytes 1179656 | tf_op jit(solution)/shard_map/ppermute | solution.py:310
  42.6 1.6 %collective-permute-start.6 = (bf16[512,256]{1,0:T(8,128)(2,1)S(1)}, bf16[512,256]{1,0:T(8,128)(2,1)S(1)}, u32[]{:S(2)}, u32[]{:S(2)}) collective-permute-start(bf16[512,256]{1,0:T(8,128)(2,1)S(1)} %shard_map.104), channel_id=1, source_target_pairs={{0,8},{1,9},{2,10},{3,11},{4,12},{5,13},{6,14},{7,15},{8,0},{9,1},... | collective-permute-start | bytes 786440 | tf_op jit(solution)/shard_map/ppermute | solution.py:310
  44.2 2.5 %collective-permute-start.7 = (bf16[512,256]{1,0:T(8,128)(2,1)}, bf16[512,256]{1,0:T(8,128)(2,1)S(1)}, u32[]{:S(2)}, u32[]{:S(2)}) collective-permute-start(bf16[512,256]{1,0:T(8,128)(2,1)} %get-tuple-element.61), channel_id=1, source_target_pairs={{0,4},{1,5},{2,6},{3,7},{4,0},{5,1},{6,2},{7,3},{8,12},{9,13},{10,... | collective-permute-start | bytes 786440 | tf_op jit(solution)/shard_map/ppermute | solution.py:310
  46.6 0.0 all-to-all-done.tok_ref
  46.6 0.9 copy-done.3
  47.6 4.9 %shard_map.105 = (bf16[1536,1024]{1,0:T(8,128)(2,1)S(1)}, bf16[128,1024]{1,0:T(8,128)(2,1)S(1)}, bf16[1024,128]{1,0:T(8,128)(2,1)S(1)}, bf16[128,1536]{1,0:T(8,128)(2,1)S(1)}, bf16[1536,128]{1,0:T(8,128)(2,1)S(1)}) custom-call(bf16[8,384,128]{2,1,0:T(8,128)(2,1)S(1)} %all-to-all-done.tok_ref, bf16[2,512,128]{2,1,0:T(8,128)(2,1)S(1)} %copy-done.3), custom_call_target="tpu_custom_call" | custom-call | flops 805306368 | bytes 6291456 | tf_op jit(solution)/shard_map/pallas_call | solution.py:147
  52.5 0.1 collective-permute-start.10
  52.6 0.9 collective-permute-start.11
  53.5 5.6 %collective-permute-done.6.far_ref = bf16[512,256]{1,0:T(8,128)(2,1)S(1)} collective-permute-done((bf16[512,256]{1,0:T(8,128)(2,1)S(1)}, bf16[512,256]{1,0:T(8,128)(2,1)S(1)}, u32[]{:S(2)}, u32[]{:S(2)}) %collective-permute-start.6) | collective-permute-done | bytes 262176 | tf_op jit(solution)/shard_map/ppermute | solution.py:310
  59.0 0.0 collective-permute-done.7.near_ref
  59.0 0.0 collective-permute-done.8.refs_2_
  59.0 0.1 shard_map.106
  59.2 0.8 collective-permute-start.12
  59.9 0.0 collective-permute-start.9
  59.9 4.3 %collective-permute-done.12.refs_1_ = bf16[512,128]{1,0:T(8,128)(2,1)S(1)} collective-permute-done((bf16[512,128]{1,0:T(8,128)(2,1)S(1)}, bf16[512,128]{1,0:T(8,128)(2,1)S(1)}, u32[]{:S(2)}, u32[]{:S(2)}) %collective-permute-start.12) | collective-permute-done | bytes 131104 | tf_op jit(solution)/shard_map/ppermute | solution.py:310
  64.2 4.4 %shard_map.107 = bf16[8,384,128]{2,1,0:T(8,128)(2,1)} custom-call(bf16[1024,128]{1,0:T(8,128)(2,1)S(1)} %get-tuple-element.66.queries_ref, bf16[128,1536]{1,0:T(8,128)(2,1)S(1)} %get-tuple-element.67.keys_t_ref, bf16[1536,128]{1,0:T(8,128)(2,1)S(1)} %get-tuple-element.68.vals_ref, bf16[1536,1024]{1,0:T(8,128)(2,1)S(1)} %get-tuple-element.69.probs_ref, ...), custom_call_target="tpu_custom_call" | custom-call | tf_op jit(solution)/shard_map/pallas_call | solution.py:147
  68.6 0.0 collective-permute-done.10.refs_6_
  68.6 0.1 collective-permute-done.11.refs_5_
  68.7 0.7 copy-done.6
  69.4 0.0 collective-permute-start.13
  69.4 4.1 %all-to-all-start.1 = ((bf16[8,384,128]{2,1,0:T(8,128)(2,1)}), bf16[8,384,128]{2,1,0:T(8,128)(2,1)S(1)}, u32[]{:S(2)}, u32[]{:S(2)}) async-start(bf16[8,384,128]{2,1,0:T(8,128)(2,1)} %shard_map.107), calls=%async_computation.1 | async-start | bytes 1572864 | tf_op jit(solution)/shard_map/all_to_all | solution.py:388
  73.6 5.1 %collective-permute-done.13.refs_7_ = bf16[128,1024]{1,0:T(8,128)(2,1)S(1)} collective-permute-done((bf16[128,1024]{1,0:T(8,128)(2,1)S(1)}, bf16[128,1024]{1,0:T(8,128)(2,1)S(1)}, u32[]{:S(2)}, u32[]{:S(2)}) %collective-permute-start.13) | collective-permute-done | bytes 262176 | tf_op jit(solution)/shard_map/ppermute | solution.py:310
  78.7 0.7 copy-done.8
  79.4 0.9 copy-done.5
  80.3 0.9 copy-done.7
  81.3 0.9 copy-done.9
  82.2 1.4 %shard_map.108 = (bf16[512,384]{1,0:T(8,128)(2,1)S(1)}, bf16[512,384]{1,0:T(8,128)(2,1)S(1)}) custom-call(bf16[256,768]{1,0:T(8,128)(2,1)S(1)} %constant_dynamic-update-slice_fusion.piece_ref.refs_0_, bf16[256,768]{1,0:T(8,128)(2,1)S(1)} %copy-done.2, bf16[256,768]{1,0:T(8,128)(2,1)S(1)} %collective-permute-done.8.refs_2_, ...), custom_call_target="tpu_custom_call" | custom-call | flops 9663676416 | bytes 1572864 | tf_op jit(solution)/shard_map/pallas_call | solution.py:147
  83.6 1.1 %collective-permute-start.14 = (bf16[512,384]{1,0:T(8,128)(2,1)S(1)}, bf16[512,384]{1,0:T(8,128)(2,1)S(1)}, u32[]{:S(2)}, u32[]{:S(2)}) collective-permute-start(bf16[512,384]{1,0:T(8,128)(2,1)S(1)} %get-tuple-element.77), channel_id=1, source_target_pairs={{0,2},{1,3},{2,0},{3,1},{4,6},{5,7},{6,4},{7,5},{8,10},{9,11},{10,... | collective-permute-start | bytes 1179656 | tf_op jit(solution)/shard_map/ppermute | solution.py:310
  84.7 8.7 %all-to-all-done.1.tok_ref = bf16[8,384,128]{2,1,0:T(8,128)(2,1)S(1)} async-done(((bf16[8,384,128]{2,1,0:T(8,128)(2,1)}), bf16[8,384,128]{2,1,0:T(8,128)(2,1)S(1)}, u32[]{:S(2)}, u32[]{:S(2)}) %all-to-all-start.1) | async-done | bytes 786464 | tf_op jit(solution)/shard_map/all_to_all | solution.py:388
  93.4 1.1 %shard_map.109 = (bf16[128,1024]{1,0:T(8,128)(2,1)}, bf16[128,1024]{1,0:T(8,128)(2,1)}, bf16[128,1024]{1,0:T(8,128)(2,1)}) custom-call(bf16[8,384,128]{2,1,0:T(8,128)(2,1)S(1)} %all-to-all-done.1.tok_ref), custom_call_target="tpu_custom_call" | custom-call | bytes 1572864 | tf_op jit(solution)/shard_map/pallas_call | solution.py:147
  94.4 0.8 collective-permute-done.14.other_ref
  95.2 1.5 %shard_map.110 = f32[384,1024]{1,0:T(8,128)} custom-call(bf16[512,384]{1,0:T(8,128)(2,1)S(1)} %get-tuple-element.84.own_ref, bf16[512,384]{1,0:T(8,128)(2,1)S(1)} %collective-permute-done.14.other_ref), custom_call_target="tpu_custom_call" | custom-call | bytes 2359296 | tf_op jit(solution)/shard_map/pallas_call | solution.py:147
  (20 shorter events, 0.1 us)
Async XLA Ops:
  0.6 24.1 %copy-start = (bf16[384,1024]{1,0:T(8,128)(2,1)S(1)}, bf16[384,1024]{1,0:T(8,128)(2,1)}, u32[]{:S(2)}) copy-start(bf16[384,1024]{1,0:T(8,128)(2,1)} %own_ref.1) | copy-start | bytes 2359300
  0.6 22.2 %collective-permute-start.3 = (bf16[384,1024]{1,0:T(8,128)(2,1)}, bf16[384,1024]{1,0:T(8,128)(2,1)S(1)}, u32[]{:S(2)}, u32[]{:S(2)}) collective-permute-start(bf16[384,1024]{1,0:T(8,128)(2,1)} %own_ref.1), channel_id=1, source_target_pairs={{0,2},{1,3},{2,0},{3,1},{4,6},{5,7},{6,4},{7,5},{8,10},{9,11},{10,... | collective-permute-start | bytes 2359304 | tf_op jit(solution)/shard_map/ppermute | solution.py:310
  4.7 6.8 %collective-permute-start = (bf16[64,768]{1,0:T(8,128)(2,1)S(1)}, bf16[64,768]{1,0:T(8,128)(2,1)S(1)}, u32[]{:S(2)}, u32[]{:S(2)}) collective-permute-start(bf16[64,768]{1,0:T(8,128)(2,1)S(1)} %get-tuple-element.87), channel_id=1, source_target_pairs={{0,4},{1,5},{2,6},{3,7},{4,0},{5,1},{6,2},{7,3},{8,12},{9,13},{10,... | collective-permute-start | bytes 294920 | tf_op jit(solution)/shard_map/ppermute | solution.py:310
  6.4 10.1 %collective-permute-start.1 = (bf16[64,768]{1,0:T(8,128)(2,1)S(1)}, bf16[64,768]{1,0:T(8,128)(2,1)S(1)}, u32[]{:S(2)}, u32[]{:S(2)}) collective-permute-start(bf16[64,768]{1,0:T(8,128)(2,1)S(1)} %get-tuple-element.89), channel_id=1, source_target_pairs={{0,8},{1,9},{2,10},{3,11},{4,12},{5,13},{6,14},{7,15},{8,0},{9,1},... | collective-permute-start | bytes 294920 | tf_op jit(solution)/shard_map/ppermute | solution.py:310
  9.0 7.6 %collective-permute-start.2 = (bf16[64,768]{1,0:T(8,128)(2,1)S(1)}, bf16[64,768]{1,0:T(8,128)(2,1)S(1)}, u32[]{:S(2)}, u32[]{:S(2)}) collective-permute-start(bf16[64,768]{1,0:T(8,128)(2,1)S(1)} %get-tuple-element.86), channel_id=1, source_target_pairs={{0,12},{1,13},{2,14},{3,15},{4,8},{5,9},{6,10},{7,11},{8,4},{9,5},... | collective-permute-start | bytes 294920 | tf_op jit(solution)/shard_map/ppermute | solution.py:310
  16.5 30.1 %all-to-all-start = ((bf16[8,384,128]{2,1,0:T(8,128)(2,1)}), bf16[8,384,128]{2,1,0:T(8,128)(2,1)S(1)}, u32[]{:S(2)}, u32[]{:S(2)}) async-start(bf16[8,384,128]{2,1,0:T(8,128)(2,1)} %get-tuple-element.63), calls=%async_computation | async-start | bytes 1572864 | tf_op jit(solution)/shard_map/all_to_all | solution.py:354
  22.9 1.8 %collective-permute-start.4 = (bf16[256,768]{1,0:T(8,128)(2,1)S(1)}, bf16[256,768]{1,0:T(8,128)(2,1)S(1)}, u32[]{:S(2)}, u32[]{:S(2)}) collective-permute-start(bf16[256,768]{1,0:T(8,128)(2,1)S(1)} %constant_dynamic-update-slice_fusion.piece_ref.refs_0_), channel_id=1, source_target_pairs={{0,1},{1,0},{2,3},{3,2},{4,5},{5,4},{6,7},{7,6},{8,9},{9,8},{10,11... | collective-permute-start | bytes 1179656 | tf_op jit(solution)/shard_map/ppermute | solution.py:310
  24.7 1.5 %copy-start.1 = (bf16[256,768]{1,0:T(8,128)(2,1)}, bf16[256,768]{1,0:T(8,128)(2,1)S(1)}, u32[]{:S(2)}) copy-start(bf16[256,768]{1,0:T(8,128)(2,1)S(1)} %collective-permute-done.4.swapped_ref.refs_1_) | copy-start | bytes 1179652
  26.2 14.2 %collective-permute-start.5 = (bf16[512,256]{1,0:T(8,128)(2,1)S(1)}, bf16[512,256]{1,0:T(8,128)(2,1)S(1)}, u32[]{:S(2)}, u32[]{:S(2)}) collective-permute-start(bf16[512,256]{1,0:T(8,128)(2,1)S(1)} %get-tuple-element.56), channel_id=1, source_target_pairs={{0,4},{1,5},{2,6},{3,7},{4,0},{5,1},{6,2},{7,3},{8,12},{9,13},{10,... | collective-permute-start | bytes 786440 | tf_op jit(solution)/shard_map/ppermute | solution.py:310
  40.4 18.6 %collective-permute-start.8 = (bf16[256,768]{1,0:T(8,128)(2,1)S(1)}, bf16[256,768]{1,0:T(8,128)(2,1)S(1)}, u32[]{:S(2)}, u32[]{:S(2)}) collective-permute-start(bf16[256,768]{1,0:T(8,128)(2,1)S(1)} %constant_dynamic-update-slice_fusion.piece_ref.refs_0_), channel_id=1, source_target_pairs={{0,2},{1,3},{2,0},{3,1},{4,6},{5,7},{6,4},{7,5},{8,10},{9,11},{10,... | collective-permute-start | bytes 1179656 | tf_op jit(solution)/shard_map/ppermute | solution.py:310
  42.6 16.5 %collective-permute-start.6 = (bf16[512,256]{1,0:T(8,128)(2,1)S(1)}, bf16[512,256]{1,0:T(8,128)(2,1)S(1)}, u32[]{:S(2)}, u32[]{:S(2)}) collective-permute-start(bf16[512,256]{1,0:T(8,128)(2,1)S(1)} %shard_map.104), channel_id=1, source_target_pairs={{0,8},{1,9},{2,10},{3,11},{4,12},{5,13},{6,14},{7,15},{8,0},{9,1},... | collective-permute-start | bytes 786440 | tf_op jit(solution)/shard_map/ppermute | solution.py:310
  44.2 14.9 %collective-permute-start.7 = (bf16[512,256]{1,0:T(8,128)(2,1)}, bf16[512,256]{1,0:T(8,128)(2,1)S(1)}, u32[]{:S(2)}, u32[]{:S(2)}) collective-permute-start(bf16[512,256]{1,0:T(8,128)(2,1)} %get-tuple-element.61), channel_id=1, source_target_pairs={{0,4},{1,5},{2,6},{3,7},{4,0},{5,1},{6,2},{7,3},{8,12},{9,13},{10,... | collective-permute-start | bytes 786440 | tf_op jit(solution)/shard_map/ppermute | solution.py:310
  46.6 1.0 copy-start.3
  52.5 16.1 %collective-permute-start.10 = (bf16[128,1024]{1,0:T(8,128)(2,1)S(1)}, bf16[128,1024]{1,0:T(8,128)(2,1)S(1)}, u32[]{:S(2)}, u32[]{:S(2)}) collective-permute-start(bf16[128,1024]{1,0:T(8,128)(2,1)S(1)} %get-tuple-element.65.out_ref.refs_4_), channel_id=1, source_target_pairs={{0,8},{1,9},{2,10},{3,11},{4,12},{5,13},{6,14},{7,15},{8,0},{9,1},... | collective-permute-start | bytes 786440 | tf_op jit(solution)/shard_map/ppermute | solution.py:310
  52.6 16.1 %collective-permute-start.11 = (bf16[128,1024]{1,0:T(8,128)(2,1)S(1)}, bf16[128,1024]{1,0:T(8,128)(2,1)S(1)}, u32[]{:S(2)}, u32[]{:S(2)}) collective-permute-start(bf16[128,1024]{1,0:T(8,128)(2,1)S(1)} %get-tuple-element.65.out_ref.refs_4_), channel_id=1, source_target_pairs={{0,4},{1,5},{2,6},{3,7},{4,0},{5,1},{6,2},{7,3},{8,12},{9,13},{10,... | collective-permute-start | bytes 786440 | tf_op jit(solution)/shard_map/ppermute | solution.py:310
  59.2 5.0 %collective-permute-start.12 = (bf16[512,128]{1,0:T(8,128)(2,1)S(1)}, bf16[512,128]{1,0:T(8,128)(2,1)S(1)}, u32[]{:S(2)}, u32[]{:S(2)}) collective-permute-start(bf16[512,128]{1,0:T(8,128)(2,1)S(1)} %get-tuple-element.74), channel_id=1, source_target_pairs={{0,2},{1,3},{2,0},{3,1},{4,6},{5,7},{6,4},{7,5},{8,10},{9,11},{10,... | collective-permute-start | bytes 393224 | tf_op jit(solution)/shard_map/ppermute | solution.py:310
  59.9 19.5 %collective-permute-start.9 = (bf16[256,768]{1,0:T(8,128)(2,1)S(1)}, bf16[256,768]{1,0:T(8,128)(2,1)S(1)}, u32[]{:S(2)}, u32[]{:S(2)}) collective-permute-start(bf16[256,768]{1,0:T(8,128)(2,1)S(1)} %collective-permute-done.8.refs_2_), channel_id=1, source_target_pairs={{0,1},{1,0},{2,3},{3,2},{4,5},{5,4},{6,7},{7,6},{8,9},{9,8},{10,11... | collective-permute-start | bytes 1179656 | tf_op jit(solution)/shard_map/ppermute | solution.py:310
  64.2 15.2 %copy-start.2 = (bf16[256,768]{1,0:T(8,128)(2,1)S(1)}, bf16[256,768]{1,0:T(8,128)(2,1)}, u32[]{:S(2)}) copy-start(bf16[256,768]{1,0:T(8,128)(2,1)} %copy-done.1) | copy-start | bytes 1179652
  68.6 10.0 %copy-start.4 = (bf16[128,1024]{1,0:T(8,128)(2,1)}, bf16[128,1024]{1,0:T(8,128)(2,1)S(1)}, u32[]{:S(2)}) copy-start(bf16[128,1024]{1,0:T(8,128)(2,1)S(1)} %collective-permute-done.10.refs_6_) | copy-start | bytes 786436
  68.7 0.7 copy-start.6
  69.4 9.2 %collective-permute-start.13 = (bf16[128,1024]{1,0:T(8,128)(2,1)S(1)}, bf16[128,1024]{1,0:T(8,128)(2,1)S(1)}, u32[]{:S(2)}, u32[]{:S(2)}) collective-permute-start(bf16[128,1024]{1,0:T(8,128)(2,1)S(1)} %collective-permute-done.10.refs_6_), channel_id=1, source_target_pairs={{0,4},{1,5},{2,6},{3,7},{4,0},{5,1},{6,2},{7,3},{8,12},{9,13},{10,... | collective-permute-start | bytes 786440 | tf_op jit(solution)/shard_map/ppermute | solution.py:310
  69.4 23.9 %all-to-all-start.1 = ((bf16[8,384,128]{2,1,0:T(8,128)(2,1)}), bf16[8,384,128]{2,1,0:T(8,128)(2,1)S(1)}, u32[]{:S(2)}, u32[]{:S(2)}) async-start(bf16[8,384,128]{2,1,0:T(8,128)(2,1)} %shard_map.107), calls=%async_computation.1 | async-start | bytes 1572864 | tf_op jit(solution)/shard_map/all_to_all | solution.py:388
  78.7 0.7 copy-start.8
  79.4 1.0 copy-start.5
  80.3 0.9 copy-start.7
  81.3 0.9 copy-start.9
  83.6 11.6 %collective-permute-start.14 = (bf16[512,384]{1,0:T(8,128)(2,1)S(1)}, bf16[512,384]{1,0:T(8,128)(2,1)S(1)}, u32[]{:S(2)}, u32[]{:S(2)}) collective-permute-start(bf16[512,384]{1,0:T(8,128)(2,1)S(1)} %get-tuple-element.77), channel_id=1, source_target_pairs={{0,2},{1,3},{2,0},{3,1},{4,6},{5,7},{6,4},{7,5},{8,10},{9,11},{10,... | collective-permute-start | bytes 1179656 | tf_op jit(solution)/shard_map/ppermute | solution.py:310

commit v33 on v32

--- a/solution.py
+++ b/solution.py
@@ -299,7 +299,7 @@
 def unpack_weight_kernel(own_ref, other_ref, w_ref):
     for other_row, ref in enumerate((own_ref, other_ref)):
         for i, step in enumerate(STEPS):
-            w_ref[:, head_columns(step, other_row)] = ref[i * HD : (i + 1) * HD, :].astype(F32).T
+            w_ref[:, head_columns(step, other_row)] = ref[i * HD : (i + 1) * HD, :].T.astype(F32)
 
 
 def exchange(array, distance=0, cores=False):

time: 97.1 us -> 97.1 us (level)
  no operation moved by 1% of the time
where the time goes in v33:
time: 97.1 us; the launch traced here: 96.6 us
  waiting for transfers between devices  45.4 us (47%)
  starting transfers between devices  27 us (28%)
  Pallas kernels  17.2 us (18%)
  local copies, waits for them, and re-layouts  6.33 us (7%)
    ppermute x15, waiting for transfers between devices, exchange(): return lax.ppermute(array, ('seq', 'fsdp'), pairs)  36.7 us
    ppermute x15, starting transfers between devices, exchange(): return lax.ppermute(array, ('seq', 'fsdp'), pairs)  19 us
    pallas_call x9, Pallas kernels, call(): pl.pallas_call(kernel, out_shape=outs, grid_spec=pltpu.PrefetchScalarGrid...  17.2 us
    all_to_all x1, waiting for transfers between devices, local(): lax.all_to_all(grad_out, 'seq', split_axis=0, concat_axis=0, tiled=True)  8.69 us
    unnamed x23, local copies, waits for them, and re-layouts  5.26 us
    all_to_all x1, starting transfers between devices, local(): lax.all_to_all(grad_out, 'seq', split_axis=0, concat_axis=0, tiled=True)  4.14 us
    all_to_all x1, starting transfers between devices, local(): lax.all_to_all(tok_out, 'seq', split_axis=0, concat_axis=0, tiled=True)  3.9 us
  transfers between devices with their start and end apart: 17, of which 10 were waited for; matrix products, arithmetic and copies ran while one was open for 1% of the time, Pallas kernels for 16%

profile of v33, /device:TPU:0, one launch (start us, length us, event | category | flops | bytes accessed | tf_op | source)
XLA Modules:
  0.0 96.6 jit_solution(8216490951878919962)
XLA Ops:
  0.6 3.0 %collective-permute-start.3 = (bf16[384,1024]{1,0:T(8,128)(2,1)}, bf16[384,1024]{1,0:T(8,128)(2,1)S(1)}, u32[]{:S(2)}, u32[]{:S(2)}) collective-permute-start(bf16[384,1024]{1,0:T(8,128)(2,1)} %own_ref.1), channel_id=1, source_target_pairs={{0,2},{1,3},{2,0},{3,1},{4,6},{5,7},{6,4},{7,5},{8,10},{9,11},{10,... | collective-permute-start | bytes 2359304 | tf_op jit(solution)/shard_map/ppermute | solution.py:310
  3.7 1.1 %fusion = (bf16[64,768]{1,0:T(8,128)(2,1)S(1)}, bf16[64,768]{1,0:T(8,128)(2,1)S(1)}, bf16[64,768]{1,0:T(8,128)(2,1)S(1)}, bf16[64,768]{1,0:T(8,128)(2,1)S(1)}) fusion(bf16[128,3072]{1,0:T(8,128)(2,1)} %param.13, s32[]{:T(128)S(6)} %select_n.23, s32[]{:T(128)S(6)} %select_n.28, s32[]{:T(128)S(6)} %select_n.26, s32[]{:T(128)S(6)} %select_n.25, s32[]{:T(128)S(6)} %select_n.27), kind=kLoop, calls=%fused_computation.4 | loop fusion | bytes 786452 | tf_op jit(solution)/shard_map/dynamic_slice | solution.py:319
  4.7 1.6 %collective-permute-start = (bf16[64,768]{1,0:T(8,128)(2,1)S(1)}, bf16[64,768]{1,0:T(8,128)(2,1)S(1)}, u32[]{:S(2)}, u32[]{:S(2)}) collective-permute-start(bf16[64,768]{1,0:T(8,128)(2,1)S(1)} %get-tuple-element.87), channel_id=1, source_target_pairs={{0,4},{1,5},{2,6},{3,7},{4,0},{5,1},{6,2},{7,3},{8,12},{9,13},{10,... | collective-permute-start | bytes 294920 | tf_op jit(solution)/shard_map/ppermute | solution.py:310
  6.4 2.6 %collective-permute-start.1 = (bf16[64,768]{1,0:T(8,128)(2,1)S(1)}, bf16[64,768]{1,0:T(8,128)(2,1)S(1)}, u32[]{:S(2)}, u32[]{:S(2)}) collective-permute-start(bf16[64,768]{1,0:T(8,128)(2,1)S(1)} %get-tuple-element.89), channel_id=1, source_target_pairs={{0,8},{1,9},{2,10},{3,11},{4,12},{5,13},{6,14},{7,15},{8,0},{9,1},... | collective-permute-start | bytes 294920 | tf_op jit(solution)/shard_map/ppermute | solution.py:310
  9.0 0.2 collective-permute-start.2
  9.2 2.3 %shard_map.102 = (bf16[8,384,128]{2,1,0:T(8,128)(2,1)}, bf16[2,512,128]{2,1,0:T(8,128)(2,1)}) custom-call(s32[1]{0:T(128)} %bitcast.me_ref, bf16[128,1024]{1,0:T(8,128)(2,1)} %q_ref.1, bf16[128,1024]{1,0:T(8,128)(2,1)} %k_ref.1, bf16[128,1024]{1,0:T(8,128)(2,1)} %v_ref.1, bf16[512,1024]{1,0:T(8,128)(2,1)} %kt_ref.1, bf16[512,1024]{1,0:T(8,128)(2,1)} %vt_ref.1), custom_call_target="tpu_custom_call" | custom-call | bytes 1572864 | tf_op jit(solution)/shard_map/pallas_call | solution.py:147
  11.5 0.0 collective-permute-done
  11.5 5.0 %collective-permute-done.1 = bf16[64,768]{1,0:T(8,128)(2,1)S(1)} collective-permute-done((bf16[64,768]{1,0:T(8,128)(2,1)S(1)}, bf16[64,768]{1,0:T(8,128)(2,1)S(1)}, u32[]{:S(2)}, u32[]{:S(2)}) %collective-permute-start.1) | collective-permute-done | bytes 98336 | tf_op jit(solution)/shard_map/ppermute | solution.py:310
  16.5 0.0 collective-permute-done.2
  16.5 3.9 %all-to-all-start = ((bf16[8,384,128]{2,1,0:T(8,128)(2,1)}), bf16[8,384,128]{2,1,0:T(8,128)(2,1)S(1)}, u32[]{:S(2)}, u32[]{:S(2)}) async-start(bf16[8,384,128]{2,1,0:T(8,128)(2,1)} %get-tuple-element.63), calls=%async_computation | async-start | bytes 1572864 | tf_op jit(solution)/shard_map/all_to_all | solution.py:354
  20.4 2.4 %collective-permute-done.3.other_ref = bf16[384,1024]{1,0:T(8,128)(2,1)S(1)} collective-permute-done((bf16[384,1024]{1,0:T(8,128)(2,1)}, bf16[384,1024]{1,0:T(8,128)(2,1)S(1)}, u32[]{:S(2)}, u32[]{:S(2)}) %collective-permute-start.3) | collective-permute-done | bytes 786464 | tf_op jit(solution)/shard_map/ppermute | solution.py:310
  22.9 0.1 collective-permute-start.4
  23.0 1.7 %collective-permute-done.4.swapped_ref.refs_1_ = bf16[256,768]{1,0:T(8,128)(2,1)S(1)} collective-permute-done((bf16[256,768]{1,0:T(8,128)(2,1)S(1)}, bf16[256,768]{1,0:T(8,128)(2,1)S(1)}, u32[]{:S(2)}, u32[]{:S(2)}) %collective-permute-start.4) | collective-permute-done | bytes 393248 | tf_op jit(solution)/shard_map/ppermute | solution.py:310
  24.7 1.5 %shard_map.103 = (f32[512,256]{1,0:T(8,128)S(1)}, bf16[512,256]{1,0:T(8,128)(2,1)}, f32[512,256]{1,0:T(8,128)S(1)}, bf16[512,256]{1,0:T(8,128)(2,1)S(1)}) custom-call(bf16[256,768]{1,0:T(8,128)(2,1)S(1)} %constant_dynamic-update-slice_fusion.piece_ref.refs_0_, bf16[256,768]{1,0:T(8,128)(2,1)S(1)} %collective-permute-done.4.swapped_ref.refs_1_, ...), custom_call_target="tpu_custom_call" | custom-call | flops 805306368 | bytes 1572864 | tf_op jit(solution)/shard_map/pallas_call | solution.py:147
  26.2 2.5 %collective-permute-start.5 = (bf16[512,256]{1,0:T(8,128)(2,1)S(1)}, bf16[512,256]{1,0:T(8,128)(2,1)S(1)}, u32[]{:S(2)}, u32[]{:S(2)}) collective-permute-start(bf16[512,256]{1,0:T(8,128)(2,1)S(1)} %get-tuple-element.56), channel_id=1, source_target_pairs={{0,4},{1,5},{2,6},{3,7},{4,0},{5,1},{6,2},{7,3},{8,12},{9,13},{10,... | collective-permute-start | bytes 786440 | tf_op jit(solution)/shard_map/ppermute | solution.py:310
  28.6 11.8 %collective-permute-done.5.received_ref = bf16[512,256]{1,0:T(8,128)(2,1)S(1)} collective-permute-done((bf16[512,256]{1,0:T(8,128)(2,1)S(1)}, bf16[512,256]{1,0:T(8,128)(2,1)S(1)}, u32[]{:S(2)}, u32[]{:S(2)}) %collective-permute-start.5) | collective-permute-done | bytes 262176 | tf_op jit(solution)/shard_map/ppermute | solution.py:310
  40.4 2.1 %collective-permute-start.8 = (bf16[256,768]{1,0:T(8,128)(2,1)S(1)}, bf16[256,768]{1,0:T(8,128)(2,1)S(1)}, u32[]{:S(2)}, u32[]{:S(2)}) collective-permute-start(bf16[256,768]{1,0:T(8,128)(2,1)S(1)} %constant_dynamic-update-slice_fusion.piece_ref.refs_0_), channel_id=1, source_target_pairs={{0,2},{1,3},{2,0},{3,1},{4,6},{5,7},{6,4},{7,5},{8,10},{9,11},{10,... | collective-permute-start | bytes 1179656 | tf_op jit(solution)/shard_map/ppermute | solution.py:310
  42.6 1.6 %collective-permute-start.6 = (bf16[512,256]{1,0:T(8,128)(2,1)S(1)}, bf16[512,256]{1,0:T(8,128)(2,1)S(1)}, u32[]{:S(2)}, u32[]{:S(2)}) collective-permute-start(bf16[512,256]{1,0:T(8,128)(2,1)S(1)} %shard_map.104), channel_id=1, source_target_pairs={{0,8},{1,9},{2,10},{3,11},{4,12},{5,13},{6,14},{7,15},{8,0},{9,1},... | collective-permute-start | bytes 786440 | tf_op jit(solution)/shard_map/ppermute | solution.py:310
  44.2 2.5 %collective-permute-start.7 = (bf16[512,256]{1,0:T(8,128)(2,1)}, bf16[512,256]{1,0:T(8,128)(2,1)S(1)}, u32[]{:S(2)}, u32[]{:S(2)}) collective-permute-start(bf16[512,256]{1,0:T(8,128)(2,1)} %get-tuple-element.61), channel_id=1, source_target_pairs={{0,4},{1,5},{2,6},{3,7},{4,0},{5,1},{6,2},{7,3},{8,12},{9,13},{10,... | collective-permute-start | bytes 786440 | tf_op jit(solution)/shard_map/ppermute | solution.py:310
  46.6 0.0 all-to-all-done.tok_ref
  46.6 0.9 copy-done.3
  47.6 4.9 %shard_map.105 = (bf16[1536,1024]{1,0:T(8,128)(2,1)S(1)}, bf16[128,1024]{1,0:T(8,128)(2,1)S(1)}, bf16[1024,128]{1,0:T(8,128)(2,1)S(1)}, bf16[128,1536]{1,0:T(8,128)(2,1)S(1)}, bf16[1536,128]{1,0:T(8,128)(2,1)S(1)}) custom-call(bf16[8,384,128]{2,1,0:T(8,128)(2,1)S(1)} %all-to-all-done.tok_ref, bf16[2,512,128]{2,1,0:T(8,128)(2,1)S(1)} %copy-done.3), custom_call_target="tpu_custom_call" | custom-call | flops 805306368 | bytes 6291456 | tf_op jit(solution)/shard_map/pallas_call | solution.py:147
  52.5 0.1 collective-permute-start.10
  52.6 0.9 collective-permute-start.11
  53.5 5.6 %collective-permute-done.6.far_ref = bf16[512,256]{1,0:T(8,128)(2,1)S(1)} collective-permute-done((bf16[512,256]{1,0:T(8,128)(2,1)S(1)}, bf16[512,256]{1,0:T(8,128)(2,1)S(1)}, u32[]{:S(2)}, u32[]{:S(2)}) %collective-permute-start.6) | collective-permute-done | bytes 262176 | tf_op jit(solution)/shard_map/ppermute | solution.py:310
  59.0 0.0 collective-permute-done.7.near_ref
  59.0 0.0 collective-permute-done.8.refs_2_
  59.0 0.1 shard_map.106
  59.2 0.8 collective-permute-start.12
  59.9 0.0 collective-permute-start.9
  59.9 4.3 %collective-permute-done.12.refs_1_ = bf16[512,128]{1,0:T(8,128)(2,1)S(1)} collective-permute-done((bf16[512,128]{1,0:T(8,128)(2,1)S(1)}, bf16[512,128]{1,0:T(8,128)(2,1)S(1)}, u32[]{:S(2)}, u32[]{:S(2)}) %collective-permute-start.12) | collective-permute-done | bytes 131104 | tf_op jit(solution)/shard_map/ppermute | solution.py:310
  64.2 4.4 %shard_map.107 = bf16[8,384,128]{2,1,0:T(8,128)(2,1)} custom-call(bf16[1024,128]{1,0:T(8,128)(2,1)S(1)} %get-tuple-element.66.queries_ref, bf16[128,1536]{1,0:T(8,128)(2,1)S(1)} %get-tuple-element.67.keys_t_ref, bf16[1536,128]{1,0:T(8,128)(2,1)S(1)} %get-tuple-element.68.vals_ref, bf16[1536,1024]{1,0:T(8,128)(2,1)S(1)} %get-tuple-element.69.probs_ref, ...), custom_call_target="tpu_custom_call" | custom-call | tf_op jit(solution)/shard_map/pallas_call | solution.py:147
  68.6 0.0 collective-permute-done.10.refs_6_
  68.6 0.1 collective-permute-done.11.refs_5_
  68.7 0.7 copy-done.6
  69.4 4.1 %all-to-all-start.1 = ((bf16[8,384,128]{2,1,0:T(8,128)(2,1)}), bf16[8,384,128]{2,1,0:T(8,128)(2,1)S(1)}, u32[]{:S(2)}, u32[]{:S(2)}) async-start(bf16[8,384,128]{2,1,0:T(8,128)(2,1)} %shard_map.107), calls=%async_computation.1 | async-start | bytes 1572864 | tf_op jit(solution)/shard_map/all_to_all | solution.py:388
  73.6 5.1 %collective-permute-done.13.refs_7_ = bf16[128,1024]{1,0:T(8,128)(2,1)S(1)} collective-permute-done((bf16[128,1024]{1,0:T(8,128)(2,1)S(1)}, bf16[128,1024]{1,0:T(8,128)(2,1)S(1)}, u32[]{:S(2)}, u32[]{:S(2)}) %collective-permute-start.13) | collective-permute-done | bytes 262176 | tf_op jit(solution)/shard_map/ppermute | solution.py:310
  78.7 0.7 copy-done.8
  79.4 0.0 collective-permute-done.9.refs_3_
  79.4 0.9 copy-done.5
  80.3 0.9 copy-done.7
  81.3 0.9 copy-done.9
  82.2 1.4 %shard_map.108 = (bf16[512,384]{1,0:T(8,128)(2,1)S(1)}, bf16[512,384]{1,0:T(8,128)(2,1)S(1)}) custom-call(bf16[256,768]{1,0:T(8,128)(2,1)S(1)} %constant_dynamic-update-slice_fusion.piece_ref.refs_0_, bf16[256,768]{1,0:T(8,128)(2,1)S(1)} %copy-done.2, bf16[256,768]{1,0:T(8,128)(2,1)S(1)} %collective-permute-done.8.refs_2_, ...), custom_call_target="tpu_custom_call" | custom-call | flops 9663676416 | bytes 1572864 | tf_op jit(solution)/shard_map/pallas_call | solution.py:147
  83.6 1.1 %collective-permute-start.14 = (bf16[512,384]{1,0:T(8,128)(2,1)S(1)}, bf16[512,384]{1,0:T(8,128)(2,1)S(1)}, u32[]{:S(2)}, u32[]{:S(2)}) collective-permute-start(bf16[512,384]{1,0:T(8,128)(2,1)S(1)} %get-tuple-element.77), channel_id=1, source_target_pairs={{0,2},{1,3},{2,0},{3,1},{4,6},{5,7},{6,4},{7,5},{8,10},{9,11},{10,... | collective-permute-start | bytes 1179656 | tf_op jit(solution)/shard_map/ppermute | solution.py:310
  84.7 8.7 %all-to-all-done.1.tok_ref = bf16[8,384,128]{2,1,0:T(8,128)(2,1)S(1)} async-done(((bf16[8,384,128]{2,1,0:T(8,128)(2,1)}), bf16[8,384,128]{2,1,0:T(8,128)(2,1)S(1)}, u32[]{:S(2)}, u32[]{:S(2)}) %all-to-all-start.1) | async-done | bytes 786464 | tf_op jit(solution)/shard_map/all_to_all | solution.py:388
  93.4 1.1 %shard_map.109 = (bf16[128,1024]{1,0:T(8,128)(2,1)}, bf16[128,1024]{1,0:T(8,128)(2,1)}, bf16[128,1024]{1,0:T(8,128)(2,1)}) custom-call(bf16[8,384,128]{2,1,0:T(8,128)(2,1)S(1)} %all-to-all-done.1.tok_ref), custom_call_target="tpu_custom_call" | custom-call | bytes 1572864 | tf_op jit(solution)/shard_map/pallas_call | solution.py:147
  94.4 0.8 collective-permute-done.14.other_ref
  95.2 1.4 %shard_map.110 = f32[384,1024]{1,0:T(8,128)} custom-call(bf16[512,384]{1,0:T(8,128)(2,1)S(1)} %get-tuple-element.84.own_ref, bf16[512,384]{1,0:T(8,128)(2,1)S(1)} %collective-permute-done.14.other_ref), custom_call_target="tpu_custom_call" | custom-call | bytes 2359296 | tf_op jit(solution)/shard_map/pallas_call | solution.py:147
  (20 shorter events, 0.1 us)
Async XLA Ops:
  0.6 24.1 %copy-start = (bf16[384,1024]{1,0:T(8,128)(2,1)S(1)}, bf16[384,1024]{1,0:T(8,128)(2,1)}, u32[]{:S(2)}) copy-start(bf16[384,1024]{1,0:T(8,128)(2,1)} %own_ref.1) | copy-start | bytes 2359300
  0.6 22.2 %collective-permute-start.3 = (bf16[384,1024]{1,0:T(8,128)(2,1)}, bf16[384,1024]{1,0:T(8,128)(2,1)S(1)}, u32[]{:S(2)}, u32[]{:S(2)}) collective-permute-start(bf16[384,1024]{1,0:T(8,128)(2,1)} %own_ref.1), channel_id=1, source_target_pairs={{0,2},{1,3},{2,0},{3,1},{4,6},{5,7},{6,4},{7,5},{8,10},{9,11},{10,... | collective-permute-start | bytes 2359304 | tf_op jit(solution)/shard_map/ppermute | solution.py:310
  4.7 6.8 %collective-permute-start = (bf16[64,768]{1,0:T(8,128)(2,1)S(1)}, bf16[64,768]{1,0:T(8,128)(2,1)S(1)}, u32[]{:S(2)}, u32[]{:S(2)}) collective-permute-start(bf16[64,768]{1,0:T(8,128)(2,1)S(1)} %get-tuple-element.87), channel_id=1, source_target_pairs={{0,4},{1,5},{2,6},{3,7},{4,0},{5,1},{6,2},{7,3},{8,12},{9,13},{10,... | collective-permute-start | bytes 294920 | tf_op jit(solution)/shard_map/ppermute | solution.py:310
  6.4 10.1 %collective-permute-start.1 = (bf16[64,768]{1,0:T(8,128)(2,1)S(1)}, bf16[64,768]{1,0:T(8,128)(2,1)S(1)}, u32[]{:S(2)}, u32[]{:S(2)}) collective-permute-start(bf16[64,768]{1,0:T(8,128)(2,1)S(1)} %get-tuple-element.89), channel_id=1, source_target_pairs={{0,8},{1,9},{2,10},{3,11},{4,12},{5,13},{6,14},{7,15},{8,0},{9,1},... | collective-permute-start | bytes 294920 | tf_op jit(solution)/shard_map/ppermute | solution.py:310
  9.0 7.6 %collective-permute-start.2 = (bf16[64,768]{1,0:T(8,128)(2,1)S(1)}, bf16[64,768]{1,0:T(8,128)(2,1)S(1)}, u32[]{:S(2)}, u32[]{:S(2)}) collective-permute-start(bf16[64,768]{1,0:T(8,128)(2,1)S(1)} %get-tuple-element.86), channel_id=1, source_target_pairs={{0,12},{1,13},{2,14},{3,15},{4,8},{5,9},{6,10},{7,11},{8,4},{9,5},... | collective-permute-start | bytes 294920 | tf_op jit(solution)/shard_map/ppermute | solution.py:310
  16.5 30.1 %all-to-all-start = ((bf16[8,384,128]{2,1,0:T(8,128)(2,1)}), bf16[8,384,128]{2,1,0:T(8,128)(2,1)S(1)}, u32[]{:S(2)}, u32[]{:S(2)}) async-start(bf16[8,384,128]{2,1,0:T(8,128)(2,1)} %get-tuple-element.63), calls=%async_computation | async-start | bytes 1572864 | tf_op jit(solution)/shard_map/all_to_all | solution.py:354
  22.9 1.8 %collective-permute-start.4 = (bf16[256,768]{1,0:T(8,128)(2,1)S(1)}, bf16[256,768]{1,0:T(8,128)(2,1)S(1)}, u32[]{:S(2)}, u32[]{:S(2)}) collective-permute-start(bf16[256,768]{1,0:T(8,128)(2,1)S(1)} %constant_dynamic-update-slice_fusion.piece_ref.refs_0_), channel_id=1, source_target_pairs={{0,1},{1,0},{2,3},{3,2},{4,5},{5,4},{6,7},{7,6},{8,9},{9,8},{10,11... | collective-permute-start | bytes 1179656 | tf_op jit(solution)/shard_map/ppermute | solution.py:310
  24.7 1.5 %copy-start.1 = (bf16[256,768]{1,0:T(8,128)(2,1)}, bf16[256,768]{1,0:T(8,128)(2,1)S(1)}, u32[]{:S(2)}) copy-start(bf16[256,768]{1,0:T(8,128)(2,1)S(1)} %collective-permute-done.4.swapped_ref.refs_1_) | copy-start | bytes 1179652
  26.2 14.2 %collective-permute-start.5 = (bf16[512,256]{1,0:T(8,128)(2,1)S(1)}, bf16[512,256]{1,0:T(8,128)(2,1)S(1)}, u32[]{:S(2)}, u32[]{:S(2)}) collective-permute-start(bf16[512,256]{1,0:T(8,128)(2,1)S(1)} %get-tuple-element.56), channel_id=1, source_target_pairs={{0,4},{1,5},{2,6},{3,7},{4,0},{5,1},{6,2},{7,3},{8,12},{9,13},{10,... | collective-permute-start | bytes 786440 | tf_op jit(solution)/shard_map/ppermute | solution.py:310
  40.4 18.6 %collective-permute-start.8 = (bf16[256,768]{1,0:T(8,128)(2,1)S(1)}, bf16[256,768]{1,0:T(8,128)(2,1)S(1)}, u32[]{:S(2)}, u32[]{:S(2)}) collective-permute-start(bf16[256,768]{1,0:T(8,128)(2,1)S(1)} %constant_dynamic-update-slice_fusion.piece_ref.refs_0_), channel_id=1, source_target_pairs={{0,2},{1,3},{2,0},{3,1},{4,6},{5,7},{6,4},{7,5},{8,10},{9,11},{10,... | collective-permute-start | bytes 1179656 | tf_op jit(solution)/shard_map/ppermute | solution.py:310
  42.6 16.5 %collective-permute-start.6 = (bf16[512,256]{1,0:T(8,128)(2,1)S(1)}, bf16[512,256]{1,0:T(8,128)(2,1)S(1)}, u32[]{:S(2)}, u32[]{:S(2)}) collective-permute-start(bf16[512,256]{1,0:T(8,128)(2,1)S(1)} %shard_map.104), channel_id=1, source_target_pairs={{0,8},{1,9},{2,10},{3,11},{4,12},{5,13},{6,14},{7,15},{8,0},{9,1},... | collective-permute-start | bytes 786440 | tf_op jit(solution)/shard_map/ppermute | solution.py:310
  44.2 14.9 %collective-permute-start.7 = (bf16[512,256]{1,0:T(8,128)(2,1)}, bf16[512,256]{1,0:T(8,128)(2,1)S(1)}, u32[]{:S(2)}, u32[]{:S(2)}) collective-permute-start(bf16[512,256]{1,0:T(8,128)(2,1)} %get-tuple-element.61), channel_id=1, source_target_pairs={{0,4},{1,5},{2,6},{3,7},{4,0},{5,1},{6,2},{7,3},{8,12},{9,13},{10,... | collective-permute-start | bytes 786440 | tf_op jit(solution)/shard_map/ppermute | solution.py:310
  46.6 1.0 copy-start.3
  52.5 16.1 %collective-permute-start.10 = (bf16[128,1024]{1,0:T(8,128)(2,1)S(1)}, bf16[128,1024]{1,0:T(8,128)(2,1)S(1)}, u32[]{:S(2)}, u32[]{:S(2)}) collective-permute-start(bf16[128,1024]{1,0:T(8,128)(2,1)S(1)} %get-tuple-element.65.out_ref.refs_4_), channel_id=1, source_target_pairs={{0,8},{1,9},{2,10},{3,11},{4,12},{5,13},{6,14},{7,15},{8,0},{9,1},... | collective-permute-start | bytes 786440 | tf_op jit(solution)/shard_map/ppermute | solution.py:310
  52.6 16.1 %collective-permute-start.11 = (bf16[128,1024]{1,0:T(8,128)(2,1)S(1)}, bf16[128,1024]{1,0:T(8,128)(2,1)S(1)}, u32[]{:S(2)}, u32[]{:S(2)}) collective-permute-start(bf16[128,1024]{1,0:T(8,128)(2,1)S(1)} %get-tuple-element.65.out_ref.refs_4_), channel_id=1, source_target_pairs={{0,4},{1,5},{2,6},{3,7},{4,0},{5,1},{6,2},{7,3},{8,12},{9,13},{10,... | collective-permute-start | bytes 786440 | tf_op jit(solution)/shard_map/ppermute | solution.py:310
  59.2 5.0 %collective-permute-start.12 = (bf16[512,128]{1,0:T(8,128)(2,1)S(1)}, bf16[512,128]{1,0:T(8,128)(2,1)S(1)}, u32[]{:S(2)}, u32[]{:S(2)}) collective-permute-start(bf16[512,128]{1,0:T(8,128)(2,1)S(1)} %get-tuple-element.74), channel_id=1, source_target_pairs={{0,2},{1,3},{2,0},{3,1},{4,6},{5,7},{6,4},{7,5},{8,10},{9,11},{10,... | collective-permute-start | bytes 393224 | tf_op jit(solution)/shard_map/ppermute | solution.py:310
  59.9 19.5 %collective-permute-start.9 = (bf16[256,768]{1,0:T(8,128)(2,1)S(1)}, bf16[256,768]{1,0:T(8,128)(2,1)S(1)}, u32[]{:S(2)}, u32[]{:S(2)}) collective-permute-start(bf16[256,768]{1,0:T(8,128)(2,1)S(1)} %collective-permute-done.8.refs_2_), channel_id=1, source_target_pairs={{0,1},{1,0},{2,3},{3,2},{4,5},{5,4},{6,7},{7,6},{8,9},{9,8},{10,11... | collective-permute-start | bytes 1179656 | tf_op jit(solution)/shard_map/ppermute | solution.py:310
  64.2 15.2 %copy-start.2 = (bf16[256,768]{1,0:T(8,128)(2,1)S(1)}, bf16[256,768]{1,0:T(8,128)(2,1)}, u32[]{:S(2)}) copy-start(bf16[256,768]{1,0:T(8,128)(2,1)} %copy-done.1) | copy-start | bytes 1179652
  68.6 10.0 %copy-start.4 = (bf16[128,1024]{1,0:T(8,128)(2,1)}, bf16[128,1024]{1,0:T(8,128)(2,1)S(1)}, u32[]{:S(2)}) copy-start(bf16[128,1024]{1,0:T(8,128)(2,1)S(1)} %collective-permute-done.10.refs_6_) | copy-start | bytes 786436
  68.7 0.7 copy-start.6
  69.4 9.2 %collective-permute-start.13 = (bf16[128,1024]{1,0:T(8,128)(2,1)S(1)}, bf16[128,1024]{1,0:T(8,128)(2,1)S(1)}, u32[]{:S(2)}, u32[]{:S(2)}) collective-permute-start(bf16[128,1024]{1,0:T(8,128)(2,1)S(1)} %collective-permute-done.10.refs_6_), channel_id=1, source_target_pairs={{0,4},{1,5},{2,6},{3,7},{4,0},{5,1},{6,2},{7,3},{8,12},{9,13},{10,... | collective-permute-start | bytes 786440 | tf_op jit(solution)/shard_map/ppermute | solution.py:310
  69.4 23.9 %all-to-all-start.1 = ((bf16[8,384,128]{2,1,0:T(8,128)(2,1)}), bf16[8,384,128]{2,1,0:T(8,128)(2,1)S(1)}, u32[]{:S(2)}, u32[]{:S(2)}) async-start(bf16[8,384,128]{2,1,0:T(8,128)(2,1)} %shard_map.107), calls=%async_computation.1 | async-start | bytes 1572864 | tf_op jit(solution)/shard_map/all_to_all | solution.py:388
  78.7 0.7 copy-start.8
  79.4 1.0 copy-start.5
  80.3 0.9 copy-start.7
  81.3 0.9 copy-start.9
  83.6 11.6 %collective-permute-start.14 = (bf16[512,384]{1,0:T(8,128)(2,1)S(1)}, bf16[512,384]{1,0:T(8,128)(2,1)S(1)}, u32[]{:S(2)}, u32[]{:S(2)}) collective-permute-start(bf16[512,384]{1,0:T(8,128)(2,1)S(1)} %get-tuple-element.77), channel_id=1, source_target_pairs={{0,2},{1,3},{2,0},{3,1},{4,6},{5,7},{6,4},{7,5},{8,10},{9,11},{10,... | collective-permute-start | bytes 1179656 | tf_op jit(solution)/shard_map/ppermute | solution.py:310
